TPU v7x, 32 devices: a whole 2x2x4 slice. The times are simulated.
32 devices in a mesh: groups: 2 (over x), rows: 16 (over z, y, core).
Axes of the slice: x: 2, y: 2, z: 4, core: 2. Of those that a mesh axis runs over, the one named last changes fastest.
Arguments:
- right_sides: float32 [16, 65536], P('groups', 'rows'), parts along dimension 0, may hold values from -108 to 108
- near_blocks: bfloat16 [512, 8, 128, 128], P('rows'), may hold values from -0.125 to 0.125
- near_cols: int32 [512, 8], P('rows'), may hold values from 0 to 511, as said below
- near_counts: int32 [512], P('rows'), may hold values from 3 to 8, as said below
- basis_in: bfloat16 [512, 16, 128], P('rows'), may hold values from -0.5 to 0.5
- target_basis: bfloat16 [512, 16, 128], P('rows'), may hold values from -1.5 to 1.5
- coupling: float32 [512, 8, 16, 16], P('rows'), may hold values from -0.375 to 0.375
- far_cols: int32 [512, 8], P('rows'), may hold values from 0 to 511
Outputs:
- solution: float32 [16, 65536], P('groups', 'rows'), parts along dimension 0
- next_basis: float32 [16, 65536], P('groups', 'rows'), parts along dimension 0
There are 2 independent parts, one for each index of `groups`. A program takes and returns all parts, laid end to end along the dimension named above; an argument that names none is the same for every part. Nothing has to cross between parts.
Inputs may be any that keep to these rules, and one draw needn't show every extreme that they name: near_cols[i, k] = (i + o) mod 512 with -64 <= o <= 64; slot 0 is i itself; in the first of each device's 32 rows slot 1 has o = 64 and slot 2 has o = -64. The live slots of row i are its first near_counts[i] slots.
All inputs are finite; a program needn't handle non-finite values.
Results may differ from a plain program's by a relative error of at most 0.0053.
Values may be sent and summed in bfloat16 or wider, within the bound.
No kernel may reach another device: no remote copies, remote signals or barrier semaphores. Data moves between devices by JAX's collectives and lax.ppermute only.
A program may use at most 128 MiB of HBM per device.

v0:
```python
import jax
import jax.numpy as jnp
from jax import lax
from jax.sharding import PartitionSpec as P

epsilon = 1e-06


def shifted(block, axis, distance):
    devices = range(lax.axis_size(axis))
    route = [((i - distance) % len(devices), i) for i in devices]
    return lax.ppermute(block, axis, route)


def neighbour_slabs(shaped):
    fetched = {}
    for shift_by in (2, 1, -1, -2):
        fetched[shift_by] = shifted(shaped, "rows", shift_by)
    return [fetched[2], fetched[1], shaped, fetched[-1], fetched[-2]]


def apply_operator(
    vector, near_blocks, near_cols, near_counts, basis_in, target_basis, coupling, far_cols
):
    rhs_count, local_width = vector.shape
    clusters = near_cols.shape[0]
    slot_count = near_cols.shape[1]
    cluster_size = near_blocks.shape[2]
    rank_size = basis_in.shape[1]
    slab_count = lax.axis_size("rows")
    all_clusters = clusters * slab_count
    lowered = vector.astype(jnp.bfloat16)
    shaped = lowered.reshape(rhs_count, clusters, cluster_size)
    window = jnp.concatenate(neighbour_slabs(shaped), axis=1)
    reach_len = 2 * clusters
    first_cluster = lax.axis_index("rows") * clusters
    here_rows = first_cluster + jnp.arange(clusters, dtype=jnp.int32)
    relative = (near_cols - here_rows[:, None] + reach_len) % all_clusters - reach_len
    placed = relative + reach_len + jnp.arange(clusters, dtype=jnp.int32)[:, None]
    source = jnp.take(window, placed, axis=1)
    live_mask = (jnp.arange(slot_count, dtype=jnp.int32)[None, :] < near_counts[:, None]).astype(
        jnp.bfloat16
    )
    source = source * live_mask[None, :, :, None]
    near_part = jnp.einsum(
        "ckab,rckb->rca", near_blocks, source, preferred_element_type=jnp.float32
    )
    compressed = jnp.einsum("cqb,rcb->rqc", basis_in, shaped, preferred_element_type=jnp.float32)
    collected = lax.all_gather(
        compressed.reshape(rhs_count * rank_size, clusters), "rows", axis=1, tiled=True
    )
    collected = collected.reshape(rhs_count, rank_size, all_clusters)
    picked = jnp.take(collected, far_cols, axis=2)
    coupled_matrix = jnp.einsum(
        "ckpq,rqck->rcp",
        coupling,
        picked,
        precision=lax.Precision.HIGHEST,
        preferred_element_type=jnp.float32,
    ).astype(jnp.bfloat16)
    far_field_part = jnp.einsum(
        "feq,kfe->kfq", target_basis, coupled_matrix, preferred_element_type=jnp.float32
    )
    return 0.5 * vector + (near_part + far_field_part).reshape(rhs_count, local_width)


def on_device(
    right_sides, near_blocks, near_cols, near_counts, basis_in, target_basis, coupling, far_cols
):
    unknowns = float(right_sides.shape[1] * lax.axis_size("rows"))
    start_norm = jnp.sqrt(
        lax.psum(jnp.sum(right_sides * right_sides, axis=1), "rows") / unknowns + epsilon
    )
    krylov = [right_sides / start_norm[:, None]]
    columns = []
    for iteration in range(2):
        candidate = apply_operator(
            krylov[iteration],
            near_blocks,
            near_cols,
            near_counts,
            basis_in,
            target_basis,
            coupling,
            far_cols,
        )
        products = [jnp.sum(earlier * candidate, axis=1) for earlier in krylov]
        products.append(jnp.sum(candidate * candidate, axis=1))
        summed = lax.psum(jnp.stack(products), "rows") / unknowns
        entries = [summed[position] for position in range(len(krylov))]
        remainder = summed[len(krylov)]
        for weight_k, earlier in zip(entries, krylov):
            candidate = candidate - weight_k[:, None] * earlier
            remainder = remainder - weight_k * weight_k
        length = jnp.sqrt(remainder + epsilon)
        krylov.append(candidate / length[:, None])
        columns.append(entries + [length])
    first_diag, first_sub = columns[0]
    second_top, second_diag, second_sub = columns[1]
    gram_first = first_diag * first_diag + first_sub * first_sub
    gram_cross = first_diag * second_top + first_sub * second_diag
    gram_second = second_top * second_top + second_diag * second_diag + second_sub * second_sub
    target_first = start_norm * first_diag
    target_second = start_norm * second_top
    determinant = gram_first * gram_second - gram_cross * gram_cross
    coef_first = (gram_second * target_first - gram_cross * target_second) / determinant
    coef_second = (gram_first * target_second - gram_cross * target_first) / determinant
    solution = coef_first[:, None] * krylov[0] + coef_second[:, None] * krylov[1]
    return (solution, krylov[2])


def solution(mesh):
    return jax.shard_map(
        on_device,
        mesh=mesh,
        in_specs=(
            P("groups", "rows"),
            P("rows", None, None, None),
            P("rows", None),
            P("rows"),
            P("rows", None, None),
            P("rows", None, None),
            P("rows", None, None, None),
            P("rows", None),
        ),
        out_specs=(P("groups", "rows"), P("groups", "rows")),
        check_vma=False,
    )
```

profile of v0, /device:TPU:0, one launch (start us, length us, event | category | flops | bytes accessed | tf_op | source)
XLA Modules:
  0.0 191.6 jit_solution(11703410561269266246)
XLA Ops:
  0.7 1.1 multiply_reduce_fusion.5
  1.8 34.9 %psum.21 = f32[8]{0:T(128)S(1)} all-reduce(f32[8]{0:T(128)S(1)} %multiply_reduce_fusion.5), channel_id=1, replica_groups=mesh['groups'=2,'rows'=16] {'rows'}, use_global_device_ids=true, to_apply=%region_1.0 | all-reduce | flops 8 | bytes 64 | tf_op jit(solution)/shard_map/psum | solution.py:72
  36.7 1.0 convert_bitcast_fusion.1
  37.8 4.4 %collective-permute-start.2 = (bf16[8,32,128]{2,0,1:T(8,128)(2,1)S(1)}, bf16[8,32,128]{2,0,1:T(8,128)(2,1)}, u32[]{:S(2)}, u32[]{:S(2)}) collective-permute-start(bf16[8,32,128]{2,0,1:T(8,128)(2,1)S(1)} %convert_bitcast_fusion.1), channel_id=1, source_target_pairs={{1,0},{2,1},{3,2},{4,3},{5,4},{6,5},{7,6},{8,7},{9,8},{10,9},{11,1... | collective-permute-start | bytes 196616 | tf_op jit(solution)/shard_map/ppermute | solution.py:12
  42.3 2.0 %collective-permute-start.3 = (bf16[8,32,128]{2,0,1:T(8,128)(2,1)S(1)}, bf16[8,32,128]{2,0,1:T(8,128)(2,1)S(1)}, u32[]{:S(2)}, u32[]{:S(2)}) collective-permute-start(bf16[8,32,128]{2,0,1:T(8,128)(2,1)S(1)} %convert_bitcast_fusion.1), channel_id=1, source_target_pairs={{2,0},{3,1},{4,2},{5,3},{6,4},{7,5},{8,6},{9,7},{10,8},{11,9},{12,... | collective-permute-start | bytes 196616 | tf_op jit(solution)/shard_map/ppermute | solution.py:12
  45.6 3.0 %copy.46 = f32[32,8,16,16]{3,2,1,0:T(8,128)S(1)} copy(f32[32,8,16,16]{0,3,2,1:T(8,128)} %param.18) | data formatting | bytes 524288 | tf_op args[6]
  49.0 17.9 %all_gather.6 = f32[128,512]{0,1:T(8,128)S(1)} all-gather(f32[128,32]{0,1:T(8,128)S(1)} %copy.42), channel_id=1, replica_groups=mesh['groups'=2,'rows'=16] {'rows'}, dimensions={1}, use_global_device_ids=true | all-gather | bytes 278528 | tf_op jit(solution)/shard_map/all_gather | solution.py:49
  67.0 2.0 %copy.45 = f32[8,16,512]{1,0,2:T(8,128)} copy(f32[8,16,512]{2,1,0:T(8,128)S(1)} %bitcast.150) | data formatting | bytes 524288 | tf_op jit(solution)/shard_map/reshape | solution.py:52
  71.3 2.3 %gather_fusion.1 = f32[256,8,16]{2,1,0:T(8,128)S(1)} fusion(f32[8,16,512]{1,0,2:T(8,128)} %copy.45, s32[1024]{0:T(1024)S(1)} %pad_clamp_fusion), kind=kCustom, calls=%fused_computation.1.clone | custom fusion | bytes 263168 | tf_op jit(solution)/shard_map/jit(_take)/gather | solution.py:53
  73.7 2.7 %fusion.9 = bf16[8,32,16]{2,0,1:T(8,128)(2,1)S(1)} fusion(f32[32,8,16,16]{3,2,1,0:T(8,128)S(1)} %copy.46, f32[32,8,8,16]{3,2,1,0:T(8,128)S(1)} %bitcast.149, pred[32,8]{1,0:T(8,128)(4,1)S(1)} %copy.40), kind=kOutput, calls=%fused_computation.19 | convolution fusion | flops 6328320 | bytes 401664 | tf_op jit(solution)/shard_map/ckpq,rqck->rcp/dot_general | solution.py:54
  77.4 0.9 constant_dynamic-update-slice_fusion.3
  78.4 0.9 constant_dynamic-update-slice_fusion.1
  80.1 5.5 %multiply_reduce_fusion.4 = (f32[8]{0:T(128)S(1)}, f32[8]{0:T(128)S(1)}, f32[8,4096]{1,0:T(8,128)S(1)}) fusion(f32[8,4096]{1,0:T(8,128)S(1)} %copy-done.1, f32[8]{0:T(128)} %copy-done.5, f32[32,8,128]{2,1,0:T(8,128)S(1)} %fusion.39, bf16[32,8,128,128]{3,2,1,0:T(8,128)(2,1)} %param.13, bf16[32,8,8,128]{3,2,1,0:T(8,128)(2,1)S(1)} %bitcast.153, ...), kind=kOutput, calls=%fused_computation.45 | convolution fusion | flops 67895280 | bytes 9306976 | tf_op jit(solution)/shard_map/ckab,rckb->rca/dot_general | solution.py:45
  85.6 31.6 %psum.22 = f32[2,8]{1,0:T(2,128)S(1)} all-reduce(f32[2,8]{1,0:T(2,128)S(1)} %pad_maximum_fusion.1), channel_id=1, replica_groups=mesh['groups'=2,'rows'=16] {'rows'}, use_global_device_ids=true, to_apply=%region_4.7 | all-reduce | flops 16 | bytes 128 | tf_op jit(solution)/shard_map/psum | solution.py:89
  118.3 4.4 %collective-permute-start.6 = (bf16[8,32,128]{2,0,1:T(8,128)(2,1)S(1)}, bf16[8,32,128]{2,0,1:T(8,128)(2,1)}, u32[]{:S(2)}, u32[]{:S(2)}) collective-permute-start(bf16[8,32,128]{2,0,1:T(8,128)(2,1)S(1)} %get-tuple-element.11), channel_id=1, source_target_pairs={{1,0},{2,1},{3,2},{4,3},{5,4},{6,5},{7,6},{8,7},{9,8},{10,9},{11,1... | collective-permute-start | bytes 196616 | tf_op jit(solution)/shard_map/ppermute | solution.py:12
  122.7 2.0 %collective-permute-start.7 = (bf16[8,32,128]{2,0,1:T(8,128)(2,1)S(1)}, bf16[8,32,128]{2,0,1:T(8,128)(2,1)S(1)}, u32[]{:S(2)}, u32[]{:S(2)}) collective-permute-start(bf16[8,32,128]{2,0,1:T(8,128)(2,1)S(1)} %get-tuple-element.11), channel_id=1, source_target_pairs={{2,0},{3,1},{4,2},{5,3},{6,4},{7,5},{8,6},{9,7},{10,8},{11,9},{12,... | collective-permute-start | bytes 196616 | tf_op jit(solution)/shard_map/ppermute | solution.py:12
  124.8 17.9 %all_gather.7 = f32[128,512]{0,1:T(8,128)S(1)} all-gather(f32[128,32]{0,1:T(8,128)S(1)} %copy.51), channel_id=1, replica_groups=mesh['groups'=2,'rows'=16] {'rows'}, dimensions={1}, use_global_device_ids=true | all-gather | bytes 278528 | tf_op jit(solution)/shard_map/all_gather | solution.py:49
  142.8 2.0 %copy.54 = f32[8,16,512]{1,0,2:T(8,128)} copy(f32[8,16,512]{2,1,0:T(8,128)S(1)} %bitcast.151) | data formatting | bytes 524288 | tf_op jit(solution)/shard_map/reshape | solution.py:52
  144.8 2.3 %gather_fusion.3 = f32[256,8,16]{2,1,0:T(8,128)S(1)} fusion(f32[8,16,512]{1,0,2:T(8,128)} %copy.54, s32[1024]{0:T(1024)S(1)} %pad_clamp_fusion), kind=kCustom, calls=%fused_computation.3.clone | custom fusion | bytes 263168 | tf_op jit(solution)/shard_map/jit(_take)/gather | solution.py:53
  147.1 2.7 %fusion.8 = bf16[8,32,16]{2,0,1:T(8,128)(2,1)S(1)} fusion(f32[32,8,16,16]{3,2,1,0:T(8,128)S(1)} %copy.46, f32[32,8,8,16]{3,2,1,0:T(8,128)S(1)} %bitcast.148, pred[32,8]{1,0:T(8,128)(4,1)S(1)} %copy.40), kind=kOutput, calls=%fused_computation.18 | convolution fusion | flops 6328320 | bytes 401664 | tf_op jit(solution)/shard_map/ckpq,rqck->rcp/dot_general | solution.py:54
  150.8 0.9 constant_dynamic-update-slice_fusion.8
  151.7 0.9 constant_dynamic-update-slice_fusion.6
  153.5 5.7 %multiply_reduce_fusion.2 = (f32[8]{0:T(128)S(1)}, f32[8]{0:T(128)S(1)}, f32[8]{0:T(128)S(1)}, f32[8,4096]{1,0:T(8,128)S(1)}) fusion(f32[8,4096]{1,0:T(8,128)S(1)} %copy-done.1, f32[8]{0:T(128)S(1)} %copy-done.7, f32[8,4096]{1,0:T(8,128)} %get-tuple-element.12, f32[32,8,128]{2,1,0:T(8,128)S(1)} %fusion.40, bf16[32,8,128,128]{3,2,1,0:T(8,128)(2,1)} %param.13, ...), kind=kOutput, calls=%fused_computation.42 | convolution fusion | flops 67960808 | bytes 9438080 | tf_op jit(solution)/shard_map/ckab,rckb->rca/dot_general | solution.py:45
  159.2 31.6 %psum.23 = f32[3,8]{1,0:T(4,128)S(1)} all-reduce(f32[3,8]{1,0:T(4,128)S(1)} %pad_maximum_fusion), channel_id=1, replica_groups=mesh['groups'=2,'rows'=16] {'rows'}, use_global_device_ids=true, to_apply=%region_8.11 | all-reduce | flops 24 | bytes 192 | tf_op jit(solution)/shard_map/psum | solution.py:89
  (81 shorter events, 10.5 us)
Async XLA Ops:
  0.6 75.7 %copy-start = (bf16[32,16,128]{2,1,0:T(8,128)(2,1)S(1)}, bf16[32,16,128]{2,1,0:T(8,128)(2,1)}, u32[]{:S(2)}) copy-start(bf16[32,16,128]{2,1,0:T(8,128)(2,1)} %param.17) | copy-start | bytes 393220
  0.6 47.9 %copy-start.2 = (bf16[32,16,128]{2,1,0:T(8,128)(2,1)S(1)}, bf16[32,16,128]{2,1,0:T(8,128)(2,1)}, u32[]{:S(2)}) copy-start(bf16[32,16,128]{2,1,0:T(8,128)(2,1)} %param.16) | copy-start | bytes 393220
  36.7 8.9 %copy-start.10 = (f32[8]{0:T(128)}, f32[8]{0:T(128)S(1)}, u32[]{:S(2)}) copy-start(f32[8]{0:T(128)S(1)} %psum.21) | copy-start | bytes 100
  36.7 41.6 %copy-start.5 = (f32[8]{0:T(128)}, f32[8]{0:T(128)S(1)}, u32[]{:S(2)}) copy-start(f32[8]{0:T(128)S(1)} %add_sqrt_fusion) | copy-start | bytes 100
  37.7 38.9 %collective-permute-start = (bf16[8,32,128]{2,0,1:T(8,128)(2,1)S(1)}, bf16[8,32,128]{2,0,1:T(8,128)(2,1)}, u32[]{:S(2)}, u32[]{:S(2)}) collective-permute-start(bf16[8,32,128]{2,0,1:T(8,128)(2,1)S(1)} %convert_bitcast_fusion.1), channel_id=1, source_target_pairs={{14,0},{15,1},{0,2},{1,3},{2,4},{3,5},{4,6},{5,7},{6,8},{7,9},{8,1... | collective-permute-start | bytes 196616 | tf_op jit(solution)/shard_map/ppermute | solution.py:12
  37.8 39.7 %collective-permute-start.1 = (bf16[8,32,128]{2,0,1:T(8,128)(2,1)S(1)}, bf16[8,32,128]{2,0,1:T(8,128)(2,1)}, u32[]{:S(2)}, u32[]{:S(2)}) collective-permute-start(bf16[8,32,128]{2,0,1:T(8,128)(2,1)S(1)} %convert_bitcast_fusion.1), channel_id=1, source_target_pairs={{15,0},{0,1},{1,2},{2,3},{3,4},{4,5},{5,6},{6,7},{7,8},{8,9},{9,10... | collective-permute-start | bytes 196616 | tf_op jit(solution)/shard_map/ppermute | solution.py:12
  37.8 40.6 %collective-permute-start.2 = (bf16[8,32,128]{2,0,1:T(8,128)(2,1)S(1)}, bf16[8,32,128]{2,0,1:T(8,128)(2,1)}, u32[]{:S(2)}, u32[]{:S(2)}) collective-permute-start(bf16[8,32,128]{2,0,1:T(8,128)(2,1)S(1)} %convert_bitcast_fusion.1), channel_id=1, source_target_pairs={{1,0},{2,1},{3,2},{4,3},{5,4},{6,5},{7,6},{8,7},{9,8},{10,9},{11,1... | collective-permute-start | bytes 196616 | tf_op jit(solution)/shard_map/ppermute | solution.py:12
  42.3 37.0 %collective-permute-start.3 = (bf16[8,32,128]{2,0,1:T(8,128)(2,1)S(1)}, bf16[8,32,128]{2,0,1:T(8,128)(2,1)S(1)}, u32[]{:S(2)}, u32[]{:S(2)}) collective-permute-start(bf16[8,32,128]{2,0,1:T(8,128)(2,1)S(1)} %convert_bitcast_fusion.1), channel_id=1, source_target_pairs={{2,0},{3,1},{4,2},{5,3},{6,4},{7,5},{8,6},{9,7},{10,8},{11,9},{12,... | collective-permute-start | bytes 196616 | tf_op jit(solution)/shard_map/ppermute | solution.py:12
  48.6 20.6 %copy-start.9 = (s32[32,8]{0,1:T(8,128)S(1)}, s32[32,8]{0,1:T(8,128)}, u32[]{:S(2)}) copy-start(s32[32,8]{0,1:T(8,128)} %param.14) | copy-start | bytes 3076
  48.6 22.0 %copy-start.12 = (s32[32]{0:T(128)S(1)}, s32[32]{0:T(128)}, u32[]{:S(2)}) copy-start(s32[32]{0:T(128)} %param.15) | copy-start | bytes 388
  73.7 2.9 %copy-start.8 = (s32[256]{0:T(256)S(1)}, s32[256]{0:T(256)}, u32[]{:S(2)}) copy-start(s32[256]{0:T(256)} %reshape.148) | copy-start | bytes 3076
  73.7 4.6 %copy-start.1 = (f32[8,4096]{1,0:T(8,128)S(1)}, f32[8,4096]{1,0:T(8,128)}, u32[]{:S(2)}) copy-start(f32[8,4096]{1,0:T(8,128)} %param.12) | copy-start | bytes 393220
  80.1 37.1 %copy-start.6 = (f32[8]{0:T(128)S(1)}, f32[8]{0:T(128)}, u32[]{:S(2)}) copy-start(f32[8]{0:T(128)} %copy-done.5) | copy-start | bytes 100
  80.1 37.8 %copy-start.3 = (bf16[32,16,128]{2,1,0:T(8,128)(2,1)S(1)}, bf16[32,16,128]{2,1,0:T(8,128)(2,1)}, u32[]{:S(2)}) copy-start(bf16[32,16,128]{2,1,0:T(8,128)(2,1)} %param.16) | copy-start | bytes 393220
  118.1 31.9 %collective-permute-start.4 = (bf16[8,32,128]{2,0,1:T(8,128)(2,1)S(1)}, bf16[8,32,128]{2,0,1:T(8,128)(2,1)}, u32[]{:S(2)}, u32[]{:S(2)}) collective-permute-start(bf16[8,32,128]{2,0,1:T(8,128)(2,1)S(1)} %get-tuple-element.11), channel_id=1, source_target_pairs={{14,0},{15,1},{0,2},{1,3},{2,4},{3,5},{4,6},{5,7},{6,8},{7,9},{8,1... | collective-permute-start | bytes 196616 | tf_op jit(solution)/shard_map/ppermute | solution.py:12
  118.2 32.6 %collective-permute-start.5 = (bf16[8,32,128]{2,0,1:T(8,128)(2,1)S(1)}, bf16[8,32,128]{2,0,1:T(8,128)(2,1)}, u32[]{:S(2)}, u32[]{:S(2)}) collective-permute-start(bf16[8,32,128]{2,0,1:T(8,128)(2,1)S(1)} %get-tuple-element.11), channel_id=1, source_target_pairs={{15,0},{0,1},{1,2},{2,3},{3,4},{4,5},{5,6},{6,7},{7,8},{8,9},{9,10... | collective-permute-start | bytes 196616 | tf_op jit(solution)/shard_map/ppermute | solution.py:12
  118.3 33.5 %collective-permute-start.6 = (bf16[8,32,128]{2,0,1:T(8,128)(2,1)S(1)}, bf16[8,32,128]{2,0,1:T(8,128)(2,1)}, u32[]{:S(2)}, u32[]{:S(2)}) collective-permute-start(bf16[8,32,128]{2,0,1:T(8,128)(2,1)S(1)} %get-tuple-element.11), channel_id=1, source_target_pairs={{1,0},{2,1},{3,2},{4,3},{5,4},{6,5},{7,6},{8,7},{9,8},{10,9},{11,1... | collective-permute-start | bytes 196616 | tf_op jit(solution)/shard_map/ppermute | solution.py:12
  122.7 29.9 %collective-permute-start.7 = (bf16[8,32,128]{2,0,1:T(8,128)(2,1)S(1)}, bf16[8,32,128]{2,0,1:T(8,128)(2,1)S(1)}, u32[]{:S(2)}, u32[]{:S(2)}) collective-permute-start(bf16[8,32,128]{2,0,1:T(8,128)(2,1)S(1)} %get-tuple-element.11), channel_id=1, source_target_pairs={{2,0},{3,1},{4,2},{5,3},{6,4},{7,5},{8,6},{9,7},{10,8},{11,9},{12,... | collective-permute-start | bytes 196616 | tf_op jit(solution)/shard_map/ppermute | solution.py:12
  147.1 6.3 %copy-start.7 = (f32[8]{0:T(128)S(1)}, f32[8]{0:T(128)}, u32[]{:S(2)}) copy-start(f32[8]{0:T(128)} %copy-done.5) | copy-start | bytes 100
  153.4 37.3 %copy-start.11 = (f32[8]{0:T(128)S(1)}, f32[8]{0:T(128)}, u32[]{:S(2)}) copy-start(f32[8]{0:T(128)} %copy-done.10) | copy-start | bytes 100
  153.4 37.3 %copy-start.4 = (f32[8,4096]{1,0:T(8,128)S(1)}, f32[8,4096]{1,0:T(8,128)}, u32[]{:S(2)}) copy-start(f32[8,4096]{1,0:T(8,128)} %get-tuple-element.12) | copy-start | bytes 393220
where the time goes:
time: 192 us
  blocking collectives  134 us (70%)
  local copies, waits for them, and re-layouts  20.7 us (11%)
  matrix products  17.2 us (9%)
  starting transfers between devices  13 us (7%)
  other arithmetic  5.94 us (3%)
    psum x2, blocking collectives, on_device(): summed = lax.psum(jnp.stack(products), 'rows') / unknowns  63.1 us
    all_gather x2, blocking collectives, apply_operator(): lax.all_gather(compressed.reshape(rhs_count * rank_size, clusters), 'rows...  35.8 us
    psum x1, blocking collectives, on_device(): lax.psum(jnp.sum(right_sides * right_sides, axis=1), 'rows') / unknowns  34.9 us
    ppermute x8, starting transfers between devices, shifted(): return lax.ppermute(block, axis, route)  13 us
    dot_general x2, matrix products, apply_operator(): jnp.einsum('ckab,rckb->rca', near_blocks, source, preferred_element_type=...  11.2 us
    unnamed x34, local copies, waits for them, and re-layouts  8.16 us
    dot_general x2, matrix products, apply_operator(): jnp.einsum('ckpq,rqck->rcp', coupling, picked, precision=lax.Precision.HI...  5.33 us
    gather x2, local copies, waits for them, and re-layouts, apply_operator(): picked = jnp.take(collected, far_cols, axis=2)  4.69 us
  transfers between devices with their start and end apart: 8, of which 0 were waited for; matrix products, arithmetic and copies ran while one was open for 14% of the time, Pallas kernels for 0%

commit v1 on v0

v1 whole, which is shorter than its diff:
```python
import jax
import jax.numpy as jnp
from jax import lax
from jax.sharding import PartitionSpec as P

epsilon = 1e-06


def shifted(block, distance):
    size = lax.axis_size("rows")
    route = [((i - distance) % size, i) for i in range(size)]
    return lax.ppermute(block, "rows", route)


def gather_exchange(payload):
    size = lax.axis_size("rows")
    spread = jnp.broadcast_to(payload[None], (size,) + payload.shape)
    return lax.all_to_all(spread, "rows", 0, 0)


def digits():
    rest, stride, found = lax.axis_size("rows") // 2, 2, []
    while rest > 1:
        length = 4 if rest % 4 == 0 and rest % 8 != 0 else 2
        found.append((stride, length))
        stride, rest = stride * length, rest // length
    return found + [(1, 2)]


def digit_shift(block, stride, length, step):
    size = lax.axis_size("rows")

    def target(i):
        d = (i // stride) % length
        return i + ((d + step) % length - d) * stride

    return lax.ppermute(block, "rows", [(i, target(i)) for i in range(size)])


def gather_by_digits(payload):
    size = lax.axis_size("rows")
    me = lax.axis_index("rows")
    held = payload[None]
    places = me[None]
    for stride, length in digits():
        parts, spots = [held], [places]
        for step in range(1, length):
            parts.append(digit_shift(held, stride, length, step))
            d = (places // stride) % length
            spots.append(places + ((d - step) % length - d) * stride)
        held, places = jnp.concatenate(parts), jnp.concatenate(spots)
    return held, places


def sum_by_digits(values):
    size = lax.axis_size("rows")
    for stride, length in digits():
        groups = [
            [base + d * stride for d in range(length)]
            for base in range(size)
            if (base // stride) % length == 0
        ]
        values = lax.psum(values, "rows", axis_index_groups=groups)
    return values


def operator(field, lowered, near_sources, near_blocks, compressed, coupling, far_cols, target_basis, scale):
    window, placed, live = near_sources
    rhs_count, local_width = field.shape
    source = jnp.take(window, placed, axis=1) * live[None, :, :, None]
    near = jnp.einsum("ckab,rckb->rca", near_blocks, source, preferred_element_type=jnp.float32)
    picked = jnp.take(compressed, far_cols, axis=2)
    coupled = jnp.einsum(
        "ckpq,rqck->rcp", coupling, picked, precision=lax.Precision.HIGHEST,
        preferred_element_type=jnp.float32,
    )
    coupled = (coupled * scale[:, None, None]).astype(jnp.bfloat16)
    far = jnp.einsum("feq,kfe->kfq", target_basis, coupled, preferred_element_type=jnp.float32)
    near = near * scale[:, None, None]
    return 0.5 * field * scale[:, None] + (near + far).reshape(rhs_count, local_width)


def on_device(
    right_sides, near_blocks, near_cols, near_counts, basis_in, target_basis, coupling, far_cols
):
    rhs_count, local_width = right_sides.shape
    clusters, slot_count = near_cols.shape
    cluster_size = near_blocks.shape[2]
    rank = basis_in.shape[1]
    size = lax.axis_size("rows")
    every = clusters * size
    unknowns = float(local_width * size)

    here = lax.axis_index("rows") * clusters + jnp.arange(clusters, dtype=jnp.int32)
    reach = 2 * clusters
    relative = (near_cols - here[:, None] + reach) % every - reach
    placed = relative + reach + jnp.arange(clusters, dtype=jnp.int32)[:, None]
    live = (jnp.arange(slot_count, dtype=jnp.int32)[None, :] < near_counts[:, None]).astype(jnp.bfloat16)

    def send(field, sums, way):
        lowered = field.astype(jnp.bfloat16).reshape(rhs_count, clusters, cluster_size)
        compressed = jnp.einsum(
            "cqb,rcb->rqc", basis_in.astype(jnp.float32), field.reshape(lowered.shape),
            precision=lax.Precision.HIGHEST,
        ).reshape(clusters, rhs_count * rank)
        tail = jnp.zeros((8, rhs_count * rank), jnp.float32).at[: len(sums), :rhs_count].set(jnp.stack(sums))
        payload = jnp.concatenate([compressed, tail])
        slabs = {d: shifted(lowered, d) for d in (2, 1, -1, -2)}
        if way == "exchange":
            got = gather_exchange(payload)
        else:
            got, places = gather_by_digits(payload)
            order = jnp.zeros((size,), jnp.int32).at[places].set(jnp.arange(size, dtype=jnp.int32))
            got = got[order]
        window = jnp.concatenate([slabs[2], slabs[1], lowered, slabs[-1], slabs[-2]], axis=1)
        totals = jnp.sum(got[:, clusters : clusters + len(sums), :rhs_count], axis=0) / unknowns
        whole = got[:, :clusters].reshape(size, rhs_count, rank, clusters)
        whole = jnp.moveaxis(whole, 0, 2).reshape(rhs_count, rank, every)
        return (window, placed, live), whole, totals

    def dots(*pairs):
        return [jnp.sum(f * g, axis=1) for f, g in pairs]

    sources, whole, totals = send(right_sides, dots((right_sides, right_sides)), "exchange")
    start_square = totals[0] + epsilon
    start_norm = jnp.sqrt(start_square)
    first = right_sides / start_norm[:, None]
    image = operator(
        right_sides, None, sources, near_blocks, whole, coupling, far_cols, target_basis, 1.0 / start_norm
    )
    sources, whole, totals2 = send(image, dots((first, image), (image, image)), "digits")
    h11 = totals2[0]
    v11 = totals[0] / start_square
    uu = jnp.maximum(totals2[1] - 2.0 * h11 * h11 + h11 * h11 * v11, 0.0)
    h21 = jnp.sqrt(uu + epsilon)
    second = (image - h11[:, None] * first) / h21[:, None]
    twice = operator(
        image, None, sources, near_blocks, whole, coupling, far_cols, target_basis, jnp.ones_like(h11)
    )
    candidate = (twice - h11[:, None] * image) / h21[:, None]
    v22 = uu / (uu + epsilon)
    v12 = h11 * (1.0 - v11) / h21
    totals3 = sum_by_digits(jnp.stack(dots((first, candidate), (second, candidate), (candidate, candidate)))) / unknowns
    h12, h22 = totals3[0], totals3[1]
    uu2 = (
        totals3[2] - 2.0 * (h12 * h12 + h22 * h22)
        + h12 * h12 * v11 + h22 * h22 * v22 + 2.0 * h12 * h22 * v12
    )
    h32 = jnp.sqrt(jnp.maximum(uu2, 0.0) + epsilon)
    third = (candidate - h12[:, None] * first - h22[:, None] * second) / h32[:, None]
    g11 = h11 * h11 + h21 * h21
    g12 = h11 * h12 + h21 * h22
    g22 = h12 * h12 + h22 * h22 + h32 * h32
    t1, t2 = start_norm * h11, start_norm * h12
    det = g11 * g22 - g12 * g12
    y1 = (g22 * t1 - g12 * t2) / det
    y2 = (g11 * t2 - g12 * t1) / det
    return y1[:, None] * first + y2[:, None] * second, third


def solution(mesh):
    return jax.shard_map(
        on_device,
        mesh=mesh,
        in_specs=(
            P("groups", "rows"),
            P("rows", None, None, None),
            P("rows", None),
            P("rows"),
            P("rows", None, None),
            P("rows", None, None),
            P("rows", None, None, None),
            P("rows", None),
        ),
        out_specs=(P("groups", "rows"), P("groups", "rows")),
        check_vma=False,
    )
```

time: 192 us -> 102 us (0.53)
  blocking collectives: 134 us -> 17.9 us
  waiting for transfers between devices: 0.02 us -> 12.8 us
  starting transfers between devices: 13 us -> 20.7 us
  local copies, waits for them, and re-layouts: 20.7 us -> 23.9 us
  other arithmetic: 5.94 us -> 8.32 us
    psum x3, blocking collectives: 98 us -> 17.9 us  [sum_by_digits(): values = lax.psum(values, 'rows', axis_index_groups=groups)]
    all_gather x2 -> x0, blocking collectives: 35.8 us -> none  [apply_operator(): lax.all_gather(compressed.reshape(rhs_count * rank_size, clusters), 'rows...]
    ppermute x8 -> x13, waiting for transfers between devices: 0.02 us -> 12.5 us  [the longest x5 12.5 us: digit_shift(): return lax.ppermute(block, 'rows', [(i, target(i)) for i in range(size)])]
    all_to_all x0 -> x1, starting transfers between devices: none -> 4.24 us  [gather_exchange(): return lax.all_to_all(spread, 'rows', 0, 0)]
    ppermute x8 -> x13, starting transfers between devices: 13 us -> 16.5 us  [the longest x8 14.3 us: shifted(): return lax.ppermute(block, 'rows', route)]
    unnamed x34 -> x52, local copies, waits for them, and re-layouts: 8.16 us -> 5 us
    gather x4 -> x5, local copies, waits for them, and re-layouts: 6.32 us -> 8.59 us  [the longest x2 4.69 us: operator(): picked = jnp.take(compressed, far_cols, axis=2)]
    reshape x4 -> x6, local copies, waits for them, and re-layouts: 4.05 us -> 5.62 us  [the longest x2 3.97 us: send(): whole = jnp.moveaxis(whole, 0, 2).reshape(rhs_count, rank, every)]
  transfers between devices with their start and end apart: 8 -> 14, of which waited for: 0 -> 4; matrix products, arithmetic and copies ran while one was open for 14% -> 17% of each run, Pallas kernels for 0% -> 0%
where the time goes in v1:
time: 102 us
  local copies, waits for them, and re-layouts  23.9 us (23%)
  starting transfers between devices  20.7 us (20%)
  blocking collectives  17.9 us (18%)
  matrix products  16.9 us (17%)
  waiting for transfers between devices  12.8 us (13%)
  other arithmetic  8.32 us (8%)
  between operations  1.24 us (1%)
    psum x3, blocking collectives, sum_by_digits(): values = lax.psum(values, 'rows', axis_index_groups=groups)  17.9 us
    ppermute x8, starting transfers between devices, shifted(): return lax.ppermute(block, 'rows', route)  14.3 us
    ppermute x5, waiting for transfers between devices, digit_shift(): return lax.ppermute(block, 'rows', [(i, target(i)) for i in range(size)])  12.5 us
    dot_general x2, matrix products, operator(): jnp.einsum('ckab,rckb->rca', near_blocks, source, preferred_element_type=...  9.65 us
    dot_general x2, matrix products, operator(): jnp.einsum('ckpq,rqck->rcp', coupling, picked, precision=lax.Precision.HI...  5.33 us
    unnamed x52, local copies, waits for them, and re-layouts  5 us
    gather x2, local copies, waits for them, and re-layouts, operator(): picked = jnp.take(compressed, far_cols, axis=2)  4.69 us
    all_to_all x1, starting transfers between devices, gather_exchange(): return lax.all_to_all(spread, 'rows', 0, 0)  4.24 us
  transfers between devices with their start and end apart: 14, of which 4 were waited for; matrix products, arithmetic and copies ran while one was open for 17% of the time, Pallas kernels for 0%

profile of v1, /device:TPU:0, one launch (start us, length us, event | category | flops | bytes accessed | tf_op | source)
XLA Modules:
  0.0 101.7 jit_solution(1632792168128339339)
XLA Ops:
  1.8 3.0 %collective-permute-start = (bf16[8,32,128]{2,0,1:T(8,128)(2,1)S(1)}, bf16[8,32,128]{2,0,1:T(8,128)(2,1)S(1)}, u32[]{:S(2)}, u32[]{:S(2)}) collective-permute-start(bf16[8,32,128]{2,0,1:T(8,128)(2,1)S(1)} %get-tuple-element.49), channel_id=1, source_target_pairs={{14,0},{15,1},{0,2},{1,3},{2,4},{3,5},{4,6},{5,7},{6,8},{7,9},{8,1... | collective-permute-start | bytes 196616 | tf_op jit(solution)/shard_map/ppermute | solution.py:12
  4.8 4.4 %collective-permute-start.2 = (bf16[8,32,128]{2,0,1:T(8,128)(2,1)S(1)}, bf16[8,32,128]{2,0,1:T(8,128)(2,1)S(1)}, u32[]{:S(2)}, u32[]{:S(2)}) collective-permute-start(bf16[8,32,128]{2,0,1:T(8,128)(2,1)S(1)} %get-tuple-element.49), channel_id=1, source_target_pairs={{1,0},{2,1},{3,2},{4,3},{5,4},{6,5},{7,6},{8,7},{9,8},{10,9},{11,1... | collective-permute-start | bytes 196616 | tf_op jit(solution)/shard_map/ppermute | solution.py:12
  11.9 4.2 %all-to-all-start = ((f32[16,40,128]{2,1,0:T(8,128)}), f32[16,40,128]{2,1,0:T(8,128)S(1)}, u32[]{:S(2)}, u32[]{:S(2)}) async-start(f32[16,40,128]{2,1,0:T(8,128)} %broadcast_in_dim.26), calls=%async_computation | async-start | bytes 655360 | tf_op jit(solution)/shard_map/all_to_all | solution.py:18
  18.4 1.3 %fusion.31 = bf16[32,8]{1,0:T(8,128)(2,1)} fusion(s32[32]{0:T(128)} %param.19), kind=kLoop, calls=%fused_computation.85 | loop fusion | flops 512 | bytes 640 | tf_op jit(solution)/shard_map/convert_element_type | solution.py:98
  22.2 3.0 %copy.34 = f32[32,8,16,16]{3,2,1,0:T(8,128)S(1)} copy(f32[32,8,16,16]{0,3,2,1:T(8,128)} %param.22) | data formatting | bytes 524288 | tf_op args[6]
  25.4 1.6 %gather_fusion.1 = bf16[256,8,128]{2,1,0:T(8,128)(2,1)} fusion(bf16[8,160,128]{2,0,1:T(8,128)(2,1)S(1)} %constant_dynamic-update-slice_fusion, s32[1024]{0:T(1024)S(1)} %pad_clamp_fusion.2), kind=kCustom, calls=%fused_computation.clone | custom fusion | bytes 1049600 | tf_op jit(solution)/shard_map/jit(_take)/gather | solution.py:70
  28.1 2.0 %copy.47 = f32[8,16,16,32]{1,0,3,2:T(8,128)} copy(f32[8,16,16,32]{3,1,0,2:T(8,128)S(1)} %bitcast.181) | data formatting | bytes 524288 | tf_op jit(solution)/shard_map/reshape | solution.py:118
  30.1 2.3 %gather_fusion.2 = f32[256,8,16]{2,1,0:T(8,128)S(1)} fusion(f32[8,16,512]{1,0,2:T(8,128)} %bitcast.180, s32[1024]{0:T(1024)S(1)} %pad_clamp_fusion.1), kind=kCustom, calls=%fused_computation.1.clone | custom fusion | bytes 263168 | tf_op jit(solution)/shard_map/jit(_take)/gather | solution.py:72
  32.5 2.7 %fusion.11 = bf16[8,32,16]{2,0,1:T(8,128)(2,1)S(1)} fusion(f32[32,8,16,16]{3,2,1,0:T(8,128)S(1)} %copy.34, f32[32,8,8,16]{3,2,1,0:T(8,128)S(1)} %bitcast.178, pred[32,8]{1,0:T(8,128)(4,1)S(1)} %copy.30, f32[8]{0:T(128)S(1)} %copy-done.17), kind=kOutput, calls=%fused_computation.24 | convolution fusion | flops 6332416 | bytes 401696 | tf_op jit(solution)/shard_map/ckpq,rqck->rcp/dot_general | solution.py:73
  35.2 4.8 %fusion.5 = f32[32,8,128]{2,1,0:T(8,128)S(1)} fusion(bf16[32,8,128,128]{3,2,1,0:T(8,128)(2,1)} %param.17, bf16[32,8,8,128]{3,2,1,0:T(8,128)(2,1)S(1)} %bitcast.184, pred[32,8]{1,0:T(8,128)(4,1)S(1)} %copy-done.12, bf16[32,8]{1,0:T(8,128)(2,1)S(1)} %copy-done.5, f32[8]{0:T(128)S(1)} %copy-done.17), kind=kOutput, calls=%fused_computation.13 | convolution fusion | flops 67665920 | bytes 9044768 | tf_op jit(solution)/shard_map/ckab,rckb->rca/dot_general | solution.py:71
  41.0 1.7 %collective-permute-start.8 = (f32[1,40,128]{2,1,0:T(8,128)S(1)}, f32[1,40,128]{2,1,0:T(8,128)S(1)}, u32[]{:S(2)}, u32[]{:S(2)}) collective-permute-start(f32[1,40,128]{2,1,0:T(8,128)S(1)} %maximum_bitcast_fusion), channel_id=1, source_target_pairs={{0,2},{1,3},{2,0},{3,1},{4,6},{5,7},{6,4},{7,5},{8,10},{9,11},{10,... | collective-permute-start | bytes 61448 | tf_op jit(solution)/shard_map/ppermute | solution.py:37
  43.7 4.4 %collective-permute-start.6 = (bf16[8,32,128]{2,0,1:T(8,128)(2,1)S(1)}, bf16[8,32,128]{2,0,1:T(8,128)(2,1)S(1)}, u32[]{:S(2)}, u32[]{:S(2)}) collective-permute-start(bf16[8,32,128]{2,0,1:T(8,128)(2,1)S(1)} %get-tuple-element.47), channel_id=1, source_target_pairs={{1,0},{2,1},{3,2},{4,3},{5,4},{6,5},{7,6},{8,7},{9,8},{10,9},{11,1... | collective-permute-start | bytes 196616 | tf_op jit(solution)/shard_map/ppermute | solution.py:12
  48.1 1.7 %collective-permute-start.7 = (bf16[8,32,128]{2,0,1:T(8,128)(2,1)S(1)}, bf16[8,32,128]{2,0,1:T(8,128)(2,1)S(1)}, u32[]{:S(2)}, u32[]{:S(2)}) collective-permute-start(bf16[8,32,128]{2,0,1:T(8,128)(2,1)S(1)} %get-tuple-element.47), channel_id=1, source_target_pairs={{2,0},{3,1},{4,2},{5,3},{6,4},{7,5},{8,6},{9,7},{10,8},{11,9},{12,... | collective-permute-start | bytes 196616 | tf_op jit(solution)/shard_map/ppermute | solution.py:12
  50.4 5.2 %collective-permute-done.9 = f32[2,40,128]{2,1,0:T(8,128)S(1)} collective-permute-done((f32[2,40,128]{2,1,0:T(8,128)S(1)}, f32[2,40,128]{2,1,0:T(8,128)S(1)}, u32[]{:S(2)}, u32[]{:S(2)}) %collective-permute-start.9) | collective-permute-done | bytes 40992 | tf_op jit(solution)/shard_map/ppermute | solution.py:37
  56.2 4.3 %collective-permute-done.10 = f32[2,40,128]{2,1,0:T(8,128)S(1)} collective-permute-done((f32[2,40,128]{2,1,0:T(8,128)S(1)}, f32[2,40,128]{2,1,0:T(8,128)S(1)}, u32[]{:S(2)}, u32[]{:S(2)}) %collective-permute-start.10) | collective-permute-done | bytes 40992 | tf_op jit(solution)/shard_map/ppermute | solution.py:37
  61.5 3.0 %collective-permute-done.11 = f32[2,40,128]{2,1,0:T(8,128)S(1)} collective-permute-done((f32[2,40,128]{2,1,0:T(8,128)S(1)}, f32[2,40,128]{2,1,0:T(8,128)S(1)}, u32[]{:S(2)}, u32[]{:S(2)}) %collective-permute-start.11) | collective-permute-done | bytes 40992 | tf_op jit(solution)/shard_map/ppermute | solution.py:37
  65.2 1.6 %gather_fusion.3 = bf16[256,8,128]{2,1,0:T(8,128)(2,1)} fusion(bf16[8,160,128]{2,0,1:T(8,128)(2,1)S(1)} %constant_dynamic-update-slice_fusion.5, s32[1024]{0:T(1024)S(1)} %pad_clamp_fusion.2), kind=kCustom, calls=%fused_computation.2.clone | custom fusion | bytes 1049600 | tf_op jit(solution)/shard_map/jit(_take)/gather | solution.py:70
  70.6 2.0 %copy.48 = f32[8,16,16,32]{1,0,3,2:T(8,128)} copy(f32[8,16,16,32]{3,1,0,2:T(8,128)S(1)} %bitcast.182) | data formatting | bytes 524288 | tf_op jit(solution)/shard_map/reshape | solution.py:118
  72.6 2.3 %gather_fusion.4 = f32[256,8,16]{2,1,0:T(8,128)S(1)} fusion(f32[8,16,512]{1,0,2:T(8,128)} %bitcast.179, s32[1024]{0:T(1024)S(1)} %pad_clamp_fusion.1), kind=kCustom, calls=%fused_computation.3.clone | custom fusion | bytes 263168 | tf_op jit(solution)/shard_map/jit(_take)/gather | solution.py:72
  75.0 2.7 %fusion.12 = bf16[8,32,16]{2,0,1:T(8,128)(2,1)S(1)} fusion(f32[32,8,16,16]{3,2,1,0:T(8,128)S(1)} %copy.34, f32[32,8,8,16]{3,2,1,0:T(8,128)S(1)} %bitcast.177, pred[32,8]{1,0:T(8,128)(4,1)S(1)} %copy.30), kind=kOutput, calls=%fused_computation.25 | convolution fusion | flops 6328320 | bytes 401664 | tf_op jit(solution)/shard_map/ckpq,rqck->rcp/dot_general | solution.py:73
  78.0 4.9 %multiply_reduce_fusion.2 = (f32[8]{0:T(128)S(1)}, f32[8]{0:T(128)S(1)}, f32[8]{0:T(128)S(1)}, f32[8,4096]{1,0:T(8,128)S(1)}) fusion(f32[8,4096]{1,0:T(8,128)S(1)} %copy-done.1, f32[8]{0:T(128)S(1)} %copy-done.9, f32[8]{0:T(128)S(1)} %copy-done.14, f32[8,4096]{1,0:T(8,128)S(1)} %fusion.7, f32[8]{0:T(128)S(1)} %copy-done.18, f32[32,8,128]{2,1,0:T(8,128)S(1)} %fusion.60, ...), kind=kOutput, calls=%fused_computation.51 | convolution fusion | flops 68157416 | bytes 9438144 | tf_op jit(solution)/shard_map/ckab,rckb->rca/dot_general | solution.py:71
  82.9 4.9 %psum.21 = f32[3,8]{1,0:T(4,128)S(1)} all-reduce(f32[3,8]{1,0:T(4,128)S(1)} %pad_maximum_fusion.1), channel_id=1, replica_groups={{0,2},{1,3},{4,6},{5,7},{8,10},{9,11},{12,14},{13,15},{16,18},{17,19},{..., use_global_device_ids=true, to_apply=%region_9.12 | all-reduce | flops 24 | bytes 192 | tf_op jit(solution)/shard_map/psum | solution.py:63
  87.8 10.5 %psum.22 = f32[3,8]{1,0:T(4,128)S(1)} all-reduce(f32[3,8]{1,0:T(4,128)S(1)} %psum.21), channel_id=1, replica_groups={{0,4,8,12},{1,5,9,13},{2,6,10,14},{3,7,11,15},{16,20,24,28},{17,21,25,2..., use_global_device_ids=true, to_apply=%region_10.13 | all-reduce | flops 24 | bytes 192 | tf_op jit(solution)/shard_map/psum | solution.py:63
  98.3 2.4 %psum.23 = f32[3,8]{1,0:T(4,128)S(1)} all-reduce(f32[3,8]{1,0:T(4,128)S(1)} %psum.22), channel_id=1, replica_groups={{0,1},{2,3},{4,5},{6,7},{8,9},{10,11},{12,13},{14,15},{16,17},{18,19},{..., use_global_device_ids=true, to_apply=%region_11.14 | all-reduce | flops 24 | bytes 192 | tf_op jit(solution)/shard_map/psum | solution.py:63
  (130 shorter events, 19.4 us)
Async XLA Ops:
  0.6 39.4 %copy-start = (bf16[32,16,128]{2,1,0:T(8,128)(2,1)S(1)}, bf16[32,16,128]{2,1,0:T(8,128)(2,1)}, u32[]{:S(2)}) copy-start(bf16[32,16,128]{2,1,0:T(8,128)(2,1)} %param.21) | copy-start | bytes 393220
  1.8 23.5 %collective-permute-start = (bf16[8,32,128]{2,0,1:T(8,128)(2,1)S(1)}, bf16[8,32,128]{2,0,1:T(8,128)(2,1)S(1)}, u32[]{:S(2)}, u32[]{:S(2)}) collective-permute-start(bf16[8,32,128]{2,0,1:T(8,128)(2,1)S(1)} %get-tuple-element.49), channel_id=1, source_target_pairs={{14,0},{15,1},{0,2},{1,3},{2,4},{3,5},{4,6},{5,7},{6,8},{7,9},{8,1... | collective-permute-start | bytes 196616 | tf_op jit(solution)/shard_map/ppermute | solution.py:12
  4.8 20.5 %collective-permute-start.1 = (bf16[8,32,128]{2,0,1:T(8,128)(2,1)S(1)}, bf16[8,32,128]{2,0,1:T(8,128)(2,1)S(1)}, u32[]{:S(2)}, u32[]{:S(2)}) collective-permute-start(bf16[8,32,128]{2,0,1:T(8,128)(2,1)S(1)} %get-tuple-element.49), channel_id=1, source_target_pairs={{15,0},{0,1},{1,2},{2,3},{3,4},{4,5},{5,6},{6,7},{7,8},{8,9},{9,10... | collective-permute-start | bytes 196616 | tf_op jit(solution)/shard_map/ppermute | solution.py:12
  4.8 20.5 %collective-permute-start.2 = (bf16[8,32,128]{2,0,1:T(8,128)(2,1)S(1)}, bf16[8,32,128]{2,0,1:T(8,128)(2,1)S(1)}, u32[]{:S(2)}, u32[]{:S(2)}) collective-permute-start(bf16[8,32,128]{2,0,1:T(8,128)(2,1)S(1)} %get-tuple-element.49), channel_id=1, source_target_pairs={{1,0},{2,1},{3,2},{4,3},{5,4},{6,5},{7,6},{8,7},{9,8},{10,9},{11,1... | collective-permute-start | bytes 196616 | tf_op jit(solution)/shard_map/ppermute | solution.py:12
  9.2 16.1 %collective-permute-start.3 = (bf16[8,32,128]{2,0,1:T(8,128)(2,1)S(1)}, bf16[8,32,128]{2,0,1:T(8,128)(2,1)S(1)}, u32[]{:S(2)}, u32[]{:S(2)}) collective-permute-start(bf16[8,32,128]{2,0,1:T(8,128)(2,1)S(1)} %get-tuple-element.49), channel_id=1, source_target_pairs={{2,0},{3,1},{4,2},{5,3},{6,4},{7,5},{8,6},{9,7},{10,8},{11,9},{12,... | collective-permute-start | bytes 196616 | tf_op jit(solution)/shard_map/ppermute | solution.py:12
  11.9 15.3 %all-to-all-start = ((f32[16,40,128]{2,1,0:T(8,128)}), f32[16,40,128]{2,1,0:T(8,128)S(1)}, u32[]{:S(2)}, u32[]{:S(2)}) async-start(f32[16,40,128]{2,1,0:T(8,128)} %broadcast_in_dim.26), calls=%async_computation | async-start | bytes 655360 | tf_op jit(solution)/shard_map/all_to_all | solution.py:18
  35.2 4.8 %copy-start.1 = (f32[8,4096]{1,0:T(8,128)S(1)}, f32[8,4096]{1,0:T(8,128)}, u32[]{:S(2)}) copy-start(f32[8,4096]{1,0:T(8,128)} %param.16) | copy-start | bytes 393220
  35.2 4.8 %copy-start.16 = (f32[8]{0:T(128)S(1)}, f32[8]{0:T(128)}, u32[]{:S(2)}) copy-start(f32[8]{0:T(128)} %get-tuple-element.65) | copy-start | bytes 100
  35.2 5.0 %copy-start.2 = (bf16[32,16,128]{2,1,0:T(8,128)(2,1)S(1)}, bf16[32,16,128]{2,1,0:T(8,128)(2,1)}, u32[]{:S(2)}) copy-start(bf16[32,16,128]{2,1,0:T(8,128)(2,1)} %param.20) | copy-start | bytes 393220
  35.2 5.3 %copy-start.8 = (f32[8]{0:T(128)S(1)}, f32[8]{0:T(128)}, u32[]{:S(2)}) copy-start(f32[8]{0:T(128)} %get-tuple-element.64) | copy-start | bytes 100
  41.0 8.8 %collective-permute-start.8 = (f32[1,40,128]{2,1,0:T(8,128)S(1)}, f32[1,40,128]{2,1,0:T(8,128)S(1)}, u32[]{:S(2)}, u32[]{:S(2)}) collective-permute-start(f32[1,40,128]{2,1,0:T(8,128)S(1)} %maximum_bitcast_fusion), channel_id=1, source_target_pairs={{0,2},{1,3},{2,0},{3,1},{4,6},{5,7},{6,4},{7,5},{8,10},{9,11},{10,... | collective-permute-start | bytes 61448 | tf_op jit(solution)/shard_map/ppermute | solution.py:37
  43.3 21.8 %collective-permute-start.4 = (bf16[8,32,128]{2,0,1:T(8,128)(2,1)S(1)}, bf16[8,32,128]{2,0,1:T(8,128)(2,1)S(1)}, u32[]{:S(2)}, u32[]{:S(2)}) collective-permute-start(bf16[8,32,128]{2,0,1:T(8,128)(2,1)S(1)} %get-tuple-element.47), channel_id=1, source_target_pairs={{14,0},{15,1},{0,2},{1,3},{2,4},{3,5},{4,6},{5,7},{6,8},{7,9},{8,1... | collective-permute-start | bytes 196616 | tf_op jit(solution)/shard_map/ppermute | solution.py:12
  43.7 21.5 %collective-permute-start.5 = (bf16[8,32,128]{2,0,1:T(8,128)(2,1)S(1)}, bf16[8,32,128]{2,0,1:T(8,128)(2,1)S(1)}, u32[]{:S(2)}, u32[]{:S(2)}) collective-permute-start(bf16[8,32,128]{2,0,1:T(8,128)(2,1)S(1)} %get-tuple-element.47), channel_id=1, source_target_pairs={{15,0},{0,1},{1,2},{2,3},{3,4},{4,5},{5,6},{6,7},{7,8},{8,9},{9,10... | collective-permute-start | bytes 196616 | tf_op jit(solution)/shard_map/ppermute | solution.py:12
  43.7 21.5 %collective-permute-start.6 = (bf16[8,32,128]{2,0,1:T(8,128)(2,1)S(1)}, bf16[8,32,128]{2,0,1:T(8,128)(2,1)S(1)}, u32[]{:S(2)}, u32[]{:S(2)}) collective-permute-start(bf16[8,32,128]{2,0,1:T(8,128)(2,1)S(1)} %get-tuple-element.47), channel_id=1, source_target_pairs={{1,0},{2,1},{3,2},{4,3},{5,4},{6,5},{7,6},{8,7},{9,8},{10,9},{11,1... | collective-permute-start | bytes 196616 | tf_op jit(solution)/shard_map/ppermute | solution.py:12
  48.1 17.1 %collective-permute-start.7 = (bf16[8,32,128]{2,0,1:T(8,128)(2,1)S(1)}, bf16[8,32,128]{2,0,1:T(8,128)(2,1)S(1)}, u32[]{:S(2)}, u32[]{:S(2)}) collective-permute-start(bf16[8,32,128]{2,0,1:T(8,128)(2,1)S(1)} %get-tuple-element.47), channel_id=1, source_target_pairs={{2,0},{3,1},{4,2},{5,3},{6,4},{7,5},{8,6},{9,7},{10,8},{11,9},{12,... | collective-permute-start | bytes 196616 | tf_op jit(solution)/shard_map/ppermute | solution.py:12
  49.8 5.8 %collective-permute-start.9 = (f32[2,40,128]{2,1,0:T(8,128)S(1)}, f32[2,40,128]{2,1,0:T(8,128)S(1)}, u32[]{:S(2)}, u32[]{:S(2)}) collective-permute-start(f32[2,40,128]{2,1,0:T(8,128)S(1)} %pad_maximum_fusion), channel_id=1, source_target_pairs={{0,4},{1,5},{2,6},{3,7},{4,8},{5,9},{6,10},{7,11},{8,12},{9,13},{1... | collective-permute-start | bytes 122888 | tf_op jit(solution)/shard_map/ppermute | solution.py:37
  55.6 4.9 %collective-permute-start.10 = (f32[2,40,128]{2,1,0:T(8,128)S(1)}, f32[2,40,128]{2,1,0:T(8,128)S(1)}, u32[]{:S(2)}, u32[]{:S(2)}) collective-permute-start(f32[2,40,128]{2,1,0:T(8,128)S(1)} %pad_maximum_fusion), channel_id=1, source_target_pairs={{0,8},{1,9},{2,10},{3,11},{4,12},{5,13},{6,14},{7,15},{8,0},{9,1},... | collective-permute-start | bytes 122888 | tf_op jit(solution)/shard_map/ppermute | solution.py:37
  60.5 4.0 %collective-permute-start.11 = (f32[2,40,128]{2,1,0:T(8,128)S(1)}, f32[2,40,128]{2,1,0:T(8,128)S(1)}, u32[]{:S(2)}, u32[]{:S(2)}) collective-permute-start(f32[2,40,128]{2,1,0:T(8,128)S(1)} %pad_maximum_fusion), channel_id=1, source_target_pairs={{0,12},{1,13},{2,14},{3,15},{4,0},{5,1},{6,2},{7,3},{8,4},{9,5},{1... | collective-permute-start | bytes 122888 | tf_op jit(solution)/shard_map/ppermute | solution.py:37
  65.1 1.7 %collective-permute-start.12 = (f32[8,40,128]{2,1,0:T(8,128)}, f32[8,40,128]{2,1,0:T(8,128)S(1)}, u32[]{:S(2)}, u32[]{:S(2)}) collective-permute-start(f32[8,40,128]{2,1,0:T(8,128)} %get-tuple-element.50), channel_id=1, source_target_pairs={{0,1},{1,0},{2,3},{3,2},{4,5},{5,4},{6,7},{7,6},{8,9},{9,8},{10,11... | collective-permute-start | bytes 491528 | tf_op jit(solution)/shard_map/ppermute | solution.py:37
  77.9 22.9 %copy-start.7 = (f32[8]{0:T(128)S(1)}, f32[8]{0:T(128)}, u32[]{:S(2)}) copy-start(f32[8]{0:T(128)} %get-tuple-element.38) | copy-start | bytes 100
  77.9 22.9 %copy-start.11 = (f32[8]{0:T(128)S(1)}, f32[8]{0:T(128)}, u32[]{:S(2)}) copy-start(f32[8]{0:T(128)} %get-tuple-element.39) | copy-start | bytes 100
  77.9 22.9 %copy-start.10 = (f32[8]{0:T(128)S(1)}, f32[8]{0:T(128)}, u32[]{:S(2)}) copy-start(f32[8]{0:T(128)} %get-tuple-element.64) | copy-start | bytes 100
  77.9 22.9 %copy-start.15 = (f32[8]{0:T(128)S(1)}, f32[8]{0:T(128)}, u32[]{:S(2)}) copy-start(f32[8]{0:T(128)} %get-tuple-element.37) | copy-start | bytes 100
  78.0 22.9 %copy-start.19 = (f32[8]{0:T(128)S(1)}, f32[8]{0:T(128)}, u32[]{:S(2)}) copy-start(f32[8]{0:T(128)} %slice_bitcast_fusion.2) | copy-start | bytes 100
  (10 other events, 27.9 us)

commit v2 on v0

v2 whole, which is shorter than its diff:
```python
import functools

import jax
import jax.numpy as jnp
from jax import lax
from jax.experimental import pallas as pl
from jax.experimental.pallas import tpu as pltpu
from jax.sharding import PartitionSpec as P

epsilon = 1e-06
f32, bf16 = jnp.float32, jnp.bfloat16
VMEM = pl.BlockSpec(memory_space=pltpu.VMEM)
SMEM = pl.BlockSpec(memory_space=pltpu.SMEM)
ANY = pl.BlockSpec(memory_space=pl.ANY)
R = 8
LANES = 128
SUM_SLOTS = 8
TAIL = 16
PARAMS = pltpu.CompilerParams(vmem_limit_bytes=40 * 1024 * 1024)


def lane_ids(rows=R):
    return lax.broadcasted_iota(jnp.int32, (rows, LANES), 1)


def rows_of(ref, j):
    return ref[pl.ds(j * R, R), :]


def dot(a, b, contract=(1, 0)):
    return lax.dot_general(a, b, (((contract[0],), (contract[1],)), ((), ())), preferred_element_type=f32)


def sums_tile(sums):
    lane = lane_ids()
    tile = jnp.zeros((R, LANES), f32)
    for t, partial in enumerate(sums):
        total = jnp.sum(partial, axis=1, keepdims=True)
        high = total.astype(bf16).astype(f32)
        middle = (total - high).astype(bf16).astype(f32)
        low = total - high - middle
        for part, value in enumerate((high, middle, low)):
            tile = jnp.where(lane == part * SUM_SLOTS + t, value, tile)
    return jnp.concatenate([tile, jnp.zeros((TAIL - R, LANES), f32)], axis=0).astype(bf16)


def read_sums(got, first_row, count, unknowns):
    total = jnp.zeros((R, LANES), f32)
    for device in range(got.shape[0]):
        total = total + got[device, pl.ds(first_row, TAIL), :].astype(f32)[:R]
    return [
        sum(total[:, p * SUM_SLOTS + t : p * SUM_SLOTS + t + 1] for p in range(3)) * (1.0 / unknowns)
        for t in range(count)
    ]


def compress(tiles, basis, group):
    stacked = jnp.concatenate(tiles, axis=0)
    high = stacked.astype(bf16)
    low = (stacked - high.astype(f32)).astype(bf16)
    both = dot(jnp.concatenate([high, low], axis=0), basis[pl.ds(group * LANES, LANES), :], (1, 1))
    rows = len(tiles) * R
    both = both[:rows] + both[rows:]
    lane = lane_ids()
    rank = LANES // len(tiles)
    tile = jnp.zeros((R, LANES), f32)
    for m in range(len(tiles)):
        tile = jnp.where(lane // rank == m, both[m * R : (m + 1) * R], tile)
    return tile


def write_payload(payload, tiles, basis, sums, per_group):
    groups = len(tiles) // per_group
    parts = [compress(tiles[g * per_group : (g + 1) * per_group], basis, g) for g in range(groups)]
    block = jnp.concatenate([jnp.concatenate(parts, axis=0).astype(bf16), sums_tile(sums)], axis=0)
    for device in range(payload.shape[0]):
        payload[device] = block


def start_kernel(per_group, b, basis, lowered, payload):
    clusters = b.shape[1] // LANES
    tiles = [b[:, j * LANES : (j + 1) * LANES] for j in range(clusters)]
    lowered[...] = jnp.concatenate(tiles, axis=0).astype(bf16)
    square = sum(t * t for t in tiles)
    write_payload(payload, tiles, basis, [square], per_group)


def prepare_kernel(coupling, target, high_out, low_out, target_out):
    slots, rank, _, clusters = coupling.shape
    per_tile = LANES // clusters
    for s in range(rank // per_tile):
        pieces = [
            coupling[:, s * per_tile + p].reshape(slots * rank, clusters) for p in range(per_tile)
        ]
        tile = jnp.concatenate(pieces, axis=1)
        high = tile.astype(bf16)
        high_out[:, s * LANES : (s + 1) * LANES] = high
        low_out[:, s * LANES : (s + 1) * LANES] = (tile - high.astype(f32)).astype(bf16)
    size = rank * clusters
    row = lax.broadcasted_iota(jnp.int32, (size, size), 0)
    column = lax.broadcasted_iota(jnp.int32, (size, size), 1)
    wanted = (row % clusters) * rank + row // clusters
    target_out[...] = dot((column == wanted).astype(bf16), target[...]).astype(bf16)


def far_field(got, far_cols, high, low, target, table, clusters, rank, far):
    slots = far_cols.shape[0]
    per_group = LANES // rank
    groups = clusters // per_group
    head = groups * R
    for device in range(got.shape[0]):
        table[pl.ds(device * head, head), :] = got[device, pl.ds(0, head), :].astype(f32)
    lane = lane_ids()
    picked = []
    for i in range(clusters):
        tile = jnp.zeros((R, LANES), f32)
        for k in range(slots):
            j = far_cols[k, i]
            found = table[pl.ds(pl.multiple_of(lax.div(j, per_group) * R, R), R), :]
            shift = ((k - j) * rank) & (LANES - 1)
            tile = jnp.where(lane // rank == k, pltpu.roll(found, shift, 1), tile)
        picked.append(tile)
    picked = jnp.concatenate(picked, axis=0).astype(bf16)
    crossed = dot(picked, high[...]) + dot(picked, low[...])
    expanded_high, expanded_low = [], []
    for s in range(rank * clusters // LANES):
        tile = jnp.zeros((R, LANES), f32)
        for i in range(clusters):
            part = crossed[i * R : (i + 1) * R, s * LANES : (s + 1) * LANES]
            tile = jnp.where(lane % clusters == i, part, tile)
        tile_high = tile.astype(bf16).astype(f32)
        tile_low = tile - tile_high
        for source, kept in ((tile_high, expanded_high), (tile_low, expanded_low)):
            spread = [jnp.where(lane % clusters == i, source, 0.0) for i in range(clusters)]
            kept.append(jnp.concatenate(spread, axis=0).astype(bf16))
    far[...] = dot(jnp.concatenate(expanded_high, axis=1), target[...]) + dot(
        jnp.concatenate(expanded_low, axis=1), target[...]
    )


def near_field(slabs, placed, blocks, window, near, copies):
    rows = slabs[0].shape[0]
    for at, slab in enumerate(slabs):
        window[pl.ds(at * rows, rows), :] = slab[...].astype(f32)
    window[pl.ds(len(slabs) * rows, R), :] = jnp.zeros((R, LANES), f32)
    slots, clusters = placed.shape
    chunks = copies.chunks
    per_chunk = clusters // chunks

    def body(chunk, carry):
        copies.wait(chunk)
        for inner in range(per_chunk):
            i = chunk * per_chunk + inner
            total = jnp.zeros((R, LANES), f32)
            for k in range(slots):
                source = window[pl.ds(pl.multiple_of(placed[k, i] * R, R), R), :].astype(bf16)
                total = total + dot(source, blocks[i * slots + k], (1, 1))
            near[pl.ds(pl.multiple_of(i * R, R), R), :] = total
        return carry

    lax.fori_loop(0, chunks, body, 0)


class BlockCopies:
    chunks = 8

    def __init__(self, source, target, sems):
        self.source, self.target, self.sems = source, target, sems
        self.rows = source.shape[0] // self.chunks

    def copy(self, chunk):
        span = pl.ds(chunk * self.rows, self.rows)
        return pltpu.make_async_copy(self.source.at[span], self.target.at[span], self.sems.at[chunk])

    def start(self):
        for chunk in range(self.chunks):
            self.copy(chunk).start()

    def wait(self, chunk):
        self.copy(chunk).wait()


def norm_parts(sums):
    square = sums[0]
    whole = square + epsilon
    return jnp.sqrt(whole), square / whole


def first_kernel(
    per_group, unknowns, b, slab_a, slab_b, slab_c, slab_d, slab_e, got, placed, far_cols, blocks_hbm,
    basis, high, low, target, image, lowered, payload, blocks, window, table, near, far, sems,
):
    copies = BlockCopies(blocks_hbm, blocks, sems)
    copies.start()
    slots, clusters = placed.shape
    head = clusters // per_group * R
    far_field(got, far_cols, high, low, target, table, clusters, LANES // per_group, far)
    near_field((slab_a, slab_b, slab_c, slab_d, slab_e), placed, blocks, window, near, copies)
    start_norm, _ = norm_parts(read_sums(got, head, 1, unknowns))
    scale = 1.0 / start_norm
    cross = jnp.zeros((R, LANES), f32)
    square = jnp.zeros((R, LANES), f32)
    tiles = []
    for j in range(clusters):
        field = b[:, j * LANES : (j + 1) * LANES]
        made = (0.5 * field + (rows_of(near, j) + rows_of(far, j))) * scale
        cross = cross + (field * scale) * made
        square = square + made * made
        image[pl.ds(j * R, R), :] = made
        tiles.append(made)
    lowered[...] = jnp.concatenate(tiles, axis=0).astype(bf16)
    write_payload(payload, tiles, basis, [cross, square], per_group)


def arnoldi_one(sums0, sums1):
    _, v11 = norm_parts(sums0)
    h11 = sums1[0]
    uu = jnp.maximum(sums1[1] - 2.0 * h11 * h11 + h11 * h11 * v11, 0.0)
    h21 = jnp.sqrt(uu + epsilon)
    return h11, h21, v11, uu / (uu + epsilon), h11 * (1.0 - v11) / h21


def second_kernel(
    per_group, unknowns, b, image, slab_a, slab_b, slab_c, slab_d, slab_e, got0, got, placed, far_cols,
    blocks_hbm, high, low, target, candidate, payload, blocks, window, table, near, far, sems,
):
    copies = BlockCopies(blocks_hbm, blocks, sems)
    copies.start()
    slots, clusters = placed.shape
    head = clusters // per_group * R
    far_field(got, far_cols, high, low, target, table, clusters, LANES // per_group, far)
    near_field((slab_a, slab_b, slab_c, slab_d, slab_e), placed, blocks, window, near, copies)
    sums0 = read_sums(got0, head, 1, unknowns)
    scale = 1.0 / norm_parts(sums0)[0]
    h11, h21, _, _, _ = arnoldi_one(sums0, read_sums(got, head, 2, unknowns))
    inverse = 1.0 / h21
    sums = [jnp.zeros((R, LANES), f32) for _ in range(3)]
    for j in range(clusters):
        held = rows_of(image, j)
        first = b[:, j * LANES : (j + 1) * LANES] * scale
        second = (held - h11 * first) * inverse
        made = (0.5 * held + (rows_of(near, j) + rows_of(far, j)) - h11 * held) * inverse
        sums = [s + v * made for s, v in zip(sums, (first, second, made))]
        candidate[pl.ds(j * R, R), :] = made
    block = sums_tile(sums)
    for device in range(payload.shape[0]):
        payload[device] = block


def finish_kernel(per_group, unknowns, b, image, candidate, got0, got1, got2, solution_out, next_out):
    clusters = b.shape[1] // LANES
    head = clusters // per_group * R
    sums0 = read_sums(got0, head, 1, unknowns)
    start_norm, _ = norm_parts(sums0)
    h11, h21, v11, v22, v12 = arnoldi_one(sums0, read_sums(got1, head, 2, unknowns))
    h12, h22, ww = read_sums(got2, 0, 3, unknowns)
    uu = ww - 2.0 * (h12 * h12 + h22 * h22) + h12 * h12 * v11 + h22 * h22 * v22 + 2.0 * h12 * h22 * v12
    h32 = jnp.sqrt(jnp.maximum(uu, 0.0) + epsilon)
    g11 = h11 * h11 + h21 * h21
    g12 = h11 * h12 + h21 * h22
    g22 = h12 * h12 + h22 * h22 + h32 * h32
    t1, t2 = start_norm * h11, start_norm * h12
    det = g11 * g22 - g12 * g12
    y1 = (g22 * t1 - g12 * t2) / det
    y2 = (g11 * t2 - g12 * t1) / det
    scale, inverse, last = 1.0 / start_norm, 1.0 / h21, 1.0 / h32
    for j in range(clusters):
        span = slice(j * LANES, (j + 1) * LANES)
        first = b[:, span] * scale
        second = (rows_of(image, j) - h11 * first) * inverse
        solution_out[:, span] = y1 * first + y2 * second
        next_out[:, span] = (rows_of(candidate, j) - h12 * first - h22 * second) * last


def shifted(block, distance):
    size = lax.axis_size("rows")
    return lax.ppermute(block, "rows", [((i - distance) % size, i) for i in range(size)])


def on_device(
    right_sides, near_blocks, near_cols, near_counts, basis_in, target_basis, coupling, far_cols
):
    width = right_sides.shape[1]
    clusters, slots = near_cols.shape
    rank = basis_in.shape[1]
    per_group = LANES // rank
    head = clusters // per_group * R
    size = lax.axis_size("rows")
    every = clusters * size
    unknowns = float(width * size)
    rows = clusters * R

    def shape(*dims, dtype=f32):
        return jax.ShapeDtypeStruct(dims, dtype)

    basis = basis_in.reshape(clusters * rank, LANES)
    blocks = near_blocks.reshape(clusters * slots, LANES, LANES)
    lowered, payload = pl.pallas_call(
        functools.partial(start_kernel, per_group),
        out_shape=(shape(rows, LANES, dtype=bf16), shape(size, head + TAIL, LANES, dtype=bf16)),
        in_specs=[VMEM] * 2, out_specs=[VMEM] * 2, compiler_params=PARAMS, name="start",
    )(right_sides, basis)

    def exchange(block):
        return lax.all_to_all(block, "rows", 0, 0)

    def slabs_of(block):
        got = {d: shifted(block, d) for d in (2, 1, -1, -2)}
        return [got[2], got[1], block, got[-1], got[-2]]

    got0 = exchange(payload)
    slabs = slabs_of(lowered)

    high, low, target = pl.pallas_call(
        prepare_kernel,
        out_shape=(
            shape(slots * rank, rank * clusters, dtype=bf16),
            shape(slots * rank, rank * clusters, dtype=bf16),
            shape(rank * clusters, LANES, dtype=bf16),
        ),
        in_specs=[VMEM] * 2, out_specs=[VMEM] * 3, compiler_params=PARAMS, name="prepare",
    )(jnp.transpose(coupling, (1, 2, 3, 0)), target_basis.reshape(clusters * rank, LANES))
    reach = 2 * clusters
    start = lax.axis_index("rows") * clusters
    placed = (near_cols.T - start + reach) % every
    live = jnp.arange(slots, dtype=jnp.int32)[:, None] < near_counts[None, :]
    placed = jnp.where(live, placed, 5 * clusters).astype(jnp.int32)
    far_index = far_cols.T

    scratch = [
        pltpu.VMEM((clusters * slots, LANES, LANES), bf16),
        pltpu.VMEM((5 * rows + R, LANES), f32),
        pltpu.VMEM((size * head, LANES), f32),
        pltpu.VMEM((rows, LANES), f32),
        pltpu.VMEM((rows, LANES), f32),
        pltpu.SemaphoreType.DMA((BlockCopies.chunks,)),
    ]
    cost = pl.CostEstimate(flops=2 * 8 * blocks.size, bytes_accessed=2 * blocks.size, transcendentals=0)
    image, lowered, payload = pl.pallas_call(
        functools.partial(first_kernel, per_group, unknowns),
        out_shape=(
            shape(rows, LANES), shape(rows, LANES, dtype=bf16), shape(size, head + TAIL, LANES, dtype=bf16),
        ),
        in_specs=[VMEM] * 7 + [SMEM] * 2 + [ANY] + [VMEM] * 4,
        out_specs=[VMEM] * 3, scratch_shapes=scratch, compiler_params=PARAMS, cost_estimate=cost,
        name="operator_one",
    )(right_sides, *slabs, got0, placed, far_index, blocks, basis, high, low, target)
    got1 = exchange(payload)
    slabs = slabs_of(lowered)
    candidate, payload = pl.pallas_call(
        functools.partial(second_kernel, per_group, unknowns),
        out_shape=(shape(rows, LANES), shape(size, TAIL, LANES, dtype=bf16)),
        in_specs=[VMEM] * 9 + [SMEM] * 2 + [ANY] + [VMEM] * 3,
        out_specs=[VMEM] * 2, scratch_shapes=scratch, compiler_params=PARAMS, cost_estimate=cost,
        name="operator_two",
    )(right_sides, image, *slabs, got0, got1, placed, far_index, blocks, high, low, target)
    got2 = exchange(payload)
    return pl.pallas_call(
        functools.partial(finish_kernel, per_group, unknowns),
        out_shape=(shape(R, width), shape(R, width)),
        in_specs=[VMEM] * 6, out_specs=[VMEM] * 2, compiler_params=PARAMS, name="finish",
    )(right_sides, image, candidate, got0, got1, got2)


def solution(mesh):
    return jax.shard_map(
        on_device,
        mesh=mesh,
        in_specs=(
            P("groups", "rows"),
            P("rows", None, None, None),
            P("rows", None),
            P("rows"),
            P("rows", None, None),
            P("rows", None, None),
            P("rows", None, None, None),
            P("rows", None),
        ),
        out_specs=(P("groups", "rows"), P("groups", "rows")),
        check_vma=False,
    )
```

time: 192 us -> 77.3 us (0.40)
  blocking collectives: 134 us -> 9.48 us
  Pallas kernels: 0 us -> 19.6 us
  matrix products: 17.2 us -> 0 us
  starting transfers between devices: 13 us -> 23.2 us
  waiting for transfers between devices: 0.02 us -> 9.83 us
  local copies, waits for them, and re-layouts: 20.7 us -> 13.2 us
  other arithmetic: 5.94 us -> 0.7 us
    psum x3 -> x0, blocking collectives: 98 us -> none  [the longest x2 63.1 us: on_device(): summed = lax.psum(jnp.stack(products), 'rows') / unknowns]
    all_gather x2 -> x0, blocking collectives: 35.8 us -> none  [apply_operator(): lax.all_gather(compressed.reshape(rhs_count * rank_size, clusters), 'rows...]
    pallas_call x0 -> x5, Pallas kernels: none -> 19.6 us  [the longest x1 8.87 us: on_device(): pl.pallas_call(functools.partial(first_kernel, per_group, unknowns), out_...]
    dot_general x8 -> x0, matrix products: 17.2 us -> none  [the longest x2 11.2 us: apply_operator(): jnp.einsum('ckab,rckb->rca', near_blocks, source, preferred_element_type=...]
    all_to_all x0 -> x2, starting transfers between devices: none -> 10.9 us  [exchange(): return lax.all_to_all(block, 'rows', 0, 0)]
    ppermute x8, waiting for transfers between devices: 0.02 us -> 9.82 us  [shifted(): lax.ppermute(block, 'rows', [((i - distance) % size, i) for i in range(si...]
    all_to_all x0 -> x1, blocking collectives: none -> 9.48 us  [exchange(): return lax.all_to_all(block, 'rows', 0, 0)]
    gather x4 -> x0, local copies, waits for them, and re-layouts: 6.32 us -> none  [the longest x2 4.69 us: apply_operator(): picked = jnp.take(collected, far_cols, axis=2)]
  transfers between devices with their start and end apart: 8 -> 10, of which waited for: 0 -> 6; matrix products, arithmetic and copies ran while one was open for 14% -> 1% of each run, Pallas kernels for 0% -> 0%
where the time goes in v2:
time: 77.3 us; the launch traced here: 76.7 us
  starting transfers between devices  23.2 us (30%)
  Pallas kernels  19.6 us (25%)
  local copies, waits for them, and re-layouts  13.2 us (17%)
  waiting for transfers between devices  9.83 us (13%)
  blocking collectives  9.48 us (12%)
    unnamed x22, local copies, waits for them, and re-layouts  13.2 us
    ppermute x8, starting transfers between devices, shifted(): lax.ppermute(block, 'rows', [((i - distance) % size, i) for i in range(si...  12.3 us
    all_to_all x2, starting transfers between devices, exchange(): return lax.all_to_all(block, 'rows', 0, 0)  10.9 us
    ppermute x8, waiting for transfers between devices, shifted(): lax.ppermute(block, 'rows', [((i - distance) % size, i) for i in range(si...  9.82 us
    all_to_all x1, blocking collectives, exchange(): return lax.all_to_all(block, 'rows', 0, 0)  9.48 us
    pallas_call x1, Pallas kernels, on_device(): pl.pallas_call(functools.partial(first_kernel, per_group, unknowns), out_...  8.87 us
    pallas_call x1, Pallas kernels, on_device(): pl.pallas_call(functools.partial(second_kernel, per_group, unknowns), out...  8.3 us
  transfers between devices with their start and end apart: 10, of which 6 were waited for; matrix products, arithmetic and copies ran while one was open for 1% of the time, Pallas kernels for 0%

profile of v2, /device:TPU:0, one launch (start us, length us, event | category | flops | bytes accessed | tf_op | source)
XLA Modules:
  0.0 76.7 jit_solution(10057660075330576136)
XLA Ops:
  0.6 0.9 %copy-done.2 = f32[8,4096]{1,0:T(8,128)S(1)} copy-done((f32[8,4096]{1,0:T(8,128)S(1)}, f32[8,4096]{1,0:T(8,128)}, u32[]{:S(2)}) %copy-start.2) | copy-done | bytes 131096
  1.5 0.9 %copy-done.6 = bf16[32,16,128]{2,1,0:T(8,128)(2,1)S(1)} copy-done((bf16[32,16,128]{2,1,0:T(8,128)(2,1)S(1)}, bf16[32,16,128]{2,1,0:T(8,128)(2,1)}, u32[]{:S(2)}) %copy-start.6) | copy-done | bytes 131096
  2.4 0.9 %start.1 = (bf16[256,128]{1,0:T(8,128)(2,1)S(1)}, bf16[16,48,128]{2,1,0:T(8,128)(2,1)}) custom-call(f32[8,4096]{1,0:T(8,128)S(1)} %copy-done.2, bf16[512,128]{1,0:T(8,128)(2,1)S(1)} %bitcast.12), custom_call_target="tpu_custom_call" | custom-call | tf_op jit(solution)/shard_map/start/pallas_call | solution.py:298
  3.3 7.4 %all-to-all-start = ((bf16[16,48,128]{2,1,0:T(8,128)(2,1)}), bf16[16,48,128]{2,1,0:T(8,128)(2,1)S(1)}, u32[]{:S(2)}, u32[]{:S(2)}) async-start(bf16[16,48,128]{2,1,0:T(8,128)(2,1)} %get-tuple-element.13), calls=%async_computation | async-start | bytes 393216 | tf_op jit(solution)/shard_map/all_to_all | solution.py:305
  10.7 4.6 %collective-permute-start.3 = (bf16[256,128]{1,0:T(8,128)(2,1)S(1)}, bf16[256,128]{1,0:T(8,128)(2,1)S(1)}, u32[]{:S(2)}, u32[]{:S(2)}) collective-permute-start(bf16[256,128]{1,0:T(8,128)(2,1)S(1)} %get-tuple-element.12.slab_c), channel_id=1, source_target_pairs={{2,0},{3,1},{4,2},{5,3},{6,4},{7,5},{8,6},{9,7},{10,8},{11,9},{12,... | collective-permute-start | bytes 196616 | tf_op jit(solution)/shard_map/ppermute | solution.py:277
  15.9 1.0 %collective-permute-start = (bf16[256,128]{1,0:T(8,128)(2,1)S(1)}, bf16[256,128]{1,0:T(8,128)(2,1)S(1)}, u32[]{:S(2)}, u32[]{:S(2)}) collective-permute-start(bf16[256,128]{1,0:T(8,128)(2,1)S(1)} %get-tuple-element.12.slab_c), channel_id=1, source_target_pairs={{14,0},{15,1},{0,2},{1,3},{2,4},{3,5},{4,6},{5,7},{6,8},{7,9},{8,1... | collective-permute-start | bytes 196616 | tf_op jit(solution)/shard_map/ppermute | solution.py:277
  16.9 0.7 fusion.1.placed
  17.6 1.2 %copy-done.5 = f32[32,8,16,16]{0,3,2,1:T(8,128)S(1)} copy-done((f32[32,8,16,16]{0,3,2,1:T(8,128)S(1)}, f32[32,8,16,16]{0,3,2,1:T(8,128)}, u32[]{:S(2)}) %copy-start.5) | copy-done | bytes 262168
  18.8 0.9 %copy-done.8 = bf16[32,16,128]{2,1,0:T(8,128)(2,1)S(1)} copy-done((bf16[32,16,128]{2,1,0:T(8,128)(2,1)S(1)}, bf16[32,16,128]{2,1,0:T(8,128)(2,1)}, u32[]{:S(2)}) %copy-start.8) | copy-done | bytes 131096
  20.1 1.7 %collective-permute-done.1.slab_b = bf16[256,128]{1,0:T(8,128)(2,1)S(1)} collective-permute-done((bf16[256,128]{1,0:T(8,128)(2,1)S(1)}, bf16[256,128]{1,0:T(8,128)(2,1)S(1)}, u32[]{:S(2)}, u32[]{:S(2)}) %collective-permute-start.1) | collective-permute-done | bytes 65568 | tf_op jit(solution)/shard_map/ppermute | solution.py:277
  21.8 1.6 %collective-permute-done.slab_a = bf16[256,128]{1,0:T(8,128)(2,1)S(1)} collective-permute-done((bf16[256,128]{1,0:T(8,128)(2,1)S(1)}, bf16[256,128]{1,0:T(8,128)(2,1)S(1)}, u32[]{:S(2)}, u32[]{:S(2)}) %collective-permute-start) | collective-permute-done | bytes 65568 | tf_op jit(solution)/shard_map/ppermute | solution.py:277
  23.4 3.4 %copy-done = bf16[32,8,128,128]{3,2,1,0:T(8,128)(2,1)S(1)} copy-done((bf16[32,8,128,128]{3,2,1,0:T(8,128)(2,1)S(1)}, bf16[32,8,128,128]{3,2,1,0:T(8,128)(2,1)}, u32[]{:S(2)}) %copy-start) | copy-done | bytes 8388632
  26.8 0.9 %copy-done.3 = f32[8,4096]{1,0:T(8,128)S(1)} copy-done((f32[8,4096]{1,0:T(8,128)S(1)}, f32[8,4096]{1,0:T(8,128)}, u32[]{:S(2)}) %copy-start.3) | copy-done | bytes 131096
  27.7 0.9 %copy-done.7 = bf16[32,16,128]{2,1,0:T(8,128)(2,1)S(1)} copy-done((bf16[32,16,128]{2,1,0:T(8,128)(2,1)S(1)}, bf16[32,16,128]{2,1,0:T(8,128)(2,1)}, u32[]{:S(2)}) %copy-start.7) | copy-done | bytes 131096
  29.3 8.9 %operator_one.1 = (f32[256,128]{1,0:T(8,128)S(1)}, bf16[256,128]{1,0:T(8,128)(2,1)S(1)}, bf16[16,48,128]{2,1,0:T(8,128)(2,1)}) custom-call(f32[8,4096]{1,0:T(8,128)S(1)} %copy-done.3, bf16[256,128]{1,0:T(8,128)(2,1)S(1)} %collective-permute-done.slab_a, bf16[256,128]{1,0:T(8,128)(2,1)S(1)} %collective-permute-done.1.slab_b, ...), custom_call_target="tpu_custom_call" | custom-call | flops 67108864 | bytes 8388608 | tf_op jit(solution)/shard_map/operator_one/pallas_call | solution.py:339
  38.2 3.5 %all-to-all-start.1 = ((bf16[16,48,128]{2,1,0:T(8,128)(2,1)}), bf16[16,48,128]{2,1,0:T(8,128)(2,1)S(1)}, u32[]{:S(2)}, u32[]{:S(2)}) async-start(bf16[16,48,128]{2,1,0:T(8,128)(2,1)} %get-tuple-element.19), calls=%async_computation.1 | async-start | bytes 393216 | tf_op jit(solution)/shard_map/all_to_all | solution.py:305
  41.7 4.6 %collective-permute-start.7 = (bf16[256,128]{1,0:T(8,128)(2,1)S(1)}, bf16[256,128]{1,0:T(8,128)(2,1)S(1)}, u32[]{:S(2)}, u32[]{:S(2)}) collective-permute-start(bf16[256,128]{1,0:T(8,128)(2,1)S(1)} %get-tuple-element.18.slab_c), channel_id=1, source_target_pairs={{2,0},{3,1},{4,2},{5,3},{6,4},{7,5},{8,6},{9,7},{10,8},{11,9},{12,... | collective-permute-start | bytes 196616 | tf_op jit(solution)/shard_map/ppermute | solution.py:277
  46.8 1.0 %collective-permute-start.4 = (bf16[256,128]{1,0:T(8,128)(2,1)S(1)}, bf16[256,128]{1,0:T(8,128)(2,1)S(1)}, u32[]{:S(2)}, u32[]{:S(2)}) collective-permute-start(bf16[256,128]{1,0:T(8,128)(2,1)S(1)} %get-tuple-element.18.slab_c), channel_id=1, source_target_pairs={{14,0},{15,1},{0,2},{1,3},{2,4},{3,5},{4,6},{5,7},{6,8},{7,9},{8,1... | collective-permute-start | bytes 196616 | tf_op jit(solution)/shard_map/ppermute | solution.py:277
  48.8 3.9 %collective-permute-done.5.slab_b = bf16[256,128]{1,0:T(8,128)(2,1)S(1)} collective-permute-done((bf16[256,128]{1,0:T(8,128)(2,1)S(1)}, bf16[256,128]{1,0:T(8,128)(2,1)S(1)}, u32[]{:S(2)}, u32[]{:S(2)}) %collective-permute-start.5) | collective-permute-done | bytes 65568 | tf_op jit(solution)/shard_map/ppermute | solution.py:277
  52.7 1.6 %collective-permute-done.4.slab_a = bf16[256,128]{1,0:T(8,128)(2,1)S(1)} collective-permute-done((bf16[256,128]{1,0:T(8,128)(2,1)S(1)}, bf16[256,128]{1,0:T(8,128)(2,1)S(1)}, u32[]{:S(2)}, u32[]{:S(2)}) %collective-permute-start.4) | collective-permute-done | bytes 65568 | tf_op jit(solution)/shard_map/ppermute | solution.py:277
  54.4 3.4 %copy-done.1 = bf16[32,8,128,128]{3,2,1,0:T(8,128)(2,1)S(1)} copy-done((bf16[32,8,128,128]{3,2,1,0:T(8,128)(2,1)S(1)}, bf16[32,8,128,128]{3,2,1,0:T(8,128)(2,1)}, u32[]{:S(2)}) %copy-start.1) | copy-done | bytes 8388632
  57.7 8.3 %operator_two.1 = (f32[256,128]{1,0:T(8,128)S(1)}, bf16[16,16,128]{2,1,0:T(8,128)(2,1)S(1)}) custom-call(f32[8,4096]{1,0:T(8,128)S(1)} %copy-done.4, f32[256,128]{1,0:T(8,128)S(1)} %get-tuple-element.17.image, bf16[256,128]{1,0:T(8,128)(2,1)S(1)} %collective-permute-done.4.slab_a, bf16[256,128]{1,0:T(8,128)(2,1)S(1)} %collective-permute-done.5.slab_b, ...), custom_call_target="tpu_custom_call" | custom-call | flops 67108864 | bytes 8388608 | tf_op jit(solution)/shard_map/operator_two/pallas_call | solution.py:350
  66.0 9.5 %all_to_all.15.got2 = bf16[16,16,128]{2,1,0:T(8,128)(2,1)S(1)} all-to-all(bf16[16,16,128]{2,1,0:T(8,128)(2,1)S(1)} %get-tuple-element.21), channel_id=1, replica_groups=mesh['groups'=2,'rows'=16] {'rows'}, dimensions={0} | all-to-all | bytes 131072 | tf_op jit(solution)/shard_map/all_to_all | solution.py:305
  75.5 1.2 %finish.1 = (f32[8,4096]{1,0:T(8,128)}, f32[8,4096]{1,0:T(8,128)}) custom-call(f32[8,4096]{1,0:T(8,128)S(1)} %copy-done.4, f32[256,128]{1,0:T(8,128)S(1)} %get-tuple-element.17.image, f32[256,128]{1,0:T(8,128)S(1)} %get-tuple-element.20.candidate, bf16[16,48,128]{2,1,0:T(8,128)(2,1)S(1)} %all-to-all-done.got.got0, ...), custom_call_target="tpu_custom_call" | custom-call | tf_op jit(solution)/shard_map/finish/pallas_call | solution.py:358
  (25 shorter events, 3.1 us)
Async XLA Ops:
  0.6 0.9 %copy-start.2 = (f32[8,4096]{1,0:T(8,128)S(1)}, f32[8,4096]{1,0:T(8,128)}, u32[]{:S(2)}) copy-start(f32[8,4096]{1,0:T(8,128)} %b.7) | copy-start | bytes 393220
  1.5 0.9 %copy-start.6 = (bf16[32,16,128]{2,1,0:T(8,128)(2,1)S(1)}, bf16[32,16,128]{2,1,0:T(8,128)(2,1)}, u32[]{:S(2)}) copy-start(bf16[32,16,128]{2,1,0:T(8,128)(2,1)} %param.12) | copy-start | bytes 393220
  2.4 51.9 %copy-start.4 = (f32[8,4096]{1,0:T(8,128)S(1)}, f32[8,4096]{1,0:T(8,128)}, u32[]{:S(2)}) copy-start(f32[8,4096]{1,0:T(8,128)} %b.7) | copy-start | bytes 393220
  2.4 51.9 %copy-start.10 = (s32[32,8]{0,1:T(8,128)S(1)}, s32[32,8]{0,1:T(8,128)}, u32[]{:S(2)}) copy-start(s32[32,8]{0,1:T(8,128)} %param.15) | copy-start | bytes 3076
  3.3 20.1 %all-to-all-start = ((bf16[16,48,128]{2,1,0:T(8,128)(2,1)}), bf16[16,48,128]{2,1,0:T(8,128)(2,1)S(1)}, u32[]{:S(2)}, u32[]{:S(2)}) async-start(bf16[16,48,128]{2,1,0:T(8,128)(2,1)} %get-tuple-element.13), calls=%async_computation | async-start | bytes 393216 | tf_op jit(solution)/shard_map/all_to_all | solution.py:305
  10.7 9.3 %collective-permute-start.3 = (bf16[256,128]{1,0:T(8,128)(2,1)S(1)}, bf16[256,128]{1,0:T(8,128)(2,1)S(1)}, u32[]{:S(2)}, u32[]{:S(2)}) collective-permute-start(bf16[256,128]{1,0:T(8,128)(2,1)S(1)} %get-tuple-element.12.slab_c), channel_id=1, source_target_pairs={{2,0},{3,1},{4,2},{5,3},{6,4},{7,5},{8,6},{9,7},{10,8},{11,9},{12,... | collective-permute-start | bytes 196616 | tf_op jit(solution)/shard_map/ppermute | solution.py:277
  15.4 4.7 %collective-permute-start.2 = (bf16[256,128]{1,0:T(8,128)(2,1)S(1)}, bf16[256,128]{1,0:T(8,128)(2,1)S(1)}, u32[]{:S(2)}, u32[]{:S(2)}) collective-permute-start(bf16[256,128]{1,0:T(8,128)(2,1)S(1)} %get-tuple-element.12.slab_c), channel_id=1, source_target_pairs={{1,0},{2,1},{3,2},{4,3},{5,4},{6,5},{7,6},{8,7},{9,8},{10,9},{11,1... | collective-permute-start | bytes 196616 | tf_op jit(solution)/shard_map/ppermute | solution.py:277
  15.4 6.4 %collective-permute-start.1 = (bf16[256,128]{1,0:T(8,128)(2,1)S(1)}, bf16[256,128]{1,0:T(8,128)(2,1)S(1)}, u32[]{:S(2)}, u32[]{:S(2)}) collective-permute-start(bf16[256,128]{1,0:T(8,128)(2,1)S(1)} %get-tuple-element.12.slab_c), channel_id=1, source_target_pairs={{15,0},{0,1},{1,2},{2,3},{3,4},{4,5},{5,6},{6,7},{7,8},{8,9},{9,10... | collective-permute-start | bytes 196616 | tf_op jit(solution)/shard_map/ppermute | solution.py:277
  15.9 7.5 %collective-permute-start = (bf16[256,128]{1,0:T(8,128)(2,1)S(1)}, bf16[256,128]{1,0:T(8,128)(2,1)S(1)}, u32[]{:S(2)}, u32[]{:S(2)}) collective-permute-start(bf16[256,128]{1,0:T(8,128)(2,1)S(1)} %get-tuple-element.12.slab_c), channel_id=1, source_target_pairs={{14,0},{15,1},{0,2},{1,3},{2,4},{3,5},{4,6},{5,7},{6,8},{7,9},{8,1... | collective-permute-start | bytes 196616 | tf_op jit(solution)/shard_map/ppermute | solution.py:277
  17.6 1.2 %copy-start.5 = (f32[32,8,16,16]{0,3,2,1:T(8,128)S(1)}, f32[32,8,16,16]{0,3,2,1:T(8,128)}, u32[]{:S(2)}) copy-start(f32[32,8,16,16]{0,3,2,1:T(8,128)} %param.14) | copy-start | bytes 786436
  18.8 0.9 %copy-start.8 = (bf16[32,16,128]{2,1,0:T(8,128)(2,1)S(1)}, bf16[32,16,128]{2,1,0:T(8,128)(2,1)}, u32[]{:S(2)}) copy-start(bf16[32,16,128]{2,1,0:T(8,128)(2,1)} %param.13) | copy-start | bytes 393220
  23.4 3.4 %copy-start = (bf16[32,8,128,128]{3,2,1,0:T(8,128)(2,1)S(1)}, bf16[32,8,128,128]{3,2,1,0:T(8,128)(2,1)}, u32[]{:S(2)}) copy-start(bf16[32,8,128,128]{3,2,1,0:T(8,128)(2,1)} %param.9) | copy-start | bytes 25165828
  26.8 0.9 %copy-start.3 = (f32[8,4096]{1,0:T(8,128)S(1)}, f32[8,4096]{1,0:T(8,128)}, u32[]{:S(2)}) copy-start(f32[8,4096]{1,0:T(8,128)} %b.7) | copy-start | bytes 393220
  27.7 0.9 %copy-start.7 = (bf16[32,16,128]{2,1,0:T(8,128)(2,1)S(1)}, bf16[32,16,128]{2,1,0:T(8,128)(2,1)}, u32[]{:S(2)}) copy-start(bf16[32,16,128]{2,1,0:T(8,128)(2,1)} %param.12) | copy-start | bytes 393220
  28.6 0.7 copy-start.9
  38.2 16.2 %all-to-all-start.1 = ((bf16[16,48,128]{2,1,0:T(8,128)(2,1)}), bf16[16,48,128]{2,1,0:T(8,128)(2,1)S(1)}, u32[]{:S(2)}, u32[]{:S(2)}) async-start(bf16[16,48,128]{2,1,0:T(8,128)(2,1)} %get-tuple-element.19), calls=%async_computation.1 | async-start | bytes 393216 | tf_op jit(solution)/shard_map/all_to_all | solution.py:305
  41.7 6.5 %collective-permute-start.7 = (bf16[256,128]{1,0:T(8,128)(2,1)S(1)}, bf16[256,128]{1,0:T(8,128)(2,1)S(1)}, u32[]{:S(2)}, u32[]{:S(2)}) collective-permute-start(bf16[256,128]{1,0:T(8,128)(2,1)S(1)} %get-tuple-element.18.slab_c), channel_id=1, source_target_pairs={{2,0},{3,1},{4,2},{5,3},{6,4},{7,5},{8,6},{9,7},{10,8},{11,9},{12,... | collective-permute-start | bytes 196616 | tf_op jit(solution)/shard_map/ppermute | solution.py:277
  46.3 2.5 %collective-permute-start.6 = (bf16[256,128]{1,0:T(8,128)(2,1)S(1)}, bf16[256,128]{1,0:T(8,128)(2,1)S(1)}, u32[]{:S(2)}, u32[]{:S(2)}) collective-permute-start(bf16[256,128]{1,0:T(8,128)(2,1)S(1)} %get-tuple-element.18.slab_c), channel_id=1, source_target_pairs={{1,0},{2,1},{3,2},{4,3},{5,4},{6,5},{7,6},{8,7},{9,8},{10,9},{11,1... | collective-permute-start | bytes 196616 | tf_op jit(solution)/shard_map/ppermute | solution.py:277
  46.3 6.4 %collective-permute-start.5 = (bf16[256,128]{1,0:T(8,128)(2,1)S(1)}, bf16[256,128]{1,0:T(8,128)(2,1)S(1)}, u32[]{:S(2)}, u32[]{:S(2)}) collective-permute-start(bf16[256,128]{1,0:T(8,128)(2,1)S(1)} %get-tuple-element.18.slab_c), channel_id=1, source_target_pairs={{15,0},{0,1},{1,2},{2,3},{3,4},{4,5},{5,6},{6,7},{7,8},{8,9},{9,10... | collective-permute-start | bytes 196616 | tf_op jit(solution)/shard_map/ppermute | solution.py:277
  46.8 7.5 %collective-permute-start.4 = (bf16[256,128]{1,0:T(8,128)(2,1)S(1)}, bf16[256,128]{1,0:T(8,128)(2,1)S(1)}, u32[]{:S(2)}, u32[]{:S(2)}) collective-permute-start(bf16[256,128]{1,0:T(8,128)(2,1)S(1)} %get-tuple-element.18.slab_c), channel_id=1, source_target_pairs={{14,0},{15,1},{0,2},{1,3},{2,4},{3,5},{4,6},{5,7},{6,8},{7,9},{8,1... | collective-permute-start | bytes 196616 | tf_op jit(solution)/shard_map/ppermute | solution.py:277
  54.4 3.4 %copy-start.1 = (bf16[32,8,128,128]{3,2,1,0:T(8,128)(2,1)S(1)}, bf16[32,8,128,128]{3,2,1,0:T(8,128)(2,1)}, u32[]{:S(2)}) copy-start(bf16[32,8,128,128]{3,2,1,0:T(8,128)(2,1)} %param.9) | copy-start | bytes 25165828

commit v3 on v2

--- a/solution.py
+++ b/solution.py
@@ -11,12 +11,12 @@
 f32, bf16 = jnp.float32, jnp.bfloat16
 VMEM = pl.BlockSpec(memory_space=pltpu.VMEM)
 SMEM = pl.BlockSpec(memory_space=pltpu.SMEM)
-ANY = pl.BlockSpec(memory_space=pl.ANY)
+HBM = pl.BlockSpec(memory_space=pltpu.HBM)
 R = 8
 LANES = 128
 SUM_SLOTS = 8
 TAIL = 16
-PARAMS = pltpu.CompilerParams(vmem_limit_bytes=40 * 1024 * 1024)
+PARAMS = pltpu.CompilerParams(vmem_limit_bytes=24 * 1024 * 1024)
 
 
 def lane_ids(rows=R):
@@ -77,15 +77,44 @@
         payload[device] = block
 
 
-def start_kernel(per_group, b, basis, lowered, payload):
+def start_kernel(per_group, b_hbm, basis_hbm, field, basis, lowered, payload, b, sems):
+    copies = [
+        pltpu.make_async_copy(b_hbm, b, sems.at[0]),
+        pltpu.make_async_copy(basis_hbm, basis, sems.at[1]),
+    ]
+    for copy in copies:
+        copy.start()
+    for copy in copies:
+        copy.wait()
     clusters = b.shape[1] // LANES
     tiles = [b[:, j * LANES : (j + 1) * LANES] for j in range(clusters)]
+    field[...] = jnp.concatenate(tiles, axis=0)
     lowered[...] = jnp.concatenate(tiles, axis=0).astype(bf16)
     square = sum(t * t for t in tiles)
     write_payload(payload, tiles, basis, [square], per_group)
 
 
-def prepare_kernel(coupling, target, high_out, low_out, target_out):
+def prepare_kernel(
+    coupling_hbm, target_hbm, blocks_hbm, high_out, low_out, target_out, turned, coupling, target, blocks,
+    block_sems, sems,
+):
+    others = [
+        pltpu.make_async_copy(coupling_hbm, coupling, sems.at[0]),
+        pltpu.make_async_copy(target_hbm, target, sems.at[1]),
+    ]
+    for copy in others:
+        copy.start()
+    chunks = block_sems.shape[0]
+    rows = blocks.shape[0] // chunks
+
+    def copy_of(chunk):
+        span = pl.ds(chunk * rows, rows)
+        return pltpu.make_async_copy(blocks_hbm.at[span], blocks.at[span], block_sems.at[chunk])
+
+    for chunk in range(chunks):
+        copy_of(chunk).start()
+    for copy in others:
+        copy.wait()
     slots, rank, _, clusters = coupling.shape
     per_tile = LANES // clusters
     for s in range(rank // per_tile):
@@ -101,6 +130,20 @@
     column = lax.broadcasted_iota(jnp.int32, (size, size), 1)
     wanted = (row % clusters) * rank + row // clusters
     target_out[...] = dot((column == wanted).astype(bf16), target[...]).astype(bf16)
+
+    pairs_each = rows // (2 * slots)
+
+    def body(chunk, carry):
+        copy_of(chunk).wait()
+        for inner in range(pairs_each):
+            pair = chunk * pairs_each + inner
+            for k in range(slots):
+                for side in range(2):
+                    block = blocks[(2 * pair + side) * slots + k]
+                    turned[pair, k * LANES : (k + 1) * LANES, side * LANES : (side + 1) * LANES] = block.T
+        return carry
+
+    lax.fori_loop(0, chunks, body, 0)
 
 
 def far_field(got, far_cols, high, low, target, table, clusters, rank, far):
@@ -138,46 +181,24 @@
     )
 
 
-def near_field(slabs, placed, blocks, window, near, copies):
+def near_field(slabs, placed, turned, window, near):
     rows = slabs[0].shape[0]
     for at, slab in enumerate(slabs):
         window[pl.ds(at * rows, rows), :] = slab[...].astype(f32)
     window[pl.ds(len(slabs) * rows, R), :] = jnp.zeros((R, LANES), f32)
     slots, clusters = placed.shape
-    chunks = copies.chunks
-    per_chunk = clusters // chunks
-
-    def body(chunk, carry):
-        copies.wait(chunk)
-        for inner in range(per_chunk):
-            i = chunk * per_chunk + inner
-            total = jnp.zeros((R, LANES), f32)
-            for k in range(slots):
-                source = window[pl.ds(pl.multiple_of(placed[k, i] * R, R), R), :].astype(bf16)
-                total = total + dot(source, blocks[i * slots + k], (1, 1))
-            near[pl.ds(pl.multiple_of(i * R, R), R), :] = total
-        return carry
-
-    lax.fori_loop(0, chunks, body, 0)
-
-
-class BlockCopies:
-    chunks = 8
-
-    def __init__(self, source, target, sems):
-        self.source, self.target, self.sems = source, target, sems
-        self.rows = source.shape[0] // self.chunks
-
-    def copy(self, chunk):
-        span = pl.ds(chunk * self.rows, self.rows)
-        return pltpu.make_async_copy(self.source.at[span], self.target.at[span], self.sems.at[chunk])
-
-    def start(self):
-        for chunk in range(self.chunks):
-            self.copy(chunk).start()
-
-    def wait(self, chunk):
-        self.copy(chunk).wait()
+
+    def fetch(k, i):
+        return window[pl.ds(pl.multiple_of(placed[k, i] * R, R), R), :]
+
+    for pair in range(clusters // 2):
+        sources = [
+            jnp.concatenate([fetch(k, 2 * pair), fetch(k, 2 * pair + 1)], axis=0).astype(bf16)
+            for k in range(slots)
+        ]
+        both = dot(jnp.concatenate(sources, axis=1), turned[pair])
+        near[pl.ds(2 * pair * R, R), :] = both[:R, :LANES]
+        near[pl.ds((2 * pair + 1) * R, R), :] = both[R:, LANES:]
 
 
 def norm_parts(sums):
@@ -187,22 +208,20 @@
 
 
 def first_kernel(
-    per_group, unknowns, b, slab_a, slab_b, slab_c, slab_d, slab_e, got, placed, far_cols, blocks_hbm,
-    basis, high, low, target, image, lowered, payload, blocks, window, table, near, far, sems,
+    per_group, unknowns, b, slab_a, slab_b, slab_c, slab_d, slab_e, got, placed, far_cols, turned,
+    basis, high, low, target, image, lowered, payload, window, table, near, far,
 ):
-    copies = BlockCopies(blocks_hbm, blocks, sems)
-    copies.start()
     slots, clusters = placed.shape
     head = clusters // per_group * R
     far_field(got, far_cols, high, low, target, table, clusters, LANES // per_group, far)
-    near_field((slab_a, slab_b, slab_c, slab_d, slab_e), placed, blocks, window, near, copies)
+    near_field((slab_a, slab_b, slab_c, slab_d, slab_e), placed, turned, window, near)
     start_norm, _ = norm_parts(read_sums(got, head, 1, unknowns))
     scale = 1.0 / start_norm
     cross = jnp.zeros((R, LANES), f32)
     square = jnp.zeros((R, LANES), f32)
     tiles = []
     for j in range(clusters):
-        field = b[:, j * LANES : (j + 1) * LANES]
+        field = rows_of(b, j)
         made = (0.5 * field + (rows_of(near, j) + rows_of(far, j))) * scale
         cross = cross + (field * scale) * made
         square = square + made * made
@@ -222,14 +241,12 @@
 
 def second_kernel(
     per_group, unknowns, b, image, slab_a, slab_b, slab_c, slab_d, slab_e, got0, got, placed, far_cols,
-    blocks_hbm, high, low, target, candidate, payload, blocks, window, table, near, far, sems,
+    turned, high, low, target, candidate, sums_out, window, table, near, far,
 ):
-    copies = BlockCopies(blocks_hbm, blocks, sems)
-    copies.start()
     slots, clusters = placed.shape
     head = clusters // per_group * R
     far_field(got, far_cols, high, low, target, table, clusters, LANES // per_group, far)
-    near_field((slab_a, slab_b, slab_c, slab_d, slab_e), placed, blocks, window, near, copies)
+    near_field((slab_a, slab_b, slab_c, slab_d, slab_e), placed, turned, window, near)
     sums0 = read_sums(got0, head, 1, unknowns)
     scale = 1.0 / norm_parts(sums0)[0]
     h11, h21, _, _, _ = arnoldi_one(sums0, read_sums(got, head, 2, unknowns))
@@ -237,23 +254,27 @@
     sums = [jnp.zeros((R, LANES), f32) for _ in range(3)]
     for j in range(clusters):
         held = rows_of(image, j)
-        first = b[:, j * LANES : (j + 1) * LANES] * scale
+        first = rows_of(b, j) * scale
         second = (held - h11 * first) * inverse
         made = (0.5 * held + (rows_of(near, j) + rows_of(far, j)) - h11 * held) * inverse
         sums = [s + v * made for s, v in zip(sums, (first, second, made))]
         candidate[pl.ds(j * R, R), :] = made
-    block = sums_tile(sums)
-    for device in range(payload.shape[0]):
-        payload[device] = block
-
-
-def finish_kernel(per_group, unknowns, b, image, candidate, got0, got1, got2, solution_out, next_out):
-    clusters = b.shape[1] // LANES
+    lane = lane_ids()
+    tile = jnp.zeros((R, LANES), f32)
+    for t, partial in enumerate(sums):
+        tile = jnp.where(lane == t, jnp.sum(partial, axis=1, keepdims=True), tile)
+    sums_out[...] = tile
+
+
+def finish_kernel(per_group, unknowns, b, image, candidate, got0, got1, *rest):
+    *got2, solution_out, next_out = rest
+    clusters = b.shape[0] // R
     head = clusters // per_group * R
     sums0 = read_sums(got0, head, 1, unknowns)
     start_norm, _ = norm_parts(sums0)
     h11, h21, v11, v22, v12 = arnoldi_one(sums0, read_sums(got1, head, 2, unknowns))
-    h12, h22, ww = read_sums(got2, 0, 3, unknowns)
+    total = sum(part[...] for part in got2)
+    h12, h22, ww = [total[:, t : t + 1] * (1.0 / unknowns) for t in range(3)]
     uu = ww - 2.0 * (h12 * h12 + h22 * h22) + h12 * h12 * v11 + h22 * h22 * v22 + 2.0 * h12 * h22 * v12
     h32 = jnp.sqrt(jnp.maximum(uu, 0.0) + epsilon)
     g11 = h11 * h11 + h21 * h21
@@ -266,7 +287,7 @@
     scale, inverse, last = 1.0 / start_norm, 1.0 / h21, 1.0 / h32
     for j in range(clusters):
         span = slice(j * LANES, (j + 1) * LANES)
-        first = b[:, span] * scale
+        first = rows_of(b, j) * scale
         second = (rows_of(image, j) - h11 * first) * inverse
         solution_out[:, span] = y1 * first + y2 * second
         next_out[:, span] = (rows_of(candidate, j) - h12 * first - h22 * second) * last
@@ -275,6 +296,25 @@
 def shifted(block, distance):
     size = lax.axis_size("rows")
     return lax.ppermute(block, "rows", [((i - distance) % size, i) for i in range(size)])
+
+
+def stages():
+    rest, stride, found = lax.axis_size("rows"), 1, []
+    while rest > 1:
+        length = 4 if rest % 4 == 0 else 2
+        found.append((stride, length))
+        stride, rest = stride * length, rest // length
+    return found
+
+
+def digit_parts(block, stride, length):
+    size = lax.axis_size("rows")
+    parts = [block]
+    for step in range(1, length):
+        parts.append(
+            lax.ppermute(block, "rows", [(i, i ^ (step * stride)) for i in range(size)])
+        )
+    return parts
 
 
 def on_device(
@@ -293,12 +333,20 @@
     def shape(*dims, dtype=f32):
         return jax.ShapeDtypeStruct(dims, dtype)
 
+    def scratch(*dims, dtype=f32):
+        return pltpu.VMEM(dims, dtype)
+
     basis = basis_in.reshape(clusters * rank, LANES)
     blocks = near_blocks.reshape(clusters * slots, LANES, LANES)
-    lowered, payload = pl.pallas_call(
+    field, basis, lowered, payload = pl.pallas_call(
         functools.partial(start_kernel, per_group),
-        out_shape=(shape(rows, LANES, dtype=bf16), shape(size, head + TAIL, LANES, dtype=bf16)),
-        in_specs=[VMEM] * 2, out_specs=[VMEM] * 2, compiler_params=PARAMS, name="start",
+        out_shape=(
+            shape(rows, LANES), shape(clusters * rank, LANES, dtype=bf16), shape(rows, LANES, dtype=bf16),
+            shape(size, head + TAIL, LANES, dtype=bf16),
+        ),
+        in_specs=[HBM] * 2, out_specs=[VMEM] * 4,
+        scratch_shapes=[scratch(R, width), pltpu.SemaphoreType.DMA((2,))],
+        compiler_params=PARAMS, name="start",
     )(right_sides, basis)
 
     def exchange(block):
@@ -311,15 +359,23 @@
     got0 = exchange(payload)
     slabs = slabs_of(lowered)
 
-    high, low, target = pl.pallas_call(
+    turned_shape = (clusters // 2, slots * LANES, 2 * LANES)
+    high, low, target, turned = pl.pallas_call(
         prepare_kernel,
         out_shape=(
             shape(slots * rank, rank * clusters, dtype=bf16),
             shape(slots * rank, rank * clusters, dtype=bf16),
             shape(rank * clusters, LANES, dtype=bf16),
+            shape(*turned_shape, dtype=bf16),
         ),
-        in_specs=[VMEM] * 2, out_specs=[VMEM] * 3, compiler_params=PARAMS, name="prepare",
-    )(jnp.transpose(coupling, (1, 2, 3, 0)), target_basis.reshape(clusters * rank, LANES))
+        in_specs=[HBM] * 3, out_specs=[VMEM] * 4,
+        scratch_shapes=[
+            scratch(slots, rank, rank, clusters), scratch(clusters * rank, LANES, dtype=bf16),
+            scratch(clusters * slots, LANES, LANES, dtype=bf16),
+            pltpu.SemaphoreType.DMA((8,)), pltpu.SemaphoreType.DMA((2,)),
+        ],
+        compiler_params=PARAMS, name="prepare",
+    )(jnp.transpose(coupling, (1, 2, 3, 0)), target_basis.reshape(clusters * rank, LANES), blocks)
     reach = 2 * clusters
     start = lax.axis_index("rows") * clusters
     placed = (near_cols.T - start + reach) % every
@@ -327,39 +383,33 @@
     placed = jnp.where(live, placed, 5 * clusters).astype(jnp.int32)
     far_index = far_cols.T
 
-    scratch = [
-        pltpu.VMEM((clusters * slots, LANES, LANES), bf16),
-        pltpu.VMEM((5 * rows + R, LANES), f32),
-        pltpu.VMEM((size * head, LANES), f32),
-        pltpu.VMEM((rows, LANES), f32),
-        pltpu.VMEM((rows, LANES), f32),
-        pltpu.SemaphoreType.DMA((BlockCopies.chunks,)),
+    kept = [
+        scratch(5 * rows + R, LANES), scratch(size * head, LANES), scratch(rows, LANES), scratch(rows, LANES),
     ]
-    cost = pl.CostEstimate(flops=2 * 8 * blocks.size, bytes_accessed=2 * blocks.size, transcendentals=0)
     image, lowered, payload = pl.pallas_call(
         functools.partial(first_kernel, per_group, unknowns),
         out_shape=(
             shape(rows, LANES), shape(rows, LANES, dtype=bf16), shape(size, head + TAIL, LANES, dtype=bf16),
         ),
-        in_specs=[VMEM] * 7 + [SMEM] * 2 + [ANY] + [VMEM] * 4,
-        out_specs=[VMEM] * 3, scratch_shapes=scratch, compiler_params=PARAMS, cost_estimate=cost,
-        name="operator_one",
-    )(right_sides, *slabs, got0, placed, far_index, blocks, basis, high, low, target)
+        in_specs=[VMEM] * 7 + [SMEM] * 2 + [VMEM] * 5,
+        out_specs=[VMEM] * 3, scratch_shapes=kept, compiler_params=PARAMS, name="operator_one",
+    )(field, *slabs, got0, placed, far_index, turned, basis, high, low, target)
     got1 = exchange(payload)
     slabs = slabs_of(lowered)
-    candidate, payload = pl.pallas_call(
+    candidate, sums = pl.pallas_call(
         functools.partial(second_kernel, per_group, unknowns),
-        out_shape=(shape(rows, LANES), shape(size, TAIL, LANES, dtype=bf16)),
-        in_specs=[VMEM] * 9 + [SMEM] * 2 + [ANY] + [VMEM] * 3,
-        out_specs=[VMEM] * 2, scratch_shapes=scratch, compiler_params=PARAMS, cost_estimate=cost,
-        name="operator_two",
-    )(right_sides, image, *slabs, got0, got1, placed, far_index, blocks, high, low, target)
-    got2 = exchange(payload)
+        out_shape=(shape(rows, LANES), shape(R, LANES)),
+        in_specs=[VMEM] * 9 + [SMEM] * 2 + [VMEM] * 4,
+        out_specs=[VMEM] * 2, scratch_shapes=kept, compiler_params=PARAMS, name="operator_two",
+    )(field, image, *slabs, got0, got1, placed, far_index, turned, high, low, target)
+    parts = [sums]
+    for stride, length in stages():
+        parts = digit_parts(sum(parts), stride, length)
     return pl.pallas_call(
         functools.partial(finish_kernel, per_group, unknowns),
         out_shape=(shape(R, width), shape(R, width)),
-        in_specs=[VMEM] * 6, out_specs=[VMEM] * 2, compiler_params=PARAMS, name="finish",
-    )(right_sides, image, candidate, got0, got1, got2)
+        in_specs=[VMEM] * (5 + len(parts)), out_specs=[VMEM] * 2, compiler_params=PARAMS, name="finish",
+    )(field, image, candidate, got0, got1, *parts)
 
 
 def solution(mesh):

time: 77.3 us -> 74.1 us (0.959)
  blocking collectives: 9.48 us -> 0 us
  starting transfers between devices: 23.2 us -> 31.6 us
  Pallas kernels: 19.6 us -> 13.3 us
  local copies, waits for them, and re-layouts: 13.2 us -> 17.3 us
    all_to_all x1 -> x0, blocking collectives: 9.48 us -> none  [exchange(): return lax.all_to_all(block, 'rows', 0, 0)]
    ppermute x0 -> x6, starting transfers between devices: none -> 6.31 us  [digit_parts(): lax.ppermute(block, 'rows', [(i, i ^ step * stride) for i in range(size)])]
    pallas_call x1, Pallas kernels: 8.3 us -> 3.15 us  [on_device(): pl.pallas_call(functools.partial(second_kernel, per_group, unknowns), out...]
    pallas_call x1, Pallas kernels: 8.87 us -> 3.88 us  [on_device(): pl.pallas_call(functools.partial(first_kernel, per_group, unknowns), out_...]
    unnamed x22 -> x18, local copies, waits for them, and re-layouts: 13.2 us -> 17.3 us
    pallas_call x1, Pallas kernels: 0.33 us -> 3.83 us  [on_device(): pl.pallas_call(prepare_kernel, out_shape=(shape(slots * rank, rank * clus...]
    ppermute x0 -> x6, waiting for transfers between devices: none -> 3.4 us  [digit_parts(): lax.ppermute(block, 'rows', [(i, i ^ step * stride) for i in range(size)])]
    ppermute x8, waiting for transfers between devices: 9.82 us -> 6.51 us  [shifted(): lax.ppermute(block, 'rows', [((i - distance) % size, i) for i in range(si...]
  transfers between devices with their start and end apart: 10 -> 16, of which waited for: 6 -> 9; matrix products, arithmetic and copies ran while one was open for 1% -> 1% of each run, Pallas kernels for 0% -> 5%
where the time goes in v3:
time: 74.1 us; the launch traced here: 73.6 us
  starting transfers between devices  31.6 us (43%)
  local copies, waits for them, and re-layouts  17.3 us (23%)
  Pallas kernels  13.3 us (18%)
  waiting for transfers between devices  9.92 us (13%)
  between operations  0.75 us (1%)
    unnamed x18, local copies, waits for them, and re-layouts  17.3 us
    all_to_all x2, starting transfers between devices, exchange(): return lax.all_to_all(block, 'rows', 0, 0)  12.9 us
    ppermute x8, starting transfers between devices, shifted(): lax.ppermute(block, 'rows', [((i - distance) % size, i) for i in range(si...  12.3 us
    ppermute x8, waiting for transfers between devices, shifted(): lax.ppermute(block, 'rows', [((i - distance) % size, i) for i in range(si...  6.51 us
    ppermute x6, starting transfers between devices, digit_parts(): lax.ppermute(block, 'rows', [(i, i ^ step * stride) for i in range(size)])  6.31 us
    pallas_call x1, Pallas kernels, on_device(): pl.pallas_call(functools.partial(first_kernel, per_group, unknowns), out_...  3.88 us
    pallas_call x1, Pallas kernels, on_device(): pl.pallas_call(prepare_kernel, out_shape=(shape(slots * rank, rank * clus...  3.83 us
    ppermute x6, waiting for transfers between devices, digit_parts(): lax.ppermute(block, 'rows', [(i, i ^ step * stride) for i in range(size)])  3.4 us
  transfers between devices with their start and end apart: 16, of which 9 were waited for; matrix products, arithmetic and copies ran while one was open for 1% of the time, Pallas kernels for 5%

profile of v3, /device:TPU:0, one launch (start us, length us, event | category | flops | bytes accessed | tf_op | source)
XLA Modules:
  0.0 73.6 jit_solution(10286103302466455879)
XLA Ops:
  1.5 0.9 %copy-done.7 = bf16[32,16,128]{2,1,0:T(8,128)(2,1)S(1)} copy-done((bf16[32,16,128]{2,1,0:T(8,128)(2,1)S(1)}, bf16[32,16,128]{2,1,0:T(8,128)(2,1)}, u32[]{:S(2)}) %copy-start.7) | copy-done | bytes 131096
  2.4 1.2 %start.1 = (f32[256,128]{1,0:T(8,128)S(1)}, bf16[512,128]{1,0:T(8,128)(2,1)S(1)}, bf16[256,128]{1,0:T(8,128)(2,1)S(1)}, bf16[16,48,128]{2,1,0:T(8,128)(2,1)}) custom-call(f32[8,4096]{1,0:T(8,128)S(1)} %copy-done.6, bf16[512,128]{1,0:T(8,128)(2,1)S(1)} %bitcast.12), custom_call_target="tpu_custom_call" | custom-call | tf_op jit(solution)/shard_map/start/pallas_call | solution.py:341
  3.7 7.4 %all-to-all-start = ((bf16[16,48,128]{2,1,0:T(8,128)(2,1)}), bf16[16,48,128]{2,1,0:T(8,128)(2,1)S(1)}, u32[]{:S(2)}, u32[]{:S(2)}) async-start(bf16[16,48,128]{2,1,0:T(8,128)(2,1)} %get-tuple-element.17), calls=%async_computation | async-start | bytes 393216 | tf_op jit(solution)/shard_map/all_to_all | solution.py:353
  11.1 4.6 %collective-permute-start.3 = (bf16[256,128]{1,0:T(8,128)(2,1)S(1)}, bf16[256,128]{1,0:T(8,128)(2,1)S(1)}, u32[]{:S(2)}, u32[]{:S(2)}) collective-permute-start(bf16[256,128]{1,0:T(8,128)(2,1)S(1)} %get-tuple-element.16.slab_c), channel_id=1, source_target_pairs={{2,0},{3,1},{4,2},{5,3},{6,4},{7,5},{8,6},{9,7},{10,8},{11,9},{12,... | collective-permute-start | bytes 196616 | tf_op jit(solution)/shard_map/ppermute | solution.py:298
  16.2 1.0 %collective-permute-start = (bf16[256,128]{1,0:T(8,128)(2,1)S(1)}, bf16[256,128]{1,0:T(8,128)(2,1)S(1)}, u32[]{:S(2)}, u32[]{:S(2)}) collective-permute-start(bf16[256,128]{1,0:T(8,128)(2,1)S(1)} %get-tuple-element.16.slab_c), channel_id=1, source_target_pairs={{14,0},{15,1},{0,2},{1,3},{2,4},{3,5},{4,6},{5,7},{6,8},{7,9},{8,1... | collective-permute-start | bytes 196616 | tf_op jit(solution)/shard_map/ppermute | solution.py:298
  18.0 3.4 %copy-done.3 = bf16[32,8,128,128]{3,2,1,0:T(8,128)(2,1)S(1)} copy-done((bf16[32,8,128,128]{3,2,1,0:T(8,128)(2,1)S(1)}, bf16[32,8,128,128]{3,2,1,0:T(8,128)(2,1)}, u32[]{:S(2)}) %copy-start.3) | copy-done | bytes 8388632
  21.3 1.2 %copy-done.4 = f32[32,8,16,16]{0,3,2,1:T(8,128)S(1)} copy-done((f32[32,8,16,16]{0,3,2,1:T(8,128)S(1)}, f32[32,8,16,16]{0,3,2,1:T(8,128)}, u32[]{:S(2)}) %copy-start.4) | copy-done | bytes 262168
  23.5 3.8 %prepare.1 = (bf16[128,512]{1,0:T(8,128)(2,1)S(1)}, bf16[128,512]{1,0:T(8,128)(2,1)S(1)}, bf16[512,128]{1,0:T(8,128)(2,1)S(1)}, bf16[16,1024,256]{2,1,0:T(8,128)(2,1)S(1)}) custom-call(f32[8,16,16,32]{3,2,1,0:T(8,128)S(1)} %bitcast.10, bf16[512,128]{1,0:T(8,128)(2,1)S(1)} %bitcast.11, bf16[256,128,128]{2,1,0:T(8,128)(2,1)S(1)} %bitcast.9), custom_call_target="tpu_custom_call" | custom-call | tf_op jit(solution)/shard_map/prepare/pallas_call | solution.py:363
  27.3 3.3 %copy-done = bf16[16,1024,256]{2,1,0:T(8,128)(2,1)} copy-done((bf16[16,1024,256]{2,1,0:T(8,128)(2,1)}, bf16[16,1024,256]{2,1,0:T(8,128)(2,1)S(1)}, u32[]{:S(2)}) %copy-start) | copy-done | bytes 8388632
  30.6 3.4 %copy-done.1 = bf16[16,1024,256]{2,1,0:T(8,128)(2,1)S(1)} copy-done((bf16[16,1024,256]{2,1,0:T(8,128)(2,1)S(1)}, bf16[16,1024,256]{2,1,0:T(8,128)(2,1)}, u32[]{:S(2)}) %copy-start.1) | copy-done | bytes 8388632
  34.0 3.9 %operator_one.1 = (f32[256,128]{1,0:T(8,128)S(1)}, bf16[256,128]{1,0:T(8,128)(2,1)S(1)}, bf16[16,48,128]{2,1,0:T(8,128)(2,1)}) custom-call(f32[256,128]{1,0:T(8,128)S(1)} %get-tuple-element.15.b, bf16[256,128]{1,0:T(8,128)(2,1)S(1)} %collective-permute-done.slab_a, bf16[256,128]{1,0:T(8,128)(2,1)S(1)} %collective-permute-done.1.slab_b, ...), custom_call_target="tpu_custom_call" | custom-call | tf_op jit(solution)/shard_map/operator_one/pallas_call | solution.py:389
  37.9 5.5 %all-to-all-start.1 = ((bf16[16,48,128]{2,1,0:T(8,128)(2,1)}), bf16[16,48,128]{2,1,0:T(8,128)(2,1)S(1)}, u32[]{:S(2)}, u32[]{:S(2)}) async-start(bf16[16,48,128]{2,1,0:T(8,128)(2,1)} %get-tuple-element.25), calls=%async_computation.1 | async-start | bytes 393216 | tf_op jit(solution)/shard_map/all_to_all | solution.py:353
  43.4 4.6 %collective-permute-start.7 = (bf16[256,128]{1,0:T(8,128)(2,1)S(1)}, bf16[256,128]{1,0:T(8,128)(2,1)S(1)}, u32[]{:S(2)}, u32[]{:S(2)}) collective-permute-start(bf16[256,128]{1,0:T(8,128)(2,1)S(1)} %get-tuple-element.24.slab_c), channel_id=1, source_target_pairs={{2,0},{3,1},{4,2},{5,3},{6,4},{7,5},{8,6},{9,7},{10,8},{11,9},{12,... | collective-permute-start | bytes 196616 | tf_op jit(solution)/shard_map/ppermute | solution.py:298
  48.6 1.0 %collective-permute-start.4 = (bf16[256,128]{1,0:T(8,128)(2,1)S(1)}, bf16[256,128]{1,0:T(8,128)(2,1)S(1)}, u32[]{:S(2)}, u32[]{:S(2)}) collective-permute-start(bf16[256,128]{1,0:T(8,128)(2,1)S(1)} %get-tuple-element.24.slab_c), channel_id=1, source_target_pairs={{14,0},{15,1},{0,2},{1,3},{2,4},{3,5},{4,6},{5,7},{6,8},{7,9},{8,1... | collective-permute-start | bytes 196616 | tf_op jit(solution)/shard_map/ppermute | solution.py:298
  50.6 3.9 %collective-permute-done.5.slab_b = bf16[256,128]{1,0:T(8,128)(2,1)S(1)} collective-permute-done((bf16[256,128]{1,0:T(8,128)(2,1)S(1)}, bf16[256,128]{1,0:T(8,128)(2,1)S(1)}, u32[]{:S(2)}, u32[]{:S(2)}) %collective-permute-start.5) | collective-permute-done | bytes 65568 | tf_op jit(solution)/shard_map/ppermute | solution.py:298
  54.5 1.6 %collective-permute-done.4.slab_a = bf16[256,128]{1,0:T(8,128)(2,1)S(1)} collective-permute-done((bf16[256,128]{1,0:T(8,128)(2,1)S(1)}, bf16[256,128]{1,0:T(8,128)(2,1)S(1)}, u32[]{:S(2)}, u32[]{:S(2)}) %collective-permute-start.4) | collective-permute-done | bytes 65568 | tf_op jit(solution)/shard_map/ppermute | solution.py:298
  56.1 3.4 %copy-done.2 = bf16[16,1024,256]{2,1,0:T(8,128)(2,1)S(1)} copy-done((bf16[16,1024,256]{2,1,0:T(8,128)(2,1)S(1)}, bf16[16,1024,256]{2,1,0:T(8,128)(2,1)}, u32[]{:S(2)}) %copy-start.2) | copy-done | bytes 8388632
  59.5 3.1 %operator_two.1 = (f32[256,128]{1,0:T(8,128)S(1)}, f32[8,128]{1,0:T(8,128)S(1)}) custom-call(f32[256,128]{1,0:T(8,128)S(1)} %get-tuple-element.15.b, f32[256,128]{1,0:T(8,128)S(1)} %get-tuple-element.23.image, bf16[256,128]{1,0:T(8,128)(2,1)S(1)} %collective-permute-done.4.slab_a, bf16[256,128]{1,0:T(8,128)(2,1)S(1)} %collective-permute-done.5.slab_b, ...), custom_call_target="tpu_custom_call" | custom-call | tf_op jit(solution)/shard_map/operator_two/pallas_call | solution.py:399
  62.6 1.8 %collective-permute-start.9 = (f32[8,128]{1,0:T(8,128)S(1)}, f32[8,128]{1,0:T(8,128)S(1)}, u32[]{:S(2)}, u32[]{:S(2)}) collective-permute-start(f32[8,128]{1,0:T(8,128)S(1)} %get-tuple-element.27), channel_id=1, source_target_pairs={{0,2},{1,3},{2,0},{3,1},{4,6},{5,7},{6,4},{7,5},{8,10},{9,11},{10,... | collective-permute-start | bytes 12296 | tf_op jit(solution)/shard_map/ppermute | solution.py:315
  64.5 1.2 %collective-permute-done.10 = f32[8,128]{1,0:T(8,128)S(1)} collective-permute-done((f32[8,128]{1,0:T(8,128)S(1)}, f32[8,128]{1,0:T(8,128)S(1)}, u32[]{:S(2)}, u32[]{:S(2)}) %collective-permute-start.10) | collective-permute-done | bytes 4128 | tf_op jit(solution)/shard_map/ppermute | solution.py:315
  66.3 1.2 %collective-permute-start.13 = (f32[8,128]{1,0:T(8,128)S(1)}, f32[8,128]{1,0:T(8,128)S(1)}, u32[]{:S(2)}, u32[]{:S(2)}) collective-permute-start(f32[8,128]{1,0:T(8,128)S(1)} %add_add_fusion.rest_0_), channel_id=1, source_target_pairs={{0,12},{1,13},{2,14},{3,15},{4,8},{5,9},{6,10},{7,11},{8,4},{9,5},... | collective-permute-start | bytes 12296 | tf_op jit(solution)/shard_map/ppermute | solution.py:315
  67.5 3.3 %collective-permute-start.11 = (f32[8,128]{1,0:T(8,128)S(1)}, f32[8,128]{1,0:T(8,128)S(1)}, u32[]{:S(2)}, u32[]{:S(2)}) collective-permute-start(f32[8,128]{1,0:T(8,128)S(1)} %add_add_fusion.rest_0_), channel_id=1, source_target_pairs={{0,4},{1,5},{2,6},{3,7},{4,0},{5,1},{6,2},{7,3},{8,12},{9,13},{10,... | collective-permute-start | bytes 12296 | tf_op jit(solution)/shard_map/ppermute | solution.py:315
  70.8 1.0 %collective-permute-done.13.rest_3_ = f32[8,128]{1,0:T(8,128)S(1)} collective-permute-done((f32[8,128]{1,0:T(8,128)S(1)}, f32[8,128]{1,0:T(8,128)S(1)}, u32[]{:S(2)}, u32[]{:S(2)}) %collective-permute-start.13) | collective-permute-done | bytes 4128 | tf_op jit(solution)/shard_map/ppermute | solution.py:315
  72.4 1.2 %finish.1 = (f32[8,4096]{1,0:T(8,128)}, f32[8,4096]{1,0:T(8,128)}) custom-call(f32[256,128]{1,0:T(8,128)S(1)} %get-tuple-element.15.b, f32[256,128]{1,0:T(8,128)S(1)} %get-tuple-element.23.image, f32[256,128]{1,0:T(8,128)S(1)} %get-tuple-element.26.candidate, bf16[16,48,128]{2,1,0:T(8,128)(2,1)S(1)} %all-to-all-done.got.got0, ...), custom_call_target="tpu_custom_call" | custom-call | tf_op jit(solution)/shard_map/finish/pallas_call | solution.py:408
  (33 shorter events, 5.9 us)
Async XLA Ops:
  0.6 0.9 %copy-start.6 = (f32[8,4096]{1,0:T(8,128)S(1)}, f32[8,4096]{1,0:T(8,128)}, u32[]{:S(2)}) copy-start(f32[8,4096]{1,0:T(8,128)} %b_hbm.1) | copy-start | bytes 393220
  1.5 0.9 %copy-start.7 = (bf16[32,16,128]{2,1,0:T(8,128)(2,1)S(1)}, bf16[32,16,128]{2,1,0:T(8,128)(2,1)}, u32[]{:S(2)}) copy-start(bf16[32,16,128]{2,1,0:T(8,128)(2,1)} %param.12) | copy-start | bytes 393220
  2.4 28.2 %copy-start.8 = (s32[32,8]{0,1:T(8,128)S(1)}, s32[32,8]{0,1:T(8,128)}, u32[]{:S(2)}) copy-start(s32[32,8]{0,1:T(8,128)} %param.15) | copy-start | bytes 3076
  3.7 26.9 %all-to-all-start = ((bf16[16,48,128]{2,1,0:T(8,128)(2,1)}), bf16[16,48,128]{2,1,0:T(8,128)(2,1)S(1)}, u32[]{:S(2)}, u32[]{:S(2)}) async-start(bf16[16,48,128]{2,1,0:T(8,128)(2,1)} %get-tuple-element.17), calls=%async_computation | async-start | bytes 393216 | tf_op jit(solution)/shard_map/all_to_all | solution.py:353
  11.1 19.5 %collective-permute-start.3 = (bf16[256,128]{1,0:T(8,128)(2,1)S(1)}, bf16[256,128]{1,0:T(8,128)(2,1)S(1)}, u32[]{:S(2)}, u32[]{:S(2)}) collective-permute-start(bf16[256,128]{1,0:T(8,128)(2,1)S(1)} %get-tuple-element.16.slab_c), channel_id=1, source_target_pairs={{2,0},{3,1},{4,2},{5,3},{6,4},{7,5},{8,6},{9,7},{10,8},{11,9},{12,... | collective-permute-start | bytes 196616 | tf_op jit(solution)/shard_map/ppermute | solution.py:298
  15.7 14.9 %collective-permute-start.2 = (bf16[256,128]{1,0:T(8,128)(2,1)S(1)}, bf16[256,128]{1,0:T(8,128)(2,1)S(1)}, u32[]{:S(2)}, u32[]{:S(2)}) collective-permute-start(bf16[256,128]{1,0:T(8,128)(2,1)S(1)} %get-tuple-element.16.slab_c), channel_id=1, source_target_pairs={{1,0},{2,1},{3,2},{4,3},{5,4},{6,5},{7,6},{8,7},{9,8},{10,9},{11,1... | collective-permute-start | bytes 196616 | tf_op jit(solution)/shard_map/ppermute | solution.py:298
  15.8 14.8 %collective-permute-start.1 = (bf16[256,128]{1,0:T(8,128)(2,1)S(1)}, bf16[256,128]{1,0:T(8,128)(2,1)S(1)}, u32[]{:S(2)}, u32[]{:S(2)}) collective-permute-start(bf16[256,128]{1,0:T(8,128)(2,1)S(1)} %get-tuple-element.16.slab_c), channel_id=1, source_target_pairs={{15,0},{0,1},{1,2},{2,3},{3,4},{4,5},{5,6},{6,7},{7,8},{8,9},{9,10... | collective-permute-start | bytes 196616 | tf_op jit(solution)/shard_map/ppermute | solution.py:298
  16.2 14.4 %collective-permute-start = (bf16[256,128]{1,0:T(8,128)(2,1)S(1)}, bf16[256,128]{1,0:T(8,128)(2,1)S(1)}, u32[]{:S(2)}, u32[]{:S(2)}) collective-permute-start(bf16[256,128]{1,0:T(8,128)(2,1)S(1)} %get-tuple-element.16.slab_c), channel_id=1, source_target_pairs={{14,0},{15,1},{0,2},{1,3},{2,4},{3,5},{4,6},{5,7},{6,8},{7,9},{8,1... | collective-permute-start | bytes 196616 | tf_op jit(solution)/shard_map/ppermute | solution.py:298
  18.0 3.4 %copy-start.3 = (bf16[32,8,128,128]{3,2,1,0:T(8,128)(2,1)S(1)}, bf16[32,8,128,128]{3,2,1,0:T(8,128)(2,1)}, u32[]{:S(2)}) copy-start(bf16[32,8,128,128]{3,2,1,0:T(8,128)(2,1)} %param.9) | copy-start | bytes 25165828
  21.3 1.2 %copy-start.4 = (f32[32,8,16,16]{0,3,2,1:T(8,128)S(1)}, f32[32,8,16,16]{0,3,2,1:T(8,128)}, u32[]{:S(2)}) copy-start(f32[32,8,16,16]{0,3,2,1:T(8,128)} %param.14) | copy-start | bytes 786436
  27.3 3.3 %copy-start = (bf16[16,1024,256]{2,1,0:T(8,128)(2,1)}, bf16[16,1024,256]{2,1,0:T(8,128)(2,1)S(1)}, u32[]{:S(2)}) copy-start(bf16[16,1024,256]{2,1,0:T(8,128)(2,1)S(1)} %get-tuple-element.18.turned) | copy-start | bytes 25165828
  30.6 3.4 %copy-start.1 = (bf16[16,1024,256]{2,1,0:T(8,128)(2,1)S(1)}, bf16[16,1024,256]{2,1,0:T(8,128)(2,1)}, u32[]{:S(2)}) copy-start(bf16[16,1024,256]{2,1,0:T(8,128)(2,1)} %copy-done) | copy-start | bytes 25165828
  37.9 18.2 %all-to-all-start.1 = ((bf16[16,48,128]{2,1,0:T(8,128)(2,1)}), bf16[16,48,128]{2,1,0:T(8,128)(2,1)S(1)}, u32[]{:S(2)}, u32[]{:S(2)}) async-start(bf16[16,48,128]{2,1,0:T(8,128)(2,1)} %get-tuple-element.25), calls=%async_computation.1 | async-start | bytes 393216 | tf_op jit(solution)/shard_map/all_to_all | solution.py:353
  43.4 6.5 %collective-permute-start.7 = (bf16[256,128]{1,0:T(8,128)(2,1)S(1)}, bf16[256,128]{1,0:T(8,128)(2,1)S(1)}, u32[]{:S(2)}, u32[]{:S(2)}) collective-permute-start(bf16[256,128]{1,0:T(8,128)(2,1)S(1)} %get-tuple-element.24.slab_c), channel_id=1, source_target_pairs={{2,0},{3,1},{4,2},{5,3},{6,4},{7,5},{8,6},{9,7},{10,8},{11,9},{12,... | collective-permute-start | bytes 196616 | tf_op jit(solution)/shard_map/ppermute | solution.py:298
  48.1 2.5 %collective-permute-start.6 = (bf16[256,128]{1,0:T(8,128)(2,1)S(1)}, bf16[256,128]{1,0:T(8,128)(2,1)S(1)}, u32[]{:S(2)}, u32[]{:S(2)}) collective-permute-start(bf16[256,128]{1,0:T(8,128)(2,1)S(1)} %get-tuple-element.24.slab_c), channel_id=1, source_target_pairs={{1,0},{2,1},{3,2},{4,3},{5,4},{6,5},{7,6},{8,7},{9,8},{10,9},{11,1... | collective-permute-start | bytes 196616 | tf_op jit(solution)/shard_map/ppermute | solution.py:298
  48.1 6.4 %collective-permute-start.5 = (bf16[256,128]{1,0:T(8,128)(2,1)S(1)}, bf16[256,128]{1,0:T(8,128)(2,1)S(1)}, u32[]{:S(2)}, u32[]{:S(2)}) collective-permute-start(bf16[256,128]{1,0:T(8,128)(2,1)S(1)} %get-tuple-element.24.slab_c), channel_id=1, source_target_pairs={{15,0},{0,1},{1,2},{2,3},{3,4},{4,5},{5,6},{6,7},{7,8},{8,9},{9,10... | collective-permute-start | bytes 196616 | tf_op jit(solution)/shard_map/ppermute | solution.py:298
  48.6 7.5 %collective-permute-start.4 = (bf16[256,128]{1,0:T(8,128)(2,1)S(1)}, bf16[256,128]{1,0:T(8,128)(2,1)S(1)}, u32[]{:S(2)}, u32[]{:S(2)}) collective-permute-start(bf16[256,128]{1,0:T(8,128)(2,1)S(1)} %get-tuple-element.24.slab_c), channel_id=1, source_target_pairs={{14,0},{15,1},{0,2},{1,3},{2,4},{3,5},{4,6},{5,7},{6,8},{7,9},{8,1... | collective-permute-start | bytes 196616 | tf_op jit(solution)/shard_map/ppermute | solution.py:298
  56.1 3.4 %copy-start.2 = (bf16[16,1024,256]{2,1,0:T(8,128)(2,1)S(1)}, bf16[16,1024,256]{2,1,0:T(8,128)(2,1)}, u32[]{:S(2)}) copy-start(bf16[16,1024,256]{2,1,0:T(8,128)(2,1)} %copy-done) | copy-start | bytes 25165828
  62.6 3.0 %collective-permute-start.10 = (f32[8,128]{1,0:T(8,128)S(1)}, f32[8,128]{1,0:T(8,128)S(1)}, u32[]{:S(2)}, u32[]{:S(2)}) collective-permute-start(f32[8,128]{1,0:T(8,128)S(1)} %get-tuple-element.27), channel_id=1, source_target_pairs={{0,3},{1,2},{2,1},{3,0},{4,7},{5,6},{6,5},{7,4},{8,11},{9,10},{10,... | collective-permute-start | bytes 12296 | tf_op jit(solution)/shard_map/ppermute | solution.py:315
  62.6 3.7 %collective-permute-start.9 = (f32[8,128]{1,0:T(8,128)S(1)}, f32[8,128]{1,0:T(8,128)S(1)}, u32[]{:S(2)}, u32[]{:S(2)}) collective-permute-start(f32[8,128]{1,0:T(8,128)S(1)} %get-tuple-element.27), channel_id=1, source_target_pairs={{0,2},{1,3},{2,0},{3,1},{4,6},{5,7},{6,4},{7,5},{8,10},{9,11},{10,... | collective-permute-start | bytes 12296 | tf_op jit(solution)/shard_map/ppermute | solution.py:315
  64.4 1.9 %collective-permute-start.8 = (f32[8,128]{1,0:T(8,128)S(1)}, f32[8,128]{1,0:T(8,128)S(1)}, u32[]{:S(2)}, u32[]{:S(2)}) collective-permute-start(f32[8,128]{1,0:T(8,128)S(1)} %get-tuple-element.27), channel_id=1, source_target_pairs={{0,1},{1,0},{2,3},{3,2},{4,5},{5,4},{6,7},{7,6},{8,9},{9,8},{10,11... | collective-permute-start | bytes 12296 | tf_op jit(solution)/shard_map/ppermute | solution.py:315
  66.3 5.5 %collective-permute-start.13 = (f32[8,128]{1,0:T(8,128)S(1)}, f32[8,128]{1,0:T(8,128)S(1)}, u32[]{:S(2)}, u32[]{:S(2)}) collective-permute-start(f32[8,128]{1,0:T(8,128)S(1)} %add_add_fusion.rest_0_), channel_id=1, source_target_pairs={{0,12},{1,13},{2,14},{3,15},{4,8},{5,9},{6,10},{7,11},{8,4},{9,5},... | collective-permute-start | bytes 12296 | tf_op jit(solution)/shard_map/ppermute | solution.py:315
  67.5 4.5 %collective-permute-start.12 = (f32[8,128]{1,0:T(8,128)S(1)}, f32[8,128]{1,0:T(8,128)S(1)}, u32[]{:S(2)}, u32[]{:S(2)}) collective-permute-start(f32[8,128]{1,0:T(8,128)S(1)} %add_add_fusion.rest_0_), channel_id=1, source_target_pairs={{0,8},{1,9},{2,10},{3,11},{4,12},{5,13},{6,14},{7,15},{8,0},{9,1},... | collective-permute-start | bytes 12296 | tf_op jit(solution)/shard_map/ppermute | solution.py:315
  67.5 4.8 %collective-permute-start.11 = (f32[8,128]{1,0:T(8,128)S(1)}, f32[8,128]{1,0:T(8,128)S(1)}, u32[]{:S(2)}, u32[]{:S(2)}) collective-permute-start(f32[8,128]{1,0:T(8,128)S(1)} %add_add_fusion.rest_0_), channel_id=1, source_target_pairs={{0,4},{1,5},{2,6},{3,7},{4,0},{5,1},{6,2},{7,3},{8,12},{9,13},{10,... | collective-permute-start | bytes 12296 | tf_op jit(solution)/shard_map/ppermute | solution.py:315
  (1 other events, 0.9 us)

commit v4 on v3

--- a/solution.py
+++ b/solution.py
@@ -69,29 +69,33 @@
     return tile
 
 
-def write_payload(payload, tiles, basis, sums, per_group):
-    groups = len(tiles) // per_group
-    parts = [compress(tiles[g * per_group : (g + 1) * per_group], basis, g) for g in range(groups)]
-    block = jnp.concatenate([jnp.concatenate(parts, axis=0).astype(bf16), sums_tile(sums)], axis=0)
-    for device in range(payload.shape[0]):
-        payload[device] = block
-
-
-def start_kernel(per_group, b_hbm, basis_hbm, field, basis, lowered, payload, b, sems):
+def start_kernel(b_hbm, basis_hbm, field, basis, lowered, b, sems):
     copies = [
         pltpu.make_async_copy(b_hbm, b, sems.at[0]),
         pltpu.make_async_copy(basis_hbm, basis, sems.at[1]),
     ]
     for copy in copies:
         copy.start()
-    for copy in copies:
-        copy.wait()
+    copies[0].wait()
     clusters = b.shape[1] // LANES
-    tiles = [b[:, j * LANES : (j + 1) * LANES] for j in range(clusters)]
-    field[...] = jnp.concatenate(tiles, axis=0)
-    lowered[...] = jnp.concatenate(tiles, axis=0).astype(bf16)
-    square = sum(t * t for t in tiles)
-    write_payload(payload, tiles, basis, [square], per_group)
+    tiles = jnp.concatenate([b[:, j * LANES : (j + 1) * LANES] for j in range(clusters)], axis=0)
+    field[...] = tiles
+    lowered[...] = tiles.astype(bf16)
+    copies[1].wait()
+
+
+def compress_kernel(per_group, pairs, *refs):
+    *fields, basis, payload = refs
+    clusters = fields[0].shape[0] // R
+    tiles = [rows_of(fields[-1], j) for j in range(clusters)]
+    sums = [
+        sum(rows_of(fields[f], j) * rows_of(fields[g], j) for j in range(clusters)) for f, g in pairs
+    ]
+    groups = clusters // per_group
+    parts = [compress(tiles[g * per_group : (g + 1) * per_group], basis, g) for g in range(groups)]
+    block = jnp.concatenate([jnp.concatenate(parts, axis=0).astype(bf16), sums_tile(sums)], axis=0)
+    for device in range(payload.shape[0]):
+        payload[device] = block
 
 
 def prepare_kernel(
@@ -181,7 +185,8 @@
     )
 
 
-def near_field(slabs, placed, turned, window, near):
+def near_kernel(*refs):
+    *slabs, placed, turned, near, window = refs
     rows = slabs[0].shape[0]
     for at, slab in enumerate(slabs):
         window[pl.ds(at * rows, rows), :] = slab[...].astype(f32)
@@ -207,46 +212,35 @@
     return jnp.sqrt(whole), square / whole
 
 
-def first_kernel(
-    per_group, unknowns, b, slab_a, slab_b, slab_c, slab_d, slab_e, got, placed, far_cols, turned,
-    basis, high, low, target, image, lowered, payload, window, table, near, far,
-):
-    slots, clusters = placed.shape
+def first_kernel(per_group, unknowns, b, near, got, far_cols, high, low, target, image, lowered, table, far):
+    clusters = far_cols.shape[1]
     head = clusters // per_group * R
     far_field(got, far_cols, high, low, target, table, clusters, LANES // per_group, far)
-    near_field((slab_a, slab_b, slab_c, slab_d, slab_e), placed, turned, window, near)
     start_norm, _ = norm_parts(read_sums(got, head, 1, unknowns))
     scale = 1.0 / start_norm
-    cross = jnp.zeros((R, LANES), f32)
-    square = jnp.zeros((R, LANES), f32)
-    tiles = []
-    for j in range(clusters):
-        field = rows_of(b, j)
-        made = (0.5 * field + (rows_of(near, j) + rows_of(far, j))) * scale
-        cross = cross + (field * scale) * made
-        square = square + made * made
-        image[pl.ds(j * R, R), :] = made
-        tiles.append(made)
-    lowered[...] = jnp.concatenate(tiles, axis=0).astype(bf16)
-    write_payload(payload, tiles, basis, [cross, square], per_group)
+    for j in range(0, clusters, 2):
+        made = [
+            (0.5 * rows_of(b, i) + (rows_of(near, i) + rows_of(far, i))) * scale for i in (j, j + 1)
+        ]
+        both = jnp.concatenate(made, axis=0)
+        image[pl.ds(j * R, 2 * R), :] = both
+        lowered[pl.ds(j * R, 2 * R), :] = both.astype(bf16)
 
 
 def arnoldi_one(sums0, sums1):
-    _, v11 = norm_parts(sums0)
-    h11 = sums1[0]
+    start_norm, v11 = norm_parts(sums0)
+    h11 = sums1[0] * (1.0 / start_norm)
     uu = jnp.maximum(sums1[1] - 2.0 * h11 * h11 + h11 * h11 * v11, 0.0)
     h21 = jnp.sqrt(uu + epsilon)
     return h11, h21, v11, uu / (uu + epsilon), h11 * (1.0 - v11) / h21
 
 
 def second_kernel(
-    per_group, unknowns, b, image, slab_a, slab_b, slab_c, slab_d, slab_e, got0, got, placed, far_cols,
-    turned, high, low, target, candidate, sums_out, window, table, near, far,
+    per_group, unknowns, b, image, near, got0, got, far_cols, high, low, target, candidate, sums_out, table, far,
 ):
-    slots, clusters = placed.shape
+    clusters = far_cols.shape[1]
     head = clusters // per_group * R
     far_field(got, far_cols, high, low, target, table, clusters, LANES // per_group, far)
-    near_field((slab_a, slab_b, slab_c, slab_d, slab_e), placed, turned, window, near)
     sums0 = read_sums(got0, head, 1, unknowns)
     scale = 1.0 / norm_parts(sums0)[0]
     h11, h21, _, _, _ = arnoldi_one(sums0, read_sums(got, head, 2, unknowns))
@@ -263,17 +257,17 @@
     tile = jnp.zeros((R, LANES), f32)
     for t, partial in enumerate(sums):
         tile = jnp.where(lane == t, jnp.sum(partial, axis=1, keepdims=True), tile)
-    sums_out[...] = tile
-
-
-def finish_kernel(per_group, unknowns, b, image, candidate, got0, got1, *rest):
-    *got2, solution_out, next_out = rest
+    for device in range(sums_out.shape[0]):
+        sums_out[device] = tile
+
+
+def finish_kernel(per_group, unknowns, b, image, candidate, got0, got1, got2, solution_out, next_out):
     clusters = b.shape[0] // R
     head = clusters // per_group * R
     sums0 = read_sums(got0, head, 1, unknowns)
     start_norm, _ = norm_parts(sums0)
     h11, h21, v11, v22, v12 = arnoldi_one(sums0, read_sums(got1, head, 2, unknowns))
-    total = sum(part[...] for part in got2)
+    total = sum(got2[device] for device in range(got2.shape[0]))
     h12, h22, ww = [total[:, t : t + 1] * (1.0 / unknowns) for t in range(3)]
     uu = ww - 2.0 * (h12 * h12 + h22 * h22) + h12 * h12 * v11 + h22 * h22 * v22 + 2.0 * h12 * h22 * v12
     h32 = jnp.sqrt(jnp.maximum(uu, 0.0) + epsilon)
@@ -293,28 +287,47 @@
         next_out[:, span] = (rows_of(candidate, j) - h12 * first - h22 * second) * last
 
 
-def shifted(block, distance):
-    size = lax.axis_size("rows")
-    return lax.ppermute(block, "rows", [((i - distance) % size, i) for i in range(size)])
-
-
-def stages():
-    rest, stride, found = lax.axis_size("rows"), 1, []
-    while rest > 1:
-        length = 4 if rest % 4 == 0 else 2
-        found.append((stride, length))
-        stride, rest = stride * length, rest // length
-    return found
-
-
-def digit_parts(block, stride, length):
-    size = lax.axis_size("rows")
-    parts = [block]
-    for step in range(1, length):
-        parts.append(
-            lax.ppermute(block, "rows", [(i, i ^ (step * stride)) for i in range(size)])
-        )
-    return parts
+def swapped(block, partner):
+    return lax.ppermute(block, "rows", [(i, partner(i)) for i in range(lax.axis_size("rows"))])
+
+
+def core_mate(i):
+    return i ^ 1
+
+
+def even_mate(i):
+    return i ^ 2
+
+
+def odd_mate(i):
+    chip = i // 2
+    other = chip + 1 if chip % 2 else chip - 1
+    return 2 * (other % (lax.axis_size("rows") // 2)) + i % 2
+
+
+def slabs_of(block):
+    odd = swapped(block, odd_mate)
+    even = swapped(block, even_mate)
+    mate = swapped(block, core_mate)
+    return [block, mate, even, odd, swapped(even, core_mate), swapped(odd, core_mate)]
+
+
+def window_place(distance, clusters):
+    me = lax.axis_index("rows")
+    core, chip = me % 2, me // 2
+    before, after = 3 - chip % 2, 2 + chip % 2
+    slot = [
+        before,
+        jnp.where(core == 0, before + 2, 1),
+        0,
+        jnp.where(core == 0, 1, after + 2),
+        after,
+    ]
+    slab = distance // clusters
+    chosen = jnp.zeros_like(distance)
+    for s, value in enumerate(slot):
+        chosen = jnp.where(slab == s, value, chosen)
+    return chosen * clusters + distance % clusters
 
 
 def on_device(
@@ -336,28 +349,31 @@
     def scratch(*dims, dtype=f32):
         return pltpu.VMEM(dims, dtype)
 
-    basis = basis_in.reshape(clusters * rank, LANES)
-    blocks = near_blocks.reshape(clusters * slots, LANES, LANES)
-    field, basis, lowered, payload = pl.pallas_call(
-        functools.partial(start_kernel, per_group),
-        out_shape=(
-            shape(rows, LANES), shape(clusters * rank, LANES, dtype=bf16), shape(rows, LANES, dtype=bf16),
-            shape(size, head + TAIL, LANES, dtype=bf16),
-        ),
-        in_specs=[HBM] * 2, out_specs=[VMEM] * 4,
-        scratch_shapes=[scratch(R, width), pltpu.SemaphoreType.DMA((2,))],
-        compiler_params=PARAMS, name="start",
-    )(right_sides, basis)
+    def in_hbm(array):
+        return pltpu.with_memory_space_constraint(array, pltpu.HBM)
+
+    def call(kernel, name, out, ins, *args, scratch_shapes=()):
+        return pl.pallas_call(
+            kernel, out_shape=out, in_specs=ins, out_specs=jax.tree.map(lambda _: VMEM, out),
+            scratch_shapes=scratch_shapes, compiler_params=PARAMS, name=name,
+        )(*args)
 
     def exchange(block):
         return lax.all_to_all(block, "rows", 0, 0)
 
-    def slabs_of(block):
-        got = {d: shifted(block, d) for d in (2, 1, -1, -2)}
-        return [got[2], got[1], block, got[-1], got[-2]]
-
+    field, basis, lowered = call(
+        start_kernel, "start",
+        (shape(rows, LANES), shape(clusters * rank, LANES, dtype=bf16), shape(rows, LANES, dtype=bf16)),
+        [HBM] * 2, in_hbm(right_sides), in_hbm(basis_in.reshape(clusters * rank, LANES)),
+        scratch_shapes=[scratch(R, width), pltpu.SemaphoreType.DMA((2,))],
+    )
+    slabs = slabs_of(lowered)
+    payload_shape = shape(size, head + TAIL, LANES, dtype=bf16)
+    payload = call(
+        functools.partial(compress_kernel, per_group, [(0, 0)]), "compress_one", payload_shape,
+        [VMEM] * 2, field, basis,
+    )
     got0 = exchange(payload)
-    slabs = slabs_of(lowered)
 
     turned_shape = (clusters // 2, slots * LANES, 2 * LANES)
     high, low, target, turned = pl.pallas_call(
@@ -366,7 +382,7 @@
             shape(slots * rank, rank * clusters, dtype=bf16),
             shape(slots * rank, rank * clusters, dtype=bf16),
             shape(rank * clusters, LANES, dtype=bf16),
-            shape(*turned_shape, dtype=bf16),
+            pltpu.VMEM(turned_shape, bf16),
         ),
         in_specs=[HBM] * 3, out_specs=[VMEM] * 4,
         scratch_shapes=[
@@ -375,41 +391,49 @@
             pltpu.SemaphoreType.DMA((8,)), pltpu.SemaphoreType.DMA((2,)),
         ],
         compiler_params=PARAMS, name="prepare",
-    )(jnp.transpose(coupling, (1, 2, 3, 0)), target_basis.reshape(clusters * rank, LANES), blocks)
+    )(
+        in_hbm(jnp.transpose(coupling, (1, 2, 3, 0))),
+        in_hbm(target_basis.reshape(clusters * rank, LANES)),
+        in_hbm(near_blocks.reshape(clusters * slots, LANES, LANES)),
+    )
+    turned = pltpu.with_memory_space_constraint(turned, pltpu.VMEM)
     reach = 2 * clusters
     start = lax.axis_index("rows") * clusters
-    placed = (near_cols.T - start + reach) % every
+    distance = (near_cols.T - start + reach) % every
     live = jnp.arange(slots, dtype=jnp.int32)[:, None] < near_counts[None, :]
-    placed = jnp.where(live, placed, 5 * clusters).astype(jnp.int32)
+    placed = jnp.where(live, window_place(distance, clusters), len(slabs) * clusters).astype(jnp.int32)
     far_index = far_cols.T
 
-    kept = [
-        scratch(5 * rows + R, LANES), scratch(size * head, LANES), scratch(rows, LANES), scratch(rows, LANES),
-    ]
-    image, lowered, payload = pl.pallas_call(
-        functools.partial(first_kernel, per_group, unknowns),
-        out_shape=(
-            shape(rows, LANES), shape(rows, LANES, dtype=bf16), shape(size, head + TAIL, LANES, dtype=bf16),
-        ),
-        in_specs=[VMEM] * 7 + [SMEM] * 2 + [VMEM] * 5,
-        out_specs=[VMEM] * 3, scratch_shapes=kept, compiler_params=PARAMS, name="operator_one",
-    )(field, *slabs, got0, placed, far_index, turned, basis, high, low, target)
+    def near_of(slabs):
+        return call(
+            near_kernel, "near", shape(rows, LANES), [VMEM] * len(slabs) + [SMEM, VMEM], *slabs, placed, turned,
+            scratch_shapes=[scratch(len(slabs) * rows + R, LANES)],
+        )
+
+    kept = [scratch(size * head, LANES), scratch(rows, LANES)]
+    near = near_of(slabs)
+    image, lowered = call(
+        functools.partial(first_kernel, per_group, unknowns), "far_one",
+        (shape(rows, LANES), shape(rows, LANES, dtype=bf16)), [VMEM] * 3 + [SMEM] + [VMEM] * 3,
+        field, near, got0, far_index, high, low, target, scratch_shapes=kept,
+    )
+    slabs = slabs_of(lowered)
+    payload = call(
+        functools.partial(compress_kernel, per_group, [(0, 1), (1, 1)]), "compress_two", payload_shape,
+        [VMEM] * 3, field, image, basis,
+    )
     got1 = exchange(payload)
-    slabs = slabs_of(lowered)
-    candidate, sums = pl.pallas_call(
-        functools.partial(second_kernel, per_group, unknowns),
-        out_shape=(shape(rows, LANES), shape(R, LANES)),
-        in_specs=[VMEM] * 9 + [SMEM] * 2 + [VMEM] * 4,
-        out_specs=[VMEM] * 2, scratch_shapes=kept, compiler_params=PARAMS, name="operator_two",
-    )(field, image, *slabs, got0, got1, placed, far_index, turned, high, low, target)
-    parts = [sums]
-    for stride, length in stages():
-        parts = digit_parts(sum(parts), stride, length)
-    return pl.pallas_call(
-        functools.partial(finish_kernel, per_group, unknowns),
-        out_shape=(shape(R, width), shape(R, width)),
-        in_specs=[VMEM] * (5 + len(parts)), out_specs=[VMEM] * 2, compiler_params=PARAMS, name="finish",
-    )(field, image, candidate, got0, got1, *parts)
+    near = near_of(slabs)
+    candidate, sums = call(
+        functools.partial(second_kernel, per_group, unknowns), "far_two",
+        (shape(rows, LANES), shape(size, R, LANES)), [VMEM] * 5 + [SMEM] + [VMEM] * 3,
+        field, image, near, got0, got1, far_index, high, low, target, scratch_shapes=kept,
+    )
+    got2 = exchange(sums)
+    return call(
+        functools.partial(finish_kernel, per_group, unknowns), "finish", (shape(R, width), shape(R, width)),
+        [VMEM] * 6, field, image, candidate, got0, got1, got2,
+    )
 
 
 def solution(mesh):

time: 74.1 us -> 69.3 us (0.935)
  local copies, waits for them, and re-layouts: 17.3 us -> 6.62 us
  starting transfers between devices: 31.6 us -> 21.3 us
  blocking collectives: 0 us -> 9.77 us
  Pallas kernels: 13.3 us -> 18.1 us
  waiting for transfers between devices: 9.92 us -> 11.7 us
    unnamed x18 -> x6, local copies, waits for them, and re-layouts: 17.3 us -> 6.62 us
    all_to_all x0 -> x1, blocking collectives: none -> 9.77 us  [exchange(): return lax.all_to_all(block, 'rows', 0, 0)]
    ppermute x14 -> x10, starting transfers between devices: 18.6 us -> 10.3 us  [swapped(): lax.ppermute(block, 'rows', [(i, partner(i)) for i in range(lax.axis_size...]
    pallas_call x1, Pallas kernels: 3.83 us -> 6.41 us  [on_device(): pl.pallas_call(prepare_kernel, out_shape=(shape(slots * rank, rank * clus...]
    pallas_call x4 -> x8, Pallas kernels: 9.45 us -> 11.7 us  [call(): pl.pallas_call(kernel, out_shape=out, in_specs=ins, out_specs=jax.tree.ma...]
    all_to_all x2, starting transfers between devices: 12.9 us -> 10.9 us  [exchange(): return lax.all_to_all(block, 'rows', 0, 0)]
    ppermute x14 -> x10, waiting for transfers between devices: 9.92 us -> 11.7 us  [swapped(): lax.ppermute(block, 'rows', [(i, partner(i)) for i in range(lax.axis_size...]
  transfers between devices with their start and end apart: 16 -> 12, of which waited for: 9 -> 5; matrix products, arithmetic and copies ran while one was open for 1% -> 1% of each run, Pallas kernels for 5% -> 15%
where the time goes in v4:
time: 69.3 us; the launch traced here: 68.9 us
  starting transfers between devices  21.3 us (31%)
  Pallas kernels  18.1 us (26%)
  waiting for transfers between devices  11.7 us (17%)
  blocking collectives  9.77 us (14%)
  local copies, waits for them, and re-layouts  6.62 us (10%)
  between operations  0.72 us (1%)
  other arithmetic  0.71 us (1%)
    ppermute x10, waiting for transfers between devices, swapped(): lax.ppermute(block, 'rows', [(i, partner(i)) for i in range(lax.axis_size...  11.7 us
    pallas_call x8, Pallas kernels, call(): pl.pallas_call(kernel, out_shape=out, in_specs=ins, out_specs=jax.tree.ma...  11.7 us
    all_to_all x2, starting transfers between devices, exchange(): return lax.all_to_all(block, 'rows', 0, 0)  10.9 us
    ppermute x10, starting transfers between devices, swapped(): lax.ppermute(block, 'rows', [(i, partner(i)) for i in range(lax.axis_size...  10.3 us
    all_to_all x1, blocking collectives, exchange(): return lax.all_to_all(block, 'rows', 0, 0)  9.77 us
    unnamed x6, local copies, waits for them, and re-layouts  6.62 us
    pallas_call x1, Pallas kernels, on_device(): pl.pallas_call(prepare_kernel, out_shape=(shape(slots * rank, rank * clus...  6.41 us
  transfers between devices with their start and end apart: 12, of which 5 were waited for; matrix products, arithmetic and copies ran while one was open for 1% of the time, Pallas kernels for 15%

profile of v4, /device:TPU:0, one launch (start us, length us, event | category | flops | bytes accessed | tf_op | source)
XLA Modules:
  0.0 68.9 jit_solution(18314488963262798274)
XLA Ops:
  0.6 1.0 %start.1 = (f32[256,128]{1,0:T(8,128)S(1)}, bf16[512,128]{1,0:T(8,128)(2,1)S(1)}, bf16[256,128]{1,0:T(8,128)(2,1)S(1)}) custom-call(f32[8,4096]{1,0:T(8,128)} %b_hbm.1, bf16[512,128]{1,0:T(8,128)(2,1)} %bitcast.14), custom_call_target="tpu_custom_call" | custom-call | tf_op jit(solution)/shard_map/start/pallas_call | solution.py:356
  1.6 0.9 %compress_one.1 = bf16[16,48,128]{2,1,0:T(8,128)(2,1)} custom-call(f32[256,128]{1,0:T(8,128)S(1)} %get-tuple-element.13.refs_0_.b, bf16[512,128]{1,0:T(8,128)(2,1)S(1)} %get-tuple-element.16.refs_1_.refs_2_), custom_call_target="tpu_custom_call" | custom-call | tf_op jit(solution)/shard_map/compress_one/pallas_call | solution.py:356
  2.5 7.4 %all-to-all-start = ((bf16[16,48,128]{2,1,0:T(8,128)(2,1)}), bf16[16,48,128]{2,1,0:T(8,128)(2,1)S(1)}, u32[]{:S(2)}, u32[]{:S(2)}) async-start(bf16[16,48,128]{2,1,0:T(8,128)(2,1)} %compress_one.1), calls=%async_computation | async-start | bytes 393216 | tf_op jit(solution)/shard_map/all_to_all | solution.py:362
  9.9 1.9 %collective-permute-start.1 = (bf16[256,128]{1,0:T(8,128)(2,1)S(1)}, bf16[256,128]{1,0:T(8,128)(2,1)S(1)}, u32[]{:S(2)}, u32[]{:S(2)}) collective-permute-start(bf16[256,128]{1,0:T(8,128)(2,1)S(1)} %get-tuple-element.14.refs_0_), channel_id=1, source_target_pairs={{0,2},{1,3},{2,0},{3,1},{4,6},{5,7},{6,4},{7,5},{8,10},{9,11},{10,... | collective-permute-start | bytes 196616 | tf_op jit(solution)/shard_map/ppermute | solution.py:291
  11.8 3.3 %collective-permute-start.2 = (bf16[256,128]{1,0:T(8,128)(2,1)S(1)}, bf16[256,128]{1,0:T(8,128)(2,1)S(1)}, u32[]{:S(2)}, u32[]{:S(2)}) collective-permute-start(bf16[256,128]{1,0:T(8,128)(2,1)S(1)} %get-tuple-element.14.refs_0_), channel_id=1, source_target_pairs={{0,14},{1,15},{2,4},{3,5},{4,2},{5,3},{6,8},{7,9},{8,6},{9,7},{10,... | collective-permute-start | bytes 196616 | tf_op jit(solution)/shard_map/ppermute | solution.py:291
  15.1 0.8 %collective-permute-done.1.refs_2_ = bf16[256,128]{1,0:T(8,128)(2,1)S(1)} collective-permute-done((bf16[256,128]{1,0:T(8,128)(2,1)S(1)}, bf16[256,128]{1,0:T(8,128)(2,1)S(1)}, u32[]{:S(2)}, u32[]{:S(2)}) %collective-permute-start.1) | collective-permute-done | bytes 65568 | tf_op jit(solution)/shard_map/ppermute | solution.py:291
  15.9 4.4 %collective-permute-done.2.refs_3_ = bf16[256,128]{1,0:T(8,128)(2,1)S(1)} collective-permute-done((bf16[256,128]{1,0:T(8,128)(2,1)S(1)}, bf16[256,128]{1,0:T(8,128)(2,1)S(1)}, u32[]{:S(2)}, u32[]{:S(2)}) %collective-permute-start.2) | collective-permute-done | bytes 65568 | tf_op jit(solution)/shard_map/ppermute | solution.py:291
  20.3 0.7 %fusion.2.refs_6_ = s32[8,32]{1,0:T(8,128)S(1)} fusion(s32[32,8]{0,1:T(8,128)} %param.10, s32[]{:T(128)S(6)} %sub.24, s32[]{:T(128)S(6)} %select_n.67, s32[]{:T(128)S(6)} %select_n.66, s32[]{:T(128)S(6)} %add.49, s32[]{:T(128)S(6)} %mul.7, s32[32]{0:T(128)} %param.11), kind=kLoop, calls=%fused_computation.10 | loop fusion | flops 11776 | bytes 2196 | tf_op jit(solution)/shard_map/jit(_where)/select_n | solution.py:404
  21.1 6.4 %prepare.1 = (bf16[128,512]{1,0:T(8,128)(2,1)S(1)}, bf16[128,512]{1,0:T(8,128)(2,1)S(1)}, bf16[512,128]{1,0:T(8,128)(2,1)S(1)}, bf16[16,1024,256]{2,1,0:T(8,128)(2,1)S(1)}) custom-call(f32[8,16,16,32]{3,2,1,0:T(8,128)} %bitcast.12, bf16[512,128]{1,0:T(8,128)(2,1)} %bitcast.13, bf16[256,128,128]{2,1,0:T(8,128)(2,1)} %bitcast.11), custom_call_target="tpu_custom_call" | custom-call | tf_op jit(solution)/shard_map/prepare/pallas_call | solution.py:379
  27.5 1.9 %near.2 = f32[256,128]{1,0:T(8,128)S(1)} custom-call(bf16[256,128]{1,0:T(8,128)(2,1)S(1)} %get-tuple-element.14.refs_0_, bf16[256,128]{1,0:T(8,128)(2,1)S(1)} %collective-permute-done.refs_1_, bf16[256,128]{1,0:T(8,128)(2,1)S(1)} %collective-permute-done.1.refs_2_, bf16[256,128]{1,0:T(8,128)(2,1)S(1)} %collective-permute-done.2.refs_3_, ...), custom_call_target="tpu_custom_call" | custom-call | tf_op jit(solution)/shard_map/near/pallas_call | solution.py:356
  29.4 3.2 %copy-done = bf16[16,1024,256]{2,1,0:T(8,128)(2,1)} copy-done((bf16[16,1024,256]{2,1,0:T(8,128)(2,1)}, bf16[16,1024,256]{2,1,0:T(8,128)(2,1)S(1)}, u32[]{:S(2)}) %copy-start) | copy-done | bytes 8388632
  32.6 1.9 %far_one.1 = (f32[256,128]{1,0:T(8,128)S(1)}, bf16[256,128]{1,0:T(8,128)(2,1)S(1)}) custom-call(f32[256,128]{1,0:T(8,128)S(1)} %get-tuple-element.13.refs_0_.b, f32[256,128]{1,0:T(8,128)S(1)} %near.2, bf16[16,48,128]{2,1,0:T(8,128)(2,1)S(1)} %all-to-all-done.got.got0, s32[8,32]{1,0:T(8,128)S(1)} %bitcast.9, bf16[128,512]{1,0:T(8,128)(2,1)S(1)} %get-tuple-element.17.high, ...), custom_call_target="tpu_custom_call" | custom-call | tf_op jit(solution)/shard_map/far_one/pallas_call | solution.py:356
  34.5 0.9 %compress_two.1 = bf16[16,48,128]{2,1,0:T(8,128)(2,1)} custom-call(f32[256,128]{1,0:T(8,128)S(1)} %get-tuple-element.13.refs_0_.b, f32[256,128]{1,0:T(8,128)S(1)} %get-tuple-element.20.refs_1_.image, bf16[512,128]{1,0:T(8,128)(2,1)S(1)} %get-tuple-element.16.refs_1_.refs_2_), custom_call_target="tpu_custom_call" | custom-call | tf_op jit(solution)/shard_map/compress_two/pallas_call | solution.py:356
  35.5 3.5 %all-to-all-start.1 = ((bf16[16,48,128]{2,1,0:T(8,128)(2,1)}), bf16[16,48,128]{2,1,0:T(8,128)(2,1)S(1)}, u32[]{:S(2)}, u32[]{:S(2)}) async-start(bf16[16,48,128]{2,1,0:T(8,128)(2,1)} %compress_two.1), calls=%async_computation.1 | async-start | bytes 393216 | tf_op jit(solution)/shard_map/all_to_all | solution.py:362
  39.0 1.8 %collective-permute-start.6 = (bf16[256,128]{1,0:T(8,128)(2,1)S(1)}, bf16[256,128]{1,0:T(8,128)(2,1)S(1)}, u32[]{:S(2)}, u32[]{:S(2)}) collective-permute-start(bf16[256,128]{1,0:T(8,128)(2,1)S(1)} %get-tuple-element.21.refs_0_), channel_id=1, source_target_pairs={{0,2},{1,3},{2,0},{3,1},{4,6},{5,7},{6,4},{7,5},{8,10},{9,11},{10,... | collective-permute-start | bytes 196616 | tf_op jit(solution)/shard_map/ppermute | solution.py:291
  40.8 3.3 %collective-permute-start.7 = (bf16[256,128]{1,0:T(8,128)(2,1)S(1)}, bf16[256,128]{1,0:T(8,128)(2,1)S(1)}, u32[]{:S(2)}, u32[]{:S(2)}) collective-permute-start(bf16[256,128]{1,0:T(8,128)(2,1)S(1)} %get-tuple-element.21.refs_0_), channel_id=1, source_target_pairs={{0,14},{1,15},{2,4},{3,5},{4,2},{5,3},{6,8},{7,9},{8,6},{9,7},{10,... | collective-permute-start | bytes 196616 | tf_op jit(solution)/shard_map/ppermute | solution.py:291
  44.1 0.7 %collective-permute-done.6.refs_2_ = bf16[256,128]{1,0:T(8,128)(2,1)S(1)} collective-permute-done((bf16[256,128]{1,0:T(8,128)(2,1)S(1)}, bf16[256,128]{1,0:T(8,128)(2,1)S(1)}, u32[]{:S(2)}, u32[]{:S(2)}) %collective-permute-start.6) | collective-permute-done | bytes 65568 | tf_op jit(solution)/shard_map/ppermute | solution.py:291
  44.9 4.5 %collective-permute-done.7.refs_3_ = bf16[256,128]{1,0:T(8,128)(2,1)S(1)} collective-permute-done((bf16[256,128]{1,0:T(8,128)(2,1)S(1)}, bf16[256,128]{1,0:T(8,128)(2,1)S(1)}, u32[]{:S(2)}, u32[]{:S(2)}) %collective-permute-start.7) | collective-permute-done | bytes 65568 | tf_op jit(solution)/shard_map/ppermute | solution.py:291
  49.4 1.2 %collective-permute-done.9.refs_5_ = bf16[256,128]{1,0:T(8,128)(2,1)S(1)} collective-permute-done((bf16[256,128]{1,0:T(8,128)(2,1)S(1)}, bf16[256,128]{1,0:T(8,128)(2,1)S(1)}, u32[]{:S(2)}, u32[]{:S(2)}) %collective-permute-start.9) | collective-permute-done | bytes 65568 | tf_op jit(solution)/shard_map/ppermute | solution.py:291
  50.6 3.4 %copy-done.1 = bf16[16,1024,256]{2,1,0:T(8,128)(2,1)S(1)} copy-done((bf16[16,1024,256]{2,1,0:T(8,128)(2,1)S(1)}, bf16[16,1024,256]{2,1,0:T(8,128)(2,1)}, u32[]{:S(2)}) %copy-start.1) | copy-done | bytes 8388632
  54.0 1.8 %near.3 = f32[256,128]{1,0:T(8,128)S(1)} custom-call(bf16[256,128]{1,0:T(8,128)(2,1)S(1)} %get-tuple-element.21.refs_0_, bf16[256,128]{1,0:T(8,128)(2,1)S(1)} %collective-permute-done.5.refs_1_, bf16[256,128]{1,0:T(8,128)(2,1)S(1)} %collective-permute-done.6.refs_2_, bf16[256,128]{1,0:T(8,128)(2,1)S(1)} %collective-permute-done.7.refs_3_, ...), custom_call_target="tpu_custom_call" | custom-call | tf_op jit(solution)/shard_map/near/pallas_call | solution.py:356
  55.9 2.0 %far_two.1 = (f32[256,128]{1,0:T(8,128)S(1)}, f32[16,8,128]{2,1,0:T(8,128)S(1)}) custom-call(f32[256,128]{1,0:T(8,128)S(1)} %get-tuple-element.13.refs_0_.b, f32[256,128]{1,0:T(8,128)S(1)} %get-tuple-element.20.refs_1_.image, f32[256,128]{1,0:T(8,128)S(1)} %near.3, bf16[16,48,128]{2,1,0:T(8,128)(2,1)S(1)} %all-to-all-done.got.got0, ...), custom_call_target="tpu_custom_call" | custom-call | tf_op jit(solution)/shard_map/far_two/pallas_call | solution.py:356
  57.9 9.8 %all_to_all.15.got2 = f32[16,8,128]{2,1,0:T(8,128)S(1)} all-to-all(f32[16,8,128]{2,1,0:T(8,128)S(1)} %get-tuple-element.23), channel_id=1, replica_groups=mesh['groups'=2,'rows'=16] {'rows'}, dimensions={0} | all-to-all | bytes 131072 | tf_op jit(solution)/shard_map/all_to_all | solution.py:362
  67.7 1.2 %finish.1 = (f32[8,4096]{1,0:T(8,128)}, f32[8,4096]{1,0:T(8,128)}) custom-call(f32[256,128]{1,0:T(8,128)S(1)} %get-tuple-element.13.refs_0_.b, f32[256,128]{1,0:T(8,128)S(1)} %get-tuple-element.20.refs_1_.image, f32[256,128]{1,0:T(8,128)S(1)} %get-tuple-element.22.candidate, bf16[16,48,128]{2,1,0:T(8,128)(2,1)S(1)} %all-to-all-done.got.got0, ...), custom_call_target="tpu_custom_call" | custom-call | tf_op jit(solution)/shard_map/finish/pallas_call | solution.py:356
  (17 shorter events, 0.0 us)
Async XLA Ops:
  2.5 30.1 %all-to-all-start = ((bf16[16,48,128]{2,1,0:T(8,128)(2,1)}), bf16[16,48,128]{2,1,0:T(8,128)(2,1)S(1)}, u32[]{:S(2)}, u32[]{:S(2)}) async-start(bf16[16,48,128]{2,1,0:T(8,128)(2,1)} %compress_one.1), calls=%async_computation | async-start | bytes 393216 | tf_op jit(solution)/shard_map/all_to_all | solution.py:362
  9.9 6.0 %collective-permute-start.1 = (bf16[256,128]{1,0:T(8,128)(2,1)S(1)}, bf16[256,128]{1,0:T(8,128)(2,1)S(1)}, u32[]{:S(2)}, u32[]{:S(2)}) collective-permute-start(bf16[256,128]{1,0:T(8,128)(2,1)S(1)} %get-tuple-element.14.refs_0_), channel_id=1, source_target_pairs={{0,2},{1,3},{2,0},{3,1},{4,6},{5,7},{6,4},{7,5},{8,10},{9,11},{10,... | collective-permute-start | bytes 196616 | tf_op jit(solution)/shard_map/ppermute | solution.py:291
  11.8 8.5 %collective-permute-start.2 = (bf16[256,128]{1,0:T(8,128)(2,1)S(1)}, bf16[256,128]{1,0:T(8,128)(2,1)S(1)}, u32[]{:S(2)}, u32[]{:S(2)}) collective-permute-start(bf16[256,128]{1,0:T(8,128)(2,1)S(1)} %get-tuple-element.14.refs_0_), channel_id=1, source_target_pairs={{0,14},{1,15},{2,4},{3,5},{4,2},{5,3},{6,8},{7,9},{8,6},{9,7},{10,... | collective-permute-start | bytes 196616 | tf_op jit(solution)/shard_map/ppermute | solution.py:291
  15.1 12.4 %collective-permute-start = (bf16[256,128]{1,0:T(8,128)(2,1)S(1)}, bf16[256,128]{1,0:T(8,128)(2,1)S(1)}, u32[]{:S(2)}, u32[]{:S(2)}) collective-permute-start(bf16[256,128]{1,0:T(8,128)(2,1)S(1)} %get-tuple-element.14.refs_0_), channel_id=1, source_target_pairs={{0,1},{1,0},{2,3},{3,2},{4,5},{5,4},{6,7},{7,6},{8,9},{9,8},{10,11... | collective-permute-start | bytes 196616 | tf_op jit(solution)/shard_map/ppermute | solution.py:291
  15.9 11.6 %collective-permute-start.3 = (bf16[256,128]{1,0:T(8,128)(2,1)S(1)}, bf16[256,128]{1,0:T(8,128)(2,1)S(1)}, u32[]{:S(2)}, u32[]{:S(2)}) collective-permute-start(bf16[256,128]{1,0:T(8,128)(2,1)S(1)} %collective-permute-done.1.refs_2_), channel_id=1, source_target_pairs={{0,1},{1,0},{2,3},{3,2},{4,5},{5,4},{6,7},{7,6},{8,9},{9,8},{10,11... | collective-permute-start | bytes 196616 | tf_op jit(solution)/shard_map/ppermute | solution.py:291
  20.3 7.2 %collective-permute-start.4 = (bf16[256,128]{1,0:T(8,128)(2,1)S(1)}, bf16[256,128]{1,0:T(8,128)(2,1)S(1)}, u32[]{:S(2)}, u32[]{:S(2)}) collective-permute-start(bf16[256,128]{1,0:T(8,128)(2,1)S(1)} %collective-permute-done.2.refs_3_), channel_id=1, source_target_pairs={{0,1},{1,0},{2,3},{3,2},{4,5},{5,4},{6,7},{7,6},{8,9},{9,8},{10,11... | collective-permute-start | bytes 196616 | tf_op jit(solution)/shard_map/ppermute | solution.py:291
  21.0 11.6 %copy-start.2 = (s32[32,8]{0,1:T(8,128)S(1)}, s32[32,8]{0,1:T(8,128)}, u32[]{:S(2)}) copy-start(s32[32,8]{0,1:T(8,128)} %param.15) | copy-start | bytes 3076
  29.4 3.2 %copy-start = (bf16[16,1024,256]{2,1,0:T(8,128)(2,1)}, bf16[16,1024,256]{2,1,0:T(8,128)(2,1)S(1)}, u32[]{:S(2)}) copy-start(bf16[16,1024,256]{2,1,0:T(8,128)(2,1)S(1)} %get-tuple-element.15.refs_7_) | copy-start | bytes 25165828
  35.5 20.4 %all-to-all-start.1 = ((bf16[16,48,128]{2,1,0:T(8,128)(2,1)}), bf16[16,48,128]{2,1,0:T(8,128)(2,1)S(1)}, u32[]{:S(2)}, u32[]{:S(2)}) async-start(bf16[16,48,128]{2,1,0:T(8,128)(2,1)} %compress_two.1), calls=%async_computation.1 | async-start | bytes 393216 | tf_op jit(solution)/shard_map/all_to_all | solution.py:362
  39.0 5.9 %collective-permute-start.6 = (bf16[256,128]{1,0:T(8,128)(2,1)S(1)}, bf16[256,128]{1,0:T(8,128)(2,1)S(1)}, u32[]{:S(2)}, u32[]{:S(2)}) collective-permute-start(bf16[256,128]{1,0:T(8,128)(2,1)S(1)} %get-tuple-element.21.refs_0_), channel_id=1, source_target_pairs={{0,2},{1,3},{2,0},{3,1},{4,6},{5,7},{6,4},{7,5},{8,10},{9,11},{10,... | collective-permute-start | bytes 196616 | tf_op jit(solution)/shard_map/ppermute | solution.py:291
  40.8 8.6 %collective-permute-start.7 = (bf16[256,128]{1,0:T(8,128)(2,1)S(1)}, bf16[256,128]{1,0:T(8,128)(2,1)S(1)}, u32[]{:S(2)}, u32[]{:S(2)}) collective-permute-start(bf16[256,128]{1,0:T(8,128)(2,1)S(1)} %get-tuple-element.21.refs_0_), channel_id=1, source_target_pairs={{0,14},{1,15},{2,4},{3,5},{4,2},{5,3},{6,8},{7,9},{8,6},{9,7},{10,... | collective-permute-start | bytes 196616 | tf_op jit(solution)/shard_map/ppermute | solution.py:291
  44.1 5.3 %collective-permute-start.5 = (bf16[256,128]{1,0:T(8,128)(2,1)S(1)}, bf16[256,128]{1,0:T(8,128)(2,1)S(1)}, u32[]{:S(2)}, u32[]{:S(2)}) collective-permute-start(bf16[256,128]{1,0:T(8,128)(2,1)S(1)} %get-tuple-element.21.refs_0_), channel_id=1, source_target_pairs={{0,1},{1,0},{2,3},{3,2},{4,5},{5,4},{6,7},{7,6},{8,9},{9,8},{10,11... | collective-permute-start | bytes 196616 | tf_op jit(solution)/shard_map/ppermute | solution.py:291
  44.8 4.6 %collective-permute-start.8 = (bf16[256,128]{1,0:T(8,128)(2,1)S(1)}, bf16[256,128]{1,0:T(8,128)(2,1)S(1)}, u32[]{:S(2)}, u32[]{:S(2)}) collective-permute-start(bf16[256,128]{1,0:T(8,128)(2,1)S(1)} %collective-permute-done.6.refs_2_), channel_id=1, source_target_pairs={{0,1},{1,0},{2,3},{3,2},{4,5},{5,4},{6,7},{7,6},{8,9},{9,8},{10,11... | collective-permute-start | bytes 196616 | tf_op jit(solution)/shard_map/ppermute | solution.py:291
  49.4 1.3 %collective-permute-start.9 = (bf16[256,128]{1,0:T(8,128)(2,1)S(1)}, bf16[256,128]{1,0:T(8,128)(2,1)S(1)}, u32[]{:S(2)}, u32[]{:S(2)}) collective-permute-start(bf16[256,128]{1,0:T(8,128)(2,1)S(1)} %collective-permute-done.7.refs_3_), channel_id=1, source_target_pairs={{0,1},{1,0},{2,3},{3,2},{4,5},{5,4},{6,7},{7,6},{8,9},{9,8},{10,11... | collective-permute-start | bytes 196616 | tf_op jit(solution)/shard_map/ppermute | solution.py:291
  50.6 3.4 %copy-start.1 = (bf16[16,1024,256]{2,1,0:T(8,128)(2,1)S(1)}, bf16[16,1024,256]{2,1,0:T(8,128)(2,1)}, u32[]{:S(2)}) copy-start(bf16[16,1024,256]{2,1,0:T(8,128)(2,1)} %copy-done) | copy-start | bytes 25165828

commit v5 on v4

--- a/solution.py
+++ b/solution.py
@@ -12,6 +12,7 @@
 VMEM = pl.BlockSpec(memory_space=pltpu.VMEM)
 SMEM = pl.BlockSpec(memory_space=pltpu.SMEM)
 HBM = pl.BlockSpec(memory_space=pltpu.HBM)
+ANY = pl.BlockSpec(memory_space=pl.ANY)
 R = 8
 LANES = 128
 SUM_SLOTS = 8
@@ -85,7 +86,7 @@
 
 
 def compress_kernel(per_group, pairs, *refs):
-    *fields, basis, payload = refs
+    *fields, basis, _, payload = refs
     clusters = fields[0].shape[0] // R
     tiles = [rows_of(fields[-1], j) for j in range(clusters)]
     sums = [
@@ -99,8 +100,8 @@
 
 
 def prepare_kernel(
-    coupling_hbm, target_hbm, blocks_hbm, high_out, low_out, target_out, turned, coupling, target, blocks,
-    block_sems, sems,
+    coupling_hbm, target_hbm, blocks_hbm, _, high_out, low_out, target_out, turned_hbm, coupling, target, blocks,
+    turned, block_sems, turned_sems, sems,
 ):
     others = [
         pltpu.make_async_copy(coupling_hbm, coupling, sems.at[0]),
@@ -137,6 +138,10 @@
 
     pairs_each = rows // (2 * slots)
 
+    def copy_out(chunk):
+        span = pl.ds(chunk * pairs_each, pairs_each)
+        return pltpu.make_async_copy(turned.at[span], turned_hbm.at[span], turned_sems.at[chunk])
+
     def body(chunk, carry):
         copy_of(chunk).wait()
         for inner in range(pairs_each):
@@ -145,9 +150,12 @@
                 for side in range(2):
                     block = blocks[(2 * pair + side) * slots + k]
                     turned[pair, k * LANES : (k + 1) * LANES, side * LANES : (side + 1) * LANES] = block.T
+        copy_out(chunk).start()
         return carry
 
     lax.fori_loop(0, chunks, body, 0)
+    for chunk in range(chunks):
+        copy_out(chunk).wait()
 
 
 def far_field(got, far_cols, high, low, target, table, clusters, rank, far):
@@ -185,18 +193,36 @@
     )
 
 
+def relay_kernel(even, odd, _, both):
+    rows = even.shape[0]
+    both[pl.ds(0, rows), :] = even[...]
+    both[pl.ds(rows, rows), :] = odd[...]
+
+
 def near_kernel(*refs):
-    *slabs, placed, turned, near, window = refs
-    rows = slabs[0].shape[0]
-    for at, slab in enumerate(slabs):
-        window[pl.ds(at * rows, rows), :] = slab[...].astype(f32)
-    window[pl.ds(len(slabs) * rows, R), :] = jnp.zeros((R, LANES), f32)
+    *slabs, placed, turned_hbm, near, window, turned, sems = refs
     slots, clusters = placed.shape
+    chunks = sems.shape[0]
+    pairs_each = turned.shape[0] // chunks
+
+    def copy_of(chunk):
+        span = pl.ds(chunk * pairs_each, pairs_each)
+        return pltpu.make_async_copy(turned_hbm.at[span], turned.at[span], sems.at[chunk])
+
+    for chunk in range(chunks):
+        copy_of(chunk).start()
+    at = 0
+    for slab in slabs:
+        window[pl.ds(at, slab.shape[0]), :] = slab[...].astype(f32)
+        at += slab.shape[0]
+    window[pl.ds(at, R), :] = jnp.zeros((R, LANES), f32)
 
     def fetch(k, i):
         return window[pl.ds(pl.multiple_of(placed[k, i] * R, R), R), :]
 
     for pair in range(clusters // 2):
+        if pair % pairs_each == 0:
+            copy_of(pair // pairs_each).wait()
         sources = [
             jnp.concatenate([fetch(k, 2 * pair), fetch(k, 2 * pair + 1)], axis=0).astype(bf16)
             for k in range(slots)
@@ -305,11 +331,8 @@
     return 2 * (other % (lax.axis_size("rows") // 2)) + i % 2
 
 
-def slabs_of(block):
-    odd = swapped(block, odd_mate)
-    even = swapped(block, even_mate)
-    mate = swapped(block, core_mate)
-    return [block, mate, even, odd, swapped(even, core_mate), swapped(odd, core_mate)]
+def sends_of(block):
+    return [block] + [swapped(block, partner) for partner in (core_mate, even_mate, odd_mate)]
 
 
 def window_place(distance, clusters):
@@ -352,10 +375,11 @@
     def in_hbm(array):
         return pltpu.with_memory_space_constraint(array, pltpu.HBM)
 
-    def call(kernel, name, out, ins, *args, scratch_shapes=()):
+    def call(kernel, name, out, ins, *args, scratch_shapes=(), cost_estimate=None):
         return pl.pallas_call(
             kernel, out_shape=out, in_specs=ins, out_specs=jax.tree.map(lambda _: VMEM, out),
             scratch_shapes=scratch_shapes, compiler_params=PARAMS, name=name,
+            cost_estimate=cost_estimate,
         )(*args)
 
     def exchange(block):
@@ -367,13 +391,19 @@
         [HBM] * 2, in_hbm(right_sides), in_hbm(basis_in.reshape(clusters * rank, LANES)),
         scratch_shapes=[scratch(R, width), pltpu.SemaphoreType.DMA((2,))],
     )
-    slabs = slabs_of(lowered)
+    held = sends_of(lowered)
     payload_shape = shape(size, head + TAIL, LANES, dtype=bf16)
     payload = call(
         functools.partial(compress_kernel, per_group, [(0, 0)]), "compress_one", payload_shape,
-        [VMEM] * 2, field, basis,
+        [VMEM] * 2 + [ANY], field, basis, held[1],
     )
     got0 = exchange(payload)
+
+    def relayed(held, payload):
+        both = call(
+            relay_kernel, "relay", shape(2 * rows, LANES, dtype=bf16), [VMEM] * 2 + [ANY], *held[2:], payload
+        )
+        return swapped(both, core_mate)
 
     turned_shape = (clusters // 2, slots * LANES, 2 * LANES)
     high, low, target, turned = pl.pallas_call(
@@ -382,48 +412,56 @@
             shape(slots * rank, rank * clusters, dtype=bf16),
             shape(slots * rank, rank * clusters, dtype=bf16),
             shape(rank * clusters, LANES, dtype=bf16),
-            pltpu.VMEM(turned_shape, bf16),
+            pltpu.HBM(turned_shape, bf16),
         ),
-        in_specs=[HBM] * 3, out_specs=[VMEM] * 4,
+        in_specs=[HBM] * 3 + [ANY], out_specs=[VMEM] * 3 + [HBM],
         scratch_shapes=[
             scratch(slots, rank, rank, clusters), scratch(clusters * rank, LANES, dtype=bf16),
-            scratch(clusters * slots, LANES, LANES, dtype=bf16),
-            pltpu.SemaphoreType.DMA((8,)), pltpu.SemaphoreType.DMA((2,)),
+            scratch(clusters * slots, LANES, LANES, dtype=bf16), scratch(*turned_shape, dtype=bf16),
+            pltpu.SemaphoreType.DMA((8,)), pltpu.SemaphoreType.DMA((8,)), pltpu.SemaphoreType.DMA((2,)),
         ],
         compiler_params=PARAMS, name="prepare",
+        cost_estimate=pl.CostEstimate(flops=0, bytes_accessed=4 * near_blocks.size, transcendentals=0),
     )(
         in_hbm(jnp.transpose(coupling, (1, 2, 3, 0))),
         in_hbm(target_basis.reshape(clusters * rank, LANES)),
         in_hbm(near_blocks.reshape(clusters * slots, LANES, LANES)),
-    )
-    turned = pltpu.with_memory_space_constraint(turned, pltpu.VMEM)
+        payload,
+    )
+    turned = in_hbm(turned)
     reach = 2 * clusters
     start = lax.axis_index("rows") * clusters
     distance = (near_cols.T - start + reach) % every
     live = jnp.arange(slots, dtype=jnp.int32)[:, None] < near_counts[None, :]
-    placed = jnp.where(live, window_place(distance, clusters), len(slabs) * clusters).astype(jnp.int32)
+    placed = jnp.where(live, window_place(distance, clusters), 6 * clusters).astype(jnp.int32)
     far_index = far_cols.T
 
     def near_of(slabs):
         return call(
-            near_kernel, "near", shape(rows, LANES), [VMEM] * len(slabs) + [SMEM, VMEM], *slabs, placed, turned,
-            scratch_shapes=[scratch(len(slabs) * rows + R, LANES)],
+            near_kernel, "near", shape(rows, LANES), [VMEM] * len(slabs) + [SMEM, HBM], *slabs, placed, turned,
+            scratch_shapes=[
+                scratch(6 * rows + R, LANES), scratch(*turned_shape, dtype=bf16),
+                pltpu.SemaphoreType.DMA((8,)),
+            ],
+            cost_estimate=pl.CostEstimate(
+                flops=32 * near_blocks.size, bytes_accessed=2 * near_blocks.size, transcendentals=0
+            ),
         )
 
     kept = [scratch(size * head, LANES), scratch(rows, LANES)]
-    near = near_of(slabs)
+    near = near_of(held + [relayed(held, payload)])
     image, lowered = call(
         functools.partial(first_kernel, per_group, unknowns), "far_one",
         (shape(rows, LANES), shape(rows, LANES, dtype=bf16)), [VMEM] * 3 + [SMEM] + [VMEM] * 3,
         field, near, got0, far_index, high, low, target, scratch_shapes=kept,
     )
-    slabs = slabs_of(lowered)
+    held = sends_of(lowered)
     payload = call(
         functools.partial(compress_kernel, per_group, [(0, 1), (1, 1)]), "compress_two", payload_shape,
-        [VMEM] * 3, field, image, basis,
+        [VMEM] * 3 + [ANY], field, image, basis, held[1],
     )
     got1 = exchange(payload)
-    near = near_of(slabs)
+    near = near_of(held + [relayed(held, payload)])
     candidate, sums = call(
         functools.partial(second_kernel, per_group, unknowns), "far_two",
         (shape(rows, LANES), shape(size, R, LANES)), [VMEM] * 5 + [SMEM] + [VMEM] * 3,

time: 69.3 us -> 71.8 us (1.036)
  local copies, waits for them, and re-layouts: 6.62 us -> 0.01 us
  Pallas kernels: 18.1 us -> 24.2 us
  waiting for transfers between devices: 11.7 us -> 13.6 us
  starting transfers between devices: 21.3 us -> 22.4 us
    unnamed x6 -> x2, local copies, waits for them, and re-layouts: 6.62 us -> 0.01 us
    pallas_call x8 -> x10, Pallas kernels: 11.7 us -> 16.7 us  [call(): pl.pallas_call(kernel, out_shape=out, in_specs=ins, out_specs=jax.tree.ma...]
    ppermute x10 -> x8, waiting for transfers between devices: 11.7 us -> 13.6 us  [swapped(): lax.ppermute(block, 'rows', [(i, partner(i)) for i in range(lax.axis_size...]
    ppermute x10 -> x8, starting transfers between devices: 10.3 us -> 11.6 us  [swapped(): lax.ppermute(block, 'rows', [(i, partner(i)) for i in range(lax.axis_size...]
    pallas_call x1, Pallas kernels: 6.41 us -> 7.52 us  [on_device(): pl.pallas_call(prepare_kernel, out_shape=(shape(slots * rank, rank * clus...]
  transfers between devices with their start and end apart: 12 -> 10, of which waited for: 5 -> 7; matrix products, arithmetic and copies ran while one was open for 1% -> 1% of each run, Pallas kernels for 15% -> 23%
where the time goes in v5:
time: 71.8 us; the launch traced here: 71.4 us
  Pallas kernels  24.2 us (34%)
  starting transfers between devices  22.4 us (31%)
  waiting for transfers between devices  13.6 us (19%)
  blocking collectives  9.76 us (14%)
  between operations  0.75 us (1%)
  other arithmetic  0.72 us (1%)
    pallas_call x10, Pallas kernels, call(): pl.pallas_call(kernel, out_shape=out, in_specs=ins, out_specs=jax.tree.ma...  16.7 us
    ppermute x8, waiting for transfers between devices, swapped(): lax.ppermute(block, 'rows', [(i, partner(i)) for i in range(lax.axis_size...  13.6 us
    ppermute x8, starting transfers between devices, swapped(): lax.ppermute(block, 'rows', [(i, partner(i)) for i in range(lax.axis_size...  11.6 us
    all_to_all x2, starting transfers between devices, exchange(): return lax.all_to_all(block, 'rows', 0, 0)  10.8 us
    all_to_all x1, blocking collectives, exchange(): return lax.all_to_all(block, 'rows', 0, 0)  9.76 us
    pallas_call x1, Pallas kernels, on_device(): pl.pallas_call(prepare_kernel, out_shape=(shape(slots * rank, rank * clus...  7.52 us
  transfers between devices with their start and end apart: 10, of which 7 were waited for; matrix products, arithmetic and copies ran while one was open for 1% of the time, Pallas kernels for 23%

profile of v5, /device:TPU:0, one launch (start us, length us, event | category | flops | bytes accessed | tf_op | source)
XLA Modules:
  0.0 71.4 jit_solution(9438803729386704055)
XLA Ops:
  0.6 1.0 %start.1 = (f32[256,128]{1,0:T(8,128)S(1)}, bf16[512,128]{1,0:T(8,128)(2,1)S(1)}, bf16[256,128]{1,0:T(8,128)(2,1)S(1)}) custom-call(f32[8,4096]{1,0:T(8,128)} %b_hbm.1, bf16[512,128]{1,0:T(8,128)(2,1)} %bitcast.14), custom_call_target="tpu_custom_call" | custom-call | tf_op jit(solution)/shard_map/start/pallas_call | solution.py:379
  2.1 0.9 %collective-permute-done.refs_2_.refs_1_ = bf16[256,128]{1,0:T(8,128)(2,1)S(1)} collective-permute-done((bf16[256,128]{1,0:T(8,128)(2,1)S(1)}, bf16[256,128]{1,0:T(8,128)(2,1)S(1)}, u32[]{:S(2)}, u32[]{:S(2)}) %collective-permute-start) | collective-permute-done | bytes 65568 | tf_op jit(solution)/shard_map/ppermute | solution.py:317
  3.0 0.9 %compress_one.1._ = bf16[16,48,128]{2,1,0:T(8,128)(2,1)} custom-call(f32[256,128]{1,0:T(8,128)S(1)} %get-tuple-element.13.refs_0_.b, bf16[512,128]{1,0:T(8,128)(2,1)S(1)} %get-tuple-element.15.refs_1_.refs_2_, bf16[256,128]{1,0:T(8,128)(2,1)S(1)} %collective-permute-done.refs_2_.refs_1_), custom_call_target="tpu_custom_call" | custom-call | tf_op jit(solution)/shard_map/compress_one/pallas_call | solution.py:379
  3.9 7.3 %all-to-all-start = ((bf16[16,48,128]{2,1,0:T(8,128)(2,1)}), bf16[16,48,128]{2,1,0:T(8,128)(2,1)S(1)}, u32[]{:S(2)}, u32[]{:S(2)}) async-start(bf16[16,48,128]{2,1,0:T(8,128)(2,1)} %compress_one.1._), calls=%async_computation | async-start | bytes 393216 | tf_op jit(solution)/shard_map/all_to_all | solution.py:386
  11.2 1.9 %collective-permute-start.1 = (bf16[256,128]{1,0:T(8,128)(2,1)S(1)}, bf16[256,128]{1,0:T(8,128)(2,1)S(1)}, u32[]{:S(2)}, u32[]{:S(2)}) collective-permute-start(bf16[256,128]{1,0:T(8,128)(2,1)S(1)} %get-tuple-element.14.refs_0_), channel_id=1, source_target_pairs={{0,2},{1,3},{2,0},{3,1},{4,6},{5,7},{6,4},{7,5},{8,10},{9,11},{10,... | collective-permute-start | bytes 196616 | tf_op jit(solution)/shard_map/ppermute | solution.py:317
  13.2 3.3 %collective-permute-start.2 = (bf16[256,128]{1,0:T(8,128)(2,1)S(1)}, bf16[256,128]{1,0:T(8,128)(2,1)S(1)}, u32[]{:S(2)}, u32[]{:S(2)}) collective-permute-start(bf16[256,128]{1,0:T(8,128)(2,1)S(1)} %get-tuple-element.14.refs_0_), channel_id=1, source_target_pairs={{0,14},{1,15},{2,4},{3,5},{4,2},{5,3},{6,8},{7,9},{8,6},{9,7},{10,... | collective-permute-start | bytes 196616 | tf_op jit(solution)/shard_map/ppermute | solution.py:317
  16.4 0.8 %collective-permute-done.1.even.refs_2_ = bf16[256,128]{1,0:T(8,128)(2,1)S(1)} collective-permute-done((bf16[256,128]{1,0:T(8,128)(2,1)S(1)}, bf16[256,128]{1,0:T(8,128)(2,1)S(1)}, u32[]{:S(2)}, u32[]{:S(2)}) %collective-permute-start.1) | collective-permute-done | bytes 65568 | tf_op jit(solution)/shard_map/ppermute | solution.py:317
  17.2 4.4 %collective-permute-done.2.odd.refs_3_ = bf16[256,128]{1,0:T(8,128)(2,1)S(1)} collective-permute-done((bf16[256,128]{1,0:T(8,128)(2,1)S(1)}, bf16[256,128]{1,0:T(8,128)(2,1)S(1)}, u32[]{:S(2)}, u32[]{:S(2)}) %collective-permute-start.2) | collective-permute-done | bytes 65568 | tf_op jit(solution)/shard_map/ppermute | solution.py:317
  21.7 0.7 %fusion.2.refs_5_ = s32[8,32]{1,0:T(8,128)S(1)} fusion(s32[32,8]{0,1:T(8,128)} %param.10, s32[]{:T(128)S(6)} %sub.24, s32[]{:T(128)S(6)} %select_n.67, s32[]{:T(128)S(6)} %select_n.66, s32[]{:T(128)S(6)} %add.49, s32[]{:T(128)S(6)} %mul.7, s32[32]{0:T(128)} %param.11), kind=kLoop, calls=%fused_computation.10 | loop fusion | flops 11776 | bytes 2196 | tf_op jit(solution)/shard_map/jit(_where)/select_n | solution.py:436
  22.5 7.5 %prepare.1 = (bf16[128,512]{1,0:T(8,128)(2,1)S(1)}, bf16[128,512]{1,0:T(8,128)(2,1)S(1)}, bf16[512,128]{1,0:T(8,128)(2,1)S(1)}, bf16[16,1024,256]{2,1,0:T(8,128)(2,1)}) custom-call(f32[8,16,16,32]{3,2,1,0:T(8,128)} %bitcast.12, bf16[512,128]{1,0:T(8,128)(2,1)} %bitcast.13, bf16[256,128,128]{2,1,0:T(8,128)(2,1)} %bitcast.11, bf16[16,48,128]{2,1,0:T(8,128)(2,1)} %compress_one.1._), custom_call_target="tpu_custom_call" | custom-call | bytes 16777216 | tf_op jit(solution)/shard_map/prepare/pallas_call | solution.py:409
  30.0 4.3 %near.2 = f32[256,128]{1,0:T(8,128)S(1)} custom-call(bf16[256,128]{1,0:T(8,128)(2,1)S(1)} %get-tuple-element.14.refs_0_, bf16[256,128]{1,0:T(8,128)(2,1)S(1)} %collective-permute-done.refs_2_.refs_1_, bf16[256,128]{1,0:T(8,128)(2,1)S(1)} %collective-permute-done.1.even.refs_2_, bf16[256,128]{1,0:T(8,128)(2,1)S(1)} %collective-permute-done.2.odd.refs_3_, ...), custom_call_target="tpu_custom_call" | custom-call | flops 134217728 | bytes 8388608 | tf_op jit(solution)/shard_map/near/pallas_call | solution.py:379
  34.4 2.0 %far_one.1 = (f32[256,128]{1,0:T(8,128)S(1)}, bf16[256,128]{1,0:T(8,128)(2,1)S(1)}) custom-call(f32[256,128]{1,0:T(8,128)S(1)} %get-tuple-element.13.refs_0_.b, f32[256,128]{1,0:T(8,128)S(1)} %near.2, bf16[16,48,128]{2,1,0:T(8,128)(2,1)S(1)} %all-to-all-done.got.got0, s32[8,32]{1,0:T(8,128)S(1)} %bitcast.9, bf16[128,512]{1,0:T(8,128)(2,1)S(1)} %get-tuple-element.17.high, ...), custom_call_target="tpu_custom_call" | custom-call | tf_op jit(solution)/shard_map/far_one/pallas_call | solution.py:379
  36.9 0.9 %collective-permute-done.4.refs_3_.refs_1_ = bf16[256,128]{1,0:T(8,128)(2,1)S(1)} collective-permute-done((bf16[256,128]{1,0:T(8,128)(2,1)S(1)}, bf16[256,128]{1,0:T(8,128)(2,1)S(1)}, u32[]{:S(2)}, u32[]{:S(2)}) %collective-permute-start.4) | collective-permute-done | bytes 65568 | tf_op jit(solution)/shard_map/ppermute | solution.py:317
  37.8 0.9 %compress_two.1._ = bf16[16,48,128]{2,1,0:T(8,128)(2,1)} custom-call(f32[256,128]{1,0:T(8,128)S(1)} %get-tuple-element.13.refs_0_.b, f32[256,128]{1,0:T(8,128)S(1)} %get-tuple-element.20.refs_1_.image, bf16[512,128]{1,0:T(8,128)(2,1)S(1)} %get-tuple-element.15.refs_1_.refs_2_, bf16[256,128]{1,0:T(8,128)(2,1)S(1)} %collective-permute-done.4.refs_3_.refs_1_), custom_call_target="tpu_custom_call" | custom-call | tf_op jit(solution)/shard_map/compress_two/pallas_call | solution.py:379
  38.7 3.5 %all-to-all-start.1 = ((bf16[16,48,128]{2,1,0:T(8,128)(2,1)}), bf16[16,48,128]{2,1,0:T(8,128)(2,1)S(1)}, u32[]{:S(2)}, u32[]{:S(2)}) async-start(bf16[16,48,128]{2,1,0:T(8,128)(2,1)} %compress_two.1._), calls=%async_computation.1 | async-start | bytes 393216 | tf_op jit(solution)/shard_map/all_to_all | solution.py:386
  42.2 1.8 %collective-permute-start.5 = (bf16[256,128]{1,0:T(8,128)(2,1)S(1)}, bf16[256,128]{1,0:T(8,128)(2,1)S(1)}, u32[]{:S(2)}, u32[]{:S(2)}) collective-permute-start(bf16[256,128]{1,0:T(8,128)(2,1)S(1)} %get-tuple-element.21.refs_0_), channel_id=1, source_target_pairs={{0,2},{1,3},{2,0},{3,1},{4,6},{5,7},{6,4},{7,5},{8,10},{9,11},{10,... | collective-permute-start | bytes 196616 | tf_op jit(solution)/shard_map/ppermute | solution.py:317
  44.0 3.3 %collective-permute-start.6 = (bf16[256,128]{1,0:T(8,128)(2,1)S(1)}, bf16[256,128]{1,0:T(8,128)(2,1)S(1)}, u32[]{:S(2)}, u32[]{:S(2)}) collective-permute-start(bf16[256,128]{1,0:T(8,128)(2,1)S(1)} %get-tuple-element.21.refs_0_), channel_id=1, source_target_pairs={{0,14},{1,15},{2,4},{3,5},{4,2},{5,3},{6,8},{7,9},{8,6},{9,7},{10,... | collective-permute-start | bytes 196616 | tf_op jit(solution)/shard_map/ppermute | solution.py:317
  47.3 0.7 %collective-permute-done.5.even.refs_2_ = bf16[256,128]{1,0:T(8,128)(2,1)S(1)} collective-permute-done((bf16[256,128]{1,0:T(8,128)(2,1)S(1)}, bf16[256,128]{1,0:T(8,128)(2,1)S(1)}, u32[]{:S(2)}, u32[]{:S(2)}) %collective-permute-start.5) | collective-permute-done | bytes 65568 | tf_op jit(solution)/shard_map/ppermute | solution.py:317
  48.1 4.5 %collective-permute-done.6.odd.refs_3_ = bf16[256,128]{1,0:T(8,128)(2,1)S(1)} collective-permute-done((bf16[256,128]{1,0:T(8,128)(2,1)S(1)}, bf16[256,128]{1,0:T(8,128)(2,1)S(1)}, u32[]{:S(2)}, u32[]{:S(2)}) %collective-permute-start.6) | collective-permute-done | bytes 65568 | tf_op jit(solution)/shard_map/ppermute | solution.py:317
  52.7 1.3 %collective-permute-done.7.refs_4_ = bf16[512,128]{1,0:T(8,128)(2,1)S(1)} collective-permute-done((bf16[512,128]{1,0:T(8,128)(2,1)S(1)}, bf16[512,128]{1,0:T(8,128)(2,1)S(1)}, u32[]{:S(2)}, u32[]{:S(2)}) %collective-permute-start.7) | collective-permute-done | bytes 131104 | tf_op jit(solution)/shard_map/ppermute | solution.py:317
  54.0 4.3 %near.3 = f32[256,128]{1,0:T(8,128)S(1)} custom-call(bf16[256,128]{1,0:T(8,128)(2,1)S(1)} %get-tuple-element.21.refs_0_, bf16[256,128]{1,0:T(8,128)(2,1)S(1)} %collective-permute-done.4.refs_3_.refs_1_, bf16[256,128]{1,0:T(8,128)(2,1)S(1)} %collective-permute-done.5.even.refs_2_, bf16[256,128]{1,0:T(8,128)(2,1)S(1)} %collective-permute-done.6.odd.refs_3_, ...), custom_call_target="tpu_custom_call" | custom-call | flops 134217728 | bytes 8388608 | tf_op jit(solution)/shard_map/near/pallas_call | solution.py:379
  58.4 2.0 %far_two.1 = (f32[256,128]{1,0:T(8,128)S(1)}, f32[16,8,128]{2,1,0:T(8,128)S(1)}) custom-call(f32[256,128]{1,0:T(8,128)S(1)} %get-tuple-element.13.refs_0_.b, f32[256,128]{1,0:T(8,128)S(1)} %get-tuple-element.20.refs_1_.image, f32[256,128]{1,0:T(8,128)S(1)} %near.3, bf16[16,48,128]{2,1,0:T(8,128)(2,1)S(1)} %all-to-all-done.got.got0, ...), custom_call_target="tpu_custom_call" | custom-call | tf_op jit(solution)/shard_map/far_two/pallas_call | solution.py:379
  60.4 9.8 %all_to_all.15.got2 = f32[16,8,128]{2,1,0:T(8,128)S(1)} all-to-all(f32[16,8,128]{2,1,0:T(8,128)S(1)} %get-tuple-element.23), channel_id=1, replica_groups=mesh['groups'=2,'rows'=16] {'rows'}, dimensions={0} | all-to-all | bytes 131072 | tf_op jit(solution)/shard_map/all_to_all | solution.py:386
  70.2 1.2 %finish.1 = (f32[8,4096]{1,0:T(8,128)}, f32[8,4096]{1,0:T(8,128)}) custom-call(f32[256,128]{1,0:T(8,128)S(1)} %get-tuple-element.13.refs_0_.b, f32[256,128]{1,0:T(8,128)S(1)} %get-tuple-element.20.refs_1_.image, f32[256,128]{1,0:T(8,128)S(1)} %get-tuple-element.22.candidate, bf16[16,48,128]{2,1,0:T(8,128)(2,1)S(1)} %all-to-all-done.got.got0, ...), custom_call_target="tpu_custom_call" | custom-call | tf_op jit(solution)/shard_map/finish/pallas_call | solution.py:379
  (11 shorter events, 1.3 us)
Async XLA Ops:
  1.6 1.4 %collective-permute-start = (bf16[256,128]{1,0:T(8,128)(2,1)S(1)}, bf16[256,128]{1,0:T(8,128)(2,1)S(1)}, u32[]{:S(2)}, u32[]{:S(2)}) collective-permute-start(bf16[256,128]{1,0:T(8,128)(2,1)S(1)} %get-tuple-element.14.refs_0_), channel_id=1, source_target_pairs={{0,1},{1,0},{2,3},{3,2},{4,5},{5,4},{6,7},{7,6},{8,9},{9,8},{10,11... | collective-permute-start | bytes 196616 | tf_op jit(solution)/shard_map/ppermute | solution.py:317
  3.9 30.4 %all-to-all-start = ((bf16[16,48,128]{2,1,0:T(8,128)(2,1)}), bf16[16,48,128]{2,1,0:T(8,128)(2,1)S(1)}, u32[]{:S(2)}, u32[]{:S(2)}) async-start(bf16[16,48,128]{2,1,0:T(8,128)(2,1)} %compress_one.1._), calls=%async_computation | async-start | bytes 393216 | tf_op jit(solution)/shard_map/all_to_all | solution.py:386
  11.2 6.0 %collective-permute-start.1 = (bf16[256,128]{1,0:T(8,128)(2,1)S(1)}, bf16[256,128]{1,0:T(8,128)(2,1)S(1)}, u32[]{:S(2)}, u32[]{:S(2)}) collective-permute-start(bf16[256,128]{1,0:T(8,128)(2,1)S(1)} %get-tuple-element.14.refs_0_), channel_id=1, source_target_pairs={{0,2},{1,3},{2,0},{3,1},{4,6},{5,7},{6,4},{7,5},{8,10},{9,11},{10,... | collective-permute-start | bytes 196616 | tf_op jit(solution)/shard_map/ppermute | solution.py:317
  13.2 8.5 %collective-permute-start.2 = (bf16[256,128]{1,0:T(8,128)(2,1)S(1)}, bf16[256,128]{1,0:T(8,128)(2,1)S(1)}, u32[]{:S(2)}, u32[]{:S(2)}) collective-permute-start(bf16[256,128]{1,0:T(8,128)(2,1)S(1)} %get-tuple-element.14.refs_0_), channel_id=1, source_target_pairs={{0,14},{1,15},{2,4},{3,5},{4,2},{5,3},{6,8},{7,9},{8,6},{9,7},{10,... | collective-permute-start | bytes 196616 | tf_op jit(solution)/shard_map/ppermute | solution.py:317
  21.6 8.3 %collective-permute-start.3 = (bf16[512,128]{1,0:T(8,128)(2,1)S(1)}, bf16[512,128]{1,0:T(8,128)(2,1)S(1)}, u32[]{:S(2)}, u32[]{:S(2)}) collective-permute-start(bf16[512,128]{1,0:T(8,128)(2,1)S(1)} %relay.2), channel_id=1, source_target_pairs={{0,1},{1,0},{2,3},{3,2},{4,5},{5,4},{6,7},{7,6},{8,9},{9,8},{10,11... | collective-permute-start | bytes 393224 | tf_op jit(solution)/shard_map/ppermute | solution.py:317
  22.4 11.9 %copy-start = (s32[32,8]{0,1:T(8,128)S(1)}, s32[32,8]{0,1:T(8,128)}, u32[]{:S(2)}) copy-start(s32[32,8]{0,1:T(8,128)} %param.15) | copy-start | bytes 3076
  36.3 1.5 %collective-permute-start.4 = (bf16[256,128]{1,0:T(8,128)(2,1)S(1)}, bf16[256,128]{1,0:T(8,128)(2,1)S(1)}, u32[]{:S(2)}, u32[]{:S(2)}) collective-permute-start(bf16[256,128]{1,0:T(8,128)(2,1)S(1)} %get-tuple-element.21.refs_0_), channel_id=1, source_target_pairs={{0,1},{1,0},{2,3},{3,2},{4,5},{5,4},{6,7},{7,6},{8,9},{9,8},{10,11... | collective-permute-start | bytes 196616 | tf_op jit(solution)/shard_map/ppermute | solution.py:317
  38.7 19.7 %all-to-all-start.1 = ((bf16[16,48,128]{2,1,0:T(8,128)(2,1)}), bf16[16,48,128]{2,1,0:T(8,128)(2,1)S(1)}, u32[]{:S(2)}, u32[]{:S(2)}) async-start(bf16[16,48,128]{2,1,0:T(8,128)(2,1)} %compress_two.1._), calls=%async_computation.1 | async-start | bytes 393216 | tf_op jit(solution)/shard_map/all_to_all | solution.py:386
  42.2 5.9 %collective-permute-start.5 = (bf16[256,128]{1,0:T(8,128)(2,1)S(1)}, bf16[256,128]{1,0:T(8,128)(2,1)S(1)}, u32[]{:S(2)}, u32[]{:S(2)}) collective-permute-start(bf16[256,128]{1,0:T(8,128)(2,1)S(1)} %get-tuple-element.21.refs_0_), channel_id=1, source_target_pairs={{0,2},{1,3},{2,0},{3,1},{4,6},{5,7},{6,4},{7,5},{8,10},{9,11},{10,... | collective-permute-start | bytes 196616 | tf_op jit(solution)/shard_map/ppermute | solution.py:317
  44.0 8.6 %collective-permute-start.6 = (bf16[256,128]{1,0:T(8,128)(2,1)S(1)}, bf16[256,128]{1,0:T(8,128)(2,1)S(1)}, u32[]{:S(2)}, u32[]{:S(2)}) collective-permute-start(bf16[256,128]{1,0:T(8,128)(2,1)S(1)} %get-tuple-element.21.refs_0_), channel_id=1, source_target_pairs={{0,14},{1,15},{2,4},{3,5},{4,2},{5,3},{6,8},{7,9},{8,6},{9,7},{10,... | collective-permute-start | bytes 196616 | tf_op jit(solution)/shard_map/ppermute | solution.py:317
  52.6 1.4 %collective-permute-start.7 = (bf16[512,128]{1,0:T(8,128)(2,1)S(1)}, bf16[512,128]{1,0:T(8,128)(2,1)S(1)}, u32[]{:S(2)}, u32[]{:S(2)}) collective-permute-start(bf16[512,128]{1,0:T(8,128)(2,1)S(1)} %relay.3), channel_id=1, source_target_pairs={{0,1},{1,0},{2,3},{3,2},{4,5},{5,4},{6,7},{7,6},{8,9},{9,8},{10,11... | collective-permute-start | bytes 393224 | tf_op jit(solution)/shard_map/ppermute | solution.py:317

commit v6 on v5

--- a/solution.py
+++ b/solution.py
@@ -86,7 +86,7 @@
 
 
 def compress_kernel(per_group, pairs, *refs):
-    *fields, basis, _, payload = refs
+    *fields, basis, payload = refs
     clusters = fields[0].shape[0] // R
     tiles = [rows_of(fields[-1], j) for j in range(clusters)]
     sums = [
@@ -395,7 +395,7 @@
     payload_shape = shape(size, head + TAIL, LANES, dtype=bf16)
     payload = call(
         functools.partial(compress_kernel, per_group, [(0, 0)]), "compress_one", payload_shape,
-        [VMEM] * 2 + [ANY], field, basis, held[1],
+        [VMEM] * 2, field, basis,
     )
     got0 = exchange(payload)
 
@@ -436,6 +436,8 @@
     placed = jnp.where(live, window_place(distance, clusters), 6 * clusters).astype(jnp.int32)
     far_index = far_cols.T
 
+    near_cost = pl.CostEstimate(flops=32 * near_blocks.size, bytes_accessed=32 * near_blocks.size, transcendentals=0)
+
     def near_of(slabs):
         return call(
             near_kernel, "near", shape(rows, LANES), [VMEM] * len(slabs) + [SMEM, HBM], *slabs, placed, turned,
@@ -443,9 +445,7 @@
                 scratch(6 * rows + R, LANES), scratch(*turned_shape, dtype=bf16),
                 pltpu.SemaphoreType.DMA((8,)),
             ],
-            cost_estimate=pl.CostEstimate(
-                flops=32 * near_blocks.size, bytes_accessed=2 * near_blocks.size, transcendentals=0
-            ),
+            cost_estimate=near_cost,
         )
 
     kept = [scratch(size * head, LANES), scratch(rows, LANES)]
@@ -458,7 +458,7 @@
     held = sends_of(lowered)
     payload = call(
         functools.partial(compress_kernel, per_group, [(0, 1), (1, 1)]), "compress_two", payload_shape,
-        [VMEM] * 3 + [ANY], field, image, basis, held[1],
+        [VMEM] * 3, field, image, basis,
     )
     got1 = exchange(payload)
     near = near_of(held + [relayed(held, payload)])

time: 71.8 us -> 69.1 us (0.962)
  waiting for transfers between devices: 13.6 us -> 11.4 us
    ppermute x8, waiting for transfers between devices: 13.6 us -> 11.4 us  [swapped(): lax.ppermute(block, 'rows', [(i, partner(i)) for i in range(lax.axis_size...]
  transfers between devices with their start and end apart: 10 -> 10, of which waited for: 7 -> 5; matrix products, arithmetic and copies ran while one was open for 1% -> 1% of each run, Pallas kernels for 23% -> 24%
where the time goes in v6:
time: 69.1 us; the launch traced here: 68.7 us
  Pallas kernels  24.2 us (35%)
  starting transfers between devices  21.9 us (32%)
  waiting for transfers between devices  11.4 us (16%)
  blocking collectives  9.78 us (14%)
  between operations  0.76 us (1%)
  other arithmetic  0.72 us (1%)
    pallas_call x10, Pallas kernels, call(): pl.pallas_call(kernel, out_shape=out, in_specs=ins, out_specs=jax.tree.ma...  16.6 us
    ppermute x8, waiting for transfers between devices, swapped(): lax.ppermute(block, 'rows', [(i, partner(i)) for i in range(lax.axis_size...  11.4 us
    ppermute x8, starting transfers between devices, swapped(): lax.ppermute(block, 'rows', [(i, partner(i)) for i in range(lax.axis_size...  11 us
    all_to_all x2, starting transfers between devices, exchange(): return lax.all_to_all(block, 'rows', 0, 0)  10.9 us
    all_to_all x1, blocking collectives, exchange(): return lax.all_to_all(block, 'rows', 0, 0)  9.78 us
    pallas_call x1, Pallas kernels, on_device(): pl.pallas_call(prepare_kernel, out_shape=(shape(slots * rank, rank * clus...  7.52 us
  transfers between devices with their start and end apart: 10, of which 5 were waited for; matrix products, arithmetic and copies ran while one was open for 1% of the time, Pallas kernels for 24%

profile of v6, /device:TPU:0, one launch (start us, length us, event | category | flops | bytes accessed | tf_op | source)
XLA Modules:
  0.0 68.7 jit_solution(16975576055280000594)
XLA Ops:
  0.6 1.0 %start.1 = (f32[256,128]{1,0:T(8,128)S(1)}, bf16[512,128]{1,0:T(8,128)(2,1)S(1)}, bf16[256,128]{1,0:T(8,128)(2,1)S(1)}) custom-call(f32[8,4096]{1,0:T(8,128)} %b_hbm.1, bf16[512,128]{1,0:T(8,128)(2,1)} %bitcast.14), custom_call_target="tpu_custom_call" | custom-call | tf_op jit(solution)/shard_map/start/pallas_call | solution.py:379
  1.6 0.9 %compress_one.1._ = bf16[16,48,128]{2,1,0:T(8,128)(2,1)} custom-call(f32[256,128]{1,0:T(8,128)S(1)} %get-tuple-element.13.refs_0_.b, bf16[512,128]{1,0:T(8,128)(2,1)S(1)} %get-tuple-element.15.refs_1_.refs_2_), custom_call_target="tpu_custom_call" | custom-call | tf_op jit(solution)/shard_map/compress_one/pallas_call | solution.py:379
  2.5 7.4 %all-to-all-start = ((bf16[16,48,128]{2,1,0:T(8,128)(2,1)}), bf16[16,48,128]{2,1,0:T(8,128)(2,1)S(1)}, u32[]{:S(2)}, u32[]{:S(2)}) async-start(bf16[16,48,128]{2,1,0:T(8,128)(2,1)} %compress_one.1._), calls=%async_computation | async-start | bytes 393216 | tf_op jit(solution)/shard_map/all_to_all | solution.py:386
  9.9 1.9 %collective-permute-start.1 = (bf16[256,128]{1,0:T(8,128)(2,1)S(1)}, bf16[256,128]{1,0:T(8,128)(2,1)S(1)}, u32[]{:S(2)}, u32[]{:S(2)}) collective-permute-start(bf16[256,128]{1,0:T(8,128)(2,1)S(1)} %get-tuple-element.14.refs_0_), channel_id=1, source_target_pairs={{0,2},{1,3},{2,0},{3,1},{4,6},{5,7},{6,4},{7,5},{8,10},{9,11},{10,... | collective-permute-start | bytes 196616 | tf_op jit(solution)/shard_map/ppermute | solution.py:317
  11.8 3.3 %collective-permute-start.2 = (bf16[256,128]{1,0:T(8,128)(2,1)S(1)}, bf16[256,128]{1,0:T(8,128)(2,1)S(1)}, u32[]{:S(2)}, u32[]{:S(2)}) collective-permute-start(bf16[256,128]{1,0:T(8,128)(2,1)S(1)} %get-tuple-element.14.refs_0_), channel_id=1, source_target_pairs={{0,14},{1,15},{2,4},{3,5},{4,2},{5,3},{6,8},{7,9},{8,6},{9,7},{10,... | collective-permute-start | bytes 196616 | tf_op jit(solution)/shard_map/ppermute | solution.py:317
  15.1 0.8 %collective-permute-done.1.even.refs_2_ = bf16[256,128]{1,0:T(8,128)(2,1)S(1)} collective-permute-done((bf16[256,128]{1,0:T(8,128)(2,1)S(1)}, bf16[256,128]{1,0:T(8,128)(2,1)S(1)}, u32[]{:S(2)}, u32[]{:S(2)}) %collective-permute-start.1) | collective-permute-done | bytes 65568 | tf_op jit(solution)/shard_map/ppermute | solution.py:317
  15.9 4.4 %collective-permute-done.2.odd.refs_3_ = bf16[256,128]{1,0:T(8,128)(2,1)S(1)} collective-permute-done((bf16[256,128]{1,0:T(8,128)(2,1)S(1)}, bf16[256,128]{1,0:T(8,128)(2,1)S(1)}, u32[]{:S(2)}, u32[]{:S(2)}) %collective-permute-start.2) | collective-permute-done | bytes 65568 | tf_op jit(solution)/shard_map/ppermute | solution.py:317
  20.3 0.1 collective-permute-start.3
  20.4 0.7 %fusion.2.refs_5_ = s32[8,32]{1,0:T(8,128)S(1)} fusion(s32[32,8]{0,1:T(8,128)} %param.10, s32[]{:T(128)S(6)} %sub.24, s32[]{:T(128)S(6)} %select_n.67, s32[]{:T(128)S(6)} %select_n.66, s32[]{:T(128)S(6)} %add.49, s32[]{:T(128)S(6)} %mul.7, s32[32]{0:T(128)} %param.11), kind=kLoop, calls=%fused_computation.10 | loop fusion | flops 11776 | bytes 2196 | tf_op jit(solution)/shard_map/jit(_where)/select_n | solution.py:436
  21.1 7.5 %prepare.1 = (bf16[128,512]{1,0:T(8,128)(2,1)S(1)}, bf16[128,512]{1,0:T(8,128)(2,1)S(1)}, bf16[512,128]{1,0:T(8,128)(2,1)S(1)}, bf16[16,1024,256]{2,1,0:T(8,128)(2,1)}) custom-call(f32[8,16,16,32]{3,2,1,0:T(8,128)} %bitcast.12, bf16[512,128]{1,0:T(8,128)(2,1)} %bitcast.13, bf16[256,128,128]{2,1,0:T(8,128)(2,1)} %bitcast.11, bf16[16,48,128]{2,1,0:T(8,128)(2,1)} %compress_one.1._), custom_call_target="tpu_custom_call" | custom-call | bytes 16777216 | tf_op jit(solution)/shard_map/prepare/pallas_call | solution.py:409
  28.7 4.3 %near.2 = f32[256,128]{1,0:T(8,128)S(1)} custom-call(bf16[256,128]{1,0:T(8,128)(2,1)S(1)} %get-tuple-element.14.refs_0_, bf16[256,128]{1,0:T(8,128)(2,1)S(1)} %collective-permute-done.refs_1_, bf16[256,128]{1,0:T(8,128)(2,1)S(1)} %collective-permute-done.1.even.refs_2_, bf16[256,128]{1,0:T(8,128)(2,1)S(1)} %collective-permute-done.2.odd.refs_3_, ...), custom_call_target="tpu_custom_call" | custom-call | flops 134217728 | bytes 134217728 | tf_op jit(solution)/shard_map/near/pallas_call | solution.py:379
  33.0 2.0 %far_one.1 = (f32[256,128]{1,0:T(8,128)S(1)}, bf16[256,128]{1,0:T(8,128)(2,1)S(1)}) custom-call(f32[256,128]{1,0:T(8,128)S(1)} %get-tuple-element.13.refs_0_.b, f32[256,128]{1,0:T(8,128)S(1)} %near.2, bf16[16,48,128]{2,1,0:T(8,128)(2,1)S(1)} %all-to-all-done.got.got0, s32[8,32]{1,0:T(8,128)S(1)} %bitcast.9, bf16[128,512]{1,0:T(8,128)(2,1)S(1)} %get-tuple-element.17.high, ...), custom_call_target="tpu_custom_call" | custom-call | tf_op jit(solution)/shard_map/far_one/pallas_call | solution.py:379
  35.0 0.9 %compress_two.1._ = bf16[16,48,128]{2,1,0:T(8,128)(2,1)} custom-call(f32[256,128]{1,0:T(8,128)S(1)} %get-tuple-element.13.refs_0_.b, f32[256,128]{1,0:T(8,128)S(1)} %get-tuple-element.20.refs_1_.image, bf16[512,128]{1,0:T(8,128)(2,1)S(1)} %get-tuple-element.15.refs_1_.refs_2_), custom_call_target="tpu_custom_call" | custom-call | tf_op jit(solution)/shard_map/compress_two/pallas_call | solution.py:379
  35.9 3.5 %all-to-all-start.1 = ((bf16[16,48,128]{2,1,0:T(8,128)(2,1)}), bf16[16,48,128]{2,1,0:T(8,128)(2,1)S(1)}, u32[]{:S(2)}, u32[]{:S(2)}) async-start(bf16[16,48,128]{2,1,0:T(8,128)(2,1)} %compress_two.1._), calls=%async_computation.1 | async-start | bytes 393216 | tf_op jit(solution)/shard_map/all_to_all | solution.py:386
  39.4 1.8 %collective-permute-start.5 = (bf16[256,128]{1,0:T(8,128)(2,1)S(1)}, bf16[256,128]{1,0:T(8,128)(2,1)S(1)}, u32[]{:S(2)}, u32[]{:S(2)}) collective-permute-start(bf16[256,128]{1,0:T(8,128)(2,1)S(1)} %get-tuple-element.21.refs_0_), channel_id=1, source_target_pairs={{0,2},{1,3},{2,0},{3,1},{4,6},{5,7},{6,4},{7,5},{8,10},{9,11},{10,... | collective-permute-start | bytes 196616 | tf_op jit(solution)/shard_map/ppermute | solution.py:317
  41.2 3.3 %collective-permute-start.6 = (bf16[256,128]{1,0:T(8,128)(2,1)S(1)}, bf16[256,128]{1,0:T(8,128)(2,1)S(1)}, u32[]{:S(2)}, u32[]{:S(2)}) collective-permute-start(bf16[256,128]{1,0:T(8,128)(2,1)S(1)} %get-tuple-element.21.refs_0_), channel_id=1, source_target_pairs={{0,14},{1,15},{2,4},{3,5},{4,2},{5,3},{6,8},{7,9},{8,6},{9,7},{10,... | collective-permute-start | bytes 196616 | tf_op jit(solution)/shard_map/ppermute | solution.py:317
  44.6 0.7 %collective-permute-done.5.even.refs_2_ = bf16[256,128]{1,0:T(8,128)(2,1)S(1)} collective-permute-done((bf16[256,128]{1,0:T(8,128)(2,1)S(1)}, bf16[256,128]{1,0:T(8,128)(2,1)S(1)}, u32[]{:S(2)}, u32[]{:S(2)}) %collective-permute-start.5) | collective-permute-done | bytes 65568 | tf_op jit(solution)/shard_map/ppermute | solution.py:317
  45.3 4.5 %collective-permute-done.6.odd.refs_3_ = bf16[256,128]{1,0:T(8,128)(2,1)S(1)} collective-permute-done((bf16[256,128]{1,0:T(8,128)(2,1)S(1)}, bf16[256,128]{1,0:T(8,128)(2,1)S(1)}, u32[]{:S(2)}, u32[]{:S(2)}) %collective-permute-start.6) | collective-permute-done | bytes 65568 | tf_op jit(solution)/shard_map/ppermute | solution.py:317
  49.9 0.5 collective-permute-start.4
  50.4 0.9 %collective-permute-done.4.refs_1_ = bf16[256,128]{1,0:T(8,128)(2,1)S(1)} collective-permute-done((bf16[256,128]{1,0:T(8,128)(2,1)S(1)}, bf16[256,128]{1,0:T(8,128)(2,1)S(1)}, u32[]{:S(2)}, u32[]{:S(2)}) %collective-permute-start.4) | collective-permute-done | bytes 65568 | tf_op jit(solution)/shard_map/ppermute | solution.py:317
  51.4 4.3 %near.3 = f32[256,128]{1,0:T(8,128)S(1)} custom-call(bf16[256,128]{1,0:T(8,128)(2,1)S(1)} %get-tuple-element.21.refs_0_, bf16[256,128]{1,0:T(8,128)(2,1)S(1)} %collective-permute-done.4.refs_1_, bf16[256,128]{1,0:T(8,128)(2,1)S(1)} %collective-permute-done.5.even.refs_2_, bf16[256,128]{1,0:T(8,128)(2,1)S(1)} %collective-permute-done.6.odd.refs_3_, ...), custom_call_target="tpu_custom_call" | custom-call | flops 134217728 | bytes 134217728 | tf_op jit(solution)/shard_map/near/pallas_call | solution.py:379
  55.7 2.0 %far_two.1 = (f32[256,128]{1,0:T(8,128)S(1)}, f32[16,8,128]{2,1,0:T(8,128)S(1)}) custom-call(f32[256,128]{1,0:T(8,128)S(1)} %get-tuple-element.13.refs_0_.b, f32[256,128]{1,0:T(8,128)S(1)} %get-tuple-element.20.refs_1_.image, f32[256,128]{1,0:T(8,128)S(1)} %near.3, bf16[16,48,128]{2,1,0:T(8,128)(2,1)S(1)} %all-to-all-done.got.got0, ...), custom_call_target="tpu_custom_call" | custom-call | tf_op jit(solution)/shard_map/far_two/pallas_call | solution.py:379
  57.7 9.8 %all_to_all.15.got2 = f32[16,8,128]{2,1,0:T(8,128)S(1)} all-to-all(f32[16,8,128]{2,1,0:T(8,128)S(1)} %get-tuple-element.23), channel_id=1, replica_groups=mesh['groups'=2,'rows'=16] {'rows'}, dimensions={0} | all-to-all | bytes 131072 | tf_op jit(solution)/shard_map/all_to_all | solution.py:386
  67.5 1.2 %finish.1 = (f32[8,4096]{1,0:T(8,128)}, f32[8,4096]{1,0:T(8,128)}) custom-call(f32[256,128]{1,0:T(8,128)S(1)} %get-tuple-element.13.refs_0_.b, f32[256,128]{1,0:T(8,128)S(1)} %get-tuple-element.20.refs_1_.image, f32[256,128]{1,0:T(8,128)S(1)} %get-tuple-element.22.candidate, bf16[16,48,128]{2,1,0:T(8,128)(2,1)S(1)} %all-to-all-done.got.got0, ...), custom_call_target="tpu_custom_call" | custom-call | tf_op jit(solution)/shard_map/finish/pallas_call | solution.py:379
  (11 shorter events, 0.1 us)
Async XLA Ops:
  2.5 30.5 %all-to-all-start = ((bf16[16,48,128]{2,1,0:T(8,128)(2,1)}), bf16[16,48,128]{2,1,0:T(8,128)(2,1)S(1)}, u32[]{:S(2)}, u32[]{:S(2)}) async-start(bf16[16,48,128]{2,1,0:T(8,128)(2,1)} %compress_one.1._), calls=%async_computation | async-start | bytes 393216 | tf_op jit(solution)/shard_map/all_to_all | solution.py:386
  9.9 6.0 %collective-permute-start.1 = (bf16[256,128]{1,0:T(8,128)(2,1)S(1)}, bf16[256,128]{1,0:T(8,128)(2,1)S(1)}, u32[]{:S(2)}, u32[]{:S(2)}) collective-permute-start(bf16[256,128]{1,0:T(8,128)(2,1)S(1)} %get-tuple-element.14.refs_0_), channel_id=1, source_target_pairs={{0,2},{1,3},{2,0},{3,1},{4,6},{5,7},{6,4},{7,5},{8,10},{9,11},{10,... | collective-permute-start | bytes 196616 | tf_op jit(solution)/shard_map/ppermute | solution.py:317
  11.8 8.5 %collective-permute-start.2 = (bf16[256,128]{1,0:T(8,128)(2,1)S(1)}, bf16[256,128]{1,0:T(8,128)(2,1)S(1)}, u32[]{:S(2)}, u32[]{:S(2)}) collective-permute-start(bf16[256,128]{1,0:T(8,128)(2,1)S(1)} %get-tuple-element.14.refs_0_), channel_id=1, source_target_pairs={{0,14},{1,15},{2,4},{3,5},{4,2},{5,3},{6,8},{7,9},{8,6},{9,7},{10,... | collective-permute-start | bytes 196616 | tf_op jit(solution)/shard_map/ppermute | solution.py:317
  15.1 13.6 %collective-permute-start = (bf16[256,128]{1,0:T(8,128)(2,1)S(1)}, bf16[256,128]{1,0:T(8,128)(2,1)S(1)}, u32[]{:S(2)}, u32[]{:S(2)}) collective-permute-start(bf16[256,128]{1,0:T(8,128)(2,1)S(1)} %get-tuple-element.14.refs_0_), channel_id=1, source_target_pairs={{0,1},{1,0},{2,3},{3,2},{4,5},{5,4},{6,7},{7,6},{8,9},{9,8},{10,11... | collective-permute-start | bytes 196616 | tf_op jit(solution)/shard_map/ppermute | solution.py:317
  20.3 8.4 %collective-permute-start.3 = (bf16[512,128]{1,0:T(8,128)(2,1)S(1)}, bf16[512,128]{1,0:T(8,128)(2,1)S(1)}, u32[]{:S(2)}, u32[]{:S(2)}) collective-permute-start(bf16[512,128]{1,0:T(8,128)(2,1)S(1)} %relay.2), channel_id=1, source_target_pairs={{0,1},{1,0},{2,3},{3,2},{4,5},{5,4},{6,7},{7,6},{8,9},{9,8},{10,11... | collective-permute-start | bytes 393224 | tf_op jit(solution)/shard_map/ppermute | solution.py:317
  21.1 11.9 %copy-start = (s32[32,8]{0,1:T(8,128)S(1)}, s32[32,8]{0,1:T(8,128)}, u32[]{:S(2)}) copy-start(s32[32,8]{0,1:T(8,128)} %param.15) | copy-start | bytes 3076
  35.9 19.8 %all-to-all-start.1 = ((bf16[16,48,128]{2,1,0:T(8,128)(2,1)}), bf16[16,48,128]{2,1,0:T(8,128)(2,1)S(1)}, u32[]{:S(2)}, u32[]{:S(2)}) async-start(bf16[16,48,128]{2,1,0:T(8,128)(2,1)} %compress_two.1._), calls=%async_computation.1 | async-start | bytes 393216 | tf_op jit(solution)/shard_map/all_to_all | solution.py:386
  39.4 5.9 %collective-permute-start.5 = (bf16[256,128]{1,0:T(8,128)(2,1)S(1)}, bf16[256,128]{1,0:T(8,128)(2,1)S(1)}, u32[]{:S(2)}, u32[]{:S(2)}) collective-permute-start(bf16[256,128]{1,0:T(8,128)(2,1)S(1)} %get-tuple-element.21.refs_0_), channel_id=1, source_target_pairs={{0,2},{1,3},{2,0},{3,1},{4,6},{5,7},{6,4},{7,5},{8,10},{9,11},{10,... | collective-permute-start | bytes 196616 | tf_op jit(solution)/shard_map/ppermute | solution.py:317
  41.2 8.6 %collective-permute-start.6 = (bf16[256,128]{1,0:T(8,128)(2,1)S(1)}, bf16[256,128]{1,0:T(8,128)(2,1)S(1)}, u32[]{:S(2)}, u32[]{:S(2)}) collective-permute-start(bf16[256,128]{1,0:T(8,128)(2,1)S(1)} %get-tuple-element.21.refs_0_), channel_id=1, source_target_pairs={{0,14},{1,15},{2,4},{3,5},{4,2},{5,3},{6,8},{7,9},{8,6},{9,7},{10,... | collective-permute-start | bytes 196616 | tf_op jit(solution)/shard_map/ppermute | solution.py:317
  49.9 1.5 %collective-permute-start.7 = (bf16[512,128]{1,0:T(8,128)(2,1)S(1)}, bf16[512,128]{1,0:T(8,128)(2,1)S(1)}, u32[]{:S(2)}, u32[]{:S(2)}) collective-permute-start(bf16[512,128]{1,0:T(8,128)(2,1)S(1)} %relay.3), channel_id=1, source_target_pairs={{0,1},{1,0},{2,3},{3,2},{4,5},{5,4},{6,7},{7,6},{8,9},{9,8},{10,11... | collective-permute-start | bytes 393224 | tf_op jit(solution)/shard_map/ppermute | solution.py:317
  49.9 1.4 %collective-permute-start.4 = (bf16[256,128]{1,0:T(8,128)(2,1)S(1)}, bf16[256,128]{1,0:T(8,128)(2,1)S(1)}, u32[]{:S(2)}, u32[]{:S(2)}) collective-permute-start(bf16[256,128]{1,0:T(8,128)(2,1)S(1)} %get-tuple-element.21.refs_0_), channel_id=1, source_target_pairs={{0,1},{1,0},{2,3},{3,2},{4,5},{5,4},{6,7},{7,6},{8,9},{9,8},{10,11... | collective-permute-start | bytes 196616 | tf_op jit(solution)/shard_map/ppermute | solution.py:317

commit v7 on v6

--- a/solution.py
+++ b/solution.py
@@ -99,26 +99,14 @@
         payload[device] = block
 
 
-def prepare_kernel(
-    coupling_hbm, target_hbm, blocks_hbm, _, high_out, low_out, target_out, turned_hbm, coupling, target, blocks,
-    turned, block_sems, turned_sems, sems,
-):
-    others = [
+def prepare_kernel(coupling_hbm, target_hbm, _, high_out, low_out, target_out, coupling, target, sems):
+    copies = [
         pltpu.make_async_copy(coupling_hbm, coupling, sems.at[0]),
         pltpu.make_async_copy(target_hbm, target, sems.at[1]),
     ]
-    for copy in others:
+    for copy in copies:
         copy.start()
-    chunks = block_sems.shape[0]
-    rows = blocks.shape[0] // chunks
-
-    def copy_of(chunk):
-        span = pl.ds(chunk * rows, rows)
-        return pltpu.make_async_copy(blocks_hbm.at[span], blocks.at[span], block_sems.at[chunk])
-
-    for chunk in range(chunks):
-        copy_of(chunk).start()
-    for copy in others:
+    for copy in copies:
         copy.wait()
     slots, rank, _, clusters = coupling.shape
     per_tile = LANES // clusters
@@ -135,27 +123,6 @@
     column = lax.broadcasted_iota(jnp.int32, (size, size), 1)
     wanted = (row % clusters) * rank + row // clusters
     target_out[...] = dot((column == wanted).astype(bf16), target[...]).astype(bf16)
-
-    pairs_each = rows // (2 * slots)
-
-    def copy_out(chunk):
-        span = pl.ds(chunk * pairs_each, pairs_each)
-        return pltpu.make_async_copy(turned.at[span], turned_hbm.at[span], turned_sems.at[chunk])
-
-    def body(chunk, carry):
-        copy_of(chunk).wait()
-        for inner in range(pairs_each):
-            pair = chunk * pairs_each + inner
-            for k in range(slots):
-                for side in range(2):
-                    block = blocks[(2 * pair + side) * slots + k]
-                    turned[pair, k * LANES : (k + 1) * LANES, side * LANES : (side + 1) * LANES] = block.T
-        copy_out(chunk).start()
-        return carry
-
-    lax.fori_loop(0, chunks, body, 0)
-    for chunk in range(chunks):
-        copy_out(chunk).wait()
 
 
 def far_field(got, far_cols, high, low, target, table, clusters, rank, far):
@@ -200,14 +167,14 @@
 
 
 def near_kernel(*refs):
-    *slabs, placed, turned_hbm, near, window, turned, sems = refs
+    *slabs, placed, blocks_hbm, near, window, blocks, sems = refs
     slots, clusters = placed.shape
     chunks = sems.shape[0]
-    pairs_each = turned.shape[0] // chunks
+    each = clusters // chunks
 
     def copy_of(chunk):
-        span = pl.ds(chunk * pairs_each, pairs_each)
-        return pltpu.make_async_copy(turned_hbm.at[span], turned.at[span], sems.at[chunk])
+        span = pl.ds(chunk * each * slots, each * slots)
+        return pltpu.make_async_copy(blocks_hbm.at[span], blocks.at[span], sems.at[chunk])
 
     for chunk in range(chunks):
         copy_of(chunk).start()
@@ -220,16 +187,23 @@
     def fetch(k, i):
         return window[pl.ds(pl.multiple_of(placed[k, i] * R, R), R), :]
 
-    for pair in range(clusters // 2):
-        if pair % pairs_each == 0:
-            copy_of(pair // pairs_each).wait()
-        sources = [
-            jnp.concatenate([fetch(k, 2 * pair), fetch(k, 2 * pair + 1)], axis=0).astype(bf16)
-            for k in range(slots)
-        ]
-        both = dot(jnp.concatenate(sources, axis=1), turned[pair])
-        near[pl.ds(2 * pair * R, R), :] = both[:R, :LANES]
-        near[pl.ds((2 * pair + 1) * R, R), :] = both[R:, LANES:]
+    def block(k, i):
+        return blocks[i * slots + k]
+
+    for i in range(0, clusters, 2):
+        if i % each == 0:
+            copy_of(i // each).wait()
+        both = jnp.zeros((2 * R, 2 * LANES), f32)
+        for k in range(0, slots, 2):
+            sources = jnp.concatenate(
+                [jnp.concatenate([fetch(k + n, i), fetch(k + n, i + 1)], axis=0) for n in range(2)], axis=1
+            )
+            weights = jnp.concatenate(
+                [jnp.concatenate([block(k + n, i), block(k + n, i + 1)], axis=0) for n in range(2)], axis=1
+            )
+            both = both + dot(sources.astype(bf16), weights, (1, 1))
+        near[pl.ds(i * R, R), :] = both[:R, :LANES]
+        near[pl.ds((i + 1) * R, R), :] = both[R:, LANES:]
 
 
 def norm_parts(sums):
@@ -392,10 +366,11 @@
         scratch_shapes=[scratch(R, width), pltpu.SemaphoreType.DMA((2,))],
     )
     held = sends_of(lowered)
+    compress_cost = pl.CostEstimate(flops=0, bytes_accessed=64 * basis.size * rank, transcendentals=0)
     payload_shape = shape(size, head + TAIL, LANES, dtype=bf16)
     payload = call(
         functools.partial(compress_kernel, per_group, [(0, 0)]), "compress_one", payload_shape,
-        [VMEM] * 2, field, basis,
+        [VMEM] * 2, field, basis, cost_estimate=compress_cost,
     )
     got0 = exchange(payload)
 
@@ -405,30 +380,21 @@
         )
         return swapped(both, core_mate)
 
-    turned_shape = (clusters // 2, slots * LANES, 2 * LANES)
-    high, low, target, turned = pl.pallas_call(
-        prepare_kernel,
-        out_shape=(
+    high, low, target = call(
+        prepare_kernel, "prepare",
+        (
             shape(slots * rank, rank * clusters, dtype=bf16),
             shape(slots * rank, rank * clusters, dtype=bf16),
             shape(rank * clusters, LANES, dtype=bf16),
-            pltpu.HBM(turned_shape, bf16),
         ),
-        in_specs=[HBM] * 3 + [ANY], out_specs=[VMEM] * 3 + [HBM],
+        [HBM] * 2 + [ANY],
+        in_hbm(jnp.transpose(coupling, (1, 2, 3, 0))), in_hbm(target_basis.reshape(clusters * rank, LANES)), payload,
         scratch_shapes=[
             scratch(slots, rank, rank, clusters), scratch(clusters * rank, LANES, dtype=bf16),
-            scratch(clusters * slots, LANES, LANES, dtype=bf16), scratch(*turned_shape, dtype=bf16),
-            pltpu.SemaphoreType.DMA((8,)), pltpu.SemaphoreType.DMA((8,)), pltpu.SemaphoreType.DMA((2,)),
+            pltpu.SemaphoreType.DMA((2,)),
         ],
-        compiler_params=PARAMS, name="prepare",
-        cost_estimate=pl.CostEstimate(flops=0, bytes_accessed=4 * near_blocks.size, transcendentals=0),
-    )(
-        in_hbm(jnp.transpose(coupling, (1, 2, 3, 0))),
-        in_hbm(target_basis.reshape(clusters * rank, LANES)),
-        in_hbm(near_blocks.reshape(clusters * slots, LANES, LANES)),
-        payload,
-    )
-    turned = in_hbm(turned)
+    )
+    blocks = in_hbm(near_blocks.reshape(clusters * slots, LANES, LANES))
     reach = 2 * clusters
     start = lax.axis_index("rows") * clusters
     distance = (near_cols.T - start + reach) % every
@@ -440,9 +406,9 @@
 
     def near_of(slabs):
         return call(
-            near_kernel, "near", shape(rows, LANES), [VMEM] * len(slabs) + [SMEM, HBM], *slabs, placed, turned,
+            near_kernel, "near", shape(rows, LANES), [VMEM] * len(slabs) + [SMEM, HBM], *slabs, placed, blocks,
             scratch_shapes=[
-                scratch(6 * rows + R, LANES), scratch(*turned_shape, dtype=bf16),
+                scratch(6 * rows + R, LANES), scratch(*blocks.shape, dtype=bf16),
                 pltpu.SemaphoreType.DMA((8,)),
             ],
             cost_estimate=near_cost,
@@ -458,7 +424,7 @@
     held = sends_of(lowered)
     payload = call(
         functools.partial(compress_kernel, per_group, [(0, 1), (1, 1)]), "compress_two", payload_shape,
-        [VMEM] * 3, field, image, basis,
+        [VMEM] * 3, field, image, basis, cost_estimate=compress_cost,
     )
     got1 = exchange(payload)
     near = near_of(held + [relayed(held, payload)])

time: 69.1 us -> 64.6 us (0.935)
  Pallas kernels: 24.2 us -> 19.6 us
    pallas_call x1 -> x0, Pallas kernels: 7.52 us -> none  [on_device(): pl.pallas_call(prepare_kernel, out_shape=(shape(slots * rank, rank * clus...]
    pallas_call x10 -> x11, Pallas kernels: 16.6 us -> 19.6 us  [call(): pl.pallas_call(kernel, out_shape=out, in_specs=ins, out_specs=jax.tree.ma...]
  transfers between devices with their start and end apart: 10 -> 10, of which waited for: 5 -> 5; matrix products, arithmetic and copies ran while one was open for 1% -> 1% of each run, Pallas kernels for 24% -> 18%
where the time goes in v7:
time: 64.6 us; the launch traced here: 64.2 us
  starting transfers between devices  21.9 us (34%)
  Pallas kernels  19.6 us (30%)
  waiting for transfers between devices  11.4 us (18%)
  blocking collectives  9.78 us (15%)
  between operations  0.76 us (1%)
  other arithmetic  0.72 us (1%)
    pallas_call x11, Pallas kernels, call(): pl.pallas_call(kernel, out_shape=out, in_specs=ins, out_specs=jax.tree.ma...  19.6 us
    ppermute x8, waiting for transfers between devices, swapped(): lax.ppermute(block, 'rows', [(i, partner(i)) for i in range(lax.axis_size...  11.4 us
    ppermute x8, starting transfers between devices, swapped(): lax.ppermute(block, 'rows', [(i, partner(i)) for i in range(lax.axis_size...  11 us
    all_to_all x2, starting transfers between devices, exchange(): return lax.all_to_all(block, 'rows', 0, 0)  10.9 us
    all_to_all x1, blocking collectives, exchange(): return lax.all_to_all(block, 'rows', 0, 0)  9.78 us
  transfers between devices with their start and end apart: 10, of which 5 were waited for; matrix products, arithmetic and copies ran while one was open for 1% of the time, Pallas kernels for 18%

profile of v7, /device:TPU:0, one launch (start us, length us, event | category | flops | bytes accessed | tf_op | source)
XLA Modules:
  0.0 64.2 jit_solution(3096369064184919444)
XLA Ops:
  0.6 1.0 %start.1 = (f32[256,128]{1,0:T(8,128)S(1)}, bf16[512,128]{1,0:T(8,128)(2,1)S(1)}, bf16[256,128]{1,0:T(8,128)(2,1)S(1)}) custom-call(f32[8,4096]{1,0:T(8,128)} %b_hbm.1, bf16[512,128]{1,0:T(8,128)(2,1)} %bitcast.14), custom_call_target="tpu_custom_call" | custom-call | tf_op jit(solution)/shard_map/start/pallas_call | solution.py:353
  1.6 0.9 %compress_one.1._ = bf16[16,48,128]{2,1,0:T(8,128)(2,1)} custom-call(f32[256,128]{1,0:T(8,128)S(1)} %get-tuple-element.12.refs_0_.b, bf16[512,128]{1,0:T(8,128)(2,1)S(1)} %get-tuple-element.14.refs_1_.refs_2_), custom_call_target="tpu_custom_call" | custom-call | bytes 67108864 | tf_op jit(solution)/shard_map/compress_one/pallas_call | solution.py:353
  2.5 7.4 %all-to-all-start = ((bf16[16,48,128]{2,1,0:T(8,128)(2,1)}), bf16[16,48,128]{2,1,0:T(8,128)(2,1)S(1)}, u32[]{:S(2)}, u32[]{:S(2)}) async-start(bf16[16,48,128]{2,1,0:T(8,128)(2,1)} %compress_one.1._), calls=%async_computation | async-start | bytes 393216 | tf_op jit(solution)/shard_map/all_to_all | solution.py:360
  9.9 1.9 %collective-permute-start.1 = (bf16[256,128]{1,0:T(8,128)(2,1)S(1)}, bf16[256,128]{1,0:T(8,128)(2,1)S(1)}, u32[]{:S(2)}, u32[]{:S(2)}) collective-permute-start(bf16[256,128]{1,0:T(8,128)(2,1)S(1)} %get-tuple-element.13.refs_0_), channel_id=1, source_target_pairs={{0,2},{1,3},{2,0},{3,1},{4,6},{5,7},{6,4},{7,5},{8,10},{9,11},{10,... | collective-permute-start | bytes 196616 | tf_op jit(solution)/shard_map/ppermute | solution.py:291
  11.9 3.3 %collective-permute-start.2 = (bf16[256,128]{1,0:T(8,128)(2,1)S(1)}, bf16[256,128]{1,0:T(8,128)(2,1)S(1)}, u32[]{:S(2)}, u32[]{:S(2)}) collective-permute-start(bf16[256,128]{1,0:T(8,128)(2,1)S(1)} %get-tuple-element.13.refs_0_), channel_id=1, source_target_pairs={{0,14},{1,15},{2,4},{3,5},{4,2},{5,3},{6,8},{7,9},{8,6},{9,7},{10,... | collective-permute-start | bytes 196616 | tf_op jit(solution)/shard_map/ppermute | solution.py:291
  15.1 0.8 %collective-permute-done.1.even.refs_2_ = bf16[256,128]{1,0:T(8,128)(2,1)S(1)} collective-permute-done((bf16[256,128]{1,0:T(8,128)(2,1)S(1)}, bf16[256,128]{1,0:T(8,128)(2,1)S(1)}, u32[]{:S(2)}, u32[]{:S(2)}) %collective-permute-start.1) | collective-permute-done | bytes 65568 | tf_op jit(solution)/shard_map/ppermute | solution.py:291
  15.9 4.4 %collective-permute-done.2.odd.refs_3_ = bf16[256,128]{1,0:T(8,128)(2,1)S(1)} collective-permute-done((bf16[256,128]{1,0:T(8,128)(2,1)S(1)}, bf16[256,128]{1,0:T(8,128)(2,1)S(1)}, u32[]{:S(2)}, u32[]{:S(2)}) %collective-permute-start.2) | collective-permute-done | bytes 65568 | tf_op jit(solution)/shard_map/ppermute | solution.py:291
  20.3 0.1 collective-permute-start.3
  20.4 0.7 %fusion.2.refs_5_ = s32[8,32]{1,0:T(8,128)S(1)} fusion(s32[32,8]{0,1:T(8,128)} %param.10, s32[]{:T(128)S(6)} %sub.24, s32[]{:T(128)S(6)} %select_n.67, s32[]{:T(128)S(6)} %select_n.66, s32[]{:T(128)S(6)} %add.49, s32[]{:T(128)S(6)} %mul.7, s32[32]{0:T(128)} %param.11), kind=kLoop, calls=%fused_computation.10 | loop fusion | flops 11776 | bytes 2196 | tf_op jit(solution)/shard_map/jit(_where)/select_n | solution.py:402
  21.1 1.6 %prepare.1 = (bf16[128,512]{1,0:T(8,128)(2,1)S(1)}, bf16[128,512]{1,0:T(8,128)(2,1)S(1)}, bf16[512,128]{1,0:T(8,128)(2,1)S(1)}) custom-call(f32[8,16,16,32]{3,2,1,0:T(8,128)} %bitcast.13, bf16[512,128]{1,0:T(8,128)(2,1)} %bitcast.15, bf16[16,48,128]{2,1,0:T(8,128)(2,1)} %compress_one.1._), custom_call_target="tpu_custom_call" | custom-call | tf_op jit(solution)/shard_map/prepare/pallas_call | solution.py:353
  22.7 5.0 %near.2 = f32[256,128]{1,0:T(8,128)S(1)} custom-call(bf16[256,128]{1,0:T(8,128)(2,1)S(1)} %get-tuple-element.13.refs_0_, bf16[256,128]{1,0:T(8,128)(2,1)S(1)} %collective-permute-done.refs_1_, bf16[256,128]{1,0:T(8,128)(2,1)S(1)} %collective-permute-done.1.even.refs_2_, bf16[256,128]{1,0:T(8,128)(2,1)S(1)} %collective-permute-done.2.odd.refs_3_, ...), custom_call_target="tpu_custom_call" | custom-call | flops 134217728 | bytes 134217728 | tf_op jit(solution)/shard_map/near/pallas_call | solution.py:353
  27.8 2.0 %far_one.1 = (f32[256,128]{1,0:T(8,128)S(1)}, bf16[256,128]{1,0:T(8,128)(2,1)S(1)}) custom-call(f32[256,128]{1,0:T(8,128)S(1)} %get-tuple-element.12.refs_0_.b, f32[256,128]{1,0:T(8,128)S(1)} %near.2, bf16[16,48,128]{2,1,0:T(8,128)(2,1)S(1)} %all-to-all-done.got.got0, s32[8,32]{1,0:T(8,128)S(1)} %bitcast.9, bf16[128,512]{1,0:T(8,128)(2,1)S(1)} %get-tuple-element.15.high, ...), custom_call_target="tpu_custom_call" | custom-call | tf_op jit(solution)/shard_map/far_one/pallas_call | solution.py:353
  29.7 0.9 %compress_two.1._ = bf16[16,48,128]{2,1,0:T(8,128)(2,1)} custom-call(f32[256,128]{1,0:T(8,128)S(1)} %get-tuple-element.12.refs_0_.b, f32[256,128]{1,0:T(8,128)S(1)} %get-tuple-element.18.refs_1_.image, bf16[512,128]{1,0:T(8,128)(2,1)S(1)} %get-tuple-element.14.refs_1_.refs_2_), custom_call_target="tpu_custom_call" | custom-call | bytes 67108864 | tf_op jit(solution)/shard_map/compress_two/pallas_call | solution.py:353
  30.6 3.5 %all-to-all-start.1 = ((bf16[16,48,128]{2,1,0:T(8,128)(2,1)}), bf16[16,48,128]{2,1,0:T(8,128)(2,1)S(1)}, u32[]{:S(2)}, u32[]{:S(2)}) async-start(bf16[16,48,128]{2,1,0:T(8,128)(2,1)} %compress_two.1._), calls=%async_computation.1 | async-start | bytes 393216 | tf_op jit(solution)/shard_map/all_to_all | solution.py:360
  34.2 1.8 %collective-permute-start.5 = (bf16[256,128]{1,0:T(8,128)(2,1)S(1)}, bf16[256,128]{1,0:T(8,128)(2,1)S(1)}, u32[]{:S(2)}, u32[]{:S(2)}) collective-permute-start(bf16[256,128]{1,0:T(8,128)(2,1)S(1)} %get-tuple-element.19.refs_0_), channel_id=1, source_target_pairs={{0,2},{1,3},{2,0},{3,1},{4,6},{5,7},{6,4},{7,5},{8,10},{9,11},{10,... | collective-permute-start | bytes 196616 | tf_op jit(solution)/shard_map/ppermute | solution.py:291
  36.0 3.3 %collective-permute-start.6 = (bf16[256,128]{1,0:T(8,128)(2,1)S(1)}, bf16[256,128]{1,0:T(8,128)(2,1)S(1)}, u32[]{:S(2)}, u32[]{:S(2)}) collective-permute-start(bf16[256,128]{1,0:T(8,128)(2,1)S(1)} %get-tuple-element.19.refs_0_), channel_id=1, source_target_pairs={{0,14},{1,15},{2,4},{3,5},{4,2},{5,3},{6,8},{7,9},{8,6},{9,7},{10,... | collective-permute-start | bytes 196616 | tf_op jit(solution)/shard_map/ppermute | solution.py:291
  39.3 0.7 %collective-permute-done.5.even.refs_2_ = bf16[256,128]{1,0:T(8,128)(2,1)S(1)} collective-permute-done((bf16[256,128]{1,0:T(8,128)(2,1)S(1)}, bf16[256,128]{1,0:T(8,128)(2,1)S(1)}, u32[]{:S(2)}, u32[]{:S(2)}) %collective-permute-start.5) | collective-permute-done | bytes 65568 | tf_op jit(solution)/shard_map/ppermute | solution.py:291
  40.0 4.5 %collective-permute-done.6.odd.refs_3_ = bf16[256,128]{1,0:T(8,128)(2,1)S(1)} collective-permute-done((bf16[256,128]{1,0:T(8,128)(2,1)S(1)}, bf16[256,128]{1,0:T(8,128)(2,1)S(1)}, u32[]{:S(2)}, u32[]{:S(2)}) %collective-permute-start.6) | collective-permute-done | bytes 65568 | tf_op jit(solution)/shard_map/ppermute | solution.py:291
  44.7 0.5 collective-permute-start.4
  45.2 0.9 %collective-permute-done.4.refs_1_ = bf16[256,128]{1,0:T(8,128)(2,1)S(1)} collective-permute-done((bf16[256,128]{1,0:T(8,128)(2,1)S(1)}, bf16[256,128]{1,0:T(8,128)(2,1)S(1)}, u32[]{:S(2)}, u32[]{:S(2)}) %collective-permute-start.4) | collective-permute-done | bytes 65568 | tf_op jit(solution)/shard_map/ppermute | solution.py:291
  46.1 5.0 %near.3 = f32[256,128]{1,0:T(8,128)S(1)} custom-call(bf16[256,128]{1,0:T(8,128)(2,1)S(1)} %get-tuple-element.19.refs_0_, bf16[256,128]{1,0:T(8,128)(2,1)S(1)} %collective-permute-done.4.refs_1_, bf16[256,128]{1,0:T(8,128)(2,1)S(1)} %collective-permute-done.5.even.refs_2_, bf16[256,128]{1,0:T(8,128)(2,1)S(1)} %collective-permute-done.6.odd.refs_3_, ...), custom_call_target="tpu_custom_call" | custom-call | flops 134217728 | bytes 134217728 | tf_op jit(solution)/shard_map/near/pallas_call | solution.py:353
  51.1 2.0 %far_two.1 = (f32[256,128]{1,0:T(8,128)S(1)}, f32[16,8,128]{2,1,0:T(8,128)S(1)}) custom-call(f32[256,128]{1,0:T(8,128)S(1)} %get-tuple-element.12.refs_0_.b, f32[256,128]{1,0:T(8,128)S(1)} %get-tuple-element.18.refs_1_.image, f32[256,128]{1,0:T(8,128)S(1)} %near.3, bf16[16,48,128]{2,1,0:T(8,128)(2,1)S(1)} %all-to-all-done.got.got0, ...), custom_call_target="tpu_custom_call" | custom-call | tf_op jit(solution)/shard_map/far_two/pallas_call | solution.py:353
  53.2 9.8 %all_to_all.15.got2 = f32[16,8,128]{2,1,0:T(8,128)S(1)} all-to-all(f32[16,8,128]{2,1,0:T(8,128)S(1)} %get-tuple-element.21), channel_id=1, replica_groups=mesh['groups'=2,'rows'=16] {'rows'}, dimensions={0} | all-to-all | bytes 131072 | tf_op jit(solution)/shard_map/all_to_all | solution.py:360
  63.0 1.2 %finish.1 = (f32[8,4096]{1,0:T(8,128)}, f32[8,4096]{1,0:T(8,128)}) custom-call(f32[256,128]{1,0:T(8,128)S(1)} %get-tuple-element.12.refs_0_.b, f32[256,128]{1,0:T(8,128)S(1)} %get-tuple-element.18.refs_1_.image, f32[256,128]{1,0:T(8,128)S(1)} %get-tuple-element.20.candidate, bf16[16,48,128]{2,1,0:T(8,128)(2,1)S(1)} %all-to-all-done.got.got0, ...), custom_call_target="tpu_custom_call" | custom-call | tf_op jit(solution)/shard_map/finish/pallas_call | solution.py:353
  (11 shorter events, 0.1 us)
Async XLA Ops:
  0.6 27.1 %copy-start = (s32[32,8]{0,1:T(8,128)S(1)}, s32[32,8]{0,1:T(8,128)}, u32[]{:S(2)}) copy-start(s32[32,8]{0,1:T(8,128)} %param.15) | copy-start | bytes 3076
  2.5 25.2 %all-to-all-start = ((bf16[16,48,128]{2,1,0:T(8,128)(2,1)}), bf16[16,48,128]{2,1,0:T(8,128)(2,1)S(1)}, u32[]{:S(2)}, u32[]{:S(2)}) async-start(bf16[16,48,128]{2,1,0:T(8,128)(2,1)} %compress_one.1._), calls=%async_computation | async-start | bytes 393216 | tf_op jit(solution)/shard_map/all_to_all | solution.py:360
  9.9 6.0 %collective-permute-start.1 = (bf16[256,128]{1,0:T(8,128)(2,1)S(1)}, bf16[256,128]{1,0:T(8,128)(2,1)S(1)}, u32[]{:S(2)}, u32[]{:S(2)}) collective-permute-start(bf16[256,128]{1,0:T(8,128)(2,1)S(1)} %get-tuple-element.13.refs_0_), channel_id=1, source_target_pairs={{0,2},{1,3},{2,0},{3,1},{4,6},{5,7},{6,4},{7,5},{8,10},{9,11},{10,... | collective-permute-start | bytes 196616 | tf_op jit(solution)/shard_map/ppermute | solution.py:291
  11.9 8.5 %collective-permute-start.2 = (bf16[256,128]{1,0:T(8,128)(2,1)S(1)}, bf16[256,128]{1,0:T(8,128)(2,1)S(1)}, u32[]{:S(2)}, u32[]{:S(2)}) collective-permute-start(bf16[256,128]{1,0:T(8,128)(2,1)S(1)} %get-tuple-element.13.refs_0_), channel_id=1, source_target_pairs={{0,14},{1,15},{2,4},{3,5},{4,2},{5,3},{6,8},{7,9},{8,6},{9,7},{10,... | collective-permute-start | bytes 196616 | tf_op jit(solution)/shard_map/ppermute | solution.py:291
  15.1 7.6 %collective-permute-start = (bf16[256,128]{1,0:T(8,128)(2,1)S(1)}, bf16[256,128]{1,0:T(8,128)(2,1)S(1)}, u32[]{:S(2)}, u32[]{:S(2)}) collective-permute-start(bf16[256,128]{1,0:T(8,128)(2,1)S(1)} %get-tuple-element.13.refs_0_), channel_id=1, source_target_pairs={{0,1},{1,0},{2,3},{3,2},{4,5},{5,4},{6,7},{7,6},{8,9},{9,8},{10,11... | collective-permute-start | bytes 196616 | tf_op jit(solution)/shard_map/ppermute | solution.py:291
  20.3 2.4 %collective-permute-start.3 = (bf16[512,128]{1,0:T(8,128)(2,1)S(1)}, bf16[512,128]{1,0:T(8,128)(2,1)S(1)}, u32[]{:S(2)}, u32[]{:S(2)}) collective-permute-start(bf16[512,128]{1,0:T(8,128)(2,1)S(1)} %relay.2), channel_id=1, source_target_pairs={{0,1},{1,0},{2,3},{3,2},{4,5},{5,4},{6,7},{7,6},{8,9},{9,8},{10,11... | collective-permute-start | bytes 393224 | tf_op jit(solution)/shard_map/ppermute | solution.py:291
  30.6 20.5 %all-to-all-start.1 = ((bf16[16,48,128]{2,1,0:T(8,128)(2,1)}), bf16[16,48,128]{2,1,0:T(8,128)(2,1)S(1)}, u32[]{:S(2)}, u32[]{:S(2)}) async-start(bf16[16,48,128]{2,1,0:T(8,128)(2,1)} %compress_two.1._), calls=%async_computation.1 | async-start | bytes 393216 | tf_op jit(solution)/shard_map/all_to_all | solution.py:360
  34.2 5.9 %collective-permute-start.5 = (bf16[256,128]{1,0:T(8,128)(2,1)S(1)}, bf16[256,128]{1,0:T(8,128)(2,1)S(1)}, u32[]{:S(2)}, u32[]{:S(2)}) collective-permute-start(bf16[256,128]{1,0:T(8,128)(2,1)S(1)} %get-tuple-element.19.refs_0_), channel_id=1, source_target_pairs={{0,2},{1,3},{2,0},{3,1},{4,6},{5,7},{6,4},{7,5},{8,10},{9,11},{10,... | collective-permute-start | bytes 196616 | tf_op jit(solution)/shard_map/ppermute | solution.py:291
  36.0 8.6 %collective-permute-start.6 = (bf16[256,128]{1,0:T(8,128)(2,1)S(1)}, bf16[256,128]{1,0:T(8,128)(2,1)S(1)}, u32[]{:S(2)}, u32[]{:S(2)}) collective-permute-start(bf16[256,128]{1,0:T(8,128)(2,1)S(1)} %get-tuple-element.19.refs_0_), channel_id=1, source_target_pairs={{0,14},{1,15},{2,4},{3,5},{4,2},{5,3},{6,8},{7,9},{8,6},{9,7},{10,... | collective-permute-start | bytes 196616 | tf_op jit(solution)/shard_map/ppermute | solution.py:291
  44.6 1.5 %collective-permute-start.7 = (bf16[512,128]{1,0:T(8,128)(2,1)S(1)}, bf16[512,128]{1,0:T(8,128)(2,1)S(1)}, u32[]{:S(2)}, u32[]{:S(2)}) collective-permute-start(bf16[512,128]{1,0:T(8,128)(2,1)S(1)} %relay.3), channel_id=1, source_target_pairs={{0,1},{1,0},{2,3},{3,2},{4,5},{5,4},{6,7},{7,6},{8,9},{9,8},{10,11... | collective-permute-start | bytes 393224 | tf_op jit(solution)/shard_map/ppermute | solution.py:291
  44.7 1.4 %collective-permute-start.4 = (bf16[256,128]{1,0:T(8,128)(2,1)S(1)}, bf16[256,128]{1,0:T(8,128)(2,1)S(1)}, u32[]{:S(2)}, u32[]{:S(2)}) collective-permute-start(bf16[256,128]{1,0:T(8,128)(2,1)S(1)} %get-tuple-element.19.refs_0_), channel_id=1, source_target_pairs={{0,1},{1,0},{2,3},{3,2},{4,5},{5,4},{6,7},{7,6},{8,9},{9,8},{10,11... | collective-permute-start | bytes 196616 | tf_op jit(solution)/shard_map/ppermute | solution.py:291

commit v8 on v7

--- a/solution.py
+++ b/solution.py
@@ -70,36 +70,31 @@
     return tile
 
 
-def start_kernel(b_hbm, basis_hbm, field, basis, lowered, b, sems):
+def write_payload(payload, tiles, sums, basis, per_group):
+    groups = len(tiles) // per_group
+    parts = [compress(tiles[g * per_group : (g + 1) * per_group], basis, g) for g in range(groups)]
+    block = jnp.concatenate([jnp.concatenate(parts, axis=0).astype(bf16), sums_tile(sums)], axis=0)
+    for device in range(payload.shape[0]):
+        payload[device] = block
+
+
+def start_kernel(per_group, b_hbm, basis_hbm, field, basis, lowered, payload, b, sems):
     copies = [
         pltpu.make_async_copy(b_hbm, b, sems.at[0]),
         pltpu.make_async_copy(basis_hbm, basis, sems.at[1]),
     ]
     for copy in copies:
         copy.start()
-    copies[0].wait()
+    for copy in copies:
+        copy.wait()
     clusters = b.shape[1] // LANES
-    tiles = jnp.concatenate([b[:, j * LANES : (j + 1) * LANES] for j in range(clusters)], axis=0)
-    field[...] = tiles
-    lowered[...] = tiles.astype(bf16)
-    copies[1].wait()
-
-
-def compress_kernel(per_group, pairs, *refs):
-    *fields, basis, payload = refs
-    clusters = fields[0].shape[0] // R
-    tiles = [rows_of(fields[-1], j) for j in range(clusters)]
-    sums = [
-        sum(rows_of(fields[f], j) * rows_of(fields[g], j) for j in range(clusters)) for f, g in pairs
-    ]
-    groups = clusters // per_group
-    parts = [compress(tiles[g * per_group : (g + 1) * per_group], basis, g) for g in range(groups)]
-    block = jnp.concatenate([jnp.concatenate(parts, axis=0).astype(bf16), sums_tile(sums)], axis=0)
-    for device in range(payload.shape[0]):
-        payload[device] = block
-
-
-def prepare_kernel(coupling_hbm, target_hbm, _, high_out, low_out, target_out, coupling, target, sems):
+    tiles = [b[:, j * LANES : (j + 1) * LANES] for j in range(clusters)]
+    field[...] = jnp.concatenate(tiles, axis=0)
+    lowered[...] = jnp.concatenate(tiles, axis=0).astype(bf16)
+    write_payload(payload, tiles, [sum(t * t for t in tiles)], basis, per_group)
+
+
+def prepare_kernel(coupling_hbm, target_hbm, _, __, high_out, low_out, target_out, coupling, target, sems):
     copies = [
         pltpu.make_async_copy(coupling_hbm, coupling, sems.at[0]),
         pltpu.make_async_copy(target_hbm, target, sems.at[1]),
@@ -125,9 +120,9 @@
     target_out[...] = dot((column == wanted).astype(bf16), target[...]).astype(bf16)
 
 
-def far_field(got, far_cols, high, low, target, table, clusters, rank, far):
-    slots = far_cols.shape[0]
-    per_group = LANES // rank
+def far_kernel(per_group, got, far_cols, high, low, target, far, table):
+    slots, clusters = far_cols.shape
+    rank = LANES // per_group
     groups = clusters // per_group
     head = groups * R
     for device in range(got.shape[0]):
@@ -166,18 +161,8 @@
     both[pl.ds(rows, rows), :] = odd[...]
 
 
-def near_kernel(*refs):
-    *slabs, placed, blocks_hbm, near, window, blocks, sems = refs
+def near_field(slabs, placed, blocks, near, window):
     slots, clusters = placed.shape
-    chunks = sems.shape[0]
-    each = clusters // chunks
-
-    def copy_of(chunk):
-        span = pl.ds(chunk * each * slots, each * slots)
-        return pltpu.make_async_copy(blocks_hbm.at[span], blocks.at[span], sems.at[chunk])
-
-    for chunk in range(chunks):
-        copy_of(chunk).start()
     at = 0
     for slab in slabs:
         window[pl.ds(at, slab.shape[0]), :] = slab[...].astype(f32)
@@ -191,8 +176,6 @@
         return blocks[i * slots + k]
 
     for i in range(0, clusters, 2):
-        if i % each == 0:
-            copy_of(i // each).wait()
         both = jnp.zeros((2 * R, 2 * LANES), f32)
         for k in range(0, slots, 2):
             sources = jnp.concatenate(
@@ -212,19 +195,28 @@
     return jnp.sqrt(whole), square / whole
 
 
-def first_kernel(per_group, unknowns, b, near, got, far_cols, high, low, target, image, lowered, table, far):
-    clusters = far_cols.shape[1]
+def first_kernel(
+    per_group, unknowns, own, mate, even, odd, relayed, placed, blocks, b, far, got, basis,
+    image, lowered, payload, near, window,
+):
+    near_field((own, mate, even, odd, relayed), placed, blocks, near, window)
+    clusters = placed.shape[1]
     head = clusters // per_group * R
-    far_field(got, far_cols, high, low, target, table, clusters, LANES // per_group, far)
     start_norm, _ = norm_parts(read_sums(got, head, 1, unknowns))
     scale = 1.0 / start_norm
-    for j in range(0, clusters, 2):
-        made = [
-            (0.5 * rows_of(b, i) + (rows_of(near, i) + rows_of(far, i))) * scale for i in (j, j + 1)
-        ]
-        both = jnp.concatenate(made, axis=0)
-        image[pl.ds(j * R, 2 * R), :] = both
-        lowered[pl.ds(j * R, 2 * R), :] = both.astype(bf16)
+    tiles = []
+    cross, square = jnp.zeros((R, LANES), f32), jnp.zeros((R, LANES), f32)
+    for i in range(clusters):
+        field = rows_of(b, i)
+        made = (0.5 * field + (rows_of(near, i) + rows_of(far, i))) * scale
+        cross = cross + field * made
+        square = square + made * made
+        tiles.append(made)
+    for i in range(0, clusters, 2):
+        both = jnp.concatenate(tiles[i : i + 2], axis=0)
+        image[pl.ds(i * R, 2 * R), :] = both
+        lowered[pl.ds(i * R, 2 * R), :] = both.astype(bf16)
+    write_payload(payload, tiles, [cross, square], basis, per_group)
 
 
 def arnoldi_one(sums0, sums1):
@@ -236,11 +228,12 @@
 
 
 def second_kernel(
-    per_group, unknowns, b, image, near, got0, got, far_cols, high, low, target, candidate, sums_out, table, far,
+    per_group, unknowns, own, mate, even, odd, relayed, placed, blocks, b, image, far, got0, got,
+    candidate, sums_out, near, window,
 ):
-    clusters = far_cols.shape[1]
+    near_field((own, mate, even, odd, relayed), placed, blocks, near, window)
+    clusters = placed.shape[1]
     head = clusters // per_group * R
-    far_field(got, far_cols, high, low, target, table, clusters, LANES // per_group, far)
     sums0 = read_sums(got0, head, 1, unknowns)
     scale = 1.0 / norm_parts(sums0)[0]
     h11, h21, _, _, _ = arnoldi_one(sums0, read_sums(got, head, 2, unknowns))
@@ -349,37 +342,34 @@
     def in_hbm(array):
         return pltpu.with_memory_space_constraint(array, pltpu.HBM)
 
-    def call(kernel, name, out, ins, *args, scratch_shapes=(), cost_estimate=None):
+    def call(kernel, name, out, ins, *args, scratch_shapes=()):
         return pl.pallas_call(
             kernel, out_shape=out, in_specs=ins, out_specs=jax.tree.map(lambda _: VMEM, out),
             scratch_shapes=scratch_shapes, compiler_params=PARAMS, name=name,
-            cost_estimate=cost_estimate,
         )(*args)
 
     def exchange(block):
         return lax.all_to_all(block, "rows", 0, 0)
 
-    field, basis, lowered = call(
-        start_kernel, "start",
-        (shape(rows, LANES), shape(clusters * rank, LANES, dtype=bf16), shape(rows, LANES, dtype=bf16)),
+    payload_shape = shape(size, head + TAIL, LANES, dtype=bf16)
+    field, basis, lowered, payload = call(
+        functools.partial(start_kernel, per_group), "start",
+        (
+            shape(rows, LANES), shape(clusters * rank, LANES, dtype=bf16), shape(rows, LANES, dtype=bf16),
+            payload_shape,
+        ),
         [HBM] * 2, in_hbm(right_sides), in_hbm(basis_in.reshape(clusters * rank, LANES)),
         scratch_shapes=[scratch(R, width), pltpu.SemaphoreType.DMA((2,))],
     )
+    got0 = exchange(payload)
     held = sends_of(lowered)
-    compress_cost = pl.CostEstimate(flops=0, bytes_accessed=64 * basis.size * rank, transcendentals=0)
-    payload_shape = shape(size, head + TAIL, LANES, dtype=bf16)
-    payload = call(
-        functools.partial(compress_kernel, per_group, [(0, 0)]), "compress_one", payload_shape,
-        [VMEM] * 2, field, basis, cost_estimate=compress_cost,
-    )
-    got0 = exchange(payload)
-
-    def relayed(held, payload):
-        both = call(
-            relay_kernel, "relay", shape(2 * rows, LANES, dtype=bf16), [VMEM] * 2 + [ANY], *held[2:], payload
-        )
-        return swapped(both, core_mate)
-
+
+    reach = 2 * clusters
+    start = lax.axis_index("rows") * clusters
+    distance = (near_cols.T - start + reach) % every
+    live = jnp.arange(slots, dtype=jnp.int32)[:, None] < near_counts[None, :]
+    placed = jnp.where(live, window_place(distance, clusters), 6 * clusters).astype(jnp.int32)
+    far_index = far_cols.T
     high, low, target = call(
         prepare_kernel, "prepare",
         (
@@ -387,51 +377,45 @@
             shape(slots * rank, rank * clusters, dtype=bf16),
             shape(rank * clusters, LANES, dtype=bf16),
         ),
-        [HBM] * 2 + [ANY],
-        in_hbm(jnp.transpose(coupling, (1, 2, 3, 0))), in_hbm(target_basis.reshape(clusters * rank, LANES)), payload,
+        [HBM] * 2 + [ANY] * 2,
+        in_hbm(jnp.transpose(coupling, (1, 2, 3, 0))), in_hbm(target_basis.reshape(clusters * rank, LANES)),
+        payload, placed,
         scratch_shapes=[
             scratch(slots, rank, rank, clusters), scratch(clusters * rank, LANES, dtype=bf16),
             pltpu.SemaphoreType.DMA((2,)),
         ],
     )
-    blocks = in_hbm(near_blocks.reshape(clusters * slots, LANES, LANES))
-    reach = 2 * clusters
-    start = lax.axis_index("rows") * clusters
-    distance = (near_cols.T - start + reach) % every
-    live = jnp.arange(slots, dtype=jnp.int32)[:, None] < near_counts[None, :]
-    placed = jnp.where(live, window_place(distance, clusters), 6 * clusters).astype(jnp.int32)
-    far_index = far_cols.T
-
-    near_cost = pl.CostEstimate(flops=32 * near_blocks.size, bytes_accessed=32 * near_blocks.size, transcendentals=0)
-
-    def near_of(slabs):
+    blocks = pltpu.with_memory_space_constraint(
+        near_blocks.reshape(clusters * slots, LANES, LANES), pltpu.VMEM
+    )
+
+    def far_of(got):
         return call(
-            near_kernel, "near", shape(rows, LANES), [VMEM] * len(slabs) + [SMEM, HBM], *slabs, placed, blocks,
-            scratch_shapes=[
-                scratch(6 * rows + R, LANES), scratch(*blocks.shape, dtype=bf16),
-                pltpu.SemaphoreType.DMA((8,)),
-            ],
-            cost_estimate=near_cost,
+            functools.partial(far_kernel, per_group), "far", shape(rows, LANES), [VMEM, SMEM] + [VMEM] * 3,
+            got, far_index, high, low, target, scratch_shapes=[scratch(size * head, LANES)],
         )
 
-    kept = [scratch(size * head, LANES), scratch(rows, LANES)]
-    near = near_of(held + [relayed(held, payload)])
-    image, lowered = call(
-        functools.partial(first_kernel, per_group, unknowns), "far_one",
-        (shape(rows, LANES), shape(rows, LANES, dtype=bf16)), [VMEM] * 3 + [SMEM] + [VMEM] * 3,
-        field, near, got0, far_index, high, low, target, scratch_shapes=kept,
-    )
+    def relayed(held, far):
+        both = call(
+            relay_kernel, "relay", shape(2 * rows, LANES, dtype=bf16), [VMEM] * 2 + [ANY], *held[2:], far
+        )
+        return swapped(both, core_mate)
+
+    kept = [scratch(rows, LANES), scratch(6 * rows + R, LANES)]
+    far = far_of(got0)
+    image, lowered, payload = call(
+        functools.partial(first_kernel, per_group, unknowns), "near_one",
+        (shape(rows, LANES), shape(rows, LANES, dtype=bf16), payload_shape),
+        [VMEM] * 5 + [SMEM] + [VMEM] * 5,
+        *held, relayed(held, far), placed, blocks, field, far, got0, basis, scratch_shapes=kept,
+    )
+    got1 = exchange(payload)
     held = sends_of(lowered)
-    payload = call(
-        functools.partial(compress_kernel, per_group, [(0, 1), (1, 1)]), "compress_two", payload_shape,
-        [VMEM] * 3, field, image, basis, cost_estimate=compress_cost,
-    )
-    got1 = exchange(payload)
-    near = near_of(held + [relayed(held, payload)])
+    far = far_of(got1)
     candidate, sums = call(
-        functools.partial(second_kernel, per_group, unknowns), "far_two",
-        (shape(rows, LANES), shape(size, R, LANES)), [VMEM] * 5 + [SMEM] + [VMEM] * 3,
-        field, image, near, got0, got1, far_index, high, low, target, scratch_shapes=kept,
+        functools.partial(second_kernel, per_group, unknowns), "near_two",
+        (shape(rows, LANES), shape(size, R, LANES)), [VMEM] * 5 + [SMEM] + [VMEM] * 6,
+        *held, relayed(held, far), placed, blocks, field, image, far, got0, got1, scratch_shapes=kept,
     )
     got2 = exchange(sums)
     return call(

time: 64.6 us -> 65.6 us (1.015)
  local copies, waits for them, and re-layouts: 0.01 us -> 7.46 us
  Pallas kernels: 19.6 us -> 15.3 us
  waiting for transfers between devices: 11.4 us -> 9.29 us
    ppermute x8, waiting for transfers between devices: 11.4 us -> 1.88 us  [swapped(): lax.ppermute(block, 'rows', [(i, partner(i)) for i in range(lax.axis_size...]
    unnamed x2 -> x8, local copies, waits for them, and re-layouts: 0.01 us -> 7.46 us
    all_to_all x2, waiting for transfers between devices: 0.01 us -> 7.42 us  [exchange(): return lax.all_to_all(block, 'rows', 0, 0)]
    pallas_call x11 -> x9, Pallas kernels: 19.6 us -> 15.3 us  [call(): pl.pallas_call(kernel, out_shape=out, in_specs=ins, out_specs=jax.tree.ma...]
  transfers between devices with their start and end apart: 10 -> 10, of which waited for: 5 -> 4; matrix products, arithmetic and copies ran while one was open for 1% -> 1% of each run, Pallas kernels for 18% -> 8%
where the time goes in v8:
time: 65.6 us; the launch traced here: 65.1 us
  starting transfers between devices  21.4 us (33%)
  Pallas kernels  15.3 us (23%)
  blocking collectives  10.2 us (16%)
  waiting for transfers between devices  9.29 us (14%)
  local copies, waits for them, and re-layouts  7.46 us (11%)
  between operations  0.76 us (1%)
  other arithmetic  0.71 us (1%)
    pallas_call x9, Pallas kernels, call(): pl.pallas_call(kernel, out_shape=out, in_specs=ins, out_specs=jax.tree.ma...  15.3 us
    all_to_all x2, starting transfers between devices, exchange(): return lax.all_to_all(block, 'rows', 0, 0)  11 us
    ppermute x8, starting transfers between devices, swapped(): lax.ppermute(block, 'rows', [(i, partner(i)) for i in range(lax.axis_size...  10.4 us
    all_to_all x1, blocking collectives, exchange(): return lax.all_to_all(block, 'rows', 0, 0)  10.2 us
    unnamed x8, local copies, waits for them, and re-layouts  7.46 us
    all_to_all x2, waiting for transfers between devices, exchange(): return lax.all_to_all(block, 'rows', 0, 0)  7.42 us
    ppermute x8, waiting for transfers between devices, swapped(): lax.ppermute(block, 'rows', [(i, partner(i)) for i in range(lax.axis_size...  1.88 us
  transfers between devices with their start and end apart: 10, of which 4 were waited for; matrix products, arithmetic and copies ran while one was open for 1% of the time, Pallas kernels for 8%

profile of v8, /device:TPU:0, one launch (start us, length us, event | category | flops | bytes accessed | tf_op | source)
XLA Modules:
  0.0 65.1 jit_solution(17702705980543258951)
XLA Ops:
  0.6 1.9 %start.1 = (f32[256,128]{1,0:T(8,128)S(1)}, bf16[512,128]{1,0:T(8,128)(2,1)S(1)}, bf16[256,128]{1,0:T(8,128)(2,1)S(1)}, bf16[16,48,128]{2,1,0:T(8,128)(2,1)}) custom-call(f32[8,4096]{1,0:T(8,128)} %b_hbm.1, bf16[512,128]{1,0:T(8,128)(2,1)} %bitcast.14), custom_call_target="tpu_custom_call" | custom-call | tf_op jit(solution)/shard_map/start/pallas_call | solution.py:346
  2.5 7.4 %all-to-all-start = ((bf16[16,48,128]{2,1,0:T(8,128)(2,1)}), bf16[16,48,128]{2,1,0:T(8,128)(2,1)S(1)}, u32[]{:S(2)}, u32[]{:S(2)}) async-start(bf16[16,48,128]{2,1,0:T(8,128)(2,1)} %get-tuple-element.16._), calls=%async_computation | async-start | bytes 393216 | tf_op jit(solution)/shard_map/all_to_all | solution.py:352
  9.9 4.6 %collective-permute-start.2 = (bf16[256,128]{1,0:T(8,128)(2,1)S(1)}, bf16[256,128]{1,0:T(8,128)(2,1)S(1)}, u32[]{:S(2)}, u32[]{:S(2)}) collective-permute-start(bf16[256,128]{1,0:T(8,128)(2,1)S(1)} %get-tuple-element.15.own), channel_id=1, source_target_pairs={{0,14},{1,15},{2,4},{3,5},{4,2},{5,3},{6,8},{7,9},{8,6},{9,7},{10,... | collective-permute-start | bytes 196616 | tf_op jit(solution)/shard_map/ppermute | solution.py:284
  14.6 0.7 %fusion.2.__.placed = s32[8,32]{1,0:T(8,128)S(1)} fusion(s32[32,8]{0,1:T(8,128)} %param.10, s32[]{:T(128)S(6)} %sub.24, s32[]{:T(128)S(6)} %select_n.67, s32[]{:T(128)S(6)} %select_n.66, s32[]{:T(128)S(6)} %add.49, s32[]{:T(128)S(6)} %mul.7, s32[32]{0:T(128)} %param.11), kind=kLoop, calls=%fused_computation.10 | loop fusion | flops 11776 | bytes 2196 | tf_op jit(solution)/shard_map/jit(_where)/select_n | solution.py:371
  15.3 1.6 %prepare.1 = (bf16[128,512]{1,0:T(8,128)(2,1)S(1)}, bf16[128,512]{1,0:T(8,128)(2,1)S(1)}, bf16[512,128]{1,0:T(8,128)(2,1)S(1)}) custom-call(f32[8,16,16,32]{3,2,1,0:T(8,128)} %bitcast.13, bf16[512,128]{1,0:T(8,128)(2,1)} %bitcast.15, bf16[16,48,128]{2,1,0:T(8,128)(2,1)} %get-tuple-element.16._, s32[8,32]{1,0:T(8,128)S(1)} %fusion.2.__.placed), custom_call_target="tpu_custom_call" | custom-call | tf_op jit(solution)/shard_map/prepare/pallas_call | solution.py:346
  16.9 2.6 %all-to-all-done.got.got0 = bf16[16,48,128]{2,1,0:T(8,128)(2,1)S(1)} async-done(((bf16[16,48,128]{2,1,0:T(8,128)(2,1)}), bf16[16,48,128]{2,1,0:T(8,128)(2,1)S(1)}, u32[]{:S(2)}, u32[]{:S(2)}) %all-to-all-start) | async-done | bytes 196640 | tf_op jit(solution)/shard_map/all_to_all | solution.py:352
  19.4 0.7 %copy-done.2 = s32[32,8]{0,1:T(8,128)S(1)} copy-done((s32[32,8]{0,1:T(8,128)S(1)}, s32[32,8]{0,1:T(8,128)}, u32[]{:S(2)}) %copy-start.2) | copy-done | bytes 1048
  20.1 1.9 %far.2._ = f32[256,128]{1,0:T(8,128)S(1)} custom-call(bf16[16,48,128]{2,1,0:T(8,128)(2,1)S(1)} %all-to-all-done.got.got0, s32[8,32]{1,0:T(8,128)S(1)} %bitcast.11, bf16[128,512]{1,0:T(8,128)(2,1)S(1)} %get-tuple-element.17.high, bf16[128,512]{1,0:T(8,128)(2,1)S(1)} %get-tuple-element.18.low, bf16[512,128]{1,0:T(8,128)(2,1)S(1)} %get-tuple-element.19.target), custom_call_target="tpu_custom_call" | custom-call | tf_op jit(solution)/shard_map/far/pallas_call | solution.py:346
  22.1 0.1 collective-permute-start.3
  22.2 0.5 collective-permute-start
  22.7 0.9 %collective-permute-done.mate = bf16[256,128]{1,0:T(8,128)(2,1)S(1)} collective-permute-done((bf16[256,128]{1,0:T(8,128)(2,1)S(1)}, bf16[256,128]{1,0:T(8,128)(2,1)S(1)}, u32[]{:S(2)}, u32[]{:S(2)}) %collective-permute-start) | collective-permute-done | bytes 65568 | tf_op jit(solution)/shard_map/ppermute | solution.py:284
  23.6 3.4 %copy-done = bf16[32,8,128,128]{3,2,1,0:T(8,128)(2,1)S(1)} copy-done((bf16[32,8,128,128]{3,2,1,0:T(8,128)(2,1)S(1)}, bf16[32,8,128,128]{3,2,1,0:T(8,128)(2,1)}, u32[]{:S(2)}) %copy-start) | copy-done | bytes 8388632
  27.0 3.7 %near_one.1 = (f32[256,128]{1,0:T(8,128)S(1)}, bf16[256,128]{1,0:T(8,128)(2,1)S(1)}, bf16[16,48,128]{2,1,0:T(8,128)(2,1)}) custom-call(bf16[256,128]{1,0:T(8,128)(2,1)S(1)} %get-tuple-element.15.own, bf16[256,128]{1,0:T(8,128)(2,1)S(1)} %collective-permute-done.mate, bf16[256,128]{1,0:T(8,128)(2,1)S(1)} %collective-permute-done.1.even, ...), custom_call_target="tpu_custom_call" | custom-call | tf_op jit(solution)/shard_map/near_one/pallas_call | solution.py:346
  30.7 3.6 %all-to-all-start.1 = ((bf16[16,48,128]{2,1,0:T(8,128)(2,1)}), bf16[16,48,128]{2,1,0:T(8,128)(2,1)S(1)}, u32[]{:S(2)}, u32[]{:S(2)}) async-start(bf16[16,48,128]{2,1,0:T(8,128)(2,1)} %get-tuple-element.23), calls=%async_computation.1 | async-start | bytes 393216 | tf_op jit(solution)/shard_map/all_to_all | solution.py:352
  34.3 4.6 %collective-permute-start.6 = (bf16[256,128]{1,0:T(8,128)(2,1)S(1)}, bf16[256,128]{1,0:T(8,128)(2,1)S(1)}, u32[]{:S(2)}, u32[]{:S(2)}) collective-permute-start(bf16[256,128]{1,0:T(8,128)(2,1)S(1)} %get-tuple-element.22.own), channel_id=1, source_target_pairs={{0,14},{1,15},{2,4},{3,5},{4,2},{5,3},{6,8},{7,9},{8,6},{9,7},{10,... | collective-permute-start | bytes 196616 | tf_op jit(solution)/shard_map/ppermute | solution.py:284
  38.9 4.9 %all-to-all-done.1.got.got1 = bf16[16,48,128]{2,1,0:T(8,128)(2,1)S(1)} async-done(((bf16[16,48,128]{2,1,0:T(8,128)(2,1)}), bf16[16,48,128]{2,1,0:T(8,128)(2,1)S(1)}, u32[]{:S(2)}, u32[]{:S(2)}) %all-to-all-start.1) | async-done | bytes 196640 | tf_op jit(solution)/shard_map/all_to_all | solution.py:352
  43.8 1.9 %far.3._ = f32[256,128]{1,0:T(8,128)S(1)} custom-call(bf16[16,48,128]{2,1,0:T(8,128)(2,1)S(1)} %all-to-all-done.1.got.got1, s32[8,32]{1,0:T(8,128)S(1)} %bitcast.12, bf16[128,512]{1,0:T(8,128)(2,1)S(1)} %get-tuple-element.17.high, bf16[128,512]{1,0:T(8,128)(2,1)S(1)} %get-tuple-element.18.low, bf16[512,128]{1,0:T(8,128)(2,1)S(1)} %get-tuple-element.19.target), custom_call_target="tpu_custom_call" | custom-call | tf_op jit(solution)/shard_map/far/pallas_call | solution.py:346
  45.8 0.1 collective-permute-start.7
  45.8 0.5 collective-permute-start.4
  46.3 0.9 %collective-permute-done.4.mate = bf16[256,128]{1,0:T(8,128)(2,1)S(1)} collective-permute-done((bf16[256,128]{1,0:T(8,128)(2,1)S(1)}, bf16[256,128]{1,0:T(8,128)(2,1)S(1)}, u32[]{:S(2)}, u32[]{:S(2)}) %collective-permute-start.4) | collective-permute-done | bytes 65568 | tf_op jit(solution)/shard_map/ppermute | solution.py:284
  47.3 3.4 %copy-done.1 = bf16[32,8,128,128]{3,2,1,0:T(8,128)(2,1)S(1)} copy-done((bf16[32,8,128,128]{3,2,1,0:T(8,128)(2,1)S(1)}, bf16[32,8,128,128]{3,2,1,0:T(8,128)(2,1)}, u32[]{:S(2)}) %copy-start.1) | copy-done | bytes 8388632
  50.7 3.0 %near_two.1 = (f32[256,128]{1,0:T(8,128)S(1)}, f32[16,8,128]{2,1,0:T(8,128)S(1)}) custom-call(bf16[256,128]{1,0:T(8,128)(2,1)S(1)} %get-tuple-element.22.own, bf16[256,128]{1,0:T(8,128)(2,1)S(1)} %collective-permute-done.4.mate, bf16[256,128]{1,0:T(8,128)(2,1)S(1)} %collective-permute-done.5.even, bf16[256,128]{1,0:T(8,128)(2,1)S(1)} %collective-permute-done.6.odd, ...), custom_call_target="tpu_custom_call" | custom-call | tf_op jit(solution)/shard_map/near_two/pallas_call | solution.py:346
  53.7 10.2 %all_to_all.15.got2 = f32[16,8,128]{2,1,0:T(8,128)S(1)} all-to-all(f32[16,8,128]{2,1,0:T(8,128)S(1)} %get-tuple-element.25), channel_id=1, replica_groups=mesh['groups'=2,'rows'=16] {'rows'}, dimensions={0} | all-to-all | bytes 131072 | tf_op jit(solution)/shard_map/all_to_all | solution.py:352
  63.9 1.2 %finish.1 = (f32[8,4096]{1,0:T(8,128)}, f32[8,4096]{1,0:T(8,128)}) custom-call(f32[256,128]{1,0:T(8,128)S(1)} %get-tuple-element.14.b, f32[256,128]{1,0:T(8,128)S(1)} %get-tuple-element.21.image, f32[256,128]{1,0:T(8,128)S(1)} %get-tuple-element.24.candidate, bf16[16,48,128]{2,1,0:T(8,128)(2,1)S(1)} %all-to-all-done.got.got0, ...), custom_call_target="tpu_custom_call" | custom-call | tf_op jit(solution)/shard_map/finish/pallas_call | solution.py:346
  (15 shorter events, 0.1 us)
Async XLA Ops:
  0.6 43.1 %copy-start.3 = (s32[32,8]{0,1:T(8,128)S(1)}, s32[32,8]{0,1:T(8,128)}, u32[]{:S(2)}) copy-start(s32[32,8]{0,1:T(8,128)} %param.15) | copy-start | bytes 3076
  2.5 16.9 %all-to-all-start = ((bf16[16,48,128]{2,1,0:T(8,128)(2,1)}), bf16[16,48,128]{2,1,0:T(8,128)(2,1)S(1)}, u32[]{:S(2)}, u32[]{:S(2)}) async-start(bf16[16,48,128]{2,1,0:T(8,128)(2,1)} %get-tuple-element.16._), calls=%async_computation | async-start | bytes 393216 | tf_op jit(solution)/shard_map/all_to_all | solution.py:352
  9.9 12.1 %collective-permute-start.2 = (bf16[256,128]{1,0:T(8,128)(2,1)S(1)}, bf16[256,128]{1,0:T(8,128)(2,1)S(1)}, u32[]{:S(2)}, u32[]{:S(2)}) collective-permute-start(bf16[256,128]{1,0:T(8,128)(2,1)S(1)} %get-tuple-element.15.own), channel_id=1, source_target_pairs={{0,14},{1,15},{2,4},{3,5},{4,2},{5,3},{6,8},{7,9},{8,6},{9,7},{10,... | collective-permute-start | bytes 196616 | tf_op jit(solution)/shard_map/ppermute | solution.py:284
  14.6 7.5 %collective-permute-start.1 = (bf16[256,128]{1,0:T(8,128)(2,1)S(1)}, bf16[256,128]{1,0:T(8,128)(2,1)S(1)}, u32[]{:S(2)}, u32[]{:S(2)}) collective-permute-start(bf16[256,128]{1,0:T(8,128)(2,1)S(1)} %get-tuple-element.15.own), channel_id=1, source_target_pairs={{0,2},{1,3},{2,0},{3,1},{4,6},{5,7},{6,4},{7,5},{8,10},{9,11},{10,... | collective-permute-start | bytes 196616 | tf_op jit(solution)/shard_map/ppermute | solution.py:284
  19.4 0.7 %copy-start.2 = (s32[32,8]{0,1:T(8,128)S(1)}, s32[32,8]{0,1:T(8,128)}, u32[]{:S(2)}) copy-start(s32[32,8]{0,1:T(8,128)} %param.15) | copy-start | bytes 3076
  22.1 1.5 %collective-permute-start.3 = (bf16[512,128]{1,0:T(8,128)(2,1)S(1)}, bf16[512,128]{1,0:T(8,128)(2,1)S(1)}, u32[]{:S(2)}, u32[]{:S(2)}) collective-permute-start(bf16[512,128]{1,0:T(8,128)(2,1)S(1)} %relay.2), channel_id=1, source_target_pairs={{0,1},{1,0},{2,3},{3,2},{4,5},{5,4},{6,7},{7,6},{8,9},{9,8},{10,11... | collective-permute-start | bytes 393224 | tf_op jit(solution)/shard_map/ppermute | solution.py:284
  22.2 1.4 %collective-permute-start = (bf16[256,128]{1,0:T(8,128)(2,1)S(1)}, bf16[256,128]{1,0:T(8,128)(2,1)S(1)}, u32[]{:S(2)}, u32[]{:S(2)}) collective-permute-start(bf16[256,128]{1,0:T(8,128)(2,1)S(1)} %get-tuple-element.15.own), channel_id=1, source_target_pairs={{0,1},{1,0},{2,3},{3,2},{4,5},{5,4},{6,7},{7,6},{8,9},{9,8},{10,11... | collective-permute-start | bytes 196616 | tf_op jit(solution)/shard_map/ppermute | solution.py:284
  23.6 3.4 %copy-start = (bf16[32,8,128,128]{3,2,1,0:T(8,128)(2,1)S(1)}, bf16[32,8,128,128]{3,2,1,0:T(8,128)(2,1)}, u32[]{:S(2)}) copy-start(bf16[32,8,128,128]{3,2,1,0:T(8,128)(2,1)} %param.9) | copy-start | bytes 25165828
  30.7 13.1 %all-to-all-start.1 = ((bf16[16,48,128]{2,1,0:T(8,128)(2,1)}), bf16[16,48,128]{2,1,0:T(8,128)(2,1)S(1)}, u32[]{:S(2)}, u32[]{:S(2)}) async-start(bf16[16,48,128]{2,1,0:T(8,128)(2,1)} %get-tuple-element.23), calls=%async_computation.1 | async-start | bytes 393216 | tf_op jit(solution)/shard_map/all_to_all | solution.py:352
  34.3 11.4 %collective-permute-start.6 = (bf16[256,128]{1,0:T(8,128)(2,1)S(1)}, bf16[256,128]{1,0:T(8,128)(2,1)S(1)}, u32[]{:S(2)}, u32[]{:S(2)}) collective-permute-start(bf16[256,128]{1,0:T(8,128)(2,1)S(1)} %get-tuple-element.22.own), channel_id=1, source_target_pairs={{0,14},{1,15},{2,4},{3,5},{4,2},{5,3},{6,8},{7,9},{8,6},{9,7},{10,... | collective-permute-start | bytes 196616 | tf_op jit(solution)/shard_map/ppermute | solution.py:284
  38.9 6.8 %collective-permute-start.5 = (bf16[256,128]{1,0:T(8,128)(2,1)S(1)}, bf16[256,128]{1,0:T(8,128)(2,1)S(1)}, u32[]{:S(2)}, u32[]{:S(2)}) collective-permute-start(bf16[256,128]{1,0:T(8,128)(2,1)S(1)} %get-tuple-element.22.own), channel_id=1, source_target_pairs={{0,2},{1,3},{2,0},{3,1},{4,6},{5,7},{6,4},{7,5},{8,10},{9,11},{10,... | collective-permute-start | bytes 196616 | tf_op jit(solution)/shard_map/ppermute | solution.py:284
  45.8 1.5 %collective-permute-start.7 = (bf16[512,128]{1,0:T(8,128)(2,1)S(1)}, bf16[512,128]{1,0:T(8,128)(2,1)S(1)}, u32[]{:S(2)}, u32[]{:S(2)}) collective-permute-start(bf16[512,128]{1,0:T(8,128)(2,1)S(1)} %relay.3), channel_id=1, source_target_pairs={{0,1},{1,0},{2,3},{3,2},{4,5},{5,4},{6,7},{7,6},{8,9},{9,8},{10,11... | collective-permute-start | bytes 393224 | tf_op jit(solution)/shard_map/ppermute | solution.py:284
  45.8 1.4 %collective-permute-start.4 = (bf16[256,128]{1,0:T(8,128)(2,1)S(1)}, bf16[256,128]{1,0:T(8,128)(2,1)S(1)}, u32[]{:S(2)}, u32[]{:S(2)}) collective-permute-start(bf16[256,128]{1,0:T(8,128)(2,1)S(1)} %get-tuple-element.22.own), channel_id=1, source_target_pairs={{0,1},{1,0},{2,3},{3,2},{4,5},{5,4},{6,7},{7,6},{8,9},{9,8},{10,11... | collective-permute-start | bytes 196616 | tf_op jit(solution)/shard_map/ppermute | solution.py:284
  47.3 3.4 %copy-start.1 = (bf16[32,8,128,128]{3,2,1,0:T(8,128)(2,1)S(1)}, bf16[32,8,128,128]{3,2,1,0:T(8,128)(2,1)}, u32[]{:S(2)}) copy-start(bf16[32,8,128,128]{3,2,1,0:T(8,128)(2,1)} %param.9) | copy-start | bytes 25165828

commit v9 on v8

--- a/solution.py
+++ b/solution.py
@@ -42,13 +42,14 @@
         low = total - high - middle
         for part, value in enumerate((high, middle, low)):
             tile = jnp.where(lane == part * SUM_SLOTS + t, value, tile)
-    return jnp.concatenate([tile, jnp.zeros((TAIL - R, LANES), f32)], axis=0).astype(bf16)
-
-
-def read_sums(got, first_row, count, unknowns):
+    return tile
+
+
+def read_sums(gathered, first_row, rows, count, unknowns):
     total = jnp.zeros((R, LANES), f32)
-    for device in range(got.shape[0]):
-        total = total + got[device, pl.ds(first_row, TAIL), :].astype(f32)[:R]
+    for got in gathered:
+        for device in range(got.shape[0]):
+            total = total + got[device, pl.ds(first_row, rows), :].astype(f32)[:R]
     return [
         sum(total[:, p * SUM_SLOTS + t : p * SUM_SLOTS + t + 1] for p in range(3)) * (1.0 / unknowns)
         for t in range(count)
@@ -73,7 +74,9 @@
 def write_payload(payload, tiles, sums, basis, per_group):
     groups = len(tiles) // per_group
     parts = [compress(tiles[g * per_group : (g + 1) * per_group], basis, g) for g in range(groups)]
-    block = jnp.concatenate([jnp.concatenate(parts, axis=0).astype(bf16), sums_tile(sums)], axis=0)
+    if sums:
+        parts += [sums_tile(sums), jnp.zeros((TAIL - R, LANES), f32)]
+    block = jnp.concatenate(parts, axis=0).astype(bf16)
     for device in range(payload.shape[0]):
         payload[device] = block
 
@@ -91,10 +94,10 @@
     tiles = [b[:, j * LANES : (j + 1) * LANES] for j in range(clusters)]
     field[...] = jnp.concatenate(tiles, axis=0)
     lowered[...] = jnp.concatenate(tiles, axis=0).astype(bf16)
-    write_payload(payload, tiles, [sum(t * t for t in tiles)], basis, per_group)
-
-
-def prepare_kernel(coupling_hbm, target_hbm, _, __, high_out, low_out, target_out, coupling, target, sems):
+    write_payload(payload, tiles, [], basis, per_group)
+
+
+def prepare_kernel(coupling_hbm, target_hbm, _, __, ___, high_out, low_out, target_out, coupling, target, sems):
     copies = [
         pltpu.make_async_copy(coupling_hbm, coupling, sems.at[0]),
         pltpu.make_async_copy(target_hbm, target, sems.at[1]),
@@ -120,13 +123,27 @@
     target_out[...] = dot((column == wanted).astype(bf16), target[...]).astype(bf16)
 
 
-def far_kernel(per_group, got, far_cols, high, low, target, far, table):
+def far_kernel(
+    per_group, got, got_mate, far_cols, high, low, target, blocks_hbm, _, far, blocks, table, sems,
+):
+    chunks = sems.shape[0]
+    each = blocks.shape[0] // chunks
+    copies = [
+        pltpu.make_async_copy(
+            blocks_hbm.at[pl.ds(c * each, each)], blocks.at[pl.ds(c * each, each)], sems.at[c]
+        )
+        for c in range(chunks)
+    ]
+    for copy in copies:
+        copy.start()
     slots, clusters = far_cols.shape
     rank = LANES // per_group
     groups = clusters // per_group
     head = groups * R
-    for device in range(got.shape[0]):
-        table[pl.ds(device * head, head), :] = got[device, pl.ds(0, head), :].astype(f32)
+    for part, values in enumerate((got, got_mate)):
+        for device in range(values.shape[0]):
+            at = (part * values.shape[0] + device) * head
+            table[pl.ds(at, head), :] = values[device, pl.ds(0, head), :].astype(f32)
     lane = lane_ids()
     picked = []
     for i in range(clusters):
@@ -153,9 +170,11 @@
     far[...] = dot(jnp.concatenate(expanded_high, axis=1), target[...]) + dot(
         jnp.concatenate(expanded_low, axis=1), target[...]
     )
-
-
-def relay_kernel(even, odd, _, both):
+    for copy in copies:
+        copy.wait()
+
+
+def relay_kernel(even, odd, both):
     rows = even.shape[0]
     both[pl.ds(0, rows), :] = even[...]
     both[pl.ds(rows, rows), :] = odd[...]
@@ -189,79 +208,64 @@
         near[pl.ds((i + 1) * R, R), :] = both[R:, LANES:]
 
 
-def norm_parts(sums):
-    square = sums[0]
-    whole = square + epsilon
-    return jnp.sqrt(whole), square / whole
-
-
 def first_kernel(
-    per_group, unknowns, own, mate, even, odd, relayed, placed, blocks, b, far, got, basis,
-    image, lowered, payload, near, window,
+    per_group, own, mate, even, odd, relayed, placed, blocks, b, far, basis, image, lowered, payload, near, window,
 ):
     near_field((own, mate, even, odd, relayed), placed, blocks, near, window)
     clusters = placed.shape[1]
-    head = clusters // per_group * R
-    start_norm, _ = norm_parts(read_sums(got, head, 1, unknowns))
-    scale = 1.0 / start_norm
     tiles = []
-    cross, square = jnp.zeros((R, LANES), f32), jnp.zeros((R, LANES), f32)
+    sums = [jnp.zeros((R, LANES), f32) for _ in range(3)]
     for i in range(clusters):
         field = rows_of(b, i)
-        made = (0.5 * field + (rows_of(near, i) + rows_of(far, i))) * scale
-        cross = cross + field * made
-        square = square + made * made
+        made = 0.5 * field + (rows_of(near, i) + rows_of(far, i))
+        sums = [s + f * g for s, f, g in zip(sums, (field, field, made), (field, made, made))]
         tiles.append(made)
     for i in range(0, clusters, 2):
         both = jnp.concatenate(tiles[i : i + 2], axis=0)
         image[pl.ds(i * R, 2 * R), :] = both
         lowered[pl.ds(i * R, 2 * R), :] = both.astype(bf16)
-    write_payload(payload, tiles, [cross, square], basis, per_group)
-
-
-def arnoldi_one(sums0, sums1):
-    start_norm, v11 = norm_parts(sums0)
-    h11 = sums1[0] * (1.0 / start_norm)
-    uu = jnp.maximum(sums1[1] - 2.0 * h11 * h11 + h11 * h11 * v11, 0.0)
+    write_payload(payload, tiles, sums, basis, per_group)
+
+
+def arnoldi_one(bb, bw, ww):
+    whole = bb + epsilon
+    start_norm = jnp.sqrt(whole)
+    scale = 1.0 / start_norm
+    v11 = bb / whole
+    h11 = (bw * scale) * scale
+    uu = jnp.maximum((ww * scale) * scale - 2.0 * h11 * h11 + h11 * h11 * v11, 0.0)
     h21 = jnp.sqrt(uu + epsilon)
-    return h11, h21, v11, uu / (uu + epsilon), h11 * (1.0 - v11) / h21
+    return start_norm, h11, h21, v11, uu / (uu + epsilon), h11 * (1.0 - v11) / h21
 
 
 def second_kernel(
-    per_group, unknowns, own, mate, even, odd, relayed, placed, blocks, b, image, far, got0, got,
+    per_group, unknowns, own, mate, even, odd, relayed, placed, blocks, b, image, far, got, got_mate,
     candidate, sums_out, near, window,
 ):
     near_field((own, mate, even, odd, relayed), placed, blocks, near, window)
     clusters = placed.shape[1]
     head = clusters // per_group * R
-    sums0 = read_sums(got0, head, 1, unknowns)
-    scale = 1.0 / norm_parts(sums0)[0]
-    h11, h21, _, _, _ = arnoldi_one(sums0, read_sums(got, head, 2, unknowns))
+    start_norm, h11, h21, _, _, _ = arnoldi_one(*read_sums((got, got_mate), head, TAIL, 3, unknowns))
+    scale = 1.0 / start_norm
     inverse = 1.0 / h21
     sums = [jnp.zeros((R, LANES), f32) for _ in range(3)]
     for j in range(clusters):
-        held = rows_of(image, j)
+        held = rows_of(image, j) * scale
         first = rows_of(b, j) * scale
         second = (held - h11 * first) * inverse
-        made = (0.5 * held + (rows_of(near, j) + rows_of(far, j)) - h11 * held) * inverse
+        made = (0.5 * held + (rows_of(near, j) + rows_of(far, j)) * scale - h11 * held) * inverse
         sums = [s + v * made for s, v in zip(sums, (first, second, made))]
         candidate[pl.ds(j * R, R), :] = made
-    lane = lane_ids()
-    tile = jnp.zeros((R, LANES), f32)
-    for t, partial in enumerate(sums):
-        tile = jnp.where(lane == t, jnp.sum(partial, axis=1, keepdims=True), tile)
+    tile = sums_tile(sums).astype(bf16)
     for device in range(sums_out.shape[0]):
         sums_out[device] = tile
 
 
-def finish_kernel(per_group, unknowns, b, image, candidate, got0, got1, got2, solution_out, next_out):
+def finish_kernel(per_group, unknowns, b, image, candidate, got1, got1_mate, got2, solution_out, next_out):
     clusters = b.shape[0] // R
     head = clusters // per_group * R
-    sums0 = read_sums(got0, head, 1, unknowns)
-    start_norm, _ = norm_parts(sums0)
-    h11, h21, v11, v22, v12 = arnoldi_one(sums0, read_sums(got1, head, 2, unknowns))
-    total = sum(got2[device] for device in range(got2.shape[0]))
-    h12, h22, ww = [total[:, t : t + 1] * (1.0 / unknowns) for t in range(3)]
+    start_norm, h11, h21, v11, v22, v12 = arnoldi_one(*read_sums((got1, got1_mate), head, TAIL, 3, unknowns))
+    h12, h22, ww = read_sums((got2,), 0, R, 3, unknowns)
     uu = ww - 2.0 * (h12 * h12 + h22 * h22) + h12 * h12 * v11 + h22 * h22 * v22 + 2.0 * h12 * h22 * v12
     h32 = jnp.sqrt(jnp.maximum(uu, 0.0) + epsilon)
     g11 = h11 * h11 + h21 * h21
@@ -275,7 +279,7 @@
     for j in range(clusters):
         span = slice(j * LANES, (j + 1) * LANES)
         first = rows_of(b, j) * scale
-        second = (rows_of(image, j) - h11 * first) * inverse
+        second = (rows_of(image, j) * scale - h11 * first) * inverse
         solution_out[:, span] = y1 * first + y2 * second
         next_out[:, span] = (rows_of(candidate, j) - h12 * first - h22 * second) * last
 
@@ -351,17 +355,21 @@
     def exchange(block):
         return lax.all_to_all(block, "rows", 0, 0)
 
-    payload_shape = shape(size, head + TAIL, LANES, dtype=bf16)
+    def gathered(block):
+        groups = [list(range(core, size, 2)) for core in range(2)]
+        got = lax.all_to_all(block, "rows", 0, 0, axis_index_groups=groups)
+        return got, swapped(got, core_mate)
+
     field, basis, lowered, payload = call(
         functools.partial(start_kernel, per_group), "start",
         (
             shape(rows, LANES), shape(clusters * rank, LANES, dtype=bf16), shape(rows, LANES, dtype=bf16),
-            payload_shape,
+            shape(size // 2, head, LANES, dtype=bf16),
         ),
         [HBM] * 2, in_hbm(right_sides), in_hbm(basis_in.reshape(clusters * rank, LANES)),
         scratch_shapes=[scratch(R, width), pltpu.SemaphoreType.DMA((2,))],
     )
-    got0 = exchange(payload)
+    got = gathered(payload)
     held = sends_of(lowered)
 
     reach = 2 * clusters
@@ -369,7 +377,9 @@
     distance = (near_cols.T - start + reach) % every
     live = jnp.arange(slots, dtype=jnp.int32)[:, None] < near_counts[None, :]
     placed = jnp.where(live, window_place(distance, clusters), 6 * clusters).astype(jnp.int32)
-    far_index = far_cols.T
+    owner = far_cols.T // clusters
+    other_core = (owner % 2) ^ (lax.axis_index("rows") % 2)
+    far_index = (other_core * (size // 2) + owner // 2) * clusters + far_cols.T % clusters
     high, low, target = call(
         prepare_kernel, "prepare",
         (
@@ -377,50 +387,54 @@
             shape(slots * rank, rank * clusters, dtype=bf16),
             shape(rank * clusters, LANES, dtype=bf16),
         ),
-        [HBM] * 2 + [ANY] * 2,
+        [HBM] * 2 + [ANY] * 3,
         in_hbm(jnp.transpose(coupling, (1, 2, 3, 0))), in_hbm(target_basis.reshape(clusters * rank, LANES)),
-        payload, placed,
+        payload, placed, far_index,
         scratch_shapes=[
             scratch(slots, rank, rank, clusters), scratch(clusters * rank, LANES, dtype=bf16),
             pltpu.SemaphoreType.DMA((2,)),
         ],
     )
-    blocks = pltpu.with_memory_space_constraint(
-        near_blocks.reshape(clusters * slots, LANES, LANES), pltpu.VMEM
-    )
-
-    def far_of(got):
-        return call(
-            functools.partial(far_kernel, per_group), "far", shape(rows, LANES), [VMEM, SMEM] + [VMEM] * 3,
-            got, far_index, high, low, target, scratch_shapes=[scratch(size * head, LANES)],
+    blocks = in_hbm(near_blocks.reshape(clusters * slots, LANES, LANES))
+
+    def far_of(got, relay):
+        far, near = call(
+            functools.partial(far_kernel, per_group), "far",
+            (shape(rows, LANES), pltpu.VMEM(blocks.shape, bf16)), [VMEM] * 2 + [SMEM] + [VMEM] * 3 + [HBM, ANY],
+            *got, far_index, high, low, target, blocks, relay,
+            scratch_shapes=[scratch(size * head, LANES), pltpu.SemaphoreType.DMA((8,))],
         )
-
-    def relayed(held, far):
-        both = call(
-            relay_kernel, "relay", shape(2 * rows, LANES, dtype=bf16), [VMEM] * 2 + [ANY], *held[2:], far
-        )
-        return swapped(both, core_mate)
+        return far, pltpu.with_memory_space_constraint(near, pltpu.VMEM)
+
+    def relay_of(held):
+        return call(relay_kernel, "relay", shape(2 * rows, LANES, dtype=bf16), [VMEM] * 2, *held[2:])
 
     kept = [scratch(rows, LANES), scratch(6 * rows + R, LANES)]
-    far = far_of(got0)
+    relay = relay_of(held)
+    relayed = swapped(relay, core_mate)
+    far, near_here = far_of(got, relay)
     image, lowered, payload = call(
-        functools.partial(first_kernel, per_group, unknowns), "near_one",
-        (shape(rows, LANES), shape(rows, LANES, dtype=bf16), payload_shape),
-        [VMEM] * 5 + [SMEM] + [VMEM] * 5,
-        *held, relayed(held, far), placed, blocks, field, far, got0, basis, scratch_shapes=kept,
-    )
-    got1 = exchange(payload)
+        functools.partial(first_kernel, per_group), "near_one",
+        (
+            shape(rows, LANES), shape(rows, LANES, dtype=bf16),
+            shape(size // 2, head + TAIL, LANES, dtype=bf16),
+        ),
+        [VMEM] * 5 + [SMEM] + [VMEM] * 4,
+        *held, relayed, placed, near_here, field, far, basis, scratch_shapes=kept,
+    )
+    got = gathered(payload)
     held = sends_of(lowered)
-    far = far_of(got1)
+    relay = relay_of(held)
+    relayed = swapped(relay, core_mate)
+    far, near_here = far_of(got, relay)
     candidate, sums = call(
         functools.partial(second_kernel, per_group, unknowns), "near_two",
-        (shape(rows, LANES), shape(size, R, LANES)), [VMEM] * 5 + [SMEM] + [VMEM] * 6,
-        *held, relayed(held, far), placed, blocks, field, image, far, got0, got1, scratch_shapes=kept,
-    )
-    got2 = exchange(sums)
+        (shape(rows, LANES), shape(size, R, LANES, dtype=bf16)), [VMEM] * 5 + [SMEM] + [VMEM] * 6,
+        *held, relayed, placed, near_here, field, image, far, *got, scratch_shapes=kept,
+    )
     return call(
         functools.partial(finish_kernel, per_group, unknowns), "finish", (shape(R, width), shape(R, width)),
-        [VMEM] * 6, field, image, candidate, got0, got1, got2,
+        [VMEM] * 6, field, image, candidate, *got, exchange(sums),
     )
 
 

time: 65.6 us -> 65.1 us (level)
  local copies, waits for them, and re-layouts: 7.46 us -> 0 us
  Pallas kernels: 15.3 us -> 21.4 us
  starting transfers between devices: 21.4 us -> 19.7 us
  blocking collectives: 10.2 us -> 11.1 us
  waiting for transfers between devices: 9.29 us -> 10.1 us
  other arithmetic: 0.71 us -> 1.43 us
    unnamed x8 -> x0, local copies, waits for them, and re-layouts: 7.46 us -> none
    pallas_call x9, Pallas kernels: 15.3 us -> 21.4 us  [call(): pl.pallas_call(kernel, out_shape=out, in_specs=ins, out_specs=jax.tree.ma...]
    all_to_all x2, starting transfers between devices: 11 us -> 6.71 us  [gathered(): got = lax.all_to_all(block, 'rows', 0, 0, axis_index_groups=groups)]
    ppermute x8 -> x10, waiting for transfers between devices: 1.88 us -> 4.61 us  [swapped(): lax.ppermute(block, 'rows', [(i, partner(i)) for i in range(lax.axis_size...]
    ppermute x8 -> x10, starting transfers between devices: 10.4 us -> 13 us  [swapped(): lax.ppermute(block, 'rows', [(i, partner(i)) for i in range(lax.axis_size...]
    all_to_all x2, waiting for transfers between devices: 7.42 us -> 5.53 us  [gathered(): got = lax.all_to_all(block, 'rows', 0, 0, axis_index_groups=groups)]
    all_to_all x1, blocking collectives: 10.2 us -> 11.1 us  [exchange(): return lax.all_to_all(block, 'rows', 0, 0)]
    add x0 -> x1, other arithmetic: none -> 0.71 us  [on_device(): (other_core * (size // 2) + owner // 2) * clusters + far_cols.T % clusters]
  transfers between devices with their start and end apart: 10 -> 12, of which waited for: 4 -> 3; matrix products, arithmetic and copies ran while one was open for 1% -> 2% of each run, Pallas kernels for 8% -> 18%
where the time goes in v9:
time: 65.1 us; the launch traced here: 64.6 us
  Pallas kernels  21.4 us (33%)
  starting transfers between devices  19.7 us (30%)
  blocking collectives  11.1 us (17%)
  waiting for transfers between devices  10.1 us (16%)
  other arithmetic  1.43 us (2%)
  between operations  0.82 us (1%)
    pallas_call x9, Pallas kernels, call(): pl.pallas_call(kernel, out_shape=out, in_specs=ins, out_specs=jax.tree.ma...  21.4 us
    ppermute x10, starting transfers between devices, swapped(): lax.ppermute(block, 'rows', [(i, partner(i)) for i in range(lax.axis_size...  13 us
    all_to_all x1, blocking collectives, exchange(): return lax.all_to_all(block, 'rows', 0, 0)  11.1 us
    all_to_all x2, starting transfers between devices, gathered(): got = lax.all_to_all(block, 'rows', 0, 0, axis_index_groups=groups)  6.71 us
    all_to_all x2, waiting for transfers between devices, gathered(): got = lax.all_to_all(block, 'rows', 0, 0, axis_index_groups=groups)  5.53 us
    ppermute x10, waiting for transfers between devices, swapped(): lax.ppermute(block, 'rows', [(i, partner(i)) for i in range(lax.axis_size...  4.61 us
  transfers between devices with their start and end apart: 12, of which 3 were waited for; matrix products, arithmetic and copies ran while one was open for 2% of the time, Pallas kernels for 18%

profile of v9, /device:TPU:0, one launch (start us, length us, event | category | flops | bytes accessed | tf_op | source)
XLA Modules:
  0.0 64.6 jit_solution(17655933398234943132)
XLA Ops:
  0.6 1.8 %start.1 = (f32[256,128]{1,0:T(8,128)S(1)}, bf16[512,128]{1,0:T(8,128)(2,1)S(1)}, bf16[256,128]{1,0:T(8,128)(2,1)S(1)}, bf16[8,32,128]{2,1,0:T(8,128)(2,1)}) custom-call(f32[8,4096]{1,0:T(8,128)} %b_hbm.1, bf16[512,128]{1,0:T(8,128)(2,1)} %bitcast.28), custom_call_target="tpu_custom_call" | custom-call | tf_op jit(solution)/shard_map/start/pallas_call | solution.py:350
  2.5 3.0 %collective-permute-start.1 = (bf16[256,128]{1,0:T(8,128)(2,1)S(1)}, bf16[256,128]{1,0:T(8,128)(2,1)S(1)}, u32[]{:S(2)}, u32[]{:S(2)}) collective-permute-start(bf16[256,128]{1,0:T(8,128)(2,1)S(1)} %get-tuple-element.19.own), channel_id=1, source_target_pairs={{0,2},{1,3},{2,0},{3,1},{4,6},{5,7},{6,4},{7,5},{8,10},{9,11},{10,... | collective-permute-start | bytes 196616 | tf_op jit(solution)/shard_map/ppermute | solution.py:288
  5.5 3.5 %collective-permute-start.2 = (bf16[256,128]{1,0:T(8,128)(2,1)S(1)}, bf16[256,128]{1,0:T(8,128)(2,1)S(1)}, u32[]{:S(2)}, u32[]{:S(2)}) collective-permute-start(bf16[256,128]{1,0:T(8,128)(2,1)S(1)} %get-tuple-element.19.own), channel_id=1, source_target_pairs={{0,14},{1,15},{2,4},{3,5},{4,2},{5,3},{6,8},{7,9},{8,6},{9,7},{10,... | collective-permute-start | bytes 196616 | tf_op jit(solution)/shard_map/ppermute | solution.py:288
  9.0 3.4 %all-to-all-start = ((bf16[8,32,128]{2,1,0:T(8,128)(2,1)}), bf16[8,32,128]{2,1,0:T(8,128)(2,1)S(1)}, u32[]{:S(2)}, u32[]{:S(2)}) async-start(bf16[8,32,128]{2,1,0:T(8,128)(2,1)} %get-tuple-element.20._), calls=%async_computation | async-start | bytes 131072 | tf_op jit(solution)/shard_map/all_to_all | solution.py:360
  12.4 0.7 %fusion.2.__.placed = s32[8,32]{1,0:T(8,128)S(1)} fusion(s32[32,8]{0,1:T(8,128)} %param.10, s32[]{:T(128)S(6)} %sub.32, s32[]{:T(128)S(6)} %select_n.83, s32[]{:T(128)S(6)} %select_n.82, s32[]{:T(128)S(6)} %add.66, s32[]{:T(128)S(6)} %mul.15, s32[32]{0:T(128)} %param.11), kind=kLoop, calls=%fused_computation.20 | loop fusion | flops 11776 | bytes 2196 | tf_op jit(solution)/shard_map/jit(_where)/select_n | solution.py:379
  13.2 0.6 collective-permute-start.3
  13.8 5.5 %all-to-all-done.got = bf16[8,32,128]{2,1,0:T(8,128)(2,1)S(1)} async-done(((bf16[8,32,128]{2,1,0:T(8,128)(2,1)}), bf16[8,32,128]{2,1,0:T(8,128)(2,1)S(1)}, u32[]{:S(2)}, u32[]{:S(2)}) %all-to-all-start) | async-done | bytes 65568 | tf_op jit(solution)/shard_map/all_to_all | solution.py:360
  19.3 0.7 %fusion.7.___.far_cols = s32[8,32]{1,0:T(8,128)S(1)} fusion(s32[32,8]{0,1:T(8,128)} %param.15, s32[]{:T(128)S(6)} %select_n.81), kind=kLoop, calls=%fused_computation.25 | loop fusion | flops 11008 | bytes 2052 | tf_op jit(solution)/shard_map/add | solution.py:382
  20.0 1.6 %prepare.1 = (bf16[128,512]{1,0:T(8,128)(2,1)S(1)}, bf16[128,512]{1,0:T(8,128)(2,1)S(1)}, bf16[512,128]{1,0:T(8,128)(2,1)S(1)}) custom-call(f32[8,16,16,32]{3,2,1,0:T(8,128)} %bitcast.26, bf16[512,128]{1,0:T(8,128)(2,1)} %bitcast.27, bf16[8,32,128]{2,1,0:T(8,128)(2,1)} %get-tuple-element.20._, s32[8,32]{1,0:T(8,128)S(1)} %fusion.2.__.placed, ...), custom_call_target="tpu_custom_call" | custom-call | tf_op jit(solution)/shard_map/prepare/pallas_call | solution.py:350
  21.6 4.9 %far.2 = (f32[256,128]{1,0:T(8,128)S(1)}, bf16[256,128,128]{2,1,0:T(8,128)(2,1)S(1)}) custom-call(bf16[8,32,128]{2,1,0:T(8,128)(2,1)S(1)} %all-to-all-done.got, bf16[8,32,128]{2,1,0:T(8,128)(2,1)S(1)} %collective-permute-done.4.got_mate, s32[8,32]{1,0:T(8,128)S(1)} %fusion.7.___.far_cols, bf16[128,512]{1,0:T(8,128)(2,1)S(1)} %get-tuple-element.21.high, ...), custom_call_target="tpu_custom_call" | custom-call | tf_op jit(solution)/shard_map/far/pallas_call | solution.py:350
  26.6 3.7 %near_one.1 = (f32[256,128]{1,0:T(8,128)S(1)}, bf16[256,128]{1,0:T(8,128)(2,1)S(1)}, bf16[8,48,128]{2,1,0:T(8,128)(2,1)}) custom-call(bf16[256,128]{1,0:T(8,128)(2,1)S(1)} %get-tuple-element.19.own, bf16[256,128]{1,0:T(8,128)(2,1)S(1)} %collective-permute-done.mate, bf16[256,128]{1,0:T(8,128)(2,1)S(1)} %collective-permute-done.1.even, ...), custom_call_target="tpu_custom_call" | custom-call | tf_op jit(solution)/shard_map/near_one/pallas_call | solution.py:350
  30.3 3.4 %all-to-all-start.1 = ((bf16[8,48,128]{2,1,0:T(8,128)(2,1)}), bf16[8,48,128]{2,1,0:T(8,128)(2,1)S(1)}, u32[]{:S(2)}, u32[]{:S(2)}) async-start(bf16[8,48,128]{2,1,0:T(8,128)(2,1)} %get-tuple-element.29), calls=%async_computation.1 | async-start | bytes 196608 | tf_op jit(solution)/shard_map/all_to_all | solution.py:360
  33.6 1.9 %collective-permute-start.6 = (bf16[256,128]{1,0:T(8,128)(2,1)S(1)}, bf16[256,128]{1,0:T(8,128)(2,1)S(1)}, u32[]{:S(2)}, u32[]{:S(2)}) collective-permute-start(bf16[256,128]{1,0:T(8,128)(2,1)S(1)} %get-tuple-element.28.own), channel_id=1, source_target_pairs={{0,2},{1,3},{2,0},{3,1},{4,6},{5,7},{6,4},{7,5},{8,10},{9,11},{10,... | collective-permute-start | bytes 196616 | tf_op jit(solution)/shard_map/ppermute | solution.py:288
  35.6 3.3 %collective-permute-start.7 = (bf16[256,128]{1,0:T(8,128)(2,1)S(1)}, bf16[256,128]{1,0:T(8,128)(2,1)S(1)}, u32[]{:S(2)}, u32[]{:S(2)}) collective-permute-start(bf16[256,128]{1,0:T(8,128)(2,1)S(1)} %get-tuple-element.28.own), channel_id=1, source_target_pairs={{0,14},{1,15},{2,4},{3,5},{4,2},{5,3},{6,8},{7,9},{8,6},{9,7},{10,... | collective-permute-start | bytes 196616 | tf_op jit(solution)/shard_map/ppermute | solution.py:288
  38.9 0.0 collective-permute-done.6.even
  38.9 3.7 %collective-permute-done.7.odd = bf16[256,128]{1,0:T(8,128)(2,1)S(1)} collective-permute-done((bf16[256,128]{1,0:T(8,128)(2,1)S(1)}, bf16[256,128]{1,0:T(8,128)(2,1)S(1)}, u32[]{:S(2)}, u32[]{:S(2)}) %collective-permute-start.7) | collective-permute-done | bytes 65568 | tf_op jit(solution)/shard_map/ppermute | solution.py:288
  42.6 0.1 collective-permute-start.8
  42.7 0.5 collective-permute-start.9
  43.2 0.1 collective-permute-start.5
  43.2 0.9 %collective-permute-done.9.got_mate.got1_mate = bf16[8,48,128]{2,1,0:T(8,128)(2,1)S(1)} collective-permute-done((bf16[8,48,128]{2,1,0:T(8,128)(2,1)S(1)}, bf16[8,48,128]{2,1,0:T(8,128)(2,1)S(1)}, u32[]{:S(2)}, u32[]{:S(2)}) %collective-permute-start.9) | collective-permute-done | bytes 98336 | tf_op jit(solution)/shard_map/ppermute | solution.py:288
  44.1 4.9 %far.3 = (f32[256,128]{1,0:T(8,128)S(1)}, bf16[256,128,128]{2,1,0:T(8,128)(2,1)S(1)}) custom-call(bf16[8,48,128]{2,1,0:T(8,128)(2,1)S(1)} %all-to-all-done.1.got.got1, bf16[8,48,128]{2,1,0:T(8,128)(2,1)S(1)} %collective-permute-done.9.got_mate.got1_mate, s32[8,32]{1,0:T(8,128)S(1)} %fusion.7.___.far_cols, bf16[128,512]{1,0:T(8,128)(2,1)S(1)} %get-tuple-element.21.high, ...), custom_call_target="tpu_custom_call" | custom-call | tf_op jit(solution)/shard_map/far/pallas_call | solution.py:350
  49.1 3.0 %near_two.1 = (f32[256,128]{1,0:T(8,128)S(1)}, bf16[16,8,128]{2,1,0:T(8,128)(2,1)S(1)}) custom-call(bf16[256,128]{1,0:T(8,128)(2,1)S(1)} %get-tuple-element.28.own, bf16[256,128]{1,0:T(8,128)(2,1)S(1)} %collective-permute-done.5.mate, bf16[256,128]{1,0:T(8,128)(2,1)S(1)} %collective-permute-done.6.even, bf16[256,128]{1,0:T(8,128)(2,1)S(1)} %collective-permute-done.7.odd, ...), custom_call_target="tpu_custom_call" | custom-call | tf_op jit(solution)/shard_map/near_two/pallas_call | solution.py:350
  52.1 11.1 %all_to_all.15.got2 = bf16[16,8,128]{2,1,0:T(8,128)(2,1)S(1)} all-to-all(bf16[16,8,128]{2,1,0:T(8,128)(2,1)S(1)} %get-tuple-element.33), channel_id=1, replica_groups=mesh['groups'=2,'rows'=16] {'rows'}, dimensions={0} | all-to-all | bytes 65536 | tf_op jit(solution)/shard_map/all_to_all | solution.py:356
  63.2 1.5 %finish.1 = (f32[8,4096]{1,0:T(8,128)}, f32[8,4096]{1,0:T(8,128)}) custom-call(f32[256,128]{1,0:T(8,128)S(1)} %get-tuple-element.18.b, f32[256,128]{1,0:T(8,128)S(1)} %get-tuple-element.27.image, f32[256,128]{1,0:T(8,128)S(1)} %get-tuple-element.32.candidate, bf16[8,48,128]{2,1,0:T(8,128)(2,1)S(1)} %all-to-all-done.1.got.got1, ...), custom_call_target="tpu_custom_call" | custom-call | tf_op jit(solution)/shard_map/finish/pallas_call | solution.py:350
  (12 shorter events, 0.0 us)
Async XLA Ops:
  2.5 10.7 %collective-permute-start.1 = (bf16[256,128]{1,0:T(8,128)(2,1)S(1)}, bf16[256,128]{1,0:T(8,128)(2,1)S(1)}, u32[]{:S(2)}, u32[]{:S(2)}) collective-permute-start(bf16[256,128]{1,0:T(8,128)(2,1)S(1)} %get-tuple-element.19.own), channel_id=1, source_target_pairs={{0,2},{1,3},{2,0},{3,1},{4,6},{5,7},{6,4},{7,5},{8,10},{9,11},{10,... | collective-permute-start | bytes 196616 | tf_op jit(solution)/shard_map/ppermute | solution.py:288
  5.5 7.7 %collective-permute-start.2 = (bf16[256,128]{1,0:T(8,128)(2,1)S(1)}, bf16[256,128]{1,0:T(8,128)(2,1)S(1)}, u32[]{:S(2)}, u32[]{:S(2)}) collective-permute-start(bf16[256,128]{1,0:T(8,128)(2,1)S(1)} %get-tuple-element.19.own), channel_id=1, source_target_pairs={{0,14},{1,15},{2,4},{3,5},{4,2},{5,3},{6,8},{7,9},{8,6},{9,7},{10,... | collective-permute-start | bytes 196616 | tf_op jit(solution)/shard_map/ppermute | solution.py:288
  9.0 17.5 %collective-permute-start = (bf16[256,128]{1,0:T(8,128)(2,1)S(1)}, bf16[256,128]{1,0:T(8,128)(2,1)S(1)}, u32[]{:S(2)}, u32[]{:S(2)}) collective-permute-start(bf16[256,128]{1,0:T(8,128)(2,1)S(1)} %get-tuple-element.19.own), channel_id=1, source_target_pairs={{0,1},{1,0},{2,3},{3,2},{4,5},{5,4},{6,7},{7,6},{8,9},{9,8},{10,11... | collective-permute-start | bytes 196616 | tf_op jit(solution)/shard_map/ppermute | solution.py:288
  9.0 10.3 %all-to-all-start = ((bf16[8,32,128]{2,1,0:T(8,128)(2,1)}), bf16[8,32,128]{2,1,0:T(8,128)(2,1)S(1)}, u32[]{:S(2)}, u32[]{:S(2)}) async-start(bf16[8,32,128]{2,1,0:T(8,128)(2,1)} %get-tuple-element.20._), calls=%async_computation | async-start | bytes 131072 | tf_op jit(solution)/shard_map/all_to_all | solution.py:360
  13.2 13.4 %collective-permute-start.3 = (bf16[512,128]{1,0:T(8,128)(2,1)S(1)}, bf16[512,128]{1,0:T(8,128)(2,1)S(1)}, u32[]{:S(2)}, u32[]{:S(2)}) collective-permute-start(bf16[512,128]{1,0:T(8,128)(2,1)S(1)} %relay.2._), channel_id=1, source_target_pairs={{0,1},{1,0},{2,3},{3,2},{4,5},{5,4},{6,7},{7,6},{8,9},{9,8},{10,11... | collective-permute-start | bytes 393224 | tf_op jit(solution)/shard_map/ppermute | solution.py:288
  19.3 2.3 %collective-permute-start.4 = (bf16[8,32,128]{2,1,0:T(8,128)(2,1)S(1)}, bf16[8,32,128]{2,1,0:T(8,128)(2,1)S(1)}, u32[]{:S(2)}, u32[]{:S(2)}) collective-permute-start(bf16[8,32,128]{2,1,0:T(8,128)(2,1)S(1)} %all-to-all-done.got), channel_id=1, source_target_pairs={{0,1},{1,0},{2,3},{3,2},{4,5},{5,4},{6,7},{7,6},{8,9},{9,8},{10,11... | collective-permute-start | bytes 196616 | tf_op jit(solution)/shard_map/ppermute | solution.py:288
  30.3 12.4 %all-to-all-start.1 = ((bf16[8,48,128]{2,1,0:T(8,128)(2,1)}), bf16[8,48,128]{2,1,0:T(8,128)(2,1)S(1)}, u32[]{:S(2)}, u32[]{:S(2)}) async-start(bf16[8,48,128]{2,1,0:T(8,128)(2,1)} %get-tuple-element.29), calls=%async_computation.1 | async-start | bytes 196608 | tf_op jit(solution)/shard_map/all_to_all | solution.py:360
  33.6 5.3 %collective-permute-start.6 = (bf16[256,128]{1,0:T(8,128)(2,1)S(1)}, bf16[256,128]{1,0:T(8,128)(2,1)S(1)}, u32[]{:S(2)}, u32[]{:S(2)}) collective-permute-start(bf16[256,128]{1,0:T(8,128)(2,1)S(1)} %get-tuple-element.28.own), channel_id=1, source_target_pairs={{0,2},{1,3},{2,0},{3,1},{4,6},{5,7},{6,4},{7,5},{8,10},{9,11},{10,... | collective-permute-start | bytes 196616 | tf_op jit(solution)/shard_map/ppermute | solution.py:288
  35.6 7.0 %collective-permute-start.7 = (bf16[256,128]{1,0:T(8,128)(2,1)S(1)}, bf16[256,128]{1,0:T(8,128)(2,1)S(1)}, u32[]{:S(2)}, u32[]{:S(2)}) collective-permute-start(bf16[256,128]{1,0:T(8,128)(2,1)S(1)} %get-tuple-element.28.own), channel_id=1, source_target_pairs={{0,14},{1,15},{2,4},{3,5},{4,2},{5,3},{6,8},{7,9},{8,6},{9,7},{10,... | collective-permute-start | bytes 196616 | tf_op jit(solution)/shard_map/ppermute | solution.py:288
  42.6 6.5 %collective-permute-start.8 = (bf16[512,128]{1,0:T(8,128)(2,1)S(1)}, bf16[512,128]{1,0:T(8,128)(2,1)S(1)}, u32[]{:S(2)}, u32[]{:S(2)}) collective-permute-start(bf16[512,128]{1,0:T(8,128)(2,1)S(1)} %relay.3._), channel_id=1, source_target_pairs={{0,1},{1,0},{2,3},{3,2},{4,5},{5,4},{6,7},{7,6},{8,9},{9,8},{10,11... | collective-permute-start | bytes 393224 | tf_op jit(solution)/shard_map/ppermute | solution.py:288
  42.7 1.5 %collective-permute-start.9 = (bf16[8,48,128]{2,1,0:T(8,128)(2,1)S(1)}, bf16[8,48,128]{2,1,0:T(8,128)(2,1)S(1)}, u32[]{:S(2)}, u32[]{:S(2)}) collective-permute-start(bf16[8,48,128]{2,1,0:T(8,128)(2,1)S(1)} %all-to-all-done.1.got.got1), channel_id=1, source_target_pairs={{0,1},{1,0},{2,3},{3,2},{4,5},{5,4},{6,7},{7,6},{8,9},{9,8},{10,11... | collective-permute-start | bytes 294920 | tf_op jit(solution)/shard_map/ppermute | solution.py:288
  43.2 5.9 %collective-permute-start.5 = (bf16[256,128]{1,0:T(8,128)(2,1)S(1)}, bf16[256,128]{1,0:T(8,128)(2,1)S(1)}, u32[]{:S(2)}, u32[]{:S(2)}) collective-permute-start(bf16[256,128]{1,0:T(8,128)(2,1)S(1)} %get-tuple-element.28.own), channel_id=1, source_target_pairs={{0,1},{1,0},{2,3},{3,2},{4,5},{5,4},{6,7},{7,6},{8,9},{9,8},{10,11... | collective-permute-start | bytes 196616 | tf_op jit(solution)/shard_map/ppermute | solution.py:288

commit v10 on v9

--- a/solution.py
+++ b/solution.py
@@ -123,19 +123,22 @@
     target_out[...] = dot((column == wanted).astype(bf16), target[...]).astype(bf16)
 
 
-def far_kernel(
-    per_group, got, got_mate, far_cols, high, low, target, blocks_hbm, _, far, blocks, table, sems,
-):
+def chunk_copies(source, first, target, sems):
     chunks = sems.shape[0]
-    each = blocks.shape[0] // chunks
+    each = target.shape[0] // chunks
     copies = [
         pltpu.make_async_copy(
-            blocks_hbm.at[pl.ds(c * each, each)], blocks.at[pl.ds(c * each, each)], sems.at[c]
+            source.at[pl.ds(first + c * each, each)], target.at[pl.ds(c * each, each)], sems.at[c]
         )
         for c in range(chunks)
     ]
-    for copy in copies:
-        copy.start()
+    for c, copy in enumerate(copies):
+        copy.start(priority=c % 2)
+    return copies
+
+
+def far_kernel(per_group, got, got_mate, far_cols, high, low, target, blocks_hbm, far, blocks, table, sems):
+    copies = chunk_copies(blocks_hbm, 0, blocks, sems)
     slots, clusters = far_cols.shape
     rank = LANES // per_group
     groups = clusters // per_group
@@ -174,14 +177,20 @@
         copy.wait()
 
 
-def relay_kernel(even, odd, both):
+def behind_kernel(values, _, out):
+    out[...] = values[...]
+
+
+def relay_kernel(even, odd, _, both):
     rows = even.shape[0]
     both[pl.ds(0, rows), :] = even[...]
     both[pl.ds(rows, rows), :] = odd[...]
 
 
-def near_field(slabs, placed, blocks, near, window):
+def near_field(slabs, placed, blocks, blocks_hbm, near, window, later, sems):
     slots, clusters = placed.shape
+    copies = chunk_copies(blocks_hbm, blocks.shape[0], later, sems)
+    each = later.shape[0] // len(copies)
     at = 0
     for slab in slabs:
         window[pl.ds(at, slab.shape[0]), :] = slab[...].astype(f32)
@@ -192,9 +201,13 @@
         return window[pl.ds(pl.multiple_of(placed[k, i] * R, R), R), :]
 
     def block(k, i):
-        return blocks[i * slots + k]
+        at = i * slots + k
+        return blocks[at] if at < blocks.shape[0] else later[at - blocks.shape[0]]
 
     for i in range(0, clusters, 2):
+        beyond = i * slots - blocks.shape[0]
+        if beyond >= 0 and beyond % each == 0:
+            copies[beyond // each].wait()
         both = jnp.zeros((2 * R, 2 * LANES), f32)
         for k in range(0, slots, 2):
             sources = jnp.concatenate(
@@ -209,9 +222,10 @@
 
 
 def first_kernel(
-    per_group, own, mate, even, odd, relayed, placed, blocks, b, far, basis, image, lowered, payload, near, window,
+    per_group, own, mate, even, odd, relayed, placed, blocks, blocks_hbm, b, far, basis,
+    image, lowered, payload, near, window, later, sems,
 ):
-    near_field((own, mate, even, odd, relayed), placed, blocks, near, window)
+    near_field((own, mate, even, odd, relayed), placed, blocks, blocks_hbm, near, window, later, sems)
     clusters = placed.shape[1]
     tiles = []
     sums = [jnp.zeros((R, LANES), f32) for _ in range(3)]
@@ -239,10 +253,10 @@
 
 
 def second_kernel(
-    per_group, unknowns, own, mate, even, odd, relayed, placed, blocks, b, image, far, got, got_mate,
-    candidate, sums_out, near, window,
+    per_group, unknowns, own, mate, even, odd, relayed, placed, blocks, blocks_hbm, b, image, far,
+    got, got_mate, candidate, sums_out, near, window, later, sems,
 ):
-    near_field((own, mate, even, odd, relayed), placed, blocks, near, window)
+    near_field((own, mate, even, odd, relayed), placed, blocks, blocks_hbm, near, window, later, sems)
     clusters = placed.shape[1]
     head = clusters // per_group * R
     start_norm, h11, h21, _, _, _ = arnoldi_one(*read_sums((got, got_mate), head, TAIL, 3, unknowns))
@@ -355,10 +369,9 @@
     def exchange(block):
         return lax.all_to_all(block, "rows", 0, 0)
 
-    def gathered(block):
+    def gather(block):
         groups = [list(range(core, size, 2)) for core in range(2)]
-        got = lax.all_to_all(block, "rows", 0, 0, axis_index_groups=groups)
-        return got, swapped(got, core_mate)
+        return lax.all_to_all(block, "rows", 0, 0, axis_index_groups=groups)
 
     field, basis, lowered, payload = call(
         functools.partial(start_kernel, per_group), "start",
@@ -369,7 +382,7 @@
         [HBM] * 2, in_hbm(right_sides), in_hbm(basis_in.reshape(clusters * rank, LANES)),
         scratch_shapes=[scratch(R, width), pltpu.SemaphoreType.DMA((2,))],
     )
-    got = gathered(payload)
+    got = gather(payload)
     held = sends_of(lowered)
 
     reach = 2 * clusters
@@ -397,40 +410,46 @@
     )
     blocks = in_hbm(near_blocks.reshape(clusters * slots, LANES, LANES))
 
-    def far_of(got, relay):
-        far, near = call(
+    here = blocks.shape[0] // 2
+
+    def far_of(got):
+        far, first = call(
             functools.partial(far_kernel, per_group), "far",
-            (shape(rows, LANES), pltpu.VMEM(blocks.shape, bf16)), [VMEM] * 2 + [SMEM] + [VMEM] * 3 + [HBM, ANY],
-            *got, far_index, high, low, target, blocks, relay,
-            scratch_shapes=[scratch(size * head, LANES), pltpu.SemaphoreType.DMA((8,))],
+            (shape(rows, LANES), pltpu.VMEM((here, LANES, LANES), bf16)), [VMEM] * 2 + [SMEM] + [VMEM] * 3 + [HBM],
+            *got, far_index, high, low, target, blocks,
+            scratch_shapes=[scratch(size * head, LANES), pltpu.SemaphoreType.DMA((4,))],
         )
-        return far, pltpu.with_memory_space_constraint(near, pltpu.VMEM)
-
-    def relay_of(held):
-        return call(relay_kernel, "relay", shape(2 * rows, LANES, dtype=bf16), [VMEM] * 2, *held[2:])
-
-    kept = [scratch(rows, LANES), scratch(6 * rows + R, LANES)]
-    relay = relay_of(held)
-    relayed = swapped(relay, core_mate)
-    far, near_here = far_of(got, relay)
+        return far, pltpu.with_memory_space_constraint(first, pltpu.VMEM)
+
+    def relayed(held, far):
+        both = call(
+            relay_kernel, "relay", shape(2 * rows, LANES, dtype=bf16), [VMEM] * 2 + [ANY], *held[2:], far
+        )
+        return swapped(both, core_mate)
+
+    kept = [
+        scratch(rows, LANES), scratch(6 * rows + R, LANES),
+        scratch(blocks.shape[0] - here, LANES, LANES, dtype=bf16), pltpu.SemaphoreType.DMA((4,)),
+    ]
+    got = call(behind_kernel, "behind", shape(*got.shape, dtype=bf16), [VMEM, ANY], got, target)
+    far, first = far_of((got, swapped(got, core_mate)))
     image, lowered, payload = call(
         functools.partial(first_kernel, per_group), "near_one",
         (
             shape(rows, LANES), shape(rows, LANES, dtype=bf16),
             shape(size // 2, head + TAIL, LANES, dtype=bf16),
         ),
-        [VMEM] * 5 + [SMEM] + [VMEM] * 4,
-        *held, relayed, placed, near_here, field, far, basis, scratch_shapes=kept,
-    )
-    got = gathered(payload)
+        [VMEM] * 5 + [SMEM, VMEM, HBM] + [VMEM] * 3,
+        *held, relayed(held, far), placed, first, blocks, field, far, basis, scratch_shapes=kept,
+    )
+    got = gather(payload)
+    got = (got, swapped(got, core_mate))
     held = sends_of(lowered)
-    relay = relay_of(held)
-    relayed = swapped(relay, core_mate)
-    far, near_here = far_of(got, relay)
+    far, first = far_of(got)
     candidate, sums = call(
         functools.partial(second_kernel, per_group, unknowns), "near_two",
-        (shape(rows, LANES), shape(size, R, LANES, dtype=bf16)), [VMEM] * 5 + [SMEM] + [VMEM] * 6,
-        *held, relayed, placed, near_here, field, image, far, *got, scratch_shapes=kept,
+        (shape(rows, LANES), shape(size, R, LANES, dtype=bf16)), [VMEM] * 5 + [SMEM, VMEM, HBM] + [VMEM] * 5,
+        *held, relayed(held, far), placed, first, blocks, field, image, far, *got, scratch_shapes=kept,
     )
     return call(
         functools.partial(finish_kernel, per_group, unknowns), "finish", (shape(R, width), shape(R, width)),

time: 65.1 us -> 66.6 us (1.023)
  blocking collectives: 11.1 us -> 20.8 us
  starting transfers between devices: 19.7 us -> 11.7 us
    all_to_all x0 -> x1, blocking collectives: none -> 10.5 us  [gather(): return lax.all_to_all(block, 'rows', 0, 0, axis_index_groups=groups)]
    ppermute x10, starting transfers between devices: 13 us -> 4.39 us  [swapped(): lax.ppermute(block, 'rows', [(i, partner(i)) for i in range(lax.axis_size...]
    all_to_all x2 -> x1, waiting for transfers between devices: 5.53 us -> 3.89 us  [gather(): return lax.all_to_all(block, 'rows', 0, 0, axis_index_groups=groups)]
    ppermute x10, waiting for transfers between devices: 4.61 us -> 5.79 us  [swapped(): lax.ppermute(block, 'rows', [(i, partner(i)) for i in range(lax.axis_size...]
    all_to_all x1, blocking collectives: 11.1 us -> 10.3 us  [exchange(): return lax.all_to_all(block, 'rows', 0, 0)]
    all_to_all x2 -> x1, starting transfers between devices: 6.71 us -> 7.3 us  [gather(): return lax.all_to_all(block, 'rows', 0, 0, axis_index_groups=groups)]
    pallas_call x9 -> x10, Pallas kernels: 21.4 us -> 21.8 us  [call(): pl.pallas_call(kernel, out_shape=out, in_specs=ins, out_specs=jax.tree.ma...]
  transfers between devices with their start and end apart: 12 -> 11, of which waited for: 3 -> 5; matrix products, arithmetic and copies ran while one was open for 2% -> 2% of each run, Pallas kernels for 18% -> 13%
where the time goes in v10:
time: 66.6 us; the launch traced here: 66.2 us
  Pallas kernels  21.8 us (33%)
  blocking collectives  20.8 us (31%)
  starting transfers between devices  11.7 us (18%)
  waiting for transfers between devices  9.68 us (15%)
  other arithmetic  1.43 us (2%)
  between operations  0.72 us (1%)
    pallas_call x10, Pallas kernels, call(): pl.pallas_call(kernel, out_shape=out, in_specs=ins, out_specs=jax.tree.ma...  21.8 us
    all_to_all x1, blocking collectives, gather(): return lax.all_to_all(block, 'rows', 0, 0, axis_index_groups=groups)  10.5 us
    all_to_all x1, blocking collectives, exchange(): return lax.all_to_all(block, 'rows', 0, 0)  10.3 us
    all_to_all x1, starting transfers between devices, gather(): return lax.all_to_all(block, 'rows', 0, 0, axis_index_groups=groups)  7.3 us
    ppermute x10, waiting for transfers between devices, swapped(): lax.ppermute(block, 'rows', [(i, partner(i)) for i in range(lax.axis_size...  5.79 us
    ppermute x10, starting transfers between devices, swapped(): lax.ppermute(block, 'rows', [(i, partner(i)) for i in range(lax.axis_size...  4.39 us
    all_to_all x1, waiting for transfers between devices, gather(): return lax.all_to_all(block, 'rows', 0, 0, axis_index_groups=groups)  3.89 us
  transfers between devices with their start and end apart: 11, of which 5 were waited for; matrix products, arithmetic and copies ran while one was open for 2% of the time, Pallas kernels for 13%

profile of v10, /device:TPU:0, one launch (start us, length us, event | category | flops | bytes accessed | tf_op | source)
XLA Modules:
  0.0 66.2 jit_solution(1175925984639598231)
XLA Ops:
  0.6 1.8 %start.1 = (f32[256,128]{1,0:T(8,128)S(1)}, bf16[512,128]{1,0:T(8,128)(2,1)S(1)}, bf16[256,128]{1,0:T(8,128)(2,1)S(1)}, bf16[8,32,128]{2,1,0:T(8,128)(2,1)}) custom-call(f32[8,4096]{1,0:T(8,128)} %b_hbm.1, bf16[512,128]{1,0:T(8,128)(2,1)} %bitcast.30), custom_call_target="tpu_custom_call" | custom-call | tf_op jit(solution)/shard_map/start/pallas_call | solution.py:364
  2.5 7.3 %all-to-all-start = ((bf16[8,32,128]{2,1,0:T(8,128)(2,1)}), bf16[8,32,128]{2,1,0:T(8,128)(2,1)S(1)}, u32[]{:S(2)}, u32[]{:S(2)}) async-start(bf16[8,32,128]{2,1,0:T(8,128)(2,1)} %get-tuple-element.20._), calls=%async_computation | async-start | bytes 131072 | tf_op jit(solution)/shard_map/all_to_all | solution.py:374
  9.8 0.7 %fusion.2.__.placed = s32[8,32]{1,0:T(8,128)S(1)} fusion(s32[32,8]{0,1:T(8,128)} %param.10, s32[]{:T(128)S(6)} %sub.32, s32[]{:T(128)S(6)} %select_n.83, s32[]{:T(128)S(6)} %select_n.82, s32[]{:T(128)S(6)} %add.66, s32[]{:T(128)S(6)} %mul.15, s32[32]{0:T(128)} %param.11), kind=kLoop, calls=%fused_computation.20 | loop fusion | flops 11776 | bytes 2196 | tf_op jit(solution)/shard_map/jit(_where)/select_n | solution.py:392
  10.5 0.7 %fusion.7.___.far_cols = s32[8,32]{1,0:T(8,128)S(1)} fusion(s32[32,8]{0,1:T(8,128)} %param.15, s32[]{:T(128)S(6)} %select_n.81), kind=kLoop, calls=%fused_computation.25 | loop fusion | flops 11008 | bytes 2052 | tf_op jit(solution)/shard_map/add | solution.py:395
  11.2 1.6 %prepare.1 = (bf16[128,512]{1,0:T(8,128)(2,1)S(1)}, bf16[128,512]{1,0:T(8,128)(2,1)S(1)}, bf16[512,128]{1,0:T(8,128)(2,1)S(1)}) custom-call(f32[8,16,16,32]{3,2,1,0:T(8,128)} %bitcast.28, bf16[512,128]{1,0:T(8,128)(2,1)} %bitcast.29, bf16[8,32,128]{2,1,0:T(8,128)(2,1)} %get-tuple-element.20._, s32[8,32]{1,0:T(8,128)S(1)} %fusion.2.__.placed, ...), custom_call_target="tpu_custom_call" | custom-call | tf_op jit(solution)/shard_map/prepare/pallas_call | solution.py:364
  12.8 3.9 %all-to-all-done.values = bf16[8,32,128]{2,1,0:T(8,128)(2,1)S(1)} async-done(((bf16[8,32,128]{2,1,0:T(8,128)(2,1)}), bf16[8,32,128]{2,1,0:T(8,128)(2,1)S(1)}, u32[]{:S(2)}, u32[]{:S(2)}) %all-to-all-start) | async-done | bytes 65568 | tf_op jit(solution)/shard_map/all_to_all | solution.py:374
  16.7 1.0 %collective-permute-start.2 = (bf16[256,128]{1,0:T(8,128)(2,1)S(1)}, bf16[256,128]{1,0:T(8,128)(2,1)S(1)}, u32[]{:S(2)}, u32[]{:S(2)}) collective-permute-start(bf16[256,128]{1,0:T(8,128)(2,1)S(1)} %get-tuple-element.19.own), channel_id=1, source_target_pairs={{0,14},{1,15},{2,4},{3,5},{4,2},{5,3},{6,8},{7,9},{8,6},{9,7},{10,... | collective-permute-start | bytes 196616 | tf_op jit(solution)/shard_map/ppermute | solution.py:302
  17.7 0.8 %collective-permute-start.1 = (bf16[256,128]{1,0:T(8,128)(2,1)S(1)}, bf16[256,128]{1,0:T(8,128)(2,1)S(1)}, u32[]{:S(2)}, u32[]{:S(2)}) collective-permute-start(bf16[256,128]{1,0:T(8,128)(2,1)S(1)} %get-tuple-element.19.own), channel_id=1, source_target_pairs={{0,2},{1,3},{2,0},{3,1},{4,6},{5,7},{6,4},{7,5},{8,10},{9,11},{10,... | collective-permute-start | bytes 196616 | tf_op jit(solution)/shard_map/ppermute | solution.py:302
  18.4 3.6 %far.2 = (f32[256,128]{1,0:T(8,128)S(1)}, bf16[128,128,128]{2,1,0:T(8,128)(2,1)S(1)}) custom-call(bf16[8,32,128]{2,1,0:T(8,128)(2,1)S(1)} %behind.1.got, bf16[8,32,128]{2,1,0:T(8,128)(2,1)S(1)} %collective-permute-done.3.got_mate, s32[8,32]{1,0:T(8,128)S(1)} %fusion.7.___.far_cols, bf16[128,512]{1,0:T(8,128)(2,1)S(1)} %get-tuple-element.22.high, ...), custom_call_target="tpu_custom_call" | custom-call | tf_op jit(solution)/shard_map/far/pallas_call | solution.py:364
  22.0 1.8 %collective-permute-done.2.odd = bf16[256,128]{1,0:T(8,128)(2,1)S(1)} collective-permute-done((bf16[256,128]{1,0:T(8,128)(2,1)S(1)}, bf16[256,128]{1,0:T(8,128)(2,1)S(1)}, u32[]{:S(2)}, u32[]{:S(2)}) %collective-permute-start.2) | collective-permute-done | bytes 65568 | tf_op jit(solution)/shard_map/ppermute | solution.py:302
  23.9 0.1 collective-permute-start.4
  24.0 0.5 collective-permute-start
  24.5 0.9 %collective-permute-done.mate = bf16[256,128]{1,0:T(8,128)(2,1)S(1)} collective-permute-done((bf16[256,128]{1,0:T(8,128)(2,1)S(1)}, bf16[256,128]{1,0:T(8,128)(2,1)S(1)}, u32[]{:S(2)}, u32[]{:S(2)}) %collective-permute-start) | collective-permute-done | bytes 65568 | tf_op jit(solution)/shard_map/ppermute | solution.py:302
  25.4 4.9 %near_one.1 = (f32[256,128]{1,0:T(8,128)S(1)}, bf16[256,128]{1,0:T(8,128)(2,1)S(1)}, bf16[8,48,128]{2,1,0:T(8,128)(2,1)S(1)}) custom-call(bf16[256,128]{1,0:T(8,128)(2,1)S(1)} %get-tuple-element.19.own, bf16[256,128]{1,0:T(8,128)(2,1)S(1)} %collective-permute-done.mate, bf16[256,128]{1,0:T(8,128)(2,1)S(1)} %collective-permute-done.1.even, ...), custom_call_target="tpu_custom_call" | custom-call | tf_op jit(solution)/shard_map/near_one/pallas_call | solution.py:364
  30.3 10.5 %all_to_all.15.got.got1 = bf16[8,48,128]{2,1,0:T(8,128)(2,1)S(1)} all-to-all(bf16[8,48,128]{2,1,0:T(8,128)(2,1)S(1)} %get-tuple-element.29), channel_id=1, replica_groups={{0,2,4,6,8,10,12,14},{1,3,5,7,9,11,13,15},{16,18,20,22,24,26,28,30},{17..., dimensions={0} | all-to-all | bytes 196608 | tf_op jit(solution)/shard_map/all_to_all | solution.py:374
  40.8 1.1 %collective-permute-start.7 = (bf16[256,128]{1,0:T(8,128)(2,1)S(1)}, bf16[256,128]{1,0:T(8,128)(2,1)S(1)}, u32[]{:S(2)}, u32[]{:S(2)}) collective-permute-start(bf16[256,128]{1,0:T(8,128)(2,1)S(1)} %get-tuple-element.28.own), channel_id=1, source_target_pairs={{0,14},{1,15},{2,4},{3,5},{4,2},{5,3},{6,8},{7,9},{8,6},{9,7},{10,... | collective-permute-start | bytes 196616 | tf_op jit(solution)/shard_map/ppermute | solution.py:302
  41.9 0.4 collective-permute-start.6
  42.3 3.6 %far.3 = (f32[256,128]{1,0:T(8,128)S(1)}, bf16[128,128,128]{2,1,0:T(8,128)(2,1)S(1)}) custom-call(bf16[8,48,128]{2,1,0:T(8,128)(2,1)S(1)} %all_to_all.15.got.got1, bf16[8,48,128]{2,1,0:T(8,128)(2,1)S(1)} %collective-permute-done.8.got_mate.got1_mate, s32[8,32]{1,0:T(8,128)S(1)} %fusion.7.___.far_cols, bf16[128,512]{1,0:T(8,128)(2,1)S(1)} %get-tuple-element.22.high, ...), custom_call_target="tpu_custom_call" | custom-call | tf_op jit(solution)/shard_map/far/pallas_call | solution.py:364
  46.0 2.1 %collective-permute-done.7.odd = bf16[256,128]{1,0:T(8,128)(2,1)S(1)} collective-permute-done((bf16[256,128]{1,0:T(8,128)(2,1)S(1)}, bf16[256,128]{1,0:T(8,128)(2,1)S(1)}, u32[]{:S(2)}, u32[]{:S(2)}) %collective-permute-start.7) | collective-permute-done | bytes 65568 | tf_op jit(solution)/shard_map/ppermute | solution.py:302
  48.1 0.5 collective-permute-start.5
  48.6 0.9 %collective-permute-done.5.mate = bf16[256,128]{1,0:T(8,128)(2,1)S(1)} collective-permute-done((bf16[256,128]{1,0:T(8,128)(2,1)S(1)}, bf16[256,128]{1,0:T(8,128)(2,1)S(1)}, u32[]{:S(2)}, u32[]{:S(2)}) %collective-permute-start.5) | collective-permute-done | bytes 65568 | tf_op jit(solution)/shard_map/ppermute | solution.py:302
  49.6 4.8 %near_two.1 = (f32[256,128]{1,0:T(8,128)S(1)}, bf16[16,8,128]{2,1,0:T(8,128)(2,1)S(1)}) custom-call(bf16[256,128]{1,0:T(8,128)(2,1)S(1)} %get-tuple-element.28.own, bf16[256,128]{1,0:T(8,128)(2,1)S(1)} %collective-permute-done.5.mate, bf16[256,128]{1,0:T(8,128)(2,1)S(1)} %collective-permute-done.6.even, bf16[256,128]{1,0:T(8,128)(2,1)S(1)} %collective-permute-done.7.odd, ...), custom_call_target="tpu_custom_call" | custom-call | tf_op jit(solution)/shard_map/near_two/pallas_call | solution.py:364
  54.4 10.3 %all_to_all.16.got2 = bf16[16,8,128]{2,1,0:T(8,128)(2,1)S(1)} all-to-all(bf16[16,8,128]{2,1,0:T(8,128)(2,1)S(1)} %get-tuple-element.33), channel_id=1, replica_groups=mesh['groups'=2,'rows'=16] {'rows'}, dimensions={0} | all-to-all | bytes 65536 | tf_op jit(solution)/shard_map/all_to_all | solution.py:370
  64.7 1.5 %finish.1 = (f32[8,4096]{1,0:T(8,128)}, f32[8,4096]{1,0:T(8,128)}) custom-call(f32[256,128]{1,0:T(8,128)S(1)} %get-tuple-element.18.b, f32[256,128]{1,0:T(8,128)S(1)} %get-tuple-element.27.image, f32[256,128]{1,0:T(8,128)S(1)} %get-tuple-element.32.candidate, bf16[8,48,128]{2,1,0:T(8,128)(2,1)S(1)} %all_to_all.15.got.got1, ...), custom_call_target="tpu_custom_call" | custom-call | tf_op jit(solution)/shard_map/finish/pallas_call | solution.py:364
  (12 shorter events, 0.1 us)
Async XLA Ops:
  2.5 14.2 %all-to-all-start = ((bf16[8,32,128]{2,1,0:T(8,128)(2,1)}), bf16[8,32,128]{2,1,0:T(8,128)(2,1)S(1)}, u32[]{:S(2)}, u32[]{:S(2)}) async-start(bf16[8,32,128]{2,1,0:T(8,128)(2,1)} %get-tuple-element.20._), calls=%async_computation | async-start | bytes 131072 | tf_op jit(solution)/shard_map/all_to_all | solution.py:374
  16.7 1.8 %collective-permute-start.3 = (bf16[8,32,128]{2,1,0:T(8,128)(2,1)S(1)}, bf16[8,32,128]{2,1,0:T(8,128)(2,1)S(1)}, u32[]{:S(2)}, u32[]{:S(2)}) collective-permute-start(bf16[8,32,128]{2,1,0:T(8,128)(2,1)S(1)} %behind.1.got), channel_id=1, source_target_pairs={{0,1},{1,0},{2,3},{3,2},{4,5},{5,4},{6,7},{7,6},{8,9},{9,8},{10,11... | collective-permute-start | bytes 196616 | tf_op jit(solution)/shard_map/ppermute | solution.py:302
  16.7 7.2 %collective-permute-start.2 = (bf16[256,128]{1,0:T(8,128)(2,1)S(1)}, bf16[256,128]{1,0:T(8,128)(2,1)S(1)}, u32[]{:S(2)}, u32[]{:S(2)}) collective-permute-start(bf16[256,128]{1,0:T(8,128)(2,1)S(1)} %get-tuple-element.19.own), channel_id=1, source_target_pairs={{0,14},{1,15},{2,4},{3,5},{4,2},{5,3},{6,8},{7,9},{8,6},{9,7},{10,... | collective-permute-start | bytes 196616 | tf_op jit(solution)/shard_map/ppermute | solution.py:302
  17.7 6.2 %collective-permute-start.1 = (bf16[256,128]{1,0:T(8,128)(2,1)S(1)}, bf16[256,128]{1,0:T(8,128)(2,1)S(1)}, u32[]{:S(2)}, u32[]{:S(2)}) collective-permute-start(bf16[256,128]{1,0:T(8,128)(2,1)S(1)} %get-tuple-element.19.own), channel_id=1, source_target_pairs={{0,2},{1,3},{2,0},{3,1},{4,6},{5,7},{6,4},{7,5},{8,10},{9,11},{10,... | collective-permute-start | bytes 196616 | tf_op jit(solution)/shard_map/ppermute | solution.py:302
  23.9 1.5 %collective-permute-start.4 = (bf16[512,128]{1,0:T(8,128)(2,1)S(1)}, bf16[512,128]{1,0:T(8,128)(2,1)S(1)}, u32[]{:S(2)}, u32[]{:S(2)}) collective-permute-start(bf16[512,128]{1,0:T(8,128)(2,1)S(1)} %relay.2), channel_id=1, source_target_pairs={{0,1},{1,0},{2,3},{3,2},{4,5},{5,4},{6,7},{7,6},{8,9},{9,8},{10,11... | collective-permute-start | bytes 393224 | tf_op jit(solution)/shard_map/ppermute | solution.py:302
  24.0 1.4 %collective-permute-start = (bf16[256,128]{1,0:T(8,128)(2,1)S(1)}, bf16[256,128]{1,0:T(8,128)(2,1)S(1)}, u32[]{:S(2)}, u32[]{:S(2)}) collective-permute-start(bf16[256,128]{1,0:T(8,128)(2,1)S(1)} %get-tuple-element.19.own), channel_id=1, source_target_pairs={{0,1},{1,0},{2,3},{3,2},{4,5},{5,4},{6,7},{7,6},{8,9},{9,8},{10,11... | collective-permute-start | bytes 196616 | tf_op jit(solution)/shard_map/ppermute | solution.py:302
  40.8 1.5 %collective-permute-start.8 = (bf16[8,48,128]{2,1,0:T(8,128)(2,1)S(1)}, bf16[8,48,128]{2,1,0:T(8,128)(2,1)S(1)}, u32[]{:S(2)}, u32[]{:S(2)}) collective-permute-start(bf16[8,48,128]{2,1,0:T(8,128)(2,1)S(1)} %all_to_all.15.got.got1), channel_id=1, source_target_pairs={{0,1},{1,0},{2,3},{3,2},{4,5},{5,4},{6,7},{7,6},{8,9},{9,8},{10,11... | collective-permute-start | bytes 294920 | tf_op jit(solution)/shard_map/ppermute | solution.py:302
  40.8 7.2 %collective-permute-start.7 = (bf16[256,128]{1,0:T(8,128)(2,1)S(1)}, bf16[256,128]{1,0:T(8,128)(2,1)S(1)}, u32[]{:S(2)}, u32[]{:S(2)}) collective-permute-start(bf16[256,128]{1,0:T(8,128)(2,1)S(1)} %get-tuple-element.28.own), channel_id=1, source_target_pairs={{0,14},{1,15},{2,4},{3,5},{4,2},{5,3},{6,8},{7,9},{8,6},{9,7},{10,... | collective-permute-start | bytes 196616 | tf_op jit(solution)/shard_map/ppermute | solution.py:302
  41.9 6.1 %collective-permute-start.6 = (bf16[256,128]{1,0:T(8,128)(2,1)S(1)}, bf16[256,128]{1,0:T(8,128)(2,1)S(1)}, u32[]{:S(2)}, u32[]{:S(2)}) collective-permute-start(bf16[256,128]{1,0:T(8,128)(2,1)S(1)} %get-tuple-element.28.own), channel_id=1, source_target_pairs={{0,2},{1,3},{2,0},{3,1},{4,6},{5,7},{6,4},{7,5},{8,10},{9,11},{10,... | collective-permute-start | bytes 196616 | tf_op jit(solution)/shard_map/ppermute | solution.py:302
  48.0 1.5 %collective-permute-start.9 = (bf16[512,128]{1,0:T(8,128)(2,1)S(1)}, bf16[512,128]{1,0:T(8,128)(2,1)S(1)}, u32[]{:S(2)}, u32[]{:S(2)}) collective-permute-start(bf16[512,128]{1,0:T(8,128)(2,1)S(1)} %relay.3), channel_id=1, source_target_pairs={{0,1},{1,0},{2,3},{3,2},{4,5},{5,4},{6,7},{7,6},{8,9},{9,8},{10,11... | collective-permute-start | bytes 393224 | tf_op jit(solution)/shard_map/ppermute | solution.py:302
  48.1 1.4 %collective-permute-start.5 = (bf16[256,128]{1,0:T(8,128)(2,1)S(1)}, bf16[256,128]{1,0:T(8,128)(2,1)S(1)}, u32[]{:S(2)}, u32[]{:S(2)}) collective-permute-start(bf16[256,128]{1,0:T(8,128)(2,1)S(1)} %get-tuple-element.28.own), channel_id=1, source_target_pairs={{0,1},{1,0},{2,3},{3,2},{4,5},{5,4},{6,7},{7,6},{8,9},{9,8},{10,11... | collective-permute-start | bytes 196616 | tf_op jit(solution)/shard_map/ppermute | solution.py:302

commit v11 on v9

--- a/solution.py
+++ b/solution.py
@@ -123,9 +123,8 @@
     target_out[...] = dot((column == wanted).astype(bf16), target[...]).astype(bf16)
 
 
-def far_kernel(
-    per_group, got, got_mate, far_cols, high, low, target, blocks_hbm, _, far, blocks, table, sems,
-):
+def fetch_kernel(blocks_hbm, *refs):
+    *_, blocks, token, sems = refs
     chunks = sems.shape[0]
     each = blocks.shape[0] // chunks
     copies = [
@@ -136,6 +135,16 @@
     ]
     for copy in copies:
         copy.start()
+    token[...] = jnp.zeros_like(token)
+    for copy in copies:
+        copy.wait()
+
+
+def behind_kernel(values, *refs):
+    refs[-1][...] = values[...]
+
+
+def far_kernel(per_group, got, got_mate, far_cols, high, low, target, _, far, table):
     slots, clusters = far_cols.shape
     rank = LANES // per_group
     groups = clusters // per_group
@@ -170,11 +179,9 @@
     far[...] = dot(jnp.concatenate(expanded_high, axis=1), target[...]) + dot(
         jnp.concatenate(expanded_low, axis=1), target[...]
     )
-    for copy in copies:
-        copy.wait()
-
-
-def relay_kernel(even, odd, both):
+
+
+def relay_kernel(even, odd, _, both):
     rows = even.shape[0]
     both[pl.ds(0, rows), :] = even[...]
     both[pl.ds(rows, rows), :] = odd[...]
@@ -355,10 +362,9 @@
     def exchange(block):
         return lax.all_to_all(block, "rows", 0, 0)
 
-    def gathered(block):
+    def gather(block):
         groups = [list(range(core, size, 2)) for core in range(2)]
-        got = lax.all_to_all(block, "rows", 0, 0, axis_index_groups=groups)
-        return got, swapped(got, core_mate)
+        return lax.all_to_all(block, "rows", 0, 0, axis_index_groups=groups)
 
     field, basis, lowered, payload = call(
         functools.partial(start_kernel, per_group), "start",
@@ -369,7 +375,7 @@
         [HBM] * 2, in_hbm(right_sides), in_hbm(basis_in.reshape(clusters * rank, LANES)),
         scratch_shapes=[scratch(R, width), pltpu.SemaphoreType.DMA((2,))],
     )
-    got = gathered(payload)
+    got = gather(payload)
     held = sends_of(lowered)
 
     reach = 2 * clusters
@@ -397,22 +403,30 @@
     )
     blocks = in_hbm(near_blocks.reshape(clusters * slots, LANES, LANES))
 
-    def far_of(got, relay):
-        far, near = call(
-            functools.partial(far_kernel, per_group), "far",
-            (shape(rows, LANES), pltpu.VMEM(blocks.shape, bf16)), [VMEM] * 2 + [SMEM] + [VMEM] * 3 + [HBM, ANY],
-            *got, far_index, high, low, target, blocks, relay,
-            scratch_shapes=[scratch(size * head, LANES), pltpu.SemaphoreType.DMA((8,))],
+
+    def arrived(got, held, *made):
+        near_blocks_here, token = call(
+            fetch_kernel, "fetch", (pltpu.VMEM(blocks.shape, bf16), shape(R, LANES)),
+            [HBM] + [ANY] * (1 + len(made)), blocks, got, *made,
+            scratch_shapes=[pltpu.SemaphoreType.DMA((8,))],
         )
-        return far, pltpu.with_memory_space_constraint(near, pltpu.VMEM)
-
-    def relay_of(held):
-        return call(relay_kernel, "relay", shape(2 * rows, LANES, dtype=bf16), [VMEM] * 2, *held[2:])
+        near_blocks_here = pltpu.with_memory_space_constraint(near_blocks_here, pltpu.VMEM)
+        got = call(
+            behind_kernel, "behind", shape(*got.shape, dtype=bf16), [VMEM] + [ANY] * 2, got, held[3], token
+        )
+        got = (got, swapped(got, core_mate))
+        relay = call(
+            relay_kernel, "relay", shape(2 * rows, LANES, dtype=bf16), [VMEM] * 2 + [ANY], *held[2:], got[0]
+        )
+        far = call(
+            functools.partial(far_kernel, per_group), "far", shape(rows, LANES),
+            [VMEM] * 2 + [SMEM] + [VMEM] * 3 + [ANY], *got, far_index, high, low, target, relay,
+            scratch_shapes=[scratch(size * head, LANES)],
+        )
+        return got, near_blocks_here, held + [swapped(relay, core_mate)], far
 
     kept = [scratch(rows, LANES), scratch(6 * rows + R, LANES)]
-    relay = relay_of(held)
-    relayed = swapped(relay, core_mate)
-    far, near_here = far_of(got, relay)
+    got, near_blocks_here, held, far = arrived(got, held, target)
     image, lowered, payload = call(
         functools.partial(first_kernel, per_group), "near_one",
         (
@@ -420,17 +434,15 @@
             shape(size // 2, head + TAIL, LANES, dtype=bf16),
         ),
         [VMEM] * 5 + [SMEM] + [VMEM] * 4,
-        *held, relayed, placed, near_here, field, far, basis, scratch_shapes=kept,
-    )
-    got = gathered(payload)
+        *held, placed, near_blocks_here, field, far, basis, scratch_shapes=kept,
+    )
+    got = gather(payload)
     held = sends_of(lowered)
-    relay = relay_of(held)
-    relayed = swapped(relay, core_mate)
-    far, near_here = far_of(got, relay)
+    got, near_blocks_here, held, far = arrived(got, held)
     candidate, sums = call(
         functools.partial(second_kernel, per_group, unknowns), "near_two",
         (shape(rows, LANES), shape(size, R, LANES, dtype=bf16)), [VMEM] * 5 + [SMEM] + [VMEM] * 6,
-        *held, relayed, placed, near_here, field, image, far, *got, scratch_shapes=kept,
+        *held, placed, near_blocks_here, field, image, far, *got, scratch_shapes=kept,
     )
     return call(
         functools.partial(finish_kernel, per_group, unknowns), "finish", (shape(R, width), shape(R, width)),

time: 65.1 us -> 61.8 us (0.949)
  blocking collectives: 11.1 us -> 9.2 us
  Pallas kernels: 21.4 us -> 22.5 us
  starting transfers between devices: 19.7 us -> 18.7 us
  waiting for transfers between devices: 10.1 us -> 9.35 us
  other arithmetic: 1.43 us -> 0.75 us
    ppermute x10, waiting for transfers between devices: 4.61 us -> 1.77 us  [swapped(): lax.ppermute(block, 'rows', [(i, partner(i)) for i in range(lax.axis_size...]
    all_to_all x2, waiting for transfers between devices: 5.53 us -> 7.57 us  [gather(): return lax.all_to_all(block, 'rows', 0, 0, axis_index_groups=groups)]
    all_to_all x1, blocking collectives: 11.1 us -> 9.2 us  [exchange(): return lax.all_to_all(block, 'rows', 0, 0)]
    pallas_call x9 -> x13, Pallas kernels: 21.4 us -> 22.5 us  [call(): pl.pallas_call(kernel, out_shape=out, in_specs=ins, out_specs=jax.tree.ma...]
    ppermute x10, starting transfers between devices: 13 us -> 12 us  [swapped(): lax.ppermute(block, 'rows', [(i, partner(i)) for i in range(lax.axis_size...]
    add x1 -> x0, other arithmetic: 0.71 us -> none  [on_device(): (other_core * (size // 2) + owner // 2) * clusters + far_cols.T % clusters]
  transfers between devices with their start and end apart: 12 -> 12, of which waited for: 3 -> 4; matrix products, arithmetic and copies ran while one was open for 2% -> 1% of each run, Pallas kernels for 18% -> 20%
where the time goes in v11:
time: 61.8 us; the launch traced here: 61.4 us
  Pallas kernels  22.5 us (36%)
  starting transfers between devices  18.7 us (30%)
  waiting for transfers between devices  9.35 us (15%)
  blocking collectives  9.2 us (15%)
  between operations  0.86 us (1%)
  other arithmetic  0.75 us (1%)
    pallas_call x13, Pallas kernels, call(): pl.pallas_call(kernel, out_shape=out, in_specs=ins, out_specs=jax.tree.ma...  22.5 us
    ppermute x10, starting transfers between devices, swapped(): lax.ppermute(block, 'rows', [(i, partner(i)) for i in range(lax.axis_size...  12 us
    all_to_all x1, blocking collectives, exchange(): return lax.all_to_all(block, 'rows', 0, 0)  9.2 us
    all_to_all x2, waiting for transfers between devices, gather(): return lax.all_to_all(block, 'rows', 0, 0, axis_index_groups=groups)  7.57 us
    all_to_all x2, starting transfers between devices, gather(): return lax.all_to_all(block, 'rows', 0, 0, axis_index_groups=groups)  6.71 us
    ppermute x10, waiting for transfers between devices, swapped(): lax.ppermute(block, 'rows', [(i, partner(i)) for i in range(lax.axis_size...  1.77 us
  transfers between devices with their start and end apart: 12, of which 4 were waited for; matrix products, arithmetic and copies ran while one was open for 1% of the time, Pallas kernels for 20%

profile of v11, /device:TPU:0, one launch (start us, length us, event | category | flops | bytes accessed | tf_op | source)
XLA Modules:
  0.0 61.4 jit_solution(478414365910375493)
XLA Ops:
  0.6 1.8 %start.1 = (f32[256,128]{1,0:T(8,128)S(1)}, bf16[512,128]{1,0:T(8,128)(2,1)S(1)}, bf16[256,128]{1,0:T(8,128)(2,1)S(1)}, bf16[8,32,128]{2,1,0:T(8,128)(2,1)}) custom-call(f32[8,4096]{1,0:T(8,128)} %b_hbm.1, bf16[512,128]{1,0:T(8,128)(2,1)} %bitcast.28), custom_call_target="tpu_custom_call" | custom-call | tf_op jit(solution)/shard_map/start/pallas_call | solution.py:357
  2.5 6.1 %collective-permute-start.2 = (bf16[256,128]{1,0:T(8,128)(2,1)S(1)}, bf16[256,128]{1,0:T(8,128)(2,1)S(1)}, u32[]{:S(2)}, u32[]{:S(2)}) collective-permute-start(bf16[256,128]{1,0:T(8,128)(2,1)S(1)} %get-tuple-element.19.own), channel_id=1, source_target_pairs={{0,14},{1,15},{2,4},{3,5},{4,2},{5,3},{6,8},{7,9},{8,6},{9,7},{10,... | collective-permute-start | bytes 196616 | tf_op jit(solution)/shard_map/ppermute | solution.py:295
  8.5 3.4 %all-to-all-start = ((bf16[8,32,128]{2,1,0:T(8,128)(2,1)}), bf16[8,32,128]{2,1,0:T(8,128)(2,1)S(1)}, u32[]{:S(2)}, u32[]{:S(2)}) async-start(bf16[8,32,128]{2,1,0:T(8,128)(2,1)} %get-tuple-element.20._), calls=%async_computation | async-start | bytes 131072 | tf_op jit(solution)/shard_map/all_to_all | solution.py:367
  11.9 0.7 %fusion.2 = (s32[8,32]{1,0:T(8,128)S(1)}, s32[8,32]{1,0:T(8,128)S(1)}) fusion(s32[32,8]{0,1:T(8,128)} %param.10, s32[]{:T(128)S(6)} %sub.32, s32[]{:T(128)S(6)} %select_n.83, s32[]{:T(128)S(6)} %select_n.82, s32[]{:T(128)S(6)} %add.66, s32[]{:T(128)S(6)} %mul.15, s32[32]{0:T(128)} %param.11, s32[]{:T(128)S(6)} %select_n.81, s32[32,8]{0,1:T(8,128)} %param.15), kind=kLoop, calls=%fused_computation.20 | loop fusion | flops 22784 | bytes 4248 | tf_op jit(solution)/shard_map/jit(_where)/select_n | solution.py:385
  12.7 1.6 %prepare.1 = (bf16[128,512]{1,0:T(8,128)(2,1)S(1)}, bf16[128,512]{1,0:T(8,128)(2,1)S(1)}, bf16[512,128]{1,0:T(8,128)(2,1)S(1)}) custom-call(f32[8,16,16,32]{3,2,1,0:T(8,128)} %bitcast.26, bf16[512,128]{1,0:T(8,128)(2,1)} %bitcast.27, bf16[8,32,128]{2,1,0:T(8,128)(2,1)} %get-tuple-element.20._, s32[8,32]{1,0:T(8,128)S(1)} %get-tuple-element.34.__.placed, ...), custom_call_target="tpu_custom_call" | custom-call | tf_op jit(solution)/shard_map/prepare/pallas_call | solution.py:357
  14.3 4.5 %all-to-all-done.refs_0_.values = bf16[8,32,128]{2,1,0:T(8,128)(2,1)S(1)} async-done(((bf16[8,32,128]{2,1,0:T(8,128)(2,1)}), bf16[8,32,128]{2,1,0:T(8,128)(2,1)S(1)}, u32[]{:S(2)}, u32[]{:S(2)}) %all-to-all-start) | async-done | bytes 65568 | tf_op jit(solution)/shard_map/all_to_all | solution.py:367
  18.7 3.5 %fetch.2 = (bf16[256,128,128]{2,1,0:T(8,128)(2,1)S(1)}, f32[8,128]{1,0:T(8,128)S(1)}) custom-call(bf16[256,128,128]{2,1,0:T(8,128)(2,1)} %bitcast.24, bf16[8,32,128]{2,1,0:T(8,128)(2,1)S(1)} %all-to-all-done.refs_0_.values, bf16[512,128]{1,0:T(8,128)(2,1)S(1)} %get-tuple-element.21.refs_1_.target), custom_call_target="tpu_custom_call" | custom-call | tf_op jit(solution)/shard_map/fetch/pallas_call | solution.py:357
  22.3 0.1 collective-permute-start.3
  22.4 0.5 collective-permute-start.4
  22.9 0.1 collective-permute-start
  22.9 0.9 %collective-permute-done.4.got_mate = bf16[8,32,128]{2,1,0:T(8,128)(2,1)S(1)} collective-permute-done((bf16[8,32,128]{2,1,0:T(8,128)(2,1)S(1)}, bf16[8,32,128]{2,1,0:T(8,128)(2,1)S(1)}, u32[]{:S(2)}, u32[]{:S(2)}) %collective-permute-start.4) | collective-permute-done | bytes 65568 | tf_op jit(solution)/shard_map/ppermute | solution.py:295
  23.8 1.9 %far.2 = f32[256,128]{1,0:T(8,128)S(1)} custom-call(bf16[8,32,128]{2,1,0:T(8,128)(2,1)S(1)} %behind.2._.got, bf16[8,32,128]{2,1,0:T(8,128)(2,1)S(1)} %collective-permute-done.4.got_mate, s32[8,32]{1,0:T(8,128)S(1)} %get-tuple-element.35.___.far_cols, bf16[128,512]{1,0:T(8,128)(2,1)S(1)} %get-tuple-element.24.high, ...), custom_call_target="tpu_custom_call" | custom-call | tf_op jit(solution)/shard_map/far/pallas_call | solution.py:357
  25.8 3.7 %near_one.1 = (f32[256,128]{1,0:T(8,128)S(1)}, bf16[256,128]{1,0:T(8,128)(2,1)S(1)}, bf16[8,48,128]{2,1,0:T(8,128)(2,1)}) custom-call(bf16[256,128]{1,0:T(8,128)(2,1)S(1)} %get-tuple-element.19.own, bf16[256,128]{1,0:T(8,128)(2,1)S(1)} %collective-permute-done.mate, bf16[256,128]{1,0:T(8,128)(2,1)S(1)} %collective-permute-done.1.even, ...), custom_call_target="tpu_custom_call" | custom-call | tf_op jit(solution)/shard_map/near_one/pallas_call | solution.py:357
  29.5 3.4 %all-to-all-start.1 = ((bf16[8,48,128]{2,1,0:T(8,128)(2,1)}), bf16[8,48,128]{2,1,0:T(8,128)(2,1)S(1)}, u32[]{:S(2)}, u32[]{:S(2)}) async-start(bf16[8,48,128]{2,1,0:T(8,128)(2,1)} %get-tuple-element.29), calls=%async_computation.1 | async-start | bytes 196608 | tf_op jit(solution)/shard_map/all_to_all | solution.py:367
  32.8 4.7 %collective-permute-start.7 = (bf16[256,128]{1,0:T(8,128)(2,1)S(1)}, bf16[256,128]{1,0:T(8,128)(2,1)S(1)}, u32[]{:S(2)}, u32[]{:S(2)}) collective-permute-start(bf16[256,128]{1,0:T(8,128)(2,1)S(1)} %get-tuple-element.28.own), channel_id=1, source_target_pairs={{0,14},{1,15},{2,4},{3,5},{4,2},{5,3},{6,8},{7,9},{8,6},{9,7},{10,... | collective-permute-start | bytes 196616 | tf_op jit(solution)/shard_map/ppermute | solution.py:295
  37.5 3.1 %all-to-all-done.1.refs_0_.values = bf16[8,48,128]{2,1,0:T(8,128)(2,1)S(1)} async-done(((bf16[8,48,128]{2,1,0:T(8,128)(2,1)}), bf16[8,48,128]{2,1,0:T(8,128)(2,1)S(1)}, u32[]{:S(2)}, u32[]{:S(2)}) %all-to-all-start.1) | async-done | bytes 98336 | tf_op jit(solution)/shard_map/all_to_all | solution.py:367
  40.6 3.5 %fetch.3 = (bf16[256,128,128]{2,1,0:T(8,128)(2,1)S(1)}, f32[8,128]{1,0:T(8,128)S(1)}) custom-call(bf16[256,128,128]{2,1,0:T(8,128)(2,1)} %bitcast.25, bf16[8,48,128]{2,1,0:T(8,128)(2,1)S(1)} %all-to-all-done.1.refs_0_.values), custom_call_target="tpu_custom_call" | custom-call | tf_op jit(solution)/shard_map/fetch/pallas_call | solution.py:357
  44.2 0.5 collective-permute-start.9
  44.7 0.1 collective-permute-start.5
  44.8 0.9 %collective-permute-done.9.got_mate.got1_mate = bf16[8,48,128]{2,1,0:T(8,128)(2,1)S(1)} collective-permute-done((bf16[8,48,128]{2,1,0:T(8,128)(2,1)S(1)}, bf16[8,48,128]{2,1,0:T(8,128)(2,1)S(1)}, u32[]{:S(2)}, u32[]{:S(2)}) %collective-permute-start.9) | collective-permute-done | bytes 98336 | tf_op jit(solution)/shard_map/ppermute | solution.py:295
  45.7 1.9 %far.3 = f32[256,128]{1,0:T(8,128)S(1)} custom-call(bf16[8,48,128]{2,1,0:T(8,128)(2,1)S(1)} %behind.3._.got.got1, bf16[8,48,128]{2,1,0:T(8,128)(2,1)S(1)} %collective-permute-done.9.got_mate.got1_mate, s32[8,32]{1,0:T(8,128)S(1)} %get-tuple-element.35.___.far_cols, bf16[128,512]{1,0:T(8,128)(2,1)S(1)} %get-tuple-element.24.high, ...), custom_call_target="tpu_custom_call" | custom-call | tf_op jit(solution)/shard_map/far/pallas_call | solution.py:357
  47.7 3.0 %near_two.1 = (f32[256,128]{1,0:T(8,128)S(1)}, bf16[16,8,128]{2,1,0:T(8,128)(2,1)S(1)}) custom-call(bf16[256,128]{1,0:T(8,128)(2,1)S(1)} %get-tuple-element.28.own, bf16[256,128]{1,0:T(8,128)(2,1)S(1)} %collective-permute-done.5.mate, bf16[256,128]{1,0:T(8,128)(2,1)S(1)} %collective-permute-done.6.even, ...), custom_call_target="tpu_custom_call" | custom-call | tf_op jit(solution)/shard_map/near_two/pallas_call | solution.py:357
  50.7 9.2 %all_to_all.15.got2 = bf16[16,8,128]{2,1,0:T(8,128)(2,1)S(1)} all-to-all(bf16[16,8,128]{2,1,0:T(8,128)(2,1)S(1)} %get-tuple-element.33), channel_id=1, replica_groups=mesh['groups'=2,'rows'=16] {'rows'}, dimensions={0} | all-to-all | bytes 65536 | tf_op jit(solution)/shard_map/all_to_all | solution.py:363
  59.9 1.5 %finish.1 = (f32[8,4096]{1,0:T(8,128)}, f32[8,4096]{1,0:T(8,128)}) custom-call(f32[256,128]{1,0:T(8,128)S(1)} %get-tuple-element.18.b, f32[256,128]{1,0:T(8,128)S(1)} %get-tuple-element.27.image, f32[256,128]{1,0:T(8,128)S(1)} %get-tuple-element.32.candidate, bf16[8,48,128]{2,1,0:T(8,128)(2,1)S(1)} %behind.3._.got.got1, ...), custom_call_target="tpu_custom_call" | custom-call | tf_op jit(solution)/shard_map/finish/pallas_call | solution.py:357
  (15 shorter events, 0.1 us)
Async XLA Ops:
  2.5 19.8 %collective-permute-start.2 = (bf16[256,128]{1,0:T(8,128)(2,1)S(1)}, bf16[256,128]{1,0:T(8,128)(2,1)S(1)}, u32[]{:S(2)}, u32[]{:S(2)}) collective-permute-start(bf16[256,128]{1,0:T(8,128)(2,1)S(1)} %get-tuple-element.19.own), channel_id=1, source_target_pairs={{0,14},{1,15},{2,4},{3,5},{4,2},{5,3},{6,8},{7,9},{8,6},{9,7},{10,... | collective-permute-start | bytes 196616 | tf_op jit(solution)/shard_map/ppermute | solution.py:295
  8.5 13.7 %collective-permute-start.1 = (bf16[256,128]{1,0:T(8,128)(2,1)S(1)}, bf16[256,128]{1,0:T(8,128)(2,1)S(1)}, u32[]{:S(2)}, u32[]{:S(2)}) collective-permute-start(bf16[256,128]{1,0:T(8,128)(2,1)S(1)} %get-tuple-element.19.own), channel_id=1, source_target_pairs={{0,2},{1,3},{2,0},{3,1},{4,6},{5,7},{6,4},{7,5},{8,10},{9,11},{10,... | collective-permute-start | bytes 196616 | tf_op jit(solution)/shard_map/ppermute | solution.py:295
  8.5 10.2 %all-to-all-start = ((bf16[8,32,128]{2,1,0:T(8,128)(2,1)}), bf16[8,32,128]{2,1,0:T(8,128)(2,1)S(1)}, u32[]{:S(2)}, u32[]{:S(2)}) async-start(bf16[8,32,128]{2,1,0:T(8,128)(2,1)} %get-tuple-element.20._), calls=%async_computation | async-start | bytes 131072 | tf_op jit(solution)/shard_map/all_to_all | solution.py:367
  22.3 3.5 %collective-permute-start.3 = (bf16[512,128]{1,0:T(8,128)(2,1)S(1)}, bf16[512,128]{1,0:T(8,128)(2,1)S(1)}, u32[]{:S(2)}, u32[]{:S(2)}) collective-permute-start(bf16[512,128]{1,0:T(8,128)(2,1)S(1)} %relay.2._), channel_id=1, source_target_pairs={{0,1},{1,0},{2,3},{3,2},{4,5},{5,4},{6,7},{7,6},{8,9},{9,8},{10,11... | collective-permute-start | bytes 393224 | tf_op jit(solution)/shard_map/ppermute | solution.py:295
  22.4 1.4 %collective-permute-start.4 = (bf16[8,32,128]{2,1,0:T(8,128)(2,1)S(1)}, bf16[8,32,128]{2,1,0:T(8,128)(2,1)S(1)}, u32[]{:S(2)}, u32[]{:S(2)}) collective-permute-start(bf16[8,32,128]{2,1,0:T(8,128)(2,1)S(1)} %behind.2._.got), channel_id=1, source_target_pairs={{0,1},{1,0},{2,3},{3,2},{4,5},{5,4},{6,7},{7,6},{8,9},{9,8},{10,11... | collective-permute-start | bytes 196616 | tf_op jit(solution)/shard_map/ppermute | solution.py:295
  22.9 2.9 %collective-permute-start = (bf16[256,128]{1,0:T(8,128)(2,1)S(1)}, bf16[256,128]{1,0:T(8,128)(2,1)S(1)}, u32[]{:S(2)}, u32[]{:S(2)}) collective-permute-start(bf16[256,128]{1,0:T(8,128)(2,1)S(1)} %get-tuple-element.19.own), channel_id=1, source_target_pairs={{0,1},{1,0},{2,3},{3,2},{4,5},{5,4},{6,7},{7,6},{8,9},{9,8},{10,11... | collective-permute-start | bytes 196616 | tf_op jit(solution)/shard_map/ppermute | solution.py:295
  29.5 11.1 %all-to-all-start.1 = ((bf16[8,48,128]{2,1,0:T(8,128)(2,1)}), bf16[8,48,128]{2,1,0:T(8,128)(2,1)S(1)}, u32[]{:S(2)}, u32[]{:S(2)}) async-start(bf16[8,48,128]{2,1,0:T(8,128)(2,1)} %get-tuple-element.29), calls=%async_computation.1 | async-start | bytes 196608 | tf_op jit(solution)/shard_map/all_to_all | solution.py:367
  32.8 11.3 %collective-permute-start.7 = (bf16[256,128]{1,0:T(8,128)(2,1)S(1)}, bf16[256,128]{1,0:T(8,128)(2,1)S(1)}, u32[]{:S(2)}, u32[]{:S(2)}) collective-permute-start(bf16[256,128]{1,0:T(8,128)(2,1)S(1)} %get-tuple-element.28.own), channel_id=1, source_target_pairs={{0,14},{1,15},{2,4},{3,5},{4,2},{5,3},{6,8},{7,9},{8,6},{9,7},{10,... | collective-permute-start | bytes 196616 | tf_op jit(solution)/shard_map/ppermute | solution.py:295
  37.5 6.6 %collective-permute-start.6 = (bf16[256,128]{1,0:T(8,128)(2,1)S(1)}, bf16[256,128]{1,0:T(8,128)(2,1)S(1)}, u32[]{:S(2)}, u32[]{:S(2)}) collective-permute-start(bf16[256,128]{1,0:T(8,128)(2,1)S(1)} %get-tuple-element.28.own), channel_id=1, source_target_pairs={{0,2},{1,3},{2,0},{3,1},{4,6},{5,7},{6,4},{7,5},{8,10},{9,11},{10,... | collective-permute-start | bytes 196616 | tf_op jit(solution)/shard_map/ppermute | solution.py:295
  44.1 3.5 %collective-permute-start.8 = (bf16[512,128]{1,0:T(8,128)(2,1)S(1)}, bf16[512,128]{1,0:T(8,128)(2,1)S(1)}, u32[]{:S(2)}, u32[]{:S(2)}) collective-permute-start(bf16[512,128]{1,0:T(8,128)(2,1)S(1)} %relay.3._), channel_id=1, source_target_pairs={{0,1},{1,0},{2,3},{3,2},{4,5},{5,4},{6,7},{7,6},{8,9},{9,8},{10,11... | collective-permute-start | bytes 393224 | tf_op jit(solution)/shard_map/ppermute | solution.py:295
  44.2 1.5 %collective-permute-start.9 = (bf16[8,48,128]{2,1,0:T(8,128)(2,1)S(1)}, bf16[8,48,128]{2,1,0:T(8,128)(2,1)S(1)}, u32[]{:S(2)}, u32[]{:S(2)}) collective-permute-start(bf16[8,48,128]{2,1,0:T(8,128)(2,1)S(1)} %behind.3._.got.got1), channel_id=1, source_target_pairs={{0,1},{1,0},{2,3},{3,2},{4,5},{5,4},{6,7},{7,6},{8,9},{9,8},{10,11... | collective-permute-start | bytes 294920 | tf_op jit(solution)/shard_map/ppermute | solution.py:295
  44.7 2.9 %collective-permute-start.5 = (bf16[256,128]{1,0:T(8,128)(2,1)S(1)}, bf16[256,128]{1,0:T(8,128)(2,1)S(1)}, u32[]{:S(2)}, u32[]{:S(2)}) collective-permute-start(bf16[256,128]{1,0:T(8,128)(2,1)S(1)} %get-tuple-element.28.own), channel_id=1, source_target_pairs={{0,1},{1,0},{2,3},{3,2},{4,5},{5,4},{6,7},{7,6},{8,9},{9,8},{10,11... | collective-permute-start | bytes 196616 | tf_op jit(solution)/shard_map/ppermute | solution.py:295

commit v12 on v11

--- a/solution.py
+++ b/solution.py
@@ -97,7 +97,7 @@
     write_payload(payload, tiles, [], basis, per_group)
 
 
-def prepare_kernel(coupling_hbm, target_hbm, _, __, ___, high_out, low_out, target_out, coupling, target, sems):
+def prepare_kernel(coupling_hbm, target_hbm, _, __, high_out, low_out, target_out, coupling, target, sems):
     copies = [
         pltpu.make_async_copy(coupling_hbm, coupling, sems.at[0]),
         pltpu.make_async_copy(target_hbm, target, sems.at[1]),
@@ -123,46 +123,90 @@
     target_out[...] = dot((column == wanted).astype(bf16), target[...]).astype(bf16)
 
 
-def fetch_kernel(blocks_hbm, *refs):
+def fetch_kernel(least, blocks_hbm, places, *refs):
     *_, blocks, token, sems = refs
-    chunks = sems.shape[0]
-    each = blocks.shape[0] // chunks
-    copies = [
-        pltpu.make_async_copy(
-            blocks_hbm.at[pl.ds(c * each, each)], blocks.at[pl.ds(c * each, each)], sems.at[c]
-        )
-        for c in range(chunks)
-    ]
-    for copy in copies:
-        copy.start()
+    clusters = sems.shape[0]
+    slots = blocks.shape[0] // clusters
+
+    def for_live(i, act):
+        count = places[2 * slots, i]
+        for live in range(least, slots + 1):
+            pl.when(count <= live if live == least else count == live)(functools.partial(act, i, live))
+
+    def copy_of(i, live):
+        span = pl.ds(i * slots, live)
+        return pltpu.make_async_copy(blocks_hbm.at[span], blocks.at[span], sems.at[i])
+
+    def start(i, live):
+        copy_of(i, live).start()
+        if live < slots:
+            blocks[pl.ds(i * slots + live, slots - live)] = jnp.zeros((slots - live, LANES, LANES), bf16)
+
+    def body(act, i, carry):
+        for_live(i, act)
+        return carry
+
+    lax.fori_loop(0, clusters, functools.partial(body, start), 0)
     token[...] = jnp.zeros_like(token)
-    for copy in copies:
-        copy.wait()
+    lax.fori_loop(0, clusters, functools.partial(body, lambda i, live: copy_of(i, live).wait()), 0)
 
 
 def behind_kernel(values, *refs):
     refs[-1][...] = values[...]
 
 
-def far_kernel(per_group, got, got_mate, far_cols, high, low, target, _, far, table):
-    slots, clusters = far_cols.shape
+def relay_kernel(even, odd, _, both):
+    rows = even.shape[0]
+    both[pl.ds(0, rows), :] = even[...]
+    both[pl.ds(rows, rows), :] = odd[...]
+
+
+def apply(per_group, slabs, places, blocks, got, got_mate, high, low, target, near, far, window, table):
+    clusters = near.shape[0] // R
+    slots = blocks.shape[0] // clusters
     rank = LANES // per_group
-    groups = clusters // per_group
-    head = groups * R
+    head = clusters // per_group * R
+    at = 0
+    for slab in slabs:
+        window[pl.ds(at, slab.shape[0]), :] = slab[...].astype(f32)
+        at += slab.shape[0]
+    window[pl.ds(at, R), :] = jnp.zeros((R, LANES), f32)
     for part, values in enumerate((got, got_mate)):
         for device in range(values.shape[0]):
             at = (part * values.shape[0] + device) * head
             table[pl.ds(at, head), :] = values[device, pl.ds(0, head), :].astype(f32)
     lane = lane_ids()
-    picked = []
-    for i in range(clusters):
+
+    def fetch(k, i):
+        return window[pl.ds(pl.multiple_of(places[k, i] * R, R), R), :]
+
+    def block(k, i):
+        return blocks[i * slots + k]
+
+    def pick(i):
         tile = jnp.zeros((R, LANES), f32)
         for k in range(slots):
-            j = far_cols[k, i]
+            j = places[slots + k, i]
             found = table[pl.ds(pl.multiple_of(lax.div(j, per_group) * R, R), R), :]
             shift = ((k - j) * rank) & (LANES - 1)
             tile = jnp.where(lane // rank == k, pltpu.roll(found, shift, 1), tile)
-        picked.append(tile)
+        return tile
+
+    picked = []
+    for i in range(0, clusters, 2):
+        both = jnp.zeros((2 * R, 2 * LANES), f32)
+        for k in range(0, slots, 2):
+            sources = jnp.concatenate(
+                [jnp.concatenate([fetch(k + n, i), fetch(k + n, i + 1)], axis=0) for n in range(2)], axis=1
+            )
+            weights = jnp.concatenate(
+                [jnp.concatenate([block(k + n, i), block(k + n, i + 1)], axis=0) for n in range(2)], axis=1
+            )
+            both = both + dot(sources.astype(bf16), weights, (1, 1))
+        near[pl.ds(i * R, R), :] = both[:R, :LANES]
+        near[pl.ds((i + 1) * R, R), :] = both[R:, LANES:]
+        picked += [pick(i), pick(i + 1)]
+
     picked = jnp.concatenate(picked, axis=0).astype(bf16)
     crossed = dot(picked, high[...]) + dot(picked, low[...])
     expanded_high, expanded_low = [], []
@@ -181,45 +225,13 @@
     )
 
 
-def relay_kernel(even, odd, _, both):
-    rows = even.shape[0]
-    both[pl.ds(0, rows), :] = even[...]
-    both[pl.ds(rows, rows), :] = odd[...]
-
-
-def near_field(slabs, placed, blocks, near, window):
-    slots, clusters = placed.shape
-    at = 0
-    for slab in slabs:
-        window[pl.ds(at, slab.shape[0]), :] = slab[...].astype(f32)
-        at += slab.shape[0]
-    window[pl.ds(at, R), :] = jnp.zeros((R, LANES), f32)
-
-    def fetch(k, i):
-        return window[pl.ds(pl.multiple_of(placed[k, i] * R, R), R), :]
-
-    def block(k, i):
-        return blocks[i * slots + k]
-
-    for i in range(0, clusters, 2):
-        both = jnp.zeros((2 * R, 2 * LANES), f32)
-        for k in range(0, slots, 2):
-            sources = jnp.concatenate(
-                [jnp.concatenate([fetch(k + n, i), fetch(k + n, i + 1)], axis=0) for n in range(2)], axis=1
-            )
-            weights = jnp.concatenate(
-                [jnp.concatenate([block(k + n, i), block(k + n, i + 1)], axis=0) for n in range(2)], axis=1
-            )
-            both = both + dot(sources.astype(bf16), weights, (1, 1))
-        near[pl.ds(i * R, R), :] = both[:R, :LANES]
-        near[pl.ds((i + 1) * R, R), :] = both[R:, LANES:]
-
-
 def first_kernel(
-    per_group, own, mate, even, odd, relayed, placed, blocks, b, far, basis, image, lowered, payload, near, window,
+    per_group, own, mate, even, odd, relayed, places, blocks, got, got_mate, high, low, target, b, basis,
+    image, lowered, payload, near, far, window, table,
 ):
-    near_field((own, mate, even, odd, relayed), placed, blocks, near, window)
-    clusters = placed.shape[1]
+    slabs = (own, mate, even, odd, relayed)
+    apply(per_group, slabs, places, blocks, got, got_mate, high, low, target, near, far, window, table)
+    clusters = near.shape[0] // R
     tiles = []
     sums = [jnp.zeros((R, LANES), f32) for _ in range(3)]
     for i in range(clusters):
@@ -246,11 +258,12 @@
 
 
 def second_kernel(
-    per_group, unknowns, own, mate, even, odd, relayed, placed, blocks, b, image, far, got, got_mate,
-    candidate, sums_out, near, window,
+    per_group, unknowns, own, mate, even, odd, relayed, places, blocks, got, got_mate, high, low, target, b, image,
+    candidate, sums_out, near, far, window, table,
 ):
-    near_field((own, mate, even, odd, relayed), placed, blocks, near, window)
-    clusters = placed.shape[1]
+    slabs = (own, mate, even, odd, relayed)
+    apply(per_group, slabs, places, blocks, got, got_mate, high, low, target, near, far, window, table)
+    clusters = near.shape[0] // R
     head = clusters // per_group * R
     start_norm, h11, h21, _, _, _ = arnoldi_one(*read_sums((got, got_mate), head, TAIL, 3, unknowns))
     scale = 1.0 / start_norm
@@ -386,6 +399,7 @@
     owner = far_cols.T // clusters
     other_core = (owner % 2) ^ (lax.axis_index("rows") % 2)
     far_index = (other_core * (size // 2) + owner // 2) * clusters + far_cols.T % clusters
+    places = jnp.concatenate([placed, far_index, near_counts[None, :]], axis=0)
     high, low, target = call(
         prepare_kernel, "prepare",
         (
@@ -393,9 +407,9 @@
             shape(slots * rank, rank * clusters, dtype=bf16),
             shape(rank * clusters, LANES, dtype=bf16),
         ),
-        [HBM] * 2 + [ANY] * 3,
+        [HBM] * 2 + [ANY] * 2,
         in_hbm(jnp.transpose(coupling, (1, 2, 3, 0))), in_hbm(target_basis.reshape(clusters * rank, LANES)),
-        payload, placed, far_index,
+        payload, places,
         scratch_shapes=[
             scratch(slots, rank, rank, clusters), scratch(clusters * rank, LANES, dtype=bf16),
             pltpu.SemaphoreType.DMA((2,)),
@@ -406,43 +420,37 @@
 
     def arrived(got, held, *made):
         near_blocks_here, token = call(
-            fetch_kernel, "fetch", (pltpu.VMEM(blocks.shape, bf16), shape(R, LANES)),
-            [HBM] + [ANY] * (1 + len(made)), blocks, got, *made,
-            scratch_shapes=[pltpu.SemaphoreType.DMA((8,))],
+            functools.partial(fetch_kernel, 3), "fetch", (pltpu.VMEM(blocks.shape, bf16), shape(R, LANES)),
+            [HBM, SMEM] + [ANY] * (1 + len(made)), blocks, places, got, *made,
+            scratch_shapes=[pltpu.SemaphoreType.DMA((clusters,))],
         )
         near_blocks_here = pltpu.with_memory_space_constraint(near_blocks_here, pltpu.VMEM)
         got = call(
             behind_kernel, "behind", shape(*got.shape, dtype=bf16), [VMEM] + [ANY] * 2, got, held[3], token
         )
+        relay = call(
+            relay_kernel, "relay", shape(2 * rows, LANES, dtype=bf16), [VMEM] * 2 + [ANY], *held[2:], got
+        )
         got = (got, swapped(got, core_mate))
-        relay = call(
-            relay_kernel, "relay", shape(2 * rows, LANES, dtype=bf16), [VMEM] * 2 + [ANY], *held[2:], got[0]
-        )
-        far = call(
-            functools.partial(far_kernel, per_group), "far", shape(rows, LANES),
-            [VMEM] * 2 + [SMEM] + [VMEM] * 3 + [ANY], *got, far_index, high, low, target, relay,
-            scratch_shapes=[scratch(size * head, LANES)],
-        )
-        return got, near_blocks_here, held + [swapped(relay, core_mate)], far
-
-    kept = [scratch(rows, LANES), scratch(6 * rows + R, LANES)]
-    got, near_blocks_here, held, far = arrived(got, held, target)
+        return (*held, swapped(relay, core_mate)), near_blocks_here, got
+
+    kept = [scratch(rows, LANES), scratch(rows, LANES), scratch(6 * rows + R, LANES), scratch(size * head, LANES)]
+    operands = [VMEM] * 5 + [SMEM] + [VMEM] * 8
+    slabs, near_blocks_here, got = arrived(got, held, target)
     image, lowered, payload = call(
-        functools.partial(first_kernel, per_group), "near_one",
+        functools.partial(first_kernel, per_group), "operator_one",
         (
             shape(rows, LANES), shape(rows, LANES, dtype=bf16),
             shape(size // 2, head + TAIL, LANES, dtype=bf16),
         ),
-        [VMEM] * 5 + [SMEM] + [VMEM] * 4,
-        *held, placed, near_blocks_here, field, far, basis, scratch_shapes=kept,
+        operands, *slabs, places, near_blocks_here, *got, high, low, target, field, basis, scratch_shapes=kept,
     )
     got = gather(payload)
-    held = sends_of(lowered)
-    got, near_blocks_here, held, far = arrived(got, held)
+    slabs, near_blocks_here, got = arrived(got, sends_of(lowered))
     candidate, sums = call(
-        functools.partial(second_kernel, per_group, unknowns), "near_two",
-        (shape(rows, LANES), shape(size, R, LANES, dtype=bf16)), [VMEM] * 5 + [SMEM] + [VMEM] * 6,
-        *held, placed, near_blocks_here, field, image, far, *got, scratch_shapes=kept,
+        functools.partial(second_kernel, per_group, unknowns), "operator_two",
+        (shape(rows, LANES), shape(size, R, LANES, dtype=bf16)),
+        operands, *slabs, places, near_blocks_here, *got, high, low, target, field, image, scratch_shapes=kept,
     )
     return call(
         functools.partial(finish_kernel, per_group, unknowns), "finish", (shape(R, width), shape(R, width)),

time: 61.8 us -> 61.4 us (level)
  Pallas kernels: 22.5 us -> 21.3 us
  other arithmetic: 0.75 us -> 1.41 us
    pallas_call x13 -> x11, Pallas kernels: 22.5 us -> 21.3 us  [call(): pl.pallas_call(kernel, out_shape=out, in_specs=ins, out_specs=jax.tree.ma...]
    all_to_all x2, waiting for transfers between devices: 7.57 us -> 6.88 us  [gather(): return lax.all_to_all(block, 'rows', 0, 0, axis_index_groups=groups)]
    concatenate x0 -> x1, other arithmetic: none -> 0.66 us  [on_device(): places = jnp.concatenate([placed, far_index, near_counts[None, :]], axis=0)]
  transfers between devices with their start and end apart: 12 -> 12, of which waited for: 4 -> 5; matrix products, arithmetic and copies ran while one was open for 1% -> 2% of each run, Pallas kernels for 20% -> 15%
where the time goes in v12:
time: 61.4 us; the launch traced here: 60.7 us
  Pallas kernels  21.3 us (35%)
  starting transfers between devices  18.7 us (30%)
  waiting for transfers between devices  9.25 us (15%)
  blocking collectives  9.2 us (15%)
  other arithmetic  1.41 us (2%)
  between operations  0.82 us (1%)
    pallas_call x11, Pallas kernels, call(): pl.pallas_call(kernel, out_shape=out, in_specs=ins, out_specs=jax.tree.ma...  21.3 us
    ppermute x10, starting transfers between devices, swapped(): lax.ppermute(block, 'rows', [(i, partner(i)) for i in range(lax.axis_size...  12 us
    all_to_all x1, blocking collectives, exchange(): return lax.all_to_all(block, 'rows', 0, 0)  9.2 us
    all_to_all x2, waiting for transfers between devices, gather(): return lax.all_to_all(block, 'rows', 0, 0, axis_index_groups=groups)  6.88 us
    all_to_all x2, starting transfers between devices, gather(): return lax.all_to_all(block, 'rows', 0, 0, axis_index_groups=groups)  6.71 us
    ppermute x10, waiting for transfers between devices, swapped(): lax.ppermute(block, 'rows', [(i, partner(i)) for i in range(lax.axis_size...  2.37 us
  transfers between devices with their start and end apart: 12, of which 5 were waited for; matrix products, arithmetic and copies ran while one was open for 2% of the time, Pallas kernels for 15%

profile of v12, /device:TPU:0, one launch (start us, length us, event | category | flops | bytes accessed | tf_op | source)
XLA Modules:
  0.0 60.7 jit_solution(13924301071496247031)
XLA Ops:
  0.6 1.8 %start.1 = (f32[256,128]{1,0:T(8,128)S(1)}, bf16[512,128]{1,0:T(8,128)(2,1)S(1)}, bf16[256,128]{1,0:T(8,128)(2,1)S(1)}, bf16[8,32,128]{2,1,0:T(8,128)(2,1)}) custom-call(f32[8,4096]{1,0:T(8,128)} %b_hbm.1, bf16[512,128]{1,0:T(8,128)(2,1)} %bitcast.29), custom_call_target="tpu_custom_call" | custom-call | tf_op jit(solution)/shard_map/start/pallas_call | solution.py:370
  2.5 6.1 %collective-permute-start.2 = (bf16[256,128]{1,0:T(8,128)(2,1)S(1)}, bf16[256,128]{1,0:T(8,128)(2,1)S(1)}, u32[]{:S(2)}, u32[]{:S(2)}) collective-permute-start(bf16[256,128]{1,0:T(8,128)(2,1)S(1)} %get-tuple-element.19.own), channel_id=1, source_target_pairs={{0,14},{1,15},{2,4},{3,5},{4,2},{5,3},{6,8},{7,9},{8,6},{9,7},{10,... | collective-permute-start | bytes 196616 | tf_op jit(solution)/shard_map/ppermute | solution.py:308
  8.5 3.4 %all-to-all-start = ((bf16[8,32,128]{2,1,0:T(8,128)(2,1)}), bf16[8,32,128]{2,1,0:T(8,128)(2,1)S(1)}, u32[]{:S(2)}, u32[]{:S(2)}) async-start(bf16[8,32,128]{2,1,0:T(8,128)(2,1)} %get-tuple-element.20._), calls=%async_computation | async-start | bytes 131072 | tf_op jit(solution)/shard_map/all_to_all | solution.py:380
  11.9 0.7 %fusion.2 = (s32[8,32]{1,0:T(8,128)S(1)}, s32[8,32]{1,0:T(8,128)S(1)}) fusion(s32[32,8]{0,1:T(8,128)} %param.10, s32[]{:T(128)S(6)} %sub.32, s32[]{:T(128)S(6)} %select_n.83, s32[]{:T(128)S(6)} %select_n.82, s32[]{:T(128)S(6)} %add.66, s32[]{:T(128)S(6)} %mul.15, s32[32]{0:T(128)} %param.11, s32[]{:T(128)S(6)} %select_n.81, s32[32,8]{0,1:T(8,128)} %param.15), kind=kLoop, calls=%fused_computation.21 | loop fusion | flops 22784 | bytes 4248 | tf_op jit(solution)/shard_map/jit(_where)/select_n | solution.py:398
  12.7 0.7 %pad_add_fusion.__.places = s32[17,32]{1,0:T(8,128)S(1)} fusion(s32[1,32]{1,0:T(1,128)} %bitcast.30, s32[8,32]{1,0:T(8,128)S(1)} %get-tuple-element.35, s32[8,32]{1,0:T(8,128)S(1)} %get-tuple-element.34), kind=kLoop, calls=%fused_computation | loop fusion | flops 1088 | bytes 4352 | tf_op jit(solution)/shard_map/concatenate | solution.py:402
  13.4 1.6 %prepare.1 = (bf16[128,512]{1,0:T(8,128)(2,1)S(1)}, bf16[128,512]{1,0:T(8,128)(2,1)S(1)}, bf16[512,128]{1,0:T(8,128)(2,1)S(1)}) custom-call(f32[8,16,16,32]{3,2,1,0:T(8,128)} %bitcast.27, bf16[512,128]{1,0:T(8,128)(2,1)} %bitcast.28, bf16[8,32,128]{2,1,0:T(8,128)(2,1)} %get-tuple-element.20._, s32[17,32]{1,0:T(8,128)S(1)} %pad_add_fusion.__.places), custom_call_target="tpu_custom_call" | custom-call | tf_op jit(solution)/shard_map/prepare/pallas_call | solution.py:370
  14.9 3.8 %all-to-all-done.refs_0_.values = bf16[8,32,128]{2,1,0:T(8,128)(2,1)S(1)} async-done(((bf16[8,32,128]{2,1,0:T(8,128)(2,1)}), bf16[8,32,128]{2,1,0:T(8,128)(2,1)S(1)}, u32[]{:S(2)}, u32[]{:S(2)}) %all-to-all-start) | async-done | bytes 65568 | tf_op jit(solution)/shard_map/all_to_all | solution.py:380
  18.7 3.8 %fetch.2 = (bf16[256,128,128]{2,1,0:T(8,128)(2,1)S(1)}, f32[8,128]{1,0:T(8,128)S(1)}) custom-call(bf16[256,128,128]{2,1,0:T(8,128)(2,1)} %bitcast.25, s32[17,32]{1,0:T(8,128)S(1)} %pad_add_fusion.__.places, bf16[8,32,128]{2,1,0:T(8,128)(2,1)S(1)} %all-to-all-done.refs_0_.values, bf16[512,128]{1,0:T(8,128)(2,1)S(1)} %get-tuple-element.21.refs_1_.target), custom_call_target="tpu_custom_call" | custom-call | tf_op jit(solution)/shard_map/fetch/pallas_call | solution.py:370
  22.7 0.5 collective-permute-start
  23.2 0.1 collective-permute-start.4
  23.2 0.9 %collective-permute-done.mate = bf16[256,128]{1,0:T(8,128)(2,1)S(1)} collective-permute-done((bf16[256,128]{1,0:T(8,128)(2,1)S(1)}, bf16[256,128]{1,0:T(8,128)(2,1)S(1)}, u32[]{:S(2)}, u32[]{:S(2)}) %collective-permute-start) | collective-permute-done | bytes 65568 | tf_op jit(solution)/shard_map/ppermute | solution.py:308
  24.1 0.3 collective-permute-done.4.got_mate
  24.4 4.7 %operator_one.1 = (f32[256,128]{1,0:T(8,128)S(1)}, bf16[256,128]{1,0:T(8,128)(2,1)S(1)}, bf16[8,48,128]{2,1,0:T(8,128)(2,1)}) custom-call(bf16[256,128]{1,0:T(8,128)(2,1)S(1)} %get-tuple-element.19.own, bf16[256,128]{1,0:T(8,128)(2,1)S(1)} %collective-permute-done.mate, bf16[256,128]{1,0:T(8,128)(2,1)S(1)} %collective-permute-done.1.even, ...), custom_call_target="tpu_custom_call" | custom-call | tf_op jit(solution)/shard_map/operator_one/pallas_call | solution.py:370
  29.2 3.4 %all-to-all-start.1 = ((bf16[8,48,128]{2,1,0:T(8,128)(2,1)}), bf16[8,48,128]{2,1,0:T(8,128)(2,1)S(1)}, u32[]{:S(2)}, u32[]{:S(2)}) async-start(bf16[8,48,128]{2,1,0:T(8,128)(2,1)} %get-tuple-element.29), calls=%async_computation.1 | async-start | bytes 196608 | tf_op jit(solution)/shard_map/all_to_all | solution.py:380
  32.5 4.7 %collective-permute-start.7 = (bf16[256,128]{1,0:T(8,128)(2,1)S(1)}, bf16[256,128]{1,0:T(8,128)(2,1)S(1)}, u32[]{:S(2)}, u32[]{:S(2)}) collective-permute-start(bf16[256,128]{1,0:T(8,128)(2,1)S(1)} %get-tuple-element.28.own), channel_id=1, source_target_pairs={{0,14},{1,15},{2,4},{3,5},{4,2},{5,3},{6,8},{7,9},{8,6},{9,7},{10,... | collective-permute-start | bytes 196616 | tf_op jit(solution)/shard_map/ppermute | solution.py:308
  37.2 3.1 %all-to-all-done.1.refs_0_.values = bf16[8,48,128]{2,1,0:T(8,128)(2,1)S(1)} async-done(((bf16[8,48,128]{2,1,0:T(8,128)(2,1)}), bf16[8,48,128]{2,1,0:T(8,128)(2,1)S(1)}, u32[]{:S(2)}, u32[]{:S(2)}) %all-to-all-start.1) | async-done | bytes 98336 | tf_op jit(solution)/shard_map/all_to_all | solution.py:380
  40.3 3.8 %fetch.3 = (bf16[256,128,128]{2,1,0:T(8,128)(2,1)S(1)}, f32[8,128]{1,0:T(8,128)S(1)}) custom-call(bf16[256,128,128]{2,1,0:T(8,128)(2,1)} %bitcast.26, s32[17,32]{1,0:T(8,128)S(1)} %pad_add_fusion.__.places, bf16[8,48,128]{2,1,0:T(8,128)(2,1)S(1)} %all-to-all-done.1.refs_0_.values), custom_call_target="tpu_custom_call" | custom-call | tf_op jit(solution)/shard_map/fetch/pallas_call | solution.py:370
  44.1 0.1 collective-permute-start.8
  44.2 0.5 collective-permute-start.9
  44.7 0.1 collective-permute-start.5
  44.8 1.2 %collective-permute-done.5.mate = bf16[256,128]{1,0:T(8,128)(2,1)S(1)} collective-permute-done((bf16[256,128]{1,0:T(8,128)(2,1)S(1)}, bf16[256,128]{1,0:T(8,128)(2,1)S(1)}, u32[]{:S(2)}, u32[]{:S(2)}) %collective-permute-start.5) | collective-permute-done | bytes 65568 | tf_op jit(solution)/shard_map/ppermute | solution.py:308
  45.9 4.1 %operator_two.1 = (f32[256,128]{1,0:T(8,128)S(1)}, bf16[16,8,128]{2,1,0:T(8,128)(2,1)S(1)}) custom-call(bf16[256,128]{1,0:T(8,128)(2,1)S(1)} %get-tuple-element.28.own, bf16[256,128]{1,0:T(8,128)(2,1)S(1)} %collective-permute-done.5.mate, bf16[256,128]{1,0:T(8,128)(2,1)S(1)} %collective-permute-done.6.even, ...), custom_call_target="tpu_custom_call" | custom-call | tf_op jit(solution)/shard_map/operator_two/pallas_call | solution.py:370
  50.0 9.2 %all_to_all.15.got2 = bf16[16,8,128]{2,1,0:T(8,128)(2,1)S(1)} all-to-all(bf16[16,8,128]{2,1,0:T(8,128)(2,1)S(1)} %get-tuple-element.33), channel_id=1, replica_groups=mesh['groups'=2,'rows'=16] {'rows'}, dimensions={0} | all-to-all | bytes 65536 | tf_op jit(solution)/shard_map/all_to_all | solution.py:376
  59.2 1.5 %finish.1 = (f32[8,4096]{1,0:T(8,128)}, f32[8,4096]{1,0:T(8,128)}) custom-call(f32[256,128]{1,0:T(8,128)S(1)} %get-tuple-element.18.b, f32[256,128]{1,0:T(8,128)S(1)} %get-tuple-element.27.image, f32[256,128]{1,0:T(8,128)S(1)} %get-tuple-element.32.candidate, bf16[8,48,128]{2,1,0:T(8,128)(2,1)S(1)} %behind.3._.got.got1, ...), custom_call_target="tpu_custom_call" | custom-call | tf_op jit(solution)/shard_map/finish/pallas_call | solution.py:370
  (14 shorter events, 0.1 us)
Async XLA Ops:
  2.5 20.1 %collective-permute-start.2 = (bf16[256,128]{1,0:T(8,128)(2,1)S(1)}, bf16[256,128]{1,0:T(8,128)(2,1)S(1)}, u32[]{:S(2)}, u32[]{:S(2)}) collective-permute-start(bf16[256,128]{1,0:T(8,128)(2,1)S(1)} %get-tuple-element.19.own), channel_id=1, source_target_pairs={{0,14},{1,15},{2,4},{3,5},{4,2},{5,3},{6,8},{7,9},{8,6},{9,7},{10,... | collective-permute-start | bytes 196616 | tf_op jit(solution)/shard_map/ppermute | solution.py:308
  8.5 14.0 %collective-permute-start.1 = (bf16[256,128]{1,0:T(8,128)(2,1)S(1)}, bf16[256,128]{1,0:T(8,128)(2,1)S(1)}, u32[]{:S(2)}, u32[]{:S(2)}) collective-permute-start(bf16[256,128]{1,0:T(8,128)(2,1)S(1)} %get-tuple-element.19.own), channel_id=1, source_target_pairs={{0,2},{1,3},{2,0},{3,1},{4,6},{5,7},{6,4},{7,5},{8,10},{9,11},{10,... | collective-permute-start | bytes 196616 | tf_op jit(solution)/shard_map/ppermute | solution.py:308
  8.5 10.2 %all-to-all-start = ((bf16[8,32,128]{2,1,0:T(8,128)(2,1)}), bf16[8,32,128]{2,1,0:T(8,128)(2,1)S(1)}, u32[]{:S(2)}, u32[]{:S(2)}) async-start(bf16[8,32,128]{2,1,0:T(8,128)(2,1)} %get-tuple-element.20._), calls=%async_computation | async-start | bytes 131072 | tf_op jit(solution)/shard_map/all_to_all | solution.py:380
  22.6 1.8 %collective-permute-start.3 = (bf16[512,128]{1,0:T(8,128)(2,1)S(1)}, bf16[512,128]{1,0:T(8,128)(2,1)S(1)}, u32[]{:S(2)}, u32[]{:S(2)}) collective-permute-start(bf16[512,128]{1,0:T(8,128)(2,1)S(1)} %relay.2), channel_id=1, source_target_pairs={{0,1},{1,0},{2,3},{3,2},{4,5},{5,4},{6,7},{7,6},{8,9},{9,8},{10,11... | collective-permute-start | bytes 393224 | tf_op jit(solution)/shard_map/ppermute | solution.py:308
  22.7 1.4 %collective-permute-start = (bf16[256,128]{1,0:T(8,128)(2,1)S(1)}, bf16[256,128]{1,0:T(8,128)(2,1)S(1)}, u32[]{:S(2)}, u32[]{:S(2)}) collective-permute-start(bf16[256,128]{1,0:T(8,128)(2,1)S(1)} %get-tuple-element.19.own), channel_id=1, source_target_pairs={{0,1},{1,0},{2,3},{3,2},{4,5},{5,4},{6,7},{7,6},{8,9},{9,8},{10,11... | collective-permute-start | bytes 196616 | tf_op jit(solution)/shard_map/ppermute | solution.py:308
  23.2 1.3 %collective-permute-start.4 = (bf16[8,32,128]{2,1,0:T(8,128)(2,1)S(1)}, bf16[8,32,128]{2,1,0:T(8,128)(2,1)S(1)}, u32[]{:S(2)}, u32[]{:S(2)}) collective-permute-start(bf16[8,32,128]{2,1,0:T(8,128)(2,1)S(1)} %behind.2._.got), channel_id=1, source_target_pairs={{0,1},{1,0},{2,3},{3,2},{4,5},{5,4},{6,7},{7,6},{8,9},{9,8},{10,11... | collective-permute-start | bytes 196616 | tf_op jit(solution)/shard_map/ppermute | solution.py:308
  29.2 11.1 %all-to-all-start.1 = ((bf16[8,48,128]{2,1,0:T(8,128)(2,1)}), bf16[8,48,128]{2,1,0:T(8,128)(2,1)S(1)}, u32[]{:S(2)}, u32[]{:S(2)}) async-start(bf16[8,48,128]{2,1,0:T(8,128)(2,1)} %get-tuple-element.29), calls=%async_computation.1 | async-start | bytes 196608 | tf_op jit(solution)/shard_map/all_to_all | solution.py:380
  32.5 11.5 %collective-permute-start.7 = (bf16[256,128]{1,0:T(8,128)(2,1)S(1)}, bf16[256,128]{1,0:T(8,128)(2,1)S(1)}, u32[]{:S(2)}, u32[]{:S(2)}) collective-permute-start(bf16[256,128]{1,0:T(8,128)(2,1)S(1)} %get-tuple-element.28.own), channel_id=1, source_target_pairs={{0,14},{1,15},{2,4},{3,5},{4,2},{5,3},{6,8},{7,9},{8,6},{9,7},{10,... | collective-permute-start | bytes 196616 | tf_op jit(solution)/shard_map/ppermute | solution.py:308
  37.2 6.9 %collective-permute-start.6 = (bf16[256,128]{1,0:T(8,128)(2,1)S(1)}, bf16[256,128]{1,0:T(8,128)(2,1)S(1)}, u32[]{:S(2)}, u32[]{:S(2)}) collective-permute-start(bf16[256,128]{1,0:T(8,128)(2,1)S(1)} %get-tuple-element.28.own), channel_id=1, source_target_pairs={{0,2},{1,3},{2,0},{3,1},{4,6},{5,7},{6,4},{7,5},{8,10},{9,11},{10,... | collective-permute-start | bytes 196616 | tf_op jit(solution)/shard_map/ppermute | solution.py:308
  44.1 1.8 %collective-permute-start.8 = (bf16[512,128]{1,0:T(8,128)(2,1)S(1)}, bf16[512,128]{1,0:T(8,128)(2,1)S(1)}, u32[]{:S(2)}, u32[]{:S(2)}) collective-permute-start(bf16[512,128]{1,0:T(8,128)(2,1)S(1)} %relay.3), channel_id=1, source_target_pairs={{0,1},{1,0},{2,3},{3,2},{4,5},{5,4},{6,7},{7,6},{8,9},{9,8},{10,11... | collective-permute-start | bytes 393224 | tf_op jit(solution)/shard_map/ppermute | solution.py:308
  44.2 1.8 %collective-permute-start.9 = (bf16[8,48,128]{2,1,0:T(8,128)(2,1)S(1)}, bf16[8,48,128]{2,1,0:T(8,128)(2,1)S(1)}, u32[]{:S(2)}, u32[]{:S(2)}) collective-permute-start(bf16[8,48,128]{2,1,0:T(8,128)(2,1)S(1)} %behind.3._.got.got1), channel_id=1, source_target_pairs={{0,1},{1,0},{2,3},{3,2},{4,5},{5,4},{6,7},{7,6},{8,9},{9,8},{10,11... | collective-permute-start | bytes 294920 | tf_op jit(solution)/shard_map/ppermute | solution.py:308
  44.7 1.3 %collective-permute-start.5 = (bf16[256,128]{1,0:T(8,128)(2,1)S(1)}, bf16[256,128]{1,0:T(8,128)(2,1)S(1)}, u32[]{:S(2)}, u32[]{:S(2)}) collective-permute-start(bf16[256,128]{1,0:T(8,128)(2,1)S(1)} %get-tuple-element.28.own), channel_id=1, source_target_pairs={{0,1},{1,0},{2,3},{3,2},{4,5},{5,4},{6,7},{7,6},{8,9},{9,8},{10,11... | collective-permute-start | bytes 196616 | tf_op jit(solution)/shard_map/ppermute | solution.py:308

commit v13 on v12

--- a/solution.py
+++ b/solution.py
@@ -45,14 +45,22 @@
     return tile
 
 
-def read_sums(gathered, first_row, rows, count, unknowns):
+def read_sums(parts, count, unknowns):
     total = jnp.zeros((R, LANES), f32)
-    for got in gathered:
-        for device in range(got.shape[0]):
-            total = total + got[device, pl.ds(first_row, rows), :].astype(f32)[:R]
+    for part in parts:
+        total = total + part.astype(f32)[:R]
     return [
         sum(total[:, p * SUM_SLOTS + t : p * SUM_SLOTS + t + 1] for p in range(3)) * (1.0 / unknowns)
         for t in range(count)
+    ]
+
+
+def tails(swaps, rows, head):
+    each = head + TAIL
+    return [
+        values[pl.ds(device * each + head, TAIL), :]
+        for values in swaps
+        for device in range((values.shape[0] - rows) // each)
     ]
 
 
@@ -123,65 +131,63 @@
     target_out[...] = dot((column == wanted).astype(bf16), target[...]).astype(bf16)
 
 
-def fetch_kernel(least, blocks_hbm, places, *refs):
+def fetch_kernel(first, blocks_hbm, *refs):
     *_, blocks, token, sems = refs
-    clusters = sems.shape[0]
-    slots = blocks.shape[0] // clusters
-
-    def for_live(i, act):
-        count = places[2 * slots, i]
-        for live in range(least, slots + 1):
-            pl.when(count <= live if live == least else count == live)(functools.partial(act, i, live))
-
-    def copy_of(i, live):
-        span = pl.ds(i * slots, live)
-        return pltpu.make_async_copy(blocks_hbm.at[span], blocks.at[span], sems.at[i])
-
-    def start(i, live):
-        copy_of(i, live).start()
-        if live < slots:
-            blocks[pl.ds(i * slots + live, slots - live)] = jnp.zeros((slots - live, LANES, LANES), bf16)
-
-    def body(act, i, carry):
-        for_live(i, act)
-        return carry
-
-    lax.fori_loop(0, clusters, functools.partial(body, start), 0)
+    chunks = sems.shape[0]
+    each = blocks.shape[0] // chunks
+    copies = [
+        pltpu.make_async_copy(
+            blocks_hbm.at[pl.ds(first + c * each, each)], blocks.at[pl.ds(c * each, each)], sems.at[c]
+        )
+        for c in range(chunks)
+    ]
+    for copy in copies:
+        copy.start()
     token[...] = jnp.zeros_like(token)
-    lax.fori_loop(0, clusters, functools.partial(body, lambda i, live: copy_of(i, live).wait()), 0)
-
-
-def behind_kernel(values, *refs):
-    refs[-1][...] = values[...]
-
-
-def relay_kernel(even, odd, _, both):
-    rows = even.shape[0]
-    both[pl.ds(0, rows), :] = even[...]
-    both[pl.ds(rows, rows), :] = odd[...]
-
-
-def apply(per_group, slabs, places, blocks, got, got_mate, high, low, target, near, far, window, table):
+    for copy in copies:
+        copy.wait()
+
+
+def relay_kernel(axis, got, even, odd, _, out):
+    me = lax.axis_index(axis)
+    devices, each, _ = got.shape
+    for device in range(devices):
+        out[pl.ds(device * each, each), :] = got[device]
+    wants_even = (me // 2 + me) % 2 == 0
+    span = pl.ds(devices * each, even.shape[0])
+
+    @pl.when(wants_even)
+    def _():
+        out[span, :] = even[...]
+
+    @pl.when(jnp.logical_not(wants_even))
+    def _():
+        out[span, :] = odd[...]
+
+
+def apply(per_group, each, slabs, places, ahead, blocks, swaps, high, low, target, near, far, window, table):
     clusters = near.shape[0] // R
-    slots = blocks.shape[0] // clusters
+    slots = (ahead.shape[0] + blocks.shape[0]) // clusters
     rank = LANES // per_group
     head = clusters // per_group * R
-    at = 0
-    for slab in slabs:
-        window[pl.ds(at, slab.shape[0]), :] = slab[...].astype(f32)
-        at += slab.shape[0]
-    window[pl.ds(at, R), :] = jnp.zeros((R, LANES), f32)
-    for part, values in enumerate((got, got_mate)):
-        for device in range(values.shape[0]):
-            at = (part * values.shape[0] + device) * head
-            table[pl.ds(at, head), :] = values[device, pl.ds(0, head), :].astype(f32)
+    rows = slabs[0].shape[0]
+    devices = (swaps[0].shape[0] - rows) // each
+    for at, slab in enumerate(slabs):
+        window[pl.ds(at * rows, rows), :] = slab[...].astype(f32)
+    window[pl.ds(len(slabs) * rows, rows), :] = swaps[1][pl.ds(devices * each, rows), :].astype(f32)
+    window[pl.ds((len(slabs) + 1) * rows, R), :] = jnp.zeros((R, LANES), f32)
+    for part, values in enumerate(swaps):
+        for device in range(devices):
+            at = (part * devices + device) * head
+            table[pl.ds(at, head), :] = values[pl.ds(device * each, head), :].astype(f32)
     lane = lane_ids()
 
     def fetch(k, i):
         return window[pl.ds(pl.multiple_of(places[k, i] * R, R), R), :]
 
     def block(k, i):
-        return blocks[i * slots + k]
+        at = i * slots + k
+        return ahead[at] if at < ahead.shape[0] else blocks[at - ahead.shape[0]]
 
     def pick(i):
         tile = jnp.zeros((R, LANES), f32)
@@ -205,33 +211,35 @@
             both = both + dot(sources.astype(bf16), weights, (1, 1))
         near[pl.ds(i * R, R), :] = both[:R, :LANES]
         near[pl.ds((i + 1) * R, R), :] = both[R:, LANES:]
-        picked += [pick(i), pick(i + 1)]
-
-    picked = jnp.concatenate(picked, axis=0).astype(bf16)
-    crossed = dot(picked, high[...]) + dot(picked, low[...])
-    expanded_high, expanded_low = [], []
-    for s in range(rank * clusters // LANES):
-        tile = jnp.zeros((R, LANES), f32)
-        for i in range(clusters):
-            part = crossed[i * R : (i + 1) * R, s * LANES : (s + 1) * LANES]
-            tile = jnp.where(lane % clusters == i, part, tile)
-        tile_high = tile.astype(bf16).astype(f32)
-        tile_low = tile - tile_high
-        for source, kept in ((tile_high, expanded_high), (tile_low, expanded_low)):
-            spread = [jnp.where(lane % clusters == i, source, 0.0) for i in range(clusters)]
-            kept.append(jnp.concatenate(spread, axis=0).astype(bf16))
-    far[...] = dot(jnp.concatenate(expanded_high, axis=1), target[...]) + dot(
-        jnp.concatenate(expanded_low, axis=1), target[...]
-    )
+        if 2 * i < clusters:
+            picked += [pick(n) for n in range(2 * i, 2 * i + 4)]
+        if 2 * i == clusters - 4:
+            picked = jnp.concatenate(picked, axis=0).astype(bf16)
+            crossed = dot(picked, high[...]) + dot(picked, low[...])
+            expanded_high, expanded_low = [], []
+            for s in range(rank * clusters // LANES):
+                tile = jnp.zeros((R, LANES), f32)
+                for n in range(clusters):
+                    part = crossed[n * R : (n + 1) * R, s * LANES : (s + 1) * LANES]
+                    tile = jnp.where(lane % clusters == n, part, tile)
+                tile_high = tile.astype(bf16).astype(f32)
+                tile_low = tile - tile_high
+                for source, kept in ((tile_high, expanded_high), (tile_low, expanded_low)):
+                    spread = [jnp.where(lane % clusters == n, source, 0.0) for n in range(clusters)]
+                    kept.append(jnp.concatenate(spread, axis=0).astype(bf16))
+            far[...] = dot(jnp.concatenate(expanded_high, axis=1), target[...]) + dot(
+                jnp.concatenate(expanded_low, axis=1), target[...]
+            )
 
 
 def first_kernel(
-    per_group, own, mate, even, odd, relayed, places, blocks, got, got_mate, high, low, target, b, basis,
+    per_group, own, mate, even, odd, places, ahead, blocks, sent, received, high, low, target, b, basis,
     image, lowered, payload, near, far, window, table,
 ):
-    slabs = (own, mate, even, odd, relayed)
-    apply(per_group, slabs, places, blocks, got, got_mate, high, low, target, near, far, window, table)
     clusters = near.shape[0] // R
+    slabs, swaps = (own, mate, even, odd), (sent, received)
+    each = clusters // per_group * R
+    apply(per_group, each, slabs, places, ahead, blocks, swaps, high, low, target, near, far, window, table)
     tiles = []
     sums = [jnp.zeros((R, LANES), f32) for _ in range(3)]
     for i in range(clusters):
@@ -258,14 +266,15 @@
 
 
 def second_kernel(
-    per_group, unknowns, own, mate, even, odd, relayed, places, blocks, got, got_mate, high, low, target, b, image,
+    per_group, unknowns, own, mate, even, odd, places, ahead, blocks, sent, received, high, low, target, b, image,
     candidate, sums_out, near, far, window, table,
 ):
-    slabs = (own, mate, even, odd, relayed)
-    apply(per_group, slabs, places, blocks, got, got_mate, high, low, target, near, far, window, table)
     clusters = near.shape[0] // R
     head = clusters // per_group * R
-    start_norm, h11, h21, _, _, _ = arnoldi_one(*read_sums((got, got_mate), head, TAIL, 3, unknowns))
+    slabs, swaps = (own, mate, even, odd), (sent, received)
+    apply(per_group, head + TAIL, slabs, places, ahead, blocks, swaps, high, low, target, near, far, window, table)
+    sums = read_sums(tails(swaps, own.shape[0], head), 3, unknowns)
+    start_norm, h11, h21, _, _, _ = arnoldi_one(*sums)
     scale = 1.0 / start_norm
     inverse = 1.0 / h21
     sums = [jnp.zeros((R, LANES), f32) for _ in range(3)]
@@ -281,11 +290,11 @@
         sums_out[device] = tile
 
 
-def finish_kernel(per_group, unknowns, b, image, candidate, got1, got1_mate, got2, solution_out, next_out):
+def finish_kernel(per_group, unknowns, b, image, candidate, sent, received, got, solution_out, next_out):
     clusters = b.shape[0] // R
-    head = clusters // per_group * R
-    start_norm, h11, h21, v11, v22, v12 = arnoldi_one(*read_sums((got1, got1_mate), head, TAIL, 3, unknowns))
-    h12, h22, ww = read_sums((got2,), 0, R, 3, unknowns)
+    sums = read_sums(tails((sent, received), b.shape[0], clusters // per_group * R), 3, unknowns)
+    start_norm, h11, h21, v11, v22, v12 = arnoldi_one(*sums)
+    h12, h22, ww = read_sums([got[device] for device in range(got.shape[0])], 3, unknowns)
     uu = ww - 2.0 * (h12 * h12 + h22 * h22) + h12 * h12 * v11 + h22 * h22 * v22 + 2.0 * h12 * h22 * v12
     h32 = jnp.sqrt(jnp.maximum(uu, 0.0) + epsilon)
     g11 = h11 * h11 + h21 * h21
@@ -332,9 +341,9 @@
     before, after = 3 - chip % 2, 2 + chip % 2
     slot = [
         before,
-        jnp.where(core == 0, before + 2, 1),
+        jnp.where(core == 0, 4, 1),
         0,
-        jnp.where(core == 0, 1, after + 2),
+        jnp.where(core == 0, 1, 4),
         after,
     ]
     slab = distance // clusters
@@ -395,11 +404,11 @@
     start = lax.axis_index("rows") * clusters
     distance = (near_cols.T - start + reach) % every
     live = jnp.arange(slots, dtype=jnp.int32)[:, None] < near_counts[None, :]
-    placed = jnp.where(live, window_place(distance, clusters), 6 * clusters).astype(jnp.int32)
+    placed = jnp.where(live, window_place(distance, clusters), 5 * clusters).astype(jnp.int32)
     owner = far_cols.T // clusters
     other_core = (owner % 2) ^ (lax.axis_index("rows") % 2)
     far_index = (other_core * (size // 2) + owner // 2) * clusters + far_cols.T % clusters
-    places = jnp.concatenate([placed, far_index, near_counts[None, :]], axis=0)
+    places = jnp.concatenate([placed, far_index], axis=0)
     high, low, target = call(
         prepare_kernel, "prepare",
         (
@@ -418,43 +427,44 @@
     blocks = in_hbm(near_blocks.reshape(clusters * slots, LANES, LANES))
 
 
-    def arrived(got, held, *made):
-        near_blocks_here, token = call(
-            functools.partial(fetch_kernel, 3), "fetch", (pltpu.VMEM(blocks.shape, bf16), shape(R, LANES)),
-            [HBM, SMEM] + [ANY] * (1 + len(made)), blocks, places, got, *made,
-            scratch_shapes=[pltpu.SemaphoreType.DMA((clusters,))],
+    early = blocks.shape[0] * 3 // 16
+
+    def fetch(name, first, count, chunks, *behind):
+        here, token = call(
+            functools.partial(fetch_kernel, first), name, (pltpu.VMEM((count, LANES, LANES), bf16), shape(R, LANES)),
+            [HBM] + [ANY] * len(behind), blocks, *behind, scratch_shapes=[pltpu.SemaphoreType.DMA((chunks,))],
         )
-        near_blocks_here = pltpu.with_memory_space_constraint(near_blocks_here, pltpu.VMEM)
-        got = call(
-            behind_kernel, "behind", shape(*got.shape, dtype=bf16), [VMEM] + [ANY] * 2, got, held[3], token
+        return pltpu.with_memory_space_constraint(here, pltpu.VMEM), token
+
+    def arrived(got, held, made):
+        ahead, token = fetch("ahead", 0, early, 2, made)
+        near_blocks_here, token = fetch("fetch", early, blocks.shape[0] - early, 8, got, token)
+        sent = call(
+            functools.partial(relay_kernel, "rows"), "relay",
+            shape(got.shape[0] * got.shape[1] + rows, LANES, dtype=bf16), [VMEM] * 3 + [ANY], got, *held[2:], token
         )
-        relay = call(
-            relay_kernel, "relay", shape(2 * rows, LANES, dtype=bf16), [VMEM] * 2 + [ANY], *held[2:], got
-        )
-        got = (got, swapped(got, core_mate))
-        return (*held, swapped(relay, core_mate)), near_blocks_here, got
-
-    kept = [scratch(rows, LANES), scratch(rows, LANES), scratch(6 * rows + R, LANES), scratch(size * head, LANES)]
-    operands = [VMEM] * 5 + [SMEM] + [VMEM] * 8
-    slabs, near_blocks_here, got = arrived(got, held, target)
+        return *held, places, ahead, near_blocks_here, sent, swapped(sent, core_mate), high, low, target
+
+    kept = [scratch(rows, LANES), scratch(rows, LANES), scratch(5 * rows + R, LANES), scratch(size * head, LANES)]
+    operands = [VMEM] * 4 + [SMEM] + [VMEM] * 9
     image, lowered, payload = call(
         functools.partial(first_kernel, per_group), "operator_one",
         (
             shape(rows, LANES), shape(rows, LANES, dtype=bf16),
             shape(size // 2, head + TAIL, LANES, dtype=bf16),
         ),
-        operands, *slabs, places, near_blocks_here, *got, high, low, target, field, basis, scratch_shapes=kept,
-    )
-    got = gather(payload)
-    slabs, near_blocks_here, got = arrived(got, sends_of(lowered))
+        operands, *arrived(got, held, target), field, basis, scratch_shapes=kept,
+    )
+    held = sends_of(lowered)
+    here = arrived(gather(payload), held, held[2])
     candidate, sums = call(
         functools.partial(second_kernel, per_group, unknowns), "operator_two",
         (shape(rows, LANES), shape(size, R, LANES, dtype=bf16)),
-        operands, *slabs, places, near_blocks_here, *got, high, low, target, field, image, scratch_shapes=kept,
+        operands, *here, field, image, scratch_shapes=kept,
     )
     return call(
         functools.partial(finish_kernel, per_group, unknowns), "finish", (shape(R, width), shape(R, width)),
-        [VMEM] * 6, field, image, candidate, *got, exchange(sums),
+        [VMEM] * 6, field, image, candidate, *here[7:9], exchange(sums),
     )
 
 

time: 61.4 us -> 60.6 us (0.987)
  waiting for transfers between devices: 9.25 us -> 5.86 us
  blocking collectives: 9.2 us -> 11.3 us
  Pallas kernels: 21.3 us -> 22.3 us
  other arithmetic: 1.41 us -> 0.75 us
    all_to_all x2, waiting for transfers between devices: 6.88 us -> 3.94 us  [gather(): return lax.all_to_all(block, 'rows', 0, 0, axis_index_groups=groups)]
    all_to_all x1, blocking collectives: 9.2 us -> 11.3 us  [exchange(): return lax.all_to_all(block, 'rows', 0, 0)]
    pallas_call x11, Pallas kernels: 21.3 us -> 22.3 us  [call(): pl.pallas_call(kernel, out_shape=out, in_specs=ins, out_specs=jax.tree.ma...]
    concatenate x1, other arithmetic: 0.66 us -> 0.01 us  [on_device(): places = jnp.concatenate([placed, far_index], axis=0)]
    ppermute x10 -> x8, waiting for transfers between devices: 2.37 us -> 1.92 us  [swapped(): lax.ppermute(block, 'rows', [(i, partner(i)) for i in range(lax.axis_size...]
    ppermute x10 -> x8, starting transfers between devices: 12 us -> 12.4 us  [swapped(): lax.ppermute(block, 'rows', [(i, partner(i)) for i in range(lax.axis_size...]
  transfers between devices with their start and end apart: 12 -> 10, of which waited for: 5 -> 4; matrix products, arithmetic and copies ran while one was open for 2% -> 1% of each run, Pallas kernels for 15% -> 17%
where the time goes in v13:
time: 60.6 us; the launch traced here: 60.2 us
  Pallas kernels  22.3 us (37%)
  starting transfers between devices  19.1 us (32%)
  blocking collectives  11.3 us (19%)
  waiting for transfers between devices  5.86 us (10%)
  between operations  0.82 us (1%)
  other arithmetic  0.75 us (1%)
    pallas_call x11, Pallas kernels, call(): pl.pallas_call(kernel, out_shape=out, in_specs=ins, out_specs=jax.tree.ma...  22.3 us
    ppermute x8, starting transfers between devices, swapped(): lax.ppermute(block, 'rows', [(i, partner(i)) for i in range(lax.axis_size...  12.4 us
    all_to_all x1, blocking collectives, exchange(): return lax.all_to_all(block, 'rows', 0, 0)  11.3 us
    all_to_all x2, starting transfers between devices, gather(): return lax.all_to_all(block, 'rows', 0, 0, axis_index_groups=groups)  6.71 us
    all_to_all x2, waiting for transfers between devices, gather(): return lax.all_to_all(block, 'rows', 0, 0, axis_index_groups=groups)  3.94 us
    ppermute x8, waiting for transfers between devices, swapped(): lax.ppermute(block, 'rows', [(i, partner(i)) for i in range(lax.axis_size...  1.92 us
  transfers between devices with their start and end apart: 10, of which 4 were waited for; matrix products, arithmetic and copies ran while one was open for 1% of the time, Pallas kernels for 17%

profile of v13, /device:TPU:0, one launch (start us, length us, event | category | flops | bytes accessed | tf_op | source)
XLA Modules:
  0.0 60.2 jit_solution(16919308073469261512)
XLA Ops:
  0.6 1.8 %start.1 = (f32[256,128]{1,0:T(8,128)S(1)}, bf16[512,128]{1,0:T(8,128)(2,1)S(1)}, bf16[256,128]{1,0:T(8,128)(2,1)S(1)}, bf16[8,32,128]{2,1,0:T(8,128)(2,1)}) custom-call(f32[8,4096]{1,0:T(8,128)} %b_hbm.1, bf16[512,128]{1,0:T(8,128)(2,1)} %bitcast.30), custom_call_target="tpu_custom_call" | custom-call | tf_op jit(solution)/shard_map/start/pallas_call | solution.py:379
  2.5 6.1 %collective-permute-start.2 = (bf16[256,128]{1,0:T(8,128)(2,1)S(1)}, bf16[256,128]{1,0:T(8,128)(2,1)S(1)}, u32[]{:S(2)}, u32[]{:S(2)}) collective-permute-start(bf16[256,128]{1,0:T(8,128)(2,1)S(1)} %get-tuple-element.23.own), channel_id=1, source_target_pairs={{0,14},{1,15},{2,4},{3,5},{4,2},{5,3},{6,8},{7,9},{8,6},{9,7},{10,... | collective-permute-start | bytes 196616 | tf_op jit(solution)/shard_map/ppermute | solution.py:317
  8.5 3.4 %all-to-all-start = ((bf16[8,32,128]{2,1,0:T(8,128)(2,1)}), bf16[8,32,128]{2,1,0:T(8,128)(2,1)S(1)}, u32[]{:S(2)}, u32[]{:S(2)}) async-start(bf16[8,32,128]{2,1,0:T(8,128)(2,1)} %get-tuple-element.24._), calls=%async_computation | async-start | bytes 131072 | tf_op jit(solution)/shard_map/all_to_all | solution.py:389
  11.9 0.7 %fusion.2 = (s32[8,32]{1,0:T(8,128)S(1)}, s32[8,32]{1,0:T(8,128)S(1)}) fusion(s32[32,8]{0,1:T(8,128)} %param.10, s32[]{:T(128)S(6)} %sub.32, s32[]{:T(128)S(6)} %select_n.83, s32[]{:T(128)S(6)} %select_n.82, s32[]{:T(128)S(6)} %add.57, s32[]{:T(128)S(6)} %mul.15, s32[32]{0:T(128)} %param.11, s32[]{:T(128)S(6)} %select_n.81, s32[32,8]{0,1:T(8,128)} %param.15), kind=kLoop, calls=%fused_computation.21 | loop fusion | flops 22784 | bytes 4248 | tf_op jit(solution)/shard_map/jit(_where)/select_n | solution.py:407
  12.7 1.6 %prepare.1 = (bf16[128,512]{1,0:T(8,128)(2,1)S(1)}, bf16[128,512]{1,0:T(8,128)(2,1)S(1)}, bf16[512,128]{1,0:T(8,128)(2,1)S(1)}) custom-call(f32[8,16,16,32]{3,2,1,0:T(8,128)} %bitcast.28, bf16[512,128]{1,0:T(8,128)(2,1)} %bitcast.29, bf16[8,32,128]{2,1,0:T(8,128)(2,1)} %get-tuple-element.24._, s32[16,32]{1,0:T(8,128)S(1)} %pad_add_fusion.__.places), custom_call_target="tpu_custom_call" | custom-call | tf_op jit(solution)/shard_map/prepare/pallas_call | solution.py:379
  14.3 1.4 %ahead.2 = (bf16[48,128,128]{2,1,0:T(8,128)(2,1)S(1)}, f32[8,128]{1,0:T(8,128)S(1)}) custom-call(bf16[256,128,128]{2,1,0:T(8,128)(2,1)} %bitcast.24, bf16[512,128]{1,0:T(8,128)(2,1)S(1)} %get-tuple-element.25.refs_0_.target), custom_call_target="tpu_custom_call" | custom-call | tf_op jit(solution)/shard_map/ahead/pallas_call | solution.py:379
  15.7 3.1 %all-to-all-done.refs_0_.got = bf16[8,32,128]{2,1,0:T(8,128)(2,1)S(1)} async-done(((bf16[8,32,128]{2,1,0:T(8,128)(2,1)}), bf16[8,32,128]{2,1,0:T(8,128)(2,1)S(1)}, u32[]{:S(2)}, u32[]{:S(2)}) %all-to-all-start) | async-done | bytes 65568 | tf_op jit(solution)/shard_map/all_to_all | solution.py:389
  18.7 3.0 %fetch.2 = (bf16[208,128,128]{2,1,0:T(8,128)(2,1)S(1)}, f32[8,128]{1,0:T(8,128)S(1)}) custom-call(bf16[256,128,128]{2,1,0:T(8,128)(2,1)} %bitcast.25, bf16[8,32,128]{2,1,0:T(8,128)(2,1)S(1)} %all-to-all-done.refs_0_.got, f32[8,128]{1,0:T(8,128)S(1)} %get-tuple-element.27.refs_1_), custom_call_target="tpu_custom_call" | custom-call | tf_op jit(solution)/shard_map/fetch/pallas_call | solution.py:379
  21.8 0.1 collective-permute-start.3
  21.9 0.5 collective-permute-start
  22.4 0.9 %collective-permute-done.mate = bf16[256,128]{1,0:T(8,128)(2,1)S(1)} collective-permute-done((bf16[256,128]{1,0:T(8,128)(2,1)S(1)}, bf16[256,128]{1,0:T(8,128)(2,1)S(1)}, u32[]{:S(2)}, u32[]{:S(2)}) %collective-permute-start) | collective-permute-done | bytes 65568 | tf_op jit(solution)/shard_map/ppermute | solution.py:317
  23.3 4.6 %operator_one.1 = (f32[256,128]{1,0:T(8,128)S(1)}, bf16[256,128]{1,0:T(8,128)(2,1)S(1)}, bf16[8,48,128]{2,1,0:T(8,128)(2,1)}) custom-call(bf16[256,128]{1,0:T(8,128)(2,1)S(1)} %get-tuple-element.23.own, bf16[256,128]{1,0:T(8,128)(2,1)S(1)} %collective-permute-done.mate, bf16[256,128]{1,0:T(8,128)(2,1)S(1)} %collective-permute-done.1.even, ...), custom_call_target="tpu_custom_call" | custom-call | tf_op jit(solution)/shard_map/operator_one/pallas_call | solution.py:379
  27.9 3.4 %all-to-all-start.1 = ((bf16[8,48,128]{2,1,0:T(8,128)(2,1)}), bf16[8,48,128]{2,1,0:T(8,128)(2,1)S(1)}, u32[]{:S(2)}, u32[]{:S(2)}) async-start(bf16[8,48,128]{2,1,0:T(8,128)(2,1)} %get-tuple-element.36), calls=%async_computation.1 | async-start | bytes 196608 | tf_op jit(solution)/shard_map/all_to_all | solution.py:389
  31.3 1.9 %collective-permute-start.5 = (bf16[256,128]{1,0:T(8,128)(2,1)S(1)}, bf16[256,128]{1,0:T(8,128)(2,1)S(1)}, u32[]{:S(2)}, u32[]{:S(2)}) collective-permute-start(bf16[256,128]{1,0:T(8,128)(2,1)S(1)} %get-tuple-element.34.own), channel_id=1, source_target_pairs={{0,2},{1,3},{2,0},{3,1},{4,6},{5,7},{6,4},{7,5},{8,10},{9,11},{10,... | collective-permute-start | bytes 196616 | tf_op jit(solution)/shard_map/ppermute | solution.py:317
  33.2 3.3 %collective-permute-start.6 = (bf16[256,128]{1,0:T(8,128)(2,1)S(1)}, bf16[256,128]{1,0:T(8,128)(2,1)S(1)}, u32[]{:S(2)}, u32[]{:S(2)}) collective-permute-start(bf16[256,128]{1,0:T(8,128)(2,1)S(1)} %get-tuple-element.34.own), channel_id=1, source_target_pairs={{0,14},{1,15},{2,4},{3,5},{4,2},{5,3},{6,8},{7,9},{8,6},{9,7},{10,... | collective-permute-start | bytes 196616 | tf_op jit(solution)/shard_map/ppermute | solution.py:317
  36.5 1.4 %ahead.3 = (bf16[48,128,128]{2,1,0:T(8,128)(2,1)S(1)}, f32[8,128]{1,0:T(8,128)S(1)}) custom-call(bf16[256,128,128]{2,1,0:T(8,128)(2,1)} %bitcast.26, bf16[256,128]{1,0:T(8,128)(2,1)S(1)} %collective-permute-done.5.refs_0_.even), custom_call_target="tpu_custom_call" | custom-call | tf_op jit(solution)/shard_map/ahead/pallas_call | solution.py:379
  37.9 0.9 %all-to-all-done.1.refs_0_.got = bf16[8,48,128]{2,1,0:T(8,128)(2,1)S(1)} async-done(((bf16[8,48,128]{2,1,0:T(8,128)(2,1)}), bf16[8,48,128]{2,1,0:T(8,128)(2,1)S(1)}, u32[]{:S(2)}, u32[]{:S(2)}) %all-to-all-start.1) | async-done | bytes 98336 | tf_op jit(solution)/shard_map/all_to_all | solution.py:389
  38.8 3.0 %fetch.3 = (bf16[208,128,128]{2,1,0:T(8,128)(2,1)S(1)}, f32[8,128]{1,0:T(8,128)S(1)}) custom-call(bf16[256,128,128]{2,1,0:T(8,128)(2,1)} %bitcast.27, bf16[8,48,128]{2,1,0:T(8,128)(2,1)S(1)} %all-to-all-done.1.refs_0_.got, f32[8,128]{1,0:T(8,128)S(1)} %get-tuple-element.37.refs_1_), custom_call_target="tpu_custom_call" | custom-call | tf_op jit(solution)/shard_map/fetch/pallas_call | solution.py:379
  41.9 0.1 collective-permute-start.7
  42.0 0.5 collective-permute-start.4
  42.5 1.0 %collective-permute-done.4.mate = bf16[256,128]{1,0:T(8,128)(2,1)S(1)} collective-permute-done((bf16[256,128]{1,0:T(8,128)(2,1)S(1)}, bf16[256,128]{1,0:T(8,128)(2,1)S(1)}, u32[]{:S(2)}, u32[]{:S(2)}) %collective-permute-start.4) | collective-permute-done | bytes 65568 | tf_op jit(solution)/shard_map/ppermute | solution.py:317
  43.4 3.9 %operator_two.1 = (f32[256,128]{1,0:T(8,128)S(1)}, bf16[16,8,128]{2,1,0:T(8,128)(2,1)S(1)}) custom-call(bf16[256,128]{1,0:T(8,128)(2,1)S(1)} %get-tuple-element.34.own, bf16[256,128]{1,0:T(8,128)(2,1)S(1)} %collective-permute-done.4.mate, bf16[256,128]{1,0:T(8,128)(2,1)S(1)} %collective-permute-done.5.refs_0_.even, ...), custom_call_target="tpu_custom_call" | custom-call | tf_op jit(solution)/shard_map/operator_two/pallas_call | solution.py:379
  47.4 11.3 %all_to_all.15.got = bf16[16,8,128]{2,1,0:T(8,128)(2,1)S(1)} all-to-all(bf16[16,8,128]{2,1,0:T(8,128)(2,1)S(1)} %get-tuple-element.41), channel_id=1, replica_groups=mesh['groups'=2,'rows'=16] {'rows'}, dimensions={0} | all-to-all | bytes 65536 | tf_op jit(solution)/shard_map/all_to_all | solution.py:385
  58.7 1.5 %finish.1 = (f32[8,4096]{1,0:T(8,128)}, f32[8,4096]{1,0:T(8,128)}) custom-call(f32[256,128]{1,0:T(8,128)S(1)} %get-tuple-element.22.b, f32[256,128]{1,0:T(8,128)S(1)} %get-tuple-element.33.image, f32[256,128]{1,0:T(8,128)S(1)} %get-tuple-element.40.candidate, bf16[640,128]{1,0:T(8,128)(2,1)S(1)} %relay.3.sent, ...), custom_call_target="tpu_custom_call" | custom-call | tf_op jit(solution)/shard_map/finish/pallas_call | solution.py:379
  (10 shorter events, 0.1 us)
Async XLA Ops:
  2.5 19.3 %collective-permute-start.2 = (bf16[256,128]{1,0:T(8,128)(2,1)S(1)}, bf16[256,128]{1,0:T(8,128)(2,1)S(1)}, u32[]{:S(2)}, u32[]{:S(2)}) collective-permute-start(bf16[256,128]{1,0:T(8,128)(2,1)S(1)} %get-tuple-element.23.own), channel_id=1, source_target_pairs={{0,14},{1,15},{2,4},{3,5},{4,2},{5,3},{6,8},{7,9},{8,6},{9,7},{10,... | collective-permute-start | bytes 196616 | tf_op jit(solution)/shard_map/ppermute | solution.py:317
  8.5 13.2 %collective-permute-start.1 = (bf16[256,128]{1,0:T(8,128)(2,1)S(1)}, bf16[256,128]{1,0:T(8,128)(2,1)S(1)}, u32[]{:S(2)}, u32[]{:S(2)}) collective-permute-start(bf16[256,128]{1,0:T(8,128)(2,1)S(1)} %get-tuple-element.23.own), channel_id=1, source_target_pairs={{0,2},{1,3},{2,0},{3,1},{4,6},{5,7},{6,4},{7,5},{8,10},{9,11},{10,... | collective-permute-start | bytes 196616 | tf_op jit(solution)/shard_map/ppermute | solution.py:317
  8.5 10.2 %all-to-all-start = ((bf16[8,32,128]{2,1,0:T(8,128)(2,1)}), bf16[8,32,128]{2,1,0:T(8,128)(2,1)S(1)}, u32[]{:S(2)}, u32[]{:S(2)}) async-start(bf16[8,32,128]{2,1,0:T(8,128)(2,1)} %get-tuple-element.24._), calls=%async_computation | async-start | bytes 131072 | tf_op jit(solution)/shard_map/all_to_all | solution.py:389
  21.8 1.5 %collective-permute-start.3 = (bf16[512,128]{1,0:T(8,128)(2,1)S(1)}, bf16[512,128]{1,0:T(8,128)(2,1)S(1)}, u32[]{:S(2)}, u32[]{:S(2)}) collective-permute-start(bf16[512,128]{1,0:T(8,128)(2,1)S(1)} %relay.2.sent), channel_id=1, source_target_pairs={{0,1},{1,0},{2,3},{3,2},{4,5},{5,4},{6,7},{7,6},{8,9},{9,8},{10,11... | collective-permute-start | bytes 393224 | tf_op jit(solution)/shard_map/ppermute | solution.py:317
  21.9 1.4 %collective-permute-start = (bf16[256,128]{1,0:T(8,128)(2,1)S(1)}, bf16[256,128]{1,0:T(8,128)(2,1)S(1)}, u32[]{:S(2)}, u32[]{:S(2)}) collective-permute-start(bf16[256,128]{1,0:T(8,128)(2,1)S(1)} %get-tuple-element.23.own), channel_id=1, source_target_pairs={{0,1},{1,0},{2,3},{3,2},{4,5},{5,4},{6,7},{7,6},{8,9},{9,8},{10,11... | collective-permute-start | bytes 196616 | tf_op jit(solution)/shard_map/ppermute | solution.py:317
  27.9 10.9 %all-to-all-start.1 = ((bf16[8,48,128]{2,1,0:T(8,128)(2,1)}), bf16[8,48,128]{2,1,0:T(8,128)(2,1)S(1)}, u32[]{:S(2)}, u32[]{:S(2)}) async-start(bf16[8,48,128]{2,1,0:T(8,128)(2,1)} %get-tuple-element.36), calls=%async_computation.1 | async-start | bytes 196608 | tf_op jit(solution)/shard_map/all_to_all | solution.py:389
  31.3 5.2 %collective-permute-start.5 = (bf16[256,128]{1,0:T(8,128)(2,1)S(1)}, bf16[256,128]{1,0:T(8,128)(2,1)S(1)}, u32[]{:S(2)}, u32[]{:S(2)}) collective-permute-start(bf16[256,128]{1,0:T(8,128)(2,1)S(1)} %get-tuple-element.34.own), channel_id=1, source_target_pairs={{0,2},{1,3},{2,0},{3,1},{4,6},{5,7},{6,4},{7,5},{8,10},{9,11},{10,... | collective-permute-start | bytes 196616 | tf_op jit(solution)/shard_map/ppermute | solution.py:317
  33.2 8.6 %collective-permute-start.6 = (bf16[256,128]{1,0:T(8,128)(2,1)S(1)}, bf16[256,128]{1,0:T(8,128)(2,1)S(1)}, u32[]{:S(2)}, u32[]{:S(2)}) collective-permute-start(bf16[256,128]{1,0:T(8,128)(2,1)S(1)} %get-tuple-element.34.own), channel_id=1, source_target_pairs={{0,14},{1,15},{2,4},{3,5},{4,2},{5,3},{6,8},{7,9},{8,6},{9,7},{10,... | collective-permute-start | bytes 196616 | tf_op jit(solution)/shard_map/ppermute | solution.py:317
  41.9 1.6 %collective-permute-start.7 = (bf16[640,128]{1,0:T(8,128)(2,1)S(1)}, bf16[640,128]{1,0:T(8,128)(2,1)S(1)}, u32[]{:S(2)}, u32[]{:S(2)}) collective-permute-start(bf16[640,128]{1,0:T(8,128)(2,1)S(1)} %relay.3.sent), channel_id=1, source_target_pairs={{0,1},{1,0},{2,3},{3,2},{4,5},{5,4},{6,7},{7,6},{8,9},{9,8},{10,11... | collective-permute-start | bytes 491528 | tf_op jit(solution)/shard_map/ppermute | solution.py:317
  42.0 1.5 %collective-permute-start.4 = (bf16[256,128]{1,0:T(8,128)(2,1)S(1)}, bf16[256,128]{1,0:T(8,128)(2,1)S(1)}, u32[]{:S(2)}, u32[]{:S(2)}) collective-permute-start(bf16[256,128]{1,0:T(8,128)(2,1)S(1)} %get-tuple-element.34.own), channel_id=1, source_target_pairs={{0,1},{1,0},{2,3},{3,2},{4,5},{5,4},{6,7},{7,6},{8,9},{9,8},{10,11... | collective-permute-start | bytes 196616 | tf_op jit(solution)/shard_map/ppermute | solution.py:317

commit v14 on v13

--- a/solution.py
+++ b/solution.py
@@ -82,8 +82,7 @@
 def write_payload(payload, tiles, sums, basis, per_group):
     groups = len(tiles) // per_group
     parts = [compress(tiles[g * per_group : (g + 1) * per_group], basis, g) for g in range(groups)]
-    if sums:
-        parts += [sums_tile(sums), jnp.zeros((TAIL - R, LANES), f32)]
+    parts += [sums_tile(sums), jnp.zeros((TAIL - R, LANES), f32)]
     block = jnp.concatenate(parts, axis=0).astype(bf16)
     for device in range(payload.shape[0]):
         payload[device] = block
@@ -105,14 +104,17 @@
     write_payload(payload, tiles, [], basis, per_group)
 
 
-def prepare_kernel(coupling_hbm, target_hbm, _, __, high_out, low_out, target_out, coupling, target, sems):
+def prepare_kernel(
+    coupling_hbm, target_hbm, blocks_hbm, _, __, high_out, low_out, target_out, ahead, coupling, target, sems
+):
     copies = [
         pltpu.make_async_copy(coupling_hbm, coupling, sems.at[0]),
         pltpu.make_async_copy(target_hbm, target, sems.at[1]),
+        pltpu.make_async_copy(blocks_hbm.at[pl.ds(0, ahead.shape[0])], ahead, sems.at[2]),
     ]
     for copy in copies:
         copy.start()
-    for copy in copies:
+    for copy in copies[:2]:
         copy.wait()
     slots, rank, _, clusters = coupling.shape
     per_tile = LANES // clusters
@@ -129,6 +131,7 @@
     column = lax.broadcasted_iota(jnp.int32, (size, size), 1)
     wanted = (row % clusters) * rank + row // clusters
     target_out[...] = dot((column == wanted).astype(bf16), target[...]).astype(bf16)
+    copies[2].wait()
 
 
 def fetch_kernel(first, blocks_hbm, *refs):
@@ -238,7 +241,7 @@
 ):
     clusters = near.shape[0] // R
     slabs, swaps = (own, mate, even, odd), (sent, received)
-    each = clusters // per_group * R
+    each = clusters // per_group * R + TAIL
     apply(per_group, each, slabs, places, ahead, blocks, swaps, high, low, target, near, far, window, table)
     tiles = []
     sums = [jnp.zeros((R, LANES), f32) for _ in range(3)]
@@ -285,16 +288,21 @@
         made = (0.5 * held + (rows_of(near, j) + rows_of(far, j)) * scale - h11 * held) * inverse
         sums = [s + v * made for s, v in zip(sums, (first, second, made))]
         candidate[pl.ds(j * R, R), :] = made
-    tile = sums_tile(sums).astype(bf16)
-    for device in range(sums_out.shape[0]):
-        sums_out[device] = tile
-
-
-def finish_kernel(per_group, unknowns, b, image, candidate, sent, received, got, solution_out, next_out):
+    lane = lane_ids()
+    tile = jnp.zeros((R, LANES), f32)
+    for t, partial in enumerate(sums):
+        tile = jnp.where(lane == t, jnp.sum(partial, axis=1, keepdims=True), tile)
+    sums_out[...] = tile
+
+
+def finish_kernel(
+    per_group, unknowns, b, image, candidate, sent, received, total, total_mate, solution_out, next_out
+):
     clusters = b.shape[0] // R
     sums = read_sums(tails((sent, received), b.shape[0], clusters // per_group * R), 3, unknowns)
     start_norm, h11, h21, v11, v22, v12 = arnoldi_one(*sums)
-    h12, h22, ww = read_sums([got[device] for device in range(got.shape[0])], 3, unknowns)
+    totals = total[...] + total_mate[...]
+    h12, h22, ww = [totals[:, t : t + 1] * (1.0 / unknowns) for t in range(3)]
     uu = ww - 2.0 * (h12 * h12 + h22 * h22) + h12 * h12 * v11 + h22 * h22 * v22 + 2.0 * h12 * h22 * v12
     h32 = jnp.sqrt(jnp.maximum(uu, 0.0) + epsilon)
     g11 = h11 * h11 + h21 * h21
@@ -381,9 +389,6 @@
             scratch_shapes=scratch_shapes, compiler_params=PARAMS, name=name,
         )(*args)
 
-    def exchange(block):
-        return lax.all_to_all(block, "rows", 0, 0)
-
     def gather(block):
         groups = [list(range(core, size, 2)) for core in range(2)]
         return lax.all_to_all(block, "rows", 0, 0, axis_index_groups=groups)
@@ -392,7 +397,7 @@
         functools.partial(start_kernel, per_group), "start",
         (
             shape(rows, LANES), shape(clusters * rank, LANES, dtype=bf16), shape(rows, LANES, dtype=bf16),
-            shape(size // 2, head, LANES, dtype=bf16),
+            shape(size // 2, head + TAIL, LANES, dtype=bf16),
         ),
         [HBM] * 2, in_hbm(right_sides), in_hbm(basis_in.reshape(clusters * rank, LANES)),
         scratch_shapes=[scratch(R, width), pltpu.SemaphoreType.DMA((2,))],
@@ -409,25 +414,24 @@
     other_core = (owner % 2) ^ (lax.axis_index("rows") % 2)
     far_index = (other_core * (size // 2) + owner // 2) * clusters + far_cols.T % clusters
     places = jnp.concatenate([placed, far_index], axis=0)
-    high, low, target = call(
+    blocks = in_hbm(near_blocks.reshape(clusters * slots, LANES, LANES))
+    early = blocks.shape[0] // 4
+    high, low, target, ahead = call(
         prepare_kernel, "prepare",
         (
             shape(slots * rank, rank * clusters, dtype=bf16),
             shape(slots * rank, rank * clusters, dtype=bf16),
             shape(rank * clusters, LANES, dtype=bf16),
+            pltpu.VMEM((early, LANES, LANES), bf16),
         ),
-        [HBM] * 2 + [ANY] * 2,
+        [HBM] * 3 + [ANY] * 2,
         in_hbm(jnp.transpose(coupling, (1, 2, 3, 0))), in_hbm(target_basis.reshape(clusters * rank, LANES)),
-        payload, places,
+        blocks, payload, places,
         scratch_shapes=[
             scratch(slots, rank, rank, clusters), scratch(clusters * rank, LANES, dtype=bf16),
-            pltpu.SemaphoreType.DMA((2,)),
+            pltpu.SemaphoreType.DMA((3,)),
         ],
     )
-    blocks = in_hbm(near_blocks.reshape(clusters * slots, LANES, LANES))
-
-
-    early = blocks.shape[0] * 3 // 16
 
     def fetch(name, first, count, chunks, *behind):
         here, token = call(
@@ -436,15 +440,15 @@
         )
         return pltpu.with_memory_space_constraint(here, pltpu.VMEM), token
 
-    def arrived(got, held, made):
-        ahead, token = fetch("ahead", 0, early, 2, made)
-        near_blocks_here, token = fetch("fetch", early, blocks.shape[0] - early, 8, got, token)
+    def arrived(got, held, ahead, behind):
+        rest, token = fetch("fetch", early, blocks.shape[0] - early, 8, got, behind)
         sent = call(
             functools.partial(relay_kernel, "rows"), "relay",
             shape(got.shape[0] * got.shape[1] + rows, LANES, dtype=bf16), [VMEM] * 3 + [ANY], got, *held[2:], token
         )
-        return *held, places, ahead, near_blocks_here, sent, swapped(sent, core_mate), high, low, target
-
+        return *held, places, ahead, rest, sent, swapped(sent, core_mate), high, low, target
+
+    ahead = pltpu.with_memory_space_constraint(ahead, pltpu.VMEM)
     kept = [scratch(rows, LANES), scratch(rows, LANES), scratch(5 * rows + R, LANES), scratch(size * head, LANES)]
     operands = [VMEM] * 4 + [SMEM] + [VMEM] * 9
     image, lowered, payload = call(
@@ -453,18 +457,22 @@
             shape(rows, LANES), shape(rows, LANES, dtype=bf16),
             shape(size // 2, head + TAIL, LANES, dtype=bf16),
         ),
-        operands, *arrived(got, held, target), field, basis, scratch_shapes=kept,
-    )
-    held = sends_of(lowered)
-    here = arrived(gather(payload), held, held[2])
+        operands, *arrived(got, held, ahead, target), field, basis, scratch_shapes=kept,
+    )
+    got = gather(payload)
+    ahead, token = fetch("ahead", 0, early, 2, payload)
+    here = arrived(got, sends_of(lowered), ahead, token)
     candidate, sums = call(
         functools.partial(second_kernel, per_group, unknowns), "operator_two",
-        (shape(rows, LANES), shape(size, R, LANES, dtype=bf16)),
+        (shape(rows, LANES), shape(R, LANES)),
         operands, *here, field, image, scratch_shapes=kept,
     )
+    *steps, last = [1 << n for n in range((size - 1).bit_length())]
+    for step in steps:
+        sums = sums + swapped(sums, lambda i: i ^ step)
     return call(
         functools.partial(finish_kernel, per_group, unknowns), "finish", (shape(R, width), shape(R, width)),
-        [VMEM] * 6, field, image, candidate, *here[7:9], exchange(sums),
+        [VMEM] * 7, field, image, candidate, *here[7:9], sums, swapped(sums, lambda i: i ^ last),
     )
 
 

time: 60.6 us -> 62.4 us (1.030)
  waiting for transfers between devices: 5.86 us -> 19.6 us
  blocking collectives: 11.3 us -> 0 us
  Pallas kernels: 22.3 us -> 21.2 us
    ppermute x8 -> x12, waiting for transfers between devices: 1.92 us -> 13.7 us  [swapped(): lax.ppermute(block, 'rows', [(i, partner(i)) for i in range(lax.axis_size...]
    all_to_all x1 -> x0, blocking collectives: 11.3 us -> none  [exchange(): return lax.all_to_all(block, 'rows', 0, 0)]
    all_to_all x2, waiting for transfers between devices: 3.94 us -> 5.81 us  [gather(): return lax.all_to_all(block, 'rows', 0, 0, axis_index_groups=groups)]
    pallas_call x11 -> x10, Pallas kernels: 22.3 us -> 21.2 us  [call(): pl.pallas_call(kernel, out_shape=out, in_specs=ins, out_specs=jax.tree.ma...]
    ppermute x8 -> x12, starting transfers between devices: 12.4 us -> 13 us  [swapped(): lax.ppermute(block, 'rows', [(i, partner(i)) for i in range(lax.axis_size...]
  transfers between devices with their start and end apart: 10 -> 14, of which waited for: 4 -> 8; matrix products, arithmetic and copies ran while one was open for 1% -> 1% of each run, Pallas kernels for 17% -> 15%
where the time goes in v14:
time: 62.4 us; the launch traced here: 62 us
  Pallas kernels  21.2 us (34%)
  starting transfers between devices  19.7 us (32%)
  waiting for transfers between devices  19.6 us (31%)
  between operations  0.81 us (1%)
  other arithmetic  0.76 us (1%)
    pallas_call x10, Pallas kernels, call(): pl.pallas_call(kernel, out_shape=out, in_specs=ins, out_specs=jax.tree.ma...  21.2 us
    ppermute x12, waiting for transfers between devices, swapped(): lax.ppermute(block, 'rows', [(i, partner(i)) for i in range(lax.axis_size...  13.7 us
    ppermute x12, starting transfers between devices, swapped(): lax.ppermute(block, 'rows', [(i, partner(i)) for i in range(lax.axis_size...  13 us
    all_to_all x2, starting transfers between devices, gather(): return lax.all_to_all(block, 'rows', 0, 0, axis_index_groups=groups)  6.72 us
    all_to_all x2, waiting for transfers between devices, gather(): return lax.all_to_all(block, 'rows', 0, 0, axis_index_groups=groups)  5.81 us
  transfers between devices with their start and end apart: 14, of which 8 were waited for; matrix products, arithmetic and copies ran while one was open for 1% of the time, Pallas kernels for 15%

profile of v14, /device:TPU:0, one launch (start us, length us, event | category | flops | bytes accessed | tf_op | source)
XLA Modules:
  0.0 62.0 jit_solution(15050004557813007811)
XLA Ops:
  0.6 1.8 %start.1 = (f32[256,128]{1,0:T(8,128)S(1)}, bf16[512,128]{1,0:T(8,128)(2,1)S(1)}, bf16[256,128]{1,0:T(8,128)(2,1)S(1)}, bf16[8,48,128]{2,1,0:T(8,128)(2,1)}) custom-call(f32[8,4096]{1,0:T(8,128)} %b_hbm.1, bf16[512,128]{1,0:T(8,128)(2,1)} %bitcast.30), custom_call_target="tpu_custom_call" | custom-call | tf_op jit(solution)/shard_map/start/pallas_call | solution.py:387
  2.5 6.1 %collective-permute-start.2 = (bf16[256,128]{1,0:T(8,128)(2,1)S(1)}, bf16[256,128]{1,0:T(8,128)(2,1)S(1)}, u32[]{:S(2)}, u32[]{:S(2)}) collective-permute-start(bf16[256,128]{1,0:T(8,128)(2,1)S(1)} %get-tuple-element.22.own), channel_id=1, source_target_pairs={{0,14},{1,15},{2,4},{3,5},{4,2},{5,3},{6,8},{7,9},{8,6},{9,7},{10,... | collective-permute-start | bytes 196616 | tf_op jit(solution)/shard_map/ppermute | solution.py:325
  8.6 3.4 %all-to-all-start = ((bf16[8,48,128]{2,1,0:T(8,128)(2,1)}), bf16[8,48,128]{2,1,0:T(8,128)(2,1)S(1)}, u32[]{:S(2)}, u32[]{:S(2)}) async-start(bf16[8,48,128]{2,1,0:T(8,128)(2,1)} %get-tuple-element.23._), calls=%async_computation | async-start | bytes 196608 | tf_op jit(solution)/shard_map/all_to_all | solution.py:394
  12.0 0.7 %fusion.2 = (s32[8,32]{1,0:T(8,128)S(1)}, s32[8,32]{1,0:T(8,128)S(1)}) fusion(s32[32,8]{0,1:T(8,128)} %param.10, s32[]{:T(128)S(6)} %sub.32, s32[]{:T(128)S(6)} %select_n.83, s32[]{:T(128)S(6)} %select_n.82, s32[]{:T(128)S(6)} %add.66, s32[]{:T(128)S(6)} %mul.15, s32[32]{0:T(128)} %param.11, s32[]{:T(128)S(6)} %select_n.81, s32[32,8]{0,1:T(8,128)} %param.15), kind=kLoop, calls=%fused_computation.21 | loop fusion | flops 22784 | bytes 4248 | tf_op jit(solution)/shard_map/jit(_where)/select_n | solution.py:412
  12.7 2.0 %prepare.1 = (bf16[128,512]{1,0:T(8,128)(2,1)S(1)}, bf16[128,512]{1,0:T(8,128)(2,1)S(1)}, bf16[512,128]{1,0:T(8,128)(2,1)S(1)}, bf16[64,128,128]{2,1,0:T(8,128)(2,1)S(1)}) custom-call(f32[8,16,16,32]{3,2,1,0:T(8,128)} %bitcast.28, bf16[512,128]{1,0:T(8,128)(2,1)} %bitcast.29, bf16[256,128,128]{2,1,0:T(8,128)(2,1)} %bitcast.24, ...), custom_call_target="tpu_custom_call" | custom-call | tf_op jit(solution)/shard_map/prepare/pallas_call | solution.py:387
  14.7 4.3 %all-to-all-done.refs_0_.got = bf16[8,48,128]{2,1,0:T(8,128)(2,1)S(1)} async-done(((bf16[8,48,128]{2,1,0:T(8,128)(2,1)}), bf16[8,48,128]{2,1,0:T(8,128)(2,1)S(1)}, u32[]{:S(2)}, u32[]{:S(2)}) %all-to-all-start) | async-done | bytes 98336 | tf_op jit(solution)/shard_map/all_to_all | solution.py:394
  19.0 2.9 %fetch.2 = (bf16[192,128,128]{2,1,0:T(8,128)(2,1)S(1)}, f32[8,128]{1,0:T(8,128)S(1)}) custom-call(bf16[256,128,128]{2,1,0:T(8,128)(2,1)} %bitcast.25, bf16[8,48,128]{2,1,0:T(8,128)(2,1)S(1)} %all-to-all-done.refs_0_.got, bf16[512,128]{1,0:T(8,128)(2,1)S(1)} %get-tuple-element.25.refs_1_.target), custom_call_target="tpu_custom_call" | custom-call | tf_op jit(solution)/shard_map/fetch/pallas_call | solution.py:387
  22.0 0.5 collective-permute-start
  22.5 1.0 %collective-permute-done.mate = bf16[256,128]{1,0:T(8,128)(2,1)S(1)} collective-permute-done((bf16[256,128]{1,0:T(8,128)(2,1)S(1)}, bf16[256,128]{1,0:T(8,128)(2,1)S(1)}, u32[]{:S(2)}, u32[]{:S(2)}) %collective-permute-start) | collective-permute-done | bytes 65568 | tf_op jit(solution)/shard_map/ppermute | solution.py:325
  23.5 4.6 %operator_one.1 = (f32[256,128]{1,0:T(8,128)S(1)}, bf16[256,128]{1,0:T(8,128)(2,1)S(1)}, bf16[8,48,128]{2,1,0:T(8,128)(2,1)}) custom-call(bf16[256,128]{1,0:T(8,128)(2,1)S(1)} %get-tuple-element.22.own, bf16[256,128]{1,0:T(8,128)(2,1)S(1)} %collective-permute-done.mate, bf16[256,128]{1,0:T(8,128)(2,1)S(1)} %collective-permute-done.1.even, ...), custom_call_target="tpu_custom_call" | custom-call | tf_op jit(solution)/shard_map/operator_one/pallas_call | solution.py:387
  28.1 3.4 %all-to-all-start.1 = ((bf16[8,48,128]{2,1,0:T(8,128)(2,1)}), bf16[8,48,128]{2,1,0:T(8,128)(2,1)S(1)}, u32[]{:S(2)}, u32[]{:S(2)}) async-start(bf16[8,48,128]{2,1,0:T(8,128)(2,1)} %get-tuple-element.33.refs_0_), calls=%async_computation.1 | async-start | bytes 196608 | tf_op jit(solution)/shard_map/all_to_all | solution.py:394
  31.4 4.7 %collective-permute-start.6 = (bf16[256,128]{1,0:T(8,128)(2,1)S(1)}, bf16[256,128]{1,0:T(8,128)(2,1)S(1)}, u32[]{:S(2)}, u32[]{:S(2)}) collective-permute-start(bf16[256,128]{1,0:T(8,128)(2,1)S(1)} %get-tuple-element.32.own), channel_id=1, source_target_pairs={{0,14},{1,15},{2,4},{3,5},{4,2},{5,3},{6,8},{7,9},{8,6},{9,7},{10,... | collective-permute-start | bytes 196616 | tf_op jit(solution)/shard_map/ppermute | solution.py:325
  36.1 1.6 %ahead.1 = (bf16[64,128,128]{2,1,0:T(8,128)(2,1)S(1)}, f32[8,128]{1,0:T(8,128)S(1)}) custom-call(bf16[256,128,128]{2,1,0:T(8,128)(2,1)} %bitcast.26, bf16[8,48,128]{2,1,0:T(8,128)(2,1)} %get-tuple-element.33.refs_0_), custom_call_target="tpu_custom_call" | custom-call | tf_op jit(solution)/shard_map/ahead/pallas_call | solution.py:387
  37.7 1.5 %all-to-all-done.1.refs_0_.got = bf16[8,48,128]{2,1,0:T(8,128)(2,1)S(1)} async-done(((bf16[8,48,128]{2,1,0:T(8,128)(2,1)}), bf16[8,48,128]{2,1,0:T(8,128)(2,1)S(1)}, u32[]{:S(2)}, u32[]{:S(2)}) %all-to-all-start.1) | async-done | bytes 98336 | tf_op jit(solution)/shard_map/all_to_all | solution.py:394
  39.2 2.9 %fetch.3 = (bf16[192,128,128]{2,1,0:T(8,128)(2,1)S(1)}, f32[8,128]{1,0:T(8,128)S(1)}) custom-call(bf16[256,128,128]{2,1,0:T(8,128)(2,1)} %bitcast.27, bf16[8,48,128]{2,1,0:T(8,128)(2,1)S(1)} %all-to-all-done.1.refs_0_.got, f32[8,128]{1,0:T(8,128)S(1)} %get-tuple-element.35.refs_1_), custom_call_target="tpu_custom_call" | custom-call | tf_op jit(solution)/shard_map/fetch/pallas_call | solution.py:387
  42.2 0.5 collective-permute-start.4
  42.7 1.0 %collective-permute-done.4.mate = bf16[256,128]{1,0:T(8,128)(2,1)S(1)} collective-permute-done((bf16[256,128]{1,0:T(8,128)(2,1)S(1)}, bf16[256,128]{1,0:T(8,128)(2,1)S(1)}, u32[]{:S(2)}, u32[]{:S(2)}) %collective-permute-start.4) | collective-permute-done | bytes 65568 | tf_op jit(solution)/shard_map/ppermute | solution.py:325
  43.7 3.9 %operator_two.1 = (f32[256,128]{1,0:T(8,128)S(1)}, f32[8,128]{1,0:T(8,128)S(1)}) custom-call(bf16[256,128]{1,0:T(8,128)(2,1)S(1)} %get-tuple-element.32.own, bf16[256,128]{1,0:T(8,128)(2,1)S(1)} %collective-permute-done.4.mate, bf16[256,128]{1,0:T(8,128)(2,1)S(1)} %collective-permute-done.5.even, bf16[256,128]{1,0:T(8,128)(2,1)S(1)} %collective-permute-done.6.odd, ...), custom_call_target="tpu_custom_call" | custom-call | tf_op jit(solution)/shard_map/operator_two/pallas_call | solution.py:387
  47.9 0.9 %collective-permute-done.8 = f32[8,128]{1,0:T(8,128)S(1)} collective-permute-done((f32[8,128]{1,0:T(8,128)S(1)}, f32[8,128]{1,0:T(8,128)S(1)}, u32[]{:S(2)}, u32[]{:S(2)}) %collective-permute-start.8) | collective-permute-done | bytes 4128 | tf_op jit(solution)/shard_map/ppermute | solution.py:325
  48.8 0.5 collective-permute-start.9
  49.3 3.1 %collective-permute-done.9 = f32[8,128]{1,0:T(8,128)S(1)} collective-permute-done((f32[8,128]{1,0:T(8,128)S(1)}, f32[8,128]{1,0:T(8,128)S(1)}, u32[]{:S(2)}, u32[]{:S(2)}) %collective-permute-start.9) | collective-permute-done | bytes 4128 | tf_op jit(solution)/shard_map/ppermute | solution.py:325
  52.4 3.6 %collective-permute-done.10 = f32[8,128]{1,0:T(8,128)S(1)} collective-permute-done((f32[8,128]{1,0:T(8,128)S(1)}, f32[8,128]{1,0:T(8,128)S(1)}, u32[]{:S(2)}, u32[]{:S(2)}) %collective-permute-start.10) | collective-permute-done | bytes 4128 | tf_op jit(solution)/shard_map/ppermute | solution.py:325
  56.4 4.2 %collective-permute-done.11.total_mate = f32[8,128]{1,0:T(8,128)S(1)} collective-permute-done((f32[8,128]{1,0:T(8,128)S(1)}, f32[8,128]{1,0:T(8,128)S(1)}, u32[]{:S(2)}, u32[]{:S(2)}) %collective-permute-start.11) | collective-permute-done | bytes 4128 | tf_op jit(solution)/shard_map/ppermute | solution.py:325
  60.5 1.5 %finish.1 = (f32[8,4096]{1,0:T(8,128)}, f32[8,4096]{1,0:T(8,128)}) custom-call(f32[256,128]{1,0:T(8,128)S(1)} %get-tuple-element.21.b, f32[256,128]{1,0:T(8,128)S(1)} %get-tuple-element.31.image, f32[256,128]{1,0:T(8,128)S(1)} %get-tuple-element.38.candidate, bf16[640,128]{1,0:T(8,128)(2,1)S(1)} %relay.3.sent, ...), custom_call_target="tpu_custom_call" | custom-call | tf_op jit(solution)/shard_map/finish/pallas_call | solution.py:387
  (19 shorter events, 0.9 us)
Async XLA Ops:
  2.5 19.4 %collective-permute-start.2 = (bf16[256,128]{1,0:T(8,128)(2,1)S(1)}, bf16[256,128]{1,0:T(8,128)(2,1)S(1)}, u32[]{:S(2)}, u32[]{:S(2)}) collective-permute-start(bf16[256,128]{1,0:T(8,128)(2,1)S(1)} %get-tuple-element.22.own), channel_id=1, source_target_pairs={{0,14},{1,15},{2,4},{3,5},{4,2},{5,3},{6,8},{7,9},{8,6},{9,7},{10,... | collective-permute-start | bytes 196616 | tf_op jit(solution)/shard_map/ppermute | solution.py:325
  8.6 13.3 %collective-permute-start.1 = (bf16[256,128]{1,0:T(8,128)(2,1)S(1)}, bf16[256,128]{1,0:T(8,128)(2,1)S(1)}, u32[]{:S(2)}, u32[]{:S(2)}) collective-permute-start(bf16[256,128]{1,0:T(8,128)(2,1)S(1)} %get-tuple-element.22.own), channel_id=1, source_target_pairs={{0,2},{1,3},{2,0},{3,1},{4,6},{5,7},{6,4},{7,5},{8,10},{9,11},{10,... | collective-permute-start | bytes 196616 | tf_op jit(solution)/shard_map/ppermute | solution.py:325
  8.6 10.4 %all-to-all-start = ((bf16[8,48,128]{2,1,0:T(8,128)(2,1)}), bf16[8,48,128]{2,1,0:T(8,128)(2,1)S(1)}, u32[]{:S(2)}, u32[]{:S(2)}) async-start(bf16[8,48,128]{2,1,0:T(8,128)(2,1)} %get-tuple-element.23._), calls=%async_computation | async-start | bytes 196608 | tf_op jit(solution)/shard_map/all_to_all | solution.py:394
  21.9 1.6 %collective-permute-start.3 = (bf16[640,128]{1,0:T(8,128)(2,1)S(1)}, bf16[640,128]{1,0:T(8,128)(2,1)S(1)}, u32[]{:S(2)}, u32[]{:S(2)}) collective-permute-start(bf16[640,128]{1,0:T(8,128)(2,1)S(1)} %relay.2.sent), channel_id=1, source_target_pairs={{0,1},{1,0},{2,3},{3,2},{4,5},{5,4},{6,7},{7,6},{8,9},{9,8},{10,11... | collective-permute-start | bytes 491528 | tf_op jit(solution)/shard_map/ppermute | solution.py:325
  22.0 1.5 %collective-permute-start = (bf16[256,128]{1,0:T(8,128)(2,1)S(1)}, bf16[256,128]{1,0:T(8,128)(2,1)S(1)}, u32[]{:S(2)}, u32[]{:S(2)}) collective-permute-start(bf16[256,128]{1,0:T(8,128)(2,1)S(1)} %get-tuple-element.22.own), channel_id=1, source_target_pairs={{0,1},{1,0},{2,3},{3,2},{4,5},{5,4},{6,7},{7,6},{8,9},{9,8},{10,11... | collective-permute-start | bytes 196616 | tf_op jit(solution)/shard_map/ppermute | solution.py:325
  28.1 11.1 %all-to-all-start.1 = ((bf16[8,48,128]{2,1,0:T(8,128)(2,1)}), bf16[8,48,128]{2,1,0:T(8,128)(2,1)S(1)}, u32[]{:S(2)}, u32[]{:S(2)}) async-start(bf16[8,48,128]{2,1,0:T(8,128)(2,1)} %get-tuple-element.33.refs_0_), calls=%async_computation.1 | async-start | bytes 196608 | tf_op jit(solution)/shard_map/all_to_all | solution.py:394
  31.4 10.6 %collective-permute-start.6 = (bf16[256,128]{1,0:T(8,128)(2,1)S(1)}, bf16[256,128]{1,0:T(8,128)(2,1)S(1)}, u32[]{:S(2)}, u32[]{:S(2)}) collective-permute-start(bf16[256,128]{1,0:T(8,128)(2,1)S(1)} %get-tuple-element.32.own), channel_id=1, source_target_pairs={{0,14},{1,15},{2,4},{3,5},{4,2},{5,3},{6,8},{7,9},{8,6},{9,7},{10,... | collective-permute-start | bytes 196616 | tf_op jit(solution)/shard_map/ppermute | solution.py:325
  36.1 6.0 %collective-permute-start.5 = (bf16[256,128]{1,0:T(8,128)(2,1)S(1)}, bf16[256,128]{1,0:T(8,128)(2,1)S(1)}, u32[]{:S(2)}, u32[]{:S(2)}) collective-permute-start(bf16[256,128]{1,0:T(8,128)(2,1)S(1)} %get-tuple-element.32.own), channel_id=1, source_target_pairs={{0,2},{1,3},{2,0},{3,1},{4,6},{5,7},{6,4},{7,5},{8,10},{9,11},{10,... | collective-permute-start | bytes 196616 | tf_op jit(solution)/shard_map/ppermute | solution.py:325
  42.1 1.6 %collective-permute-start.7 = (bf16[640,128]{1,0:T(8,128)(2,1)S(1)}, bf16[640,128]{1,0:T(8,128)(2,1)S(1)}, u32[]{:S(2)}, u32[]{:S(2)}) collective-permute-start(bf16[640,128]{1,0:T(8,128)(2,1)S(1)} %relay.3.sent), channel_id=1, source_target_pairs={{0,1},{1,0},{2,3},{3,2},{4,5},{5,4},{6,7},{7,6},{8,9},{9,8},{10,11... | collective-permute-start | bytes 491528 | tf_op jit(solution)/shard_map/ppermute | solution.py:325
  42.2 1.5 %collective-permute-start.4 = (bf16[256,128]{1,0:T(8,128)(2,1)S(1)}, bf16[256,128]{1,0:T(8,128)(2,1)S(1)}, u32[]{:S(2)}, u32[]{:S(2)}) collective-permute-start(bf16[256,128]{1,0:T(8,128)(2,1)S(1)} %get-tuple-element.32.own), channel_id=1, source_target_pairs={{0,1},{1,0},{2,3},{3,2},{4,5},{5,4},{6,7},{7,6},{8,9},{9,8},{10,11... | collective-permute-start | bytes 196616 | tf_op jit(solution)/shard_map/ppermute | solution.py:325
  47.6 1.2 %collective-permute-start.8 = (f32[8,128]{1,0:T(8,128)S(1)}, f32[8,128]{1,0:T(8,128)S(1)}, u32[]{:S(2)}, u32[]{:S(2)}) collective-permute-start(f32[8,128]{1,0:T(8,128)S(1)} %get-tuple-element.39), channel_id=1, source_target_pairs={{0,1},{1,0},{2,3},{3,2},{4,5},{5,4},{6,7},{7,6},{8,9},{9,8},{10,11... | collective-permute-start | bytes 12296 | tf_op jit(solution)/shard_map/ppermute | solution.py:325
  48.8 3.6 %collective-permute-start.9 = (f32[8,128]{1,0:T(8,128)S(1)}, f32[8,128]{1,0:T(8,128)S(1)}, u32[]{:S(2)}, u32[]{:S(2)}) collective-permute-start(f32[8,128]{1,0:T(8,128)S(1)} %add.74), channel_id=1, source_target_pairs={{0,2},{1,3},{2,0},{3,1},{4,6},{5,7},{6,4},{7,5},{8,10},{9,11},{10,... | collective-permute-start | bytes 12296 | tf_op jit(solution)/shard_map/ppermute | solution.py:325
  52.4 3.6 %collective-permute-start.10 = (f32[8,128]{1,0:T(8,128)S(1)}, f32[8,128]{1,0:T(8,128)S(1)}, u32[]{:S(2)}, u32[]{:S(2)}) collective-permute-start(f32[8,128]{1,0:T(8,128)S(1)} %add.75), channel_id=1, source_target_pairs={{0,4},{1,5},{2,6},{3,7},{4,0},{5,1},{6,2},{7,3},{8,12},{9,13},{10,... | collective-permute-start | bytes 12296 | tf_op jit(solution)/shard_map/ppermute | solution.py:325
  56.0 4.5 %collective-permute-start.11 = (f32[8,128]{1,0:T(8,128)S(1)}, f32[8,128]{1,0:T(8,128)S(1)}, u32[]{:S(2)}, u32[]{:S(2)}) collective-permute-start(f32[8,128]{1,0:T(8,128)S(1)} %add.76.total), channel_id=1, source_target_pairs={{0,8},{1,9},{2,10},{3,11},{4,12},{5,13},{6,14},{7,15},{8,0},{9,1},... | collective-permute-start | bytes 12296 | tf_op jit(solution)/shard_map/ppermute | solution.py:325

commit v15 on v14

--- a/solution.py
+++ b/solution.py
@@ -104,17 +104,42 @@
     write_payload(payload, tiles, [], basis, per_group)
 
 
+def window_place(distance, clusters, me):
+    core, chip = me % 2, me // 2
+    before, after = 3 - chip % 2, 2 + chip % 2
+    slot = [before, jnp.where(core == 0, 4, 1), 0, jnp.where(core == 0, 1, 4), after]
+    slab = lax.div(distance, clusters)
+    chosen = jnp.zeros_like(distance)
+    for s, value in enumerate(slot):
+        chosen = jnp.where(slab == s, value, chosen)
+    return chosen * clusters + lax.rem(distance, clusters)
+
+
 def prepare_kernel(
-    coupling_hbm, target_hbm, blocks_hbm, _, __, high_out, low_out, target_out, ahead, coupling, target, sems
+    axis, size, near_cols_hbm, near_counts_hbm, far_cols_hbm, coupling_hbm, target_hbm, blocks_hbm, _,
+    places, high_out, low_out, target_out, ahead, near_cols, near_counts, far_cols, coupling, target, sems,
 ):
-    copies = [
-        pltpu.make_async_copy(coupling_hbm, coupling, sems.at[0]),
-        pltpu.make_async_copy(target_hbm, target, sems.at[1]),
-        pltpu.make_async_copy(blocks_hbm.at[pl.ds(0, ahead.shape[0])], ahead, sems.at[2]),
-    ]
+    pairs = (
+        (near_cols_hbm, near_cols), (near_counts_hbm, near_counts), (far_cols_hbm, far_cols),
+        (coupling_hbm, coupling), (target_hbm, target), (blocks_hbm.at[pl.ds(0, ahead.shape[0])], ahead),
+    )
+    copies = [pltpu.make_async_copy(source, to, sems.at[n]) for n, (source, to) in enumerate(pairs)]
     for copy in copies:
         copy.start()
-    for copy in copies[:2]:
+    for copy in copies[:3]:
+        copy.wait()
+    slots, clusters = near_cols.shape
+    me = lax.axis_index(axis)
+    every = clusters * size
+    distance = near_cols[...] - me * clusters + 2 * clusters
+    distance = jnp.where(distance < 0, distance + every, distance)
+    distance = jnp.where(distance >= every, distance - every, distance)
+    live = lax.broadcasted_iota(jnp.int32, (slots, clusters), 0) < near_counts[...]
+    places[:slots, :] = jnp.where(live, window_place(distance, clusters, me), 5 * clusters)
+    owner = lax.div(far_cols[...], clusters)
+    other_core = (owner ^ me) & 1
+    places[slots:, :] = (other_core * (size // 2) + owner // 2) * clusters + lax.rem(far_cols[...], clusters)
+    for copy in copies[3:5]:
         copy.wait()
     slots, rank, _, clusters = coupling.shape
     per_tile = LANES // clusters
@@ -131,7 +156,7 @@
     column = lax.broadcasted_iota(jnp.int32, (size, size), 1)
     wanted = (row % clusters) * rank + row // clusters
     target_out[...] = dot((column == wanted).astype(bf16), target[...]).astype(bf16)
-    copies[2].wait()
+    copies[5].wait()
 
 
 def fetch_kernel(first, blocks_hbm, *refs):
@@ -288,21 +313,16 @@
         made = (0.5 * held + (rows_of(near, j) + rows_of(far, j)) * scale - h11 * held) * inverse
         sums = [s + v * made for s, v in zip(sums, (first, second, made))]
         candidate[pl.ds(j * R, R), :] = made
-    lane = lane_ids()
-    tile = jnp.zeros((R, LANES), f32)
-    for t, partial in enumerate(sums):
-        tile = jnp.where(lane == t, jnp.sum(partial, axis=1, keepdims=True), tile)
-    sums_out[...] = tile
-
-
-def finish_kernel(
-    per_group, unknowns, b, image, candidate, sent, received, total, total_mate, solution_out, next_out
-):
+    tile = sums_tile(sums).astype(bf16)
+    for device in range(sums_out.shape[0]):
+        sums_out[device] = tile
+
+
+def finish_kernel(per_group, unknowns, b, image, candidate, sent, received, got, solution_out, next_out):
     clusters = b.shape[0] // R
     sums = read_sums(tails((sent, received), b.shape[0], clusters // per_group * R), 3, unknowns)
     start_norm, h11, h21, v11, v22, v12 = arnoldi_one(*sums)
-    totals = total[...] + total_mate[...]
-    h12, h22, ww = [totals[:, t : t + 1] * (1.0 / unknowns) for t in range(3)]
+    h12, h22, ww = read_sums([got[device] for device in range(got.shape[0])], 3, unknowns)
     uu = ww - 2.0 * (h12 * h12 + h22 * h22) + h12 * h12 * v11 + h22 * h22 * v22 + 2.0 * h12 * h22 * v12
     h32 = jnp.sqrt(jnp.maximum(uu, 0.0) + epsilon)
     g11 = h11 * h11 + h21 * h21
@@ -343,24 +363,6 @@
     return [block] + [swapped(block, partner) for partner in (core_mate, even_mate, odd_mate)]
 
 
-def window_place(distance, clusters):
-    me = lax.axis_index("rows")
-    core, chip = me % 2, me // 2
-    before, after = 3 - chip % 2, 2 + chip % 2
-    slot = [
-        before,
-        jnp.where(core == 0, 4, 1),
-        0,
-        jnp.where(core == 0, 1, 4),
-        after,
-    ]
-    slab = distance // clusters
-    chosen = jnp.zeros_like(distance)
-    for s, value in enumerate(slot):
-        chosen = jnp.where(slab == s, value, chosen)
-    return chosen * clusters + distance % clusters
-
-
 def on_device(
     right_sides, near_blocks, near_cols, near_counts, basis_in, target_basis, coupling, far_cols
 ):
@@ -370,7 +372,6 @@
     per_group = LANES // rank
     head = clusters // per_group * R
     size = lax.axis_size("rows")
-    every = clusters * size
     unknowns = float(width * size)
     rows = clusters * R
 
@@ -405,31 +406,25 @@
     got = gather(payload)
     held = sends_of(lowered)
 
-    reach = 2 * clusters
-    start = lax.axis_index("rows") * clusters
-    distance = (near_cols.T - start + reach) % every
-    live = jnp.arange(slots, dtype=jnp.int32)[:, None] < near_counts[None, :]
-    placed = jnp.where(live, window_place(distance, clusters), 5 * clusters).astype(jnp.int32)
-    owner = far_cols.T // clusters
-    other_core = (owner % 2) ^ (lax.axis_index("rows") % 2)
-    far_index = (other_core * (size // 2) + owner // 2) * clusters + far_cols.T % clusters
-    places = jnp.concatenate([placed, far_index], axis=0)
     blocks = in_hbm(near_blocks.reshape(clusters * slots, LANES, LANES))
     early = blocks.shape[0] // 4
-    high, low, target, ahead = call(
-        prepare_kernel, "prepare",
+    places, high, low, target, ahead = call(
+        functools.partial(prepare_kernel, "rows", size), "prepare",
         (
+            shape(2 * slots, clusters, dtype=jnp.int32),
             shape(slots * rank, rank * clusters, dtype=bf16),
             shape(slots * rank, rank * clusters, dtype=bf16),
             shape(rank * clusters, LANES, dtype=bf16),
             pltpu.VMEM((early, LANES, LANES), bf16),
         ),
-        [HBM] * 3 + [ANY] * 2,
+        [HBM] * 6 + [ANY], in_hbm(near_cols.T), in_hbm(near_counts.reshape(1, clusters)), in_hbm(far_cols.T),
         in_hbm(jnp.transpose(coupling, (1, 2, 3, 0))), in_hbm(target_basis.reshape(clusters * rank, LANES)),
-        blocks, payload, places,
+        blocks, held[2],
         scratch_shapes=[
+            scratch(slots, clusters, dtype=jnp.int32), scratch(1, clusters, dtype=jnp.int32),
+            scratch(slots, clusters, dtype=jnp.int32),
             scratch(slots, rank, rank, clusters), scratch(clusters * rank, LANES, dtype=bf16),
-            pltpu.SemaphoreType.DMA((3,)),
+            pltpu.SemaphoreType.DMA((6,)),
         ],
     )
 
@@ -464,15 +459,12 @@
     here = arrived(got, sends_of(lowered), ahead, token)
     candidate, sums = call(
         functools.partial(second_kernel, per_group, unknowns), "operator_two",
-        (shape(rows, LANES), shape(R, LANES)),
+        (shape(rows, LANES), shape(size, R, LANES, dtype=bf16)),
         operands, *here, field, image, scratch_shapes=kept,
     )
-    *steps, last = [1 << n for n in range((size - 1).bit_length())]
-    for step in steps:
-        sums = sums + swapped(sums, lambda i: i ^ step)
     return call(
         functools.partial(finish_kernel, per_group, unknowns), "finish", (shape(R, width), shape(R, width)),
-        [VMEM] * 7, field, image, candidate, *here[7:9], sums, swapped(sums, lambda i: i ^ last),
+        [VMEM] * 6, field, image, candidate, *here[7:9], lax.all_to_all(sums, "rows", 0, 0),
     )
 
 

time: 62.4 us -> 58.6 us (0.939)
  waiting for transfers between devices: 19.6 us -> 3.75 us
  blocking collectives: 0 us -> 9.2 us
  starting transfers between devices: 19.7 us -> 23.2 us
  other arithmetic: 0.76 us -> 0 us
    ppermute x12 -> x8, waiting for transfers between devices: 13.7 us -> 1.97 us  [swapped(): lax.ppermute(block, 'rows', [(i, partner(i)) for i in range(lax.axis_size...]
    all_to_all x0 -> x1, blocking collectives: none -> 9.2 us  [on_device(): lax.all_to_all(sums, 'rows', 0, 0)]
    all_to_all x2, starting transfers between devices: 6.72 us -> 12.1 us  [gather(): return lax.all_to_all(block, 'rows', 0, 0, axis_index_groups=groups)]
    all_to_all x2, waiting for transfers between devices: 5.81 us -> 1.78 us  [gather(): return lax.all_to_all(block, 'rows', 0, 0, axis_index_groups=groups)]
    ppermute x12 -> x8, starting transfers between devices: 13 us -> 11.1 us  [swapped(): lax.ppermute(block, 'rows', [(i, partner(i)) for i in range(lax.axis_size...]
    select_n x1 -> x0, other arithmetic: 0.75 us -> none  [on_device(): jnp.where(live, window_place(distance, clusters), 5 * clusters)]
  transfers between devices with their start and end apart: 14 -> 10, of which waited for: 8 -> 4; matrix products, arithmetic and copies ran while one was open for 1% -> 0% of each run, Pallas kernels for 15% -> 16%
where the time goes in v15:
time: 58.6 us; the launch traced here: 58.1 us
  starting transfers between devices  23.2 us (40%)
  Pallas kernels  21.2 us (36%)
  blocking collectives  9.2 us (16%)
  waiting for transfers between devices  3.75 us (6%)
  between operations  0.74 us (1%)
    pallas_call x10, Pallas kernels, call(): pl.pallas_call(kernel, out_shape=out, in_specs=ins, out_specs=jax.tree.ma...  21.2 us
    all_to_all x2, starting transfers between devices, gather(): return lax.all_to_all(block, 'rows', 0, 0, axis_index_groups=groups)  12.1 us
    ppermute x8, starting transfers between devices, swapped(): lax.ppermute(block, 'rows', [(i, partner(i)) for i in range(lax.axis_size...  11.1 us
    all_to_all x1, blocking collectives, on_device(): lax.all_to_all(sums, 'rows', 0, 0)  9.2 us
    ppermute x8, waiting for transfers between devices, swapped(): lax.ppermute(block, 'rows', [(i, partner(i)) for i in range(lax.axis_size...  1.97 us
    all_to_all x2, waiting for transfers between devices, gather(): return lax.all_to_all(block, 'rows', 0, 0, axis_index_groups=groups)  1.78 us
  transfers between devices with their start and end apart: 10, of which 4 were waited for; matrix products, arithmetic and copies ran while one was open for 0% of the time, Pallas kernels for 16%

profile of v15, /device:TPU:0, one launch (start us, length us, event | category | flops | bytes accessed | tf_op | source)
XLA Modules:
  0.0 58.1 jit_solution(12130471681212836572)
XLA Ops:
  0.6 1.8 %start.1 = (f32[256,128]{1,0:T(8,128)S(1)}, bf16[512,128]{1,0:T(8,128)(2,1)S(1)}, bf16[256,128]{1,0:T(8,128)(2,1)S(1)}, bf16[8,48,128]{2,1,0:T(8,128)(2,1)}) custom-call(f32[8,4096]{1,0:T(8,128)} %b_hbm.1, bf16[512,128]{1,0:T(8,128)(2,1)} %bitcast.13), custom_call_target="tpu_custom_call" | custom-call | tf_op jit(solution)/shard_map/start/pallas_call | solution.py:388
  2.5 7.3 %all-to-all-start = ((bf16[8,48,128]{2,1,0:T(8,128)(2,1)}), bf16[8,48,128]{2,1,0:T(8,128)(2,1)S(1)}, u32[]{:S(2)}, u32[]{:S(2)}) async-start(bf16[8,48,128]{2,1,0:T(8,128)(2,1)} %get-tuple-element.26), calls=%async_computation | async-start | bytes 196608 | tf_op jit(solution)/shard_map/all_to_all | solution.py:395
  9.8 2.0 %collective-permute-start.1 = (bf16[256,128]{1,0:T(8,128)(2,1)S(1)}, bf16[256,128]{1,0:T(8,128)(2,1)S(1)}, u32[]{:S(2)}, u32[]{:S(2)}) collective-permute-start(bf16[256,128]{1,0:T(8,128)(2,1)S(1)} %get-tuple-element.23.own), channel_id=1, source_target_pairs={{0,2},{1,3},{2,0},{3,1},{4,6},{5,7},{6,4},{7,5},{8,10},{9,11},{10,... | collective-permute-start | bytes 196616 | tf_op jit(solution)/shard_map/ppermute | solution.py:345
  11.8 3.3 %collective-permute-start.2 = (bf16[256,128]{1,0:T(8,128)(2,1)S(1)}, bf16[256,128]{1,0:T(8,128)(2,1)S(1)}, u32[]{:S(2)}, u32[]{:S(2)}) collective-permute-start(bf16[256,128]{1,0:T(8,128)(2,1)S(1)} %get-tuple-element.23.own), channel_id=1, source_target_pairs={{0,14},{1,15},{2,4},{3,5},{4,2},{5,3},{6,8},{7,9},{8,6},{9,7},{10,... | collective-permute-start | bytes 196616 | tf_op jit(solution)/shard_map/ppermute | solution.py:345
  15.1 0.0 collective-permute-done.1._.even
  15.1 2.0 %prepare.1 = (s32[16,32]{1,0:T(8,128)S(1)}, bf16[128,512]{1,0:T(8,128)(2,1)S(1)}, bf16[128,512]{1,0:T(8,128)(2,1)S(1)}, bf16[512,128]{1,0:T(8,128)(2,1)S(1)}, bf16[64,128,128]{2,1,0:T(8,128)(2,1)S(1)}) custom-call(s32[8,32]{1,0:T(8,128)} %bitcast.14, s32[1,32]{1,0:T(1,128)} %bitcast.16, s32[8,32]{1,0:T(8,128)} %bitcast.15, f32[8,16,16,32]{3,2,1,0:T(8,128)} %bitcast.11, ...), custom_call_target="tpu_custom_call" | custom-call | tf_op jit(solution)/shard_map/prepare/pallas_call | solution.py:388
  17.1 0.3 all-to-all-done.refs_0_.got
  17.4 2.9 %fetch.2 = (bf16[192,128,128]{2,1,0:T(8,128)(2,1)S(1)}, f32[8,128]{1,0:T(8,128)S(1)}) custom-call(bf16[256,128,128]{2,1,0:T(8,128)(2,1)} %bitcast.8, bf16[8,48,128]{2,1,0:T(8,128)(2,1)S(1)} %all-to-all-done.refs_0_.got, bf16[512,128]{1,0:T(8,128)(2,1)S(1)} %get-tuple-element.27.refs_1_.target), custom_call_target="tpu_custom_call" | custom-call | tf_op jit(solution)/shard_map/fetch/pallas_call | solution.py:388
  20.3 0.0 collective-permute-done.2.odd
  20.4 0.1 collective-permute-start.3
  20.4 0.5 collective-permute-start
  20.9 1.0 %collective-permute-done.mate = bf16[256,128]{1,0:T(8,128)(2,1)S(1)} collective-permute-done((bf16[256,128]{1,0:T(8,128)(2,1)S(1)}, bf16[256,128]{1,0:T(8,128)(2,1)S(1)}, u32[]{:S(2)}, u32[]{:S(2)}) %collective-permute-start) | collective-permute-done | bytes 65568 | tf_op jit(solution)/shard_map/ppermute | solution.py:345
  21.9 4.6 %operator_one.1 = (f32[256,128]{1,0:T(8,128)S(1)}, bf16[256,128]{1,0:T(8,128)(2,1)S(1)}, bf16[8,48,128]{2,1,0:T(8,128)(2,1)}) custom-call(bf16[256,128]{1,0:T(8,128)(2,1)S(1)} %get-tuple-element.23.own, bf16[256,128]{1,0:T(8,128)(2,1)S(1)} %collective-permute-done.mate, bf16[256,128]{1,0:T(8,128)(2,1)S(1)} %collective-permute-done.1._.even, ...), custom_call_target="tpu_custom_call" | custom-call | tf_op jit(solution)/shard_map/operator_one/pallas_call | solution.py:388
  26.5 4.8 %all-to-all-start.1 = ((bf16[8,48,128]{2,1,0:T(8,128)(2,1)}), bf16[8,48,128]{2,1,0:T(8,128)(2,1)S(1)}, u32[]{:S(2)}, u32[]{:S(2)}) async-start(bf16[8,48,128]{2,1,0:T(8,128)(2,1)} %get-tuple-element.35.refs_0_), calls=%async_computation.1 | async-start | bytes 196608 | tf_op jit(solution)/shard_map/all_to_all | solution.py:395
  31.3 4.7 %collective-permute-start.6 = (bf16[256,128]{1,0:T(8,128)(2,1)S(1)}, bf16[256,128]{1,0:T(8,128)(2,1)S(1)}, u32[]{:S(2)}, u32[]{:S(2)}) collective-permute-start(bf16[256,128]{1,0:T(8,128)(2,1)S(1)} %get-tuple-element.34.own), channel_id=1, source_target_pairs={{0,14},{1,15},{2,4},{3,5},{4,2},{5,3},{6,8},{7,9},{8,6},{9,7},{10,... | collective-permute-start | bytes 196616 | tf_op jit(solution)/shard_map/ppermute | solution.py:345
  36.0 1.6 %ahead.1 = (bf16[64,128,128]{2,1,0:T(8,128)(2,1)S(1)}, f32[8,128]{1,0:T(8,128)S(1)}) custom-call(bf16[256,128,128]{2,1,0:T(8,128)(2,1)} %bitcast.9, bf16[8,48,128]{2,1,0:T(8,128)(2,1)} %get-tuple-element.35.refs_0_), custom_call_target="tpu_custom_call" | custom-call | tf_op jit(solution)/shard_map/ahead/pallas_call | solution.py:388
  37.6 1.5 %all-to-all-done.1.refs_0_.got = bf16[8,48,128]{2,1,0:T(8,128)(2,1)S(1)} async-done(((bf16[8,48,128]{2,1,0:T(8,128)(2,1)}), bf16[8,48,128]{2,1,0:T(8,128)(2,1)S(1)}, u32[]{:S(2)}, u32[]{:S(2)}) %all-to-all-start.1) | async-done | bytes 98336 | tf_op jit(solution)/shard_map/all_to_all | solution.py:395
  39.0 2.9 %fetch.3 = (bf16[192,128,128]{2,1,0:T(8,128)(2,1)S(1)}, f32[8,128]{1,0:T(8,128)S(1)}) custom-call(bf16[256,128,128]{2,1,0:T(8,128)(2,1)} %bitcast.10, bf16[8,48,128]{2,1,0:T(8,128)(2,1)S(1)} %all-to-all-done.1.refs_0_.got, f32[8,128]{1,0:T(8,128)S(1)} %get-tuple-element.37.refs_1_), custom_call_target="tpu_custom_call" | custom-call | tf_op jit(solution)/shard_map/fetch/pallas_call | solution.py:388
  42.0 0.1 collective-permute-start.7
  42.0 0.5 collective-permute-start.4
  42.5 1.0 %collective-permute-done.4.mate = bf16[256,128]{1,0:T(8,128)(2,1)S(1)} collective-permute-done((bf16[256,128]{1,0:T(8,128)(2,1)S(1)}, bf16[256,128]{1,0:T(8,128)(2,1)S(1)}, u32[]{:S(2)}, u32[]{:S(2)}) %collective-permute-start.4) | collective-permute-done | bytes 65568 | tf_op jit(solution)/shard_map/ppermute | solution.py:345
  43.5 3.9 %operator_two.1 = (f32[256,128]{1,0:T(8,128)S(1)}, bf16[16,8,128]{2,1,0:T(8,128)(2,1)S(1)}) custom-call(bf16[256,128]{1,0:T(8,128)(2,1)S(1)} %get-tuple-element.34.own, bf16[256,128]{1,0:T(8,128)(2,1)S(1)} %collective-permute-done.4.mate, bf16[256,128]{1,0:T(8,128)(2,1)S(1)} %collective-permute-done.5.even, bf16[256,128]{1,0:T(8,128)(2,1)S(1)} %collective-permute-done.6.odd, ...), custom_call_target="tpu_custom_call" | custom-call | tf_op jit(solution)/shard_map/operator_two/pallas_call | solution.py:388
  47.5 9.2 %all_to_all.15.got = bf16[16,8,128]{2,1,0:T(8,128)(2,1)S(1)} all-to-all(bf16[16,8,128]{2,1,0:T(8,128)(2,1)S(1)} %get-tuple-element.41), channel_id=1, replica_groups=mesh['groups'=2,'rows'=16] {'rows'}, dimensions={0} | all-to-all | bytes 65536 | tf_op jit(solution)/shard_map/all_to_all | solution.py:467
  56.7 1.5 %finish.1 = (f32[8,4096]{1,0:T(8,128)}, f32[8,4096]{1,0:T(8,128)}) custom-call(f32[256,128]{1,0:T(8,128)S(1)} %get-tuple-element.22.b, f32[256,128]{1,0:T(8,128)S(1)} %get-tuple-element.33.image, f32[256,128]{1,0:T(8,128)S(1)} %get-tuple-element.40.candidate, bf16[640,128]{1,0:T(8,128)(2,1)S(1)} %relay.3.sent, ...), custom_call_target="tpu_custom_call" | custom-call | tf_op jit(solution)/shard_map/finish/pallas_call | solution.py:388
  (7 shorter events, 0.1 us)
Async XLA Ops:
  2.5 15.0 %all-to-all-start = ((bf16[8,48,128]{2,1,0:T(8,128)(2,1)}), bf16[8,48,128]{2,1,0:T(8,128)(2,1)S(1)}, u32[]{:S(2)}, u32[]{:S(2)}) async-start(bf16[8,48,128]{2,1,0:T(8,128)(2,1)} %get-tuple-element.26), calls=%async_computation | async-start | bytes 196608 | tf_op jit(solution)/shard_map/all_to_all | solution.py:395
  9.8 5.3 %collective-permute-start.1 = (bf16[256,128]{1,0:T(8,128)(2,1)S(1)}, bf16[256,128]{1,0:T(8,128)(2,1)S(1)}, u32[]{:S(2)}, u32[]{:S(2)}) collective-permute-start(bf16[256,128]{1,0:T(8,128)(2,1)S(1)} %get-tuple-element.23.own), channel_id=1, source_target_pairs={{0,2},{1,3},{2,0},{3,1},{4,6},{5,7},{6,4},{7,5},{8,10},{9,11},{10,... | collective-permute-start | bytes 196616 | tf_op jit(solution)/shard_map/ppermute | solution.py:345
  11.8 8.5 %collective-permute-start.2 = (bf16[256,128]{1,0:T(8,128)(2,1)S(1)}, bf16[256,128]{1,0:T(8,128)(2,1)S(1)}, u32[]{:S(2)}, u32[]{:S(2)}) collective-permute-start(bf16[256,128]{1,0:T(8,128)(2,1)S(1)} %get-tuple-element.23.own), channel_id=1, source_target_pairs={{0,14},{1,15},{2,4},{3,5},{4,2},{5,3},{6,8},{7,9},{8,6},{9,7},{10,... | collective-permute-start | bytes 196616 | tf_op jit(solution)/shard_map/ppermute | solution.py:345
  20.4 1.6 %collective-permute-start.3 = (bf16[640,128]{1,0:T(8,128)(2,1)S(1)}, bf16[640,128]{1,0:T(8,128)(2,1)S(1)}, u32[]{:S(2)}, u32[]{:S(2)}) collective-permute-start(bf16[640,128]{1,0:T(8,128)(2,1)S(1)} %relay.2.sent), channel_id=1, source_target_pairs={{0,1},{1,0},{2,3},{3,2},{4,5},{5,4},{6,7},{7,6},{8,9},{9,8},{10,11... | collective-permute-start | bytes 491528 | tf_op jit(solution)/shard_map/ppermute | solution.py:345
  20.4 1.5 %collective-permute-start = (bf16[256,128]{1,0:T(8,128)(2,1)S(1)}, bf16[256,128]{1,0:T(8,128)(2,1)S(1)}, u32[]{:S(2)}, u32[]{:S(2)}) collective-permute-start(bf16[256,128]{1,0:T(8,128)(2,1)S(1)} %get-tuple-element.23.own), channel_id=1, source_target_pairs={{0,1},{1,0},{2,3},{3,2},{4,5},{5,4},{6,7},{7,6},{8,9},{9,8},{10,11... | collective-permute-start | bytes 196616 | tf_op jit(solution)/shard_map/ppermute | solution.py:345
  26.5 12.5 %all-to-all-start.1 = ((bf16[8,48,128]{2,1,0:T(8,128)(2,1)}), bf16[8,48,128]{2,1,0:T(8,128)(2,1)S(1)}, u32[]{:S(2)}, u32[]{:S(2)}) async-start(bf16[8,48,128]{2,1,0:T(8,128)(2,1)} %get-tuple-element.35.refs_0_), calls=%async_computation.1 | async-start | bytes 196608 | tf_op jit(solution)/shard_map/all_to_all | solution.py:395
  31.3 10.6 %collective-permute-start.6 = (bf16[256,128]{1,0:T(8,128)(2,1)S(1)}, bf16[256,128]{1,0:T(8,128)(2,1)S(1)}, u32[]{:S(2)}, u32[]{:S(2)}) collective-permute-start(bf16[256,128]{1,0:T(8,128)(2,1)S(1)} %get-tuple-element.34.own), channel_id=1, source_target_pairs={{0,14},{1,15},{2,4},{3,5},{4,2},{5,3},{6,8},{7,9},{8,6},{9,7},{10,... | collective-permute-start | bytes 196616 | tf_op jit(solution)/shard_map/ppermute | solution.py:345
  36.0 5.9 %collective-permute-start.5 = (bf16[256,128]{1,0:T(8,128)(2,1)S(1)}, bf16[256,128]{1,0:T(8,128)(2,1)S(1)}, u32[]{:S(2)}, u32[]{:S(2)}) collective-permute-start(bf16[256,128]{1,0:T(8,128)(2,1)S(1)} %get-tuple-element.34.own), channel_id=1, source_target_pairs={{0,2},{1,3},{2,0},{3,1},{4,6},{5,7},{6,4},{7,5},{8,10},{9,11},{10,... | collective-permute-start | bytes 196616 | tf_op jit(solution)/shard_map/ppermute | solution.py:345
  42.0 1.6 %collective-permute-start.7 = (bf16[640,128]{1,0:T(8,128)(2,1)S(1)}, bf16[640,128]{1,0:T(8,128)(2,1)S(1)}, u32[]{:S(2)}, u32[]{:S(2)}) collective-permute-start(bf16[640,128]{1,0:T(8,128)(2,1)S(1)} %relay.3.sent), channel_id=1, source_target_pairs={{0,1},{1,0},{2,3},{3,2},{4,5},{5,4},{6,7},{7,6},{8,9},{9,8},{10,11... | collective-permute-start | bytes 491528 | tf_op jit(solution)/shard_map/ppermute | solution.py:345
  42.0 1.5 %collective-permute-start.4 = (bf16[256,128]{1,0:T(8,128)(2,1)S(1)}, bf16[256,128]{1,0:T(8,128)(2,1)S(1)}, u32[]{:S(2)}, u32[]{:S(2)}) collective-permute-start(bf16[256,128]{1,0:T(8,128)(2,1)S(1)} %get-tuple-element.34.own), channel_id=1, source_target_pairs={{0,1},{1,0},{2,3},{3,2},{4,5},{5,4},{6,7},{7,6},{8,9},{9,8},{10,11... | collective-permute-start | bytes 196616 | tf_op jit(solution)/shard_map/ppermute | solution.py:345

commit v16 on v15

--- a/solution.py
+++ b/solution.py
@@ -79,10 +79,9 @@
     return tile
 
 
-def write_payload(payload, tiles, sums, basis, per_group):
-    groups = len(tiles) // per_group
-    parts = [compress(tiles[g * per_group : (g + 1) * per_group], basis, g) for g in range(groups)]
-    parts += [sums_tile(sums), jnp.zeros((TAIL - R, LANES), f32)]
+def write_payload(payload, parts, sums):
+    if sums:
+        parts = parts + [sums_tile(sums), jnp.zeros((TAIL - R, LANES), f32)]
     block = jnp.concatenate(parts, axis=0).astype(bf16)
     for device in range(payload.shape[0]):
         payload[device] = block
@@ -101,7 +100,8 @@
     tiles = [b[:, j * LANES : (j + 1) * LANES] for j in range(clusters)]
     field[...] = jnp.concatenate(tiles, axis=0)
     lowered[...] = jnp.concatenate(tiles, axis=0).astype(bf16)
-    write_payload(payload, tiles, [], basis, per_group)
+    groups = [tiles[g : g + per_group] for g in range(0, clusters, per_group)]
+    write_payload(payload, [compress(group, basis, g) for g, group in enumerate(groups)], [])
 
 
 def window_place(distance, clusters, me):
@@ -193,7 +193,7 @@
         out[span, :] = odd[...]
 
 
-def apply(per_group, each, slabs, places, ahead, blocks, swaps, high, low, target, near, far, window, table):
+def apply(per_group, each, slabs, places, ahead, blocks, swaps, high, low, target, near, far, window, table, finish):
     clusters = near.shape[0] // R
     slots = (ahead.shape[0] + blocks.shape[0]) // clusters
     rank = LANES // per_group
@@ -258,6 +258,9 @@
             far[...] = dot(jnp.concatenate(expanded_high, axis=1), target[...]) + dot(
                 jnp.concatenate(expanded_low, axis=1), target[...]
             )
+        if 2 * i >= clusters:
+            for n in range(2 * i - clusters, 2 * i - clusters + 4):
+                finish(n)
 
 
 def first_kernel(
@@ -266,20 +269,24 @@
 ):
     clusters = near.shape[0] // R
     slabs, swaps = (own, mate, even, odd), (sent, received)
-    each = clusters // per_group * R + TAIL
-    apply(per_group, each, slabs, places, ahead, blocks, swaps, high, low, target, near, far, window, table)
-    tiles = []
+    each = clusters // per_group * R
+    tiles, parts = [], []
     sums = [jnp.zeros((R, LANES), f32) for _ in range(3)]
-    for i in range(clusters):
+
+    def finish(i):
         field = rows_of(b, i)
         made = 0.5 * field + (rows_of(near, i) + rows_of(far, i))
-        sums = [s + f * g for s, f, g in zip(sums, (field, field, made), (field, made, made))]
+        sums[:] = [s + f * g for s, f, g in zip(sums, (field, field, made), (field, made, made))]
         tiles.append(made)
-    for i in range(0, clusters, 2):
-        both = jnp.concatenate(tiles[i : i + 2], axis=0)
-        image[pl.ds(i * R, 2 * R), :] = both
-        lowered[pl.ds(i * R, 2 * R), :] = both.astype(bf16)
-    write_payload(payload, tiles, sums, basis, per_group)
+        if i % 2:
+            both = jnp.concatenate(tiles[i - 1 :], axis=0)
+            image[pl.ds((i - 1) * R, 2 * R), :] = both
+            lowered[pl.ds((i - 1) * R, 2 * R), :] = both.astype(bf16)
+        if i % per_group == per_group - 1:
+            parts.append(compress(tiles[-per_group:], basis, i // per_group))
+
+    apply(per_group, each, slabs, places, ahead, blocks, swaps, high, low, target, near, far, window, table, finish)
+    write_payload(payload, parts, sums)
 
 
 def arnoldi_one(bb, bw, ww):
@@ -300,19 +307,22 @@
     clusters = near.shape[0] // R
     head = clusters // per_group * R
     slabs, swaps = (own, mate, even, odd), (sent, received)
-    apply(per_group, head + TAIL, slabs, places, ahead, blocks, swaps, high, low, target, near, far, window, table)
-    sums = read_sums(tails(swaps, own.shape[0], head), 3, unknowns)
-    start_norm, h11, h21, _, _, _ = arnoldi_one(*sums)
+    means = read_sums(tails(swaps, own.shape[0], head), 3, unknowns)
+    start_norm, h11, h21, _, _, _ = arnoldi_one(*means)
     scale = 1.0 / start_norm
     inverse = 1.0 / h21
     sums = [jnp.zeros((R, LANES), f32) for _ in range(3)]
-    for j in range(clusters):
+
+    def finish(j):
         held = rows_of(image, j) * scale
         first = rows_of(b, j) * scale
         second = (held - h11 * first) * inverse
         made = (0.5 * held + (rows_of(near, j) + rows_of(far, j)) * scale - h11 * held) * inverse
-        sums = [s + v * made for s, v in zip(sums, (first, second, made))]
+        sums[:] = [s + v * made for s, v in zip(sums, (first, second, made))]
         candidate[pl.ds(j * R, R), :] = made
+
+    each = head + TAIL
+    apply(per_group, each, slabs, places, ahead, blocks, swaps, high, low, target, near, far, window, table, finish)
     tile = sums_tile(sums).astype(bf16)
     for device in range(sums_out.shape[0]):
         sums_out[device] = tile
@@ -398,7 +408,7 @@
         functools.partial(start_kernel, per_group), "start",
         (
             shape(rows, LANES), shape(clusters * rank, LANES, dtype=bf16), shape(rows, LANES, dtype=bf16),
-            shape(size // 2, head + TAIL, LANES, dtype=bf16),
+            shape(size // 2, head, LANES, dtype=bf16),
         ),
         [HBM] * 2, in_hbm(right_sides), in_hbm(basis_in.reshape(clusters * rank, LANES)),
         scratch_shapes=[scratch(R, width), pltpu.SemaphoreType.DMA((2,))],
@@ -419,7 +429,7 @@
         ),
         [HBM] * 6 + [ANY], in_hbm(near_cols.T), in_hbm(near_counts.reshape(1, clusters)), in_hbm(far_cols.T),
         in_hbm(jnp.transpose(coupling, (1, 2, 3, 0))), in_hbm(target_basis.reshape(clusters * rank, LANES)),
-        blocks, held[2],
+        blocks, held[1],
         scratch_shapes=[
             scratch(slots, clusters, dtype=jnp.int32), scratch(1, clusters, dtype=jnp.int32),
             scratch(slots, clusters, dtype=jnp.int32),

time: 58.6 us -> 56.6 us (0.966)
  starting transfers between devices: 23.2 us -> 20.7 us
    all_to_all x2, starting transfers between devices: 12.1 us -> 10.7 us  [gather(): return lax.all_to_all(block, 'rows', 0, 0, axis_index_groups=groups)]
    ppermute x8, starting transfers between devices: 11.1 us -> 10 us  [swapped(): lax.ppermute(block, 'rows', [(i, partner(i)) for i in range(lax.axis_size...]
  transfers between devices with their start and end apart: 10 -> 10, of which waited for: 4 -> 4; matrix products, arithmetic and copies ran while one was open for 0% -> 0% of each run, Pallas kernels for 16% -> 17%
where the time goes in v16:
time: 56.6 us; the launch traced here: 56.2 us
  Pallas kernels  21.3 us (38%)
  starting transfers between devices  20.7 us (37%)
  blocking collectives  9.2 us (16%)
  waiting for transfers between devices  4.33 us (8%)
  between operations  0.76 us (1%)
    pallas_call x10, Pallas kernels, call(): pl.pallas_call(kernel, out_shape=out, in_specs=ins, out_specs=jax.tree.ma...  21.3 us
    all_to_all x2, starting transfers between devices, gather(): return lax.all_to_all(block, 'rows', 0, 0, axis_index_groups=groups)  10.7 us
    ppermute x8, starting transfers between devices, swapped(): lax.ppermute(block, 'rows', [(i, partner(i)) for i in range(lax.axis_size...  10 us
    all_to_all x1, blocking collectives, on_device(): lax.all_to_all(sums, 'rows', 0, 0)  9.2 us
    ppermute x8, waiting for transfers between devices, swapped(): lax.ppermute(block, 'rows', [(i, partner(i)) for i in range(lax.axis_size...  2.33 us
    all_to_all x2, waiting for transfers between devices, gather(): return lax.all_to_all(block, 'rows', 0, 0, axis_index_groups=groups)  2 us
  transfers between devices with their start and end apart: 10, of which 4 were waited for; matrix products, arithmetic and copies ran while one was open for 0% of the time, Pallas kernels for 17%

profile of v16, /device:TPU:0, one launch (start us, length us, event | category | flops | bytes accessed | tf_op | source)
XLA Modules:
  0.0 56.2 jit_solution(15050870221052241159)
XLA Ops:
  0.6 1.8 %start.1 = (f32[256,128]{1,0:T(8,128)S(1)}, bf16[512,128]{1,0:T(8,128)(2,1)S(1)}, bf16[256,128]{1,0:T(8,128)(2,1)S(1)}, bf16[8,32,128]{2,1,0:T(8,128)(2,1)}) custom-call(f32[8,4096]{1,0:T(8,128)} %b_hbm.1, bf16[512,128]{1,0:T(8,128)(2,1)} %bitcast.13), custom_call_target="tpu_custom_call" | custom-call | tf_op jit(solution)/shard_map/start/pallas_call | solution.py:398
  2.5 7.3 %all-to-all-start = ((bf16[8,32,128]{2,1,0:T(8,128)(2,1)}), bf16[8,32,128]{2,1,0:T(8,128)(2,1)S(1)}, u32[]{:S(2)}, u32[]{:S(2)}) async-start(bf16[8,32,128]{2,1,0:T(8,128)(2,1)} %get-tuple-element.26), calls=%async_computation | async-start | bytes 131072 | tf_op jit(solution)/shard_map/all_to_all | solution.py:405
  9.8 4.7 %collective-permute-start.2 = (bf16[256,128]{1,0:T(8,128)(2,1)S(1)}, bf16[256,128]{1,0:T(8,128)(2,1)S(1)}, u32[]{:S(2)}, u32[]{:S(2)}) collective-permute-start(bf16[256,128]{1,0:T(8,128)(2,1)S(1)} %get-tuple-element.23.own), channel_id=1, source_target_pairs={{0,14},{1,15},{2,4},{3,5},{4,2},{5,3},{6,8},{7,9},{8,6},{9,7},{10,... | collective-permute-start | bytes 196616 | tf_op jit(solution)/shard_map/ppermute | solution.py:355
  14.5 2.0 %prepare.1 = (s32[16,32]{1,0:T(8,128)S(1)}, bf16[128,512]{1,0:T(8,128)(2,1)S(1)}, bf16[128,512]{1,0:T(8,128)(2,1)S(1)}, bf16[512,128]{1,0:T(8,128)(2,1)S(1)}, bf16[64,128,128]{2,1,0:T(8,128)(2,1)S(1)}) custom-call(s32[8,32]{1,0:T(8,128)} %bitcast.14, s32[1,32]{1,0:T(1,128)} %bitcast.16, s32[8,32]{1,0:T(8,128)} %bitcast.15, f32[8,16,16,32]{3,2,1,0:T(8,128)} %bitcast.11, ...), custom_call_target="tpu_custom_call" | custom-call | tf_op jit(solution)/shard_map/prepare/pallas_call | solution.py:398
  16.6 0.4 all-to-all-done.refs_0_.got
  17.0 2.9 %fetch.2 = (bf16[192,128,128]{2,1,0:T(8,128)(2,1)S(1)}, f32[8,128]{1,0:T(8,128)S(1)}) custom-call(bf16[256,128,128]{2,1,0:T(8,128)(2,1)} %bitcast.8, bf16[8,32,128]{2,1,0:T(8,128)(2,1)S(1)} %all-to-all-done.refs_0_.got, bf16[512,128]{1,0:T(8,128)(2,1)S(1)} %get-tuple-element.27.refs_1_.target), custom_call_target="tpu_custom_call" | custom-call | tf_op jit(solution)/shard_map/fetch/pallas_call | solution.py:398
  19.9 0.0 collective-permute-done.2.odd
  19.9 0.1 collective-permute-start.3
  20.0 1.3 %collective-permute-done.3.received = bf16[512,128]{1,0:T(8,128)(2,1)S(1)} collective-permute-done((bf16[512,128]{1,0:T(8,128)(2,1)S(1)}, bf16[512,128]{1,0:T(8,128)(2,1)S(1)}, u32[]{:S(2)}, u32[]{:S(2)}) %collective-permute-start.3) | collective-permute-done | bytes 131104 | tf_op jit(solution)/shard_map/ppermute | solution.py:355
  21.3 4.7 %operator_one.1 = (f32[256,128]{1,0:T(8,128)S(1)}, bf16[256,128]{1,0:T(8,128)(2,1)S(1)}, bf16[8,48,128]{2,1,0:T(8,128)(2,1)}) custom-call(bf16[256,128]{1,0:T(8,128)(2,1)S(1)} %get-tuple-element.23.own, bf16[256,128]{1,0:T(8,128)(2,1)S(1)} %collective-permute-done._.mate, bf16[256,128]{1,0:T(8,128)(2,1)S(1)} %collective-permute-done.1.even, ...), custom_call_target="tpu_custom_call" | custom-call | tf_op jit(solution)/shard_map/operator_one/pallas_call | solution.py:398
  26.0 3.4 %all-to-all-start.1 = ((bf16[8,48,128]{2,1,0:T(8,128)(2,1)}), bf16[8,48,128]{2,1,0:T(8,128)(2,1)S(1)}, u32[]{:S(2)}, u32[]{:S(2)}) async-start(bf16[8,48,128]{2,1,0:T(8,128)(2,1)} %get-tuple-element.35.refs_0_), calls=%async_computation.1 | async-start | bytes 196608 | tf_op jit(solution)/shard_map/all_to_all | solution.py:405
  29.4 4.7 %collective-permute-start.6 = (bf16[256,128]{1,0:T(8,128)(2,1)S(1)}, bf16[256,128]{1,0:T(8,128)(2,1)S(1)}, u32[]{:S(2)}, u32[]{:S(2)}) collective-permute-start(bf16[256,128]{1,0:T(8,128)(2,1)S(1)} %get-tuple-element.34.own), channel_id=1, source_target_pairs={{0,14},{1,15},{2,4},{3,5},{4,2},{5,3},{6,8},{7,9},{8,6},{9,7},{10,... | collective-permute-start | bytes 196616 | tf_op jit(solution)/shard_map/ppermute | solution.py:355
  34.0 0.0 collective-permute-start.5
  34.0 1.6 %ahead.1 = (bf16[64,128,128]{2,1,0:T(8,128)(2,1)S(1)}, f32[8,128]{1,0:T(8,128)S(1)}) custom-call(bf16[256,128,128]{2,1,0:T(8,128)(2,1)} %bitcast.9, bf16[8,48,128]{2,1,0:T(8,128)(2,1)} %get-tuple-element.35.refs_0_), custom_call_target="tpu_custom_call" | custom-call | tf_op jit(solution)/shard_map/ahead/pallas_call | solution.py:398
  35.6 1.6 %all-to-all-done.1.refs_0_.got = bf16[8,48,128]{2,1,0:T(8,128)(2,1)S(1)} async-done(((bf16[8,48,128]{2,1,0:T(8,128)(2,1)}), bf16[8,48,128]{2,1,0:T(8,128)(2,1)S(1)}, u32[]{:S(2)}, u32[]{:S(2)}) %all-to-all-start.1) | async-done | bytes 98336 | tf_op jit(solution)/shard_map/all_to_all | solution.py:405
  37.1 2.9 %fetch.3 = (bf16[192,128,128]{2,1,0:T(8,128)(2,1)S(1)}, f32[8,128]{1,0:T(8,128)S(1)}) custom-call(bf16[256,128,128]{2,1,0:T(8,128)(2,1)} %bitcast.10, bf16[8,48,128]{2,1,0:T(8,128)(2,1)S(1)} %all-to-all-done.1.refs_0_.got, f32[8,128]{1,0:T(8,128)S(1)} %get-tuple-element.37.refs_1_), custom_call_target="tpu_custom_call" | custom-call | tf_op jit(solution)/shard_map/fetch/pallas_call | solution.py:398
  40.0 0.0 collective-permute-done.5.even
  40.1 0.1 collective-permute-start.7
  40.1 0.5 collective-permute-start.4
  40.6 1.0 %collective-permute-done.4.mate = bf16[256,128]{1,0:T(8,128)(2,1)S(1)} collective-permute-done((bf16[256,128]{1,0:T(8,128)(2,1)S(1)}, bf16[256,128]{1,0:T(8,128)(2,1)S(1)}, u32[]{:S(2)}, u32[]{:S(2)}) %collective-permute-start.4) | collective-permute-done | bytes 65568 | tf_op jit(solution)/shard_map/ppermute | solution.py:355
  41.6 0.0 collective-permute-done.7.received
  41.6 3.9 %operator_two.1 = (f32[256,128]{1,0:T(8,128)S(1)}, bf16[16,8,128]{2,1,0:T(8,128)(2,1)S(1)}) custom-call(bf16[256,128]{1,0:T(8,128)(2,1)S(1)} %get-tuple-element.34.own, bf16[256,128]{1,0:T(8,128)(2,1)S(1)} %collective-permute-done.4.mate, bf16[256,128]{1,0:T(8,128)(2,1)S(1)} %collective-permute-done.5.even, bf16[256,128]{1,0:T(8,128)(2,1)S(1)} %collective-permute-done.6.odd, ...), custom_call_target="tpu_custom_call" | custom-call | tf_op jit(solution)/shard_map/operator_two/pallas_call | solution.py:398
  45.6 9.2 %all_to_all.15.got = bf16[16,8,128]{2,1,0:T(8,128)(2,1)S(1)} all-to-all(bf16[16,8,128]{2,1,0:T(8,128)(2,1)S(1)} %get-tuple-element.41), channel_id=1, replica_groups=mesh['groups'=2,'rows'=16] {'rows'}, dimensions={0} | all-to-all | bytes 65536 | tf_op jit(solution)/shard_map/all_to_all | solution.py:477
  54.8 1.5 %finish.1 = (f32[8,4096]{1,0:T(8,128)}, f32[8,4096]{1,0:T(8,128)}) custom-call(f32[256,128]{1,0:T(8,128)S(1)} %get-tuple-element.22.b, f32[256,128]{1,0:T(8,128)S(1)} %get-tuple-element.33.image, f32[256,128]{1,0:T(8,128)S(1)} %get-tuple-element.40.candidate, bf16[640,128]{1,0:T(8,128)(2,1)S(1)} %relay.3.sent, ...), custom_call_target="tpu_custom_call" | custom-call | tf_op jit(solution)/shard_map/finish/pallas_call | solution.py:398
  (7 shorter events, 0.1 us)
Async XLA Ops:
  2.5 14.5 %all-to-all-start = ((bf16[8,32,128]{2,1,0:T(8,128)(2,1)}), bf16[8,32,128]{2,1,0:T(8,128)(2,1)S(1)}, u32[]{:S(2)}, u32[]{:S(2)}) async-start(bf16[8,32,128]{2,1,0:T(8,128)(2,1)} %get-tuple-element.26), calls=%async_computation | async-start | bytes 131072 | tf_op jit(solution)/shard_map/all_to_all | solution.py:405
  9.8 4.7 %collective-permute-start = (bf16[256,128]{1,0:T(8,128)(2,1)S(1)}, bf16[256,128]{1,0:T(8,128)(2,1)S(1)}, u32[]{:S(2)}, u32[]{:S(2)}) collective-permute-start(bf16[256,128]{1,0:T(8,128)(2,1)S(1)} %get-tuple-element.23.own), channel_id=1, source_target_pairs={{0,1},{1,0},{2,3},{3,2},{4,5},{5,4},{6,7},{7,6},{8,9},{9,8},{10,11... | collective-permute-start | bytes 196616 | tf_op jit(solution)/shard_map/ppermute | solution.py:355
  9.8 10.1 %collective-permute-start.2 = (bf16[256,128]{1,0:T(8,128)(2,1)S(1)}, bf16[256,128]{1,0:T(8,128)(2,1)S(1)}, u32[]{:S(2)}, u32[]{:S(2)}) collective-permute-start(bf16[256,128]{1,0:T(8,128)(2,1)S(1)} %get-tuple-element.23.own), channel_id=1, source_target_pairs={{0,14},{1,15},{2,4},{3,5},{4,2},{5,3},{6,8},{7,9},{8,6},{9,7},{10,... | collective-permute-start | bytes 196616 | tf_op jit(solution)/shard_map/ppermute | solution.py:355
  14.5 5.4 %collective-permute-start.1 = (bf16[256,128]{1,0:T(8,128)(2,1)S(1)}, bf16[256,128]{1,0:T(8,128)(2,1)S(1)}, u32[]{:S(2)}, u32[]{:S(2)}) collective-permute-start(bf16[256,128]{1,0:T(8,128)(2,1)S(1)} %get-tuple-element.23.own), channel_id=1, source_target_pairs={{0,2},{1,3},{2,0},{3,1},{4,6},{5,7},{6,4},{7,5},{8,10},{9,11},{10,... | collective-permute-start | bytes 196616 | tf_op jit(solution)/shard_map/ppermute | solution.py:355
  19.9 1.4 %collective-permute-start.3 = (bf16[512,128]{1,0:T(8,128)(2,1)S(1)}, bf16[512,128]{1,0:T(8,128)(2,1)S(1)}, u32[]{:S(2)}, u32[]{:S(2)}) collective-permute-start(bf16[512,128]{1,0:T(8,128)(2,1)S(1)} %relay.2.sent), channel_id=1, source_target_pairs={{0,1},{1,0},{2,3},{3,2},{4,5},{5,4},{6,7},{7,6},{8,9},{9,8},{10,11... | collective-permute-start | bytes 393224 | tf_op jit(solution)/shard_map/ppermute | solution.py:355
  26.0 11.2 %all-to-all-start.1 = ((bf16[8,48,128]{2,1,0:T(8,128)(2,1)}), bf16[8,48,128]{2,1,0:T(8,128)(2,1)S(1)}, u32[]{:S(2)}, u32[]{:S(2)}) async-start(bf16[8,48,128]{2,1,0:T(8,128)(2,1)} %get-tuple-element.35.refs_0_), calls=%async_computation.1 | async-start | bytes 196608 | tf_op jit(solution)/shard_map/all_to_all | solution.py:405
  29.4 10.7 %collective-permute-start.6 = (bf16[256,128]{1,0:T(8,128)(2,1)S(1)}, bf16[256,128]{1,0:T(8,128)(2,1)S(1)}, u32[]{:S(2)}, u32[]{:S(2)}) collective-permute-start(bf16[256,128]{1,0:T(8,128)(2,1)S(1)} %get-tuple-element.34.own), channel_id=1, source_target_pairs={{0,14},{1,15},{2,4},{3,5},{4,2},{5,3},{6,8},{7,9},{8,6},{9,7},{10,... | collective-permute-start | bytes 196616 | tf_op jit(solution)/shard_map/ppermute | solution.py:355
  34.0 6.0 %collective-permute-start.5 = (bf16[256,128]{1,0:T(8,128)(2,1)S(1)}, bf16[256,128]{1,0:T(8,128)(2,1)S(1)}, u32[]{:S(2)}, u32[]{:S(2)}) collective-permute-start(bf16[256,128]{1,0:T(8,128)(2,1)S(1)} %get-tuple-element.34.own), channel_id=1, source_target_pairs={{0,2},{1,3},{2,0},{3,1},{4,6},{5,7},{6,4},{7,5},{8,10},{9,11},{10,... | collective-permute-start | bytes 196616 | tf_op jit(solution)/shard_map/ppermute | solution.py:355
  40.1 1.6 %collective-permute-start.7 = (bf16[640,128]{1,0:T(8,128)(2,1)S(1)}, bf16[640,128]{1,0:T(8,128)(2,1)S(1)}, u32[]{:S(2)}, u32[]{:S(2)}) collective-permute-start(bf16[640,128]{1,0:T(8,128)(2,1)S(1)} %relay.3.sent), channel_id=1, source_target_pairs={{0,1},{1,0},{2,3},{3,2},{4,5},{5,4},{6,7},{7,6},{8,9},{9,8},{10,11... | collective-permute-start | bytes 491528 | tf_op jit(solution)/shard_map/ppermute | solution.py:355
  40.1 1.5 %collective-permute-start.4 = (bf16[256,128]{1,0:T(8,128)(2,1)S(1)}, bf16[256,128]{1,0:T(8,128)(2,1)S(1)}, u32[]{:S(2)}, u32[]{:S(2)}) collective-permute-start(bf16[256,128]{1,0:T(8,128)(2,1)S(1)} %get-tuple-element.34.own), channel_id=1, source_target_pairs={{0,1},{1,0},{2,3},{3,2},{4,5},{5,4},{6,7},{7,6},{8,9},{9,8},{10,11... | collective-permute-start | bytes 196616 | tf_op jit(solution)/shard_map/ppermute | solution.py:355

commit v17 on v16

--- a/solution.py
+++ b/solution.py
@@ -88,20 +88,29 @@
 
 
 def start_kernel(per_group, b_hbm, basis_hbm, field, basis, lowered, payload, b, sems):
+    groups = basis.shape[0] // LANES
+    span = per_group * LANES
     copies = [
-        pltpu.make_async_copy(b_hbm, b, sems.at[0]),
-        pltpu.make_async_copy(basis_hbm, basis, sems.at[1]),
+        pltpu.make_async_copy(
+            b_hbm.at[:, pl.ds(g * span, span)], b.at[:, pl.ds(g * span, span)], sems.at[g]
+        )
+        for g in range(groups)
     ]
+    whole_basis = pltpu.make_async_copy(basis_hbm, basis, sems.at[groups])
     for copy in copies:
         copy.start()
-    for copy in copies:
+    whole_basis.start()
+    parts = []
+    for g, copy in enumerate(copies):
         copy.wait()
-    clusters = b.shape[1] // LANES
-    tiles = [b[:, j * LANES : (j + 1) * LANES] for j in range(clusters)]
-    field[...] = jnp.concatenate(tiles, axis=0)
-    lowered[...] = jnp.concatenate(tiles, axis=0).astype(bf16)
-    groups = [tiles[g : g + per_group] for g in range(0, clusters, per_group)]
-    write_payload(payload, [compress(group, basis, g) for g, group in enumerate(groups)], [])
+        tiles = [b[:, j * LANES : (j + 1) * LANES] for j in range(g * per_group, (g + 1) * per_group)]
+        rows = pl.ds(g * per_group * R, per_group * R)
+        field[rows, :] = jnp.concatenate(tiles, axis=0)
+        lowered[rows, :] = jnp.concatenate(tiles, axis=0).astype(bf16)
+        if g == 0:
+            whole_basis.wait()
+        parts.append(compress(tiles, basis, g))
+    write_payload(payload, parts, [])
 
 
 def window_place(distance, clusters, me):
@@ -116,7 +125,7 @@
 
 
 def prepare_kernel(
-    axis, size, near_cols_hbm, near_counts_hbm, far_cols_hbm, coupling_hbm, target_hbm, blocks_hbm, _,
+    axis, size, middle, near_cols_hbm, near_counts_hbm, far_cols_hbm, coupling_hbm, target_hbm, blocks_hbm, _,
     places, high_out, low_out, target_out, ahead, near_cols, near_counts, far_cols, coupling, target, sems,
 ):
     pairs = (
@@ -138,7 +147,9 @@
     places[:slots, :] = jnp.where(live, window_place(distance, clusters, me), 5 * clusters)
     owner = lax.div(far_cols[...], clusters)
     other_core = (owner ^ me) & 1
-    places[slots:, :] = (other_core * (size // 2) + owner // 2) * clusters + lax.rem(far_cols[...], clusters)
+    chips = size // 2
+    chip = lax.rem(owner // 2 + (chips - middle), chips)
+    places[slots:, :] = (other_core * chips + chip) * clusters + lax.rem(far_cols[...], clusters)
     for copy in copies[3:5]:
         copy.wait()
     slots, rank, _, clusters = coupling.shape
@@ -169,8 +180,8 @@
         )
         for c in range(chunks)
     ]
-    for copy in copies:
-        copy.start()
+    for c, copy in enumerate(copies):
+        copy.start(priority=c % 2)
     token[...] = jnp.zeros_like(token)
     for copy in copies:
         copy.wait()
@@ -328,7 +339,10 @@
         sums_out[device] = tile
 
 
-def finish_kernel(per_group, unknowns, b, image, candidate, sent, received, got, solution_out, next_out):
+def finish_kernel(
+    per_group, unknowns, b, image, candidate, sent, received, got, solution_hbm, next_hbm,
+    solution_here, next_here, sems,
+):
     clusters = b.shape[0] // R
     sums = read_sums(tails((sent, received), b.shape[0], clusters // per_group * R), 3, unknowns)
     start_norm, h11, h21, v11, v22, v12 = arnoldi_one(*sums)
@@ -343,12 +357,22 @@
     y1 = (g22 * t1 - g12 * t2) / det
     y2 = (g11 * t2 - g12 * t1) / det
     scale, inverse, last = 1.0 / start_norm, 1.0 / h21, 1.0 / h32
-    for j in range(clusters):
-        span = slice(j * LANES, (j + 1) * LANES)
-        first = rows_of(b, j) * scale
-        second = (rows_of(image, j) * scale - h11 * first) * inverse
-        solution_out[:, span] = y1 * first + y2 * second
-        next_out[:, span] = (rows_of(candidate, j) - h12 * first - h22 * second) * last
+    chunks = sems.shape[1]
+    each = clusters // chunks
+    copies = []
+    for c in range(chunks):
+        for j in range(c * each, (c + 1) * each):
+            span = slice(j * LANES, (j + 1) * LANES)
+            first = rows_of(b, j) * scale
+            second = (rows_of(image, j) * scale - h11 * first) * inverse
+            solution_here[:, span] = y1 * first + y2 * second
+            next_here[:, span] = (rows_of(candidate, j) - h12 * first - h22 * second) * last
+        span = pl.ds(c * each * LANES, each * LANES)
+        for n, (here, there) in enumerate(((solution_here, solution_hbm), (next_here, next_hbm))):
+            copies.append(pltpu.make_async_copy(here.at[:, span], there.at[:, span], sems.at[n, c]))
+            copies[-1].start()
+    for copy in copies:
+        copy.wait()
 
 
 def swapped(block, partner):
@@ -400,9 +424,17 @@
             scratch_shapes=scratch_shapes, compiler_params=PARAMS, name=name,
         )(*args)
 
+    chips = size // 2
+    middle = chips // 4
+    order = [(middle + n) % chips for n in range(chips)]
+
     def gather(block):
-        groups = [list(range(core, size, 2)) for core in range(2)]
+        groups = [[2 * chip + core for chip in order] for core in range(2)]
         return lax.all_to_all(block, "rows", 0, 0, axis_index_groups=groups)
+
+    def exchange(block):
+        group = [2 * chip + core for chip in order for core in range(2)]
+        return lax.all_to_all(block, "rows", 0, 0, axis_index_groups=[group])
 
     field, basis, lowered, payload = call(
         functools.partial(start_kernel, per_group), "start",
@@ -411,15 +443,15 @@
             shape(size // 2, head, LANES, dtype=bf16),
         ),
         [HBM] * 2, in_hbm(right_sides), in_hbm(basis_in.reshape(clusters * rank, LANES)),
-        scratch_shapes=[scratch(R, width), pltpu.SemaphoreType.DMA((2,))],
+        scratch_shapes=[scratch(R, width), pltpu.SemaphoreType.DMA((clusters // per_group + 1,))],
     )
     got = gather(payload)
     held = sends_of(lowered)
 
     blocks = in_hbm(near_blocks.reshape(clusters * slots, LANES, LANES))
-    early = blocks.shape[0] // 4
+    early = blocks.shape[0] * 9 // 32
     places, high, low, target, ahead = call(
-        functools.partial(prepare_kernel, "rows", size), "prepare",
+        functools.partial(prepare_kernel, "rows", size, middle), "prepare",
         (
             shape(2 * slots, clusters, dtype=jnp.int32),
             shape(slots * rank, rank * clusters, dtype=bf16),
@@ -465,17 +497,20 @@
         operands, *arrived(got, held, ahead, target), field, basis, scratch_shapes=kept,
     )
     got = gather(payload)
-    ahead, token = fetch("ahead", 0, early, 2, payload)
-    here = arrived(got, sends_of(lowered), ahead, token)
+    held = sends_of(lowered)
+    ahead, token = fetch("ahead", 0, early, 2, held[1])
+    here = arrived(got, held, ahead, token)
     candidate, sums = call(
         functools.partial(second_kernel, per_group, unknowns), "operator_two",
         (shape(rows, LANES), shape(size, R, LANES, dtype=bf16)),
         operands, *here, field, image, scratch_shapes=kept,
     )
-    return call(
-        functools.partial(finish_kernel, per_group, unknowns), "finish", (shape(R, width), shape(R, width)),
-        [VMEM] * 6, field, image, candidate, *here[7:9], lax.all_to_all(sums, "rows", 0, 0),
-    )
+    return pl.pallas_call(
+        functools.partial(finish_kernel, per_group, unknowns), out_shape=(shape(R, width), shape(R, width)),
+        in_specs=[VMEM] * 6, out_specs=[HBM] * 2,
+        scratch_shapes=[scratch(R, width), scratch(R, width), pltpu.SemaphoreType.DMA((2, 4))],
+        compiler_params=PARAMS, name="finish",
+    )(field, image, candidate, *here[7:9], exchange(sums))
 
 
 def solution(mesh):

time: 56.6 us -> 55.7 us (0.984)
  starting transfers between devices: 20.7 us -> 19 us
  local copies, waits for them, and re-layouts: 0 us -> 0.85 us
    ppermute x8, starting transfers between devices: 10 us -> 6.74 us  [swapped(): lax.ppermute(block, 'rows', [(i, partner(i)) for i in range(lax.axis_size...]
    all_to_all x2, starting transfers between devices: 10.7 us -> 12.3 us  [gather(): return lax.all_to_all(block, 'rows', 0, 0, axis_index_groups=groups)]
    pallas_call x0 -> x1, Pallas kernels: none -> 1.52 us  [on_device(): pl.pallas_call(functools.partial(finish_kernel, per_group, unknowns), out...]
    all_to_all x2, waiting for transfers between devices: 2 us -> 0.79 us  [gather(): return lax.all_to_all(block, 'rows', 0, 0, axis_index_groups=groups)]
    pallas_call x10 -> x9, Pallas kernels: 21.3 us -> 20.2 us  [call(): pl.pallas_call(kernel, out_shape=out, in_specs=ins, out_specs=jax.tree.ma...]
    ppermute x8, waiting for transfers between devices: 2.33 us -> 3.18 us  [swapped(): lax.ppermute(block, 'rows', [(i, partner(i)) for i in range(lax.axis_size...]
    unnamed x0 -> x4, local copies, waits for them, and re-layouts: none -> 0.85 us
  transfers between devices with their start and end apart: 10 -> 10, of which waited for: 4 -> 5; matrix products, arithmetic and copies ran while one was open for 0% -> 0% of each run, Pallas kernels for 17% -> 17%
where the time goes in v17:
time: 55.7 us; the launch traced here: 55.3 us
  Pallas kernels  21.8 us (39%)
  starting transfers between devices  19 us (34%)
  blocking collectives  8.98 us (16%)
  waiting for transfers between devices  3.97 us (7%)
  local copies, waits for them, and re-layouts  0.85 us (2%)
  between operations  0.74 us (1%)
    pallas_call x9, Pallas kernels, call(): pl.pallas_call(kernel, out_shape=out, in_specs=ins, out_specs=jax.tree.ma...  20.2 us
    all_to_all x2, starting transfers between devices, gather(): return lax.all_to_all(block, 'rows', 0, 0, axis_index_groups=groups)  12.3 us
    all_to_all x1, blocking collectives, exchange(): return lax.all_to_all(block, 'rows', 0, 0, axis_index_groups=[group])  8.98 us
    ppermute x8, starting transfers between devices, swapped(): lax.ppermute(block, 'rows', [(i, partner(i)) for i in range(lax.axis_size...  6.74 us
    ppermute x8, waiting for transfers between devices, swapped(): lax.ppermute(block, 'rows', [(i, partner(i)) for i in range(lax.axis_size...  3.18 us
    pallas_call x1, Pallas kernels, on_device(): pl.pallas_call(functools.partial(finish_kernel, per_group, unknowns), out...  1.52 us
  transfers between devices with their start and end apart: 10, of which 5 were waited for; matrix products, arithmetic and copies ran while one was open for 0% of the time, Pallas kernels for 17%

profile of v17, /device:TPU:0, one launch (start us, length us, event | category | flops | bytes accessed | tf_op | source)
XLA Modules:
  0.0 55.3 jit_solution(5928103440477325709)
XLA Ops:
  0.6 2.3 %start.1 = (f32[256,128]{1,0:T(8,128)S(1)}, bf16[512,128]{1,0:T(8,128)(2,1)S(1)}, bf16[256,128]{1,0:T(8,128)(2,1)S(1)}, bf16[8,32,128]{2,1,0:T(8,128)(2,1)}) custom-call(f32[8,4096]{1,0:T(8,128)} %b_hbm.1, bf16[512,128]{1,0:T(8,128)(2,1)} %bitcast.13), custom_call_target="tpu_custom_call" | custom-call | tf_op jit(solution)/shard_map/start/pallas_call | solution.py:422
  3.0 0.0 copy-start
  3.0 7.9 %all-to-all-start = ((bf16[8,32,128]{2,1,0:T(8,128)(2,1)}), bf16[8,32,128]{2,1,0:T(8,128)(2,1)S(1)}, u32[]{:S(2)}, u32[]{:S(2)}) async-start(bf16[8,32,128]{2,1,0:T(8,128)(2,1)} %get-tuple-element.26), calls=%async_computation | async-start | bytes 131072 | tf_op jit(solution)/shard_map/all_to_all | solution.py:433
  10.8 0.0 collective-permute-start
  10.8 3.3 %collective-permute-start.2 = (bf16[256,128]{1,0:T(8,128)(2,1)S(1)}, bf16[256,128]{1,0:T(8,128)(2,1)S(1)}, u32[]{:S(2)}, u32[]{:S(2)}) collective-permute-start(bf16[256,128]{1,0:T(8,128)(2,1)S(1)} %get-tuple-element.23.own), channel_id=1, source_target_pairs={{0,14},{1,15},{2,4},{3,5},{4,2},{5,3},{6,8},{7,9},{8,6},{9,7},{10,... | collective-permute-start | bytes 196616 | tf_op jit(solution)/shard_map/ppermute | solution.py:379
  14.1 2.1 %prepare.1 = (s32[16,32]{1,0:T(8,128)S(1)}, bf16[128,512]{1,0:T(8,128)(2,1)S(1)}, bf16[128,512]{1,0:T(8,128)(2,1)S(1)}, bf16[512,128]{1,0:T(8,128)(2,1)S(1)}, bf16[72,128,128]{2,1,0:T(8,128)(2,1)S(1)}) custom-call(s32[8,32]{1,0:T(8,128)} %bitcast.14, s32[1,32]{1,0:T(1,128)} %bitcast.16, s32[8,32]{1,0:T(8,128)} %bitcast.15, f32[8,16,16,32]{3,2,1,0:T(8,128)} %bitcast.11, ...), custom_call_target="tpu_custom_call" | custom-call | tf_op jit(solution)/shard_map/prepare/pallas_call | solution.py:422
  16.2 0.0 all-to-all-done.refs_0_.got
  16.3 2.8 %fetch.2 = (bf16[184,128,128]{2,1,0:T(8,128)(2,1)S(1)}, f32[8,128]{1,0:T(8,128)S(1)}) custom-call(bf16[256,128,128]{2,1,0:T(8,128)(2,1)} %bitcast.8, bf16[8,32,128]{2,1,0:T(8,128)(2,1)S(1)} %all-to-all-done.refs_0_.got, bf16[512,128]{1,0:T(8,128)(2,1)S(1)} %get-tuple-element.27.refs_1_.target), custom_call_target="tpu_custom_call" | custom-call | tf_op jit(solution)/shard_map/fetch/pallas_call | solution.py:422
  19.1 0.4 collective-permute-done.1.even
  19.5 0.1 collective-permute-start.3
  19.6 1.3 %collective-permute-done.3.received = bf16[512,128]{1,0:T(8,128)(2,1)S(1)} collective-permute-done((bf16[512,128]{1,0:T(8,128)(2,1)S(1)}, bf16[512,128]{1,0:T(8,128)(2,1)S(1)}, u32[]{:S(2)}, u32[]{:S(2)}) %collective-permute-start.3) | collective-permute-done | bytes 131104 | tf_op jit(solution)/shard_map/ppermute | solution.py:379
  20.9 0.8 %copy-done.1 = bf16[256,128]{1,0:T(8,128)(2,1)S(1)} copy-done((bf16[256,128]{1,0:T(8,128)(2,1)S(1)}, bf16[256,128]{1,0:T(8,128)(2,1)}, u32[]{:S(2)}) %copy-start.1) | copy-done | bytes 65560
  21.7 4.7 %operator_one.1 = (f32[256,128]{1,0:T(8,128)S(1)}, bf16[256,128]{1,0:T(8,128)(2,1)S(1)}, bf16[8,48,128]{2,1,0:T(8,128)(2,1)}) custom-call(bf16[256,128]{1,0:T(8,128)(2,1)S(1)} %copy-done.1, bf16[256,128]{1,0:T(8,128)(2,1)S(1)} %collective-permute-done._.mate, bf16[256,128]{1,0:T(8,128)(2,1)S(1)} %collective-permute-done.1.even, ...), custom_call_target="tpu_custom_call" | custom-call | tf_op jit(solution)/shard_map/operator_one/pallas_call | solution.py:422
  26.4 4.4 %all-to-all-start.1 = ((bf16[8,48,128]{2,1,0:T(8,128)(2,1)}), bf16[8,48,128]{2,1,0:T(8,128)(2,1)S(1)}, u32[]{:S(2)}, u32[]{:S(2)}) async-start(bf16[8,48,128]{2,1,0:T(8,128)(2,1)} %get-tuple-element.36), calls=%async_computation.1 | async-start | bytes 196608 | tf_op jit(solution)/shard_map/all_to_all | solution.py:433
  30.8 3.3 %collective-permute-start.6 = (bf16[256,128]{1,0:T(8,128)(2,1)S(1)}, bf16[256,128]{1,0:T(8,128)(2,1)S(1)}, u32[]{:S(2)}, u32[]{:S(2)}) collective-permute-start(bf16[256,128]{1,0:T(8,128)(2,1)S(1)} %get-tuple-element.34.own), channel_id=1, source_target_pairs={{0,14},{1,15},{2,4},{3,5},{4,2},{5,3},{6,8},{7,9},{8,6},{9,7},{10,... | collective-permute-start | bytes 196616 | tf_op jit(solution)/shard_map/ppermute | solution.py:379
  34.0 1.6 %ahead.1 = (bf16[72,128,128]{2,1,0:T(8,128)(2,1)S(1)}, f32[8,128]{1,0:T(8,128)S(1)}) custom-call(bf16[256,128,128]{2,1,0:T(8,128)(2,1)} %bitcast.9, bf16[256,128]{1,0:T(8,128)(2,1)S(1)} %collective-permute-done.4.refs_0_.mate), custom_call_target="tpu_custom_call" | custom-call | tf_op jit(solution)/shard_map/ahead/pallas_call | solution.py:422
  35.7 0.7 %all-to-all-done.1.refs_0_.got = bf16[8,48,128]{2,1,0:T(8,128)(2,1)S(1)} async-done(((bf16[8,48,128]{2,1,0:T(8,128)(2,1)}), bf16[8,48,128]{2,1,0:T(8,128)(2,1)S(1)}, u32[]{:S(2)}, u32[]{:S(2)}) %all-to-all-start.1) | async-done | bytes 98336 | tf_op jit(solution)/shard_map/all_to_all | solution.py:433
  36.4 2.8 %fetch.3 = (bf16[184,128,128]{2,1,0:T(8,128)(2,1)S(1)}, f32[8,128]{1,0:T(8,128)S(1)}) custom-call(bf16[256,128,128]{2,1,0:T(8,128)(2,1)} %bitcast.10, bf16[8,48,128]{2,1,0:T(8,128)(2,1)S(1)} %all-to-all-done.1.refs_0_.got, f32[8,128]{1,0:T(8,128)S(1)} %get-tuple-element.37.refs_1_), custom_call_target="tpu_custom_call" | custom-call | tf_op jit(solution)/shard_map/fetch/pallas_call | solution.py:422
  39.2 0.2 collective-permute-done.5.even
  39.4 0.1 collective-permute-start.7
  39.5 1.4 %collective-permute-done.7.received = bf16[640,128]{1,0:T(8,128)(2,1)S(1)} collective-permute-done((bf16[640,128]{1,0:T(8,128)(2,1)S(1)}, bf16[640,128]{1,0:T(8,128)(2,1)S(1)}, u32[]{:S(2)}, u32[]{:S(2)}) %collective-permute-start.7) | collective-permute-done | bytes 163872 | tf_op jit(solution)/shard_map/ppermute | solution.py:379
  40.9 3.9 %operator_two.1 = (f32[256,128]{1,0:T(8,128)S(1)}, bf16[16,8,128]{2,1,0:T(8,128)(2,1)S(1)}) custom-call(bf16[256,128]{1,0:T(8,128)(2,1)S(1)} %get-tuple-element.34.own, bf16[256,128]{1,0:T(8,128)(2,1)S(1)} %collective-permute-done.4.refs_0_.mate, bf16[256,128]{1,0:T(8,128)(2,1)S(1)} %collective-permute-done.5.even, ...), custom_call_target="tpu_custom_call" | custom-call | tf_op jit(solution)/shard_map/operator_two/pallas_call | solution.py:422
  44.8 9.0 %all_to_all.15.got = bf16[16,8,128]{2,1,0:T(8,128)(2,1)S(1)} all-to-all(bf16[16,8,128]{2,1,0:T(8,128)(2,1)S(1)} %get-tuple-element.41), channel_id=1, replica_groups={{4,5,6,7,8,9,10,11,12,13,14,15,0,1,2,3},{20,21,22,23,24,25,26,27,28,29,..., dimensions={0} | all-to-all | bytes 65536 | tf_op jit(solution)/shard_map/all_to_all | solution.py:437
  53.8 1.5 %finish.1 = (f32[8,4096]{1,0:T(8,128)}, f32[8,4096]{1,0:T(8,128)}) custom-call(f32[256,128]{1,0:T(8,128)S(1)} %get-tuple-element.22.b, f32[256,128]{1,0:T(8,128)S(1)} %get-tuple-element.33.image, f32[256,128]{1,0:T(8,128)S(1)} %get-tuple-element.40.candidate, bf16[640,128]{1,0:T(8,128)(2,1)S(1)} %relay.3.sent, ...), custom_call_target="tpu_custom_call" | custom-call | tf_op jit(solution)/shard_map/finish/pallas_call | solution.py:508
  (11 shorter events, 0.0 us)
Async XLA Ops:
  3.0 16.1 %copy-start = (bf16[256,128]{1,0:T(8,128)(2,1)}, bf16[256,128]{1,0:T(8,128)(2,1)S(1)}, u32[]{:S(2)}) copy-start(bf16[256,128]{1,0:T(8,128)(2,1)S(1)} %get-tuple-element.23.own) | copy-start | bytes 196612
  3.0 13.3 %all-to-all-start = ((bf16[8,32,128]{2,1,0:T(8,128)(2,1)}), bf16[8,32,128]{2,1,0:T(8,128)(2,1)S(1)}, u32[]{:S(2)}, u32[]{:S(2)}) async-start(bf16[8,32,128]{2,1,0:T(8,128)(2,1)} %get-tuple-element.26), calls=%async_computation | async-start | bytes 131072 | tf_op jit(solution)/shard_map/all_to_all | solution.py:433
  10.8 3.3 %collective-permute-start = (bf16[256,128]{1,0:T(8,128)(2,1)S(1)}, bf16[256,128]{1,0:T(8,128)(2,1)S(1)}, u32[]{:S(2)}, u32[]{:S(2)}) collective-permute-start(bf16[256,128]{1,0:T(8,128)(2,1)S(1)} %get-tuple-element.23.own), channel_id=1, source_target_pairs={{0,1},{1,0},{2,3},{3,2},{4,5},{5,4},{6,7},{7,6},{8,9},{9,8},{10,11... | collective-permute-start | bytes 196616 | tf_op jit(solution)/shard_map/ppermute | solution.py:379
  10.8 8.2 %collective-permute-start.2 = (bf16[256,128]{1,0:T(8,128)(2,1)S(1)}, bf16[256,128]{1,0:T(8,128)(2,1)S(1)}, u32[]{:S(2)}, u32[]{:S(2)}) collective-permute-start(bf16[256,128]{1,0:T(8,128)(2,1)S(1)} %get-tuple-element.23.own), channel_id=1, source_target_pairs={{0,14},{1,15},{2,4},{3,5},{4,2},{5,3},{6,8},{7,9},{8,6},{9,7},{10,... | collective-permute-start | bytes 196616 | tf_op jit(solution)/shard_map/ppermute | solution.py:379
  14.1 5.3 %collective-permute-start.1 = (bf16[256,128]{1,0:T(8,128)(2,1)S(1)}, bf16[256,128]{1,0:T(8,128)(2,1)S(1)}, u32[]{:S(2)}, u32[]{:S(2)}) collective-permute-start(bf16[256,128]{1,0:T(8,128)(2,1)S(1)} %get-tuple-element.23.own), channel_id=1, source_target_pairs={{0,2},{1,3},{2,0},{3,1},{4,6},{5,7},{6,4},{7,5},{8,10},{9,11},{10,... | collective-permute-start | bytes 196616 | tf_op jit(solution)/shard_map/ppermute | solution.py:379
  19.5 1.4 %collective-permute-start.3 = (bf16[512,128]{1,0:T(8,128)(2,1)S(1)}, bf16[512,128]{1,0:T(8,128)(2,1)S(1)}, u32[]{:S(2)}, u32[]{:S(2)}) collective-permute-start(bf16[512,128]{1,0:T(8,128)(2,1)S(1)} %relay.2.sent), channel_id=1, source_target_pairs={{0,1},{1,0},{2,3},{3,2},{4,5},{5,4},{6,7},{7,6},{8,9},{9,8},{10,11... | collective-permute-start | bytes 393224 | tf_op jit(solution)/shard_map/ppermute | solution.py:379
  20.9 0.8 %copy-start.1 = (bf16[256,128]{1,0:T(8,128)(2,1)S(1)}, bf16[256,128]{1,0:T(8,128)(2,1)}, u32[]{:S(2)}) copy-start(bf16[256,128]{1,0:T(8,128)(2,1)} %copy-done) | copy-start | bytes 196612
  26.4 10.1 %all-to-all-start.1 = ((bf16[8,48,128]{2,1,0:T(8,128)(2,1)}), bf16[8,48,128]{2,1,0:T(8,128)(2,1)S(1)}, u32[]{:S(2)}, u32[]{:S(2)}) async-start(bf16[8,48,128]{2,1,0:T(8,128)(2,1)} %get-tuple-element.36), calls=%async_computation.1 | async-start | bytes 196608 | tf_op jit(solution)/shard_map/all_to_all | solution.py:433
  30.8 3.3 %collective-permute-start.4 = (bf16[256,128]{1,0:T(8,128)(2,1)S(1)}, bf16[256,128]{1,0:T(8,128)(2,1)S(1)}, u32[]{:S(2)}, u32[]{:S(2)}) collective-permute-start(bf16[256,128]{1,0:T(8,128)(2,1)S(1)} %get-tuple-element.34.own), channel_id=1, source_target_pairs={{0,1},{1,0},{2,3},{3,2},{4,5},{5,4},{6,7},{7,6},{8,9},{9,8},{10,11... | collective-permute-start | bytes 196616 | tf_op jit(solution)/shard_map/ppermute | solution.py:379
  30.8 8.4 %collective-permute-start.6 = (bf16[256,128]{1,0:T(8,128)(2,1)S(1)}, bf16[256,128]{1,0:T(8,128)(2,1)S(1)}, u32[]{:S(2)}, u32[]{:S(2)}) collective-permute-start(bf16[256,128]{1,0:T(8,128)(2,1)S(1)} %get-tuple-element.34.own), channel_id=1, source_target_pairs={{0,14},{1,15},{2,4},{3,5},{4,2},{5,3},{6,8},{7,9},{8,6},{9,7},{10,... | collective-permute-start | bytes 196616 | tf_op jit(solution)/shard_map/ppermute | solution.py:379
  34.0 5.3 %collective-permute-start.5 = (bf16[256,128]{1,0:T(8,128)(2,1)S(1)}, bf16[256,128]{1,0:T(8,128)(2,1)S(1)}, u32[]{:S(2)}, u32[]{:S(2)}) collective-permute-start(bf16[256,128]{1,0:T(8,128)(2,1)S(1)} %get-tuple-element.34.own), channel_id=1, source_target_pairs={{0,2},{1,3},{2,0},{3,1},{4,6},{5,7},{6,4},{7,5},{8,10},{9,11},{10,... | collective-permute-start | bytes 196616 | tf_op jit(solution)/shard_map/ppermute | solution.py:379
  39.4 1.5 %collective-permute-start.7 = (bf16[640,128]{1,0:T(8,128)(2,1)S(1)}, bf16[640,128]{1,0:T(8,128)(2,1)S(1)}, u32[]{:S(2)}, u32[]{:S(2)}) collective-permute-start(bf16[640,128]{1,0:T(8,128)(2,1)S(1)} %relay.3.sent), channel_id=1, source_target_pairs={{0,1},{1,0},{2,3},{3,2},{4,5},{5,4},{6,7},{7,6},{8,9},{9,8},{10,11... | collective-permute-start | bytes 491528 | tf_op jit(solution)/shard_map/ppermute | solution.py:379

commit v18 on v16

--- a/solution.py
+++ b/solution.py
@@ -116,7 +116,7 @@
 
 
 def prepare_kernel(
-    axis, size, near_cols_hbm, near_counts_hbm, far_cols_hbm, coupling_hbm, target_hbm, blocks_hbm, _,
+    axis, size, middle, near_cols_hbm, near_counts_hbm, far_cols_hbm, coupling_hbm, target_hbm, blocks_hbm, _,
     places, high_out, low_out, target_out, ahead, near_cols, near_counts, far_cols, coupling, target, sems,
 ):
     pairs = (
@@ -138,7 +138,9 @@
     places[:slots, :] = jnp.where(live, window_place(distance, clusters, me), 5 * clusters)
     owner = lax.div(far_cols[...], clusters)
     other_core = (owner ^ me) & 1
-    places[slots:, :] = (other_core * (size // 2) + owner // 2) * clusters + lax.rem(far_cols[...], clusters)
+    chips = size // 2
+    chip = lax.rem(owner // 2 + (chips - middle), chips)
+    places[slots:, :] = (other_core * chips + chip) * clusters + lax.rem(far_cols[...], clusters)
     for copy in copies[3:5]:
         copy.wait()
     slots, rank, _, clusters = coupling.shape
@@ -159,8 +161,7 @@
     copies[5].wait()
 
 
-def fetch_kernel(first, blocks_hbm, *refs):
-    *_, blocks, token, sems = refs
+def fetch_kernel(first, blocks_hbm, _, __, blocks, token, sems):
     chunks = sems.shape[0]
     each = blocks.shape[0] // chunks
     copies = [
@@ -228,15 +229,13 @@
 
     picked = []
     for i in range(0, clusters, 2):
-        both = jnp.zeros((2 * R, 2 * LANES), f32)
-        for k in range(0, slots, 2):
-            sources = jnp.concatenate(
-                [jnp.concatenate([fetch(k + n, i), fetch(k + n, i + 1)], axis=0) for n in range(2)], axis=1
-            )
-            weights = jnp.concatenate(
-                [jnp.concatenate([block(k + n, i), block(k + n, i + 1)], axis=0) for n in range(2)], axis=1
-            )
-            both = both + dot(sources.astype(bf16), weights, (1, 1))
+        sources = jnp.concatenate(
+            [jnp.concatenate([fetch(k, i), fetch(k, i + 1)], axis=0) for k in range(slots)], axis=1
+        )
+        weights = jnp.concatenate(
+            [jnp.concatenate([block(k, i), block(k, i + 1)], axis=0) for k in range(slots)], axis=1
+        )
+        both = dot(sources.astype(bf16), weights, (1, 1))
         near[pl.ds(i * R, R), :] = both[:R, :LANES]
         near[pl.ds((i + 1) * R, R), :] = both[R:, LANES:]
         if 2 * i < clusters:
@@ -400,9 +399,17 @@
             scratch_shapes=scratch_shapes, compiler_params=PARAMS, name=name,
         )(*args)
 
+    chips = size // 2
+    middle = chips // 4
+    order = [(middle + n) % chips for n in range(chips)]
+
     def gather(block):
-        groups = [list(range(core, size, 2)) for core in range(2)]
+        groups = [[2 * chip + core for chip in order] for core in range(2)]
         return lax.all_to_all(block, "rows", 0, 0, axis_index_groups=groups)
+
+    def exchange(block):
+        group = [2 * chip + core for chip in order for core in range(2)]
+        return lax.all_to_all(block, "rows", 0, 0, axis_index_groups=[group])
 
     field, basis, lowered, payload = call(
         functools.partial(start_kernel, per_group), "start",
@@ -419,7 +426,7 @@
     blocks = in_hbm(near_blocks.reshape(clusters * slots, LANES, LANES))
     early = blocks.shape[0] // 4
     places, high, low, target, ahead = call(
-        functools.partial(prepare_kernel, "rows", size), "prepare",
+        functools.partial(prepare_kernel, "rows", size, middle), "prepare",
         (
             shape(2 * slots, clusters, dtype=jnp.int32),
             shape(slots * rank, rank * clusters, dtype=bf16),
@@ -438,15 +445,13 @@
         ],
     )
 
-    def fetch(name, first, count, chunks, *behind):
-        here, token = call(
-            functools.partial(fetch_kernel, first), name, (pltpu.VMEM((count, LANES, LANES), bf16), shape(R, LANES)),
-            [HBM] + [ANY] * len(behind), blocks, *behind, scratch_shapes=[pltpu.SemaphoreType.DMA((chunks,))],
+    def arrived(got, held, behind):
+        rest, token = call(
+            functools.partial(fetch_kernel, early), "fetch",
+            (pltpu.VMEM((blocks.shape[0] - early, LANES, LANES), bf16), shape(R, LANES)),
+            [HBM] + [ANY] * 2, blocks, got, behind, scratch_shapes=[pltpu.SemaphoreType.DMA((8,))],
         )
-        return pltpu.with_memory_space_constraint(here, pltpu.VMEM), token
-
-    def arrived(got, held, ahead, behind):
-        rest, token = fetch("fetch", early, blocks.shape[0] - early, 8, got, behind)
+        rest = pltpu.with_memory_space_constraint(rest, pltpu.VMEM)
         sent = call(
             functools.partial(relay_kernel, "rows"), "relay",
             shape(got.shape[0] * got.shape[1] + rows, LANES, dtype=bf16), [VMEM] * 3 + [ANY], got, *held[2:], token
@@ -462,11 +467,11 @@
             shape(rows, LANES), shape(rows, LANES, dtype=bf16),
             shape(size // 2, head + TAIL, LANES, dtype=bf16),
         ),
-        operands, *arrived(got, held, ahead, target), field, basis, scratch_shapes=kept,
+        operands, *arrived(got, held, target), field, basis, scratch_shapes=kept,
     )
     got = gather(payload)
-    ahead, token = fetch("ahead", 0, early, 2, payload)
-    here = arrived(got, sends_of(lowered), ahead, token)
+    held = sends_of(lowered)
+    here = arrived(got, held, held[1])
     candidate, sums = call(
         functools.partial(second_kernel, per_group, unknowns), "operator_two",
         (shape(rows, LANES), shape(size, R, LANES, dtype=bf16)),
@@ -474,7 +479,7 @@
     )
     return call(
         functools.partial(finish_kernel, per_group, unknowns), "finish", (shape(R, width), shape(R, width)),
-        [VMEM] * 6, field, image, candidate, *here[7:9], lax.all_to_all(sums, "rows", 0, 0),
+        [VMEM] * 6, field, image, candidate, *here[7:9], exchange(sums),
     )
 
 

time: 56.6 us -> 54.1 us (0.956)
  starting transfers between devices: 20.7 us -> 19 us
  Pallas kernels: 21.3 us -> 19.7 us
  waiting for transfers between devices: 4.33 us -> 5.55 us
    ppermute x8, starting transfers between devices: 10 us -> 6.74 us  [swapped(): lax.ppermute(block, 'rows', [(i, partner(i)) for i in range(lax.axis_size...]
    pallas_call x10 -> x9, Pallas kernels: 21.3 us -> 19.7 us  [call(): pl.pallas_call(kernel, out_shape=out, in_specs=ins, out_specs=jax.tree.ma...]
    all_to_all x2, starting transfers between devices: 10.7 us -> 12.3 us  [gather(): return lax.all_to_all(block, 'rows', 0, 0, axis_index_groups=groups)]
    ppermute x8, waiting for transfers between devices: 2.33 us -> 3.03 us  [swapped(): lax.ppermute(block, 'rows', [(i, partner(i)) for i in range(lax.axis_size...]
  transfers between devices with their start and end apart: 10 -> 10, of which waited for: 4 -> 6; matrix products, arithmetic and copies ran while one was open for 0% -> 0% of each run, Pallas kernels for 17% -> 14%
where the time goes in v18:
time: 54.1 us; the launch traced here: 53.7 us
  Pallas kernels  19.7 us (36%)
  starting transfers between devices  19 us (35%)
  blocking collectives  8.78 us (16%)
  waiting for transfers between devices  5.55 us (10%)
  between operations  0.71 us (1%)
    pallas_call x9, Pallas kernels, call(): pl.pallas_call(kernel, out_shape=out, in_specs=ins, out_specs=jax.tree.ma...  19.7 us
    all_to_all x2, starting transfers between devices, gather(): return lax.all_to_all(block, 'rows', 0, 0, axis_index_groups=groups)  12.3 us
    all_to_all x1, blocking collectives, exchange(): return lax.all_to_all(block, 'rows', 0, 0, axis_index_groups=[group])  8.78 us
    ppermute x8, starting transfers between devices, swapped(): lax.ppermute(block, 'rows', [(i, partner(i)) for i in range(lax.axis_size...  6.74 us
    ppermute x8, waiting for transfers between devices, swapped(): lax.ppermute(block, 'rows', [(i, partner(i)) for i in range(lax.axis_size...  3.03 us
    all_to_all x2, waiting for transfers between devices, gather(): return lax.all_to_all(block, 'rows', 0, 0, axis_index_groups=groups)  2.51 us
  transfers between devices with their start and end apart: 10, of which 6 were waited for; matrix products, arithmetic and copies ran while one was open for 0% of the time, Pallas kernels for 14%

profile of v18, /device:TPU:0, one launch (start us, length us, event | category | flops | bytes accessed | tf_op | source)
XLA Modules:
  0.0 53.7 jit_solution(4011704729921481023)
XLA Ops:
  0.6 1.8 %start.1 = (f32[256,128]{1,0:T(8,128)S(1)}, bf16[512,128]{1,0:T(8,128)(2,1)S(1)}, bf16[256,128]{1,0:T(8,128)(2,1)S(1)}, bf16[8,32,128]{2,1,0:T(8,128)(2,1)}) custom-call(f32[8,4096]{1,0:T(8,128)} %b_hbm.1, bf16[512,128]{1,0:T(8,128)(2,1)} %bitcast.12), custom_call_target="tpu_custom_call" | custom-call | tf_op jit(solution)/shard_map/start/pallas_call | solution.py:397
  2.5 7.9 %all-to-all-start = ((bf16[8,32,128]{2,1,0:T(8,128)(2,1)}), bf16[8,32,128]{2,1,0:T(8,128)(2,1)S(1)}, u32[]{:S(2)}, u32[]{:S(2)}) async-start(bf16[8,32,128]{2,1,0:T(8,128)(2,1)} %get-tuple-element.24), calls=%async_computation | async-start | bytes 131072 | tf_op jit(solution)/shard_map/all_to_all | solution.py:408
  10.3 0.0 collective-permute-start
  10.3 3.3 %collective-permute-start.2 = (bf16[256,128]{1,0:T(8,128)(2,1)S(1)}, bf16[256,128]{1,0:T(8,128)(2,1)S(1)}, u32[]{:S(2)}, u32[]{:S(2)}) collective-permute-start(bf16[256,128]{1,0:T(8,128)(2,1)S(1)} %get-tuple-element.21.own), channel_id=1, source_target_pairs={{0,14},{1,15},{2,4},{3,5},{4,2},{5,3},{6,8},{7,9},{8,6},{9,7},{10,... | collective-permute-start | bytes 196616 | tf_op jit(solution)/shard_map/ppermute | solution.py:354
  13.6 2.0 %prepare.1 = (s32[16,32]{1,0:T(8,128)S(1)}, bf16[128,512]{1,0:T(8,128)(2,1)S(1)}, bf16[128,512]{1,0:T(8,128)(2,1)S(1)}, bf16[512,128]{1,0:T(8,128)(2,1)S(1)}, bf16[64,128,128]{2,1,0:T(8,128)(2,1)S(1)}) custom-call(s32[8,32]{1,0:T(8,128)} %bitcast.13, s32[1,32]{1,0:T(1,128)} %bitcast.15, s32[8,32]{1,0:T(8,128)} %bitcast.14, f32[8,16,16,32]{3,2,1,0:T(8,128)} %bitcast.10, ...), custom_call_target="tpu_custom_call" | custom-call | tf_op jit(solution)/shard_map/prepare/pallas_call | solution.py:397
  15.7 0.1 all-to-all-done._.got
  15.8 2.9 %fetch.2 = (bf16[192,128,128]{2,1,0:T(8,128)(2,1)S(1)}, f32[8,128]{1,0:T(8,128)S(1)}) custom-call(bf16[256,128,128]{2,1,0:T(8,128)(2,1)} %bitcast.8, bf16[8,32,128]{2,1,0:T(8,128)(2,1)S(1)} %all-to-all-done._.got, bf16[512,128]{1,0:T(8,128)(2,1)S(1)} %get-tuple-element.25.__.target), custom_call_target="tpu_custom_call" | custom-call | tf_op jit(solution)/shard_map/fetch/pallas_call | solution.py:397
  18.6 0.0 collective-permute-done.2.odd
  18.6 0.3 collective-permute-done.1.even
  19.0 0.1 collective-permute-start.3
  19.1 1.3 %collective-permute-done.3.received = bf16[512,128]{1,0:T(8,128)(2,1)S(1)} collective-permute-done((bf16[512,128]{1,0:T(8,128)(2,1)S(1)}, bf16[512,128]{1,0:T(8,128)(2,1)S(1)}, u32[]{:S(2)}, u32[]{:S(2)}) %collective-permute-start.3) | collective-permute-done | bytes 131104 | tf_op jit(solution)/shard_map/ppermute | solution.py:354
  20.4 4.7 %operator_one.1 = (f32[256,128]{1,0:T(8,128)S(1)}, bf16[256,128]{1,0:T(8,128)(2,1)S(1)}, bf16[8,48,128]{2,1,0:T(8,128)(2,1)}) custom-call(bf16[256,128]{1,0:T(8,128)(2,1)S(1)} %get-tuple-element.21.own, bf16[256,128]{1,0:T(8,128)(2,1)S(1)} %collective-permute-done._.mate, bf16[256,128]{1,0:T(8,128)(2,1)S(1)} %collective-permute-done.1.even, ...), custom_call_target="tpu_custom_call" | custom-call | tf_op jit(solution)/shard_map/operator_one/pallas_call | solution.py:397
  25.0 4.4 %all-to-all-start.1 = ((bf16[8,48,128]{2,1,0:T(8,128)(2,1)}), bf16[8,48,128]{2,1,0:T(8,128)(2,1)S(1)}, u32[]{:S(2)}, u32[]{:S(2)}) async-start(bf16[8,48,128]{2,1,0:T(8,128)(2,1)} %get-tuple-element.33), calls=%async_computation.1 | async-start | bytes 196608 | tf_op jit(solution)/shard_map/all_to_all | solution.py:408
  29.4 0.0 collective-permute-start.4
  29.4 3.3 %collective-permute-start.6 = (bf16[256,128]{1,0:T(8,128)(2,1)S(1)}, bf16[256,128]{1,0:T(8,128)(2,1)S(1)}, u32[]{:S(2)}, u32[]{:S(2)}) collective-permute-start(bf16[256,128]{1,0:T(8,128)(2,1)S(1)} %get-tuple-element.32.own), channel_id=1, source_target_pairs={{0,14},{1,15},{2,4},{3,5},{4,2},{5,3},{6,8},{7,9},{8,6},{9,7},{10,... | collective-permute-start | bytes 196616 | tf_op jit(solution)/shard_map/ppermute | solution.py:354
  32.7 2.4 %all-to-all-done.1._.got = bf16[8,48,128]{2,1,0:T(8,128)(2,1)S(1)} async-done(((bf16[8,48,128]{2,1,0:T(8,128)(2,1)}), bf16[8,48,128]{2,1,0:T(8,128)(2,1)S(1)}, u32[]{:S(2)}, u32[]{:S(2)}) %all-to-all-start.1) | async-done | bytes 98336 | tf_op jit(solution)/shard_map/all_to_all | solution.py:408
  35.1 2.9 %fetch.3 = (bf16[192,128,128]{2,1,0:T(8,128)(2,1)S(1)}, f32[8,128]{1,0:T(8,128)S(1)}) custom-call(bf16[256,128,128]{2,1,0:T(8,128)(2,1)} %bitcast.9, bf16[8,48,128]{2,1,0:T(8,128)(2,1)S(1)} %all-to-all-done.1._.got, bf16[256,128]{1,0:T(8,128)(2,1)S(1)} %collective-permute-done.4.__.mate), custom_call_target="tpu_custom_call" | custom-call | tf_op jit(solution)/shard_map/fetch/pallas_call | solution.py:397
  38.0 0.0 collective-permute-done.6.odd
  38.0 0.1 collective-permute-done.5.even
  38.1 0.1 collective-permute-start.7
  38.2 1.4 %collective-permute-done.7.received = bf16[640,128]{1,0:T(8,128)(2,1)S(1)} collective-permute-done((bf16[640,128]{1,0:T(8,128)(2,1)S(1)}, bf16[640,128]{1,0:T(8,128)(2,1)S(1)}, u32[]{:S(2)}, u32[]{:S(2)}) %collective-permute-start.7) | collective-permute-done | bytes 163872 | tf_op jit(solution)/shard_map/ppermute | solution.py:354
  39.5 3.9 %operator_two.1 = (f32[256,128]{1,0:T(8,128)S(1)}, bf16[16,8,128]{2,1,0:T(8,128)(2,1)S(1)}) custom-call(bf16[256,128]{1,0:T(8,128)(2,1)S(1)} %get-tuple-element.32.own, bf16[256,128]{1,0:T(8,128)(2,1)S(1)} %collective-permute-done.4.__.mate, bf16[256,128]{1,0:T(8,128)(2,1)S(1)} %collective-permute-done.5.even, ...), custom_call_target="tpu_custom_call" | custom-call | tf_op jit(solution)/shard_map/operator_two/pallas_call | solution.py:397
  43.4 8.8 %all_to_all.15.got = bf16[16,8,128]{2,1,0:T(8,128)(2,1)S(1)} all-to-all(bf16[16,8,128]{2,1,0:T(8,128)(2,1)S(1)} %get-tuple-element.37), channel_id=1, replica_groups={{4,5,6,7,8,9,10,11,12,13,14,15,0,1,2,3},{20,21,22,23,24,25,26,27,28,29,..., dimensions={0} | all-to-all | bytes 65536 | tf_op jit(solution)/shard_map/all_to_all | solution.py:412
  52.2 1.5 %finish.1 = (f32[8,4096]{1,0:T(8,128)}, f32[8,4096]{1,0:T(8,128)}) custom-call(f32[256,128]{1,0:T(8,128)S(1)} %get-tuple-element.20.b, f32[256,128]{1,0:T(8,128)S(1)} %get-tuple-element.31.image, f32[256,128]{1,0:T(8,128)S(1)} %get-tuple-element.36.candidate, bf16[640,128]{1,0:T(8,128)(2,1)S(1)} %relay.3.sent, ...), custom_call_target="tpu_custom_call" | custom-call | tf_op jit(solution)/shard_map/finish/pallas_call | solution.py:397
  (6 shorter events, 0.0 us)
Async XLA Ops:
  2.5 13.3 %all-to-all-start = ((bf16[8,32,128]{2,1,0:T(8,128)(2,1)}), bf16[8,32,128]{2,1,0:T(8,128)(2,1)S(1)}, u32[]{:S(2)}, u32[]{:S(2)}) async-start(bf16[8,32,128]{2,1,0:T(8,128)(2,1)} %get-tuple-element.24), calls=%async_computation | async-start | bytes 131072 | tf_op jit(solution)/shard_map/all_to_all | solution.py:408
  10.3 3.3 %collective-permute-start = (bf16[256,128]{1,0:T(8,128)(2,1)S(1)}, bf16[256,128]{1,0:T(8,128)(2,1)S(1)}, u32[]{:S(2)}, u32[]{:S(2)}) collective-permute-start(bf16[256,128]{1,0:T(8,128)(2,1)S(1)} %get-tuple-element.21.own), channel_id=1, source_target_pairs={{0,1},{1,0},{2,3},{3,2},{4,5},{5,4},{6,7},{7,6},{8,9},{9,8},{10,11... | collective-permute-start | bytes 196616 | tf_op jit(solution)/shard_map/ppermute | solution.py:354
  10.3 8.3 %collective-permute-start.2 = (bf16[256,128]{1,0:T(8,128)(2,1)S(1)}, bf16[256,128]{1,0:T(8,128)(2,1)S(1)}, u32[]{:S(2)}, u32[]{:S(2)}) collective-permute-start(bf16[256,128]{1,0:T(8,128)(2,1)S(1)} %get-tuple-element.21.own), channel_id=1, source_target_pairs={{0,14},{1,15},{2,4},{3,5},{4,2},{5,3},{6,8},{7,9},{8,6},{9,7},{10,... | collective-permute-start | bytes 196616 | tf_op jit(solution)/shard_map/ppermute | solution.py:354
  13.6 5.3 %collective-permute-start.1 = (bf16[256,128]{1,0:T(8,128)(2,1)S(1)}, bf16[256,128]{1,0:T(8,128)(2,1)S(1)}, u32[]{:S(2)}, u32[]{:S(2)}) collective-permute-start(bf16[256,128]{1,0:T(8,128)(2,1)S(1)} %get-tuple-element.21.own), channel_id=1, source_target_pairs={{0,2},{1,3},{2,0},{3,1},{4,6},{5,7},{6,4},{7,5},{8,10},{9,11},{10,... | collective-permute-start | bytes 196616 | tf_op jit(solution)/shard_map/ppermute | solution.py:354
  19.0 1.4 %collective-permute-start.3 = (bf16[512,128]{1,0:T(8,128)(2,1)S(1)}, bf16[512,128]{1,0:T(8,128)(2,1)S(1)}, u32[]{:S(2)}, u32[]{:S(2)}) collective-permute-start(bf16[512,128]{1,0:T(8,128)(2,1)S(1)} %relay.2.sent), channel_id=1, source_target_pairs={{0,1},{1,0},{2,3},{3,2},{4,5},{5,4},{6,7},{7,6},{8,9},{9,8},{10,11... | collective-permute-start | bytes 393224 | tf_op jit(solution)/shard_map/ppermute | solution.py:354
  25.0 10.1 %all-to-all-start.1 = ((bf16[8,48,128]{2,1,0:T(8,128)(2,1)}), bf16[8,48,128]{2,1,0:T(8,128)(2,1)S(1)}, u32[]{:S(2)}, u32[]{:S(2)}) async-start(bf16[8,48,128]{2,1,0:T(8,128)(2,1)} %get-tuple-element.33), calls=%async_computation.1 | async-start | bytes 196608 | tf_op jit(solution)/shard_map/all_to_all | solution.py:408
  29.4 3.3 %collective-permute-start.4 = (bf16[256,128]{1,0:T(8,128)(2,1)S(1)}, bf16[256,128]{1,0:T(8,128)(2,1)S(1)}, u32[]{:S(2)}, u32[]{:S(2)}) collective-permute-start(bf16[256,128]{1,0:T(8,128)(2,1)S(1)} %get-tuple-element.32.own), channel_id=1, source_target_pairs={{0,1},{1,0},{2,3},{3,2},{4,5},{5,4},{6,7},{7,6},{8,9},{9,8},{10,11... | collective-permute-start | bytes 196616 | tf_op jit(solution)/shard_map/ppermute | solution.py:354
  29.4 8.5 %collective-permute-start.6 = (bf16[256,128]{1,0:T(8,128)(2,1)S(1)}, bf16[256,128]{1,0:T(8,128)(2,1)S(1)}, u32[]{:S(2)}, u32[]{:S(2)}) collective-permute-start(bf16[256,128]{1,0:T(8,128)(2,1)S(1)} %get-tuple-element.32.own), channel_id=1, source_target_pairs={{0,14},{1,15},{2,4},{3,5},{4,2},{5,3},{6,8},{7,9},{8,6},{9,7},{10,... | collective-permute-start | bytes 196616 | tf_op jit(solution)/shard_map/ppermute | solution.py:354
  32.7 5.3 %collective-permute-start.5 = (bf16[256,128]{1,0:T(8,128)(2,1)S(1)}, bf16[256,128]{1,0:T(8,128)(2,1)S(1)}, u32[]{:S(2)}, u32[]{:S(2)}) collective-permute-start(bf16[256,128]{1,0:T(8,128)(2,1)S(1)} %get-tuple-element.32.own), channel_id=1, source_target_pairs={{0,2},{1,3},{2,0},{3,1},{4,6},{5,7},{6,4},{7,5},{8,10},{9,11},{10,... | collective-permute-start | bytes 196616 | tf_op jit(solution)/shard_map/ppermute | solution.py:354
  38.1 1.5 %collective-permute-start.7 = (bf16[640,128]{1,0:T(8,128)(2,1)S(1)}, bf16[640,128]{1,0:T(8,128)(2,1)S(1)}, u32[]{:S(2)}, u32[]{:S(2)}) collective-permute-start(bf16[640,128]{1,0:T(8,128)(2,1)S(1)} %relay.3.sent), channel_id=1, source_target_pairs={{0,1},{1,0},{2,3},{3,2},{4,5},{5,4},{6,7},{7,6},{8,9},{9,8},{10,11... | collective-permute-start | bytes 491528 | tf_op jit(solution)/shard_map/ppermute | solution.py:354

commit v19 on v18

--- a/solution.py
+++ b/solution.py
@@ -116,12 +116,12 @@
 
 
 def prepare_kernel(
-    axis, size, middle, near_cols_hbm, near_counts_hbm, far_cols_hbm, coupling_hbm, target_hbm, blocks_hbm, _,
-    places, high_out, low_out, target_out, ahead, near_cols, near_counts, far_cols, coupling, target, sems,
+    axis, size, middle, near_cols_hbm, near_counts_hbm, far_cols_hbm, coupling_hbm, target_hbm, _,
+    places, high_out, low_out, target_out, near_cols, near_counts, far_cols, coupling, target, sems,
 ):
     pairs = (
         (near_cols_hbm, near_cols), (near_counts_hbm, near_counts), (far_cols_hbm, far_cols),
-        (coupling_hbm, coupling), (target_hbm, target), (blocks_hbm.at[pl.ds(0, ahead.shape[0])], ahead),
+        (coupling_hbm, coupling), (target_hbm, target),
     )
     copies = [pltpu.make_async_copy(source, to, sems.at[n]) for n, (source, to) in enumerate(pairs)]
     for copy in copies:
@@ -135,12 +135,18 @@
     distance = jnp.where(distance < 0, distance + every, distance)
     distance = jnp.where(distance >= every, distance - every, distance)
     live = lax.broadcasted_iota(jnp.int32, (slots, clusters), 0) < near_counts[...]
-    places[:slots, :] = jnp.where(live, window_place(distance, clusters, me), 5 * clusters)
+    places[:slots, :] = jnp.where(live, window_place(distance, clusters, me), 5 * clusters) * R
     owner = lax.div(far_cols[...], clusters)
     other_core = (owner ^ me) & 1
     chips = size // 2
     chip = lax.rem(owner // 2 + (chips - middle), chips)
-    places[slots:, :] = (other_core * chips + chip) * clusters + lax.rem(far_cols[...], clusters)
+    rank = coupling.shape[1]
+    per_group = LANES // rank
+    inside = lax.rem(far_cols[...], clusters)
+    tile = (other_core * chips + chip) * (clusters // per_group) + lax.div(inside, per_group)
+    places[slots : 2 * slots, :] = tile * R
+    slot = lax.broadcasted_iota(jnp.int32, (slots, clusters), 0)
+    places[2 * slots :, :] = ((slot - inside) * rank) & (LANES - 1)
     for copy in copies[3:5]:
         copy.wait()
     slots, rank, _, clusters = coupling.shape
@@ -158,10 +164,10 @@
     column = lax.broadcasted_iota(jnp.int32, (size, size), 1)
     wanted = (row % clusters) * rank + row // clusters
     target_out[...] = dot((column == wanted).astype(bf16), target[...]).astype(bf16)
-    copies[5].wait()
-
-
-def fetch_kernel(first, blocks_hbm, _, __, blocks, token, sems):
+
+
+def fetch_kernel(first, blocks_hbm, *refs):
+    *_, blocks, token, sems = refs
     chunks = sems.shape[0]
     each = blocks.shape[0] // chunks
     copies = [
@@ -212,7 +218,7 @@
     lane = lane_ids()
 
     def fetch(k, i):
-        return window[pl.ds(pl.multiple_of(places[k, i] * R, R), R), :]
+        return window[pl.ds(pl.multiple_of(places[k, i], R), R), :]
 
     def block(k, i):
         at = i * slots + k
@@ -221,10 +227,8 @@
     def pick(i):
         tile = jnp.zeros((R, LANES), f32)
         for k in range(slots):
-            j = places[slots + k, i]
-            found = table[pl.ds(pl.multiple_of(lax.div(j, per_group) * R, R), R), :]
-            shift = ((k - j) * rank) & (LANES - 1)
-            tile = jnp.where(lane // rank == k, pltpu.roll(found, shift, 1), tile)
+            found = table[pl.ds(pl.multiple_of(places[slots + k, i], R), R), :]
+            tile = jnp.where(lane // rank == k, pltpu.roll(found, places[2 * slots + k, i], 1), tile)
         return tile
 
     picked = []
@@ -425,40 +429,41 @@
 
     blocks = in_hbm(near_blocks.reshape(clusters * slots, LANES, LANES))
     early = blocks.shape[0] // 4
-    places, high, low, target, ahead = call(
+    def fetch(name, first, count, chunks, *behind):
+        here, token = call(
+            functools.partial(fetch_kernel, first), name, (pltpu.VMEM((count, LANES, LANES), bf16), shape(R, LANES)),
+            [HBM] + [ANY] * len(behind), blocks, *behind, scratch_shapes=[pltpu.SemaphoreType.DMA((chunks,))],
+        )
+        return pltpu.with_memory_space_constraint(here, pltpu.VMEM), token
+
+    def arrived(got, held, behind):
+        rest, token = fetch("fetch", early, blocks.shape[0] - early, 8, got, behind)
+        sent = call(
+            functools.partial(relay_kernel, "rows"), "relay",
+            shape(got.shape[0] * got.shape[1] + rows, LANES, dtype=bf16), [VMEM] * 3 + [ANY], got, *held[2:], token
+        )
+        return ahead, rest, sent, swapped(sent, core_mate)
+
+    ahead, token = fetch("ahead", 0, early, 2, held[1])
+    here = arrived(got, held, token)
+    prepared = call(
         functools.partial(prepare_kernel, "rows", size, middle), "prepare",
         (
-            shape(2 * slots, clusters, dtype=jnp.int32),
+            shape(3 * slots, clusters, dtype=jnp.int32),
             shape(slots * rank, rank * clusters, dtype=bf16),
             shape(slots * rank, rank * clusters, dtype=bf16),
             shape(rank * clusters, LANES, dtype=bf16),
-            pltpu.VMEM((early, LANES, LANES), bf16),
         ),
-        [HBM] * 6 + [ANY], in_hbm(near_cols.T), in_hbm(near_counts.reshape(1, clusters)), in_hbm(far_cols.T),
-        in_hbm(jnp.transpose(coupling, (1, 2, 3, 0))), in_hbm(target_basis.reshape(clusters * rank, LANES)),
-        blocks, held[1],
+        [HBM] * 5 + [ANY], in_hbm(near_cols.T), in_hbm(near_counts.reshape(1, clusters)), in_hbm(far_cols.T),
+        in_hbm(jnp.transpose(coupling, (1, 2, 3, 0))), in_hbm(target_basis.reshape(clusters * rank, LANES)), here[2],
         scratch_shapes=[
             scratch(slots, clusters, dtype=jnp.int32), scratch(1, clusters, dtype=jnp.int32),
             scratch(slots, clusters, dtype=jnp.int32),
             scratch(slots, rank, rank, clusters), scratch(clusters * rank, LANES, dtype=bf16),
-            pltpu.SemaphoreType.DMA((6,)),
+            pltpu.SemaphoreType.DMA((5,)),
         ],
     )
-
-    def arrived(got, held, behind):
-        rest, token = call(
-            functools.partial(fetch_kernel, early), "fetch",
-            (pltpu.VMEM((blocks.shape[0] - early, LANES, LANES), bf16), shape(R, LANES)),
-            [HBM] + [ANY] * 2, blocks, got, behind, scratch_shapes=[pltpu.SemaphoreType.DMA((8,))],
-        )
-        rest = pltpu.with_memory_space_constraint(rest, pltpu.VMEM)
-        sent = call(
-            functools.partial(relay_kernel, "rows"), "relay",
-            shape(got.shape[0] * got.shape[1] + rows, LANES, dtype=bf16), [VMEM] * 3 + [ANY], got, *held[2:], token
-        )
-        return *held, places, ahead, rest, sent, swapped(sent, core_mate), high, low, target
-
-    ahead = pltpu.with_memory_space_constraint(ahead, pltpu.VMEM)
+    places, *made = prepared
     kept = [scratch(rows, LANES), scratch(rows, LANES), scratch(5 * rows + R, LANES), scratch(size * head, LANES)]
     operands = [VMEM] * 4 + [SMEM] + [VMEM] * 9
     image, lowered, payload = call(
@@ -467,7 +472,7 @@
             shape(rows, LANES), shape(rows, LANES, dtype=bf16),
             shape(size // 2, head + TAIL, LANES, dtype=bf16),
         ),
-        operands, *arrived(got, held, target), field, basis, scratch_shapes=kept,
+        operands, *held, places, *here, *made, field, basis, scratch_shapes=kept,
     )
     got = gather(payload)
     held = sends_of(lowered)
@@ -475,11 +480,11 @@
     candidate, sums = call(
         functools.partial(second_kernel, per_group, unknowns), "operator_two",
         (shape(rows, LANES), shape(size, R, LANES, dtype=bf16)),
-        operands, *here, field, image, scratch_shapes=kept,
+        operands, *held, places, *here, *made, field, image, scratch_shapes=kept,
     )
     return call(
         functools.partial(finish_kernel, per_group, unknowns), "finish", (shape(R, width), shape(R, width)),
-        [VMEM] * 6, field, image, candidate, *here[7:9], exchange(sums),
+        [VMEM] * 6, field, image, candidate, *here[2:], exchange(sums),
     )
 
 

time: 54.1 us -> 53.2 us (0.983)
  waiting for transfers between devices: 5.55 us -> 4.77 us
    ppermute x8, waiting for transfers between devices: 3.03 us -> 1.72 us  [swapped(): lax.ppermute(block, 'rows', [(i, partner(i)) for i in range(lax.axis_size...]
    pallas_call x9 -> x10, Pallas kernels: 19.7 us -> 20 us  [call(): pl.pallas_call(kernel, out_shape=out, in_specs=ins, out_specs=jax.tree.ma...]
  transfers between devices with their start and end apart: 10 -> 10, of which waited for: 6 -> 5; matrix products, arithmetic and copies ran while one was open for 0% -> 0% of each run, Pallas kernels for 14% -> 17%
where the time goes in v19:
time: 53.2 us; the launch traced here: 52.8 us
  Pallas kernels  20 us (38%)
  starting transfers between devices  18.5 us (35%)
  blocking collectives  8.75 us (16%)
  waiting for transfers between devices  4.77 us (9%)
  between operations  0.73 us (1%)
    pallas_call x10, Pallas kernels, call(): pl.pallas_call(kernel, out_shape=out, in_specs=ins, out_specs=jax.tree.ma...  20 us
    all_to_all x2, starting transfers between devices, gather(): return lax.all_to_all(block, 'rows', 0, 0, axis_index_groups=groups)  11.7 us
    all_to_all x1, blocking collectives, exchange(): return lax.all_to_all(block, 'rows', 0, 0, axis_index_groups=[group])  8.75 us
    ppermute x8, starting transfers between devices, swapped(): lax.ppermute(block, 'rows', [(i, partner(i)) for i in range(lax.axis_size...  6.74 us
    all_to_all x2, waiting for transfers between devices, gather(): return lax.all_to_all(block, 'rows', 0, 0, axis_index_groups=groups)  3.04 us
    ppermute x8, waiting for transfers between devices, swapped(): lax.ppermute(block, 'rows', [(i, partner(i)) for i in range(lax.axis_size...  1.72 us
  transfers between devices with their start and end apart: 10, of which 5 were waited for; matrix products, arithmetic and copies ran while one was open for 0% of the time, Pallas kernels for 17%

profile of v19, /device:TPU:0, one launch (start us, length us, event | category | flops | bytes accessed | tf_op | source)
XLA Modules:
  0.0 52.8 jit_solution(16874390446629493289)
XLA Ops:
  0.6 1.8 %start.1 = (f32[256,128]{1,0:T(8,128)S(1)}, bf16[512,128]{1,0:T(8,128)(2,1)S(1)}, bf16[256,128]{1,0:T(8,128)(2,1)S(1)}, bf16[8,32,128]{2,1,0:T(8,128)(2,1)}) custom-call(f32[8,4096]{1,0:T(8,128)} %b_hbm.1, bf16[512,128]{1,0:T(8,128)(2,1)} %bitcast.12), custom_call_target="tpu_custom_call" | custom-call | tf_op jit(solution)/shard_map/start/pallas_call | solution.py:401
  2.5 7.9 %all-to-all-start = ((bf16[8,32,128]{2,1,0:T(8,128)(2,1)}), bf16[8,32,128]{2,1,0:T(8,128)(2,1)S(1)}, u32[]{:S(2)}, u32[]{:S(2)}) async-start(bf16[8,32,128]{2,1,0:T(8,128)(2,1)} %get-tuple-element.23), calls=%async_computation | async-start | bytes 131072 | tf_op jit(solution)/shard_map/all_to_all | solution.py:412
  10.3 3.3 %collective-permute-start.2 = (bf16[256,128]{1,0:T(8,128)(2,1)S(1)}, bf16[256,128]{1,0:T(8,128)(2,1)S(1)}, u32[]{:S(2)}, u32[]{:S(2)}) collective-permute-start(bf16[256,128]{1,0:T(8,128)(2,1)S(1)} %get-tuple-element.22.own), channel_id=1, source_target_pairs={{0,14},{1,15},{2,4},{3,5},{4,2},{5,3},{6,8},{7,9},{8,6},{9,7},{10,... | collective-permute-start | bytes 196616 | tf_op jit(solution)/shard_map/ppermute | solution.py:358
  13.6 1.6 %ahead.1 = (bf16[64,128,128]{2,1,0:T(8,128)(2,1)S(1)}, f32[8,128]{1,0:T(8,128)S(1)}) custom-call(bf16[256,128,128]{2,1,0:T(8,128)(2,1)} %bitcast.7, bf16[256,128]{1,0:T(8,128)(2,1)S(1)} %collective-permute-done.refs_0_.mate), custom_call_target="tpu_custom_call" | custom-call | tf_op jit(solution)/shard_map/ahead/pallas_call | solution.py:401
  15.2 0.6 %all-to-all-done.refs_0_.got = bf16[8,32,128]{2,1,0:T(8,128)(2,1)S(1)} async-done(((bf16[8,32,128]{2,1,0:T(8,128)(2,1)}), bf16[8,32,128]{2,1,0:T(8,128)(2,1)S(1)}, u32[]{:S(2)}, u32[]{:S(2)}) %all-to-all-start) | async-done | bytes 65568 | tf_op jit(solution)/shard_map/all_to_all | solution.py:412
  15.8 2.9 %fetch.2 = (bf16[192,128,128]{2,1,0:T(8,128)(2,1)S(1)}, f32[8,128]{1,0:T(8,128)S(1)}) custom-call(bf16[256,128,128]{2,1,0:T(8,128)(2,1)} %bitcast.8, bf16[8,32,128]{2,1,0:T(8,128)(2,1)S(1)} %all-to-all-done.refs_0_.got, f32[8,128]{1,0:T(8,128)S(1)} %get-tuple-element.24.refs_1_), custom_call_target="tpu_custom_call" | custom-call | tf_op jit(solution)/shard_map/fetch/pallas_call | solution.py:401
  18.6 0.0 collective-permute-done.2.odd
  18.6 0.3 collective-permute-done.1.even
  19.0 0.1 collective-permute-start.3
  19.1 1.6 %prepare.1 = (s32[24,32]{1,0:T(8,128)S(1)}, bf16[128,512]{1,0:T(8,128)(2,1)S(1)}, bf16[128,512]{1,0:T(8,128)(2,1)S(1)}, bf16[512,128]{1,0:T(8,128)(2,1)S(1)}) custom-call(s32[8,32]{1,0:T(8,128)} %bitcast.13, s32[1,32]{1,0:T(1,128)} %bitcast.15, s32[8,32]{1,0:T(8,128)} %bitcast.14, f32[8,16,16,32]{3,2,1,0:T(8,128)} %bitcast.10, bf16[512,128]{1,0:T(8,128)(2,1)} %bitcast.11, ...), custom_call_target="tpu_custom_call" | custom-call | tf_op jit(solution)/shard_map/prepare/pallas_call | solution.py:401
  20.7 0.0 collective-permute-done.3.received
  20.7 4.3 %operator_one.1 = (f32[256,128]{1,0:T(8,128)S(1)}, bf16[256,128]{1,0:T(8,128)(2,1)S(1)}, bf16[8,48,128]{2,1,0:T(8,128)(2,1)}) custom-call(bf16[256,128]{1,0:T(8,128)(2,1)S(1)} %get-tuple-element.22.own, bf16[256,128]{1,0:T(8,128)(2,1)S(1)} %collective-permute-done.refs_0_.mate, bf16[256,128]{1,0:T(8,128)(2,1)S(1)} %collective-permute-done.1.even, ...), custom_call_target="tpu_custom_call" | custom-call | tf_op jit(solution)/shard_map/operator_one/pallas_call | solution.py:401
  25.0 3.9 %all-to-all-start.1 = ((bf16[8,48,128]{2,1,0:T(8,128)(2,1)}), bf16[8,48,128]{2,1,0:T(8,128)(2,1)S(1)}, u32[]{:S(2)}, u32[]{:S(2)}) async-start(bf16[8,48,128]{2,1,0:T(8,128)(2,1)} %get-tuple-element.35), calls=%async_computation.1 | async-start | bytes 196608 | tf_op jit(solution)/shard_map/all_to_all | solution.py:412
  28.9 0.0 collective-permute-start.4
  28.9 3.3 %collective-permute-start.6 = (bf16[256,128]{1,0:T(8,128)(2,1)S(1)}, bf16[256,128]{1,0:T(8,128)(2,1)S(1)}, u32[]{:S(2)}, u32[]{:S(2)}) collective-permute-start(bf16[256,128]{1,0:T(8,128)(2,1)S(1)} %get-tuple-element.34.own), channel_id=1, source_target_pairs={{0,14},{1,15},{2,4},{3,5},{4,2},{5,3},{6,8},{7,9},{8,6},{9,7},{10,... | collective-permute-start | bytes 196616 | tf_op jit(solution)/shard_map/ppermute | solution.py:358
  32.2 2.4 %all-to-all-done.1.refs_0_.got = bf16[8,48,128]{2,1,0:T(8,128)(2,1)S(1)} async-done(((bf16[8,48,128]{2,1,0:T(8,128)(2,1)}), bf16[8,48,128]{2,1,0:T(8,128)(2,1)S(1)}, u32[]{:S(2)}, u32[]{:S(2)}) %all-to-all-start.1) | async-done | bytes 98336 | tf_op jit(solution)/shard_map/all_to_all | solution.py:412
  34.6 2.9 %fetch.3 = (bf16[192,128,128]{2,1,0:T(8,128)(2,1)S(1)}, f32[8,128]{1,0:T(8,128)S(1)}) custom-call(bf16[256,128,128]{2,1,0:T(8,128)(2,1)} %bitcast.9, bf16[8,48,128]{2,1,0:T(8,128)(2,1)S(1)} %all-to-all-done.1.refs_0_.got, bf16[256,128]{1,0:T(8,128)(2,1)S(1)} %collective-permute-done.4.refs_1_.mate), custom_call_target="tpu_custom_call" | custom-call | tf_op jit(solution)/shard_map/fetch/pallas_call | solution.py:401
  37.5 0.0 collective-permute-done.6.odd
  37.5 0.1 collective-permute-done.5.even
  37.6 0.1 collective-permute-start.7
  37.7 1.4 %collective-permute-done.7.received = bf16[640,128]{1,0:T(8,128)(2,1)S(1)} collective-permute-done((bf16[640,128]{1,0:T(8,128)(2,1)S(1)}, bf16[640,128]{1,0:T(8,128)(2,1)S(1)}, u32[]{:S(2)}, u32[]{:S(2)}) %collective-permute-start.7) | collective-permute-done | bytes 163872 | tf_op jit(solution)/shard_map/ppermute | solution.py:358
  39.0 3.5 %operator_two.1 = (f32[256,128]{1,0:T(8,128)S(1)}, bf16[16,8,128]{2,1,0:T(8,128)(2,1)S(1)}) custom-call(bf16[256,128]{1,0:T(8,128)(2,1)S(1)} %get-tuple-element.34.own, bf16[256,128]{1,0:T(8,128)(2,1)S(1)} %collective-permute-done.4.refs_1_.mate, bf16[256,128]{1,0:T(8,128)(2,1)S(1)} %collective-permute-done.5.even, ...), custom_call_target="tpu_custom_call" | custom-call | tf_op jit(solution)/shard_map/operator_two/pallas_call | solution.py:401
  42.5 8.8 %all_to_all.15.got = bf16[16,8,128]{2,1,0:T(8,128)(2,1)S(1)} all-to-all(bf16[16,8,128]{2,1,0:T(8,128)(2,1)S(1)} %get-tuple-element.39), channel_id=1, replica_groups={{4,5,6,7,8,9,10,11,12,13,14,15,0,1,2,3},{20,21,22,23,24,25,26,27,28,29,..., dimensions={0} | all-to-all | bytes 65536 | tf_op jit(solution)/shard_map/all_to_all | solution.py:416
  51.3 1.5 %finish.1 = (f32[8,4096]{1,0:T(8,128)}, f32[8,4096]{1,0:T(8,128)}) custom-call(f32[256,128]{1,0:T(8,128)S(1)} %get-tuple-element.21.b, f32[256,128]{1,0:T(8,128)S(1)} %get-tuple-element.33.image, f32[256,128]{1,0:T(8,128)S(1)} %get-tuple-element.38.candidate, bf16[640,128]{1,0:T(8,128)(2,1)S(1)} %relay.3.sent, ...), custom_call_target="tpu_custom_call" | custom-call | tf_op jit(solution)/shard_map/finish/pallas_call | solution.py:401
  (7 shorter events, 0.0 us)
Async XLA Ops:
  2.5 13.3 %all-to-all-start = ((bf16[8,32,128]{2,1,0:T(8,128)(2,1)}), bf16[8,32,128]{2,1,0:T(8,128)(2,1)S(1)}, u32[]{:S(2)}, u32[]{:S(2)}) async-start(bf16[8,32,128]{2,1,0:T(8,128)(2,1)} %get-tuple-element.23), calls=%async_computation | async-start | bytes 131072 | tf_op jit(solution)/shard_map/all_to_all | solution.py:412
  10.3 3.3 %collective-permute-start = (bf16[256,128]{1,0:T(8,128)(2,1)S(1)}, bf16[256,128]{1,0:T(8,128)(2,1)S(1)}, u32[]{:S(2)}, u32[]{:S(2)}) collective-permute-start(bf16[256,128]{1,0:T(8,128)(2,1)S(1)} %get-tuple-element.22.own), channel_id=1, source_target_pairs={{0,1},{1,0},{2,3},{3,2},{4,5},{5,4},{6,7},{7,6},{8,9},{9,8},{10,11... | collective-permute-start | bytes 196616 | tf_op jit(solution)/shard_map/ppermute | solution.py:358
  10.3 8.3 %collective-permute-start.2 = (bf16[256,128]{1,0:T(8,128)(2,1)S(1)}, bf16[256,128]{1,0:T(8,128)(2,1)S(1)}, u32[]{:S(2)}, u32[]{:S(2)}) collective-permute-start(bf16[256,128]{1,0:T(8,128)(2,1)S(1)} %get-tuple-element.22.own), channel_id=1, source_target_pairs={{0,14},{1,15},{2,4},{3,5},{4,2},{5,3},{6,8},{7,9},{8,6},{9,7},{10,... | collective-permute-start | bytes 196616 | tf_op jit(solution)/shard_map/ppermute | solution.py:358
  13.6 5.3 %collective-permute-start.1 = (bf16[256,128]{1,0:T(8,128)(2,1)S(1)}, bf16[256,128]{1,0:T(8,128)(2,1)S(1)}, u32[]{:S(2)}, u32[]{:S(2)}) collective-permute-start(bf16[256,128]{1,0:T(8,128)(2,1)S(1)} %get-tuple-element.22.own), channel_id=1, source_target_pairs={{0,2},{1,3},{2,0},{3,1},{4,6},{5,7},{6,4},{7,5},{8,10},{9,11},{10,... | collective-permute-start | bytes 196616 | tf_op jit(solution)/shard_map/ppermute | solution.py:358
  19.0 1.8 %collective-permute-start.3 = (bf16[512,128]{1,0:T(8,128)(2,1)S(1)}, bf16[512,128]{1,0:T(8,128)(2,1)S(1)}, u32[]{:S(2)}, u32[]{:S(2)}) collective-permute-start(bf16[512,128]{1,0:T(8,128)(2,1)S(1)} %relay.2._.sent), channel_id=1, source_target_pairs={{0,1},{1,0},{2,3},{3,2},{4,5},{5,4},{6,7},{7,6},{8,9},{9,8},{10,11... | collective-permute-start | bytes 393224 | tf_op jit(solution)/shard_map/ppermute | solution.py:358
  25.0 9.6 %all-to-all-start.1 = ((bf16[8,48,128]{2,1,0:T(8,128)(2,1)}), bf16[8,48,128]{2,1,0:T(8,128)(2,1)S(1)}, u32[]{:S(2)}, u32[]{:S(2)}) async-start(bf16[8,48,128]{2,1,0:T(8,128)(2,1)} %get-tuple-element.35), calls=%async_computation.1 | async-start | bytes 196608 | tf_op jit(solution)/shard_map/all_to_all | solution.py:412
  28.9 3.3 %collective-permute-start.4 = (bf16[256,128]{1,0:T(8,128)(2,1)S(1)}, bf16[256,128]{1,0:T(8,128)(2,1)S(1)}, u32[]{:S(2)}, u32[]{:S(2)}) collective-permute-start(bf16[256,128]{1,0:T(8,128)(2,1)S(1)} %get-tuple-element.34.own), channel_id=1, source_target_pairs={{0,1},{1,0},{2,3},{3,2},{4,5},{5,4},{6,7},{7,6},{8,9},{9,8},{10,11... | collective-permute-start | bytes 196616 | tf_op jit(solution)/shard_map/ppermute | solution.py:358
  28.9 8.6 %collective-permute-start.6 = (bf16[256,128]{1,0:T(8,128)(2,1)S(1)}, bf16[256,128]{1,0:T(8,128)(2,1)S(1)}, u32[]{:S(2)}, u32[]{:S(2)}) collective-permute-start(bf16[256,128]{1,0:T(8,128)(2,1)S(1)} %get-tuple-element.34.own), channel_id=1, source_target_pairs={{0,14},{1,15},{2,4},{3,5},{4,2},{5,3},{6,8},{7,9},{8,6},{9,7},{10,... | collective-permute-start | bytes 196616 | tf_op jit(solution)/shard_map/ppermute | solution.py:358
  32.2 5.4 %collective-permute-start.5 = (bf16[256,128]{1,0:T(8,128)(2,1)S(1)}, bf16[256,128]{1,0:T(8,128)(2,1)S(1)}, u32[]{:S(2)}, u32[]{:S(2)}) collective-permute-start(bf16[256,128]{1,0:T(8,128)(2,1)S(1)} %get-tuple-element.34.own), channel_id=1, source_target_pairs={{0,2},{1,3},{2,0},{3,1},{4,6},{5,7},{6,4},{7,5},{8,10},{9,11},{10,... | collective-permute-start | bytes 196616 | tf_op jit(solution)/shard_map/ppermute | solution.py:358
  37.6 1.5 %collective-permute-start.7 = (bf16[640,128]{1,0:T(8,128)(2,1)S(1)}, bf16[640,128]{1,0:T(8,128)(2,1)S(1)}, u32[]{:S(2)}, u32[]{:S(2)}) collective-permute-start(bf16[640,128]{1,0:T(8,128)(2,1)S(1)} %relay.3.sent), channel_id=1, source_target_pairs={{0,1},{1,0},{2,3},{3,2},{4,5},{5,4},{6,7},{7,6},{8,9},{9,8},{10,11... | collective-permute-start | bytes 491528 | tf_op jit(solution)/shard_map/ppermute | solution.py:358

commit v20 on v19

--- a/solution.py
+++ b/solution.py
@@ -160,27 +160,50 @@
         high_out[:, s * LANES : (s + 1) * LANES] = high
         low_out[:, s * LANES : (s + 1) * LANES] = (tile - high.astype(f32)).astype(bf16)
     size = rank * clusters
-    row = lax.broadcasted_iota(jnp.int32, (size, size), 0)
+    row = lax.broadcasted_iota(jnp.int32, (size, 1), 0)
     column = lax.broadcasted_iota(jnp.int32, (size, size), 1)
-    wanted = (row % clusters) * rank + row // clusters
+    wanted = lax.rem(row, clusters) * rank + lax.div(row, clusters)
     target_out[...] = dot((column == wanted).astype(bf16), target[...]).astype(bf16)
 
 
-def fetch_kernel(first, blocks_hbm, *refs):
+def fetch_kernel(slots, blocks_hbm, *refs):
     *_, blocks, token, sems = refs
+    chunks = sems.shape[1]
+    each = blocks.shape[0] // chunks
+    copies, at = [], 0
+    for n, (first, count) in enumerate(slots):
+        for c in range(chunks):
+            clusters = pl.ds(c * each, each)
+            copies.append(
+                pltpu.make_async_copy(
+                    blocks_hbm.at[clusters, pl.ds(first, count)], blocks.at[clusters, pl.ds(at, count)], sems.at[n, c]
+                )
+            )
+        at += count
+    for copy in copies:
+        copy.start()
+    token[...] = jnp.zeros_like(token)
+    for copy in copies:
+        copy.wait()
+
+
+def own_kernel(blocks_hbm, own, _, near, blocks, sems):
     chunks = sems.shape[0]
     each = blocks.shape[0] // chunks
     copies = [
         pltpu.make_async_copy(
-            blocks_hbm.at[pl.ds(first + c * each, each)], blocks.at[pl.ds(c * each, each)], sems.at[c]
+            blocks_hbm.at[pl.ds(c * each, each), pl.ds(0, 1)], blocks.at[pl.ds(c * each, each)], sems.at[c]
         )
         for c in range(chunks)
     ]
     for copy in copies:
         copy.start()
-    token[...] = jnp.zeros_like(token)
-    for copy in copies:
+    for c, copy in enumerate(copies):
         copy.wait()
+        for i in range(c * each, (c + 1) * each, 2):
+            both = dot(own[pl.ds(i * R, 2 * R), :], jnp.concatenate([blocks[i, 0], blocks[i + 1, 0]], axis=0), (1, 1))
+            near[pl.ds(i * R, R), :] = both[:R, :LANES]
+            near[pl.ds((i + 1) * R, R), :] = both[R:, LANES:]
 
 
 def relay_kernel(axis, got, even, odd, _, out):
@@ -200,9 +223,13 @@
         out[span, :] = odd[...]
 
 
-def apply(per_group, each, slabs, places, ahead, blocks, swaps, high, low, target, near, far, window, table, finish):
+def apply(
+    per_group, each, slabs, places, ahead, blocks, swaps, high, low, target, near, far, window, table, finish, started
+):
     clusters = near.shape[0] // R
-    slots = (ahead.shape[0] + blocks.shape[0]) // clusters
+    early = ahead.shape[1]
+    first = 0 if started is None else 1
+    slots = early + blocks.shape[1] + first
     rank = LANES // per_group
     head = clusters // per_group * R
     rows = slabs[0].shape[0]
@@ -221,8 +248,9 @@
         return window[pl.ds(pl.multiple_of(places[k, i], R), R), :]
 
     def block(k, i):
-        at = i * slots + k
-        return ahead[at] if at < ahead.shape[0] else blocks[at - ahead.shape[0]]
+        if 0 < k <= early:
+            return ahead[i, k - 1]
+        return blocks[i, max(k - early - first, 0)]
 
     def pick(i):
         tile = jnp.zeros((R, LANES), f32)
@@ -234,14 +262,16 @@
     picked = []
     for i in range(0, clusters, 2):
         sources = jnp.concatenate(
-            [jnp.concatenate([fetch(k, i), fetch(k, i + 1)], axis=0) for k in range(slots)], axis=1
+            [jnp.concatenate([fetch(k, i), fetch(k, i + 1)], axis=0) for k in range(first, slots)], axis=1
         )
         weights = jnp.concatenate(
-            [jnp.concatenate([block(k, i), block(k, i + 1)], axis=0) for k in range(slots)], axis=1
+            [jnp.concatenate([block(k, i), block(k, i + 1)], axis=0) for k in range(first, slots)], axis=1
         )
         both = dot(sources.astype(bf16), weights, (1, 1))
-        near[pl.ds(i * R, R), :] = both[:R, :LANES]
-        near[pl.ds((i + 1) * R, R), :] = both[R:, LANES:]
+        parts = [both[:R, :LANES], both[R:, LANES:]]
+        if started is not None:
+            parts = [part + rows_of(started, i + n) for n, part in enumerate(parts)]
+        near[pl.ds(i * R, 2 * R), :] = jnp.concatenate(parts, axis=0)
         if 2 * i < clusters:
             picked += [pick(n) for n in range(2 * i, 2 * i + 4)]
         if 2 * i == clusters - 4:
@@ -288,7 +318,9 @@
         if i % per_group == per_group - 1:
             parts.append(compress(tiles[-per_group:], basis, i // per_group))
 
-    apply(per_group, each, slabs, places, ahead, blocks, swaps, high, low, target, near, far, window, table, finish)
+    apply(
+        per_group, each, slabs, places, ahead, blocks, swaps, high, low, target, near, far, window, table, finish, None
+    )
     write_payload(payload, parts, sums)
 
 
@@ -305,7 +337,7 @@
 
 def second_kernel(
     per_group, unknowns, own, mate, even, odd, places, ahead, blocks, sent, received, high, low, target, b, image,
-    candidate, sums_out, near, far, window, table,
+    started, candidate, sums_out, near, far, window, table,
 ):
     clusters = near.shape[0] // R
     head = clusters // per_group * R
@@ -325,7 +357,9 @@
         candidate[pl.ds(j * R, R), :] = made
 
     each = head + TAIL
-    apply(per_group, each, slabs, places, ahead, blocks, swaps, high, low, target, near, far, window, table, finish)
+    apply(
+        per_group, each, slabs, places, ahead, blocks, swaps, high, low, target, near, far, window, table, finish, started
+    )
     tile = sums_tile(sums).astype(bf16)
     for device in range(sums_out.shape[0]):
         sums_out[device] = tile
@@ -427,25 +461,30 @@
     got = gather(payload)
     held = sends_of(lowered)
 
-    blocks = in_hbm(near_blocks.reshape(clusters * slots, LANES, LANES))
-    early = blocks.shape[0] // 4
-    def fetch(name, first, count, chunks, *behind):
+    blocks = in_hbm(near_blocks)
+    early = 2
+
+    def fetch(name, ranges, chunks, *behind):
+        count = sum(count for _, count in ranges)
         here, token = call(
-            functools.partial(fetch_kernel, first), name, (pltpu.VMEM((count, LANES, LANES), bf16), shape(R, LANES)),
-            [HBM] + [ANY] * len(behind), blocks, *behind, scratch_shapes=[pltpu.SemaphoreType.DMA((chunks,))],
+            functools.partial(fetch_kernel, ranges), name,
+            (pltpu.VMEM((clusters, count, LANES, LANES), bf16), shape(R, LANES)),
+            [HBM] + [ANY] * len(behind), blocks, *behind,
+            scratch_shapes=[pltpu.SemaphoreType.DMA((len(ranges), chunks))],
         )
         return pltpu.with_memory_space_constraint(here, pltpu.VMEM), token
 
-    def arrived(got, held, behind):
-        rest, token = fetch("fetch", early, blocks.shape[0] - early, 8, got, behind)
+    def arrived(got, held, ranges, behind):
+        rest, token = fetch("fetch", ranges, 4, got, behind)
         sent = call(
             functools.partial(relay_kernel, "rows"), "relay",
             shape(got.shape[0] * got.shape[1] + rows, LANES, dtype=bf16), [VMEM] * 3 + [ANY], got, *held[2:], token
         )
         return ahead, rest, sent, swapped(sent, core_mate)
 
-    ahead, token = fetch("ahead", 0, early, 2, held[1])
-    here = arrived(got, held, token)
+    late = (1 + early, slots - 1 - early)
+    ahead, token = fetch("ahead", [(1, early)], 2, held[1])
+    here = arrived(got, held, [(0, 1), late], token)
     prepared = call(
         functools.partial(prepare_kernel, "rows", size, middle), "prepare",
         (
@@ -476,11 +515,15 @@
     )
     got = gather(payload)
     held = sends_of(lowered)
-    here = arrived(got, held, held[1])
+    started = call(
+        own_kernel, "own", shape(rows, LANES), [HBM, VMEM, ANY], blocks, lowered, held[1],
+        scratch_shapes=[scratch(clusters, 1, LANES, LANES, dtype=bf16), pltpu.SemaphoreType.DMA((4,))],
+    )
+    here = arrived(got, held, [late], started)
     candidate, sums = call(
         functools.partial(second_kernel, per_group, unknowns), "operator_two",
         (shape(rows, LANES), shape(size, R, LANES, dtype=bf16)),
-        operands, *held, places, *here, *made, field, image, scratch_shapes=kept,
+        operands + [VMEM], *held, places, *here, *made, field, image, started, scratch_shapes=kept,
     )
     return call(
         functools.partial(finish_kernel, per_group, unknowns), "finish", (shape(R, width), shape(R, width)),

time: 53.2 us -> 53 us (level)
  waiting for transfers between devices: 4.77 us -> 3.3 us
  Pallas kernels: 20 us -> 21.3 us
    all_to_all x2, waiting for transfers between devices: 3.04 us -> 1.3 us  [gather(): return lax.all_to_all(block, 'rows', 0, 0, axis_index_groups=groups)]
    pallas_call x10 -> x11, Pallas kernels: 20 us -> 21.3 us  [call(): pl.pallas_call(kernel, out_shape=out, in_specs=ins, out_specs=jax.tree.ma...]
  transfers between devices with their start and end apart: 10 -> 10, of which waited for: 5 -> 5; matrix products, arithmetic and copies ran while one was open for 0% -> 0% of each run, Pallas kernels for 17% -> 20%
where the time goes in v20:
time: 53 us; the launch traced here: 52.6 us
  Pallas kernels  21.3 us (40%)
  starting transfers between devices  18.5 us (35%)
  blocking collectives  8.79 us (17%)
  waiting for transfers between devices  3.3 us (6%)
  between operations  0.73 us (1%)
    pallas_call x11, Pallas kernels, call(): pl.pallas_call(kernel, out_shape=out, in_specs=ins, out_specs=jax.tree.ma...  21.3 us
    all_to_all x2, starting transfers between devices, gather(): return lax.all_to_all(block, 'rows', 0, 0, axis_index_groups=groups)  11.8 us
    all_to_all x1, blocking collectives, exchange(): return lax.all_to_all(block, 'rows', 0, 0, axis_index_groups=[group])  8.79 us
    ppermute x8, starting transfers between devices, swapped(): lax.ppermute(block, 'rows', [(i, partner(i)) for i in range(lax.axis_size...  6.74 us
    ppermute x8, waiting for transfers between devices, swapped(): lax.ppermute(block, 'rows', [(i, partner(i)) for i in range(lax.axis_size...  2 us
    all_to_all x2, waiting for transfers between devices, gather(): return lax.all_to_all(block, 'rows', 0, 0, axis_index_groups=groups)  1.3 us
  transfers between devices with their start and end apart: 10, of which 5 were waited for; matrix products, arithmetic and copies ran while one was open for 0% of the time, Pallas kernels for 20%

profile of v20, /device:TPU:0, one launch (start us, length us, event | category | flops | bytes accessed | tf_op | source)
XLA Modules:
  0.0 52.6 jit_solution(17720449600249050699)
XLA Ops:
  0.6 1.8 %start.1 = (f32[256,128]{1,0:T(8,128)S(1)}, bf16[512,128]{1,0:T(8,128)(2,1)S(1)}, bf16[256,128]{1,0:T(8,128)(2,1)S(1)}, bf16[8,32,128]{2,1,0:T(8,128)(2,1)}) custom-call(f32[8,4096]{1,0:T(8,128)} %b_hbm.1, bf16[512,128]{1,0:T(8,128)(2,1)} %bitcast.8), custom_call_target="tpu_custom_call" | custom-call | tf_op jit(solution)/shard_map/start/pallas_call | solution.py:435
  2.5 7.9 %all-to-all-start = ((bf16[8,32,128]{2,1,0:T(8,128)(2,1)}), bf16[8,32,128]{2,1,0:T(8,128)(2,1)S(1)}, u32[]{:S(2)}, u32[]{:S(2)}) async-start(bf16[8,32,128]{2,1,0:T(8,128)(2,1)} %get-tuple-element.23), calls=%async_computation | async-start | bytes 131072 | tf_op jit(solution)/shard_map/all_to_all | solution.py:446
  10.3 3.3 %collective-permute-start.2 = (bf16[256,128]{1,0:T(8,128)(2,1)S(1)}, bf16[256,128]{1,0:T(8,128)(2,1)S(1)}, u32[]{:S(2)}, u32[]{:S(2)}) collective-permute-start(bf16[256,128]{1,0:T(8,128)(2,1)S(1)} %get-tuple-element.22.own), channel_id=1, source_target_pairs={{0,14},{1,15},{2,4},{3,5},{4,2},{5,3},{6,8},{7,9},{8,6},{9,7},{10,... | collective-permute-start | bytes 196616 | tf_op jit(solution)/shard_map/ppermute | solution.py:392
  13.6 1.6 %ahead.1 = (bf16[32,2,128,128]{3,2,1,0:T(8,128)(2,1)S(1)}, f32[8,128]{1,0:T(8,128)S(1)}) custom-call(bf16[32,8,128,128]{3,2,1,0:T(8,128)(2,1)} %blocks_hbm.7, bf16[256,128]{1,0:T(8,128)(2,1)S(1)} %collective-permute-done.refs_0_.mate), custom_call_target="tpu_custom_call" | custom-call | tf_op jit(solution)/shard_map/ahead/pallas_call | solution.py:435
  15.2 0.6 %all-to-all-done.refs_0_.got = bf16[8,32,128]{2,1,0:T(8,128)(2,1)S(1)} async-done(((bf16[8,32,128]{2,1,0:T(8,128)(2,1)}), bf16[8,32,128]{2,1,0:T(8,128)(2,1)S(1)}, u32[]{:S(2)}, u32[]{:S(2)}) %all-to-all-start) | async-done | bytes 65568 | tf_op jit(solution)/shard_map/all_to_all | solution.py:446
  15.8 2.9 %fetch.2 = (bf16[32,6,128,128]{3,2,1,0:T(8,128)(2,1)S(1)}, f32[8,128]{1,0:T(8,128)S(1)}) custom-call(bf16[32,8,128,128]{3,2,1,0:T(8,128)(2,1)} %blocks_hbm.7, bf16[8,32,128]{2,1,0:T(8,128)(2,1)S(1)} %all-to-all-done.refs_0_.got, f32[8,128]{1,0:T(8,128)S(1)} %get-tuple-element.24.refs_1_), custom_call_target="tpu_custom_call" | custom-call | tf_op jit(solution)/shard_map/fetch/pallas_call | solution.py:435
  18.7 0.0 collective-permute-done.2.odd
  18.7 0.2 collective-permute-done.1.even
  19.0 0.1 collective-permute-start.3
  19.1 1.6 %prepare.1 = (s32[24,32]{1,0:T(8,128)S(1)}, bf16[128,512]{1,0:T(8,128)(2,1)S(1)}, bf16[128,512]{1,0:T(8,128)(2,1)S(1)}, bf16[512,128]{1,0:T(8,128)(2,1)S(1)}) custom-call(s32[8,32]{1,0:T(8,128)} %bitcast.9, s32[1,32]{1,0:T(1,128)} %bitcast.11, s32[8,32]{1,0:T(8,128)} %bitcast.10, f32[8,16,16,32]{3,2,1,0:T(8,128)} %bitcast.6, bf16[512,128]{1,0:T(8,128)(2,1)} %bitcast.7, ...), custom_call_target="tpu_custom_call" | custom-call | tf_op jit(solution)/shard_map/prepare/pallas_call | solution.py:435
  20.7 0.0 collective-permute-done.3.received
  20.7 4.3 %operator_one.1 = (f32[256,128]{1,0:T(8,128)S(1)}, bf16[256,128]{1,0:T(8,128)(2,1)S(1)}, bf16[8,48,128]{2,1,0:T(8,128)(2,1)}) custom-call(bf16[256,128]{1,0:T(8,128)(2,1)S(1)} %get-tuple-element.22.own, bf16[256,128]{1,0:T(8,128)(2,1)S(1)} %collective-permute-done.refs_0_.mate, bf16[256,128]{1,0:T(8,128)(2,1)S(1)} %collective-permute-done.1.even, ...), custom_call_target="tpu_custom_call" | custom-call | tf_op jit(solution)/shard_map/operator_one/pallas_call | solution.py:435
  25.0 3.9 %all-to-all-start.1 = ((bf16[8,48,128]{2,1,0:T(8,128)(2,1)}), bf16[8,48,128]{2,1,0:T(8,128)(2,1)S(1)}, u32[]{:S(2)}, u32[]{:S(2)}) async-start(bf16[8,48,128]{2,1,0:T(8,128)(2,1)} %get-tuple-element.35), calls=%async_computation.1 | async-start | bytes 196608 | tf_op jit(solution)/shard_map/all_to_all | solution.py:446
  28.9 0.0 collective-permute-start.4
  29.0 3.3 %collective-permute-start.6 = (bf16[256,128]{1,0:T(8,128)(2,1)S(1)}, bf16[256,128]{1,0:T(8,128)(2,1)S(1)}, u32[]{:S(2)}, u32[]{:S(2)}) collective-permute-start(bf16[256,128]{1,0:T(8,128)(2,1)S(1)} %get-tuple-element.34.own), channel_id=1, source_target_pairs={{0,14},{1,15},{2,4},{3,5},{4,2},{5,3},{6,8},{7,9},{8,6},{9,7},{10,... | collective-permute-start | bytes 196616 | tf_op jit(solution)/shard_map/ppermute | solution.py:392
  32.2 1.7 %own.1.refs_1_.started = f32[256,128]{1,0:T(8,128)S(1)} custom-call(bf16[32,8,128,128]{3,2,1,0:T(8,128)(2,1)} %blocks_hbm.7, bf16[256,128]{1,0:T(8,128)(2,1)S(1)} %get-tuple-element.34.own, bf16[256,128]{1,0:T(8,128)(2,1)S(1)} %collective-permute-done.4._.mate), custom_call_target="tpu_custom_call" | custom-call | tf_op jit(solution)/shard_map/own/pallas_call | solution.py:435
  34.0 0.7 %all-to-all-done.1.refs_0_.got = bf16[8,48,128]{2,1,0:T(8,128)(2,1)S(1)} async-done(((bf16[8,48,128]{2,1,0:T(8,128)(2,1)}), bf16[8,48,128]{2,1,0:T(8,128)(2,1)S(1)}, u32[]{:S(2)}, u32[]{:S(2)}) %all-to-all-start.1) | async-done | bytes 98336 | tf_op jit(solution)/shard_map/all_to_all | solution.py:446
  34.6 2.5 %fetch.3 = (bf16[32,5,128,128]{3,2,1,0:T(8,128)(2,1)S(1)}, f32[8,128]{1,0:T(8,128)S(1)}) custom-call(bf16[32,8,128,128]{3,2,1,0:T(8,128)(2,1)} %blocks_hbm.7, bf16[8,48,128]{2,1,0:T(8,128)(2,1)S(1)} %all-to-all-done.1.refs_0_.got, f32[256,128]{1,0:T(8,128)S(1)} %own.1.refs_1_.started), custom_call_target="tpu_custom_call" | custom-call | tf_op jit(solution)/shard_map/fetch/pallas_call | solution.py:435
  37.2 0.4 collective-permute-done.5.even
  37.6 0.1 collective-permute-start.7
  37.7 1.4 %collective-permute-done.7.received = bf16[640,128]{1,0:T(8,128)(2,1)S(1)} collective-permute-done((bf16[640,128]{1,0:T(8,128)(2,1)S(1)}, bf16[640,128]{1,0:T(8,128)(2,1)S(1)}, u32[]{:S(2)}, u32[]{:S(2)}) %collective-permute-start.7) | collective-permute-done | bytes 163872 | tf_op jit(solution)/shard_map/ppermute | solution.py:392
  39.1 3.3 %operator_two.1 = (f32[256,128]{1,0:T(8,128)S(1)}, bf16[16,8,128]{2,1,0:T(8,128)(2,1)S(1)}) custom-call(bf16[256,128]{1,0:T(8,128)(2,1)S(1)} %get-tuple-element.34.own, bf16[256,128]{1,0:T(8,128)(2,1)S(1)} %collective-permute-done.4._.mate, bf16[256,128]{1,0:T(8,128)(2,1)S(1)} %collective-permute-done.5.even, ...), custom_call_target="tpu_custom_call" | custom-call | tf_op jit(solution)/shard_map/operator_two/pallas_call | solution.py:435
  42.3 8.8 %all_to_all.15.got = bf16[16,8,128]{2,1,0:T(8,128)(2,1)S(1)} all-to-all(bf16[16,8,128]{2,1,0:T(8,128)(2,1)S(1)} %get-tuple-element.39), channel_id=1, replica_groups={{4,5,6,7,8,9,10,11,12,13,14,15,0,1,2,3},{20,21,22,23,24,25,26,27,28,29,..., dimensions={0} | all-to-all | bytes 65536 | tf_op jit(solution)/shard_map/all_to_all | solution.py:450
  51.1 1.5 %finish.1 = (f32[8,4096]{1,0:T(8,128)}, f32[8,4096]{1,0:T(8,128)}) custom-call(f32[256,128]{1,0:T(8,128)S(1)} %get-tuple-element.21.b, f32[256,128]{1,0:T(8,128)S(1)} %get-tuple-element.33.image, f32[256,128]{1,0:T(8,128)S(1)} %get-tuple-element.38.candidate, bf16[640,128]{1,0:T(8,128)(2,1)S(1)} %relay.3.sent, ...), custom_call_target="tpu_custom_call" | custom-call | tf_op jit(solution)/shard_map/finish/pallas_call | solution.py:435
  (8 shorter events, 0.0 us)
Async XLA Ops:
  2.5 13.3 %all-to-all-start = ((bf16[8,32,128]{2,1,0:T(8,128)(2,1)}), bf16[8,32,128]{2,1,0:T(8,128)(2,1)S(1)}, u32[]{:S(2)}, u32[]{:S(2)}) async-start(bf16[8,32,128]{2,1,0:T(8,128)(2,1)} %get-tuple-element.23), calls=%async_computation | async-start | bytes 131072 | tf_op jit(solution)/shard_map/all_to_all | solution.py:446
  10.3 3.3 %collective-permute-start = (bf16[256,128]{1,0:T(8,128)(2,1)S(1)}, bf16[256,128]{1,0:T(8,128)(2,1)S(1)}, u32[]{:S(2)}, u32[]{:S(2)}) collective-permute-start(bf16[256,128]{1,0:T(8,128)(2,1)S(1)} %get-tuple-element.22.own), channel_id=1, source_target_pairs={{0,1},{1,0},{2,3},{3,2},{4,5},{5,4},{6,7},{7,6},{8,9},{9,8},{10,11... | collective-permute-start | bytes 196616 | tf_op jit(solution)/shard_map/ppermute | solution.py:392
  10.3 8.4 %collective-permute-start.2 = (bf16[256,128]{1,0:T(8,128)(2,1)S(1)}, bf16[256,128]{1,0:T(8,128)(2,1)S(1)}, u32[]{:S(2)}, u32[]{:S(2)}) collective-permute-start(bf16[256,128]{1,0:T(8,128)(2,1)S(1)} %get-tuple-element.22.own), channel_id=1, source_target_pairs={{0,14},{1,15},{2,4},{3,5},{4,2},{5,3},{6,8},{7,9},{8,6},{9,7},{10,... | collective-permute-start | bytes 196616 | tf_op jit(solution)/shard_map/ppermute | solution.py:392
  13.6 5.3 %collective-permute-start.1 = (bf16[256,128]{1,0:T(8,128)(2,1)S(1)}, bf16[256,128]{1,0:T(8,128)(2,1)S(1)}, u32[]{:S(2)}, u32[]{:S(2)}) collective-permute-start(bf16[256,128]{1,0:T(8,128)(2,1)S(1)} %get-tuple-element.22.own), channel_id=1, source_target_pairs={{0,2},{1,3},{2,0},{3,1},{4,6},{5,7},{6,4},{7,5},{8,10},{9,11},{10,... | collective-permute-start | bytes 196616 | tf_op jit(solution)/shard_map/ppermute | solution.py:392
  19.0 1.8 %collective-permute-start.3 = (bf16[512,128]{1,0:T(8,128)(2,1)S(1)}, bf16[512,128]{1,0:T(8,128)(2,1)S(1)}, u32[]{:S(2)}, u32[]{:S(2)}) collective-permute-start(bf16[512,128]{1,0:T(8,128)(2,1)S(1)} %relay.2._.sent), channel_id=1, source_target_pairs={{0,1},{1,0},{2,3},{3,2},{4,5},{5,4},{6,7},{7,6},{8,9},{9,8},{10,11... | collective-permute-start | bytes 393224 | tf_op jit(solution)/shard_map/ppermute | solution.py:392
  25.0 9.6 %all-to-all-start.1 = ((bf16[8,48,128]{2,1,0:T(8,128)(2,1)}), bf16[8,48,128]{2,1,0:T(8,128)(2,1)S(1)}, u32[]{:S(2)}, u32[]{:S(2)}) async-start(bf16[8,48,128]{2,1,0:T(8,128)(2,1)} %get-tuple-element.35), calls=%async_computation.1 | async-start | bytes 196608 | tf_op jit(solution)/shard_map/all_to_all | solution.py:446
  28.9 3.3 %collective-permute-start.4 = (bf16[256,128]{1,0:T(8,128)(2,1)S(1)}, bf16[256,128]{1,0:T(8,128)(2,1)S(1)}, u32[]{:S(2)}, u32[]{:S(2)}) collective-permute-start(bf16[256,128]{1,0:T(8,128)(2,1)S(1)} %get-tuple-element.34.own), channel_id=1, source_target_pairs={{0,1},{1,0},{2,3},{3,2},{4,5},{5,4},{6,7},{7,6},{8,9},{9,8},{10,11... | collective-permute-start | bytes 196616 | tf_op jit(solution)/shard_map/ppermute | solution.py:392
  29.0 8.2 %collective-permute-start.6 = (bf16[256,128]{1,0:T(8,128)(2,1)S(1)}, bf16[256,128]{1,0:T(8,128)(2,1)S(1)}, u32[]{:S(2)}, u32[]{:S(2)}) collective-permute-start(bf16[256,128]{1,0:T(8,128)(2,1)S(1)} %get-tuple-element.34.own), channel_id=1, source_target_pairs={{0,14},{1,15},{2,4},{3,5},{4,2},{5,3},{6,8},{7,9},{8,6},{9,7},{10,... | collective-permute-start | bytes 196616 | tf_op jit(solution)/shard_map/ppermute | solution.py:392
  32.2 5.4 %collective-permute-start.5 = (bf16[256,128]{1,0:T(8,128)(2,1)S(1)}, bf16[256,128]{1,0:T(8,128)(2,1)S(1)}, u32[]{:S(2)}, u32[]{:S(2)}) collective-permute-start(bf16[256,128]{1,0:T(8,128)(2,1)S(1)} %get-tuple-element.34.own), channel_id=1, source_target_pairs={{0,2},{1,3},{2,0},{3,1},{4,6},{5,7},{6,4},{7,5},{8,10},{9,11},{10,... | collective-permute-start | bytes 196616 | tf_op jit(solution)/shard_map/ppermute | solution.py:392
  37.6 1.5 %collective-permute-start.7 = (bf16[640,128]{1,0:T(8,128)(2,1)S(1)}, bf16[640,128]{1,0:T(8,128)(2,1)S(1)}, u32[]{:S(2)}, u32[]{:S(2)}) collective-permute-start(bf16[640,128]{1,0:T(8,128)(2,1)S(1)} %relay.3.sent), channel_id=1, source_target_pairs={{0,1},{1,0},{2,3},{3,2},{4,5},{5,4},{6,7},{7,6},{8,9},{9,8},{10,11... | collective-permute-start | bytes 491528 | tf_op jit(solution)/shard_map/ppermute | solution.py:392

commit v21 on v20

--- a/solution.py
+++ b/solution.py
@@ -68,14 +68,16 @@
     stacked = jnp.concatenate(tiles, axis=0)
     high = stacked.astype(bf16)
     low = (stacked - high.astype(f32)).astype(bf16)
-    both = dot(jnp.concatenate([high, low], axis=0), basis[pl.ds(group * LANES, LANES), :], (1, 1))
-    rows = len(tiles) * R
-    both = both[:rows] + both[rows:]
+    return dot(jnp.concatenate([high, low], axis=0), basis[pl.ds(group * LANES, LANES), :], (1, 1))
+
+
+def collect(products, per_group):
+    rows = per_group * R
+    both = products[:rows] + products[rows:]
     lane = lane_ids()
-    rank = LANES // len(tiles)
     tile = jnp.zeros((R, LANES), f32)
-    for m in range(len(tiles)):
-        tile = jnp.where(lane // rank == m, both[m * R : (m + 1) * R], tile)
+    for m in range(per_group):
+        tile = jnp.where(lane // (LANES // per_group) == m, both[m * R : (m + 1) * R], tile)
     return tile
 
 
@@ -101,7 +103,8 @@
     field[...] = jnp.concatenate(tiles, axis=0)
     lowered[...] = jnp.concatenate(tiles, axis=0).astype(bf16)
     groups = [tiles[g : g + per_group] for g in range(0, clusters, per_group)]
-    write_payload(payload, [compress(group, basis, g) for g, group in enumerate(groups)], [])
+    products = [compress(group, basis, g) for g, group in enumerate(groups)]
+    write_payload(payload, [collect(product, per_group) for product in products], [])
 
 
 def window_place(distance, clusters, me):
@@ -259,41 +262,60 @@
             tile = jnp.where(lane // rank == k, pltpu.roll(found, places[2 * slots + k, i], 1), tile)
         return tile
 
-    picked = []
-    for i in range(0, clusters, 2):
+    def product(i):
         sources = jnp.concatenate(
             [jnp.concatenate([fetch(k, i), fetch(k, i + 1)], axis=0) for k in range(first, slots)], axis=1
         )
         weights = jnp.concatenate(
             [jnp.concatenate([block(k, i), block(k, i + 1)], axis=0) for k in range(first, slots)], axis=1
         )
-        both = dot(sources.astype(bf16), weights, (1, 1))
+        return dot(sources.astype(bf16), weights, (1, 1))
+
+    def settle(i, both):
         parts = [both[:R, :LANES], both[R:, LANES:]]
         if started is not None:
             parts = [part + rows_of(started, i + n) for n, part in enumerate(parts)]
         near[pl.ds(i * R, 2 * R), :] = jnp.concatenate(parts, axis=0)
-        if 2 * i < clusters:
-            picked += [pick(n) for n in range(2 * i, 2 * i + 4)]
-        if 2 * i == clusters - 4:
-            picked = jnp.concatenate(picked, axis=0).astype(bf16)
-            crossed = dot(picked, high[...]) + dot(picked, low[...])
-            expanded_high, expanded_low = [], []
-            for s in range(rank * clusters // LANES):
-                tile = jnp.zeros((R, LANES), f32)
-                for n in range(clusters):
-                    part = crossed[n * R : (n + 1) * R, s * LANES : (s + 1) * LANES]
-                    tile = jnp.where(lane % clusters == n, part, tile)
-                tile_high = tile.astype(bf16).astype(f32)
-                tile_low = tile - tile_high
-                for source, kept in ((tile_high, expanded_high), (tile_low, expanded_low)):
-                    spread = [jnp.where(lane % clusters == n, source, 0.0) for n in range(clusters)]
-                    kept.append(jnp.concatenate(spread, axis=0).astype(bf16))
-            far[...] = dot(jnp.concatenate(expanded_high, axis=1), target[...]) + dot(
-                jnp.concatenate(expanded_low, axis=1), target[...]
-            )
-        if 2 * i >= clusters:
-            for n in range(2 * i - clusters, 2 * i - clusters + 4):
+
+    def expand(crossed):
+        spread = []
+        for s in range(rank * clusters // LANES):
+            tile = jnp.zeros((R, LANES), f32)
+            for n in range(clusters):
+                part = crossed[n * R : (n + 1) * R, s * LANES : (s + 1) * LANES]
+                tile = jnp.where(lane % clusters == n, part, tile)
+            tile_high = tile.astype(bf16).astype(f32)
+            for n, source in enumerate((tile_high, tile - tile_high)):
+                held = [jnp.where(lane % clusters == c, source, 0.0) for c in range(clusters)]
+                spread.append((n, jnp.concatenate(held, axis=0).astype(bf16)))
+        return [jnp.concatenate([part for m, part in spread if m == n], axis=1) for n in range(2)]
+
+    pairs = clusters // 2
+    middle = pairs // 2
+    picked, pending, done = [], None, 0
+    for p in range(pairs):
+        both = product(2 * p)
+        if pending is not None:
+            settle(2 * p - 2, pending)
+        pending = both
+        if p < middle:
+            picked += [pick(n) for n in range(4 * p, 4 * p + 4)]
+        if p == middle - 1:
+            chosen = jnp.concatenate(picked, axis=0).astype(bf16)
+            crossed = [dot(chosen, high[...]), dot(chosen, low[...])]
+        if p == middle:
+            spread = expand(crossed[0] + crossed[1])
+            made = [dot(part, target[...]) for part in spread]
+        if p == middle + 1:
+            far[...] = made[0] + made[1]
+        if p > middle + 1:
+            ready = min(2 * p, done + 6)
+            for n in range(done, ready):
                 finish(n)
+            done = ready
+    settle(clusters - 2, pending)
+    for n in range(done, clusters):
+        finish(n)
 
 
 def first_kernel(
@@ -303,7 +325,7 @@
     clusters = near.shape[0] // R
     slabs, swaps = (own, mate, even, odd), (sent, received)
     each = clusters // per_group * R
-    tiles, parts = [], []
+    tiles, products, parts = [], [], []
     sums = [jnp.zeros((R, LANES), f32) for _ in range(3)]
 
     def finish(i):
@@ -316,12 +338,13 @@
             image[pl.ds((i - 1) * R, 2 * R), :] = both
             lowered[pl.ds((i - 1) * R, 2 * R), :] = both.astype(bf16)
         if i % per_group == per_group - 1:
-            parts.append(compress(tiles[-per_group:], basis, i // per_group))
+            products.append(compress(tiles[-per_group:], basis, i // per_group))
+            parts.extend(collect(product, per_group) for product in products[-2:-1])
 
     apply(
         per_group, each, slabs, places, ahead, blocks, swaps, high, low, target, near, far, window, table, finish, None
     )
-    write_payload(payload, parts, sums)
+    write_payload(payload, parts + [collect(products[-1], per_group)], sums)
 
 
 def arnoldi_one(bb, bw, ww):

time: 53 us -> 52.9 us (level)
  no operation moved by 1% of the time
where the time goes in v21:
time: 52.9 us; the launch traced here: 52.5 us
  Pallas kernels  21.1 us (40%)
  starting transfers between devices  18.5 us (35%)
  blocking collectives  8.81 us (17%)
  waiting for transfers between devices  3.29 us (6%)
  between operations  0.73 us (1%)
    pallas_call x11, Pallas kernels, call(): pl.pallas_call(kernel, out_shape=out, in_specs=ins, out_specs=jax.tree.ma...  21.1 us
    all_to_all x2, starting transfers between devices, gather(): return lax.all_to_all(block, 'rows', 0, 0, axis_index_groups=groups)  11.8 us
    all_to_all x1, blocking collectives, exchange(): return lax.all_to_all(block, 'rows', 0, 0, axis_index_groups=[group])  8.81 us
    ppermute x8, starting transfers between devices, swapped(): lax.ppermute(block, 'rows', [(i, partner(i)) for i in range(lax.axis_size...  6.74 us
    ppermute x8, waiting for transfers between devices, swapped(): lax.ppermute(block, 'rows', [(i, partner(i)) for i in range(lax.axis_size...  2 us
    all_to_all x2, waiting for transfers between devices, gather(): return lax.all_to_all(block, 'rows', 0, 0, axis_index_groups=groups)  1.29 us
  transfers between devices with their start and end apart: 10, of which 5 were waited for; matrix products, arithmetic and copies ran while one was open for 0% of the time, Pallas kernels for 20%

profile of v21, /device:TPU:0, one launch (start us, length us, event | category | flops | bytes accessed | tf_op | source)
XLA Modules:
  0.0 52.5 jit_solution(12660147522147066066)
XLA Ops:
  0.6 1.8 %start.1 = (f32[256,128]{1,0:T(8,128)S(1)}, bf16[512,128]{1,0:T(8,128)(2,1)S(1)}, bf16[256,128]{1,0:T(8,128)(2,1)S(1)}, bf16[8,32,128]{2,1,0:T(8,128)(2,1)}) custom-call(f32[8,4096]{1,0:T(8,128)} %b_hbm.1, bf16[512,128]{1,0:T(8,128)(2,1)} %bitcast.8), custom_call_target="tpu_custom_call" | custom-call | tf_op jit(solution)/shard_map/start/pallas_call | solution.py:458
  2.5 7.9 %all-to-all-start = ((bf16[8,32,128]{2,1,0:T(8,128)(2,1)}), bf16[8,32,128]{2,1,0:T(8,128)(2,1)S(1)}, u32[]{:S(2)}, u32[]{:S(2)}) async-start(bf16[8,32,128]{2,1,0:T(8,128)(2,1)} %get-tuple-element.23), calls=%async_computation | async-start | bytes 131072 | tf_op jit(solution)/shard_map/all_to_all | solution.py:469
  10.3 3.3 %collective-permute-start.2 = (bf16[256,128]{1,0:T(8,128)(2,1)S(1)}, bf16[256,128]{1,0:T(8,128)(2,1)S(1)}, u32[]{:S(2)}, u32[]{:S(2)}) collective-permute-start(bf16[256,128]{1,0:T(8,128)(2,1)S(1)} %get-tuple-element.22.own), channel_id=1, source_target_pairs={{0,14},{1,15},{2,4},{3,5},{4,2},{5,3},{6,8},{7,9},{8,6},{9,7},{10,... | collective-permute-start | bytes 196616 | tf_op jit(solution)/shard_map/ppermute | solution.py:415
  13.6 1.6 %ahead.1 = (bf16[32,2,128,128]{3,2,1,0:T(8,128)(2,1)S(1)}, f32[8,128]{1,0:T(8,128)S(1)}) custom-call(bf16[32,8,128,128]{3,2,1,0:T(8,128)(2,1)} %blocks_hbm.7, bf16[256,128]{1,0:T(8,128)(2,1)S(1)} %collective-permute-done.refs_0_.mate), custom_call_target="tpu_custom_call" | custom-call | tf_op jit(solution)/shard_map/ahead/pallas_call | solution.py:458
  15.2 0.6 %all-to-all-done.refs_0_.got = bf16[8,32,128]{2,1,0:T(8,128)(2,1)S(1)} async-done(((bf16[8,32,128]{2,1,0:T(8,128)(2,1)}), bf16[8,32,128]{2,1,0:T(8,128)(2,1)S(1)}, u32[]{:S(2)}, u32[]{:S(2)}) %all-to-all-start) | async-done | bytes 65568 | tf_op jit(solution)/shard_map/all_to_all | solution.py:469
  15.8 2.9 %fetch.2 = (bf16[32,6,128,128]{3,2,1,0:T(8,128)(2,1)S(1)}, f32[8,128]{1,0:T(8,128)S(1)}) custom-call(bf16[32,8,128,128]{3,2,1,0:T(8,128)(2,1)} %blocks_hbm.7, bf16[8,32,128]{2,1,0:T(8,128)(2,1)S(1)} %all-to-all-done.refs_0_.got, f32[8,128]{1,0:T(8,128)S(1)} %get-tuple-element.24.refs_1_), custom_call_target="tpu_custom_call" | custom-call | tf_op jit(solution)/shard_map/fetch/pallas_call | solution.py:458
  18.7 0.0 collective-permute-done.2.odd
  18.7 0.2 collective-permute-done.1.even
  19.0 0.1 collective-permute-start.3
  19.1 1.6 %prepare.1 = (s32[24,32]{1,0:T(8,128)S(1)}, bf16[128,512]{1,0:T(8,128)(2,1)S(1)}, bf16[128,512]{1,0:T(8,128)(2,1)S(1)}, bf16[512,128]{1,0:T(8,128)(2,1)S(1)}) custom-call(s32[8,32]{1,0:T(8,128)} %bitcast.9, s32[1,32]{1,0:T(1,128)} %bitcast.11, s32[8,32]{1,0:T(8,128)} %bitcast.10, f32[8,16,16,32]{3,2,1,0:T(8,128)} %bitcast.6, bf16[512,128]{1,0:T(8,128)(2,1)} %bitcast.7, ...), custom_call_target="tpu_custom_call" | custom-call | tf_op jit(solution)/shard_map/prepare/pallas_call | solution.py:458
  20.7 0.0 collective-permute-done.3.received
  20.7 4.2 %operator_one.1 = (f32[256,128]{1,0:T(8,128)S(1)}, bf16[256,128]{1,0:T(8,128)(2,1)S(1)}, bf16[8,48,128]{2,1,0:T(8,128)(2,1)}) custom-call(bf16[256,128]{1,0:T(8,128)(2,1)S(1)} %get-tuple-element.22.own, bf16[256,128]{1,0:T(8,128)(2,1)S(1)} %collective-permute-done.refs_0_.mate, bf16[256,128]{1,0:T(8,128)(2,1)S(1)} %collective-permute-done.1.even, ...), custom_call_target="tpu_custom_call" | custom-call | tf_op jit(solution)/shard_map/operator_one/pallas_call | solution.py:458
  25.0 3.9 %all-to-all-start.1 = ((bf16[8,48,128]{2,1,0:T(8,128)(2,1)}), bf16[8,48,128]{2,1,0:T(8,128)(2,1)S(1)}, u32[]{:S(2)}, u32[]{:S(2)}) async-start(bf16[8,48,128]{2,1,0:T(8,128)(2,1)} %get-tuple-element.35), calls=%async_computation.1 | async-start | bytes 196608 | tf_op jit(solution)/shard_map/all_to_all | solution.py:469
  28.9 0.0 collective-permute-start.4
  28.9 3.3 %collective-permute-start.6 = (bf16[256,128]{1,0:T(8,128)(2,1)S(1)}, bf16[256,128]{1,0:T(8,128)(2,1)S(1)}, u32[]{:S(2)}, u32[]{:S(2)}) collective-permute-start(bf16[256,128]{1,0:T(8,128)(2,1)S(1)} %get-tuple-element.34.own), channel_id=1, source_target_pairs={{0,14},{1,15},{2,4},{3,5},{4,2},{5,3},{6,8},{7,9},{8,6},{9,7},{10,... | collective-permute-start | bytes 196616 | tf_op jit(solution)/shard_map/ppermute | solution.py:415
  32.2 1.7 %own.1.refs_1_.started = f32[256,128]{1,0:T(8,128)S(1)} custom-call(bf16[32,8,128,128]{3,2,1,0:T(8,128)(2,1)} %blocks_hbm.7, bf16[256,128]{1,0:T(8,128)(2,1)S(1)} %get-tuple-element.34.own, bf16[256,128]{1,0:T(8,128)(2,1)S(1)} %collective-permute-done.4._.mate), custom_call_target="tpu_custom_call" | custom-call | tf_op jit(solution)/shard_map/own/pallas_call | solution.py:458
  33.9 0.7 %all-to-all-done.1.refs_0_.got = bf16[8,48,128]{2,1,0:T(8,128)(2,1)S(1)} async-done(((bf16[8,48,128]{2,1,0:T(8,128)(2,1)}), bf16[8,48,128]{2,1,0:T(8,128)(2,1)S(1)}, u32[]{:S(2)}, u32[]{:S(2)}) %all-to-all-start.1) | async-done | bytes 98336 | tf_op jit(solution)/shard_map/all_to_all | solution.py:469
  34.6 2.5 %fetch.3 = (bf16[32,5,128,128]{3,2,1,0:T(8,128)(2,1)S(1)}, f32[8,128]{1,0:T(8,128)S(1)}) custom-call(bf16[32,8,128,128]{3,2,1,0:T(8,128)(2,1)} %blocks_hbm.7, bf16[8,48,128]{2,1,0:T(8,128)(2,1)S(1)} %all-to-all-done.1.refs_0_.got, f32[256,128]{1,0:T(8,128)S(1)} %own.1.refs_1_.started), custom_call_target="tpu_custom_call" | custom-call | tf_op jit(solution)/shard_map/fetch/pallas_call | solution.py:458
  37.1 0.4 collective-permute-done.5.even
  37.5 0.1 collective-permute-start.7
  37.6 1.4 %collective-permute-done.7.received = bf16[640,128]{1,0:T(8,128)(2,1)S(1)} collective-permute-done((bf16[640,128]{1,0:T(8,128)(2,1)S(1)}, bf16[640,128]{1,0:T(8,128)(2,1)S(1)}, u32[]{:S(2)}, u32[]{:S(2)}) %collective-permute-start.7) | collective-permute-done | bytes 163872 | tf_op jit(solution)/shard_map/ppermute | solution.py:415
  39.0 3.2 %operator_two.1 = (f32[256,128]{1,0:T(8,128)S(1)}, bf16[16,8,128]{2,1,0:T(8,128)(2,1)S(1)}) custom-call(bf16[256,128]{1,0:T(8,128)(2,1)S(1)} %get-tuple-element.34.own, bf16[256,128]{1,0:T(8,128)(2,1)S(1)} %collective-permute-done.4._.mate, bf16[256,128]{1,0:T(8,128)(2,1)S(1)} %collective-permute-done.5.even, ...), custom_call_target="tpu_custom_call" | custom-call | tf_op jit(solution)/shard_map/operator_two/pallas_call | solution.py:458
  42.2 8.8 %all_to_all.15.got = bf16[16,8,128]{2,1,0:T(8,128)(2,1)S(1)} all-to-all(bf16[16,8,128]{2,1,0:T(8,128)(2,1)S(1)} %get-tuple-element.39), channel_id=1, replica_groups={{4,5,6,7,8,9,10,11,12,13,14,15,0,1,2,3},{20,21,22,23,24,25,26,27,28,29,..., dimensions={0} | all-to-all | bytes 65536 | tf_op jit(solution)/shard_map/all_to_all | solution.py:473
  51.0 1.5 %finish.1 = (f32[8,4096]{1,0:T(8,128)}, f32[8,4096]{1,0:T(8,128)}) custom-call(f32[256,128]{1,0:T(8,128)S(1)} %get-tuple-element.21.b, f32[256,128]{1,0:T(8,128)S(1)} %get-tuple-element.33.image, f32[256,128]{1,0:T(8,128)S(1)} %get-tuple-element.38.candidate, bf16[640,128]{1,0:T(8,128)(2,1)S(1)} %relay.3.sent, ...), custom_call_target="tpu_custom_call" | custom-call | tf_op jit(solution)/shard_map/finish/pallas_call | solution.py:458
  (8 shorter events, 0.0 us)
Async XLA Ops:
  2.5 13.3 %all-to-all-start = ((bf16[8,32,128]{2,1,0:T(8,128)(2,1)}), bf16[8,32,128]{2,1,0:T(8,128)(2,1)S(1)}, u32[]{:S(2)}, u32[]{:S(2)}) async-start(bf16[8,32,128]{2,1,0:T(8,128)(2,1)} %get-tuple-element.23), calls=%async_computation | async-start | bytes 131072 | tf_op jit(solution)/shard_map/all_to_all | solution.py:469
  10.3 3.3 %collective-permute-start = (bf16[256,128]{1,0:T(8,128)(2,1)S(1)}, bf16[256,128]{1,0:T(8,128)(2,1)S(1)}, u32[]{:S(2)}, u32[]{:S(2)}) collective-permute-start(bf16[256,128]{1,0:T(8,128)(2,1)S(1)} %get-tuple-element.22.own), channel_id=1, source_target_pairs={{0,1},{1,0},{2,3},{3,2},{4,5},{5,4},{6,7},{7,6},{8,9},{9,8},{10,11... | collective-permute-start | bytes 196616 | tf_op jit(solution)/shard_map/ppermute | solution.py:415
  10.3 8.4 %collective-permute-start.2 = (bf16[256,128]{1,0:T(8,128)(2,1)S(1)}, bf16[256,128]{1,0:T(8,128)(2,1)S(1)}, u32[]{:S(2)}, u32[]{:S(2)}) collective-permute-start(bf16[256,128]{1,0:T(8,128)(2,1)S(1)} %get-tuple-element.22.own), channel_id=1, source_target_pairs={{0,14},{1,15},{2,4},{3,5},{4,2},{5,3},{6,8},{7,9},{8,6},{9,7},{10,... | collective-permute-start | bytes 196616 | tf_op jit(solution)/shard_map/ppermute | solution.py:415
  13.6 5.3 %collective-permute-start.1 = (bf16[256,128]{1,0:T(8,128)(2,1)S(1)}, bf16[256,128]{1,0:T(8,128)(2,1)S(1)}, u32[]{:S(2)}, u32[]{:S(2)}) collective-permute-start(bf16[256,128]{1,0:T(8,128)(2,1)S(1)} %get-tuple-element.22.own), channel_id=1, source_target_pairs={{0,2},{1,3},{2,0},{3,1},{4,6},{5,7},{6,4},{7,5},{8,10},{9,11},{10,... | collective-permute-start | bytes 196616 | tf_op jit(solution)/shard_map/ppermute | solution.py:415
  19.0 1.8 %collective-permute-start.3 = (bf16[512,128]{1,0:T(8,128)(2,1)S(1)}, bf16[512,128]{1,0:T(8,128)(2,1)S(1)}, u32[]{:S(2)}, u32[]{:S(2)}) collective-permute-start(bf16[512,128]{1,0:T(8,128)(2,1)S(1)} %relay.2._.sent), channel_id=1, source_target_pairs={{0,1},{1,0},{2,3},{3,2},{4,5},{5,4},{6,7},{7,6},{8,9},{9,8},{10,11... | collective-permute-start | bytes 393224 | tf_op jit(solution)/shard_map/ppermute | solution.py:415
  25.0 9.6 %all-to-all-start.1 = ((bf16[8,48,128]{2,1,0:T(8,128)(2,1)}), bf16[8,48,128]{2,1,0:T(8,128)(2,1)S(1)}, u32[]{:S(2)}, u32[]{:S(2)}) async-start(bf16[8,48,128]{2,1,0:T(8,128)(2,1)} %get-tuple-element.35), calls=%async_computation.1 | async-start | bytes 196608 | tf_op jit(solution)/shard_map/all_to_all | solution.py:469
  28.9 3.3 %collective-permute-start.4 = (bf16[256,128]{1,0:T(8,128)(2,1)S(1)}, bf16[256,128]{1,0:T(8,128)(2,1)S(1)}, u32[]{:S(2)}, u32[]{:S(2)}) collective-permute-start(bf16[256,128]{1,0:T(8,128)(2,1)S(1)} %get-tuple-element.34.own), channel_id=1, source_target_pairs={{0,1},{1,0},{2,3},{3,2},{4,5},{5,4},{6,7},{7,6},{8,9},{9,8},{10,11... | collective-permute-start | bytes 196616 | tf_op jit(solution)/shard_map/ppermute | solution.py:415
  28.9 8.2 %collective-permute-start.6 = (bf16[256,128]{1,0:T(8,128)(2,1)S(1)}, bf16[256,128]{1,0:T(8,128)(2,1)S(1)}, u32[]{:S(2)}, u32[]{:S(2)}) collective-permute-start(bf16[256,128]{1,0:T(8,128)(2,1)S(1)} %get-tuple-element.34.own), channel_id=1, source_target_pairs={{0,14},{1,15},{2,4},{3,5},{4,2},{5,3},{6,8},{7,9},{8,6},{9,7},{10,... | collective-permute-start | bytes 196616 | tf_op jit(solution)/shard_map/ppermute | solution.py:415
  32.1 5.4 %collective-permute-start.5 = (bf16[256,128]{1,0:T(8,128)(2,1)S(1)}, bf16[256,128]{1,0:T(8,128)(2,1)S(1)}, u32[]{:S(2)}, u32[]{:S(2)}) collective-permute-start(bf16[256,128]{1,0:T(8,128)(2,1)S(1)} %get-tuple-element.34.own), channel_id=1, source_target_pairs={{0,2},{1,3},{2,0},{3,1},{4,6},{5,7},{6,4},{7,5},{8,10},{9,11},{10,... | collective-permute-start | bytes 196616 | tf_op jit(solution)/shard_map/ppermute | solution.py:415
  37.5 1.5 %collective-permute-start.7 = (bf16[640,128]{1,0:T(8,128)(2,1)S(1)}, bf16[640,128]{1,0:T(8,128)(2,1)S(1)}, u32[]{:S(2)}, u32[]{:S(2)}) collective-permute-start(bf16[640,128]{1,0:T(8,128)(2,1)S(1)} %relay.3.sent), channel_id=1, source_target_pairs={{0,1},{1,0},{2,3},{3,2},{4,5},{5,4},{6,7},{7,6},{8,9},{9,8},{10,11... | collective-permute-start | bytes 491528 | tf_op jit(solution)/shard_map/ppermute | solution.py:415

commit v22 on v21

--- a/solution.py
+++ b/solution.py
@@ -96,12 +96,12 @@
     ]
     for copy in copies:
         copy.start()
-    for copy in copies:
-        copy.wait()
+    copies[0].wait()
     clusters = b.shape[1] // LANES
     tiles = [b[:, j * LANES : (j + 1) * LANES] for j in range(clusters)]
     field[...] = jnp.concatenate(tiles, axis=0)
     lowered[...] = jnp.concatenate(tiles, axis=0).astype(bf16)
+    copies[1].wait()
     groups = [tiles[g : g + per_group] for g in range(0, clusters, per_group)]
     products = [compress(group, basis, g) for g, group in enumerate(groups)]
     write_payload(payload, [collect(product, per_group) for product in products], [])
@@ -118,14 +118,15 @@
     return chosen * clusters + lax.rem(distance, clusters)
 
 
-def prepare_kernel(
-    axis, size, middle, near_cols_hbm, near_counts_hbm, far_cols_hbm, coupling_hbm, target_hbm, _,
-    places, high_out, low_out, target_out, near_cols, near_counts, far_cols, coupling, target, sems,
+def ahead_kernel(
+    axis, size, middle, first, rank, near_cols_hbm, near_counts_hbm, far_cols_hbm, blocks_hbm, _,
+    places, ahead, token, near_cols, near_counts, far_cols, sems,
 ):
-    pairs = (
-        (near_cols_hbm, near_cols), (near_counts_hbm, near_counts), (far_cols_hbm, far_cols),
-        (coupling_hbm, coupling), (target_hbm, target),
-    )
+    half = ahead.shape[0] // 2
+    pairs = [(near_cols_hbm, near_cols), (near_counts_hbm, near_counts), (far_cols_hbm, far_cols)]
+    for n in range(2):
+        span = pl.ds(n * half, half)
+        pairs.append((blocks_hbm.at[span, pl.ds(first, ahead.shape[1])], ahead.at[span]))
     copies = [pltpu.make_async_copy(source, to, sems.at[n]) for n, (source, to) in enumerate(pairs)]
     for copy in copies:
         copy.start()
@@ -137,22 +138,39 @@
     distance = near_cols[...] - me * clusters + 2 * clusters
     distance = jnp.where(distance < 0, distance + every, distance)
     distance = jnp.where(distance >= every, distance - every, distance)
-    live = lax.broadcasted_iota(jnp.int32, (slots, clusters), 0) < near_counts[...]
+    slot = lax.broadcasted_iota(jnp.int32, (slots, clusters), 0)
+    live = slot < near_counts[...]
     places[:slots, :] = jnp.where(live, window_place(distance, clusters, me), 5 * clusters) * R
     owner = lax.div(far_cols[...], clusters)
     other_core = (owner ^ me) & 1
     chips = size // 2
     chip = lax.rem(owner // 2 + (chips - middle), chips)
-    rank = coupling.shape[1]
     per_group = LANES // rank
     inside = lax.rem(far_cols[...], clusters)
     tile = (other_core * chips + chip) * (clusters // per_group) + lax.div(inside, per_group)
     places[slots : 2 * slots, :] = tile * R
-    slot = lax.broadcasted_iota(jnp.int32, (slots, clusters), 0)
     places[2 * slots :, :] = ((slot - inside) * rank) & (LANES - 1)
-    for copy in copies[3:5]:
+    token[...] = jnp.zeros_like(token)
+    for copy in copies[3:]:
         copy.wait()
+
+
+def prepare_kernel(coupling_hbm, target_hbm, _, high_out, low_out, target_out, coupling, target, sems):
+    copies = [
+        pltpu.make_async_copy(target_hbm, target, sems.at[0]),
+        pltpu.make_async_copy(coupling_hbm, coupling, sems.at[1]),
+    ]
+    for copy in copies:
+        copy.start()
     slots, rank, _, clusters = coupling.shape
+    size = rank * clusters
+    row = lax.broadcasted_iota(jnp.int32, (size, 1), 0)
+    column = lax.broadcasted_iota(jnp.int32, (size, size), 1)
+    wanted = lax.rem(row, clusters) * rank + lax.div(row, clusters)
+    picks = (column == wanted).astype(bf16)
+    copies[0].wait()
+    target_out[...] = dot(picks, target[...]).astype(bf16)
+    copies[1].wait()
     per_tile = LANES // clusters
     for s in range(rank // per_tile):
         pieces = [
@@ -162,11 +180,6 @@
         high = tile.astype(bf16)
         high_out[:, s * LANES : (s + 1) * LANES] = high
         low_out[:, s * LANES : (s + 1) * LANES] = (tile - high.astype(f32)).astype(bf16)
-    size = rank * clusters
-    row = lax.broadcasted_iota(jnp.int32, (size, 1), 0)
-    column = lax.broadcasted_iota(jnp.int32, (size, size), 1)
-    wanted = lax.rem(row, clusters) * rank + lax.div(row, clusters)
-    target_out[...] = dot((column == wanted).astype(bf16), target[...]).astype(bf16)
 
 
 def fetch_kernel(slots, blocks_hbm, *refs):
@@ -388,10 +401,27 @@
         sums_out[device] = tile
 
 
-def finish_kernel(per_group, unknowns, b, image, candidate, sent, received, got, solution_out, next_out):
+def ready_kernel(per_group, unknowns, b, image, sent, received, _, first, second, known):
     clusters = b.shape[0] // R
-    sums = read_sums(tails((sent, received), b.shape[0], clusters // per_group * R), 3, unknowns)
-    start_norm, h11, h21, v11, v22, v12 = arnoldi_one(*sums)
+    means = read_sums(tails((sent, received), b.shape[0], clusters // per_group * R), 3, unknowns)
+    values = arnoldi_one(*means)
+    start_norm, h11, h21, _, _, _ = values
+    lane = lane_ids()
+    tile = jnp.zeros((R, LANES), f32)
+    for n, value in enumerate(values):
+        tile = jnp.where(lane == n, value, tile)
+    known[...] = tile
+    scale, inverse = 1.0 / start_norm, 1.0 / h21
+    for j in range(clusters):
+        span = pl.ds(j * R, R)
+        one = b[span, :] * scale
+        first[span, :] = one
+        second[span, :] = (image[span, :] * scale - h11 * one) * inverse
+
+
+def finish_kernel(unknowns, first, second, candidate, known, got, solution_out, next_out):
+    clusters = first.shape[0] // R
+    start_norm, h11, h21, v11, v22, v12 = [known[:, n : n + 1] for n in range(6)]
     h12, h22, ww = read_sums([got[device] for device in range(got.shape[0])], 3, unknowns)
     uu = ww - 2.0 * (h12 * h12 + h22 * h22) + h12 * h12 * v11 + h22 * h22 * v22 + 2.0 * h12 * h22 * v12
     h32 = jnp.sqrt(jnp.maximum(uu, 0.0) + epsilon)
@@ -402,13 +432,12 @@
     det = g11 * g22 - g12 * g12
     y1 = (g22 * t1 - g12 * t2) / det
     y2 = (g11 * t2 - g12 * t1) / det
-    scale, inverse, last = 1.0 / start_norm, 1.0 / h21, 1.0 / h32
+    last = 1.0 / h32
     for j in range(clusters):
         span = slice(j * LANES, (j + 1) * LANES)
-        first = rows_of(b, j) * scale
-        second = (rows_of(image, j) * scale - h11 * first) * inverse
-        solution_out[:, span] = y1 * first + y2 * second
-        next_out[:, span] = (rows_of(candidate, j) - h12 * first - h22 * second) * last
+        one, two = rows_of(first, j), rows_of(second, j)
+        solution_out[:, span] = y1 * one + y2 * two
+        next_out[:, span] = (rows_of(candidate, j) - h12 * one - h22 * two) * last
 
 
 def swapped(block, partner):
@@ -506,26 +535,35 @@
         return ahead, rest, sent, swapped(sent, core_mate)
 
     late = (1 + early, slots - 1 - early)
-    ahead, token = fetch("ahead", [(1, early)], 2, held[1])
+    places, ahead, token = call(
+        functools.partial(ahead_kernel, "rows", size, middle, 1, rank), "ahead",
+        (
+            shape(3 * slots, clusters, dtype=jnp.int32), pltpu.VMEM((clusters, early, LANES, LANES), bf16),
+            shape(R, LANES),
+        ),
+        [HBM] * 4 + [ANY], in_hbm(near_cols.T), in_hbm(near_counts.reshape(1, clusters)), in_hbm(far_cols.T), blocks,
+        held[1],
+        scratch_shapes=[
+            scratch(slots, clusters, dtype=jnp.int32), scratch(1, clusters, dtype=jnp.int32),
+            scratch(slots, clusters, dtype=jnp.int32), pltpu.SemaphoreType.DMA((5,)),
+        ],
+    )
+    ahead = pltpu.with_memory_space_constraint(ahead, pltpu.VMEM)
     here = arrived(got, held, [(0, 1), late], token)
-    prepared = call(
-        functools.partial(prepare_kernel, "rows", size, middle), "prepare",
+    made = call(
+        prepare_kernel, "prepare",
         (
-            shape(3 * slots, clusters, dtype=jnp.int32),
             shape(slots * rank, rank * clusters, dtype=bf16),
             shape(slots * rank, rank * clusters, dtype=bf16),
             shape(rank * clusters, LANES, dtype=bf16),
         ),
-        [HBM] * 5 + [ANY], in_hbm(near_cols.T), in_hbm(near_counts.reshape(1, clusters)), in_hbm(far_cols.T),
+        [HBM] * 2 + [ANY],
         in_hbm(jnp.transpose(coupling, (1, 2, 3, 0))), in_hbm(target_basis.reshape(clusters * rank, LANES)), here[2],
         scratch_shapes=[
-            scratch(slots, clusters, dtype=jnp.int32), scratch(1, clusters, dtype=jnp.int32),
-            scratch(slots, clusters, dtype=jnp.int32),
             scratch(slots, rank, rank, clusters), scratch(clusters * rank, LANES, dtype=bf16),
-            pltpu.SemaphoreType.DMA((5,)),
+            pltpu.SemaphoreType.DMA((2,)),
         ],
     )
-    places, *made = prepared
     kept = [scratch(rows, LANES), scratch(rows, LANES), scratch(5 * rows + R, LANES), scratch(size * head, LANES)]
     operands = [VMEM] * 4 + [SMEM] + [VMEM] * 9
     image, lowered, payload = call(
@@ -548,9 +586,15 @@
         (shape(rows, LANES), shape(size, R, LANES, dtype=bf16)),
         operands + [VMEM], *held, places, *here, *made, field, image, started, scratch_shapes=kept,
     )
+    got = exchange(sums)
+    first, second, known = call(
+        functools.partial(ready_kernel, per_group, unknowns), "ready",
+        (shape(rows, LANES), shape(rows, LANES), shape(R, LANES)),
+        [VMEM] * 4 + [ANY], field, image, *here[2:], sums,
+    )
     return call(
-        functools.partial(finish_kernel, per_group, unknowns), "finish", (shape(R, width), shape(R, width)),
-        [VMEM] * 6, field, image, candidate, *here[2:], exchange(sums),
+        functools.partial(finish_kernel, unknowns), "finish", (shape(R, width), shape(R, width)),
+        [VMEM] * 5, first, second, candidate, known, got,
     )
 
 

time: 52.9 us -> 55.1 us (1.042)
  blocking collectives: 8.81 us -> 0 us
  waiting for transfers between devices: 3.29 us -> 8.08 us
  starting transfers between devices: 18.5 us -> 22.3 us
  local copies, waits for them, and re-layouts: 0 us -> 1.56 us
  Pallas kernels: 21.1 us -> 22 us
    all_to_all x1 -> x0, blocking collectives: 8.81 us -> none  [exchange(): return lax.all_to_all(block, 'rows', 0, 0, axis_index_groups=[group])]
    all_to_all x0 -> x1, waiting for transfers between devices: none -> 4.85 us  [exchange(): return lax.all_to_all(block, 'rows', 0, 0, axis_index_groups=[group])]
    all_to_all x0 -> x1, starting transfers between devices: none -> 3.73 us  [exchange(): return lax.all_to_all(block, 'rows', 0, 0, axis_index_groups=[group])]
    unnamed x0 -> x4, local copies, waits for them, and re-layouts: none -> 1.56 us
    pallas_call x11 -> x12, Pallas kernels: 21.1 us -> 22 us  [call(): pl.pallas_call(kernel, out_shape=out, in_specs=ins, out_specs=jax.tree.ma...]
  transfers between devices with their start and end apart: 10 -> 11, of which waited for: 5 -> 6; matrix products, arithmetic and copies ran while one was open for 0% -> 0% of each run, Pallas kernels for 20% -> 20%
where the time goes in v22:
time: 55.1 us; the launch traced here: 54.6 us
  starting transfers between devices  22.3 us (40%)
  Pallas kernels  22 us (40%)
  waiting for transfers between devices  8.08 us (15%)
  local copies, waits for them, and re-layouts  1.56 us (3%)
  between operations  0.73 us (1%)
    pallas_call x12, Pallas kernels, call(): pl.pallas_call(kernel, out_shape=out, in_specs=ins, out_specs=jax.tree.ma...  22 us
    all_to_all x2, starting transfers between devices, gather(): return lax.all_to_all(block, 'rows', 0, 0, axis_index_groups=groups)  11.9 us
    ppermute x8, starting transfers between devices, swapped(): lax.ppermute(block, 'rows', [(i, partner(i)) for i in range(lax.axis_size...  6.74 us
    all_to_all x1, waiting for transfers between devices, exchange(): return lax.all_to_all(block, 'rows', 0, 0, axis_index_groups=[group])  4.85 us
    all_to_all x1, starting transfers between devices, exchange(): return lax.all_to_all(block, 'rows', 0, 0, axis_index_groups=[group])  3.73 us
    ppermute x8, waiting for transfers between devices, swapped(): lax.ppermute(block, 'rows', [(i, partner(i)) for i in range(lax.axis_size...  2 us
    unnamed x4, local copies, waits for them, and re-layouts  1.56 us
    all_to_all x2, waiting for transfers between devices, gather(): return lax.all_to_all(block, 'rows', 0, 0, axis_index_groups=groups)  1.23 us
  transfers between devices with their start and end apart: 11, of which 6 were waited for; matrix products, arithmetic and copies ran while one was open for 0% of the time, Pallas kernels for 20%

profile of v22, /device:TPU:0, one launch (start us, length us, event | category | flops | bytes accessed | tf_op | source)
XLA Modules:
  0.0 54.6 jit_solution(16110007392908168910)
XLA Ops:
  0.6 1.8 %start.1 = (f32[256,128]{1,0:T(8,128)S(1)}, bf16[512,128]{1,0:T(8,128)(2,1)S(1)}, bf16[256,128]{1,0:T(8,128)(2,1)S(1)}, bf16[8,32,128]{2,1,0:T(8,128)(2,1)}) custom-call(f32[8,4096]{1,0:T(8,128)} %b_hbm.1, bf16[512,128]{1,0:T(8,128)(2,1)} %bitcast.8), custom_call_target="tpu_custom_call" | custom-call | tf_op jit(solution)/shard_map/start/pallas_call | solution.py:487
  2.5 7.9 %all-to-all-start = ((bf16[8,32,128]{2,1,0:T(8,128)(2,1)}), bf16[8,32,128]{2,1,0:T(8,128)(2,1)S(1)}, u32[]{:S(2)}, u32[]{:S(2)}) async-start(bf16[8,32,128]{2,1,0:T(8,128)(2,1)} %get-tuple-element.28), calls=%async_computation | async-start | bytes 131072 | tf_op jit(solution)/shard_map/all_to_all | solution.py:498
  10.3 3.3 %collective-permute-start.2 = (bf16[256,128]{1,0:T(8,128)(2,1)S(1)}, bf16[256,128]{1,0:T(8,128)(2,1)S(1)}, u32[]{:S(2)}, u32[]{:S(2)}) collective-permute-start(bf16[256,128]{1,0:T(8,128)(2,1)S(1)} %get-tuple-element.25.own), channel_id=1, source_target_pairs={{0,14},{1,15},{2,4},{3,5},{4,2},{5,3},{6,8},{7,9},{8,6},{9,7},{10,... | collective-permute-start | bytes 196616 | tf_op jit(solution)/shard_map/ppermute | solution.py:444
  13.6 1.6 %ahead.1 = (s32[24,32]{1,0:T(8,128)S(1)}, bf16[32,2,128,128]{3,2,1,0:T(8,128)(2,1)S(1)}, f32[8,128]{1,0:T(8,128)S(1)}) custom-call(s32[8,32]{1,0:T(8,128)} %bitcast.9, s32[1,32]{1,0:T(1,128)} %bitcast.11, s32[8,32]{1,0:T(8,128)} %bitcast.10, bf16[32,8,128,128]{3,2,1,0:T(8,128)(2,1)} %blocks_hbm.7, bf16[256,128]{1,0:T(8,128)(2,1)S(1)} %collective-permute-done._.mate), custom_call_target="tpu_custom_call" | custom-call | tf_op jit(solution)/shard_map/ahead/pallas_call | solution.py:487
  15.2 0.5 all-to-all-done.refs_0_.got
  15.8 2.9 %fetch.2 = (bf16[32,6,128,128]{3,2,1,0:T(8,128)(2,1)S(1)}, f32[8,128]{1,0:T(8,128)S(1)}) custom-call(bf16[32,8,128,128]{3,2,1,0:T(8,128)(2,1)} %blocks_hbm.7, bf16[8,32,128]{2,1,0:T(8,128)(2,1)S(1)} %all-to-all-done.refs_0_.got, f32[8,128]{1,0:T(8,128)S(1)} %get-tuple-element.29.refs_1_), custom_call_target="tpu_custom_call" | custom-call | tf_op jit(solution)/shard_map/fetch/pallas_call | solution.py:487
  18.7 0.2 collective-permute-done.1.even
  18.9 0.1 collective-permute-start.3
  19.1 1.6 %prepare.1 = (bf16[128,512]{1,0:T(8,128)(2,1)S(1)}, bf16[128,512]{1,0:T(8,128)(2,1)S(1)}, bf16[512,128]{1,0:T(8,128)(2,1)S(1)}) custom-call(f32[8,16,16,32]{3,2,1,0:T(8,128)} %bitcast.6, bf16[512,128]{1,0:T(8,128)(2,1)} %bitcast.7, bf16[512,128]{1,0:T(8,128)(2,1)S(1)} %relay.2._.sent), custom_call_target="tpu_custom_call" | custom-call | tf_op jit(solution)/shard_map/prepare/pallas_call | solution.py:487
  20.7 4.2 %operator_one.1 = (f32[256,128]{1,0:T(8,128)S(1)}, bf16[256,128]{1,0:T(8,128)(2,1)S(1)}, bf16[8,48,128]{2,1,0:T(8,128)(2,1)}) custom-call(bf16[256,128]{1,0:T(8,128)(2,1)S(1)} %get-tuple-element.25.own, bf16[256,128]{1,0:T(8,128)(2,1)S(1)} %collective-permute-done._.mate, bf16[256,128]{1,0:T(8,128)(2,1)S(1)} %collective-permute-done.1.even, ...), custom_call_target="tpu_custom_call" | custom-call | tf_op jit(solution)/shard_map/operator_one/pallas_call | solution.py:487
  24.9 4.0 %all-to-all-start.1 = ((bf16[8,48,128]{2,1,0:T(8,128)(2,1)}), bf16[8,48,128]{2,1,0:T(8,128)(2,1)S(1)}, u32[]{:S(2)}, u32[]{:S(2)}) async-start(bf16[8,48,128]{2,1,0:T(8,128)(2,1)} %get-tuple-element.37), calls=%async_computation.1 | async-start | bytes 196608 | tf_op jit(solution)/shard_map/all_to_all | solution.py:498
  28.9 3.3 %collective-permute-start.5 = (bf16[256,128]{1,0:T(8,128)(2,1)S(1)}, bf16[256,128]{1,0:T(8,128)(2,1)S(1)}, u32[]{:S(2)}, u32[]{:S(2)}) collective-permute-start(bf16[256,128]{1,0:T(8,128)(2,1)S(1)} %get-tuple-element.38.own), channel_id=1, source_target_pairs={{0,14},{1,15},{2,4},{3,5},{4,2},{5,3},{6,8},{7,9},{8,6},{9,7},{10,... | collective-permute-start | bytes 196616 | tf_op jit(solution)/shard_map/ppermute | solution.py:444
  32.2 1.7 %own.1.refs_1_.started = f32[256,128]{1,0:T(8,128)S(1)} custom-call(bf16[32,8,128,128]{3,2,1,0:T(8,128)(2,1)} %blocks_hbm.7, bf16[256,128]{1,0:T(8,128)(2,1)S(1)} %get-tuple-element.38.own, bf16[256,128]{1,0:T(8,128)(2,1)S(1)} %collective-permute-done.6._.mate), custom_call_target="tpu_custom_call" | custom-call | tf_op jit(solution)/shard_map/own/pallas_call | solution.py:487
  33.9 0.7 %all-to-all-done.1.refs_0_.got = bf16[8,48,128]{2,1,0:T(8,128)(2,1)S(1)} async-done(((bf16[8,48,128]{2,1,0:T(8,128)(2,1)}), bf16[8,48,128]{2,1,0:T(8,128)(2,1)S(1)}, u32[]{:S(2)}, u32[]{:S(2)}) %all-to-all-start.1) | async-done | bytes 98336 | tf_op jit(solution)/shard_map/all_to_all | solution.py:498
  34.6 2.5 %fetch.3 = (bf16[32,5,128,128]{3,2,1,0:T(8,128)(2,1)S(1)}, f32[8,128]{1,0:T(8,128)S(1)}) custom-call(bf16[32,8,128,128]{3,2,1,0:T(8,128)(2,1)} %blocks_hbm.7, bf16[8,48,128]{2,1,0:T(8,128)(2,1)S(1)} %all-to-all-done.1.refs_0_.got, f32[256,128]{1,0:T(8,128)S(1)} %own.1.refs_1_.started), custom_call_target="tpu_custom_call" | custom-call | tf_op jit(solution)/shard_map/fetch/pallas_call | solution.py:487
  37.2 0.4 collective-permute-done.4.even
  37.7 1.4 %collective-permute-done.7.received = bf16[640,128]{1,0:T(8,128)(2,1)S(1)} collective-permute-done((bf16[640,128]{1,0:T(8,128)(2,1)S(1)}, bf16[640,128]{1,0:T(8,128)(2,1)S(1)}, u32[]{:S(2)}, u32[]{:S(2)}) %collective-permute-start.7) | collective-permute-done | bytes 163872 | tf_op jit(solution)/shard_map/ppermute | solution.py:444
  39.0 3.8 %operator_two.1 = (f32[256,128]{1,0:T(8,128)S(1)}, bf16[16,8,128]{2,1,0:T(8,128)(2,1)}) custom-call(bf16[256,128]{1,0:T(8,128)(2,1)S(1)} %get-tuple-element.38.own, bf16[256,128]{1,0:T(8,128)(2,1)S(1)} %collective-permute-done.6._.mate, bf16[256,128]{1,0:T(8,128)(2,1)S(1)} %collective-permute-done.4.even, bf16[256,128]{1,0:T(8,128)(2,1)S(1)} %collective-permute-done.5.odd, ...), custom_call_target="tpu_custom_call" | custom-call | tf_op jit(solution)/shard_map/operator_two/pallas_call | solution.py:487
  42.8 0.7 %copy-done = f32[256,128]{1,0:T(8,128)} copy-done((f32[256,128]{1,0:T(8,128)}, f32[256,128]{1,0:T(8,128)S(1)}, u32[]{:S(2)}) %copy-start) | copy-done | bytes 131096
  43.5 3.7 %all-to-all-start.2 = ((bf16[16,8,128]{2,1,0:T(8,128)(2,1)}), bf16[16,8,128]{2,1,0:T(8,128)(2,1)S(1)}, u32[]{:S(2)}, u32[]{:S(2)}) async-start(bf16[16,8,128]{2,1,0:T(8,128)(2,1)} %get-tuple-element.41._), calls=%async_computation.2 | async-start | bytes 65536 | tf_op jit(solution)/shard_map/all_to_all | solution.py:502
  47.2 0.4 ready.1
  47.6 4.8 %all-to-all-done.2.got = bf16[16,8,128]{2,1,0:T(8,128)(2,1)S(1)} async-done(((bf16[16,8,128]{2,1,0:T(8,128)(2,1)}), bf16[16,8,128]{2,1,0:T(8,128)(2,1)S(1)}, u32[]{:S(2)}, u32[]{:S(2)}) %all-to-all-start.2) | async-done | bytes 32800 | tf_op jit(solution)/shard_map/all_to_all | solution.py:502
  52.5 0.9 %copy-done.1 = f32[256,128]{1,0:T(8,128)S(1)} copy-done((f32[256,128]{1,0:T(8,128)S(1)}, f32[256,128]{1,0:T(8,128)}, u32[]{:S(2)}) %copy-start.1) | copy-done | bytes 131096
  53.4 1.2 %finish.1 = (f32[8,4096]{1,0:T(8,128)}, f32[8,4096]{1,0:T(8,128)}) custom-call(f32[256,128]{1,0:T(8,128)S(1)} %get-tuple-element.42.first, f32[256,128]{1,0:T(8,128)S(1)} %get-tuple-element.43.second, f32[256,128]{1,0:T(8,128)S(1)} %copy-done.1, f32[8,128]{1,0:T(8,128)S(1)} %get-tuple-element.45.known, bf16[16,8,128]{2,1,0:T(8,128)(2,1)S(1)} %all-to-all-done.2.got), custom_call_target="tpu_custom_call" | custom-call | tf_op jit(solution)/shard_map/finish/pallas_call | solution.py:487
  (14 shorter events, 0.2 us)
Async XLA Ops:
  2.5 13.3 %all-to-all-start = ((bf16[8,32,128]{2,1,0:T(8,128)(2,1)}), bf16[8,32,128]{2,1,0:T(8,128)(2,1)S(1)}, u32[]{:S(2)}, u32[]{:S(2)}) async-start(bf16[8,32,128]{2,1,0:T(8,128)(2,1)} %get-tuple-element.28), calls=%async_computation | async-start | bytes 131072 | tf_op jit(solution)/shard_map/all_to_all | solution.py:498
  10.3 3.3 %collective-permute-start = (bf16[256,128]{1,0:T(8,128)(2,1)S(1)}, bf16[256,128]{1,0:T(8,128)(2,1)S(1)}, u32[]{:S(2)}, u32[]{:S(2)}) collective-permute-start(bf16[256,128]{1,0:T(8,128)(2,1)S(1)} %get-tuple-element.25.own), channel_id=1, source_target_pairs={{0,1},{1,0},{2,3},{3,2},{4,5},{5,4},{6,7},{7,6},{8,9},{9,8},{10,11... | collective-permute-start | bytes 196616 | tf_op jit(solution)/shard_map/ppermute | solution.py:444
  10.3 8.4 %collective-permute-start.2 = (bf16[256,128]{1,0:T(8,128)(2,1)S(1)}, bf16[256,128]{1,0:T(8,128)(2,1)S(1)}, u32[]{:S(2)}, u32[]{:S(2)}) collective-permute-start(bf16[256,128]{1,0:T(8,128)(2,1)S(1)} %get-tuple-element.25.own), channel_id=1, source_target_pairs={{0,14},{1,15},{2,4},{3,5},{4,2},{5,3},{6,8},{7,9},{8,6},{9,7},{10,... | collective-permute-start | bytes 196616 | tf_op jit(solution)/shard_map/ppermute | solution.py:444
  13.6 5.3 %collective-permute-start.1 = (bf16[256,128]{1,0:T(8,128)(2,1)S(1)}, bf16[256,128]{1,0:T(8,128)(2,1)S(1)}, u32[]{:S(2)}, u32[]{:S(2)}) collective-permute-start(bf16[256,128]{1,0:T(8,128)(2,1)S(1)} %get-tuple-element.25.own), channel_id=1, source_target_pairs={{0,2},{1,3},{2,0},{3,1},{4,6},{5,7},{6,4},{7,5},{8,10},{9,11},{10,... | collective-permute-start | bytes 196616 | tf_op jit(solution)/shard_map/ppermute | solution.py:444
  18.9 1.7 %collective-permute-start.3 = (bf16[512,128]{1,0:T(8,128)(2,1)S(1)}, bf16[512,128]{1,0:T(8,128)(2,1)S(1)}, u32[]{:S(2)}, u32[]{:S(2)}) collective-permute-start(bf16[512,128]{1,0:T(8,128)(2,1)S(1)} %relay.2._.sent), channel_id=1, source_target_pairs={{0,1},{1,0},{2,3},{3,2},{4,5},{5,4},{6,7},{7,6},{8,9},{9,8},{10,11... | collective-permute-start | bytes 393224 | tf_op jit(solution)/shard_map/ppermute | solution.py:444
  24.9 9.7 %all-to-all-start.1 = ((bf16[8,48,128]{2,1,0:T(8,128)(2,1)}), bf16[8,48,128]{2,1,0:T(8,128)(2,1)S(1)}, u32[]{:S(2)}, u32[]{:S(2)}) async-start(bf16[8,48,128]{2,1,0:T(8,128)(2,1)} %get-tuple-element.37), calls=%async_computation.1 | async-start | bytes 196608 | tf_op jit(solution)/shard_map/all_to_all | solution.py:498
  28.9 3.3 %collective-permute-start.6 = (bf16[256,128]{1,0:T(8,128)(2,1)S(1)}, bf16[256,128]{1,0:T(8,128)(2,1)S(1)}, u32[]{:S(2)}, u32[]{:S(2)}) collective-permute-start(bf16[256,128]{1,0:T(8,128)(2,1)S(1)} %get-tuple-element.38.own), channel_id=1, source_target_pairs={{0,1},{1,0},{2,3},{3,2},{4,5},{5,4},{6,7},{7,6},{8,9},{9,8},{10,11... | collective-permute-start | bytes 196616 | tf_op jit(solution)/shard_map/ppermute | solution.py:444
  28.9 8.2 %collective-permute-start.5 = (bf16[256,128]{1,0:T(8,128)(2,1)S(1)}, bf16[256,128]{1,0:T(8,128)(2,1)S(1)}, u32[]{:S(2)}, u32[]{:S(2)}) collective-permute-start(bf16[256,128]{1,0:T(8,128)(2,1)S(1)} %get-tuple-element.38.own), channel_id=1, source_target_pairs={{0,14},{1,15},{2,4},{3,5},{4,2},{5,3},{6,8},{7,9},{8,6},{9,7},{10,... | collective-permute-start | bytes 196616 | tf_op jit(solution)/shard_map/ppermute | solution.py:444
  32.2 5.4 %collective-permute-start.4 = (bf16[256,128]{1,0:T(8,128)(2,1)S(1)}, bf16[256,128]{1,0:T(8,128)(2,1)S(1)}, u32[]{:S(2)}, u32[]{:S(2)}) collective-permute-start(bf16[256,128]{1,0:T(8,128)(2,1)S(1)} %get-tuple-element.38.own), channel_id=1, source_target_pairs={{0,2},{1,3},{2,0},{3,1},{4,6},{5,7},{6,4},{7,5},{8,10},{9,11},{10,... | collective-permute-start | bytes 196616 | tf_op jit(solution)/shard_map/ppermute | solution.py:444
  37.6 1.5 %collective-permute-start.7 = (bf16[640,128]{1,0:T(8,128)(2,1)S(1)}, bf16[640,128]{1,0:T(8,128)(2,1)S(1)}, u32[]{:S(2)}, u32[]{:S(2)}) collective-permute-start(bf16[640,128]{1,0:T(8,128)(2,1)S(1)} %relay.3.sent), channel_id=1, source_target_pairs={{0,1},{1,0},{2,3},{3,2},{4,5},{5,4},{6,7},{7,6},{8,9},{9,8},{10,11... | collective-permute-start | bytes 491528 | tf_op jit(solution)/shard_map/ppermute | solution.py:444
  42.8 0.7 %copy-start = (f32[256,128]{1,0:T(8,128)}, f32[256,128]{1,0:T(8,128)S(1)}, u32[]{:S(2)}) copy-start(f32[256,128]{1,0:T(8,128)S(1)} %get-tuple-element.44.candidate) | copy-start | bytes 393220
  43.5 9.0 %all-to-all-start.2 = ((bf16[16,8,128]{2,1,0:T(8,128)(2,1)}), bf16[16,8,128]{2,1,0:T(8,128)(2,1)S(1)}, u32[]{:S(2)}, u32[]{:S(2)}) async-start(bf16[16,8,128]{2,1,0:T(8,128)(2,1)} %get-tuple-element.41._), calls=%async_computation.2 | async-start | bytes 65536 | tf_op jit(solution)/shard_map/all_to_all | solution.py:502
  52.5 0.9 %copy-start.1 = (f32[256,128]{1,0:T(8,128)S(1)}, f32[256,128]{1,0:T(8,128)}, u32[]{:S(2)}) copy-start(f32[256,128]{1,0:T(8,128)} %copy-done) | copy-start | bytes 393220

commit v23 on v21

--- a/solution.py
+++ b/solution.py
@@ -122,16 +122,18 @@
     axis, size, middle, near_cols_hbm, near_counts_hbm, far_cols_hbm, coupling_hbm, target_hbm, _,
     places, high_out, low_out, target_out, near_cols, near_counts, far_cols, coupling, target, sems,
 ):
+    slots, rank, _, clusters = coupling.shape
+    per_tile = LANES // clusters
+    parts = [pl.ds(p, per_tile) for p in range(0, rank, per_tile)]
     pairs = (
         (near_cols_hbm, near_cols), (near_counts_hbm, near_counts), (far_cols_hbm, far_cols),
-        (coupling_hbm, coupling), (target_hbm, target),
+        (target_hbm, target), *((coupling_hbm.at[:, part], coupling.at[:, part]) for part in parts),
     )
     copies = [pltpu.make_async_copy(source, to, sems.at[n]) for n, (source, to) in enumerate(pairs)]
     for copy in copies:
         copy.start()
     for copy in copies[:3]:
         copy.wait()
-    slots, clusters = near_cols.shape
     me = lax.axis_index(axis)
     every = clusters * size
     distance = near_cols[...] - me * clusters + 2 * clusters
@@ -143,18 +145,20 @@
     other_core = (owner ^ me) & 1
     chips = size // 2
     chip = lax.rem(owner // 2 + (chips - middle), chips)
-    rank = coupling.shape[1]
     per_group = LANES // rank
     inside = lax.rem(far_cols[...], clusters)
     tile = (other_core * chips + chip) * (clusters // per_group) + lax.div(inside, per_group)
     places[slots : 2 * slots, :] = tile * R
     slot = lax.broadcasted_iota(jnp.int32, (slots, clusters), 0)
     places[2 * slots :, :] = ((slot - inside) * rank) & (LANES - 1)
-    for copy in copies[3:5]:
+    size = rank * clusters
+    row = lax.broadcasted_iota(jnp.int32, (size, 1), 0)
+    column = lax.broadcasted_iota(jnp.int32, (size, size), 1)
+    wanted = lax.rem(row, clusters) * rank + lax.div(row, clusters)
+    copies[3].wait()
+    target_out[...] = dot((column == wanted).astype(bf16), target[...]).astype(bf16)
+    for s, copy in enumerate(copies[4:]):
         copy.wait()
-    slots, rank, _, clusters = coupling.shape
-    per_tile = LANES // clusters
-    for s in range(rank // per_tile):
         pieces = [
             coupling[:, s * per_tile + p].reshape(slots * rank, clusters) for p in range(per_tile)
         ]
@@ -162,11 +166,6 @@
         high = tile.astype(bf16)
         high_out[:, s * LANES : (s + 1) * LANES] = high
         low_out[:, s * LANES : (s + 1) * LANES] = (tile - high.astype(f32)).astype(bf16)
-    size = rank * clusters
-    row = lax.broadcasted_iota(jnp.int32, (size, 1), 0)
-    column = lax.broadcasted_iota(jnp.int32, (size, size), 1)
-    wanted = lax.rem(row, clusters) * rank + lax.div(row, clusters)
-    target_out[...] = dot((column == wanted).astype(bf16), target[...]).astype(bf16)
 
 
 def fetch_kernel(slots, blocks_hbm, *refs):
@@ -360,13 +359,19 @@
 
 def second_kernel(
     per_group, unknowns, own, mate, even, odd, places, ahead, blocks, sent, received, high, low, target, b, image,
-    started, candidate, sums_out, near, far, window, table,
+    started, candidate, sums_out, known, near, far, window, table,
 ):
     clusters = near.shape[0] // R
     head = clusters // per_group * R
     slabs, swaps = (own, mate, even, odd), (sent, received)
     means = read_sums(tails(swaps, own.shape[0], head), 3, unknowns)
-    start_norm, h11, h21, _, _, _ = arnoldi_one(*means)
+    values = arnoldi_one(*means)
+    start_norm, h11, h21, _, _, _ = values
+    lane = lane_ids()
+    tile = jnp.zeros((R, LANES), f32)
+    for n, value in enumerate(values):
+        tile = jnp.where(lane == n, value, tile)
+    known[...] = tile
     scale = 1.0 / start_norm
     inverse = 1.0 / h21
     sums = [jnp.zeros((R, LANES), f32) for _ in range(3)]
@@ -388,10 +393,9 @@
         sums_out[device] = tile
 
 
-def finish_kernel(per_group, unknowns, b, image, candidate, sent, received, got, solution_out, next_out):
+def finish_kernel(unknowns, b, image, candidate, known, got, solution_out, next_out):
     clusters = b.shape[0] // R
-    sums = read_sums(tails((sent, received), b.shape[0], clusters // per_group * R), 3, unknowns)
-    start_norm, h11, h21, v11, v22, v12 = arnoldi_one(*sums)
+    start_norm, h11, h21, v11, v22, v12 = [known[:, n : n + 1] for n in range(6)]
     h12, h22, ww = read_sums([got[device] for device in range(got.shape[0])], 3, unknowns)
     uu = ww - 2.0 * (h12 * h12 + h22 * h22) + h12 * h12 * v11 + h22 * h22 * v22 + 2.0 * h12 * h22 * v12
     h32 = jnp.sqrt(jnp.maximum(uu, 0.0) + epsilon)
@@ -461,7 +465,7 @@
         )(*args)
 
     chips = size // 2
-    middle = chips // 4
+    middle = chips // 4 + 1
     order = [(middle + n) % chips for n in range(chips)]
 
     def gather(block):
@@ -522,7 +526,7 @@
             scratch(slots, clusters, dtype=jnp.int32), scratch(1, clusters, dtype=jnp.int32),
             scratch(slots, clusters, dtype=jnp.int32),
             scratch(slots, rank, rank, clusters), scratch(clusters * rank, LANES, dtype=bf16),
-            pltpu.SemaphoreType.DMA((5,)),
+            pltpu.SemaphoreType.DMA((4 + rank * clusters // LANES,)),
         ],
     )
     places, *made = prepared
@@ -543,14 +547,14 @@
         scratch_shapes=[scratch(clusters, 1, LANES, LANES, dtype=bf16), pltpu.SemaphoreType.DMA((4,))],
     )
     here = arrived(got, held, [late], started)
-    candidate, sums = call(
+    candidate, sums, known = call(
         functools.partial(second_kernel, per_group, unknowns), "operator_two",
-        (shape(rows, LANES), shape(size, R, LANES, dtype=bf16)),
+        (shape(rows, LANES), shape(size, R, LANES, dtype=bf16), shape(R, LANES)),
         operands + [VMEM], *held, places, *here, *made, field, image, started, scratch_shapes=kept,
     )
     return call(
-        functools.partial(finish_kernel, per_group, unknowns), "finish", (shape(R, width), shape(R, width)),
-        [VMEM] * 6, field, image, candidate, *here[2:], exchange(sums),
+        functools.partial(finish_kernel, unknowns), "finish", (shape(R, width), shape(R, width)),
+        [VMEM] * 5, field, image, candidate, known, exchange(sums),
     )
 
 

time: 52.9 us -> 52.3 us (0.989)
  starting transfers between devices: 18.5 us -> 17.7 us
    ppermute x8, starting transfers between devices: 6.74 us -> 5.07 us  [swapped(): lax.ppermute(block, 'rows', [(i, partner(i)) for i in range(lax.axis_size...]
    all_to_all x2, starting transfers between devices: 11.8 us -> 12.6 us  [gather(): return lax.all_to_all(block, 'rows', 0, 0, axis_index_groups=groups)]
where the time goes in v23:
time: 52.3 us; the launch traced here: 51.9 us
  Pallas kernels  21 us (40%)
  starting transfers between devices  17.7 us (34%)
  blocking collectives  8.76 us (17%)
  waiting for transfers between devices  3.66 us (7%)
  between operations  0.75 us (1%)
    pallas_call x11, Pallas kernels, call(): pl.pallas_call(kernel, out_shape=out, in_specs=ins, out_specs=jax.tree.ma...  21 us
    all_to_all x2, starting transfers between devices, gather(): return lax.all_to_all(block, 'rows', 0, 0, axis_index_groups=groups)  12.6 us
    all_to_all x1, blocking collectives, exchange(): return lax.all_to_all(block, 'rows', 0, 0, axis_index_groups=[group])  8.76 us
    ppermute x8, starting transfers between devices, swapped(): lax.ppermute(block, 'rows', [(i, partner(i)) for i in range(lax.axis_size...  5.07 us
    ppermute x8, waiting for transfers between devices, swapped(): lax.ppermute(block, 'rows', [(i, partner(i)) for i in range(lax.axis_size...  2.03 us
    all_to_all x2, waiting for transfers between devices, gather(): return lax.all_to_all(block, 'rows', 0, 0, axis_index_groups=groups)  1.64 us
  transfers between devices with their start and end apart: 10, of which 5 were waited for; matrix products, arithmetic and copies ran while one was open for 0% of the time, Pallas kernels for 20%

profile of v23, /device:TPU:0, one launch (start us, length us, event | category | flops | bytes accessed | tf_op | source)
XLA Modules:
  0.0 51.9 jit_solution(11752857368649875776)
XLA Ops:
  0.6 1.8 %start.1 = (f32[256,128]{1,0:T(8,128)S(1)}, bf16[512,128]{1,0:T(8,128)(2,1)S(1)}, bf16[256,128]{1,0:T(8,128)(2,1)S(1)}, bf16[8,32,128]{2,1,0:T(8,128)(2,1)}) custom-call(f32[8,4096]{1,0:T(8,128)} %b_hbm.1, bf16[512,128]{1,0:T(8,128)(2,1)} %bitcast.8), custom_call_target="tpu_custom_call" | custom-call | tf_op jit(solution)/shard_map/start/pallas_call | solution.py:462
  2.5 7.9 %all-to-all-start = ((bf16[8,32,128]{2,1,0:T(8,128)(2,1)}), bf16[8,32,128]{2,1,0:T(8,128)(2,1)S(1)}, u32[]{:S(2)}, u32[]{:S(2)}) async-start(bf16[8,32,128]{2,1,0:T(8,128)(2,1)} %get-tuple-element.24), calls=%async_computation | async-start | bytes 131072 | tf_op jit(solution)/shard_map/all_to_all | solution.py:473
  10.3 2.4 %collective-permute-start.2 = (bf16[256,128]{1,0:T(8,128)(2,1)S(1)}, bf16[256,128]{1,0:T(8,128)(2,1)S(1)}, u32[]{:S(2)}, u32[]{:S(2)}) collective-permute-start(bf16[256,128]{1,0:T(8,128)(2,1)S(1)} %get-tuple-element.23.own), channel_id=1, source_target_pairs={{0,14},{1,15},{2,4},{3,5},{4,2},{5,3},{6,8},{7,9},{8,6},{9,7},{10,... | collective-permute-start | bytes 196616 | tf_op jit(solution)/shard_map/ppermute | solution.py:419
  12.7 0.0 collective-permute-start.1
  12.7 0.0 collective-permute-done.refs_0_.mate
  12.7 1.6 %ahead.1 = (bf16[32,2,128,128]{3,2,1,0:T(8,128)(2,1)S(1)}, f32[8,128]{1,0:T(8,128)S(1)}) custom-call(bf16[32,8,128,128]{3,2,1,0:T(8,128)(2,1)} %blocks_hbm.7, bf16[256,128]{1,0:T(8,128)(2,1)S(1)} %collective-permute-done.refs_0_.mate), custom_call_target="tpu_custom_call" | custom-call | tf_op jit(solution)/shard_map/ahead/pallas_call | solution.py:462
  14.3 0.9 %all-to-all-done.refs_0_.got = bf16[8,32,128]{2,1,0:T(8,128)(2,1)S(1)} async-done(((bf16[8,32,128]{2,1,0:T(8,128)(2,1)}), bf16[8,32,128]{2,1,0:T(8,128)(2,1)S(1)}, u32[]{:S(2)}, u32[]{:S(2)}) %all-to-all-start) | async-done | bytes 65568 | tf_op jit(solution)/shard_map/all_to_all | solution.py:473
  15.1 2.9 %fetch.2 = (bf16[32,6,128,128]{3,2,1,0:T(8,128)(2,1)S(1)}, f32[8,128]{1,0:T(8,128)S(1)}) custom-call(bf16[32,8,128,128]{3,2,1,0:T(8,128)(2,1)} %blocks_hbm.7, bf16[8,32,128]{2,1,0:T(8,128)(2,1)S(1)} %all-to-all-done.refs_0_.got, f32[8,128]{1,0:T(8,128)S(1)} %get-tuple-element.25.refs_1_), custom_call_target="tpu_custom_call" | custom-call | tf_op jit(solution)/shard_map/fetch/pallas_call | solution.py:462
  18.1 0.3 collective-permute-done.1.even
  18.3 0.1 collective-permute-start.3
  18.4 1.8 %prepare.1 = (s32[24,32]{1,0:T(8,128)S(1)}, bf16[128,512]{1,0:T(8,128)(2,1)S(1)}, bf16[128,512]{1,0:T(8,128)(2,1)S(1)}, bf16[512,128]{1,0:T(8,128)(2,1)S(1)}) custom-call(s32[8,32]{1,0:T(8,128)} %bitcast.9, s32[1,32]{1,0:T(1,128)} %bitcast.11, s32[8,32]{1,0:T(8,128)} %bitcast.10, f32[8,16,16,32]{3,2,1,0:T(8,128)} %bitcast.6, bf16[512,128]{1,0:T(8,128)(2,1)} %bitcast.7, ...), custom_call_target="tpu_custom_call" | custom-call | tf_op jit(solution)/shard_map/prepare/pallas_call | solution.py:462
  20.3 4.2 %operator_one.1 = (f32[256,128]{1,0:T(8,128)S(1)}, bf16[256,128]{1,0:T(8,128)(2,1)S(1)}, bf16[8,48,128]{2,1,0:T(8,128)(2,1)}) custom-call(bf16[256,128]{1,0:T(8,128)(2,1)S(1)} %get-tuple-element.23.own, bf16[256,128]{1,0:T(8,128)(2,1)S(1)} %collective-permute-done.refs_0_.mate, bf16[256,128]{1,0:T(8,128)(2,1)S(1)} %collective-permute-done.1.even, ...), custom_call_target="tpu_custom_call" | custom-call | tf_op jit(solution)/shard_map/operator_one/pallas_call | solution.py:462
  24.5 4.7 %all-to-all-start.1 = ((bf16[8,48,128]{2,1,0:T(8,128)(2,1)}), bf16[8,48,128]{2,1,0:T(8,128)(2,1)S(1)}, u32[]{:S(2)}, u32[]{:S(2)}) async-start(bf16[8,48,128]{2,1,0:T(8,128)(2,1)} %get-tuple-element.36), calls=%async_computation.1 | async-start | bytes 196608 | tf_op jit(solution)/shard_map/all_to_all | solution.py:473
  29.2 0.2 collective-permute-start.4
  29.4 2.4 %collective-permute-start.6 = (bf16[256,128]{1,0:T(8,128)(2,1)S(1)}, bf16[256,128]{1,0:T(8,128)(2,1)S(1)}, u32[]{:S(2)}, u32[]{:S(2)}) collective-permute-start(bf16[256,128]{1,0:T(8,128)(2,1)S(1)} %get-tuple-element.35.own), channel_id=1, source_target_pairs={{0,14},{1,15},{2,4},{3,5},{4,2},{5,3},{6,8},{7,9},{8,6},{9,7},{10,... | collective-permute-start | bytes 196616 | tf_op jit(solution)/shard_map/ppermute | solution.py:419
  31.8 1.7 %own.1.refs_1_.started = f32[256,128]{1,0:T(8,128)S(1)} custom-call(bf16[32,8,128,128]{3,2,1,0:T(8,128)(2,1)} %blocks_hbm.7, bf16[256,128]{1,0:T(8,128)(2,1)S(1)} %get-tuple-element.35.own, bf16[256,128]{1,0:T(8,128)(2,1)S(1)} %collective-permute-done.4._.mate), custom_call_target="tpu_custom_call" | custom-call | tf_op jit(solution)/shard_map/own/pallas_call | solution.py:462
  33.5 0.8 %all-to-all-done.1.refs_0_.got = bf16[8,48,128]{2,1,0:T(8,128)(2,1)S(1)} async-done(((bf16[8,48,128]{2,1,0:T(8,128)(2,1)}), bf16[8,48,128]{2,1,0:T(8,128)(2,1)S(1)}, u32[]{:S(2)}, u32[]{:S(2)}) %all-to-all-start.1) | async-done | bytes 98336 | tf_op jit(solution)/shard_map/all_to_all | solution.py:473
  34.3 2.5 %fetch.3 = (bf16[32,5,128,128]{3,2,1,0:T(8,128)(2,1)S(1)}, f32[8,128]{1,0:T(8,128)S(1)}) custom-call(bf16[32,8,128,128]{3,2,1,0:T(8,128)(2,1)} %blocks_hbm.7, bf16[8,48,128]{2,1,0:T(8,128)(2,1)S(1)} %all-to-all-done.1.refs_0_.got, f32[256,128]{1,0:T(8,128)S(1)} %own.1.refs_1_.started), custom_call_target="tpu_custom_call" | custom-call | tf_op jit(solution)/shard_map/fetch/pallas_call | solution.py:462
  36.8 0.4 collective-permute-done.5.even
  37.2 0.1 collective-permute-start.7
  37.3 1.4 %collective-permute-done.7.received = bf16[640,128]{1,0:T(8,128)(2,1)S(1)} collective-permute-done((bf16[640,128]{1,0:T(8,128)(2,1)S(1)}, bf16[640,128]{1,0:T(8,128)(2,1)S(1)}, u32[]{:S(2)}, u32[]{:S(2)}) %collective-permute-start.7) | collective-permute-done | bytes 163872 | tf_op jit(solution)/shard_map/ppermute | solution.py:419
  38.7 3.2 %operator_two.1 = (f32[256,128]{1,0:T(8,128)S(1)}, bf16[16,8,128]{2,1,0:T(8,128)(2,1)S(1)}, f32[8,128]{1,0:T(8,128)S(1)}) custom-call(bf16[256,128]{1,0:T(8,128)(2,1)S(1)} %get-tuple-element.35.own, bf16[256,128]{1,0:T(8,128)(2,1)S(1)} %collective-permute-done.4._.mate, bf16[256,128]{1,0:T(8,128)(2,1)S(1)} %collective-permute-done.5.even, ...), custom_call_target="tpu_custom_call" | custom-call | tf_op jit(solution)/shard_map/operator_two/pallas_call | solution.py:462
  41.9 8.8 %all_to_all.15.got = bf16[16,8,128]{2,1,0:T(8,128)(2,1)S(1)} all-to-all(bf16[16,8,128]{2,1,0:T(8,128)(2,1)S(1)} %get-tuple-element.41), channel_id=1, replica_groups={{6,7,8,9,10,11,12,13,14,15,0,1,2,3,4,5},{22,23,24,25,26,27,28,29,30,31,..., dimensions={0} | all-to-all | bytes 65536 | tf_op jit(solution)/shard_map/all_to_all | solution.py:477
  50.6 1.2 %finish.1 = (f32[8,4096]{1,0:T(8,128)}, f32[8,4096]{1,0:T(8,128)}) custom-call(f32[256,128]{1,0:T(8,128)S(1)} %get-tuple-element.22.b, f32[256,128]{1,0:T(8,128)S(1)} %get-tuple-element.34.image, f32[256,128]{1,0:T(8,128)S(1)} %get-tuple-element.39.candidate, f32[8,128]{1,0:T(8,128)S(1)} %get-tuple-element.40.known, bf16[16,8,128]{2,1,0:T(8,128)(2,1)S(1)} %all_to_all.15.got), custom_call_target="tpu_custom_call" | custom-call | tf_op jit(solution)/shard_map/finish/pallas_call | solution.py:462
  (8 shorter events, 0.0 us)
Async XLA Ops:
  2.5 12.7 %all-to-all-start = ((bf16[8,32,128]{2,1,0:T(8,128)(2,1)}), bf16[8,32,128]{2,1,0:T(8,128)(2,1)S(1)}, u32[]{:S(2)}, u32[]{:S(2)}) async-start(bf16[8,32,128]{2,1,0:T(8,128)(2,1)} %get-tuple-element.24), calls=%async_computation | async-start | bytes 131072 | tf_op jit(solution)/shard_map/all_to_all | solution.py:473
  10.3 2.4 %collective-permute-start = (bf16[256,128]{1,0:T(8,128)(2,1)S(1)}, bf16[256,128]{1,0:T(8,128)(2,1)S(1)}, u32[]{:S(2)}, u32[]{:S(2)}) collective-permute-start(bf16[256,128]{1,0:T(8,128)(2,1)S(1)} %get-tuple-element.23.own), channel_id=1, source_target_pairs={{0,1},{1,0},{2,3},{3,2},{4,5},{5,4},{6,7},{7,6},{8,9},{9,8},{10,11... | collective-permute-start | bytes 196616 | tf_op jit(solution)/shard_map/ppermute | solution.py:419
  10.3 7.7 %collective-permute-start.2 = (bf16[256,128]{1,0:T(8,128)(2,1)S(1)}, bf16[256,128]{1,0:T(8,128)(2,1)S(1)}, u32[]{:S(2)}, u32[]{:S(2)}) collective-permute-start(bf16[256,128]{1,0:T(8,128)(2,1)S(1)} %get-tuple-element.23.own), channel_id=1, source_target_pairs={{0,14},{1,15},{2,4},{3,5},{4,2},{5,3},{6,8},{7,9},{8,6},{9,7},{10,... | collective-permute-start | bytes 196616 | tf_op jit(solution)/shard_map/ppermute | solution.py:419
  12.7 5.6 %collective-permute-start.1 = (bf16[256,128]{1,0:T(8,128)(2,1)S(1)}, bf16[256,128]{1,0:T(8,128)(2,1)S(1)}, u32[]{:S(2)}, u32[]{:S(2)}) collective-permute-start(bf16[256,128]{1,0:T(8,128)(2,1)S(1)} %get-tuple-element.23.own), channel_id=1, source_target_pairs={{0,2},{1,3},{2,0},{3,1},{4,6},{5,7},{6,4},{7,5},{8,10},{9,11},{10,... | collective-permute-start | bytes 196616 | tf_op jit(solution)/shard_map/ppermute | solution.py:419
  18.3 1.9 %collective-permute-start.3 = (bf16[512,128]{1,0:T(8,128)(2,1)S(1)}, bf16[512,128]{1,0:T(8,128)(2,1)S(1)}, u32[]{:S(2)}, u32[]{:S(2)}) collective-permute-start(bf16[512,128]{1,0:T(8,128)(2,1)S(1)} %relay.2._.sent), channel_id=1, source_target_pairs={{0,1},{1,0},{2,3},{3,2},{4,5},{5,4},{6,7},{7,6},{8,9},{9,8},{10,11... | collective-permute-start | bytes 393224 | tf_op jit(solution)/shard_map/ppermute | solution.py:419
  24.5 9.8 %all-to-all-start.1 = ((bf16[8,48,128]{2,1,0:T(8,128)(2,1)}), bf16[8,48,128]{2,1,0:T(8,128)(2,1)S(1)}, u32[]{:S(2)}, u32[]{:S(2)}) async-start(bf16[8,48,128]{2,1,0:T(8,128)(2,1)} %get-tuple-element.36), calls=%async_computation.1 | async-start | bytes 196608 | tf_op jit(solution)/shard_map/all_to_all | solution.py:473
  29.2 2.6 %collective-permute-start.4 = (bf16[256,128]{1,0:T(8,128)(2,1)S(1)}, bf16[256,128]{1,0:T(8,128)(2,1)S(1)}, u32[]{:S(2)}, u32[]{:S(2)}) collective-permute-start(bf16[256,128]{1,0:T(8,128)(2,1)S(1)} %get-tuple-element.35.own), channel_id=1, source_target_pairs={{0,1},{1,0},{2,3},{3,2},{4,5},{5,4},{6,7},{7,6},{8,9},{9,8},{10,11... | collective-permute-start | bytes 196616 | tf_op jit(solution)/shard_map/ppermute | solution.py:419
  29.4 7.4 %collective-permute-start.6 = (bf16[256,128]{1,0:T(8,128)(2,1)S(1)}, bf16[256,128]{1,0:T(8,128)(2,1)S(1)}, u32[]{:S(2)}, u32[]{:S(2)}) collective-permute-start(bf16[256,128]{1,0:T(8,128)(2,1)S(1)} %get-tuple-element.35.own), channel_id=1, source_target_pairs={{0,14},{1,15},{2,4},{3,5},{4,2},{5,3},{6,8},{7,9},{8,6},{9,7},{10,... | collective-permute-start | bytes 196616 | tf_op jit(solution)/shard_map/ppermute | solution.py:419
  31.8 5.4 %collective-permute-start.5 = (bf16[256,128]{1,0:T(8,128)(2,1)S(1)}, bf16[256,128]{1,0:T(8,128)(2,1)S(1)}, u32[]{:S(2)}, u32[]{:S(2)}) collective-permute-start(bf16[256,128]{1,0:T(8,128)(2,1)S(1)} %get-tuple-element.35.own), channel_id=1, source_target_pairs={{0,2},{1,3},{2,0},{3,1},{4,6},{5,7},{6,4},{7,5},{8,10},{9,11},{10,... | collective-permute-start | bytes 196616 | tf_op jit(solution)/shard_map/ppermute | solution.py:419
  37.2 1.5 %collective-permute-start.7 = (bf16[640,128]{1,0:T(8,128)(2,1)S(1)}, bf16[640,128]{1,0:T(8,128)(2,1)S(1)}, u32[]{:S(2)}, u32[]{:S(2)}) collective-permute-start(bf16[640,128]{1,0:T(8,128)(2,1)S(1)} %relay.3.sent), channel_id=1, source_target_pairs={{0,1},{1,0},{2,3},{3,2},{4,5},{5,4},{6,7},{7,6},{8,9},{9,8},{10,11... | collective-permute-start | bytes 491528 | tf_op jit(solution)/shard_map/ppermute | solution.py:419

commit v24 on v23

--- a/solution.py
+++ b/solution.py
@@ -122,18 +122,16 @@
     axis, size, middle, near_cols_hbm, near_counts_hbm, far_cols_hbm, coupling_hbm, target_hbm, _,
     places, high_out, low_out, target_out, near_cols, near_counts, far_cols, coupling, target, sems,
 ):
-    slots, rank, _, clusters = coupling.shape
-    per_tile = LANES // clusters
-    parts = [pl.ds(p, per_tile) for p in range(0, rank, per_tile)]
     pairs = (
         (near_cols_hbm, near_cols), (near_counts_hbm, near_counts), (far_cols_hbm, far_cols),
-        (target_hbm, target), *((coupling_hbm.at[:, part], coupling.at[:, part]) for part in parts),
+        (coupling_hbm, coupling), (target_hbm, target),
     )
     copies = [pltpu.make_async_copy(source, to, sems.at[n]) for n, (source, to) in enumerate(pairs)]
     for copy in copies:
         copy.start()
     for copy in copies[:3]:
         copy.wait()
+    slots, clusters = near_cols.shape
     me = lax.axis_index(axis)
     every = clusters * size
     distance = near_cols[...] - me * clusters + 2 * clusters
@@ -145,20 +143,18 @@
     other_core = (owner ^ me) & 1
     chips = size // 2
     chip = lax.rem(owner // 2 + (chips - middle), chips)
+    rank = coupling.shape[1]
     per_group = LANES // rank
     inside = lax.rem(far_cols[...], clusters)
     tile = (other_core * chips + chip) * (clusters // per_group) + lax.div(inside, per_group)
     places[slots : 2 * slots, :] = tile * R
     slot = lax.broadcasted_iota(jnp.int32, (slots, clusters), 0)
     places[2 * slots :, :] = ((slot - inside) * rank) & (LANES - 1)
-    size = rank * clusters
-    row = lax.broadcasted_iota(jnp.int32, (size, 1), 0)
-    column = lax.broadcasted_iota(jnp.int32, (size, size), 1)
-    wanted = lax.rem(row, clusters) * rank + lax.div(row, clusters)
-    copies[3].wait()
-    target_out[...] = dot((column == wanted).astype(bf16), target[...]).astype(bf16)
-    for s, copy in enumerate(copies[4:]):
+    for copy in copies[3:5]:
         copy.wait()
+    slots, rank, _, clusters = coupling.shape
+    per_tile = LANES // clusters
+    for s in range(rank // per_tile):
         pieces = [
             coupling[:, s * per_tile + p].reshape(slots * rank, clusters) for p in range(per_tile)
         ]
@@ -166,6 +162,11 @@
         high = tile.astype(bf16)
         high_out[:, s * LANES : (s + 1) * LANES] = high
         low_out[:, s * LANES : (s + 1) * LANES] = (tile - high.astype(f32)).astype(bf16)
+    size = rank * clusters
+    row = lax.broadcasted_iota(jnp.int32, (size, 1), 0)
+    column = lax.broadcasted_iota(jnp.int32, (size, size), 1)
+    wanted = lax.rem(row, clusters) * rank + lax.div(row, clusters)
+    target_out[...] = dot((column == wanted).astype(bf16), target[...]).astype(bf16)
 
 
 def fetch_kernel(slots, blocks_hbm, *refs):
@@ -434,7 +435,8 @@
 
 
 def sends_of(block):
-    return [block] + [swapped(block, partner) for partner in (core_mate, even_mate, odd_mate)]
+    mate, odd, even = [swapped(block, partner) for partner in (core_mate, odd_mate, even_mate)]
+    return [block, mate, even, odd]
 
 
 def on_device(
@@ -526,7 +528,7 @@
             scratch(slots, clusters, dtype=jnp.int32), scratch(1, clusters, dtype=jnp.int32),
             scratch(slots, clusters, dtype=jnp.int32),
             scratch(slots, rank, rank, clusters), scratch(clusters * rank, LANES, dtype=bf16),
-            pltpu.SemaphoreType.DMA((4 + rank * clusters // LANES,)),
+            pltpu.SemaphoreType.DMA((5,)),
         ],
     )
     places, *made = prepared

time: 52.3 us -> 52.1 us (level)
  no operation moved by 1% of the time
where the time goes in v24:
time: 52.1 us; the launch traced here: 51.7 us
  Pallas kernels  20.9 us (40%)
  starting transfers between devices  17.7 us (34%)
  blocking collectives  8.77 us (17%)
  waiting for transfers between devices  3.65 us (7%)
  between operations  0.75 us (1%)
    pallas_call x11, Pallas kernels, call(): pl.pallas_call(kernel, out_shape=out, in_specs=ins, out_specs=jax.tree.ma...  20.9 us
    all_to_all x2, starting transfers between devices, gather(): return lax.all_to_all(block, 'rows', 0, 0, axis_index_groups=groups)  12.6 us
    all_to_all x1, blocking collectives, exchange(): return lax.all_to_all(block, 'rows', 0, 0, axis_index_groups=[group])  8.77 us
    ppermute x8, starting transfers between devices, swapped(): lax.ppermute(block, 'rows', [(i, partner(i)) for i in range(lax.axis_size...  5.09 us
    ppermute x8, waiting for transfers between devices, swapped(): lax.ppermute(block, 'rows', [(i, partner(i)) for i in range(lax.axis_size...  2.01 us
    all_to_all x2, waiting for transfers between devices, gather(): return lax.all_to_all(block, 'rows', 0, 0, axis_index_groups=groups)  1.64 us
  transfers between devices with their start and end apart: 10, of which 5 were waited for; matrix products, arithmetic and copies ran while one was open for 0% of the time, Pallas kernels for 20%

profile of v24, /device:TPU:0, one launch (start us, length us, event | category | flops | bytes accessed | tf_op | source)
XLA Modules:
  0.0 51.7 jit_solution(10570927916132730329)
XLA Ops:
  0.6 1.8 %start.1 = (f32[256,128]{1,0:T(8,128)S(1)}, bf16[512,128]{1,0:T(8,128)(2,1)S(1)}, bf16[256,128]{1,0:T(8,128)(2,1)S(1)}, bf16[8,32,128]{2,1,0:T(8,128)(2,1)}) custom-call(f32[8,4096]{1,0:T(8,128)} %b_hbm.1, bf16[512,128]{1,0:T(8,128)(2,1)} %bitcast.8), custom_call_target="tpu_custom_call" | custom-call | tf_op jit(solution)/shard_map/start/pallas_call | solution.py:464
  2.5 7.9 %all-to-all-start = ((bf16[8,32,128]{2,1,0:T(8,128)(2,1)}), bf16[8,32,128]{2,1,0:T(8,128)(2,1)S(1)}, u32[]{:S(2)}, u32[]{:S(2)}) async-start(bf16[8,32,128]{2,1,0:T(8,128)(2,1)} %get-tuple-element.24), calls=%async_computation | async-start | bytes 131072 | tf_op jit(solution)/shard_map/all_to_all | solution.py:475
  10.3 2.4 %collective-permute-start.2 = (bf16[256,128]{1,0:T(8,128)(2,1)S(1)}, bf16[256,128]{1,0:T(8,128)(2,1)S(1)}, u32[]{:S(2)}, u32[]{:S(2)}) collective-permute-start(bf16[256,128]{1,0:T(8,128)(2,1)S(1)} %get-tuple-element.23.own), channel_id=1, source_target_pairs={{0,14},{1,15},{2,4},{3,5},{4,2},{5,3},{6,8},{7,9},{8,6},{9,7},{10,... | collective-permute-start | bytes 196616 | tf_op jit(solution)/shard_map/ppermute | solution.py:420
  12.7 0.0 collective-permute-start.1
  12.7 0.0 collective-permute-done.refs_0_.mate
  12.7 1.6 %ahead.1 = (bf16[32,2,128,128]{3,2,1,0:T(8,128)(2,1)S(1)}, f32[8,128]{1,0:T(8,128)S(1)}) custom-call(bf16[32,8,128,128]{3,2,1,0:T(8,128)(2,1)} %blocks_hbm.7, bf16[256,128]{1,0:T(8,128)(2,1)S(1)} %collective-permute-done.refs_0_.mate), custom_call_target="tpu_custom_call" | custom-call | tf_op jit(solution)/shard_map/ahead/pallas_call | solution.py:464
  14.3 0.9 %all-to-all-done.refs_0_.got = bf16[8,32,128]{2,1,0:T(8,128)(2,1)S(1)} async-done(((bf16[8,32,128]{2,1,0:T(8,128)(2,1)}), bf16[8,32,128]{2,1,0:T(8,128)(2,1)S(1)}, u32[]{:S(2)}, u32[]{:S(2)}) %all-to-all-start) | async-done | bytes 65568 | tf_op jit(solution)/shard_map/all_to_all | solution.py:475
  15.1 2.9 %fetch.2 = (bf16[32,6,128,128]{3,2,1,0:T(8,128)(2,1)S(1)}, f32[8,128]{1,0:T(8,128)S(1)}) custom-call(bf16[32,8,128,128]{3,2,1,0:T(8,128)(2,1)} %blocks_hbm.7, bf16[8,32,128]{2,1,0:T(8,128)(2,1)S(1)} %all-to-all-done.refs_0_.got, f32[8,128]{1,0:T(8,128)S(1)} %get-tuple-element.25.refs_1_), custom_call_target="tpu_custom_call" | custom-call | tf_op jit(solution)/shard_map/fetch/pallas_call | solution.py:464
  18.1 0.3 collective-permute-done.1.even
  18.3 0.1 collective-permute-start.3
  18.4 1.7 %prepare.1 = (s32[24,32]{1,0:T(8,128)S(1)}, bf16[128,512]{1,0:T(8,128)(2,1)S(1)}, bf16[128,512]{1,0:T(8,128)(2,1)S(1)}, bf16[512,128]{1,0:T(8,128)(2,1)S(1)}) custom-call(s32[8,32]{1,0:T(8,128)} %bitcast.9, s32[1,32]{1,0:T(1,128)} %bitcast.11, s32[8,32]{1,0:T(8,128)} %bitcast.10, f32[8,16,16,32]{3,2,1,0:T(8,128)} %bitcast.6, bf16[512,128]{1,0:T(8,128)(2,1)} %bitcast.7, ...), custom_call_target="tpu_custom_call" | custom-call | tf_op jit(solution)/shard_map/prepare/pallas_call | solution.py:464
  20.1 4.2 %operator_one.1 = (f32[256,128]{1,0:T(8,128)S(1)}, bf16[256,128]{1,0:T(8,128)(2,1)S(1)}, bf16[8,48,128]{2,1,0:T(8,128)(2,1)}) custom-call(bf16[256,128]{1,0:T(8,128)(2,1)S(1)} %get-tuple-element.23.own, bf16[256,128]{1,0:T(8,128)(2,1)S(1)} %collective-permute-done.refs_0_.mate, bf16[256,128]{1,0:T(8,128)(2,1)S(1)} %collective-permute-done.1.even, ...), custom_call_target="tpu_custom_call" | custom-call | tf_op jit(solution)/shard_map/operator_one/pallas_call | solution.py:464
  24.3 4.7 %all-to-all-start.1 = ((bf16[8,48,128]{2,1,0:T(8,128)(2,1)}), bf16[8,48,128]{2,1,0:T(8,128)(2,1)S(1)}, u32[]{:S(2)}, u32[]{:S(2)}) async-start(bf16[8,48,128]{2,1,0:T(8,128)(2,1)} %get-tuple-element.36), calls=%async_computation.1 | async-start | bytes 196608 | tf_op jit(solution)/shard_map/all_to_all | solution.py:475
  29.0 0.2 collective-permute-start.4
  29.3 2.4 %collective-permute-start.6 = (bf16[256,128]{1,0:T(8,128)(2,1)S(1)}, bf16[256,128]{1,0:T(8,128)(2,1)S(1)}, u32[]{:S(2)}, u32[]{:S(2)}) collective-permute-start(bf16[256,128]{1,0:T(8,128)(2,1)S(1)} %get-tuple-element.35.own), channel_id=1, source_target_pairs={{0,14},{1,15},{2,4},{3,5},{4,2},{5,3},{6,8},{7,9},{8,6},{9,7},{10,... | collective-permute-start | bytes 196616 | tf_op jit(solution)/shard_map/ppermute | solution.py:420
  31.6 1.7 %own.1.refs_1_.started = f32[256,128]{1,0:T(8,128)S(1)} custom-call(bf16[32,8,128,128]{3,2,1,0:T(8,128)(2,1)} %blocks_hbm.7, bf16[256,128]{1,0:T(8,128)(2,1)S(1)} %get-tuple-element.35.own, bf16[256,128]{1,0:T(8,128)(2,1)S(1)} %collective-permute-done.4._.mate), custom_call_target="tpu_custom_call" | custom-call | tf_op jit(solution)/shard_map/own/pallas_call | solution.py:464
  33.4 0.8 %all-to-all-done.1.refs_0_.got = bf16[8,48,128]{2,1,0:T(8,128)(2,1)S(1)} async-done(((bf16[8,48,128]{2,1,0:T(8,128)(2,1)}), bf16[8,48,128]{2,1,0:T(8,128)(2,1)S(1)}, u32[]{:S(2)}, u32[]{:S(2)}) %all-to-all-start.1) | async-done | bytes 98336 | tf_op jit(solution)/shard_map/all_to_all | solution.py:475
  34.1 2.5 %fetch.3 = (bf16[32,5,128,128]{3,2,1,0:T(8,128)(2,1)S(1)}, f32[8,128]{1,0:T(8,128)S(1)}) custom-call(bf16[32,8,128,128]{3,2,1,0:T(8,128)(2,1)} %blocks_hbm.7, bf16[8,48,128]{2,1,0:T(8,128)(2,1)S(1)} %all-to-all-done.1.refs_0_.got, f32[256,128]{1,0:T(8,128)S(1)} %own.1.refs_1_.started), custom_call_target="tpu_custom_call" | custom-call | tf_op jit(solution)/shard_map/fetch/pallas_call | solution.py:464
  36.7 0.4 collective-permute-done.5.even
  37.1 0.1 collective-permute-start.7
  37.1 1.4 %collective-permute-done.7.received = bf16[640,128]{1,0:T(8,128)(2,1)S(1)} collective-permute-done((bf16[640,128]{1,0:T(8,128)(2,1)S(1)}, bf16[640,128]{1,0:T(8,128)(2,1)S(1)}, u32[]{:S(2)}, u32[]{:S(2)}) %collective-permute-start.7) | collective-permute-done | bytes 163872 | tf_op jit(solution)/shard_map/ppermute | solution.py:420
  38.5 3.2 %operator_two.1 = (f32[256,128]{1,0:T(8,128)S(1)}, bf16[16,8,128]{2,1,0:T(8,128)(2,1)S(1)}, f32[8,128]{1,0:T(8,128)S(1)}) custom-call(bf16[256,128]{1,0:T(8,128)(2,1)S(1)} %get-tuple-element.35.own, bf16[256,128]{1,0:T(8,128)(2,1)S(1)} %collective-permute-done.4._.mate, bf16[256,128]{1,0:T(8,128)(2,1)S(1)} %collective-permute-done.5.even, ...), custom_call_target="tpu_custom_call" | custom-call | tf_op jit(solution)/shard_map/operator_two/pallas_call | solution.py:464
  41.7 8.8 %all_to_all.15.got = bf16[16,8,128]{2,1,0:T(8,128)(2,1)S(1)} all-to-all(bf16[16,8,128]{2,1,0:T(8,128)(2,1)S(1)} %get-tuple-element.41), channel_id=1, replica_groups={{6,7,8,9,10,11,12,13,14,15,0,1,2,3,4,5},{22,23,24,25,26,27,28,29,30,31,..., dimensions={0} | all-to-all | bytes 65536 | tf_op jit(solution)/shard_map/all_to_all | solution.py:479
  50.5 1.2 %finish.1 = (f32[8,4096]{1,0:T(8,128)}, f32[8,4096]{1,0:T(8,128)}) custom-call(f32[256,128]{1,0:T(8,128)S(1)} %get-tuple-element.22.b, f32[256,128]{1,0:T(8,128)S(1)} %get-tuple-element.34.image, f32[256,128]{1,0:T(8,128)S(1)} %get-tuple-element.39.candidate, f32[8,128]{1,0:T(8,128)S(1)} %get-tuple-element.40.known, bf16[16,8,128]{2,1,0:T(8,128)(2,1)S(1)} %all_to_all.15.got), custom_call_target="tpu_custom_call" | custom-call | tf_op jit(solution)/shard_map/finish/pallas_call | solution.py:464
  (8 shorter events, 0.0 us)
Async XLA Ops:
  2.5 12.7 %all-to-all-start = ((bf16[8,32,128]{2,1,0:T(8,128)(2,1)}), bf16[8,32,128]{2,1,0:T(8,128)(2,1)S(1)}, u32[]{:S(2)}, u32[]{:S(2)}) async-start(bf16[8,32,128]{2,1,0:T(8,128)(2,1)} %get-tuple-element.24), calls=%async_computation | async-start | bytes 131072 | tf_op jit(solution)/shard_map/all_to_all | solution.py:475
  10.3 2.4 %collective-permute-start = (bf16[256,128]{1,0:T(8,128)(2,1)S(1)}, bf16[256,128]{1,0:T(8,128)(2,1)S(1)}, u32[]{:S(2)}, u32[]{:S(2)}) collective-permute-start(bf16[256,128]{1,0:T(8,128)(2,1)S(1)} %get-tuple-element.23.own), channel_id=1, source_target_pairs={{0,1},{1,0},{2,3},{3,2},{4,5},{5,4},{6,7},{7,6},{8,9},{9,8},{10,11... | collective-permute-start | bytes 196616 | tf_op jit(solution)/shard_map/ppermute | solution.py:420
  10.3 7.7 %collective-permute-start.2 = (bf16[256,128]{1,0:T(8,128)(2,1)S(1)}, bf16[256,128]{1,0:T(8,128)(2,1)S(1)}, u32[]{:S(2)}, u32[]{:S(2)}) collective-permute-start(bf16[256,128]{1,0:T(8,128)(2,1)S(1)} %get-tuple-element.23.own), channel_id=1, source_target_pairs={{0,14},{1,15},{2,4},{3,5},{4,2},{5,3},{6,8},{7,9},{8,6},{9,7},{10,... | collective-permute-start | bytes 196616 | tf_op jit(solution)/shard_map/ppermute | solution.py:420
  12.7 5.6 %collective-permute-start.1 = (bf16[256,128]{1,0:T(8,128)(2,1)S(1)}, bf16[256,128]{1,0:T(8,128)(2,1)S(1)}, u32[]{:S(2)}, u32[]{:S(2)}) collective-permute-start(bf16[256,128]{1,0:T(8,128)(2,1)S(1)} %get-tuple-element.23.own), channel_id=1, source_target_pairs={{0,2},{1,3},{2,0},{3,1},{4,6},{5,7},{6,4},{7,5},{8,10},{9,11},{10,... | collective-permute-start | bytes 196616 | tf_op jit(solution)/shard_map/ppermute | solution.py:420
  18.3 1.7 %collective-permute-start.3 = (bf16[512,128]{1,0:T(8,128)(2,1)S(1)}, bf16[512,128]{1,0:T(8,128)(2,1)S(1)}, u32[]{:S(2)}, u32[]{:S(2)}) collective-permute-start(bf16[512,128]{1,0:T(8,128)(2,1)S(1)} %relay.2._.sent), channel_id=1, source_target_pairs={{0,1},{1,0},{2,3},{3,2},{4,5},{5,4},{6,7},{7,6},{8,9},{9,8},{10,11... | collective-permute-start | bytes 393224 | tf_op jit(solution)/shard_map/ppermute | solution.py:420
  24.3 9.8 %all-to-all-start.1 = ((bf16[8,48,128]{2,1,0:T(8,128)(2,1)}), bf16[8,48,128]{2,1,0:T(8,128)(2,1)S(1)}, u32[]{:S(2)}, u32[]{:S(2)}) async-start(bf16[8,48,128]{2,1,0:T(8,128)(2,1)} %get-tuple-element.36), calls=%async_computation.1 | async-start | bytes 196608 | tf_op jit(solution)/shard_map/all_to_all | solution.py:475
  29.0 2.6 %collective-permute-start.4 = (bf16[256,128]{1,0:T(8,128)(2,1)S(1)}, bf16[256,128]{1,0:T(8,128)(2,1)S(1)}, u32[]{:S(2)}, u32[]{:S(2)}) collective-permute-start(bf16[256,128]{1,0:T(8,128)(2,1)S(1)} %get-tuple-element.35.own), channel_id=1, source_target_pairs={{0,1},{1,0},{2,3},{3,2},{4,5},{5,4},{6,7},{7,6},{8,9},{9,8},{10,11... | collective-permute-start | bytes 196616 | tf_op jit(solution)/shard_map/ppermute | solution.py:420
  29.3 7.4 %collective-permute-start.6 = (bf16[256,128]{1,0:T(8,128)(2,1)S(1)}, bf16[256,128]{1,0:T(8,128)(2,1)S(1)}, u32[]{:S(2)}, u32[]{:S(2)}) collective-permute-start(bf16[256,128]{1,0:T(8,128)(2,1)S(1)} %get-tuple-element.35.own), channel_id=1, source_target_pairs={{0,14},{1,15},{2,4},{3,5},{4,2},{5,3},{6,8},{7,9},{8,6},{9,7},{10,... | collective-permute-start | bytes 196616 | tf_op jit(solution)/shard_map/ppermute | solution.py:420
  31.6 5.4 %collective-permute-start.5 = (bf16[256,128]{1,0:T(8,128)(2,1)S(1)}, bf16[256,128]{1,0:T(8,128)(2,1)S(1)}, u32[]{:S(2)}, u32[]{:S(2)}) collective-permute-start(bf16[256,128]{1,0:T(8,128)(2,1)S(1)} %get-tuple-element.35.own), channel_id=1, source_target_pairs={{0,2},{1,3},{2,0},{3,1},{4,6},{5,7},{6,4},{7,5},{8,10},{9,11},{10,... | collective-permute-start | bytes 196616 | tf_op jit(solution)/shard_map/ppermute | solution.py:420
  37.1 1.5 %collective-permute-start.7 = (bf16[640,128]{1,0:T(8,128)(2,1)S(1)}, bf16[640,128]{1,0:T(8,128)(2,1)S(1)}, u32[]{:S(2)}, u32[]{:S(2)}) collective-permute-start(bf16[640,128]{1,0:T(8,128)(2,1)S(1)} %relay.3.sent), channel_id=1, source_target_pairs={{0,1},{1,0},{2,3},{3,2},{4,5},{5,4},{6,7},{7,6},{8,9},{9,8},{10,11... | collective-permute-start | bytes 491528 | tf_op jit(solution)/shard_map/ppermute | solution.py:420

commit v25 on v24

--- a/solution.py
+++ b/solution.py
@@ -201,12 +201,14 @@
     ]
     for copy in copies:
         copy.start()
+    products = []
     for c, copy in enumerate(copies):
         copy.wait()
         for i in range(c * each, (c + 1) * each, 2):
-            both = dot(own[pl.ds(i * R, 2 * R), :], jnp.concatenate([blocks[i, 0], blocks[i + 1, 0]], axis=0), (1, 1))
-            near[pl.ds(i * R, R), :] = both[:R, :LANES]
-            near[pl.ds((i + 1) * R, R), :] = both[R:, LANES:]
+            weights = jnp.concatenate([blocks[i, 0], blocks[i + 1, 0]], axis=0)
+            products.append(dot(own[pl.ds(i * R, 2 * R), :], weights, (1, 1)))
+    for n, both in enumerate(products):
+        near[pl.ds(2 * n * R, 2 * R), :] = jnp.concatenate([both[:R, :LANES], both[R:, LANES:]], axis=0)
 
 
 def relay_kernel(axis, got, even, odd, _, out):
@@ -546,7 +548,7 @@
     held = sends_of(lowered)
     started = call(
         own_kernel, "own", shape(rows, LANES), [HBM, VMEM, ANY], blocks, lowered, held[1],
-        scratch_shapes=[scratch(clusters, 1, LANES, LANES, dtype=bf16), pltpu.SemaphoreType.DMA((4,))],
+        scratch_shapes=[scratch(clusters, 1, LANES, LANES, dtype=bf16), pltpu.SemaphoreType.DMA((8,))],
     )
     here = arrived(got, held, [late], started)
     candidate, sums, known = call(

time: 52.1 us -> 52.6 us (level)
  transfers between devices with their start and end apart: 10 -> 10, of which waited for: 5 -> 5; matrix products, arithmetic and copies ran while one was open for 0% -> 0% of each run, Pallas kernels for 20% -> 21%
where the time goes in v25:
time: 52.6 us; the launch traced here: 52.2 us
  Pallas kernels  21.3 us (40%)
  starting transfers between devices  17.7 us (34%)
  blocking collectives  9.22 us (18%)
  waiting for transfers between devices  3.2 us (6%)
  between operations  0.75 us (1%)
    pallas_call x11, Pallas kernels, call(): pl.pallas_call(kernel, out_shape=out, in_specs=ins, out_specs=jax.tree.ma...  21.3 us
    all_to_all x2, starting transfers between devices, gather(): return lax.all_to_all(block, 'rows', 0, 0, axis_index_groups=groups)  12.6 us
    all_to_all x1, blocking collectives, exchange(): return lax.all_to_all(block, 'rows', 0, 0, axis_index_groups=[group])  9.22 us
    ppermute x8, starting transfers between devices, swapped(): lax.ppermute(block, 'rows', [(i, partner(i)) for i in range(lax.axis_size...  5.08 us
    ppermute x8, waiting for transfers between devices, swapped(): lax.ppermute(block, 'rows', [(i, partner(i)) for i in range(lax.axis_size...  2.02 us
    all_to_all x2, waiting for transfers between devices, gather(): return lax.all_to_all(block, 'rows', 0, 0, axis_index_groups=groups)  1.18 us
  transfers between devices with their start and end apart: 10, of which 5 were waited for; matrix products, arithmetic and copies ran while one was open for 0% of the time, Pallas kernels for 21%

profile of v25, /device:TPU:0, one launch (start us, length us, event | category | flops | bytes accessed | tf_op | source)
XLA Modules:
  0.0 52.2 jit_solution(9376416585430058289)
XLA Ops:
  0.6 1.8 %start.1 = (f32[256,128]{1,0:T(8,128)S(1)}, bf16[512,128]{1,0:T(8,128)(2,1)S(1)}, bf16[256,128]{1,0:T(8,128)(2,1)S(1)}, bf16[8,32,128]{2,1,0:T(8,128)(2,1)}) custom-call(f32[8,4096]{1,0:T(8,128)} %b_hbm.1, bf16[512,128]{1,0:T(8,128)(2,1)} %bitcast.8), custom_call_target="tpu_custom_call" | custom-call | tf_op jit(solution)/shard_map/start/pallas_call | solution.py:466
  2.5 7.9 %all-to-all-start = ((bf16[8,32,128]{2,1,0:T(8,128)(2,1)}), bf16[8,32,128]{2,1,0:T(8,128)(2,1)S(1)}, u32[]{:S(2)}, u32[]{:S(2)}) async-start(bf16[8,32,128]{2,1,0:T(8,128)(2,1)} %get-tuple-element.24), calls=%async_computation | async-start | bytes 131072 | tf_op jit(solution)/shard_map/all_to_all | solution.py:477
  10.3 2.4 %collective-permute-start.2 = (bf16[256,128]{1,0:T(8,128)(2,1)S(1)}, bf16[256,128]{1,0:T(8,128)(2,1)S(1)}, u32[]{:S(2)}, u32[]{:S(2)}) collective-permute-start(bf16[256,128]{1,0:T(8,128)(2,1)S(1)} %get-tuple-element.23.own), channel_id=1, source_target_pairs={{0,14},{1,15},{2,4},{3,5},{4,2},{5,3},{6,8},{7,9},{8,6},{9,7},{10,... | collective-permute-start | bytes 196616 | tf_op jit(solution)/shard_map/ppermute | solution.py:422
  12.7 0.0 collective-permute-start.1
  12.7 0.0 collective-permute-done.refs_0_.mate
  12.7 1.6 %ahead.1 = (bf16[32,2,128,128]{3,2,1,0:T(8,128)(2,1)S(1)}, f32[8,128]{1,0:T(8,128)S(1)}) custom-call(bf16[32,8,128,128]{3,2,1,0:T(8,128)(2,1)} %blocks_hbm.7, bf16[256,128]{1,0:T(8,128)(2,1)S(1)} %collective-permute-done.refs_0_.mate), custom_call_target="tpu_custom_call" | custom-call | tf_op jit(solution)/shard_map/ahead/pallas_call | solution.py:466
  14.3 0.9 %all-to-all-done.refs_0_.got = bf16[8,32,128]{2,1,0:T(8,128)(2,1)S(1)} async-done(((bf16[8,32,128]{2,1,0:T(8,128)(2,1)}), bf16[8,32,128]{2,1,0:T(8,128)(2,1)S(1)}, u32[]{:S(2)}, u32[]{:S(2)}) %all-to-all-start) | async-done | bytes 65568 | tf_op jit(solution)/shard_map/all_to_all | solution.py:477
  15.1 2.9 %fetch.2 = (bf16[32,6,128,128]{3,2,1,0:T(8,128)(2,1)S(1)}, f32[8,128]{1,0:T(8,128)S(1)}) custom-call(bf16[32,8,128,128]{3,2,1,0:T(8,128)(2,1)} %blocks_hbm.7, bf16[8,32,128]{2,1,0:T(8,128)(2,1)S(1)} %all-to-all-done.refs_0_.got, f32[8,128]{1,0:T(8,128)S(1)} %get-tuple-element.25.refs_1_), custom_call_target="tpu_custom_call" | custom-call | tf_op jit(solution)/shard_map/fetch/pallas_call | solution.py:466
  18.1 0.3 collective-permute-done.1.even
  18.3 0.1 collective-permute-start.3
  18.4 1.7 %prepare.1 = (s32[24,32]{1,0:T(8,128)S(1)}, bf16[128,512]{1,0:T(8,128)(2,1)S(1)}, bf16[128,512]{1,0:T(8,128)(2,1)S(1)}, bf16[512,128]{1,0:T(8,128)(2,1)S(1)}) custom-call(s32[8,32]{1,0:T(8,128)} %bitcast.9, s32[1,32]{1,0:T(1,128)} %bitcast.11, s32[8,32]{1,0:T(8,128)} %bitcast.10, f32[8,16,16,32]{3,2,1,0:T(8,128)} %bitcast.6, bf16[512,128]{1,0:T(8,128)(2,1)} %bitcast.7, ...), custom_call_target="tpu_custom_call" | custom-call | tf_op jit(solution)/shard_map/prepare/pallas_call | solution.py:466
  20.1 4.2 %operator_one.1 = (f32[256,128]{1,0:T(8,128)S(1)}, bf16[256,128]{1,0:T(8,128)(2,1)S(1)}, bf16[8,48,128]{2,1,0:T(8,128)(2,1)}) custom-call(bf16[256,128]{1,0:T(8,128)(2,1)S(1)} %get-tuple-element.23.own, bf16[256,128]{1,0:T(8,128)(2,1)S(1)} %collective-permute-done.refs_0_.mate, bf16[256,128]{1,0:T(8,128)(2,1)S(1)} %collective-permute-done.1.even, ...), custom_call_target="tpu_custom_call" | custom-call | tf_op jit(solution)/shard_map/operator_one/pallas_call | solution.py:466
  24.3 4.7 %all-to-all-start.1 = ((bf16[8,48,128]{2,1,0:T(8,128)(2,1)}), bf16[8,48,128]{2,1,0:T(8,128)(2,1)S(1)}, u32[]{:S(2)}, u32[]{:S(2)}) async-start(bf16[8,48,128]{2,1,0:T(8,128)(2,1)} %get-tuple-element.36), calls=%async_computation.1 | async-start | bytes 196608 | tf_op jit(solution)/shard_map/all_to_all | solution.py:477
  29.0 0.2 collective-permute-start.4
  29.3 2.4 %collective-permute-start.6 = (bf16[256,128]{1,0:T(8,128)(2,1)S(1)}, bf16[256,128]{1,0:T(8,128)(2,1)S(1)}, u32[]{:S(2)}, u32[]{:S(2)}) collective-permute-start(bf16[256,128]{1,0:T(8,128)(2,1)S(1)} %get-tuple-element.35.own), channel_id=1, source_target_pairs={{0,14},{1,15},{2,4},{3,5},{4,2},{5,3},{6,8},{7,9},{8,6},{9,7},{10,... | collective-permute-start | bytes 196616 | tf_op jit(solution)/shard_map/ppermute | solution.py:422
  31.6 2.2 %own.1.refs_1_.started = f32[256,128]{1,0:T(8,128)S(1)} custom-call(bf16[32,8,128,128]{3,2,1,0:T(8,128)(2,1)} %blocks_hbm.7, bf16[256,128]{1,0:T(8,128)(2,1)S(1)} %get-tuple-element.35.own, bf16[256,128]{1,0:T(8,128)(2,1)S(1)} %collective-permute-done.4._.mate), custom_call_target="tpu_custom_call" | custom-call | tf_op jit(solution)/shard_map/own/pallas_call | solution.py:466
  33.8 0.3 all-to-all-done.1.refs_0_.got
  34.1 2.5 %fetch.3 = (bf16[32,5,128,128]{3,2,1,0:T(8,128)(2,1)S(1)}, f32[8,128]{1,0:T(8,128)S(1)}) custom-call(bf16[32,8,128,128]{3,2,1,0:T(8,128)(2,1)} %blocks_hbm.7, bf16[8,48,128]{2,1,0:T(8,128)(2,1)S(1)} %all-to-all-done.1.refs_0_.got, f32[256,128]{1,0:T(8,128)S(1)} %own.1.refs_1_.started), custom_call_target="tpu_custom_call" | custom-call | tf_op jit(solution)/shard_map/fetch/pallas_call | solution.py:466
  36.7 0.4 collective-permute-done.5.even
  37.1 0.1 collective-permute-start.7
  37.1 1.4 %collective-permute-done.7.received = bf16[640,128]{1,0:T(8,128)(2,1)S(1)} collective-permute-done((bf16[640,128]{1,0:T(8,128)(2,1)S(1)}, bf16[640,128]{1,0:T(8,128)(2,1)S(1)}, u32[]{:S(2)}, u32[]{:S(2)}) %collective-permute-start.7) | collective-permute-done | bytes 163872 | tf_op jit(solution)/shard_map/ppermute | solution.py:422
  38.5 3.2 %operator_two.1 = (f32[256,128]{1,0:T(8,128)S(1)}, bf16[16,8,128]{2,1,0:T(8,128)(2,1)S(1)}, f32[8,128]{1,0:T(8,128)S(1)}) custom-call(bf16[256,128]{1,0:T(8,128)(2,1)S(1)} %get-tuple-element.35.own, bf16[256,128]{1,0:T(8,128)(2,1)S(1)} %collective-permute-done.4._.mate, bf16[256,128]{1,0:T(8,128)(2,1)S(1)} %collective-permute-done.5.even, ...), custom_call_target="tpu_custom_call" | custom-call | tf_op jit(solution)/shard_map/operator_two/pallas_call | solution.py:466
  41.7 9.2 %all_to_all.15.got = bf16[16,8,128]{2,1,0:T(8,128)(2,1)S(1)} all-to-all(bf16[16,8,128]{2,1,0:T(8,128)(2,1)S(1)} %get-tuple-element.41), channel_id=1, replica_groups={{6,7,8,9,10,11,12,13,14,15,0,1,2,3,4,5},{22,23,24,25,26,27,28,29,30,31,..., dimensions={0} | all-to-all | bytes 65536 | tf_op jit(solution)/shard_map/all_to_all | solution.py:481
  50.9 1.2 %finish.1 = (f32[8,4096]{1,0:T(8,128)}, f32[8,4096]{1,0:T(8,128)}) custom-call(f32[256,128]{1,0:T(8,128)S(1)} %get-tuple-element.22.b, f32[256,128]{1,0:T(8,128)S(1)} %get-tuple-element.34.image, f32[256,128]{1,0:T(8,128)S(1)} %get-tuple-element.39.candidate, f32[8,128]{1,0:T(8,128)S(1)} %get-tuple-element.40.known, bf16[16,8,128]{2,1,0:T(8,128)(2,1)S(1)} %all_to_all.15.got), custom_call_target="tpu_custom_call" | custom-call | tf_op jit(solution)/shard_map/finish/pallas_call | solution.py:466
  (8 shorter events, 0.0 us)
Async XLA Ops:
  2.5 12.7 %all-to-all-start = ((bf16[8,32,128]{2,1,0:T(8,128)(2,1)}), bf16[8,32,128]{2,1,0:T(8,128)(2,1)S(1)}, u32[]{:S(2)}, u32[]{:S(2)}) async-start(bf16[8,32,128]{2,1,0:T(8,128)(2,1)} %get-tuple-element.24), calls=%async_computation | async-start | bytes 131072 | tf_op jit(solution)/shard_map/all_to_all | solution.py:477
  10.3 2.4 %collective-permute-start = (bf16[256,128]{1,0:T(8,128)(2,1)S(1)}, bf16[256,128]{1,0:T(8,128)(2,1)S(1)}, u32[]{:S(2)}, u32[]{:S(2)}) collective-permute-start(bf16[256,128]{1,0:T(8,128)(2,1)S(1)} %get-tuple-element.23.own), channel_id=1, source_target_pairs={{0,1},{1,0},{2,3},{3,2},{4,5},{5,4},{6,7},{7,6},{8,9},{9,8},{10,11... | collective-permute-start | bytes 196616 | tf_op jit(solution)/shard_map/ppermute | solution.py:422
  10.3 7.7 %collective-permute-start.2 = (bf16[256,128]{1,0:T(8,128)(2,1)S(1)}, bf16[256,128]{1,0:T(8,128)(2,1)S(1)}, u32[]{:S(2)}, u32[]{:S(2)}) collective-permute-start(bf16[256,128]{1,0:T(8,128)(2,1)S(1)} %get-tuple-element.23.own), channel_id=1, source_target_pairs={{0,14},{1,15},{2,4},{3,5},{4,2},{5,3},{6,8},{7,9},{8,6},{9,7},{10,... | collective-permute-start | bytes 196616 | tf_op jit(solution)/shard_map/ppermute | solution.py:422
  12.7 5.6 %collective-permute-start.1 = (bf16[256,128]{1,0:T(8,128)(2,1)S(1)}, bf16[256,128]{1,0:T(8,128)(2,1)S(1)}, u32[]{:S(2)}, u32[]{:S(2)}) collective-permute-start(bf16[256,128]{1,0:T(8,128)(2,1)S(1)} %get-tuple-element.23.own), channel_id=1, source_target_pairs={{0,2},{1,3},{2,0},{3,1},{4,6},{5,7},{6,4},{7,5},{8,10},{9,11},{10,... | collective-permute-start | bytes 196616 | tf_op jit(solution)/shard_map/ppermute | solution.py:422
  18.3 1.7 %collective-permute-start.3 = (bf16[512,128]{1,0:T(8,128)(2,1)S(1)}, bf16[512,128]{1,0:T(8,128)(2,1)S(1)}, u32[]{:S(2)}, u32[]{:S(2)}) collective-permute-start(bf16[512,128]{1,0:T(8,128)(2,1)S(1)} %relay.2._.sent), channel_id=1, source_target_pairs={{0,1},{1,0},{2,3},{3,2},{4,5},{5,4},{6,7},{7,6},{8,9},{9,8},{10,11... | collective-permute-start | bytes 393224 | tf_op jit(solution)/shard_map/ppermute | solution.py:422
  24.3 9.8 %all-to-all-start.1 = ((bf16[8,48,128]{2,1,0:T(8,128)(2,1)}), bf16[8,48,128]{2,1,0:T(8,128)(2,1)S(1)}, u32[]{:S(2)}, u32[]{:S(2)}) async-start(bf16[8,48,128]{2,1,0:T(8,128)(2,1)} %get-tuple-element.36), calls=%async_computation.1 | async-start | bytes 196608 | tf_op jit(solution)/shard_map/all_to_all | solution.py:477
  29.0 2.6 %collective-permute-start.4 = (bf16[256,128]{1,0:T(8,128)(2,1)S(1)}, bf16[256,128]{1,0:T(8,128)(2,1)S(1)}, u32[]{:S(2)}, u32[]{:S(2)}) collective-permute-start(bf16[256,128]{1,0:T(8,128)(2,1)S(1)} %get-tuple-element.35.own), channel_id=1, source_target_pairs={{0,1},{1,0},{2,3},{3,2},{4,5},{5,4},{6,7},{7,6},{8,9},{9,8},{10,11... | collective-permute-start | bytes 196616 | tf_op jit(solution)/shard_map/ppermute | solution.py:422
  29.3 7.4 %collective-permute-start.6 = (bf16[256,128]{1,0:T(8,128)(2,1)S(1)}, bf16[256,128]{1,0:T(8,128)(2,1)S(1)}, u32[]{:S(2)}, u32[]{:S(2)}) collective-permute-start(bf16[256,128]{1,0:T(8,128)(2,1)S(1)} %get-tuple-element.35.own), channel_id=1, source_target_pairs={{0,14},{1,15},{2,4},{3,5},{4,2},{5,3},{6,8},{7,9},{8,6},{9,7},{10,... | collective-permute-start | bytes 196616 | tf_op jit(solution)/shard_map/ppermute | solution.py:422
  31.6 5.4 %collective-permute-start.5 = (bf16[256,128]{1,0:T(8,128)(2,1)S(1)}, bf16[256,128]{1,0:T(8,128)(2,1)S(1)}, u32[]{:S(2)}, u32[]{:S(2)}) collective-permute-start(bf16[256,128]{1,0:T(8,128)(2,1)S(1)} %get-tuple-element.35.own), channel_id=1, source_target_pairs={{0,2},{1,3},{2,0},{3,1},{4,6},{5,7},{6,4},{7,5},{8,10},{9,11},{10,... | collective-permute-start | bytes 196616 | tf_op jit(solution)/shard_map/ppermute | solution.py:422
  37.1 1.5 %collective-permute-start.7 = (bf16[640,128]{1,0:T(8,128)(2,1)S(1)}, bf16[640,128]{1,0:T(8,128)(2,1)S(1)}, u32[]{:S(2)}, u32[]{:S(2)}) collective-permute-start(bf16[640,128]{1,0:T(8,128)(2,1)S(1)} %relay.3.sent), channel_id=1, source_target_pairs={{0,1},{1,0},{2,3},{3,2},{4,5},{5,4},{6,7},{7,6},{8,9},{9,8},{10,11... | collective-permute-start | bytes 491528 | tf_op jit(solution)/shard_map/ppermute | solution.py:422

commit v26 on v25

--- a/solution.py
+++ b/solution.py
@@ -506,7 +506,7 @@
         return pltpu.with_memory_space_constraint(here, pltpu.VMEM), token
 
     def arrived(got, held, ranges, behind):
-        rest, token = fetch("fetch", ranges, 4, got, behind)
+        rest, token = fetch("fetch", ranges, 1, got, behind)
         sent = call(
             functools.partial(relay_kernel, "rows"), "relay",
             shape(got.shape[0] * got.shape[1] + rows, LANES, dtype=bf16), [VMEM] * 3 + [ANY], got, *held[2:], token
@@ -514,7 +514,7 @@
         return ahead, rest, sent, swapped(sent, core_mate)
 
     late = (1 + early, slots - 1 - early)
-    ahead, token = fetch("ahead", [(1, early)], 2, held[1])
+    ahead, token = fetch("ahead", [(1, early)], 1, held[1])
     here = arrived(got, held, [(0, 1), late], token)
     prepared = call(
         functools.partial(prepare_kernel, "rows", size, middle), "prepare",
@@ -548,7 +548,7 @@
     held = sends_of(lowered)
     started = call(
         own_kernel, "own", shape(rows, LANES), [HBM, VMEM, ANY], blocks, lowered, held[1],
-        scratch_shapes=[scratch(clusters, 1, LANES, LANES, dtype=bf16), pltpu.SemaphoreType.DMA((8,))],
+        scratch_shapes=[scratch(clusters, 1, LANES, LANES, dtype=bf16), pltpu.SemaphoreType.DMA((1,))],
     )
     here = arrived(got, held, [late], started)
     candidate, sums, known = call(

time: 52.6 us -> 52 us (0.989)
  waiting for transfers between devices: 3.2 us -> 3.83 us
  blocking collectives: 9.22 us -> 8.61 us
  Pallas kernels: 21.3 us -> 20.7 us
    pallas_call x11, Pallas kernels: 21.3 us -> 20.7 us  [call(): pl.pallas_call(kernel, out_shape=out, in_specs=ins, out_specs=jax.tree.ma...]
    all_to_all x1, blocking collectives: 9.22 us -> 8.61 us  [exchange(): return lax.all_to_all(block, 'rows', 0, 0, axis_index_groups=[group])]
  transfers between devices with their start and end apart: 10 -> 10, of which waited for: 5 -> 5; matrix products, arithmetic and copies ran while one was open for 0% -> 0% of each run, Pallas kernels for 21% -> 20%
where the time goes in v26:
time: 52 us; the launch traced here: 51.5 us
  Pallas kernels  20.7 us (40%)
  starting transfers between devices  17.6 us (34%)
  blocking collectives  8.61 us (17%)
  waiting for transfers between devices  3.83 us (7%)
  between operations  0.75 us (1%)
    pallas_call x11, Pallas kernels, call(): pl.pallas_call(kernel, out_shape=out, in_specs=ins, out_specs=jax.tree.ma...  20.7 us
    all_to_all x2, starting transfers between devices, gather(): return lax.all_to_all(block, 'rows', 0, 0, axis_index_groups=groups)  12.5 us
    all_to_all x1, blocking collectives, exchange(): return lax.all_to_all(block, 'rows', 0, 0, axis_index_groups=[group])  8.61 us
    ppermute x8, starting transfers between devices, swapped(): lax.ppermute(block, 'rows', [(i, partner(i)) for i in range(lax.axis_size...  5.07 us
    ppermute x8, waiting for transfers between devices, swapped(): lax.ppermute(block, 'rows', [(i, partner(i)) for i in range(lax.axis_size...  2.13 us
    all_to_all x2, waiting for transfers between devices, gather(): return lax.all_to_all(block, 'rows', 0, 0, axis_index_groups=groups)  1.71 us
  transfers between devices with their start and end apart: 10, of which 5 were waited for; matrix products, arithmetic and copies ran while one was open for 0% of the time, Pallas kernels for 20%

profile of v26, /device:TPU:0, one launch (start us, length us, event | category | flops | bytes accessed | tf_op | source)
XLA Modules:
  0.0 51.5 jit_solution(3628169867359984042)
XLA Ops:
  0.6 1.8 %start.1 = (f32[256,128]{1,0:T(8,128)S(1)}, bf16[512,128]{1,0:T(8,128)(2,1)S(1)}, bf16[256,128]{1,0:T(8,128)(2,1)S(1)}, bf16[8,32,128]{2,1,0:T(8,128)(2,1)}) custom-call(f32[8,4096]{1,0:T(8,128)} %b_hbm.1, bf16[512,128]{1,0:T(8,128)(2,1)} %bitcast.8), custom_call_target="tpu_custom_call" | custom-call | tf_op jit(solution)/shard_map/start/pallas_call | solution.py:466
  2.5 7.9 %all-to-all-start = ((bf16[8,32,128]{2,1,0:T(8,128)(2,1)}), bf16[8,32,128]{2,1,0:T(8,128)(2,1)S(1)}, u32[]{:S(2)}, u32[]{:S(2)}) async-start(bf16[8,32,128]{2,1,0:T(8,128)(2,1)} %get-tuple-element.24), calls=%async_computation | async-start | bytes 131072 | tf_op jit(solution)/shard_map/all_to_all | solution.py:477
  10.3 2.4 %collective-permute-start.2 = (bf16[256,128]{1,0:T(8,128)(2,1)S(1)}, bf16[256,128]{1,0:T(8,128)(2,1)S(1)}, u32[]{:S(2)}, u32[]{:S(2)}) collective-permute-start(bf16[256,128]{1,0:T(8,128)(2,1)S(1)} %get-tuple-element.23.own), channel_id=1, source_target_pairs={{0,14},{1,15},{2,4},{3,5},{4,2},{5,3},{6,8},{7,9},{8,6},{9,7},{10,... | collective-permute-start | bytes 196616 | tf_op jit(solution)/shard_map/ppermute | solution.py:422
  12.7 0.0 collective-permute-start.1
  12.7 0.0 collective-permute-done.refs_0_.mate
  12.7 1.6 %ahead.1 = (bf16[32,2,128,128]{3,2,1,0:T(8,128)(2,1)S(1)}, f32[8,128]{1,0:T(8,128)S(1)}) custom-call(bf16[32,8,128,128]{3,2,1,0:T(8,128)(2,1)} %blocks_hbm.7, bf16[256,128]{1,0:T(8,128)(2,1)S(1)} %collective-permute-done.refs_0_.mate), custom_call_target="tpu_custom_call" | custom-call | tf_op jit(solution)/shard_map/ahead/pallas_call | solution.py:466
  14.3 0.8 %all-to-all-done.refs_0_.got = bf16[8,32,128]{2,1,0:T(8,128)(2,1)S(1)} async-done(((bf16[8,32,128]{2,1,0:T(8,128)(2,1)}), bf16[8,32,128]{2,1,0:T(8,128)(2,1)S(1)}, u32[]{:S(2)}, u32[]{:S(2)}) %all-to-all-start) | async-done | bytes 65568 | tf_op jit(solution)/shard_map/all_to_all | solution.py:477
  15.1 2.8 %fetch.2 = (bf16[32,6,128,128]{3,2,1,0:T(8,128)(2,1)S(1)}, f32[8,128]{1,0:T(8,128)S(1)}) custom-call(bf16[32,8,128,128]{3,2,1,0:T(8,128)(2,1)} %blocks_hbm.7, bf16[8,32,128]{2,1,0:T(8,128)(2,1)S(1)} %all-to-all-done.refs_0_.got, f32[8,128]{1,0:T(8,128)S(1)} %get-tuple-element.25.refs_1_), custom_call_target="tpu_custom_call" | custom-call | tf_op jit(solution)/shard_map/fetch/pallas_call | solution.py:466
  18.0 0.3 collective-permute-done.1.even
  18.3 0.1 collective-permute-start.3
  18.4 1.7 %prepare.1 = (s32[24,32]{1,0:T(8,128)S(1)}, bf16[128,512]{1,0:T(8,128)(2,1)S(1)}, bf16[128,512]{1,0:T(8,128)(2,1)S(1)}, bf16[512,128]{1,0:T(8,128)(2,1)S(1)}) custom-call(s32[8,32]{1,0:T(8,128)} %bitcast.9, s32[1,32]{1,0:T(1,128)} %bitcast.11, s32[8,32]{1,0:T(8,128)} %bitcast.10, f32[8,16,16,32]{3,2,1,0:T(8,128)} %bitcast.6, bf16[512,128]{1,0:T(8,128)(2,1)} %bitcast.7, ...), custom_call_target="tpu_custom_call" | custom-call | tf_op jit(solution)/shard_map/prepare/pallas_call | solution.py:466
  20.1 4.2 %operator_one.1 = (f32[256,128]{1,0:T(8,128)S(1)}, bf16[256,128]{1,0:T(8,128)(2,1)S(1)}, bf16[8,48,128]{2,1,0:T(8,128)(2,1)}) custom-call(bf16[256,128]{1,0:T(8,128)(2,1)S(1)} %get-tuple-element.23.own, bf16[256,128]{1,0:T(8,128)(2,1)S(1)} %collective-permute-done.refs_0_.mate, bf16[256,128]{1,0:T(8,128)(2,1)S(1)} %collective-permute-done.1.even, ...), custom_call_target="tpu_custom_call" | custom-call | tf_op jit(solution)/shard_map/operator_one/pallas_call | solution.py:466
  24.3 4.7 %all-to-all-start.1 = ((bf16[8,48,128]{2,1,0:T(8,128)(2,1)}), bf16[8,48,128]{2,1,0:T(8,128)(2,1)S(1)}, u32[]{:S(2)}, u32[]{:S(2)}) async-start(bf16[8,48,128]{2,1,0:T(8,128)(2,1)} %get-tuple-element.36), calls=%async_computation.1 | async-start | bytes 196608 | tf_op jit(solution)/shard_map/all_to_all | solution.py:477
  29.0 0.2 collective-permute-start.4
  29.2 2.4 %collective-permute-start.6 = (bf16[256,128]{1,0:T(8,128)(2,1)S(1)}, bf16[256,128]{1,0:T(8,128)(2,1)S(1)}, u32[]{:S(2)}, u32[]{:S(2)}) collective-permute-start(bf16[256,128]{1,0:T(8,128)(2,1)S(1)} %get-tuple-element.35.own), channel_id=1, source_target_pairs={{0,14},{1,15},{2,4},{3,5},{4,2},{5,3},{6,8},{7,9},{8,6},{9,7},{10,... | collective-permute-start | bytes 196616 | tf_op jit(solution)/shard_map/ppermute | solution.py:422
  31.6 1.6 %own.1.refs_1_.started = f32[256,128]{1,0:T(8,128)S(1)} custom-call(bf16[32,8,128,128]{3,2,1,0:T(8,128)(2,1)} %blocks_hbm.7, bf16[256,128]{1,0:T(8,128)(2,1)S(1)} %get-tuple-element.35.own, bf16[256,128]{1,0:T(8,128)(2,1)S(1)} %collective-permute-done.4._.mate), custom_call_target="tpu_custom_call" | custom-call | tf_op jit(solution)/shard_map/own/pallas_call | solution.py:466
  33.2 0.9 %all-to-all-done.1.refs_0_.got = bf16[8,48,128]{2,1,0:T(8,128)(2,1)S(1)} async-done(((bf16[8,48,128]{2,1,0:T(8,128)(2,1)}), bf16[8,48,128]{2,1,0:T(8,128)(2,1)S(1)}, u32[]{:S(2)}, u32[]{:S(2)}) %all-to-all-start.1) | async-done | bytes 98336 | tf_op jit(solution)/shard_map/all_to_all | solution.py:477
  34.1 2.5 %fetch.3 = (bf16[32,5,128,128]{3,2,1,0:T(8,128)(2,1)S(1)}, f32[8,128]{1,0:T(8,128)S(1)}) custom-call(bf16[32,8,128,128]{3,2,1,0:T(8,128)(2,1)} %blocks_hbm.7, bf16[8,48,128]{2,1,0:T(8,128)(2,1)S(1)} %all-to-all-done.1.refs_0_.got, f32[256,128]{1,0:T(8,128)S(1)} %own.1.refs_1_.started), custom_call_target="tpu_custom_call" | custom-call | tf_op jit(solution)/shard_map/fetch/pallas_call | solution.py:466
  36.6 0.4 collective-permute-done.5.even
  37.0 0.1 collective-permute-start.7
  37.1 1.4 %collective-permute-done.7.received = bf16[640,128]{1,0:T(8,128)(2,1)S(1)} collective-permute-done((bf16[640,128]{1,0:T(8,128)(2,1)S(1)}, bf16[640,128]{1,0:T(8,128)(2,1)S(1)}, u32[]{:S(2)}, u32[]{:S(2)}) %collective-permute-start.7) | collective-permute-done | bytes 163872 | tf_op jit(solution)/shard_map/ppermute | solution.py:422
  38.5 3.2 %operator_two.1 = (f32[256,128]{1,0:T(8,128)S(1)}, bf16[16,8,128]{2,1,0:T(8,128)(2,1)S(1)}, f32[8,128]{1,0:T(8,128)S(1)}) custom-call(bf16[256,128]{1,0:T(8,128)(2,1)S(1)} %get-tuple-element.35.own, bf16[256,128]{1,0:T(8,128)(2,1)S(1)} %collective-permute-done.4._.mate, bf16[256,128]{1,0:T(8,128)(2,1)S(1)} %collective-permute-done.5.even, ...), custom_call_target="tpu_custom_call" | custom-call | tf_op jit(solution)/shard_map/operator_two/pallas_call | solution.py:466
  41.6 8.6 %all_to_all.15.got = bf16[16,8,128]{2,1,0:T(8,128)(2,1)S(1)} all-to-all(bf16[16,8,128]{2,1,0:T(8,128)(2,1)S(1)} %get-tuple-element.41), channel_id=1, replica_groups={{6,7,8,9,10,11,12,13,14,15,0,1,2,3,4,5},{22,23,24,25,26,27,28,29,30,31,..., dimensions={0} | all-to-all | bytes 65536 | tf_op jit(solution)/shard_map/all_to_all | solution.py:481
  50.3 1.2 %finish.1 = (f32[8,4096]{1,0:T(8,128)}, f32[8,4096]{1,0:T(8,128)}) custom-call(f32[256,128]{1,0:T(8,128)S(1)} %get-tuple-element.22.b, f32[256,128]{1,0:T(8,128)S(1)} %get-tuple-element.34.image, f32[256,128]{1,0:T(8,128)S(1)} %get-tuple-element.39.candidate, f32[8,128]{1,0:T(8,128)S(1)} %get-tuple-element.40.known, bf16[16,8,128]{2,1,0:T(8,128)(2,1)S(1)} %all_to_all.15.got), custom_call_target="tpu_custom_call" | custom-call | tf_op jit(solution)/shard_map/finish/pallas_call | solution.py:466
  (8 shorter events, 0.0 us)
Async XLA Ops:
  2.5 12.7 %all-to-all-start = ((bf16[8,32,128]{2,1,0:T(8,128)(2,1)}), bf16[8,32,128]{2,1,0:T(8,128)(2,1)S(1)}, u32[]{:S(2)}, u32[]{:S(2)}) async-start(bf16[8,32,128]{2,1,0:T(8,128)(2,1)} %get-tuple-element.24), calls=%async_computation | async-start | bytes 131072 | tf_op jit(solution)/shard_map/all_to_all | solution.py:477
  10.3 2.4 %collective-permute-start = (bf16[256,128]{1,0:T(8,128)(2,1)S(1)}, bf16[256,128]{1,0:T(8,128)(2,1)S(1)}, u32[]{:S(2)}, u32[]{:S(2)}) collective-permute-start(bf16[256,128]{1,0:T(8,128)(2,1)S(1)} %get-tuple-element.23.own), channel_id=1, source_target_pairs={{0,1},{1,0},{2,3},{3,2},{4,5},{5,4},{6,7},{7,6},{8,9},{9,8},{10,11... | collective-permute-start | bytes 196616 | tf_op jit(solution)/shard_map/ppermute | solution.py:422
  10.3 7.7 %collective-permute-start.2 = (bf16[256,128]{1,0:T(8,128)(2,1)S(1)}, bf16[256,128]{1,0:T(8,128)(2,1)S(1)}, u32[]{:S(2)}, u32[]{:S(2)}) collective-permute-start(bf16[256,128]{1,0:T(8,128)(2,1)S(1)} %get-tuple-element.23.own), channel_id=1, source_target_pairs={{0,14},{1,15},{2,4},{3,5},{4,2},{5,3},{6,8},{7,9},{8,6},{9,7},{10,... | collective-permute-start | bytes 196616 | tf_op jit(solution)/shard_map/ppermute | solution.py:422
  12.7 5.6 %collective-permute-start.1 = (bf16[256,128]{1,0:T(8,128)(2,1)S(1)}, bf16[256,128]{1,0:T(8,128)(2,1)S(1)}, u32[]{:S(2)}, u32[]{:S(2)}) collective-permute-start(bf16[256,128]{1,0:T(8,128)(2,1)S(1)} %get-tuple-element.23.own), channel_id=1, source_target_pairs={{0,2},{1,3},{2,0},{3,1},{4,6},{5,7},{6,4},{7,5},{8,10},{9,11},{10,... | collective-permute-start | bytes 196616 | tf_op jit(solution)/shard_map/ppermute | solution.py:422
  18.3 1.7 %collective-permute-start.3 = (bf16[512,128]{1,0:T(8,128)(2,1)S(1)}, bf16[512,128]{1,0:T(8,128)(2,1)S(1)}, u32[]{:S(2)}, u32[]{:S(2)}) collective-permute-start(bf16[512,128]{1,0:T(8,128)(2,1)S(1)} %relay.2._.sent), channel_id=1, source_target_pairs={{0,1},{1,0},{2,3},{3,2},{4,5},{5,4},{6,7},{7,6},{8,9},{9,8},{10,11... | collective-permute-start | bytes 393224 | tf_op jit(solution)/shard_map/ppermute | solution.py:422
  24.3 9.7 %all-to-all-start.1 = ((bf16[8,48,128]{2,1,0:T(8,128)(2,1)}), bf16[8,48,128]{2,1,0:T(8,128)(2,1)S(1)}, u32[]{:S(2)}, u32[]{:S(2)}) async-start(bf16[8,48,128]{2,1,0:T(8,128)(2,1)} %get-tuple-element.36), calls=%async_computation.1 | async-start | bytes 196608 | tf_op jit(solution)/shard_map/all_to_all | solution.py:477
  29.0 2.6 %collective-permute-start.4 = (bf16[256,128]{1,0:T(8,128)(2,1)S(1)}, bf16[256,128]{1,0:T(8,128)(2,1)S(1)}, u32[]{:S(2)}, u32[]{:S(2)}) collective-permute-start(bf16[256,128]{1,0:T(8,128)(2,1)S(1)} %get-tuple-element.35.own), channel_id=1, source_target_pairs={{0,1},{1,0},{2,3},{3,2},{4,5},{5,4},{6,7},{7,6},{8,9},{9,8},{10,11... | collective-permute-start | bytes 196616 | tf_op jit(solution)/shard_map/ppermute | solution.py:422
  29.2 7.4 %collective-permute-start.6 = (bf16[256,128]{1,0:T(8,128)(2,1)S(1)}, bf16[256,128]{1,0:T(8,128)(2,1)S(1)}, u32[]{:S(2)}, u32[]{:S(2)}) collective-permute-start(bf16[256,128]{1,0:T(8,128)(2,1)S(1)} %get-tuple-element.35.own), channel_id=1, source_target_pairs={{0,14},{1,15},{2,4},{3,5},{4,2},{5,3},{6,8},{7,9},{8,6},{9,7},{10,... | collective-permute-start | bytes 196616 | tf_op jit(solution)/shard_map/ppermute | solution.py:422
  31.5 5.4 %collective-permute-start.5 = (bf16[256,128]{1,0:T(8,128)(2,1)S(1)}, bf16[256,128]{1,0:T(8,128)(2,1)S(1)}, u32[]{:S(2)}, u32[]{:S(2)}) collective-permute-start(bf16[256,128]{1,0:T(8,128)(2,1)S(1)} %get-tuple-element.35.own), channel_id=1, source_target_pairs={{0,2},{1,3},{2,0},{3,1},{4,6},{5,7},{6,4},{7,5},{8,10},{9,11},{10,... | collective-permute-start | bytes 196616 | tf_op jit(solution)/shard_map/ppermute | solution.py:422
  37.0 1.5 %collective-permute-start.7 = (bf16[640,128]{1,0:T(8,128)(2,1)S(1)}, bf16[640,128]{1,0:T(8,128)(2,1)S(1)}, u32[]{:S(2)}, u32[]{:S(2)}) collective-permute-start(bf16[640,128]{1,0:T(8,128)(2,1)S(1)} %relay.3.sent), channel_id=1, source_target_pairs={{0,1},{1,0},{2,3},{3,2},{4,5},{5,4},{6,7},{7,6},{8,9},{9,8},{10,11... | collective-permute-start | bytes 491528 | tf_op jit(solution)/shard_map/ppermute | solution.py:422

commit v27 on v26

--- a/solution.py
+++ b/solution.py
@@ -142,7 +142,7 @@
     owner = lax.div(far_cols[...], clusters)
     other_core = (owner ^ me) & 1
     chips = size // 2
-    chip = lax.rem(owner // 2 + (chips - middle), chips)
+    chip = lax.rem(middle + chips - owner // 2, chips)
     rank = coupling.shape[1]
     per_group = LANES // rank
     inside = lax.rem(far_cols[...], clusters)
@@ -470,7 +470,7 @@
 
     chips = size // 2
     middle = chips // 4 + 1
-    order = [(middle + n) % chips for n in range(chips)]
+    order = [(middle - n) % chips for n in range(chips)]
 
     def gather(block):
         groups = [[2 * chip + core for chip in order] for core in range(2)]

time: 52 us -> 51.5 us (level)
  no operation moved by 1% of the time
where the time goes in v27:
time: 51.5 us; the launch traced here: 51 us
  Pallas kernels  20.7 us (40%)
  starting transfers between devices  17.3 us (34%)
  blocking collectives  8.26 us (16%)
  waiting for transfers between devices  4.04 us (8%)
  between operations  0.74 us (1%)
    pallas_call x11, Pallas kernels, call(): pl.pallas_call(kernel, out_shape=out, in_specs=ins, out_specs=jax.tree.ma...  20.7 us
    all_to_all x2, starting transfers between devices, gather(): return lax.all_to_all(block, 'rows', 0, 0, axis_index_groups=groups)  12.4 us
    all_to_all x1, blocking collectives, exchange(): return lax.all_to_all(block, 'rows', 0, 0, axis_index_groups=[group])  8.26 us
    ppermute x8, starting transfers between devices, swapped(): lax.ppermute(block, 'rows', [(i, partner(i)) for i in range(lax.axis_size...  4.88 us
    ppermute x8, waiting for transfers between devices, swapped(): lax.ppermute(block, 'rows', [(i, partner(i)) for i in range(lax.axis_size...  2.4 us
    all_to_all x2, waiting for transfers between devices, gather(): return lax.all_to_all(block, 'rows', 0, 0, axis_index_groups=groups)  1.64 us
  transfers between devices with their start and end apart: 10, of which 5 were waited for; matrix products, arithmetic and copies ran while one was open for 0% of the time, Pallas kernels for 20%

profile of v27, /device:TPU:0, one launch (start us, length us, event | category | flops | bytes accessed | tf_op | source)
XLA Modules:
  0.0 51.0 jit_solution(11610296520741005479)
XLA Ops:
  0.6 1.8 %start.1 = (f32[256,128]{1,0:T(8,128)S(1)}, bf16[512,128]{1,0:T(8,128)(2,1)S(1)}, bf16[256,128]{1,0:T(8,128)(2,1)S(1)}, bf16[8,32,128]{2,1,0:T(8,128)(2,1)}) custom-call(f32[8,4096]{1,0:T(8,128)} %b_hbm.1, bf16[512,128]{1,0:T(8,128)(2,1)} %bitcast.8), custom_call_target="tpu_custom_call" | custom-call | tf_op jit(solution)/shard_map/start/pallas_call | solution.py:466
  2.5 7.9 %all-to-all-start = ((bf16[8,32,128]{2,1,0:T(8,128)(2,1)}), bf16[8,32,128]{2,1,0:T(8,128)(2,1)S(1)}, u32[]{:S(2)}, u32[]{:S(2)}) async-start(bf16[8,32,128]{2,1,0:T(8,128)(2,1)} %get-tuple-element.24), calls=%async_computation | async-start | bytes 131072 | tf_op jit(solution)/shard_map/all_to_all | solution.py:477
  10.3 2.4 %collective-permute-start.2 = (bf16[256,128]{1,0:T(8,128)(2,1)S(1)}, bf16[256,128]{1,0:T(8,128)(2,1)S(1)}, u32[]{:S(2)}, u32[]{:S(2)}) collective-permute-start(bf16[256,128]{1,0:T(8,128)(2,1)S(1)} %get-tuple-element.23.own), channel_id=1, source_target_pairs={{0,14},{1,15},{2,4},{3,5},{4,2},{5,3},{6,8},{7,9},{8,6},{9,7},{10,... | collective-permute-start | bytes 196616 | tf_op jit(solution)/shard_map/ppermute | solution.py:422
  12.7 1.6 %ahead.1 = (bf16[32,2,128,128]{3,2,1,0:T(8,128)(2,1)S(1)}, f32[8,128]{1,0:T(8,128)S(1)}) custom-call(bf16[32,8,128,128]{3,2,1,0:T(8,128)(2,1)} %blocks_hbm.7, bf16[256,128]{1,0:T(8,128)(2,1)S(1)} %collective-permute-done.refs_0_.mate), custom_call_target="tpu_custom_call" | custom-call | tf_op jit(solution)/shard_map/ahead/pallas_call | solution.py:466
  14.3 0.5 all-to-all-done.refs_0_.got
  14.8 2.8 %fetch.2 = (bf16[32,6,128,128]{3,2,1,0:T(8,128)(2,1)S(1)}, f32[8,128]{1,0:T(8,128)S(1)}) custom-call(bf16[32,8,128,128]{3,2,1,0:T(8,128)(2,1)} %blocks_hbm.7, bf16[8,32,128]{2,1,0:T(8,128)(2,1)S(1)} %all-to-all-done.refs_0_.got, f32[8,128]{1,0:T(8,128)S(1)} %get-tuple-element.25.refs_1_), custom_call_target="tpu_custom_call" | custom-call | tf_op jit(solution)/shard_map/fetch/pallas_call | solution.py:466
  17.6 0.0 collective-permute-done.2.odd
  17.6 0.7 %collective-permute-done.1.even = bf16[256,128]{1,0:T(8,128)(2,1)S(1)} collective-permute-done((bf16[256,128]{1,0:T(8,128)(2,1)S(1)}, bf16[256,128]{1,0:T(8,128)(2,1)S(1)}, u32[]{:S(2)}, u32[]{:S(2)}) %collective-permute-start.1) | collective-permute-done | bytes 65568 | tf_op jit(solution)/shard_map/ppermute | solution.py:422
  18.3 0.1 collective-permute-start.3
  18.4 1.7 %prepare.1 = (s32[24,32]{1,0:T(8,128)S(1)}, bf16[128,512]{1,0:T(8,128)(2,1)S(1)}, bf16[128,512]{1,0:T(8,128)(2,1)S(1)}, bf16[512,128]{1,0:T(8,128)(2,1)S(1)}) custom-call(s32[8,32]{1,0:T(8,128)} %bitcast.9, s32[1,32]{1,0:T(1,128)} %bitcast.11, s32[8,32]{1,0:T(8,128)} %bitcast.10, f32[8,16,16,32]{3,2,1,0:T(8,128)} %bitcast.6, bf16[512,128]{1,0:T(8,128)(2,1)} %bitcast.7, ...), custom_call_target="tpu_custom_call" | custom-call | tf_op jit(solution)/shard_map/prepare/pallas_call | solution.py:466
  20.1 4.2 %operator_one.1 = (f32[256,128]{1,0:T(8,128)S(1)}, bf16[256,128]{1,0:T(8,128)(2,1)S(1)}, bf16[8,48,128]{2,1,0:T(8,128)(2,1)}) custom-call(bf16[256,128]{1,0:T(8,128)(2,1)S(1)} %get-tuple-element.23.own, bf16[256,128]{1,0:T(8,128)(2,1)S(1)} %collective-permute-done.refs_0_.mate, bf16[256,128]{1,0:T(8,128)(2,1)S(1)} %collective-permute-done.1.even, ...), custom_call_target="tpu_custom_call" | custom-call | tf_op jit(solution)/shard_map/operator_one/pallas_call | solution.py:466
  24.3 4.5 %all-to-all-start.1 = ((bf16[8,48,128]{2,1,0:T(8,128)(2,1)}), bf16[8,48,128]{2,1,0:T(8,128)(2,1)S(1)}, u32[]{:S(2)}, u32[]{:S(2)}) async-start(bf16[8,48,128]{2,1,0:T(8,128)(2,1)} %get-tuple-element.36), calls=%async_computation.1 | async-start | bytes 196608 | tf_op jit(solution)/shard_map/all_to_all | solution.py:477
  28.9 0.0 collective-permute-start.4
  28.9 2.4 %collective-permute-start.6 = (bf16[256,128]{1,0:T(8,128)(2,1)S(1)}, bf16[256,128]{1,0:T(8,128)(2,1)S(1)}, u32[]{:S(2)}, u32[]{:S(2)}) collective-permute-start(bf16[256,128]{1,0:T(8,128)(2,1)S(1)} %get-tuple-element.35.own), channel_id=1, source_target_pairs={{0,14},{1,15},{2,4},{3,5},{4,2},{5,3},{6,8},{7,9},{8,6},{9,7},{10,... | collective-permute-start | bytes 196616 | tf_op jit(solution)/shard_map/ppermute | solution.py:422
  31.2 0.0 collective-permute-start.5
  31.2 1.6 %own.1.refs_1_.started = f32[256,128]{1,0:T(8,128)S(1)} custom-call(bf16[32,8,128,128]{3,2,1,0:T(8,128)(2,1)} %blocks_hbm.7, bf16[256,128]{1,0:T(8,128)(2,1)S(1)} %get-tuple-element.35.own, bf16[256,128]{1,0:T(8,128)(2,1)S(1)} %collective-permute-done.4._.mate), custom_call_target="tpu_custom_call" | custom-call | tf_op jit(solution)/shard_map/own/pallas_call | solution.py:466
  32.9 1.2 %all-to-all-done.1.refs_0_.got = bf16[8,48,128]{2,1,0:T(8,128)(2,1)S(1)} async-done(((bf16[8,48,128]{2,1,0:T(8,128)(2,1)}), bf16[8,48,128]{2,1,0:T(8,128)(2,1)S(1)}, u32[]{:S(2)}, u32[]{:S(2)}) %all-to-all-start.1) | async-done | bytes 98336 | tf_op jit(solution)/shard_map/all_to_all | solution.py:477
  34.0 2.5 %fetch.3 = (bf16[32,5,128,128]{3,2,1,0:T(8,128)(2,1)S(1)}, f32[8,128]{1,0:T(8,128)S(1)}) custom-call(bf16[32,8,128,128]{3,2,1,0:T(8,128)(2,1)} %blocks_hbm.7, bf16[8,48,128]{2,1,0:T(8,128)(2,1)S(1)} %all-to-all-done.1.refs_0_.got, f32[256,128]{1,0:T(8,128)S(1)} %own.1.refs_1_.started), custom_call_target="tpu_custom_call" | custom-call | tf_op jit(solution)/shard_map/fetch/pallas_call | solution.py:466
  36.5 0.3 collective-permute-done.5.even
  36.9 0.1 collective-permute-start.7
  37.0 1.4 %collective-permute-done.7.received = bf16[640,128]{1,0:T(8,128)(2,1)S(1)} collective-permute-done((bf16[640,128]{1,0:T(8,128)(2,1)S(1)}, bf16[640,128]{1,0:T(8,128)(2,1)S(1)}, u32[]{:S(2)}, u32[]{:S(2)}) %collective-permute-start.7) | collective-permute-done | bytes 163872 | tf_op jit(solution)/shard_map/ppermute | solution.py:422
  38.3 3.2 %operator_two.1 = (f32[256,128]{1,0:T(8,128)S(1)}, bf16[16,8,128]{2,1,0:T(8,128)(2,1)S(1)}, f32[8,128]{1,0:T(8,128)S(1)}) custom-call(bf16[256,128]{1,0:T(8,128)(2,1)S(1)} %get-tuple-element.35.own, bf16[256,128]{1,0:T(8,128)(2,1)S(1)} %collective-permute-done.4._.mate, bf16[256,128]{1,0:T(8,128)(2,1)S(1)} %collective-permute-done.5.even, ...), custom_call_target="tpu_custom_call" | custom-call | tf_op jit(solution)/shard_map/operator_two/pallas_call | solution.py:466
  41.5 8.3 %all_to_all.15.got = bf16[16,8,128]{2,1,0:T(8,128)(2,1)S(1)} all-to-all(bf16[16,8,128]{2,1,0:T(8,128)(2,1)S(1)} %get-tuple-element.41), channel_id=1, replica_groups={{6,7,4,5,2,3,0,1,14,15,12,13,10,11,8,9},{22,23,20,21,18,19,16,17,30,31,..., dimensions={0} | all-to-all | bytes 65536 | tf_op jit(solution)/shard_map/all_to_all | solution.py:481
  49.8 1.2 %finish.1 = (f32[8,4096]{1,0:T(8,128)}, f32[8,4096]{1,0:T(8,128)}) custom-call(f32[256,128]{1,0:T(8,128)S(1)} %get-tuple-element.22.b, f32[256,128]{1,0:T(8,128)S(1)} %get-tuple-element.34.image, f32[256,128]{1,0:T(8,128)S(1)} %get-tuple-element.39.candidate, f32[8,128]{1,0:T(8,128)S(1)} %get-tuple-element.40.known, bf16[16,8,128]{2,1,0:T(8,128)(2,1)S(1)} %all_to_all.15.got), custom_call_target="tpu_custom_call" | custom-call | tf_op jit(solution)/shard_map/finish/pallas_call | solution.py:466
  (8 shorter events, 0.0 us)
Async XLA Ops:
  2.5 12.3 %all-to-all-start = ((bf16[8,32,128]{2,1,0:T(8,128)(2,1)}), bf16[8,32,128]{2,1,0:T(8,128)(2,1)S(1)}, u32[]{:S(2)}, u32[]{:S(2)}) async-start(bf16[8,32,128]{2,1,0:T(8,128)(2,1)} %get-tuple-element.24), calls=%async_computation | async-start | bytes 131072 | tf_op jit(solution)/shard_map/all_to_all | solution.py:477
  10.3 2.4 %collective-permute-start = (bf16[256,128]{1,0:T(8,128)(2,1)S(1)}, bf16[256,128]{1,0:T(8,128)(2,1)S(1)}, u32[]{:S(2)}, u32[]{:S(2)}) collective-permute-start(bf16[256,128]{1,0:T(8,128)(2,1)S(1)} %get-tuple-element.23.own), channel_id=1, source_target_pairs={{0,1},{1,0},{2,3},{3,2},{4,5},{5,4},{6,7},{7,6},{8,9},{9,8},{10,11... | collective-permute-start | bytes 196616 | tf_op jit(solution)/shard_map/ppermute | solution.py:422
  10.3 7.3 %collective-permute-start.2 = (bf16[256,128]{1,0:T(8,128)(2,1)S(1)}, bf16[256,128]{1,0:T(8,128)(2,1)S(1)}, u32[]{:S(2)}, u32[]{:S(2)}) collective-permute-start(bf16[256,128]{1,0:T(8,128)(2,1)S(1)} %get-tuple-element.23.own), channel_id=1, source_target_pairs={{0,14},{1,15},{2,4},{3,5},{4,2},{5,3},{6,8},{7,9},{8,6},{9,7},{10,... | collective-permute-start | bytes 196616 | tf_op jit(solution)/shard_map/ppermute | solution.py:422
  12.7 5.6 %collective-permute-start.1 = (bf16[256,128]{1,0:T(8,128)(2,1)S(1)}, bf16[256,128]{1,0:T(8,128)(2,1)S(1)}, u32[]{:S(2)}, u32[]{:S(2)}) collective-permute-start(bf16[256,128]{1,0:T(8,128)(2,1)S(1)} %get-tuple-element.23.own), channel_id=1, source_target_pairs={{0,2},{1,3},{2,0},{3,1},{4,6},{5,7},{6,4},{7,5},{8,10},{9,11},{10,... | collective-permute-start | bytes 196616 | tf_op jit(solution)/shard_map/ppermute | solution.py:422
  18.3 1.7 %collective-permute-start.3 = (bf16[512,128]{1,0:T(8,128)(2,1)S(1)}, bf16[512,128]{1,0:T(8,128)(2,1)S(1)}, u32[]{:S(2)}, u32[]{:S(2)}) collective-permute-start(bf16[512,128]{1,0:T(8,128)(2,1)S(1)} %relay.2._.sent), channel_id=1, source_target_pairs={{0,1},{1,0},{2,3},{3,2},{4,5},{5,4},{6,7},{7,6},{8,9},{9,8},{10,11... | collective-permute-start | bytes 393224 | tf_op jit(solution)/shard_map/ppermute | solution.py:422
  24.3 9.7 %all-to-all-start.1 = ((bf16[8,48,128]{2,1,0:T(8,128)(2,1)}), bf16[8,48,128]{2,1,0:T(8,128)(2,1)S(1)}, u32[]{:S(2)}, u32[]{:S(2)}) async-start(bf16[8,48,128]{2,1,0:T(8,128)(2,1)} %get-tuple-element.36), calls=%async_computation.1 | async-start | bytes 196608 | tf_op jit(solution)/shard_map/all_to_all | solution.py:477
  28.9 2.4 %collective-permute-start.4 = (bf16[256,128]{1,0:T(8,128)(2,1)S(1)}, bf16[256,128]{1,0:T(8,128)(2,1)S(1)}, u32[]{:S(2)}, u32[]{:S(2)}) collective-permute-start(bf16[256,128]{1,0:T(8,128)(2,1)S(1)} %get-tuple-element.35.own), channel_id=1, source_target_pairs={{0,1},{1,0},{2,3},{3,2},{4,5},{5,4},{6,7},{7,6},{8,9},{9,8},{10,11... | collective-permute-start | bytes 196616 | tf_op jit(solution)/shard_map/ppermute | solution.py:422
  28.9 7.7 %collective-permute-start.6 = (bf16[256,128]{1,0:T(8,128)(2,1)S(1)}, bf16[256,128]{1,0:T(8,128)(2,1)S(1)}, u32[]{:S(2)}, u32[]{:S(2)}) collective-permute-start(bf16[256,128]{1,0:T(8,128)(2,1)S(1)} %get-tuple-element.35.own), channel_id=1, source_target_pairs={{0,14},{1,15},{2,4},{3,5},{4,2},{5,3},{6,8},{7,9},{8,6},{9,7},{10,... | collective-permute-start | bytes 196616 | tf_op jit(solution)/shard_map/ppermute | solution.py:422
  31.2 5.6 %collective-permute-start.5 = (bf16[256,128]{1,0:T(8,128)(2,1)S(1)}, bf16[256,128]{1,0:T(8,128)(2,1)S(1)}, u32[]{:S(2)}, u32[]{:S(2)}) collective-permute-start(bf16[256,128]{1,0:T(8,128)(2,1)S(1)} %get-tuple-element.35.own), channel_id=1, source_target_pairs={{0,2},{1,3},{2,0},{3,1},{4,6},{5,7},{6,4},{7,5},{8,10},{9,11},{10,... | collective-permute-start | bytes 196616 | tf_op jit(solution)/shard_map/ppermute | solution.py:422
  36.9 1.5 %collective-permute-start.7 = (bf16[640,128]{1,0:T(8,128)(2,1)S(1)}, bf16[640,128]{1,0:T(8,128)(2,1)S(1)}, u32[]{:S(2)}, u32[]{:S(2)}) collective-permute-start(bf16[640,128]{1,0:T(8,128)(2,1)S(1)} %relay.3.sent), channel_id=1, source_target_pairs={{0,1},{1,0},{2,3},{3,2},{4,5},{5,4},{6,7},{7,6},{8,9},{9,8},{10,11... | collective-permute-start | bytes 491528 | tf_op jit(solution)/shard_map/ppermute | solution.py:422

commit v28 on v27

--- a/solution.py
+++ b/solution.py
@@ -123,13 +123,13 @@
     places, high_out, low_out, target_out, near_cols, near_counts, far_cols, coupling, target, sems,
 ):
     pairs = (
-        (near_cols_hbm, near_cols), (near_counts_hbm, near_counts), (far_cols_hbm, far_cols),
-        (coupling_hbm, coupling), (target_hbm, target),
+        (coupling_hbm, coupling), (near_cols_hbm, near_cols), (near_counts_hbm, near_counts),
+        (far_cols_hbm, far_cols), (target_hbm, target),
     )
     copies = [pltpu.make_async_copy(source, to, sems.at[n]) for n, (source, to) in enumerate(pairs)]
     for copy in copies:
         copy.start()
-    for copy in copies[:3]:
+    for copy in copies[1:4]:
         copy.wait()
     slots, clusters = near_cols.shape
     me = lax.axis_index(axis)
@@ -150,9 +150,15 @@
     places[slots : 2 * slots, :] = tile * R
     slot = lax.broadcasted_iota(jnp.int32, (slots, clusters), 0)
     places[2 * slots :, :] = ((slot - inside) * rank) & (LANES - 1)
-    for copy in copies[3:5]:
-        copy.wait()
-    slots, rank, _, clusters = coupling.shape
+    _, rank, _, clusters = coupling.shape
+    size = rank * clusters
+    row = lax.broadcasted_iota(jnp.int32, (size, 1), 0)
+    column = lax.broadcasted_iota(jnp.int32, (size, size), 1)
+    wanted = lax.rem(row, clusters) * rank + lax.div(row, clusters)
+    picks = (column == wanted).astype(bf16)
+    copies[4].wait()
+    target_out[...] = dot(picks, target[...]).astype(bf16)
+    copies[0].wait()
     per_tile = LANES // clusters
     for s in range(rank // per_tile):
         pieces = [
@@ -162,11 +168,6 @@
         high = tile.astype(bf16)
         high_out[:, s * LANES : (s + 1) * LANES] = high
         low_out[:, s * LANES : (s + 1) * LANES] = (tile - high.astype(f32)).astype(bf16)
-    size = rank * clusters
-    row = lax.broadcasted_iota(jnp.int32, (size, 1), 0)
-    column = lax.broadcasted_iota(jnp.int32, (size, size), 1)
-    wanted = lax.rem(row, clusters) * rank + lax.div(row, clusters)
-    target_out[...] = dot((column == wanted).astype(bf16), target[...]).astype(bf16)
 
 
 def fetch_kernel(slots, blocks_hbm, *refs):

time: 51.5 us -> 51.7 us (level)
  no operation moved by 1% of the time
where the time goes in v28:
time: 51.7 us; the launch traced here: 51.3 us
  Pallas kernels  20.9 us (40%)
  starting transfers between devices  17.3 us (33%)
  blocking collectives  8.26 us (16%)
  waiting for transfers between devices  4.04 us (8%)
  between operations  0.74 us (1%)
    pallas_call x11, Pallas kernels, call(): pl.pallas_call(kernel, out_shape=out, in_specs=ins, out_specs=jax.tree.ma...  20.9 us
    all_to_all x2, starting transfers between devices, gather(): return lax.all_to_all(block, 'rows', 0, 0, axis_index_groups=groups)  12.4 us
    all_to_all x1, blocking collectives, exchange(): return lax.all_to_all(block, 'rows', 0, 0, axis_index_groups=[group])  8.26 us
    ppermute x8, starting transfers between devices, swapped(): lax.ppermute(block, 'rows', [(i, partner(i)) for i in range(lax.axis_size...  4.88 us
    ppermute x8, waiting for transfers between devices, swapped(): lax.ppermute(block, 'rows', [(i, partner(i)) for i in range(lax.axis_size...  2.38 us
    all_to_all x2, waiting for transfers between devices, gather(): return lax.all_to_all(block, 'rows', 0, 0, axis_index_groups=groups)  1.65 us
  transfers between devices with their start and end apart: 10, of which 5 were waited for; matrix products, arithmetic and copies ran while one was open for 0% of the time, Pallas kernels for 20%

profile of v28, /device:TPU:0, one launch (start us, length us, event | category | flops | bytes accessed | tf_op | source)
XLA Modules:
  0.0 51.3 jit_solution(793724383105261964)
XLA Ops:
  0.6 1.8 %start.1 = (f32[256,128]{1,0:T(8,128)S(1)}, bf16[512,128]{1,0:T(8,128)(2,1)S(1)}, bf16[256,128]{1,0:T(8,128)(2,1)S(1)}, bf16[8,32,128]{2,1,0:T(8,128)(2,1)}) custom-call(f32[8,4096]{1,0:T(8,128)} %b_hbm.1, bf16[512,128]{1,0:T(8,128)(2,1)} %bitcast.8), custom_call_target="tpu_custom_call" | custom-call | tf_op jit(solution)/shard_map/start/pallas_call | solution.py:467
  2.5 7.9 %all-to-all-start = ((bf16[8,32,128]{2,1,0:T(8,128)(2,1)}), bf16[8,32,128]{2,1,0:T(8,128)(2,1)S(1)}, u32[]{:S(2)}, u32[]{:S(2)}) async-start(bf16[8,32,128]{2,1,0:T(8,128)(2,1)} %get-tuple-element.24), calls=%async_computation | async-start | bytes 131072 | tf_op jit(solution)/shard_map/all_to_all | solution.py:478
  10.3 2.4 %collective-permute-start.2 = (bf16[256,128]{1,0:T(8,128)(2,1)S(1)}, bf16[256,128]{1,0:T(8,128)(2,1)S(1)}, u32[]{:S(2)}, u32[]{:S(2)}) collective-permute-start(bf16[256,128]{1,0:T(8,128)(2,1)S(1)} %get-tuple-element.23.own), channel_id=1, source_target_pairs={{0,14},{1,15},{2,4},{3,5},{4,2},{5,3},{6,8},{7,9},{8,6},{9,7},{10,... | collective-permute-start | bytes 196616 | tf_op jit(solution)/shard_map/ppermute | solution.py:423
  12.7 1.6 %ahead.1 = (bf16[32,2,128,128]{3,2,1,0:T(8,128)(2,1)S(1)}, f32[8,128]{1,0:T(8,128)S(1)}) custom-call(bf16[32,8,128,128]{3,2,1,0:T(8,128)(2,1)} %blocks_hbm.7, bf16[256,128]{1,0:T(8,128)(2,1)S(1)} %collective-permute-done.refs_0_.mate), custom_call_target="tpu_custom_call" | custom-call | tf_op jit(solution)/shard_map/ahead/pallas_call | solution.py:467
  14.3 0.5 all-to-all-done.refs_0_.got
  14.8 2.8 %fetch.2 = (bf16[32,6,128,128]{3,2,1,0:T(8,128)(2,1)S(1)}, f32[8,128]{1,0:T(8,128)S(1)}) custom-call(bf16[32,8,128,128]{3,2,1,0:T(8,128)(2,1)} %blocks_hbm.7, bf16[8,32,128]{2,1,0:T(8,128)(2,1)S(1)} %all-to-all-done.refs_0_.got, f32[8,128]{1,0:T(8,128)S(1)} %get-tuple-element.25.refs_1_), custom_call_target="tpu_custom_call" | custom-call | tf_op jit(solution)/shard_map/fetch/pallas_call | solution.py:467
  17.6 0.0 collective-permute-done.2.odd
  17.6 0.7 %collective-permute-done.1.even = bf16[256,128]{1,0:T(8,128)(2,1)S(1)} collective-permute-done((bf16[256,128]{1,0:T(8,128)(2,1)S(1)}, bf16[256,128]{1,0:T(8,128)(2,1)S(1)}, u32[]{:S(2)}, u32[]{:S(2)}) %collective-permute-start.1) | collective-permute-done | bytes 65568 | tf_op jit(solution)/shard_map/ppermute | solution.py:423
  18.3 0.1 collective-permute-start.3
  18.4 1.9 %prepare.1 = (s32[24,32]{1,0:T(8,128)S(1)}, bf16[128,512]{1,0:T(8,128)(2,1)S(1)}, bf16[128,512]{1,0:T(8,128)(2,1)S(1)}, bf16[512,128]{1,0:T(8,128)(2,1)S(1)}) custom-call(s32[8,32]{1,0:T(8,128)} %bitcast.9, s32[1,32]{1,0:T(1,128)} %bitcast.11, s32[8,32]{1,0:T(8,128)} %bitcast.10, f32[8,16,16,32]{3,2,1,0:T(8,128)} %bitcast.6, bf16[512,128]{1,0:T(8,128)(2,1)} %bitcast.7, ...), custom_call_target="tpu_custom_call" | custom-call | tf_op jit(solution)/shard_map/prepare/pallas_call | solution.py:467
  20.3 0.0 collective-permute-done.3.received
  20.3 4.2 %operator_one.1 = (f32[256,128]{1,0:T(8,128)S(1)}, bf16[256,128]{1,0:T(8,128)(2,1)S(1)}, bf16[8,48,128]{2,1,0:T(8,128)(2,1)}) custom-call(bf16[256,128]{1,0:T(8,128)(2,1)S(1)} %get-tuple-element.23.own, bf16[256,128]{1,0:T(8,128)(2,1)S(1)} %collective-permute-done.refs_0_.mate, bf16[256,128]{1,0:T(8,128)(2,1)S(1)} %collective-permute-done.1.even, ...), custom_call_target="tpu_custom_call" | custom-call | tf_op jit(solution)/shard_map/operator_one/pallas_call | solution.py:467
  24.6 4.5 %all-to-all-start.1 = ((bf16[8,48,128]{2,1,0:T(8,128)(2,1)}), bf16[8,48,128]{2,1,0:T(8,128)(2,1)S(1)}, u32[]{:S(2)}, u32[]{:S(2)}) async-start(bf16[8,48,128]{2,1,0:T(8,128)(2,1)} %get-tuple-element.36), calls=%async_computation.1 | async-start | bytes 196608 | tf_op jit(solution)/shard_map/all_to_all | solution.py:478
  29.1 2.4 %collective-permute-start.6 = (bf16[256,128]{1,0:T(8,128)(2,1)S(1)}, bf16[256,128]{1,0:T(8,128)(2,1)S(1)}, u32[]{:S(2)}, u32[]{:S(2)}) collective-permute-start(bf16[256,128]{1,0:T(8,128)(2,1)S(1)} %get-tuple-element.35.own), channel_id=1, source_target_pairs={{0,14},{1,15},{2,4},{3,5},{4,2},{5,3},{6,8},{7,9},{8,6},{9,7},{10,... | collective-permute-start | bytes 196616 | tf_op jit(solution)/shard_map/ppermute | solution.py:423
  31.5 0.0 collective-permute-start.5
  31.5 1.6 %own.1.refs_1_.started = f32[256,128]{1,0:T(8,128)S(1)} custom-call(bf16[32,8,128,128]{3,2,1,0:T(8,128)(2,1)} %blocks_hbm.7, bf16[256,128]{1,0:T(8,128)(2,1)S(1)} %get-tuple-element.35.own, bf16[256,128]{1,0:T(8,128)(2,1)S(1)} %collective-permute-done.4._.mate), custom_call_target="tpu_custom_call" | custom-call | tf_op jit(solution)/shard_map/own/pallas_call | solution.py:467
  33.1 1.2 %all-to-all-done.1.refs_0_.got = bf16[8,48,128]{2,1,0:T(8,128)(2,1)S(1)} async-done(((bf16[8,48,128]{2,1,0:T(8,128)(2,1)}), bf16[8,48,128]{2,1,0:T(8,128)(2,1)S(1)}, u32[]{:S(2)}, u32[]{:S(2)}) %all-to-all-start.1) | async-done | bytes 98336 | tf_op jit(solution)/shard_map/all_to_all | solution.py:478
  34.3 2.5 %fetch.3 = (bf16[32,5,128,128]{3,2,1,0:T(8,128)(2,1)S(1)}, f32[8,128]{1,0:T(8,128)S(1)}) custom-call(bf16[32,8,128,128]{3,2,1,0:T(8,128)(2,1)} %blocks_hbm.7, bf16[8,48,128]{2,1,0:T(8,128)(2,1)S(1)} %all-to-all-done.1.refs_0_.got, f32[256,128]{1,0:T(8,128)S(1)} %own.1.refs_1_.started), custom_call_target="tpu_custom_call" | custom-call | tf_op jit(solution)/shard_map/fetch/pallas_call | solution.py:467
  36.8 0.3 collective-permute-done.5.even
  37.1 0.1 collective-permute-start.7
  37.2 1.4 %collective-permute-done.7.received = bf16[640,128]{1,0:T(8,128)(2,1)S(1)} collective-permute-done((bf16[640,128]{1,0:T(8,128)(2,1)S(1)}, bf16[640,128]{1,0:T(8,128)(2,1)S(1)}, u32[]{:S(2)}, u32[]{:S(2)}) %collective-permute-start.7) | collective-permute-done | bytes 163872 | tf_op jit(solution)/shard_map/ppermute | solution.py:423
  38.6 3.2 %operator_two.1 = (f32[256,128]{1,0:T(8,128)S(1)}, bf16[16,8,128]{2,1,0:T(8,128)(2,1)S(1)}, f32[8,128]{1,0:T(8,128)S(1)}) custom-call(bf16[256,128]{1,0:T(8,128)(2,1)S(1)} %get-tuple-element.35.own, bf16[256,128]{1,0:T(8,128)(2,1)S(1)} %collective-permute-done.4._.mate, bf16[256,128]{1,0:T(8,128)(2,1)S(1)} %collective-permute-done.5.even, ...), custom_call_target="tpu_custom_call" | custom-call | tf_op jit(solution)/shard_map/operator_two/pallas_call | solution.py:467
  41.8 8.3 %all_to_all.15.got = bf16[16,8,128]{2,1,0:T(8,128)(2,1)S(1)} all-to-all(bf16[16,8,128]{2,1,0:T(8,128)(2,1)S(1)} %get-tuple-element.41), channel_id=1, replica_groups={{6,7,4,5,2,3,0,1,14,15,12,13,10,11,8,9},{22,23,20,21,18,19,16,17,30,31,..., dimensions={0} | all-to-all | bytes 65536 | tf_op jit(solution)/shard_map/all_to_all | solution.py:482
  50.0 1.2 %finish.1 = (f32[8,4096]{1,0:T(8,128)}, f32[8,4096]{1,0:T(8,128)}) custom-call(f32[256,128]{1,0:T(8,128)S(1)} %get-tuple-element.22.b, f32[256,128]{1,0:T(8,128)S(1)} %get-tuple-element.34.image, f32[256,128]{1,0:T(8,128)S(1)} %get-tuple-element.39.candidate, f32[8,128]{1,0:T(8,128)S(1)} %get-tuple-element.40.known, bf16[16,8,128]{2,1,0:T(8,128)(2,1)S(1)} %all_to_all.15.got), custom_call_target="tpu_custom_call" | custom-call | tf_op jit(solution)/shard_map/finish/pallas_call | solution.py:467
  (8 shorter events, 0.0 us)
Async XLA Ops:
  2.5 12.3 %all-to-all-start = ((bf16[8,32,128]{2,1,0:T(8,128)(2,1)}), bf16[8,32,128]{2,1,0:T(8,128)(2,1)S(1)}, u32[]{:S(2)}, u32[]{:S(2)}) async-start(bf16[8,32,128]{2,1,0:T(8,128)(2,1)} %get-tuple-element.24), calls=%async_computation | async-start | bytes 131072 | tf_op jit(solution)/shard_map/all_to_all | solution.py:478
  10.3 2.4 %collective-permute-start = (bf16[256,128]{1,0:T(8,128)(2,1)S(1)}, bf16[256,128]{1,0:T(8,128)(2,1)S(1)}, u32[]{:S(2)}, u32[]{:S(2)}) collective-permute-start(bf16[256,128]{1,0:T(8,128)(2,1)S(1)} %get-tuple-element.23.own), channel_id=1, source_target_pairs={{0,1},{1,0},{2,3},{3,2},{4,5},{5,4},{6,7},{7,6},{8,9},{9,8},{10,11... | collective-permute-start | bytes 196616 | tf_op jit(solution)/shard_map/ppermute | solution.py:423
  10.3 7.3 %collective-permute-start.2 = (bf16[256,128]{1,0:T(8,128)(2,1)S(1)}, bf16[256,128]{1,0:T(8,128)(2,1)S(1)}, u32[]{:S(2)}, u32[]{:S(2)}) collective-permute-start(bf16[256,128]{1,0:T(8,128)(2,1)S(1)} %get-tuple-element.23.own), channel_id=1, source_target_pairs={{0,14},{1,15},{2,4},{3,5},{4,2},{5,3},{6,8},{7,9},{8,6},{9,7},{10,... | collective-permute-start | bytes 196616 | tf_op jit(solution)/shard_map/ppermute | solution.py:423
  12.7 5.6 %collective-permute-start.1 = (bf16[256,128]{1,0:T(8,128)(2,1)S(1)}, bf16[256,128]{1,0:T(8,128)(2,1)S(1)}, u32[]{:S(2)}, u32[]{:S(2)}) collective-permute-start(bf16[256,128]{1,0:T(8,128)(2,1)S(1)} %get-tuple-element.23.own), channel_id=1, source_target_pairs={{0,2},{1,3},{2,0},{3,1},{4,6},{5,7},{6,4},{7,5},{8,10},{9,11},{10,... | collective-permute-start | bytes 196616 | tf_op jit(solution)/shard_map/ppermute | solution.py:423
  18.3 2.0 %collective-permute-start.3 = (bf16[512,128]{1,0:T(8,128)(2,1)S(1)}, bf16[512,128]{1,0:T(8,128)(2,1)S(1)}, u32[]{:S(2)}, u32[]{:S(2)}) collective-permute-start(bf16[512,128]{1,0:T(8,128)(2,1)S(1)} %relay.2._.sent), channel_id=1, source_target_pairs={{0,1},{1,0},{2,3},{3,2},{4,5},{5,4},{6,7},{7,6},{8,9},{9,8},{10,11... | collective-permute-start | bytes 393224 | tf_op jit(solution)/shard_map/ppermute | solution.py:423
  24.6 9.7 %all-to-all-start.1 = ((bf16[8,48,128]{2,1,0:T(8,128)(2,1)}), bf16[8,48,128]{2,1,0:T(8,128)(2,1)S(1)}, u32[]{:S(2)}, u32[]{:S(2)}) async-start(bf16[8,48,128]{2,1,0:T(8,128)(2,1)} %get-tuple-element.36), calls=%async_computation.1 | async-start | bytes 196608 | tf_op jit(solution)/shard_map/all_to_all | solution.py:478
  29.1 2.4 %collective-permute-start.4 = (bf16[256,128]{1,0:T(8,128)(2,1)S(1)}, bf16[256,128]{1,0:T(8,128)(2,1)S(1)}, u32[]{:S(2)}, u32[]{:S(2)}) collective-permute-start(bf16[256,128]{1,0:T(8,128)(2,1)S(1)} %get-tuple-element.35.own), channel_id=1, source_target_pairs={{0,1},{1,0},{2,3},{3,2},{4,5},{5,4},{6,7},{7,6},{8,9},{9,8},{10,11... | collective-permute-start | bytes 196616 | tf_op jit(solution)/shard_map/ppermute | solution.py:423
  29.1 7.7 %collective-permute-start.6 = (bf16[256,128]{1,0:T(8,128)(2,1)S(1)}, bf16[256,128]{1,0:T(8,128)(2,1)S(1)}, u32[]{:S(2)}, u32[]{:S(2)}) collective-permute-start(bf16[256,128]{1,0:T(8,128)(2,1)S(1)} %get-tuple-element.35.own), channel_id=1, source_target_pairs={{0,14},{1,15},{2,4},{3,5},{4,2},{5,3},{6,8},{7,9},{8,6},{9,7},{10,... | collective-permute-start | bytes 196616 | tf_op jit(solution)/shard_map/ppermute | solution.py:423
  31.5 5.6 %collective-permute-start.5 = (bf16[256,128]{1,0:T(8,128)(2,1)S(1)}, bf16[256,128]{1,0:T(8,128)(2,1)S(1)}, u32[]{:S(2)}, u32[]{:S(2)}) collective-permute-start(bf16[256,128]{1,0:T(8,128)(2,1)S(1)} %get-tuple-element.35.own), channel_id=1, source_target_pairs={{0,2},{1,3},{2,0},{3,1},{4,6},{5,7},{6,4},{7,5},{8,10},{9,11},{10,... | collective-permute-start | bytes 196616 | tf_op jit(solution)/shard_map/ppermute | solution.py:423
  37.1 1.5 %collective-permute-start.7 = (bf16[640,128]{1,0:T(8,128)(2,1)S(1)}, bf16[640,128]{1,0:T(8,128)(2,1)S(1)}, u32[]{:S(2)}, u32[]{:S(2)}) collective-permute-start(bf16[640,128]{1,0:T(8,128)(2,1)S(1)} %relay.3.sent), channel_id=1, source_target_pairs={{0,1},{1,0},{2,3},{3,2},{4,5},{5,4},{6,7},{7,6},{8,9},{9,8},{10,11... | collective-permute-start | bytes 491528 | tf_op jit(solution)/shard_map/ppermute | solution.py:423

commit v29 on v27

--- a/solution.py
+++ b/solution.py
@@ -548,7 +548,7 @@
     held = sends_of(lowered)
     started = call(
         own_kernel, "own", shape(rows, LANES), [HBM, VMEM, ANY], blocks, lowered, held[1],
-        scratch_shapes=[scratch(clusters, 1, LANES, LANES, dtype=bf16), pltpu.SemaphoreType.DMA((1,))],
+        scratch_shapes=[scratch(clusters, 1, LANES, LANES, dtype=bf16), pltpu.SemaphoreType.DMA((2,))],
     )
     here = arrived(got, held, [late], started)
     candidate, sums, known = call(

time: 51.5 us -> 51.5 us (level)
  no operation moved by 1% of the time
where the time goes in v29:
time: 51.5 us; the launch traced here: 51 us
  Pallas kernels  20.6 us (40%)
  starting transfers between devices  17.3 us (34%)
  blocking collectives  8.24 us (16%)
  waiting for transfers between devices  4.1 us (8%)
  between operations  0.74 us (1%)
    pallas_call x11, Pallas kernels, call(): pl.pallas_call(kernel, out_shape=out, in_specs=ins, out_specs=jax.tree.ma...  20.6 us
    all_to_all x2, starting transfers between devices, gather(): return lax.all_to_all(block, 'rows', 0, 0, axis_index_groups=groups)  12.4 us
    all_to_all x1, blocking collectives, exchange(): return lax.all_to_all(block, 'rows', 0, 0, axis_index_groups=[group])  8.24 us
    ppermute x8, starting transfers between devices, swapped(): lax.ppermute(block, 'rows', [(i, partner(i)) for i in range(lax.axis_size...  4.88 us
    ppermute x8, waiting for transfers between devices, swapped(): lax.ppermute(block, 'rows', [(i, partner(i)) for i in range(lax.axis_size...  2.4 us
    all_to_all x2, waiting for transfers between devices, gather(): return lax.all_to_all(block, 'rows', 0, 0, axis_index_groups=groups)  1.7 us
  transfers between devices with their start and end apart: 10, of which 5 were waited for; matrix products, arithmetic and copies ran while one was open for 0% of the time, Pallas kernels for 20%

profile of v29, /device:TPU:0, one launch (start us, length us, event | category | flops | bytes accessed | tf_op | source)
XLA Modules:
  0.0 51.0 jit_solution(2608836789514006014)
XLA Ops:
  0.6 1.8 %start.1 = (f32[256,128]{1,0:T(8,128)S(1)}, bf16[512,128]{1,0:T(8,128)(2,1)S(1)}, bf16[256,128]{1,0:T(8,128)(2,1)S(1)}, bf16[8,32,128]{2,1,0:T(8,128)(2,1)}) custom-call(f32[8,4096]{1,0:T(8,128)} %b_hbm.1, bf16[512,128]{1,0:T(8,128)(2,1)} %bitcast.8), custom_call_target="tpu_custom_call" | custom-call | tf_op jit(solution)/shard_map/start/pallas_call | solution.py:466
  2.5 7.9 %all-to-all-start = ((bf16[8,32,128]{2,1,0:T(8,128)(2,1)}), bf16[8,32,128]{2,1,0:T(8,128)(2,1)S(1)}, u32[]{:S(2)}, u32[]{:S(2)}) async-start(bf16[8,32,128]{2,1,0:T(8,128)(2,1)} %get-tuple-element.24), calls=%async_computation | async-start | bytes 131072 | tf_op jit(solution)/shard_map/all_to_all | solution.py:477
  10.3 2.4 %collective-permute-start.2 = (bf16[256,128]{1,0:T(8,128)(2,1)S(1)}, bf16[256,128]{1,0:T(8,128)(2,1)S(1)}, u32[]{:S(2)}, u32[]{:S(2)}) collective-permute-start(bf16[256,128]{1,0:T(8,128)(2,1)S(1)} %get-tuple-element.23.own), channel_id=1, source_target_pairs={{0,14},{1,15},{2,4},{3,5},{4,2},{5,3},{6,8},{7,9},{8,6},{9,7},{10,... | collective-permute-start | bytes 196616 | tf_op jit(solution)/shard_map/ppermute | solution.py:422
  12.7 1.6 %ahead.1 = (bf16[32,2,128,128]{3,2,1,0:T(8,128)(2,1)S(1)}, f32[8,128]{1,0:T(8,128)S(1)}) custom-call(bf16[32,8,128,128]{3,2,1,0:T(8,128)(2,1)} %blocks_hbm.7, bf16[256,128]{1,0:T(8,128)(2,1)S(1)} %collective-permute-done.refs_0_.mate), custom_call_target="tpu_custom_call" | custom-call | tf_op jit(solution)/shard_map/ahead/pallas_call | solution.py:466
  14.3 0.5 all-to-all-done.refs_0_.got
  14.8 2.8 %fetch.2 = (bf16[32,6,128,128]{3,2,1,0:T(8,128)(2,1)S(1)}, f32[8,128]{1,0:T(8,128)S(1)}) custom-call(bf16[32,8,128,128]{3,2,1,0:T(8,128)(2,1)} %blocks_hbm.7, bf16[8,32,128]{2,1,0:T(8,128)(2,1)S(1)} %all-to-all-done.refs_0_.got, f32[8,128]{1,0:T(8,128)S(1)} %get-tuple-element.25.refs_1_), custom_call_target="tpu_custom_call" | custom-call | tf_op jit(solution)/shard_map/fetch/pallas_call | solution.py:466
  17.6 0.0 collective-permute-done.2.odd
  17.6 0.7 %collective-permute-done.1.even = bf16[256,128]{1,0:T(8,128)(2,1)S(1)} collective-permute-done((bf16[256,128]{1,0:T(8,128)(2,1)S(1)}, bf16[256,128]{1,0:T(8,128)(2,1)S(1)}, u32[]{:S(2)}, u32[]{:S(2)}) %collective-permute-start.1) | collective-permute-done | bytes 65568 | tf_op jit(solution)/shard_map/ppermute | solution.py:422
  18.3 0.1 collective-permute-start.3
  18.4 1.7 %prepare.1 = (s32[24,32]{1,0:T(8,128)S(1)}, bf16[128,512]{1,0:T(8,128)(2,1)S(1)}, bf16[128,512]{1,0:T(8,128)(2,1)S(1)}, bf16[512,128]{1,0:T(8,128)(2,1)S(1)}) custom-call(s32[8,32]{1,0:T(8,128)} %bitcast.9, s32[1,32]{1,0:T(1,128)} %bitcast.11, s32[8,32]{1,0:T(8,128)} %bitcast.10, f32[8,16,16,32]{3,2,1,0:T(8,128)} %bitcast.6, bf16[512,128]{1,0:T(8,128)(2,1)} %bitcast.7, ...), custom_call_target="tpu_custom_call" | custom-call | tf_op jit(solution)/shard_map/prepare/pallas_call | solution.py:466
  20.1 4.2 %operator_one.1 = (f32[256,128]{1,0:T(8,128)S(1)}, bf16[256,128]{1,0:T(8,128)(2,1)S(1)}, bf16[8,48,128]{2,1,0:T(8,128)(2,1)}) custom-call(bf16[256,128]{1,0:T(8,128)(2,1)S(1)} %get-tuple-element.23.own, bf16[256,128]{1,0:T(8,128)(2,1)S(1)} %collective-permute-done.refs_0_.mate, bf16[256,128]{1,0:T(8,128)(2,1)S(1)} %collective-permute-done.1.even, ...), custom_call_target="tpu_custom_call" | custom-call | tf_op jit(solution)/shard_map/operator_one/pallas_call | solution.py:466
  24.3 4.5 %all-to-all-start.1 = ((bf16[8,48,128]{2,1,0:T(8,128)(2,1)}), bf16[8,48,128]{2,1,0:T(8,128)(2,1)S(1)}, u32[]{:S(2)}, u32[]{:S(2)}) async-start(bf16[8,48,128]{2,1,0:T(8,128)(2,1)} %get-tuple-element.36), calls=%async_computation.1 | async-start | bytes 196608 | tf_op jit(solution)/shard_map/all_to_all | solution.py:477
  28.9 0.0 collective-permute-start.4
  28.9 2.4 %collective-permute-start.6 = (bf16[256,128]{1,0:T(8,128)(2,1)S(1)}, bf16[256,128]{1,0:T(8,128)(2,1)S(1)}, u32[]{:S(2)}, u32[]{:S(2)}) collective-permute-start(bf16[256,128]{1,0:T(8,128)(2,1)S(1)} %get-tuple-element.35.own), channel_id=1, source_target_pairs={{0,14},{1,15},{2,4},{3,5},{4,2},{5,3},{6,8},{7,9},{8,6},{9,7},{10,... | collective-permute-start | bytes 196616 | tf_op jit(solution)/shard_map/ppermute | solution.py:422
  31.2 0.0 collective-permute-start.5
  31.2 1.6 %own.1.refs_1_.started = f32[256,128]{1,0:T(8,128)S(1)} custom-call(bf16[32,8,128,128]{3,2,1,0:T(8,128)(2,1)} %blocks_hbm.7, bf16[256,128]{1,0:T(8,128)(2,1)S(1)} %get-tuple-element.35.own, bf16[256,128]{1,0:T(8,128)(2,1)S(1)} %collective-permute-done.4._.mate), custom_call_target="tpu_custom_call" | custom-call | tf_op jit(solution)/shard_map/own/pallas_call | solution.py:466
  32.8 1.2 %all-to-all-done.1.refs_0_.got = bf16[8,48,128]{2,1,0:T(8,128)(2,1)S(1)} async-done(((bf16[8,48,128]{2,1,0:T(8,128)(2,1)}), bf16[8,48,128]{2,1,0:T(8,128)(2,1)S(1)}, u32[]{:S(2)}, u32[]{:S(2)}) %all-to-all-start.1) | async-done | bytes 98336 | tf_op jit(solution)/shard_map/all_to_all | solution.py:477
  34.0 2.5 %fetch.3 = (bf16[32,5,128,128]{3,2,1,0:T(8,128)(2,1)S(1)}, f32[8,128]{1,0:T(8,128)S(1)}) custom-call(bf16[32,8,128,128]{3,2,1,0:T(8,128)(2,1)} %blocks_hbm.7, bf16[8,48,128]{2,1,0:T(8,128)(2,1)S(1)} %all-to-all-done.1.refs_0_.got, f32[256,128]{1,0:T(8,128)S(1)} %own.1.refs_1_.started), custom_call_target="tpu_custom_call" | custom-call | tf_op jit(solution)/shard_map/fetch/pallas_call | solution.py:466
  36.5 0.3 collective-permute-done.5.even
  36.9 0.1 collective-permute-start.7
  37.0 1.4 %collective-permute-done.7.received = bf16[640,128]{1,0:T(8,128)(2,1)S(1)} collective-permute-done((bf16[640,128]{1,0:T(8,128)(2,1)S(1)}, bf16[640,128]{1,0:T(8,128)(2,1)S(1)}, u32[]{:S(2)}, u32[]{:S(2)}) %collective-permute-start.7) | collective-permute-done | bytes 163872 | tf_op jit(solution)/shard_map/ppermute | solution.py:422
  38.3 3.2 %operator_two.1 = (f32[256,128]{1,0:T(8,128)S(1)}, bf16[16,8,128]{2,1,0:T(8,128)(2,1)S(1)}, f32[8,128]{1,0:T(8,128)S(1)}) custom-call(bf16[256,128]{1,0:T(8,128)(2,1)S(1)} %get-tuple-element.35.own, bf16[256,128]{1,0:T(8,128)(2,1)S(1)} %collective-permute-done.4._.mate, bf16[256,128]{1,0:T(8,128)(2,1)S(1)} %collective-permute-done.5.even, ...), custom_call_target="tpu_custom_call" | custom-call | tf_op jit(solution)/shard_map/operator_two/pallas_call | solution.py:466
  41.5 8.2 %all_to_all.15.got = bf16[16,8,128]{2,1,0:T(8,128)(2,1)S(1)} all-to-all(bf16[16,8,128]{2,1,0:T(8,128)(2,1)S(1)} %get-tuple-element.41), channel_id=1, replica_groups={{6,7,4,5,2,3,0,1,14,15,12,13,10,11,8,9},{22,23,20,21,18,19,16,17,30,31,..., dimensions={0} | all-to-all | bytes 65536 | tf_op jit(solution)/shard_map/all_to_all | solution.py:481
  49.8 1.2 %finish.1 = (f32[8,4096]{1,0:T(8,128)}, f32[8,4096]{1,0:T(8,128)}) custom-call(f32[256,128]{1,0:T(8,128)S(1)} %get-tuple-element.22.b, f32[256,128]{1,0:T(8,128)S(1)} %get-tuple-element.34.image, f32[256,128]{1,0:T(8,128)S(1)} %get-tuple-element.39.candidate, f32[8,128]{1,0:T(8,128)S(1)} %get-tuple-element.40.known, bf16[16,8,128]{2,1,0:T(8,128)(2,1)S(1)} %all_to_all.15.got), custom_call_target="tpu_custom_call" | custom-call | tf_op jit(solution)/shard_map/finish/pallas_call | solution.py:466
  (8 shorter events, 0.0 us)
Async XLA Ops:
  2.5 12.3 %all-to-all-start = ((bf16[8,32,128]{2,1,0:T(8,128)(2,1)}), bf16[8,32,128]{2,1,0:T(8,128)(2,1)S(1)}, u32[]{:S(2)}, u32[]{:S(2)}) async-start(bf16[8,32,128]{2,1,0:T(8,128)(2,1)} %get-tuple-element.24), calls=%async_computation | async-start | bytes 131072 | tf_op jit(solution)/shard_map/all_to_all | solution.py:477
  10.3 2.4 %collective-permute-start = (bf16[256,128]{1,0:T(8,128)(2,1)S(1)}, bf16[256,128]{1,0:T(8,128)(2,1)S(1)}, u32[]{:S(2)}, u32[]{:S(2)}) collective-permute-start(bf16[256,128]{1,0:T(8,128)(2,1)S(1)} %get-tuple-element.23.own), channel_id=1, source_target_pairs={{0,1},{1,0},{2,3},{3,2},{4,5},{5,4},{6,7},{7,6},{8,9},{9,8},{10,11... | collective-permute-start | bytes 196616 | tf_op jit(solution)/shard_map/ppermute | solution.py:422
  10.3 7.3 %collective-permute-start.2 = (bf16[256,128]{1,0:T(8,128)(2,1)S(1)}, bf16[256,128]{1,0:T(8,128)(2,1)S(1)}, u32[]{:S(2)}, u32[]{:S(2)}) collective-permute-start(bf16[256,128]{1,0:T(8,128)(2,1)S(1)} %get-tuple-element.23.own), channel_id=1, source_target_pairs={{0,14},{1,15},{2,4},{3,5},{4,2},{5,3},{6,8},{7,9},{8,6},{9,7},{10,... | collective-permute-start | bytes 196616 | tf_op jit(solution)/shard_map/ppermute | solution.py:422
  12.7 5.6 %collective-permute-start.1 = (bf16[256,128]{1,0:T(8,128)(2,1)S(1)}, bf16[256,128]{1,0:T(8,128)(2,1)S(1)}, u32[]{:S(2)}, u32[]{:S(2)}) collective-permute-start(bf16[256,128]{1,0:T(8,128)(2,1)S(1)} %get-tuple-element.23.own), channel_id=1, source_target_pairs={{0,2},{1,3},{2,0},{3,1},{4,6},{5,7},{6,4},{7,5},{8,10},{9,11},{10,... | collective-permute-start | bytes 196616 | tf_op jit(solution)/shard_map/ppermute | solution.py:422
  18.3 1.7 %collective-permute-start.3 = (bf16[512,128]{1,0:T(8,128)(2,1)S(1)}, bf16[512,128]{1,0:T(8,128)(2,1)S(1)}, u32[]{:S(2)}, u32[]{:S(2)}) collective-permute-start(bf16[512,128]{1,0:T(8,128)(2,1)S(1)} %relay.2._.sent), channel_id=1, source_target_pairs={{0,1},{1,0},{2,3},{3,2},{4,5},{5,4},{6,7},{7,6},{8,9},{9,8},{10,11... | collective-permute-start | bytes 393224 | tf_op jit(solution)/shard_map/ppermute | solution.py:422
  24.3 9.7 %all-to-all-start.1 = ((bf16[8,48,128]{2,1,0:T(8,128)(2,1)}), bf16[8,48,128]{2,1,0:T(8,128)(2,1)S(1)}, u32[]{:S(2)}, u32[]{:S(2)}) async-start(bf16[8,48,128]{2,1,0:T(8,128)(2,1)} %get-tuple-element.36), calls=%async_computation.1 | async-start | bytes 196608 | tf_op jit(solution)/shard_map/all_to_all | solution.py:477
  28.9 2.4 %collective-permute-start.4 = (bf16[256,128]{1,0:T(8,128)(2,1)S(1)}, bf16[256,128]{1,0:T(8,128)(2,1)S(1)}, u32[]{:S(2)}, u32[]{:S(2)}) collective-permute-start(bf16[256,128]{1,0:T(8,128)(2,1)S(1)} %get-tuple-element.35.own), channel_id=1, source_target_pairs={{0,1},{1,0},{2,3},{3,2},{4,5},{5,4},{6,7},{7,6},{8,9},{9,8},{10,11... | collective-permute-start | bytes 196616 | tf_op jit(solution)/shard_map/ppermute | solution.py:422
  28.9 7.7 %collective-permute-start.6 = (bf16[256,128]{1,0:T(8,128)(2,1)S(1)}, bf16[256,128]{1,0:T(8,128)(2,1)S(1)}, u32[]{:S(2)}, u32[]{:S(2)}) collective-permute-start(bf16[256,128]{1,0:T(8,128)(2,1)S(1)} %get-tuple-element.35.own), channel_id=1, source_target_pairs={{0,14},{1,15},{2,4},{3,5},{4,2},{5,3},{6,8},{7,9},{8,6},{9,7},{10,... | collective-permute-start | bytes 196616 | tf_op jit(solution)/shard_map/ppermute | solution.py:422
  31.2 5.6 %collective-permute-start.5 = (bf16[256,128]{1,0:T(8,128)(2,1)S(1)}, bf16[256,128]{1,0:T(8,128)(2,1)S(1)}, u32[]{:S(2)}, u32[]{:S(2)}) collective-permute-start(bf16[256,128]{1,0:T(8,128)(2,1)S(1)} %get-tuple-element.35.own), channel_id=1, source_target_pairs={{0,2},{1,3},{2,0},{3,1},{4,6},{5,7},{6,4},{7,5},{8,10},{9,11},{10,... | collective-permute-start | bytes 196616 | tf_op jit(solution)/shard_map/ppermute | solution.py:422
  36.9 1.5 %collective-permute-start.7 = (bf16[640,128]{1,0:T(8,128)(2,1)S(1)}, bf16[640,128]{1,0:T(8,128)(2,1)S(1)}, u32[]{:S(2)}, u32[]{:S(2)}) collective-permute-start(bf16[640,128]{1,0:T(8,128)(2,1)S(1)} %relay.3.sent), channel_id=1, source_target_pairs={{0,1},{1,0},{2,3},{3,2},{4,5},{5,4},{6,7},{7,6},{8,9},{9,8},{10,11... | collective-permute-start | bytes 491528 | tf_op jit(solution)/shard_map/ppermute | solution.py:422
